TPU v7x, 32 devices: a whole 2x2x4 slice. The times are simulated.
32 devices in a mesh: gx: 8 (over z, core), gy: 4 (over y, x).
Axes of the slice: x: 2, y: 2, z: 4, core: 2. Of those that a mesh axis runs over, the one named last changes fastest.
Arguments:
- positions: float32 [8, 4, 3, 256], P('gx', 'gy'), may hold values from 0 to 10
- species: int32 [8, 4, 256], P('gx', 'gy'), may hold values from 0 to 5
- neighbours: int32 [8, 4, 256, 12], P('gx', 'gy'), may hold values from 0 to 2303
- counts: int32 [8, 4, 256], P('gx', 'gy'), may hold values from 6 to 12
- species_embed: float32 [6, 128], replicated, may hold values from -6 to 6
- radial: float32 [2, 2, 8, 128], replicated, may hold values from -2 to 2
- mixing: float32 [2, 2, 128, 128], replicated, may hold values from -0.5 to 0.5
- read_hidden: float32 [128, 128], replicated, may hold values from -0.5 to 0.5
- read_out: float32 [128], replicated, may hold values from -0.5 to 0.5
- charge_map: float32 [128, 64], replicated, may hold values from -0.5 to 0.5
- wavevectors: int32 [3, 4096], replicated, may hold values from -8 to 8, as said below
Outputs:
- forces: float32 [8, 4, 3, 256], P('gx', 'gy')
- site_energy: float32 [8, 4, 256], P('gx', 'gy')
Inputs may be any that keep to these rules, and one draw needn't show every extreme that they name: `neighbours`: entry (3 a + b) * 256 + t names atom t of the cell offset by (a - 1, b - 1) along gx, gy, periodically. Slots n < counts are used. `wavevectors`: the 4096 triples are distinct, and no triple has its first two components both zero.
All inputs are finite; a program needn't handle non-finite values.
Results may differ from a plain program's by a relative error of at most 0.0017.
Values may be sent and summed in bfloat16 or wider, within the bound.
No kernel may reach another device: no remote copies, remote signals or barrier semaphores. Data moves between devices by JAX's collectives and lax.ppermute only.
A program may use at most 128 MiB of HBM per device.

v0:
```python
import math

import jax
import jax.numpy as jnp
from jax import lax
from jax.sharding import PartitionSpec as P

cell_width = 10.0
box_height = 30.0
cut_radius = 50.0
soften = 0.25
screen = 0.5
smear_width = 0.5
highest = lax.Precision.HIGHEST


def passed_along(block, axis, distance):
    devices = range(lax.axis_size(axis))
    route = [((i - distance) % len(devices), i) for i in devices]
    return lax.ppermute(block, axis, route)


def with_halo(block, sides, width):
    for axis, dim in sides:
        count = lax.axis_size(axis)
        forward = [(i, i + 1) for i in range(count - 1)]
        forward.append((count - 1, 0))
        backward = [(target, source) for source, target in forward]
        low = lax.ppermute(
            lax.slice_in_dim(block, block.shape[dim] - width, None, axis=dim), axis, forward
        )
        high = lax.ppermute(lax.slice_in_dim(block, 0, width, axis=dim), axis, backward)
        block = jnp.concatenate([low, block, high], axis=dim)
    return block


def build_frame(extended):
    offsets = (jnp.arange(3, dtype=jnp.float32) - 1.0) * cell_width
    shift_x = jnp.broadcast_to(offsets[:, None], (3, 3))
    shift_y = jnp.broadcast_to(offsets[None, :], (3, 3))
    shifts = jnp.stack([shift_x, shift_y, jnp.zeros((3, 3), jnp.float32)], axis=2)
    coords = extended[:, :, :3, :] + shifts[:, :, :, None]
    src_pos = jnp.moveaxis(coords, 2, 0).reshape(3, -1)
    kind_codes = extended[:, :, 3, :].reshape(-1)
    return (src_pos, kind_codes)


def embed_rows(kind_codes, species_embed):
    lookup = (
        kind_codes[:, None] == jnp.arange(species_embed.shape[0], dtype=jnp.float32)[None, :]
    ).astype(jnp.float32)
    return jnp.dot(lookup, species_embed, precision=highest)


def interact(h_dst, h_src, own_pos, src_pos, neighbour_ids, slot_counts, radial_pair, mix_pair):
    slots = neighbour_ids.shape[1]
    orders = radial_pair.shape[1]
    relative = src_pos[:, neighbour_ids] - own_pos[:, :, None]
    distance = jnp.sqrt(jnp.sum(relative * relative, axis=0) + soften)
    unit_vec = relative / distance[None]
    frequency = jnp.arange(1, orders + 1, dtype=jnp.float32) * (math.pi / cut_radius)
    arg_scaled = distance[:, :, None] * frequency
    radial_basis = jnp.sin(arg_scaled) / arg_scaled
    live_slots = (jnp.arange(slots)[None, :] < slot_counts[:, None]).astype(jnp.float32)
    weight_zero = (
        jnp.einsum("anr,rc->anc", radial_basis, radial_pair[0], precision=highest)
        * live_slots[:, :, None]
    )
    weight_one = (
        jnp.einsum("anr,rc->anc", radial_basis, radial_pair[1], precision=highest)
        * live_slots[:, :, None]
    )
    source = h_src[neighbour_ids]
    norm_factor = 1.0 / math.sqrt(slots)
    msg_zero = jnp.sum(weight_zero * source, axis=1) * norm_factor
    msg_one = (
        jnp.einsum("anc,xan->xac", weight_one * source, unit_vec, precision=highest) * norm_factor
    )
    squares = jnp.sum(msg_one * msg_one, axis=0)
    preact = jnp.dot(msg_zero, mix_pair[0], precision=highest) + jnp.dot(
        squares, mix_pair[1], precision=highest
    )
    return h_dst + jax.nn.silu(preact)


def first_layer(own_pos, src_pos, initial_src, neighbour_ids, slot_counts, radial, mixing):
    atom_count = own_pos.shape[1]
    return interact(
        initial_src[4 * atom_count : 5 * atom_count],
        initial_src,
        own_pos,
        src_pos,
        neighbour_ids,
        slot_counts,
        radial[0],
        mixing[0],
    )


def second_section(
    hidden_src,
    own_pos,
    src_pos,
    neighbour_ids,
    slot_counts,
    radial,
    mixing,
    read_hidden,
    read_out,
    charge_map,
):
    atom_count = own_pos.shape[1]
    hidden_two = interact(
        hidden_src[4 * atom_count : 5 * atom_count],
        hidden_src,
        own_pos,
        src_pos,
        neighbour_ids,
        slot_counts,
        radial[1],
        mixing[1],
    )
    energy = jnp.dot(
        jax.nn.silu(jnp.dot(hidden_two, read_hidden, precision=highest)),
        read_out,
        precision=highest,
    )
    charges = jnp.dot(hidden_two, charge_map, precision=highest)
    return (energy, charges)


def wave_terms(wavevectors, grid_x, grid_y):
    lengths = jnp.array([grid_x * cell_width, grid_y * cell_width, box_height], dtype=jnp.float32)
    wave_phys = 2.0 * math.pi * wavevectors.astype(jnp.float32) / lengths[:, None]
    wave_sq = jnp.sum(wave_phys * wave_phys, axis=0)
    green_weight = jnp.exp(-smear_width * wave_sq) / (wave_sq + screen * screen)
    return (wave_phys, green_weight)


def phase_pair(global_pos, wave_part):
    angle = (
        global_pos[0][:, None] * wave_part[0][None, :]
        + global_pos[1][:, None] * wave_part[1][None, :]
        + global_pos[2][:, None] * wave_part[2][None, :]
    )
    return (jnp.cos(angle), jnp.sin(angle))


def structure_term(charges, global_pos, wave_part):
    cosine, sine_part = phase_pair(global_pos, wave_part)
    dims = (((0,), (0,)), ((), ()))
    real_part = lax.dot_general(cosine, charges, dims, precision=highest)
    imag_part = lax.dot_general(sine_part, charges, dims, precision=highest)
    return jnp.concatenate([real_part, imag_part], axis=1)


def fold_terms(carried, piece_rows, start_row, charges, global_pos, wave_phys):
    potential, lr_grad = carried
    row_count = piece_rows.shape[0]
    lat_width = charges.shape[1]
    wave_part = lax.dynamic_slice_in_dim(
        wave_phys, jnp.asarray(start_row).astype(jnp.int32), row_count, 1
    )
    cosine, sine_part = phase_pair(global_pos, wave_part)
    weight_re = piece_rows[:, :lat_width]
    weight_im = piece_rows[:, lat_width:]
    potential = (
        potential
        + jnp.dot(cosine, weight_re, precision=highest)
        + jnp.dot(sine_part, weight_im, precision=highest)
    )
    dims = (((1,), (1,)), ((), ()))
    proj_re = lax.dot_general(charges, weight_re, dims, precision=highest)
    proj_im = lax.dot_general(charges, weight_im, dims, precision=highest)
    phase_turn = cosine * proj_im - sine_part * proj_re
    lr_grad = lr_grad + lax.dot_general(wave_part, phase_turn, dims, precision=highest)
    return (potential, lr_grad)


def send_back(cotangent_grid):
    column = cotangent_grid[:, 1]
    for shift_by, column_pick in ((1, 2), (-1, 0)):
        column = column + passed_along(cotangent_grid[:, column_pick], "gy", shift_by)
    running = column[1]
    for shift_by, column_pick in ((1, 2), (-1, 0)):
        running = running + passed_along(column[column_pick], "gx", shift_by)
    return running


def per_device(
    positions,
    species,
    neighbours,
    counts,
    species_embed,
    radial,
    mixing,
    read_hidden,
    read_out,
    charge_map,
    wavevectors,
):
    atom_count = positions.shape[3]
    width = read_hidden.shape[0]
    lat_width = charge_map.shape[1]
    wave_count = wavevectors.shape[1]
    own_pos = positions[0, 0]
    neighbour_ids = neighbours[0, 0]
    slot_counts = counts[0, 0]
    packed = jnp.concatenate([positions, species.astype(jnp.float32)[:, :, None, :]], axis=2)
    extended = with_halo(packed, (("gx", 0), ("gy", 1)), 1)
    src_pos, kind_codes = build_frame(extended)
    initial_src = embed_rows(kind_codes, species_embed)

    def layer_one(own_coords, source_coords):
        return first_layer(
            own_coords, source_coords, initial_src, neighbour_ids, slot_counts, radial, mixing
        )

    hidden_one, pull_one = jax.vjp(layer_one, own_pos, src_pos)
    hidden_low = hidden_one.astype(jnp.bfloat16)
    ghost_hidden = with_halo(hidden_low[None, None], (("gx", 0), ("gy", 1)), 1)
    hidden_src = ghost_hidden.reshape(9 * atom_count, width).astype(jnp.float32)

    def section_two(source_hidden, own_coords, source_coords):
        return second_section(
            source_hidden,
            own_coords,
            source_coords,
            neighbour_ids,
            slot_counts,
            radial,
            mixing,
            read_hidden,
            read_out,
            charge_map,
        )

    (energy_sr, charges), pull_two = jax.vjp(section_two, hidden_src, own_pos, src_pos)
    grid_x = lax.axis_size("gx")
    grid_y = lax.axis_size("gy")
    row_index = lax.axis_index("gx")
    col_index = lax.axis_index("gy")
    anchor = jnp.stack(
        [
            row_index.astype(jnp.float32) * cell_width,
            col_index.astype(jnp.float32) * cell_width,
            jnp.zeros((), jnp.float32),
        ]
    )
    global_pos = own_pos + anchor[:, None]
    wave_phys, green_weight = wave_terms(wavevectors, grid_x, grid_y)
    start_state = (
        jnp.zeros((atom_count, lat_width), jnp.float32),
        jnp.zeros((3, atom_count), jnp.float32),
    )

    def fold_piece(carried, piece_rows, start_row):
        return fold_terms(carried, piece_rows, start_row, charges, global_pos, wave_phys)

    block_rows = math.gcd(wave_count, 512)
    block_total = wave_count // block_rows

    def term_block(block_idx):
        return structure_term(
            charges,
            global_pos,
            lax.dynamic_slice_in_dim(wave_phys, block_idx * block_rows, block_rows, 1),
        )

    partial_sf = lax.map(term_block, jnp.arange(block_total)).reshape(wave_count, 2 * lat_width)
    structure = lax.psum(partial_sf, ("gx", "gy"))
    weighted = green_weight[:, None] * structure

    def fold_block(block_idx, carried):
        start_row = block_idx * block_rows
        return fold_piece(
            carried, lax.dynamic_slice_in_dim(weighted, start_row, block_rows, 0), start_row
        )

    potential, lr_grad = lax.fori_loop(0, block_total, fold_block, start_state)
    lr_scale = 1.0 / math.sqrt(wave_count * lat_width * atom_count * grid_x * grid_y)
    site_energy = energy_sr + lr_scale * jnp.sum(charges * potential, axis=1)
    grad_hidden, grad_own_two, grad_src_two = pull_two(
        (jnp.ones_like(energy_sr), 2.0 * lr_scale * potential)
    )
    grad_hidden_own = send_back(grad_hidden.reshape(3, 3, atom_count, width))
    grad_own_one, grad_src_one = pull_one(grad_hidden_own)
    grad_src = jnp.moveaxis((grad_src_one + grad_src_two).reshape(3, 3, 3, atom_count), 0, 2)
    grad_back = send_back(grad_src)
    forces = -(grad_own_one + grad_own_two + grad_back + 2.0 * lr_scale * lr_grad)
    return (forces[None, None], site_energy[None, None])


def solution(mesh):
    in_specs = (
        P("gx", "gy", None, None),
        P("gx", "gy", None),
        P("gx", "gy", None, None),
        P("gx", "gy", None),
        P(),
        P(),
        P(),
        P(),
        P(),
        P(),
        P(),
    )
    out_specs = (P("gx", "gy", None, None), P("gx", "gy", None))
    return jax.shard_map(
        per_device, mesh=mesh, in_specs=in_specs, out_specs=out_specs, check_vma=False
    )
```

profile of v0, /device:TPU:0, one launch (start us, length us, event | category | flops | bytes accessed | tf_op | source)
XLA Modules:
  0.0 531.8 jit_solution(7297382103410184547)
XLA Ops:
  8.6 4.5 collective-permute-start.1
  18.6 2.5 collective-permute-start.3
  22.6 3.1 collective-permute-done.2
  27.0 8.1 %gather_fusion = f32[3072,3]{1,0:T(8,128)S(1)} fusion(f32[3,2304]{0,1:T(8,128)S(1)} %bitcast.271, s32[3072]{0:T(1024)S(1)} %broadcast_clamp_fusion), kind=kCustom, calls=%fused_computation | custom fusion | bytes 86016 | tf_op jit(solution)/shard_map/jvp()/gather | solution.py:58
  39.2 10.8 %gather_fusion.1 = f32[3072,128]{1,0:T(8,128)} fusion(f32[2304,128]{1,0:T(8,128)S(1)} %fusion.133, s32[3072]{0:T(1024)S(1)} %broadcast_clamp_fusion), kind=kCustom, calls=%fused_computation.1 | custom fusion | bytes 3158016 | tf_op jit(solution)/shard_map/jvp()/gather | solution.py:73
  51.6 4.2 multiply_reduce_fusion.1
  55.9 4.4 multiply_multiply_fusion
  60.6 4.0 multiply_reduce_fusion.3
  68.2 3.6 collective-permute-done.4
  74.2 5.0 convolution_multiply_fusion.1
  79.7 10.8 %gather_fusion.2 = f32[3072,128]{1,0:T(8,128)} fusion(f32[2304,128]{1,0:T(8,128)S(1)} %bitcast_convert_fusion, s32[3072]{0:T(1024)S(1)} %broadcast_clamp_fusion), kind=kCustom, calls=%fused_computation.2 | custom fusion | bytes 3158016 | tf_op jit(solution)/shard_map/jvp()/gather | solution.py:73
  92.1 6.9 %copy_multiply_fusion.1 = (f32[256,12,128]{2,0,1:T(8,128)S(1)}, f32[256,128]{1,0:T(8,128)S(1)}, f32[256,12,128]{2,0,1:T(8,128)}) fusion(f32[256,12,128]{2,1,0:T(8,128)S(1)} %reshape.168, f32[256,12,128]{2,0,1:T(8,128)} %convolution_multiply_fusion.1, f32[256,12]{0,1:T(8,128)S(1)} %fusion.161, f32[2,2,8,128]{3,2,1,0:T(8,128)} %param.21, ...), kind=kOutput, calls=%fused_computation.121 | convolution fusion | flops 39337984 | bytes 6451232 | tf_op jit(solution)/shard_map/jvp(anr,rc->anc)/dot_general | solution.py:70
  99.3 4.0 multiply_reduce_fusion.2
  104.5 62.1 %while.26 = (s32[]{:T(128)}, f32[8,512,128]{2,1,0:T(8,128)}, f32[3,256]{1,0:T(4,128)S(1)}, s32[8]{0:T(128)S(1)}, f32[3,4096]{1,0:T(4,128)}, /*index=5*/f32[256,6...) while((s32[]{:T(128)}, f32[8,512,128]{2,1,0:T(8,128)}, ...), condition=%wide.region_7.8_spmd, body=%wide.region_6.7_spmd.sunk | while | flops 202702848 | bytes 2003167 | solution.py:271
  106.8 2.3 fusion.244
  109.1 2.4 fusion.243
  114.5 2.3 fusion.244
  116.9 2.4 fusion.243
  122.3 2.3 fusion.244
  124.6 2.4 fusion.243
  130.0 2.3 fusion.244
  132.3 2.4 fusion.243
  137.7 2.3 fusion.244
  140.1 2.4 fusion.243
  145.4 2.3 fusion.244
  147.8 2.4 fusion.243
  153.2 2.3 fusion.244
  155.5 2.4 fusion.243
  160.9 2.3 fusion.244
  163.3 2.4 fusion.243
  168.3 130.0 %all-reduce.3.cloned.1.call-done = f32[4096,128]{1,0:T(8,128)} async-done(((f32[4096,128]{1,0:T(8,128)}), f32[4096,128]{1,0:T(8,128)}) %all-reduce.3.cloned.1.call-update) | async-done | bytes 2097168 | tf_op jit(solution)/shard_map/psum | solution.py:272
  300.6 87.4 %while.27 = (s32[]{:T(128)}, f32[256,64]{0,1:T(8,128)S(1)}, f32[3,256]{1,0:T(4,128)S(1)}, f32[3,256]{1,0:T(4,128)S(1)}, f32[3,4096]{1,0:T(4,128)}, /*index=5*/f3...) while((s32[]{:T(128)}, f32[256,64]{0,1:T(8,128)S(1)}, ...), condition=%wide.region_10.11_spmd.clone, body=%wide.region_9.10_spmd.clone.sunk | while | flops 410437120 | bytes 3739922 | solution.py:281
  301.5 2.3 convolution_add_fusion.9
  303.8 2.3 convolution_add_fusion.10
  312.4 2.3 convolution_add_fusion.9
  314.7 2.3 convolution_add_fusion.10
  323.2 2.3 convolution_add_fusion.9
  325.5 2.3 convolution_add_fusion.10
  334.1 2.3 convolution_add_fusion.9
  336.4 2.3 convolution_add_fusion.10
  345.0 2.3 convolution_add_fusion.9
  347.3 2.3 convolution_add_fusion.10
  355.8 2.3 convolution_add_fusion.9
  358.1 2.3 convolution_add_fusion.10
  366.7 2.3 convolution_add_fusion.9
  369.0 2.3 convolution_add_fusion.10
  377.6 2.3 convolution_add_fusion.9
  379.9 2.3 convolution_add_fusion.10
  390.0 4.0 fusion.88
  399.2 17.4 %scatter_fusion = f32[2304,128]{1,0:T(8,128)S(1)} fusion(f32[2304,128]{1,0:T(8,128)S(1)} %pad.3, s32[3072]{0:T(1024)S(1)} %reshape.153, f32[3072,128]{1,0:T(8,128)S(1)} %reshape.179), kind=kCustom, calls=%fused_computation.3 | custom fusion | flops 393216 | bytes 4730880 | tf_op jit(solution)/shard_map/transpose(jvp())/scatter-add | solution.py:73
  423.6 6.1 %collective-permute-done.8 = f32[3,256,128]{2,1,0:T(8,128)S(1)} collective-permute-done((f32[3,256,128]{2,1,0:T(8,128)S(1)}, f32[3,256,128]{2,1,0:T(8,128)S(1)}, u32[]{:S(2)}, u32[]{:S(2)}) %collective-permute-start.8) | collective-permute-done | bytes 393248 | tf_op jit(solution)/shard_map/ppermute | solution.py:20
  429.7 6.2 %collective-permute-done.9 = f32[3,256,128]{2,1,0:T(8,128)S(1)} collective-permute-done((f32[3,256,128]{2,1,0:T(8,128)S(1)}, f32[3,256,128]{2,1,0:T(8,128)S(1)}, u32[]{:S(2)}, u32[]{:S(2)}) %collective-permute-start.9) | collective-permute-done | bytes 393248 | tf_op jit(solution)/shard_map/ppermute | solution.py:20
  436.0 3.6 collective-permute-start.11
  439.6 3.6 fusion.125
  444.9 4.1 fusion.47
  449.0 5.3 fusion.89
  454.3 6.2 %fusion.80 = (f32[256,12]{1,0:T(8,128)}, f32[256,12]{1,0:T(8,128)}, f32[256,3,12]{2,1,0:T(4,128)}) fusion(f32[256,12]{1,0:T(8,128)S(1)} %copy-done.30, f32[3,256]{0,1:T(8,128)S(1)} %copy.230, f32[256,12,3]{1,0,2:T(8,128)S(1)} %copy-done.13, f32[256,3,12]{2,1,0:T(4,128)S(1)} %fusion.47, f32[256,12,128]{2,0,1:T(8,128)S(1)} %copy-done.7, ...), kind=kOutput, calls=%fused_computation.110 | convolution fusion | flops 14509056 | bytes 2247680 | tf_op jit(solution)/shard_map/transpose(jvp(anc,xan->xac))/dot_general | solution.py:77
  463.7 3.9 fusion.52
  467.7 3.1 fusion.122
  471.1 3.0 fusion.201
  475.3 17.2 %scatter_custom_fusion.1 = f32[3,2304]{0,1:T(8,128)S(1)} fusion(s32[3072]{0:T(1024)S(1)} %reshape.153, f32[3072,3]{1,0:T(8,128)S(1)} %copy.264, f32[]{:T(128)} %constant.47.clone.1), kind=kCustom, calls=%fused_computation.107 | custom fusion | flops 9216 | bytes 27652 | tf_op jit(solution)/shard_map/transpose(jvp())/scatter-add | solution.py:58
  494.2 17.5 %scatter_custom_fusion.2 = f32[3,2304]{0,1:T(8,128)S(1)} fusion(s32[3072]{0:T(1024)S(1)} %reshape.153, f32[3072,3]{1,0:T(8,128)} %copy.266, f32[]{:T(128)} %constant.47.clone.1), kind=kCustom, calls=%fused_computation.105 | custom fusion | flops 9216 | bytes 28160 | tf_op jit(solution)/shard_map/transpose(jvp())/scatter-add | solution.py:58
  515.0 2.6 collective-permute-start.13
  519.3 3.5 collective-permute-start.15
  (308 shorter events, 126.3 us)
Async XLA Ops:
  7.2 160.9 %copy-start = (f32[128,128]{1,0:T(8,128)S(1)}, f32[128,128]{1,0:T(8,128)}, u32[]{:S(2)}) copy-start(f32[128,128]{1,0:T(8,128)} %param.23) | copy-start | bytes 196612
  7.2 291.2 %all-reduce.3.cloned.1.call-start = ((), (), s32[]{:S(2)}) async-start(), calls=%async_computation | async-start | bytes 4194304 | tf_op jit(solution)/shard_map/psum | solution.py:272
  8.6 8.5 %collective-permute-start.1 = (f32[1,1,4,256]{3,1,2,0:T(1,128)S(1)}, f32[1,1,4,256]{3,1,2,0:T(1,128)S(1)}, u32[]{:S(2)}, u32[]{:S(2)}) collective-permute-start(f32[1,1,4,256]{3,1,2,0:T(1,128)S(1)} %pad_maximum_fusion.5), channel_id=1, source_target_pairs={{4,0},{8,4},{12,8},{16,12},{20,16},{24,20},{28,24},{0,28},{5,1},{9... | collective-permute-start | bytes 12296 | tf_op jit(solution)/shard_map/ppermute | solution.py:32
  13.1 4.8 collective-permute-start
  18.6 4.0 collective-permute-start.3
  21.1 4.6 collective-permute-start.2
  35.1 3.0 copy-start.47
  36.0 1.3 copy-start.10
  51.6 8.6 %copy-start.4 = (f32[256,12,128]{2,1,0:T(8,128)}, f32[256,12,128]{2,1,0:T(8,128)S(1)}, u32[]{:S(2)}) copy-start(f32[256,12,128]{2,1,0:T(8,128)S(1)} %reshape.160) | copy-start | bytes 4718596
  55.8 4.4 copy-start.19
  55.8 4.7 copy-start.11
  55.9 4.7 copy-start.26
  60.2 4.3 copy-start.8
  60.5 5.7 %copy-start.39 = (f32[1,1,3,256]{3,1,2,0:T(1,128)S(1)}, f32[1,1,3,256]{3,1,2,0:T(1,128)}, u32[]{:S(2)}) copy-start(f32[1,1,3,256]{3,1,2,0:T(1,128)} %param.16) | copy-start | bytes 9220
  60.6 5.7 %copy-start.48 = (f32[3]{0:T(128)S(1)}, f32[3]{0:T(128)}, u32[]{:S(2)}) copy-start(f32[3]{0:T(128)} %pad_maximum_fusion.6) | copy-start | bytes 40
  64.8 14.8 %copy-start.17 = (f32[256,128]{1,0:T(8,128)}, f32[256,128]{1,0:T(8,128)S(1)}, u32[]{:S(2)}) copy-start(f32[256,128]{1,0:T(8,128)S(1)} %convolution_add_fusion.5) | copy-start | bytes 393220
  64.9 3.3 collective-permute-start.5
  66.3 5.5 %collective-permute-start.4 = (bf16[1,1,256,128]{3,2,1,0:T(8,128)(2,1)S(1)}, bf16[1,1,256,128]{3,2,1,0:T(8,128)(2,1)S(1)}, u32[]{:S(2)}, u32[]{:S(2)}) collective-permute-start(bf16[1,1,256,128]{3,2,1,0:T(8,128)(2,1)S(1)} %fusion.149), channel_id=1, source_target_pairs={{0,4},{4,8},{8,12},{12,16},{16,20},{20,24},{24,28},{28,0},{1,5},{5... | collective-permute-start | bytes 196616 | tf_op jit(solution)/shard_map/ppermute | solution.py:29
  71.8 7.5 %collective-permute-start.7 = (bf16[3,1,256,128]{3,2,1,0:T(8,128)(2,1)S(1)}, bf16[3,1,256,128]{3,2,1,0:T(8,128)(2,1)S(1)}, u32[]{:S(2)}, u32[]{:S(2)}) collective-permute-start(bf16[3,1,256,128]{3,2,1,0:T(8,128)(2,1)S(1)} %pad_maximum_fusion.1), channel_id=1, source_target_pairs={{1,0},{2,1},{3,2},{0,3},{5,4},{6,5},{7,6},{4,7},{9,8},{10,9},{11,1... | collective-permute-start | bytes 589832 | tf_op jit(solution)/shard_map/ppermute | solution.py:32
  72.5 7.0 %collective-permute-start.6 = (bf16[3,1,256,128]{3,2,1,0:T(8,128)(2,1)S(1)}, bf16[3,1,256,128]{3,2,1,0:T(8,128)(2,1)S(1)}, u32[]{:S(2)}, u32[]{:S(2)}) collective-permute-start(bf16[3,1,256,128]{3,2,1,0:T(8,128)(2,1)S(1)} %pad_maximum_fusion.1), channel_id=1, source_target_pairs={{0,1},{1,2},{2,3},{3,0},{4,5},{5,6},{6,7},{7,4},{8,9},{9,10},{10,1... | collective-permute-start | bytes 589832 | tf_op jit(solution)/shard_map/ppermute | solution.py:29
  92.0 7.0 %copy-start.1 = (f32[256,12,128]{2,1,0:T(8,128)}, f32[256,12,128]{2,1,0:T(8,128)S(1)}, u32[]{:S(2)}) copy-start(f32[256,12,128]{2,1,0:T(8,128)S(1)} %reshape.168) | copy-start | bytes 4718596
  92.0 7.0 %copy-start.20 = (f32[2,2,128,128]{3,2,1,0:T(8,128)S(1)}, f32[2,2,128,128]{3,2,1,0:T(8,128)}, u32[]{:S(2)}) copy-start(f32[2,2,128,128]{3,2,1,0:T(8,128)} %param.22) | copy-start | bytes 786436
  92.0 7.2 %copy-start.12 = (f32[256,12,3]{1,0,2:T(8,128)S(1)}, f32[256,12,3]{1,0,2:T(8,128)}, u32[]{:S(2)}) copy-start(f32[256,12,3]{1,0,2:T(8,128)} %copy-done.10) | copy-start | bytes 110596
  92.1 7.2 %copy-start.27 = (f32[256,12]{1,0:T(8,128)S(1)}, f32[256,12]{1,0:T(8,128)}, u32[]{:S(2)}) copy-start(f32[256,12]{1,0:T(8,128)} %copy.232) | copy-start | bytes 36868
  99.0 4.3 copy-start.6
  99.3 4.2 copy-start.46
  168.3 220.0 %copy-start.52 = (f32[256,128]{1,0:T(8,128)}, f32[256,128]{1,0:T(8,128)S(1)}, u32[]{:S(2)}) copy-start(f32[256,128]{1,0:T(8,128)S(1)} %fusion.196) | copy-start | bytes 393220
  300.5 88.0 %copy-start.50 = (f32[128]{0:T(128)S(1)}, f32[128]{0:T(128)}, u32[]{:S(2)}) copy-start(f32[128]{0:T(128)} %param.24) | copy-start | bytes 1540
  300.5 88.3 %copy-start.21 = (f32[2,2,128,128]{3,2,1,0:T(8,128)S(1)}, f32[2,2,128,128]{3,2,1,0:T(8,128)}, u32[]{:S(2)}) copy-start(f32[2,2,128,128]{3,2,1,0:T(8,128)} %param.22) | copy-start | bytes 786436
  388.9 1.2 copy-start.28
  389.5 4.6 copy-start.36
  390.0 4.0 copy-start.3
  390.0 4.0 copy-start.16
  394.0 1.3 copy-start.14
  399.2 20.4 %copy-start.51 = (f32[128]{0:T(128)S(1)}, f32[128]{0:T(128)}, u32[]{:S(2)}) copy-start(f32[128]{0:T(128)} %param.24) | copy-start | bytes 1540
  416.6 4.8 copy-start.2
  416.6 4.8 copy-start.45
  416.7 13.0 %collective-permute-start.8 = (f32[3,256,128]{2,1,0:T(8,128)S(1)}, f32[3,256,128]{2,1,0:T(8,128)S(1)}, u32[]{:S(2)}, u32[]{:S(2)}) collective-permute-start(f32[3,256,128]{2,1,0:T(8,128)S(1)} %get-tuple-element.335), channel_id=1, source_target_pairs={{3,0},{0,1},{1,2},{2,3},{7,4},{4,5},{5,6},{6,7},{11,8},{8,9},{9,10... | collective-permute-start | bytes 1179656 | tf_op jit(solution)/shard_map/ppermute | solution.py:20
  418.2 17.7 %collective-permute-start.9 = (f32[3,256,128]{2,1,0:T(8,128)S(1)}, f32[3,256,128]{2,1,0:T(8,128)S(1)}, u32[]{:S(2)}, u32[]{:S(2)}) collective-permute-start(f32[3,256,128]{2,1,0:T(8,128)S(1)} %get-tuple-element.336), channel_id=1, source_target_pairs={{1,0},{2,1},{3,2},{0,3},{5,4},{6,5},{7,6},{4,7},{9,8},{10,9},{11,1... | collective-permute-start | bytes 1179656 | tf_op jit(solution)/shard_map/ppermute | solution.py:20
  421.4 18.2 %copy-start.15 = (f32[256,12,128]{2,1,0:T(8,128)S(1)}, f32[256,12,128]{2,1,0:T(8,128)}, u32[]{:S(2)}) copy-start(f32[256,12,128]{2,1,0:T(8,128)} %copy-done.14) | copy-start | bytes 4718596
  435.9 7.6 %collective-permute-start.10 = (f32[256,128]{1,0:T(8,128)S(1)}, f32[256,128]{1,0:T(8,128)S(1)}, u32[]{:S(2)}, u32[]{:S(2)}) collective-permute-start(f32[256,128]{1,0:T(8,128)S(1)} %get-tuple-element.339), channel_id=1, source_target_pairs={{28,0},{0,4},{4,8},{8,12},{12,16},{16,20},{20,24},{24,28},{29,1},{... | collective-permute-start | bytes 393224 | tf_op jit(solution)/shard_map/ppermute | solution.py:20
  436.0 7.5 %copy-start.18 = (f32[256,128]{1,0:T(8,128)S(1)}, f32[256,128]{1,0:T(8,128)}, u32[]{:S(2)}) copy-start(f32[256,128]{1,0:T(8,128)} %copy-done.17) | copy-start | bytes 393220
  436.0 7.6 %copy-start.22 = (f32[2,2,128,128]{3,2,1,0:T(8,128)S(1)}, f32[2,2,128,128]{3,2,1,0:T(8,128)}, u32[]{:S(2)}) copy-start(f32[2,2,128,128]{3,2,1,0:T(8,128)} %param.22) | copy-start | bytes 786436
  436.0 8.8 %copy-start.9 = (f32[256,12,128]{2,0,1:T(8,128)S(1)}, f32[256,12,128]{2,0,1:T(8,128)}, u32[]{:S(2)}) copy-start(f32[256,12,128]{2,0,1:T(8,128)} %copy-done.8) | copy-start | bytes 4718596
  436.0 8.8 %copy-start.23 = (f32[256,3,128]{2,1,0:T(4,128)S(1)}, f32[256,3,128]{2,1,0:T(4,128)}, u32[]{:S(2)}) copy-start(f32[256,3,128]{2,1,0:T(4,128)} %get-tuple-element.350) | copy-start | bytes 1179652
  436.0 7.5 %collective-permute-start.11 = (f32[256,128]{1,0:T(8,128)S(1)}, f32[256,128]{1,0:T(8,128)S(1)}, u32[]{:S(2)}, u32[]{:S(2)}) collective-permute-start(f32[256,128]{1,0:T(8,128)S(1)} %get-tuple-element.340), channel_id=1, source_target_pairs={{4,0},{8,4},{12,8},{16,12},{20,16},{24,20},{28,24},{0,28},{5,1},{9... | collective-permute-start | bytes 393224 | tf_op jit(solution)/shard_map/ppermute | solution.py:20
  444.9 4.1 copy-start.29
  449.0 5.3 copy-start.7
  449.0 5.3 copy-start.25
  449.0 5.3 copy-start.30
  449.0 5.3 copy-start.37
  454.3 9.4 %copy-start.5 = (f32[256,12,128]{2,1,0:T(8,128)S(1)}, f32[256,12,128]{2,1,0:T(8,128)}, u32[]{:S(2)}) copy-start(f32[256,12,128]{2,1,0:T(8,128)} %copy-done.4) | copy-start | bytes 4718596
  463.7 3.9 copy-start.38
  467.7 3.2 copy-start.40
  467.7 3.2 copy-start.42
  467.7 3.2 copy-start.43
  511.7 5.8 %copy-start.33 = (f32[256,64]{0,1:T(8,128)S(1)}, f32[256,64]{0,1:T(8,128)}, u32[]{:S(2)}) copy-start(f32[256,64]{0,1:T(8,128)} %copy-done.32) | copy-start | bytes 196612
  511.7 5.8 %copy-start.35 = (f32[256,64]{0,1:T(8,128)S(1)}, f32[256,64]{0,1:T(8,128)}, u32[]{:S(2)}) copy-start(f32[256,64]{0,1:T(8,128)} %copy-done.34) | copy-start | bytes 196612
  511.7 11.1 %copy-start.49 = (f32[1,256]{1,0:T(1,128)S(1)}, f32[1,256]{1,0:T(1,128)}, u32[]{:S(2)}) copy-start(f32[1,256]{1,0:T(1,128)} %fusion.112) | copy-start | bytes 3076
  511.8 11.7 %copy-start.31 = (f32[3,256]{0,1:T(8,128)S(1)}, f32[3,256]{0,1:T(8,128)}, u32[]{:S(2)}) copy-start(f32[3,256]{0,1:T(8,128)} %get-tuple-element.317) | copy-start | bytes 9220
  514.6 4.6 collective-permute-start.12
  515.0 4.3 collective-permute-start.13
  519.2 4.9 collective-permute-start.14
  519.3 4.9 collective-permute-start.15
  (6 other events, 4.8 us)
Sparse Core Ops, SparseCore 0:
  166.7 131.6 all-reduce.2
where the time goes:
time: 538 us; the launch traced here: 532 us
  matrix products  184 us (34%)
  waiting for transfers between devices  154 us (29%)
  local copies, waits for them, and re-layouts  78.5 us (15%)
  other arithmetic  68.7 us (13%)
  starting transfers between devices  24 us (4%)
  between operations  15.2 us (3%)
  loops' own time  6.43 us (1%)
    psum x1, waiting for transfers between devices, per_device(): structure = lax.psum(partial_sf, ('gx', 'gy'))  130 us
    scatter-add x2, other arithmetic, interact(): relative = src_pos[:, neighbour_ids] - own_pos[:, :, None]  34.7 us
    dot_general x6, matrix products, interact(): jnp.einsum('anc,xan->xac', weight_one * source, unit_vec, precision=highest)  27.5 us
    gather x4, local copies, waits for them, and re-layouts, interact(): source = h_src[neighbour_ids]  24.7 us
    dot_general x8, matrix products, structure_term(): imag_part = lax.dot_general(sine_part, charges, dims, precision=highest)  18.9 us
    dot_general x4, matrix products, interact(): jnp.einsum('anr,rc->anc', radial_basis, radial_pair[1], precision=highest)  18.8 us
    dot_general x8, matrix products, fold_terms(): jnp.dot(sine_part, weight_im, precision=highest)  18.7 us
    dot_general x8, matrix products, structure_term(): real_part = lax.dot_general(cosine, charges, dims, precision=highest)  18.7 us
  transfers between devices with their start and end apart: 17, of which 11 were waited for; matrix products, arithmetic and copies ran while one was open for 4% of the time, Pallas kernels for 0%

commit v1 on v0

--- a/solution.py
+++ b/solution.py
@@ -1,8 +1,12 @@
+import functools
 import math
 
 import jax
 import jax.numpy as jnp
+import numpy as np
 from jax import lax
+from jax.experimental import pallas as pl
+from jax.experimental.pallas import tpu as pltpu
 from jax.sharding import PartitionSpec as P
 
 cell_width = 10.0
@@ -12,6 +16,7 @@
 screen = 0.5
 smear_width = 0.5
 highest = lax.Precision.HIGHEST
+WAVE_REACH = 8
 
 
 def passed_along(block, axis, distance):
@@ -129,52 +134,259 @@
     return (energy, charges)
 
 
-def wave_terms(wavevectors, grid_x, grid_y):
-    lengths = jnp.array([grid_x * cell_width, grid_y * cell_width, box_height], dtype=jnp.float32)
-    wave_phys = 2.0 * math.pi * wavevectors.astype(jnp.float32) / lengths[:, None]
-    wave_sq = jnp.sum(wave_phys * wave_phys, axis=0)
-    green_weight = jnp.exp(-smear_width * wave_sq) / (wave_sq + screen * screen)
-    return (wave_phys, green_weight)
-
-
-def phase_pair(global_pos, wave_part):
-    angle = (
-        global_pos[0][:, None] * wave_part[0][None, :]
-        + global_pos[1][:, None] * wave_part[1][None, :]
-        + global_pos[2][:, None] * wave_part[2][None, :]
-    )
-    return (jnp.cos(angle), jnp.sin(angle))
-
-
-def structure_term(charges, global_pos, wave_part):
-    cosine, sine_part = phase_pair(global_pos, wave_part)
-    dims = (((0,), (0,)), ((), ()))
-    real_part = lax.dot_general(cosine, charges, dims, precision=highest)
-    imag_part = lax.dot_general(sine_part, charges, dims, precision=highest)
-    return jnp.concatenate([real_part, imag_part], axis=1)
-
-
-def fold_terms(carried, piece_rows, start_row, charges, global_pos, wave_phys):
-    potential, lr_grad = carried
-    row_count = piece_rows.shape[0]
-    lat_width = charges.shape[1]
-    wave_part = lax.dynamic_slice_in_dim(
-        wave_phys, jnp.asarray(start_row).astype(jnp.int32), row_count, 1
-    )
-    cosine, sine_part = phase_pair(global_pos, wave_part)
-    weight_re = piece_rows[:, :lat_width]
-    weight_im = piece_rows[:, lat_width:]
-    potential = (
-        potential
-        + jnp.dot(cosine, weight_re, precision=highest)
-        + jnp.dot(sine_part, weight_im, precision=highest)
-    )
-    dims = (((1,), (1,)), ((), ()))
-    proj_re = lax.dot_general(charges, weight_re, dims, precision=highest)
-    proj_im = lax.dot_general(charges, weight_im, dims, precision=highest)
-    phase_turn = cosine * proj_im - sine_part * proj_re
-    lr_grad = lr_grad + lax.dot_general(wave_part, phase_turn, dims, precision=highest)
-    return (potential, lr_grad)
+def recv_from(block, axis, distance):
+    count = lax.axis_size(axis)
+    return lax.ppermute(block, axis, [((i + distance) % count, i) for i in range(count)])
+
+
+def whole(space=pltpu.VMEM):
+    return pl.BlockSpec(memory_space=space)
+
+
+def run(kernel, outs, args, scratch=(), smem=0, flops=1_000_000, name=None):
+    specs = [whole(pltpu.SMEM)] * smem + [whole()] * (len(args) - smem)
+    return pl.pallas_call(
+        kernel,
+        out_shape=outs,
+        in_specs=specs,
+        out_specs=jax.tree.map(lambda _: whole(), outs),
+        scratch_shapes=list(scratch),
+        compiler_params=pltpu.CompilerParams(vmem_limit_bytes=48 * 1024 * 1024),
+        cost_estimate=pl.CostEstimate(flops=flops, bytes_accessed=1_000_000, transcendentals=0),
+        name=name,
+    )(*args)
+
+
+def split(value):
+    high = value.astype(jnp.bfloat16)
+    return high, (value - high.astype(jnp.float32)).astype(jnp.bfloat16)
+
+
+def dot(left, right, contract=((1,), (0,))):
+    return lax.dot_general(left, right, (contract, ((), ())), preferred_element_type=jnp.float32)
+
+
+def pair_tables(parts):
+    reach = WAVE_REACH
+    pairs = [(0, y) for y in range(1, reach + 1)]
+    pairs += [(x, y) for x in range(1, reach + 1) for y in range(-reach, reach + 1)]
+    share = -(-len(pairs) // parts)
+    padded = -(-share // 8) * 8
+    side = 2 * reach + 1
+    pair_rows = np.zeros((parts, padded, 8), np.float32)
+    wave_rows = np.zeros((parts, 2 * 8 * share + padded, 8), np.float32)
+    for part in range(parts):
+        for slot, (x, y) in enumerate(pairs[part * share : (part + 1) * share]):
+            pair_rows[part, slot, :2] = (x, y)
+            rows = [(8 * slot + z - 1, z) for z in range(1, 9)]
+            rows += [(8 * share + 8 * slot + z - 1, -z) for z in range(1, 9)]
+            rows += [(16 * share + slot, 0)]
+            for row, z in rows:
+                code = ((x + reach) * side + y + reach) * side + z + reach
+                wave_rows[part, row, :5] = (x, y, z, code, 1.0)
+    return share, padded, pair_rows, wave_rows
+
+
+def table_kernel(share, padded, grid, pos_ref, pair_ref, wave_ref, vec_ref, *refs):
+    grid_x, grid_y = grid
+    blocks, (ca_ref, sa_ref, cb_ref, sb_ref, weight_ref) = refs[:grid_x], refs[grid_x:]
+    turn = 2.0 * math.pi
+    col = pos_ref[1].astype(jnp.float32) * (1.0 / grid_y)
+    kx = pair_ref[:, 0:1]
+    ky = pair_ref[:, 1:2]
+    kz = (lax.broadcasted_iota(jnp.int32, (8, 1), 0) + 1).astype(jnp.float32)
+    for d in range(grid_x):
+        row_id = lax.rem(pos_ref[0] + d, grid_x).astype(jnp.float32) * (1.0 / grid_x)
+        block = blocks[d]
+        lanes = pl.ds(d * block.shape[1], block.shape[1])
+        x = block[0:1, :] * (1.0 / (grid_x * cell_width)) + row_id
+        y = block[1:2, :] * (1.0 / (grid_y * cell_width)) + col
+        z = block[2:3, :] * (1.0 / box_height)
+        alpha = kx * x + ky * y
+        alpha = (alpha - jnp.round(alpha)) * turn
+        beta = kz * z
+        beta = (beta - jnp.round(beta)) * turn
+        ca_ref[:, lanes] = jnp.cos(alpha)
+        sa_ref[:, lanes] = jnp.sin(alpha)
+        cb_ref[:, lanes] = jnp.cos(beta)
+        sb_ref[:, lanes] = jnp.sin(beta)
+    side = 2 * WAVE_REACH + 1
+    top = side * side * side - 1
+    vec = vec_ref[...].astype(jnp.float32) + WAVE_REACH
+    code = (vec[0:1] * side + vec[1:2]) * side + vec[2:3]
+    code = jnp.maximum(code, top - code)
+    wave = wave_ref[...]
+    own = wave[:, 3:4]
+    width = code.shape[1]
+    seen = jnp.zeros((own.shape[0], 128), jnp.float32)
+    for start in range(0, width, 128):
+        seen = seen + jnp.where(own == code[:, start : start + 128], 1.0, 0.0)
+    count = jnp.sum(seen, axis=1, keepdims=True) * wave[:, 4:5]
+    sq = (
+        (wave[:, 0:1] * (turn / (grid_x * cell_width))) ** 2
+        + (wave[:, 1:2] * (turn / (grid_y * cell_width))) ** 2
+        + (wave[:, 2:3] * (turn / box_height)) ** 2
+    )
+    green = jnp.exp(-smear_width * sq) / (sq + screen * screen) * count
+    weight_ref[...] = jnp.broadcast_to(green, weight_ref.shape)
+
+
+def basis_rows(share, ca, sa, cb, sb):
+    cc, ss, sc, cs = [], [], [], []
+    for p in range(share):
+        c, s = ca[p : p + 1], sa[p : p + 1]
+        cc.append(c * cb)
+        ss.append(s * sb)
+        sc.append(s * cb)
+        cs.append(c * sb)
+    return cc, ss, sc, cs
+
+
+def unpack_rows(block):
+    half = block.shape[1] // 2
+    return jnp.concatenate([block[:, :half], block[:, half:]], axis=0)
+
+
+def pack_rows(block):
+    half = block.shape[0] // 2
+    return jnp.concatenate([block[:half], block[half:]], axis=1)
+
+
+def structure_kernel(share, padded, grid_x, *refs):
+    ca_ref, sa_ref, cb_ref, sb_ref = refs[:4]
+    blocks, (out_ref,) = refs[4 : 4 + grid_x], refs[4 + grid_x :]
+    total = None
+    for d in range(grid_x):
+        charge = unpack_rows(blocks[d][...].astype(jnp.float32))
+        q_high, q_low = split(charge)
+        atoms = charge.shape[0]
+        lanes = pl.ds(d * atoms, atoms)
+        ca, sa, cb, sb = ca_ref[:, lanes], sa_ref[:, lanes], cb_ref[:, lanes], sb_ref[:, lanes]
+        cc, ss, sc, cs = basis_rows(share, ca, sa, cb, sb)
+        high, low = split(jnp.concatenate(cc + ss + sc + cs + [ca, sa], axis=0))
+        wide = charge.shape[1]
+        both = dot(high, jnp.concatenate([q_high, q_low], axis=1))
+        term = both[:, :wide] + both[:, wide:] + dot(low, q_high)
+        total = term if total is None else total + term
+    out_ref[...] = pack_rows(total).astype(out_ref.dtype)
+
+
+def fold_kernel(share, padded, grid, *refs):
+    grid_x, grid_y = grid
+    ca_ref, sa_ref, cb_ref, sb_ref, weight_ref, pair_ref = refs[:6]
+    blocks = refs[6 : 6 + grid_x]
+    parts = refs[6 + grid_x : 6 + grid_x + grid_y]
+    outs = refs[6 + grid_x + grid_y :]
+    turn = 2.0 * math.pi
+    packed = parts[0][...].astype(jnp.float32)
+    for part in parts[1:]:
+        packed = packed + part[...].astype(jnp.float32)
+    struct = unpack_rows(packed)
+    wide = struct.shape[1]
+    span = 8 * share
+    cc, ss, sc, cs = (struct[i * span : (i + 1) * span] for i in range(4))
+    weight = weight_ref[:, :wide]
+    plus, minus, flat = weight[:span], weight[span : 2 * span], weight[2 * span :]
+    re_plus, im_plus = plus * (cc - ss), plus * (sc + cs)
+    re_minus, im_minus = minus * (cc + ss), minus * (sc - cs)
+    rows = jnp.concatenate(
+        [
+            re_plus + re_minus,
+            re_minus - re_plus,
+            im_plus + im_minus,
+            im_plus - im_minus,
+            flat * struct[4 * span : 4 * span + padded],
+            flat * struct[4 * span + padded :],
+        ],
+        axis=0,
+    )
+    row_high, row_low = split(rows)
+    row_three = jnp.concatenate([row_high, row_low, row_high], axis=1)
+    turned = rows.T
+    t_high, t_low = split(turned)
+    t_both = jnp.concatenate([t_high, t_low], axis=0)
+    kx = pair_ref[:, 0:1] * (turn / (grid_x * cell_width))
+    ky = pair_ref[:, 1:2] * (turn / (grid_y * cell_width))
+    kz = (lax.broadcasted_iota(jnp.int32, (8, 1), 0) + 1).astype(jnp.float32) * (turn / box_height)
+    for d in range(grid_x):
+        charge = unpack_rows(blocks[d][...].astype(jnp.float32))
+        q_high, q_low = split(charge)
+        atoms = charge.shape[0]
+        lanes = pl.ds(d * atoms, atoms)
+        ca, sa, cb, sb = ca_ref[:, lanes], sa_ref[:, lanes], cb_ref[:, lanes], sb_ref[:, lanes]
+        bcc, bss, bsc, bcs = basis_rows(share, ca, sa, cb, sb)
+        high, low = split(jnp.concatenate(bcc + bss + bsc + bcs + [ca, sa], axis=0))
+        both = dot(t_both, high)
+        pot = both[:wide] + both[wide:] + dot(t_high, low)
+        proj = dot(row_three, jnp.concatenate([q_high, q_high, q_low], axis=1), ((1,), (1,)))
+        by_x = jnp.zeros((8, atoms), jnp.float32)
+        by_y = jnp.zeros((8, atoms), jnp.float32)
+        by_z = jnp.zeros((8, atoms), jnp.float32)
+        for p in range(share):
+            pcc, pss, psc, pcs = (
+                proj[i * span + 8 * p : i * span + 8 * p + 8] for i in range(4)
+            )
+            slope = bcs[p] * pss - bsc[p] * pcc + bcc[p] * psc - bss[p] * pcs
+            by_x = by_x + kx[p : p + 1] * slope
+            by_y = by_y + ky[p : p + 1] * slope
+            by_z = by_z + (bsc[p] * pss - bcs[p] * pcc - bss[p] * psc + bcc[p] * pcs)
+        flat_slope = ca * proj[4 * span + padded :] - sa * proj[4 * span : 4 * span + padded]
+        grad_x = jnp.sum(by_x, axis=0, keepdims=True) + jnp.sum(kx * flat_slope, axis=0, keepdims=True)
+        grad_y = jnp.sum(by_y, axis=0, keepdims=True) + jnp.sum(ky * flat_slope, axis=0, keepdims=True)
+        grad_z = jnp.sum(kz * by_z, axis=0, keepdims=True)
+        zero = jnp.zeros((5, atoms), jnp.float32)
+        outs[d][...] = jnp.concatenate([pot, grad_x, grad_y, grad_z, zero], axis=0)
+
+
+def long_range(own_rows, charge_block, vectors, lat_width):
+    grid_x, grid_y = lax.axis_size("gx"), lax.axis_size("gy")
+    atoms = own_rows.shape[1]
+    share, padded, pair_np, wave_np = pair_tables(grid_x)
+    place = jnp.stack([lax.axis_index("gx"), lax.axis_index("gy")]).astype(jnp.int32)
+    pair_rows = lax.dynamic_index_in_dim(jnp.asarray(pair_np), place[0], 0, keepdims=False)
+    wave_rows = lax.dynamic_index_in_dim(jnp.asarray(wave_np), place[0], 0, keepdims=False)
+    row_blocks = [own_rows] + [recv_from(own_rows, "gx", d) for d in range(1, grid_x)]
+    total_atoms = grid_x * atoms
+    f32 = jnp.float32
+    tables = run(
+        functools.partial(table_kernel, share, padded, (grid_x, grid_y)),
+        [
+            jax.ShapeDtypeStruct((padded, total_atoms), f32),
+            jax.ShapeDtypeStruct((padded, total_atoms), f32),
+            jax.ShapeDtypeStruct((8, total_atoms), f32),
+            jax.ShapeDtypeStruct((8, total_atoms), f32),
+            jax.ShapeDtypeStruct((wave_np.shape[1], 128), f32),
+        ],
+        [place, pair_rows, wave_rows, vectors] + row_blocks,
+        smem=1,
+        name="tables",
+    )
+    return tables, pair_rows, share, padded
+
+
+def long_range_sum(tables, pair_rows, share, padded, charge_block, lat_width, atoms):
+    grid_x, grid_y = lax.axis_size("gx"), lax.axis_size("gy")
+    f32 = jnp.float32
+    phases, weight = list(tables[:4]), tables[4]
+    blocks = [charge_block] + [recv_from(charge_block, "gx", d) for d in range(1, grid_x)]
+    rows = 32 * share + 2 * padded
+    (part,) = run(
+        functools.partial(structure_kernel, share, padded, grid_x),
+        [jax.ShapeDtypeStruct((rows // 2, 2 * lat_width), f32)],
+        phases + blocks,
+        name="structure",
+    )
+    parts = [part] + [recv_from(part, "gy", d) for d in range(1, grid_y)]
+    folds = run(
+        functools.partial(fold_kernel, share, padded, (grid_x, grid_y)),
+        [jax.ShapeDtypeStruct((lat_width + 8, atoms), f32)] * grid_x,
+        phases + [weight, pair_rows] + blocks + parts,
+        name="fold",
+    )
+    total = folds[0]
+    for d in range(1, grid_x):
+        total = total + recv_from(folds[d], "gx", -d)
+    return total[:lat_width], total[lat_width : lat_width + 3]
 
 
 def send_back(cotangent_grid):
@@ -208,6 +420,9 @@
     neighbour_ids = neighbours[0, 0]
     slot_counts = counts[0, 0]
     packed = jnp.concatenate([positions, species.astype(jnp.float32)[:, :, None, :]], axis=2)
+    packed8 = jnp.concatenate(
+        [packed[0, 0], jnp.zeros((4, atom_count), jnp.float32)], axis=0
+    )
     extended = with_halo(packed, (("gx", 0), ("gy", 1)), 1)
     src_pos, kind_codes = build_frame(extended)
     initial_src = embed_rows(kind_codes, species_embed)
@@ -239,46 +454,11 @@
     (energy_sr, charges), pull_two = jax.vjp(section_two, hidden_src, own_pos, src_pos)
     grid_x = lax.axis_size("gx")
     grid_y = lax.axis_size("gy")
-    row_index = lax.axis_index("gx")
-    col_index = lax.axis_index("gy")
-    anchor = jnp.stack(
-        [
-            row_index.astype(jnp.float32) * cell_width,
-            col_index.astype(jnp.float32) * cell_width,
-            jnp.zeros((), jnp.float32),
-        ]
-    )
-    global_pos = own_pos + anchor[:, None]
-    wave_phys, green_weight = wave_terms(wavevectors, grid_x, grid_y)
-    start_state = (
-        jnp.zeros((atom_count, lat_width), jnp.float32),
-        jnp.zeros((3, atom_count), jnp.float32),
-    )
-
-    def fold_piece(carried, piece_rows, start_row):
-        return fold_terms(carried, piece_rows, start_row, charges, global_pos, wave_phys)
-
-    block_rows = math.gcd(wave_count, 512)
-    block_total = wave_count // block_rows
-
-    def term_block(block_idx):
-        return structure_term(
-            charges,
-            global_pos,
-            lax.dynamic_slice_in_dim(wave_phys, block_idx * block_rows, block_rows, 1),
-        )
-
-    partial_sf = lax.map(term_block, jnp.arange(block_total)).reshape(wave_count, 2 * lat_width)
-    structure = lax.psum(partial_sf, ("gx", "gy"))
-    weighted = green_weight[:, None] * structure
-
-    def fold_block(block_idx, carried):
-        start_row = block_idx * block_rows
-        return fold_piece(
-            carried, lax.dynamic_slice_in_dim(weighted, start_row, block_rows, 0), start_row
-        )
-
-    potential, lr_grad = lax.fori_loop(0, block_total, fold_block, start_state)
+    tables, pair_rows, share, padded = long_range(packed8, None, wavevectors, lat_width)
+    potential, lr_grad = long_range_sum(
+        tables, pair_rows, share, padded, pack_rows(charges), lat_width, atom_count
+    )
+    potential = potential.T
     lr_scale = 1.0 / math.sqrt(wave_count * lat_width * atom_count * grid_x * grid_y)
     site_energy = energy_sr + lr_scale * jnp.sum(charges * potential, axis=1)
     grad_hidden, grad_own_two, grad_src_two = pull_two(

time: 538 us -> 287 us (0.53)
  matrix products: 184 us -> 62.9 us
  waiting for transfers between devices: 154 us -> 38.1 us
  starting transfers between devices: 24 us -> 55.3 us
  local copies, waits for them, and re-layouts: 78.5 us -> 55.6 us
  between operations: 15.2 us -> 2.17 us
  other arithmetic: 68.7 us -> 61.7 us
  Pallas kernels: 0 us -> 6.87 us
  loops' own time: 6.43 us -> 0 us
    psum x1 -> x0, waiting for transfers between devices: 130 us -> none  [per_device(): structure = lax.psum(partial_sf, ('gx', 'gy'))]
    dot_general x56 -> x0, matrix products: 117 us -> none  [the longest x8 18.9 us: structure_term(): imag_part = lax.dot_general(sine_part, charges, dims, precision=highest)]
    ppermute x0 -> x24, starting transfers between devices: none -> 26.8 us  [recv_from(): lax.ppermute(block, axis, [((i + distance) % count, i) for i in range(cou...]
    slice x32 -> x1, local copies, waits for them, and re-layouts: 14.7 us -> 0.01 us  [pack_rows(): return jnp.concatenate([block[:half], block[half:]], axis=1)]
    ppermute x0 -> x24, waiting for transfers between devices: none -> 14.5 us  [recv_from(): lax.ppermute(block, axis, [((i + distance) % count, i) for i in range(cou...]
    pallas_call x0 -> x3, Pallas kernels: none -> 6.87 us  [run(): pl.pallas_call(kernel, out_shape=outs, in_specs=specs, out_specs=jax.tree...]
    dynamic_update_slice x16 -> x0, local copies, waits for them, and re-layouts: 6.81 us -> none  [per_device(): lax.map(term_block, jnp.arange(block_total))]
    another operation x2 -> x0, loops' own time: 6.43 us -> none  [the longest x1 5.67 us: per_device(): lax.map(term_block, jnp.arange(block_total))]
  transfers between devices with their start and end apart: 17 -> 40, of which waited for: 11 -> 16; matrix products, arithmetic and copies ran while one was open for 4% -> 29% of each run, Pallas kernels for 0% -> 1%
where the time goes in v1:
time: 287 us; the launch traced here: 283 us
  matrix products  62.9 us (22%)
  other arithmetic  61.7 us (21%)
  local copies, waits for them, and re-layouts  55.6 us (19%)
  starting transfers between devices  55.3 us (19%)
  waiting for transfers between devices  38.1 us (13%)
  Pallas kernels  6.87 us (2%)
    scatter-add x2, other arithmetic, interact(): relative = src_pos[:, neighbour_ids] - own_pos[:, :, None]  34.7 us
    ppermute x24, starting transfers between devices, recv_from(): lax.ppermute(block, axis, [((i + distance) % count, i) for i in range(cou...  26.8 us
    dot_general x6, matrix products, interact(): jnp.einsum('anc,xan->xac', weight_one * source, unit_vec, precision=highest)  26.3 us
    gather x4, local copies, waits for them, and re-layouts, interact(): source = h_src[neighbour_ids]  26 us
    scatter-add x1, other arithmetic, interact(): source = h_src[neighbour_ids]  17.4 us
    dot_general x4, matrix products, interact(): jnp.einsum('anr,rc->anc', radial_basis, radial_pair[1], precision=highest)  16.6 us
    ppermute x8, waiting for transfers between devices, passed_along(): return lax.ppermute(block, axis, route)  14.9 us
    ppermute x8, starting transfers between devices, passed_along(): return lax.ppermute(block, axis, route)  14.6 us
  transfers between devices with their start and end apart: 40, of which 16 were waited for; matrix products, arithmetic and copies ran while one was open for 29% of the time, Pallas kernels for 1%

profile of v1, /device:TPU:0, one launch (start us, length us, event | category | flops | bytes accessed | tf_op | source)
XLA Modules:
  0.0 282.6 jit_solution(5584145388269248633)
XLA Ops:
  2.6 4.1 %collective-permute-start.1 = (f32[1,1,4,256]{3,2,1,0:T(4,128)S(1)}, f32[1,1,4,256]{3,2,1,0:T(4,128)S(1)}, u32[]{:S(2)}, u32[]{:S(2)}) collective-permute-start(f32[1,1,4,256]{3,2,1,0:T(4,128)S(1)} %pad_maximum_fusion.5), channel_id=1, source_target_pairs={{4,0},{8,4},{12,8},{16,12},{20,16},{24,20},{28,24},{0,28},{5,1},{9... | collective-permute-start | bytes 12296 | tf_op jit(solution)/shard_map/ppermute | solution.py:37
  6.7 3.5 %collective-permute-start.4 = (f32[8,256]{1,0:T(8,128)S(1)}, f32[8,256]{1,0:T(8,128)S(1)}, u32[]{:S(2)}, u32[]{:S(2)}) collective-permute-start(f32[8,256]{1,0:T(8,128)S(1)} %concatenate.24.refs_0_), channel_id=1, source_target_pairs={{4,0},{8,4},{12,8},{16,12},{20,16},{24,20},{28,24},{0,28},{5,1},{9... | collective-permute-start | bytes 24584 | tf_op jit(solution)/shard_map/ppermute | solution.py:139
  12.7 1.6 collective-permute-start.2
  14.3 1.4 collective-permute-start.3
  18.5 8.1 %gather_fusion = f32[3072,3]{1,0:T(8,128)S(1)} fusion(f32[3,2304]{0,1:T(8,128)S(1)} %copy.185, s32[3072]{0:T(1024)S(1)} %broadcast_clamp_fusion), kind=kCustom, calls=%fused_computation | custom fusion | bytes 86016 | tf_op jit(solution)/shard_map/jvp()/gather | solution.py:63
  28.9 1.1 fusion.91
  30.0 10.8 %gather_fusion.1 = f32[3072,128]{1,0:T(8,128)} fusion(f32[2304,128]{1,0:T(8,128)S(1)} %fusion.91, s32[3072]{0:T(1024)S(1)} %broadcast_clamp_fusion), kind=kCustom, calls=%fused_computation.1 | custom fusion | bytes 3158016 | tf_op jit(solution)/shard_map/jvp()/gather | solution.py:78
  40.9 1.7 reshape.140
  42.5 1.5 copy.190
  44.0 4.4 %multiply_multiply_fusion = f32[256,12,128]{2,0,1:T(8,128)S(1)} fusion(f32[256,12]{0,1:T(8,128)S(1)} %fusion.117, f32[256,12,128]{2,1,0:T(8,128)S(1)} %reshape.140, f32[8]{0:T(128)S(1)} %add_multiply_fusion.2, f32[256,12]{0,1:T(8,128)} %get-tuple-element.61, f32[2,2,8,128]{3,2,1,0:T(8,128)} %param.18), kind=kOutput, calls=%fused_computation.29 | convolution fusion | flops 38584320 | bytes 3178528 | tf_op jit(solution)/shard_map/jvp(anr,rc->anc)/dot_general | solution.py:75
  48.5 3.4 %multiply_reduce_fusion.1 = f32[256,128]{1,0:T(8,128)S(1)} fusion(f32[256,12]{0,1:T(8,128)S(1)} %fusion.117, f32[256,12,128]{2,1,0:T(8,128)S(1)} %reshape.140, f32[8]{0:T(128)S(1)} %add_multiply_fusion.2, f32[256,12]{0,1:T(8,128)S(1)} %copy-done.22, f32[2,2,8,128]{3,2,1,0:T(8,128)S(1)} %copy-done.48), kind=kOutput, calls=%fused_computation.28 | convolution fusion | flops 38944768 | bytes 2265600 | tf_op jit(solution)/shard_map/jvp(anr,rc->anc)/dot_general | solution.py:71
  51.9 3.9 %multiply_reduce_fusion.3 = (f32[256,128]{1,0:T(8,128)S(1)}, f32[256,3,128]{2,1,0:T(4,128)}) fusion(f32[256,12,128]{2,0,1:T(8,128)S(1)} %multiply_multiply_fusion, f32[256,12]{1,0:T(8,128)S(1)} %copy-done.33, f32[3,256]{0,1:T(8,128)S(1)} %bitcast.205, f32[256,12,3]{1,0,2:T(8,128)S(1)} %copy-done.12), kind=kOutput, calls=%fused_computation.64 | convolution fusion | flops 14436352 | bytes 2149376 | tf_op jit(solution)/shard_map/jvp(anc,xan->xac)/dot_general | solution.py:82
  57.1 3.0 %collective-permute-start.12 = (bf16[1,1,256,128]{3,2,1,0:T(8,128)(2,1)S(1)}, bf16[1,1,256,128]{3,2,1,0:T(8,128)(2,1)S(1)}, u32[]{:S(2)}, u32[]{:S(2)}) collective-permute-start(bf16[1,1,256,128]{3,2,1,0:T(8,128)(2,1)S(1)} %fusion.106), channel_id=1, source_target_pairs={{4,0},{8,4},{12,8},{16,12},{20,16},{24,20},{28,24},{0,28},{5,1},{9... | collective-permute-start | bytes 196616 | tf_op jit(solution)/shard_map/ppermute | solution.py:37
  62.1 2.4 collective-permute-start.13
  65.3 3.2 %convolution_multiply_fusion.1 = f32[256,12,128]{2,0,1:T(8,128)S(1)} fusion(f32[256,12]{0,1:T(8,128)S(1)} %fusion.117, f32[8]{0:T(128)S(1)} %add_multiply_fusion.2, f32[256,12]{0,1:T(8,128)S(1)} %copy-done.22, f32[2,2,8,128]{3,2,1,0:T(8,128)S(1)} %copy-done.48), kind=kOutput, calls=%fused_computation.31 | convolution fusion | flops 38191104 | bytes 1610240 | tf_op jit(solution)/shard_map/jvp(anr,rc->anc)/dot_general | solution.py:71
  68.5 2.3 collective-permute-done.13
  70.7 3.9 %collective-permute-done.14 = bf16[3,1,256,128]{3,2,1,0:T(8,128)(2,1)S(1)} collective-permute-done((bf16[3,1,256,128]{3,2,1,0:T(8,128)(2,1)S(1)}, bf16[3,1,256,128]{3,2,1,0:T(8,128)(2,1)S(1)}, u32[]{:S(2)}, u32[]{:S(2)}) %collective-permute-start.14) | collective-permute-done | bytes 196640 | tf_op jit(solution)/shard_map/ppermute | solution.py:37
  74.8 10.9 %gather_fusion.2 = f32[3072,128]{1,0:T(8,128)} fusion(f32[2304,128]{1,0:T(8,128)S(1)} %bitcast_convert_fusion, s32[3072]{0:T(1024)S(1)} %broadcast_clamp_fusion), kind=kCustom, calls=%fused_computation.2 | custom fusion | bytes 3158016 | tf_op jit(solution)/shard_map/jvp()/gather | solution.py:78
  85.7 2.6 reshape.148
  88.3 6.0 %copy_multiply_fusion.1 = (f32[256,12,128]{2,0,1:T(8,128)S(1)}, f32[256,128]{1,0:T(8,128)S(1)}, f32[256,12,128]{2,0,1:T(8,128)}) fusion(f32[256,12,128]{2,1,0:T(8,128)} %reshape.148, f32[256,12,128]{2,0,1:T(8,128)S(1)} %convolution_multiply_fusion.1, f32[256,12]{0,1:T(8,128)S(1)} %fusion.117, f32[2,2,8,128]{3,2,1,0:T(8,128)} %param.18, ...), kind=kOutput, calls=%fused_computation.68 | convolution fusion | flops 39337984 | bytes 6975520 | tf_op jit(solution)/shard_map/jvp(anr,rc->anc)/dot_general | solution.py:75
  94.4 4.0 %multiply_reduce_fusion.2 = (f32[256,128]{1,0:T(8,128)S(1)}, f32[256,3,128]{2,1,0:T(4,128)}) fusion(f32[256,12,128]{2,0,1:T(8,128)S(1)} %get-tuple-element.46, f32[256,12]{1,0:T(8,128)S(1)} %copy-done.34, f32[3,256]{0,1:T(8,128)S(1)} %bitcast.206, f32[256,12,3]{1,0,2:T(8,128)S(1)} %copy-done.13), kind=kOutput, calls=%fused_computation.63 | convolution fusion | flops 14436352 | bytes 2149376 | tf_op jit(solution)/shard_map/jvp(anc,xan->xac)/dot_general | solution.py:82
  100.1 2.5 collective-permute-start.9
  102.6 3.6 %collective-permute-start.15 = (f32[128,128]{1,0:T(8,128)S(1)}, f32[128,128]{1,0:T(8,128)S(1)}, u32[]{:S(2)}, u32[]{:S(2)}) collective-permute-start(f32[128,128]{1,0:T(8,128)S(1)} %pad_maximum_fusion.2.refs_4_.refs_6_), channel_id=1, source_target_pairs={{4,0},{8,4},{12,8},{16,12},{20,16},{24,20},{28,24},{0,28},{5,1},{9... | collective-permute-start | bytes 196616 | tf_op jit(solution)/shard_map/ppermute | solution.py:139
  107.0 2.7 collective-permute-start.18
  109.7 1.1 collective-permute-start.20
  111.1 1.2 collective-permute-start.21
  112.4 2.3 tables.1
  114.6 4.1 %collective-permute-done.18.refs_8_.refs_10_ = f32[128,128]{1,0:T(8,128)S(1)} collective-permute-done((f32[128,128]{1,0:T(8,128)S(1)}, f32[128,128]{1,0:T(8,128)S(1)}, u32[]{:S(2)}, u32[]{:S(2)}) %collective-permute-start.18) | collective-permute-done | bytes 65568 | tf_op jit(solution)/shard_map/ppermute | solution.py:139
  119.6 1.8 structure.1.refs_14_
  121.5 2.4 collective-permute-start.22
  124.5 1.5 copy.209
  126.0 2.4 collective-permute-done.22.refs_15_
  128.3 3.9 %collective-permute-done.23.refs_16_ = f32[312,128]{1,0:T(8,128)S(1)} collective-permute-done((f32[312,128]{1,0:T(8,128)S(1)}, f32[312,128]{1,0:T(8,128)S(1)}, u32[]{:S(2)}, u32[]{:S(2)}) %collective-permute-start.23) | collective-permute-done | bytes 159776 | tf_op jit(solution)/shard_map/ppermute | solution.py:139
  132.2 2.8 fold.1
  135.9 1.2 fusion.152
  138.1 2.9 %collective-permute-start.28 = (f32[72,256]{1,0:T(8,128)S(1)}, f32[72,256]{1,0:T(8,128)S(1)}, u32[]{:S(2)}, u32[]{:S(2)}) collective-permute-start(f32[72,256]{1,0:T(8,128)S(1)} %get-tuple-element.24), channel_id=1, source_target_pairs={{16,0},{20,4},{24,8},{28,12},{0,16},{4,20},{8,24},{12,28},{17,1},{... | collective-permute-start | bytes 221192 | tf_op jit(solution)/shard_map/ppermute | solution.py:139
  141.0 2.2 collective-permute-start.30
  143.2 1.5 collective-permute-start.31
  145.0 2.6 collective-permute-done.27
  149.3 4.0 %fusion.45 = f32[256,12,128]{2,1,0:T(8,128)S(1)} fusion(f32[256,3,128]{2,1,0:T(4,128)S(1)} %copy-done.29, f32[256,128]{1,0:T(8,128)S(1)} %convolution_multiply_fusion.5, f32[256,12]{1,0:T(8,128)S(1)} %copy-done.35, f32[3,256]{0,1:T(8,128)S(1)} %bitcast.207, f32[256,12,3]{1,0,2:T(8,128)S(1)} %copy-done.14), kind=kOutput, calls=%fused_computation.76 | convolution fusion | flops 14469120 | bytes 2149376 | tf_op jit(solution)/shard_map/transpose(jvp(anc,xan->xac))/dot_general | solution.py:82
  154.6 2.3 copy.200
  156.9 1.6 reshape.159
  158.5 17.4 %scatter_fusion = f32[2304,128]{1,0:T(8,128)S(1)} fusion(f32[2304,128]{1,0:T(8,128)S(1)} %pad.4, s32[3072]{0:T(1024)S(1)} %reshape.133, f32[3072,128]{1,0:T(8,128)S(1)} %reshape.159), kind=kCustom, calls=%fused_computation.3 | custom fusion | flops 393216 | bytes 4730880 | tf_op jit(solution)/shard_map/transpose(jvp())/scatter-add | solution.py:78
  176.3 2.6 collective-permute-start.33
  178.9 1.7 fusion.70
  180.7 2.2 fusion.11
  182.9 4.9 %collective-permute-done.32 = f32[3,256,128]{2,1,0:T(8,128)S(1)} collective-permute-done((f32[3,256,128]{2,1,0:T(8,128)S(1)}, f32[3,256,128]{2,1,0:T(8,128)S(1)}, u32[]{:S(2)}, u32[]{:S(2)}) %collective-permute-start.32) | collective-permute-done | bytes 393248 | tf_op jit(solution)/shard_map/ppermute | solution.py:25
  187.8 7.8 %collective-permute-done.33 = f32[3,256,128]{2,1,0:T(8,128)S(1)} collective-permute-done((f32[3,256,128]{2,1,0:T(8,128)S(1)}, f32[3,256,128]{2,1,0:T(8,128)S(1)}, u32[]{:S(2)}, u32[]{:S(2)}) %collective-permute-start.33) | collective-permute-done | bytes 393248 | tf_op jit(solution)/shard_map/ppermute | solution.py:25
  196.6 4.2 %collective-permute-start.35 = (f32[256,128]{1,0:T(8,128)S(1)}, f32[256,128]{1,0:T(8,128)S(1)}, u32[]{:S(2)}, u32[]{:S(2)}) collective-permute-start(f32[256,128]{1,0:T(8,128)S(1)} %get-tuple-element.53), channel_id=1, source_target_pairs={{4,0},{8,4},{12,8},{16,12},{20,16},{24,20},{28,24},{0,28},{5,1},{9... | collective-permute-start | bytes 393224 | tf_op jit(solution)/shard_map/ppermute | solution.py:25
  200.8 3.3 %fusion.83 = f32[256,12]{0,1:T(8,128)S(1)} fusion(f32[256,12,8]{0,2,1:T(8,128)S(1)} %fusion.11, f32[256,12,128]{2,1,0:T(8,128)S(1)} %copy-done.16, f32[256,12]{0,1:T(8,128)S(1)} %fusion.117, f32[256,12,128]{2,1,0:T(8,128)S(1)} %copy-done.2, f32[8]{0:T(128)S(1)} %copy-done.53, f32[256,12]{0,1:T(8,128)S(1)} %copy-done.24, f32[2,2,8,128]{3,2,1,0:T(8,128)S(1)} %copy-done.49), kind=kOutput, calls=%fused_computation.133 | convolution fusion | flops 38827008 | bytes 4342272 | tf_op jit(solution)/shard_map/transpose(jvp(anr,rc->anc))/dot_general | solution.py:75
  205.5 4.0 %fusion.46 = f32[256,12,128]{2,1,0:T(8,128)S(1)} fusion(f32[256,3,128]{2,1,0:T(4,128)S(1)} %copy-done.28, f32[256,128]{1,0:T(8,128)S(1)} %convolution_multiply_fusion.3, f32[256,12]{1,0:T(8,128)S(1)} %copy-done.36, f32[3,256]{0,1:T(8,128)S(1)} %bitcast.208, f32[256,12,3]{1,0,2:T(8,128)S(1)} %copy-done.14), kind=kOutput, calls=%fused_computation.77 | convolution fusion | flops 14469120 | bytes 2149376 | tf_op jit(solution)/shard_map/transpose(jvp(anc,xan->xac))/dot_general | solution.py:82
  209.5 4.1 %fusion.4 = f32[256,3,12]{2,1,0:T(4,128)S(1)} fusion(f32[256,12,128]{2,0,1:T(8,128)S(1)} %copy-done.10, f32[256,3,128]{2,1,0:T(4,128)S(1)} %copy-done.28, f32[256,128]{1,0:T(8,128)S(1)} %convolution_multiply_fusion.3), kind=kOutput, calls=%fused_computation.10 | convolution fusion | flops 14450688 | bytes 2134016 | tf_op jit(solution)/shard_map/transpose(jvp(anc,xan->xac))/dot_general | solution.py:82
  213.6 3.0 %fusion.9 = f32[256,12,8]{0,2,1:T(8,128)} fusion(f32[256,12,128]{2,1,0:T(8,128)S(1)} %fusion.46, f32[256,12]{0,1:T(8,128)S(1)} %fusion.117, f32[256,12,128]{2,1,0:T(8,128)S(1)} %copy-done.6, f32[2,2,8,128]{3,2,1,0:T(8,128)S(1)} %copy-done.49), kind=kOutput, calls=%fused_computation.16 | convolution fusion | flops 38535168 | bytes 4313088 | tf_op jit(solution)/shard_map/transpose(jvp(anr,rc->anc))/dot_general | solution.py:75
  216.6 6.3 %fusion.37 = (f32[256,12]{1,0:T(8,128)}, f32[256,12]{1,0:T(8,128)}, f32[256,3,12]{2,1,0:T(4,128)}) fusion(f32[256,12]{1,0:T(8,128)S(1)} %copy-done.37, f32[3,256]{0,1:T(8,128)S(1)} %bitcast.209, f32[256,12,3]{1,0,2:T(8,128)S(1)} %copy-done.14, f32[256,3,12]{2,1,0:T(4,128)S(1)} %fusion.4, f32[256,12,128]{2,0,1:T(8,128)S(1)} %copy-done.8, ...), kind=kOutput, calls=%fused_computation.57 | convolution fusion | flops 14509056 | bytes 2247680 | tf_op jit(solution)/shard_map/transpose(jvp(anc,xan->xac))/dot_general | solution.py:82
  224.9 3.4 %fusion.80 = f32[256,12]{0,1:T(8,128)S(1)} fusion(f32[256,12,8]{0,2,1:T(8,128)} %fusion.9, f32[256,128]{1,0:T(8,128)} %convolution_multiply_fusion.2, f32[256,12]{0,1:T(8,128)S(1)} %fusion.117, f32[256,12,128]{2,1,0:T(8,128)S(1)} %copy-done.6, f32[8]{0:T(128)S(1)} %copy-done.53, f32[256,12]{0,1:T(8,128)S(1)} %copy-done.24, f32[2,2,8,128]{3,2,1,0:T(8,128)} %param.18), kind=kOutput, calls=%fused_computation.130 | convolution fusion | flops 38827008 | bytes 1843232 | tf_op jit(solution)/shard_map/transpose(jvp(anr,rc->anc))/dot_general | solution.py:71
  228.6 3.1 %fusion.157 = (f32[3,256]{0,1:T(8,128)}, f32[3,256,12]{2,0,1:T(4,128)S(1)}, f32[3,256]{0,1:T(8,128)}, f32[3,256,12]{2,0,1:T(4,128)S(1)}) fusion(f32[256,12]{1,0:T(8,128)S(1)} %copy.218, f32[3,256]{0,1:T(8,128)S(1)} %bitcast.210, f32[256,12,3]{1,0,2:T(8,128)S(1)} %copy-done.14, f32[256,3,12]{2,1,0:T(4,128)} %get-tuple-element.69, ...), kind=kLoop, calls=%fused_computation.233 | loop fusion | flops 99840 | bytes 230400 | tf_op jit(solution)/shard_map/transpose(jvp())/reduce_sum | solution.py:63
  232.5 17.2 %scatter_custom_fusion.2 = f32[3,2304]{0,1:T(8,128)S(1)} fusion(s32[3072]{0:T(1024)S(1)} %reshape.133, f32[3072,3]{1,0:T(8,128)S(1)} %copy.223, f32[]{:T(128)} %constant.20.clone.1), kind=kCustom, calls=%fused_computation.52 | custom fusion | flops 9216 | bytes 27652 | tf_op jit(solution)/shard_map/transpose(jvp())/scatter-add | solution.py:63
  250.0 1.7 copy.221
  251.6 17.5 %scatter_custom_fusion.1 = f32[3,2304]{0,1:T(8,128)S(1)} fusion(s32[3072]{0:T(1024)S(1)} %reshape.133, f32[3072,3]{1,0:T(8,128)} %copy.221, f32[]{:T(128)} %constant.20.clone.1), kind=kCustom, calls=%fused_computation.54 | custom fusion | flops 9216 | bytes 28160 | tf_op jit(solution)/shard_map/transpose(jvp())/scatter-add | solution.py:63
  269.2 1.1 add.173
  270.3 1.7 copy.225
  272.4 2.6 collective-permute-start.37
  275.0 1.6 collective-permute-done.36
  276.8 3.5 %collective-permute-start.39 = (f32[3,256]{1,0:T(4,128)S(1)}, f32[3,256]{1,0:T(4,128)S(1)}, u32[]{:S(2)}, u32[]{:S(2)}) collective-permute-start(f32[3,256]{1,0:T(4,128)S(1)} %get-tuple-element.63), channel_id=1, source_target_pairs={{4,0},{8,4},{12,8},{16,12},{20,16},{24,20},{28,24},{0,28},{5,1},{9... | collective-permute-start | bytes 9224 | tf_op jit(solution)/shard_map/ppermute | solution.py:25
  (246 shorter events, 31.3 us)
Async XLA Ops:
  0.6 135.3 %copy-start = (f32[128,128]{1,0:T(8,128)S(1)}, f32[128,128]{1,0:T(8,128)}, u32[]{:S(2)}) copy-start(f32[128,128]{1,0:T(8,128)} %param.20) | copy-start | bytes 196612
  2.1 10.6 %collective-permute-start = (f32[1,1,4,256]{3,2,1,0:T(4,128)S(1)}, f32[1,1,4,256]{3,2,1,0:T(4,128)S(1)}, u32[]{:S(2)}, u32[]{:S(2)}) collective-permute-start(f32[1,1,4,256]{3,2,1,0:T(4,128)S(1)} %pad_maximum_fusion.5), channel_id=1, source_target_pairs={{0,4},{4,8},{8,12},{12,16},{16,20},{20,24},{24,28},{28,0},{1,5},{5... | collective-permute-start | bytes 12296 | tf_op jit(solution)/shard_map/ppermute | solution.py:34
  2.6 10.1 %collective-permute-start.1 = (f32[1,1,4,256]{3,2,1,0:T(4,128)S(1)}, f32[1,1,4,256]{3,2,1,0:T(4,128)S(1)}, u32[]{:S(2)}, u32[]{:S(2)}) collective-permute-start(f32[1,1,4,256]{3,2,1,0:T(4,128)S(1)} %pad_maximum_fusion.5), channel_id=1, source_target_pairs={{4,0},{8,4},{12,8},{16,12},{20,16},{24,20},{28,24},{0,28},{5,1},{9... | collective-permute-start | bytes 12296 | tf_op jit(solution)/shard_map/ppermute | solution.py:37
  6.7 93.3 %collective-permute-start.10 = (f32[8,256]{1,0:T(8,128)S(1)}, f32[8,256]{1,0:T(8,128)S(1)}, u32[]{:S(2)}, u32[]{:S(2)}) collective-permute-start(f32[8,256]{1,0:T(8,128)S(1)} %concatenate.24.refs_0_), channel_id=1, source_target_pairs={{28,0},{0,4},{4,8},{8,12},{12,16},{16,20},{20,24},{24,28},{29,1},{... | collective-permute-start | bytes 24584 | tf_op jit(solution)/shard_map/ppermute | solution.py:139
  6.7 93.3 %collective-permute-start.4 = (f32[8,256]{1,0:T(8,128)S(1)}, f32[8,256]{1,0:T(8,128)S(1)}, u32[]{:S(2)}, u32[]{:S(2)}) collective-permute-start(f32[8,256]{1,0:T(8,128)S(1)} %concatenate.24.refs_0_), channel_id=1, source_target_pairs={{4,0},{8,4},{12,8},{16,12},{20,16},{24,20},{28,24},{0,28},{5,1},{9... | collective-permute-start | bytes 24584 | tf_op jit(solution)/shard_map/ppermute | solution.py:139
  10.3 92.3 %collective-permute-start.5 = (f32[8,256]{1,0:T(8,128)S(1)}, f32[8,256]{1,0:T(8,128)S(1)}, u32[]{:S(2)}, u32[]{:S(2)}) collective-permute-start(f32[8,256]{1,0:T(8,128)S(1)} %concatenate.24.refs_0_), channel_id=1, source_target_pairs={{8,0},{12,4},{16,8},{20,12},{24,16},{28,20},{0,24},{4,28},{9,1},{1... | collective-permute-start | bytes 24584 | tf_op jit(solution)/shard_map/ppermute | solution.py:139
  12.7 4.6 %collective-permute-start.2 = (f32[3,1,4,256]{3,2,1,0:T(4,128)S(1)}, f32[3,1,4,256]{3,2,1,0:T(4,128)S(1)}, u32[]{:S(2)}, u32[]{:S(2)}) collective-permute-start(f32[3,1,4,256]{3,2,1,0:T(4,128)S(1)} %pad_maximum_fusion.4), channel_id=1, source_target_pairs={{0,1},{1,2},{2,3},{3,0},{4,5},{5,6},{6,7},{7,4},{8,9},{9,10},{10,1... | collective-permute-start | bytes 36872 | tf_op jit(solution)/shard_map/ppermute | solution.py:34
  14.3 3.7 %collective-permute-start.3 = (f32[3,1,4,256]{3,2,1,0:T(4,128)S(1)}, f32[3,1,4,256]{3,2,1,0:T(4,128)S(1)}, u32[]{:S(2)}, u32[]{:S(2)}) collective-permute-start(f32[3,1,4,256]{3,2,1,0:T(4,128)S(1)} %pad_maximum_fusion.4), channel_id=1, source_target_pairs={{1,0},{2,1},{3,2},{0,3},{5,4},{6,5},{7,6},{4,7},{9,8},{10,9},{11,1... | collective-permute-start | bytes 36872 | tf_op jit(solution)/shard_map/ppermute | solution.py:37
  15.7 72.6 %copy-start.52 = (f32[8]{0:T(128)}, f32[8]{0:T(128)S(1)}, u32[]{:S(2)}) copy-start(f32[8]{0:T(128)S(1)} %add_multiply_fusion.2) | copy-start | bytes 100
  48.5 7.4 %copy-start.9 = (f32[256,12,128]{2,0,1:T(8,128)}, f32[256,12,128]{2,0,1:T(8,128)S(1)}, u32[]{:S(2)}) copy-start(f32[256,12,128]{2,0,1:T(8,128)S(1)} %multiply_multiply_fusion) | copy-start | bytes 4718596
  56.5 5.6 %collective-permute-start.11 = (bf16[1,1,256,128]{3,2,1,0:T(8,128)(2,1)S(1)}, bf16[1,1,256,128]{3,2,1,0:T(8,128)(2,1)S(1)}, u32[]{:S(2)}, u32[]{:S(2)}) collective-permute-start(bf16[1,1,256,128]{3,2,1,0:T(8,128)(2,1)S(1)} %fusion.106), channel_id=1, source_target_pairs={{0,4},{4,8},{8,12},{12,16},{16,20},{20,24},{24,28},{28,0},{1,5},{5... | collective-permute-start | bytes 196616 | tf_op jit(solution)/shard_map/ppermute | solution.py:34
  57.1 5.0 %collective-permute-start.12 = (bf16[1,1,256,128]{3,2,1,0:T(8,128)(2,1)S(1)}, bf16[1,1,256,128]{3,2,1,0:T(8,128)(2,1)S(1)}, u32[]{:S(2)}, u32[]{:S(2)}) collective-permute-start(bf16[1,1,256,128]{3,2,1,0:T(8,128)(2,1)S(1)} %fusion.106), channel_id=1, source_target_pairs={{4,0},{8,4},{12,8},{16,12},{20,16},{24,20},{28,24},{0,28},{5,1},{9... | collective-permute-start | bytes 196616 | tf_op jit(solution)/shard_map/ppermute | solution.py:37
  62.1 8.6 %collective-permute-start.13 = (bf16[3,1,256,128]{3,2,1,0:T(8,128)(2,1)S(1)}, bf16[3,1,256,128]{3,2,1,0:T(8,128)(2,1)S(1)}, u32[]{:S(2)}, u32[]{:S(2)}) collective-permute-start(bf16[3,1,256,128]{3,2,1,0:T(8,128)(2,1)S(1)} %pad_maximum_fusion.1), channel_id=1, source_target_pairs={{0,1},{1,2},{2,3},{3,0},{4,5},{5,6},{6,7},{7,4},{8,9},{9,10},{10,1... | collective-permute-start | bytes 589832 | tf_op jit(solution)/shard_map/ppermute | solution.py:34
  64.5 10.1 %collective-permute-start.14 = (bf16[3,1,256,128]{3,2,1,0:T(8,128)(2,1)S(1)}, bf16[3,1,256,128]{3,2,1,0:T(8,128)(2,1)S(1)}, u32[]{:S(2)}, u32[]{:S(2)}) collective-permute-start(bf16[3,1,256,128]{3,2,1,0:T(8,128)(2,1)S(1)} %pad_maximum_fusion.1), channel_id=1, source_target_pairs={{1,0},{2,1},{3,2},{0,3},{5,4},{6,5},{7,6},{4,7},{9,8},{10,9},{11,1... | collective-permute-start | bytes 589832 | tf_op jit(solution)/shard_map/ppermute | solution.py:37
  68.5 19.8 %copy-start.3 = (f32[256,12,128]{2,0,1:T(8,128)}, f32[256,12,128]{2,0,1:T(8,128)S(1)}, u32[]{:S(2)}) copy-start(f32[256,12,128]{2,0,1:T(8,128)S(1)} %convolution_multiply_fusion.1) | copy-start | bytes 4718596
  70.7 35.5 %collective-permute-start.6 = (f32[8,256]{1,0:T(8,128)S(1)}, f32[8,256]{1,0:T(8,128)S(1)}, u32[]{:S(2)}, u32[]{:S(2)}) collective-permute-start(f32[8,256]{1,0:T(8,128)S(1)} %concatenate.24.refs_0_), channel_id=1, source_target_pairs={{12,0},{16,4},{20,8},{24,12},{28,16},{0,20},{4,24},{8,28},{13,1},{... | collective-permute-start | bytes 24584 | tf_op jit(solution)/shard_map/ppermute | solution.py:139
  74.6 32.4 %collective-permute-start.7 = (f32[8,256]{1,0:T(8,128)S(1)}, f32[8,256]{1,0:T(8,128)S(1)}, u32[]{:S(2)}, u32[]{:S(2)}) collective-permute-start(f32[8,256]{1,0:T(8,128)S(1)} %concatenate.24.refs_0_), channel_id=1, source_target_pairs={{16,0},{20,4},{24,8},{28,12},{0,16},{4,20},{8,24},{12,28},{17,1},{... | collective-permute-start | bytes 24584 | tf_op jit(solution)/shard_map/ppermute | solution.py:139
  88.3 6.0 %copy-start.13 = (f32[256,12,3]{1,0,2:T(8,128)S(1)}, f32[256,12,3]{1,0,2:T(8,128)}, u32[]{:S(2)}) copy-start(f32[256,12,3]{1,0,2:T(8,128)} %copy-done.11) | copy-start | bytes 110596
  98.3 14.1 %copy-start.1 = (s32[3,4096]{1,0:T(4,128)S(1)}, s32[3,4096]{1,0:T(4,128)}, u32[]{:S(2)}) copy-start(s32[3,4096]{1,0:T(4,128)} %vec_ref.1) | copy-start | bytes 147460
  98.9 8.1 %copy-start.44 = (f32[256,128]{1,0:T(8,128)}, f32[256,128]{1,0:T(8,128)S(1)}, u32[]{:S(2)}) copy-start(f32[256,128]{1,0:T(8,128)S(1)} %convolution_add_fusion) | copy-start | bytes 393220
  100.0 7.0 %collective-permute-start.8 = (f32[8,256]{1,0:T(8,128)S(1)}, f32[8,256]{1,0:T(8,128)S(1)}, u32[]{:S(2)}, u32[]{:S(2)}) collective-permute-start(f32[8,256]{1,0:T(8,128)S(1)} %concatenate.24.refs_0_), channel_id=1, source_target_pairs={{20,0},{24,4},{28,8},{0,12},{4,16},{8,20},{12,24},{16,28},{21,1},{... | collective-permute-start | bytes 24584 | tf_op jit(solution)/shard_map/ppermute | solution.py:139
  100.1 9.6 %collective-permute-start.9 = (f32[8,256]{1,0:T(8,128)S(1)}, f32[8,256]{1,0:T(8,128)S(1)}, u32[]{:S(2)}, u32[]{:S(2)}) collective-permute-start(f32[8,256]{1,0:T(8,128)S(1)} %concatenate.24.refs_0_), channel_id=1, source_target_pairs={{24,0},{28,4},{0,8},{4,12},{8,16},{12,20},{16,24},{20,28},{25,1},{... | collective-permute-start | bytes 24584 | tf_op jit(solution)/shard_map/ppermute | solution.py:139
  102.6 7.1 %collective-permute-start.15 = (f32[128,128]{1,0:T(8,128)S(1)}, f32[128,128]{1,0:T(8,128)S(1)}, u32[]{:S(2)}, u32[]{:S(2)}) collective-permute-start(f32[128,128]{1,0:T(8,128)S(1)} %pad_maximum_fusion.2.refs_4_.refs_6_), channel_id=1, source_target_pairs={{4,0},{8,4},{12,8},{16,12},{20,16},{24,20},{28,24},{0,28},{5,1},{9... | collective-permute-start | bytes 196616 | tf_op jit(solution)/shard_map/ppermute | solution.py:139
  106.2 4.8 %collective-permute-start.16 = (f32[128,128]{1,0:T(8,128)S(1)}, f32[128,128]{1,0:T(8,128)S(1)}, u32[]{:S(2)}, u32[]{:S(2)}) collective-permute-start(f32[128,128]{1,0:T(8,128)S(1)} %pad_maximum_fusion.2.refs_4_.refs_6_), channel_id=1, source_target_pairs={{8,0},{12,4},{16,8},{20,12},{24,16},{28,20},{0,24},{4,28},{9,1},{1... | collective-permute-start | bytes 196616 | tf_op jit(solution)/shard_map/ppermute | solution.py:139
  107.0 7.7 %collective-permute-start.17 = (f32[128,128]{1,0:T(8,128)S(1)}, f32[128,128]{1,0:T(8,128)S(1)}, u32[]{:S(2)}, u32[]{:S(2)}) collective-permute-start(f32[128,128]{1,0:T(8,128)S(1)} %pad_maximum_fusion.2.refs_4_.refs_6_), channel_id=1, source_target_pairs={{12,0},{16,4},{20,8},{24,12},{28,16},{0,20},{4,24},{8,28},{13,1},{... | collective-permute-start | bytes 196616 | tf_op jit(solution)/shard_map/ppermute | solution.py:139
  107.0 11.7 %collective-permute-start.18 = (f32[128,128]{1,0:T(8,128)S(1)}, f32[128,128]{1,0:T(8,128)S(1)}, u32[]{:S(2)}, u32[]{:S(2)}) collective-permute-start(f32[128,128]{1,0:T(8,128)S(1)} %pad_maximum_fusion.2.refs_4_.refs_6_), channel_id=1, source_target_pairs={{16,0},{20,4},{24,8},{28,12},{0,16},{4,20},{8,24},{12,28},{17,1},{... | collective-permute-start | bytes 196616 | tf_op jit(solution)/shard_map/ppermute | solution.py:139
  109.7 10.0 %collective-permute-start.19 = (f32[128,128]{1,0:T(8,128)S(1)}, f32[128,128]{1,0:T(8,128)S(1)}, u32[]{:S(2)}, u32[]{:S(2)}) collective-permute-start(f32[128,128]{1,0:T(8,128)S(1)} %pad_maximum_fusion.2.refs_4_.refs_6_), channel_id=1, source_target_pairs={{20,0},{24,4},{28,8},{0,12},{4,16},{8,20},{12,24},{16,28},{21,1},{... | collective-permute-start | bytes 196616 | tf_op jit(solution)/shard_map/ppermute | solution.py:139
  109.7 10.0 %collective-permute-start.20 = (f32[128,128]{1,0:T(8,128)S(1)}, f32[128,128]{1,0:T(8,128)S(1)}, u32[]{:S(2)}, u32[]{:S(2)}) collective-permute-start(f32[128,128]{1,0:T(8,128)S(1)} %pad_maximum_fusion.2.refs_4_.refs_6_), channel_id=1, source_target_pairs={{24,0},{28,4},{0,8},{4,12},{8,16},{12,20},{16,24},{20,28},{25,1},{... | collective-permute-start | bytes 196616 | tf_op jit(solution)/shard_map/ppermute | solution.py:139
  111.1 8.6 %collective-permute-start.21 = (f32[128,128]{1,0:T(8,128)S(1)}, f32[128,128]{1,0:T(8,128)S(1)}, u32[]{:S(2)}, u32[]{:S(2)}) collective-permute-start(f32[128,128]{1,0:T(8,128)S(1)} %pad_maximum_fusion.2.refs_4_.refs_6_), channel_id=1, source_target_pairs={{28,0},{0,4},{4,8},{8,12},{12,16},{16,20},{20,24},{24,28},{29,1},{... | collective-permute-start | bytes 196616 | tf_op jit(solution)/shard_map/ppermute | solution.py:139
  121.4 23.3 %copy-start.56 = (f32[128]{0:T(128)S(1)}, f32[128]{0:T(128)}, u32[]{:S(2)}) copy-start(f32[128]{0:T(128)} %param.21) | copy-start | bytes 1540
  121.5 6.9 %collective-permute-start.22 = (f32[312,128]{1,0:T(8,128)S(1)}, f32[312,128]{1,0:T(8,128)S(1)}, u32[]{:S(2)}, u32[]{:S(2)}) collective-permute-start(f32[312,128]{1,0:T(8,128)S(1)} %structure.1.refs_14_), channel_id=1, source_target_pairs={{1,0},{2,1},{3,2},{0,3},{5,4},{6,5},{7,6},{4,7},{9,8},{10,9},{11,1... | collective-permute-start | bytes 479240 | tf_op jit(solution)/shard_map/ppermute | solution.py:139
  123.8 8.4 %collective-permute-start.23 = (f32[312,128]{1,0:T(8,128)S(1)}, f32[312,128]{1,0:T(8,128)S(1)}, u32[]{:S(2)}, u32[]{:S(2)}) collective-permute-start(f32[312,128]{1,0:T(8,128)S(1)} %structure.1.refs_14_), channel_id=1, source_target_pairs={{2,0},{3,1},{0,2},{1,3},{6,4},{7,5},{4,6},{5,7},{10,8},{11,9},{8,1... | collective-permute-start | bytes 479240 | tf_op jit(solution)/shard_map/ppermute | solution.py:139
  124.3 7.9 %collective-permute-start.24 = (f32[312,128]{1,0:T(8,128)S(1)}, f32[312,128]{1,0:T(8,128)S(1)}, u32[]{:S(2)}, u32[]{:S(2)}) collective-permute-start(f32[312,128]{1,0:T(8,128)S(1)} %structure.1.refs_14_), channel_id=1, source_target_pairs={{3,0},{0,1},{1,2},{2,3},{7,4},{4,5},{5,6},{6,7},{11,8},{8,9},{9,10... | collective-permute-start | bytes 479240 | tf_op jit(solution)/shard_map/ppermute | solution.py:139
  132.2 15.8 %copy-start.51 = (f32[128,64]{0,1:T(8,128)S(1)}, f32[128,64]{0,1:T(8,128)}, u32[]{:S(2)}) copy-start(f32[128,64]{0,1:T(8,128)} %param.22) | copy-start | bytes 98308
  135.0 13.5 %copy-start.26 = (f32[2,2,128,128]{3,2,1,0:T(8,128)S(1)}, f32[2,2,128,128]{3,2,1,0:T(8,128)}, u32[]{:S(2)}) copy-start(f32[2,2,128,128]{3,2,1,0:T(8,128)} %param.19) | copy-start | bytes 786436
  135.0 13.5 %copy-start.45 = (f32[256,128]{1,0:T(8,128)S(1)}, f32[256,128]{1,0:T(8,128)}, u32[]{:S(2)}) copy-start(f32[256,128]{1,0:T(8,128)} %copy-done.44) | copy-start | bytes 393220
  135.1 5.9 %collective-permute-start.25 = (f32[72,256]{1,0:T(8,128)S(1)}, f32[72,256]{1,0:T(8,128)S(1)}, u32[]{:S(2)}, u32[]{:S(2)}) collective-permute-start(f32[72,256]{1,0:T(8,128)S(1)} %get-tuple-element.21), channel_id=1, source_target_pairs={{28,0},{0,4},{4,8},{8,12},{12,16},{16,20},{20,24},{24,28},{29,1},{... | collective-permute-start | bytes 221192 | tf_op jit(solution)/shard_map/ppermute | solution.py:139
  135.1 8.1 %collective-permute-start.26 = (f32[72,256]{1,0:T(8,128)S(1)}, f32[72,256]{1,0:T(8,128)S(1)}, u32[]{:S(2)}, u32[]{:S(2)}) collective-permute-start(f32[72,256]{1,0:T(8,128)S(1)} %get-tuple-element.22), channel_id=1, source_target_pairs={{24,0},{28,4},{0,8},{4,12},{8,16},{12,20},{16,24},{20,28},{25,1},{... | collective-permute-start | bytes 221192 | tf_op jit(solution)/shard_map/ppermute | solution.py:139
  137.1 10.9 %copy-start.58 = (f32[256,128]{1,0:T(8,128)}, f32[256,128]{1,0:T(8,128)S(1)}, u32[]{:S(2)}) copy-start(f32[256,128]{1,0:T(8,128)S(1)} %fusion.152) | copy-start | bytes 393220
  137.1 10.5 %collective-permute-start.27 = (f32[72,256]{1,0:T(8,128)S(1)}, f32[72,256]{1,0:T(8,128)S(1)}, u32[]{:S(2)}, u32[]{:S(2)}) collective-permute-start(f32[72,256]{1,0:T(8,128)S(1)} %get-tuple-element.23), channel_id=1, source_target_pairs={{20,0},{24,4},{28,8},{0,12},{4,16},{8,20},{12,24},{16,28},{21,1},{... | collective-permute-start | bytes 221192 | tf_op jit(solution)/shard_map/ppermute | solution.py:139
  138.1 9.9 %collective-permute-start.28 = (f32[72,256]{1,0:T(8,128)S(1)}, f32[72,256]{1,0:T(8,128)S(1)}, u32[]{:S(2)}, u32[]{:S(2)}) collective-permute-start(f32[72,256]{1,0:T(8,128)S(1)} %get-tuple-element.24), channel_id=1, source_target_pairs={{16,0},{20,4},{24,8},{28,12},{0,16},{4,20},{8,24},{12,28},{17,1},{... | collective-permute-start | bytes 221192 | tf_op jit(solution)/shard_map/ppermute | solution.py:139
  141.0 7.0 %collective-permute-start.29 = (f32[72,256]{1,0:T(8,128)S(1)}, f32[72,256]{1,0:T(8,128)S(1)}, u32[]{:S(2)}, u32[]{:S(2)}) collective-permute-start(f32[72,256]{1,0:T(8,128)S(1)} %get-tuple-element.25), channel_id=1, source_target_pairs={{12,0},{16,4},{20,8},{24,12},{28,16},{0,20},{4,24},{8,28},{13,1},{... | collective-permute-start | bytes 221192 | tf_op jit(solution)/shard_map/ppermute | solution.py:139
  141.0 7.0 %collective-permute-start.30 = (f32[72,256]{1,0:T(8,128)S(1)}, f32[72,256]{1,0:T(8,128)S(1)}, u32[]{:S(2)}, u32[]{:S(2)}) collective-permute-start(f32[72,256]{1,0:T(8,128)S(1)} %get-tuple-element.26), channel_id=1, source_target_pairs={{8,0},{12,4},{16,8},{20,12},{24,16},{28,20},{0,24},{4,28},{9,1},{1... | collective-permute-start | bytes 221192 | tf_op jit(solution)/shard_map/ppermute | solution.py:139
  143.2 4.8 %collective-permute-start.31 = (f32[72,256]{1,0:T(8,128)S(1)}, f32[72,256]{1,0:T(8,128)S(1)}, u32[]{:S(2)}, u32[]{:S(2)}) collective-permute-start(f32[72,256]{1,0:T(8,128)S(1)} %get-tuple-element.27), channel_id=1, source_target_pairs={{4,0},{8,4},{12,8},{16,12},{20,16},{24,20},{28,24},{0,28},{5,1},{9... | collective-permute-start | bytes 221192 | tf_op jit(solution)/shard_map/ppermute | solution.py:139
  158.5 20.5 %copy-start.57 = (f32[128]{0:T(128)S(1)}, f32[128]{0:T(128)}, u32[]{:S(2)}) copy-start(f32[128]{0:T(128)} %param.21) | copy-start | bytes 1540
  158.5 22.2 %copy-start.32 = (f32[256,128]{1,0:T(8,128)S(1)}, f32[256,128]{1,0:T(8,128)}, u32[]{:S(2)}) copy-start(f32[256,128]{1,0:T(8,128)} %copy-done.31) | copy-start | bytes 393220
  176.0 11.9 %collective-permute-start.32 = (f32[3,256,128]{2,1,0:T(8,128)S(1)}, f32[3,256,128]{2,1,0:T(8,128)S(1)}, u32[]{:S(2)}, u32[]{:S(2)}) collective-permute-start(f32[3,256,128]{2,1,0:T(8,128)S(1)} %get-tuple-element.48), channel_id=1, source_target_pairs={{3,0},{0,1},{1,2},{2,3},{7,4},{4,5},{5,6},{6,7},{11,8},{8,9},{9,10... | collective-permute-start | bytes 1179656 | tf_op jit(solution)/shard_map/ppermute | solution.py:25
  176.3 19.3 %collective-permute-start.33 = (f32[3,256,128]{2,1,0:T(8,128)S(1)}, f32[3,256,128]{2,1,0:T(8,128)S(1)}, u32[]{:S(2)}, u32[]{:S(2)}) collective-permute-start(f32[3,256,128]{2,1,0:T(8,128)S(1)} %get-tuple-element.49), channel_id=1, source_target_pairs={{1,0},{2,1},{3,2},{0,3},{5,4},{6,5},{7,6},{4,7},{9,8},{10,9},{11,1... | collective-permute-start | bytes 1179656 | tf_op jit(solution)/shard_map/ppermute | solution.py:25
  180.7 20.2 %copy-start.16 = (f32[256,12,128]{2,1,0:T(8,128)S(1)}, f32[256,12,128]{2,1,0:T(8,128)}, u32[]{:S(2)}) copy-start(f32[256,12,128]{2,1,0:T(8,128)} %copy-done.15) | copy-start | bytes 4718596
  180.7 20.2 %copy-start.24 = (f32[256,12]{0,1:T(8,128)S(1)}, f32[256,12]{0,1:T(8,128)}, u32[]{:S(2)}) copy-start(f32[256,12]{0,1:T(8,128)} %get-tuple-element.61) | copy-start | bytes 36868
  180.7 20.1 %copy-start.53 = (f32[8]{0:T(128)S(1)}, f32[8]{0:T(128)}, u32[]{:S(2)}) copy-start(f32[8]{0:T(128)} %copy-done.52) | copy-start | bytes 100
  195.7 8.4 %collective-permute-start.34 = (f32[256,128]{1,0:T(8,128)S(1)}, f32[256,128]{1,0:T(8,128)S(1)}, u32[]{:S(2)}, u32[]{:S(2)}) collective-permute-start(f32[256,128]{1,0:T(8,128)S(1)} %get-tuple-element.52), channel_id=1, source_target_pairs={{28,0},{0,4},{4,8},{8,12},{12,16},{16,20},{20,24},{24,28},{29,1},{... | collective-permute-start | bytes 393224 | tf_op jit(solution)/shard_map/ppermute | solution.py:25
  196.6 7.5 %copy-start.19 = (f32[256,128]{1,0:T(8,128)S(1)}, f32[256,128]{1,0:T(8,128)}, u32[]{:S(2)}) copy-start(f32[256,128]{1,0:T(8,128)} %copy-done.18) | copy-start | bytes 393220
  196.6 7.6 %copy-start.27 = (f32[2,2,128,128]{3,2,1,0:T(8,128)S(1)}, f32[2,2,128,128]{3,2,1,0:T(8,128)}, u32[]{:S(2)}) copy-start(f32[2,2,128,128]{3,2,1,0:T(8,128)} %param.19) | copy-start | bytes 786436
  196.6 8.8 %copy-start.28 = (f32[256,3,128]{2,1,0:T(4,128)S(1)}, f32[256,3,128]{2,1,0:T(4,128)}, u32[]{:S(2)}) copy-start(f32[256,3,128]{2,1,0:T(4,128)} %get-tuple-element.65) | copy-start | bytes 1179652
  196.6 8.8 %copy-start.36 = (f32[256,12]{1,0:T(8,128)S(1)}, f32[256,12]{1,0:T(8,128)}, u32[]{:S(2)}) copy-start(f32[256,12]{1,0:T(8,128)} %copy.190) | copy-start | bytes 36868
  196.6 7.5 %collective-permute-start.35 = (f32[256,128]{1,0:T(8,128)S(1)}, f32[256,128]{1,0:T(8,128)S(1)}, u32[]{:S(2)}, u32[]{:S(2)}) collective-permute-start(f32[256,128]{1,0:T(8,128)S(1)} %get-tuple-element.53), channel_id=1, source_target_pairs={{4,0},{8,4},{12,8},{16,12},{20,16},{24,20},{28,24},{0,28},{5,1},{9... | collective-permute-start | bytes 393224 | tf_op jit(solution)/shard_map/ppermute | solution.py:25
  269.2 11.1 %copy-start.55 = (f32[1,256]{1,0:T(1,128)S(1)}, f32[1,256]{1,0:T(1,128)}, u32[]{:S(2)}) copy-start(f32[1,256]{1,0:T(1,128)} %fusion.70) | copy-start | bytes 3076
  269.2 11.6 %copy-start.39 = (f32[3,256]{0,1:T(8,128)S(1)}, f32[3,256]{0,1:T(8,128)}, u32[]{:S(2)}) copy-start(f32[3,256]{0,1:T(8,128)} %get-tuple-element.50) | copy-start | bytes 9220
  270.3 10.6 %copy-start.38 = (f32[3,256]{0,1:T(8,128)S(1)}, f32[3,256]{0,1:T(8,128)}, u32[]{:S(2)}) copy-start(f32[3,256]{0,1:T(8,128)} %get-tuple-element.44) | copy-start | bytes 9220
  272.0 4.6 %collective-permute-start.36 = (f32[3,3,256]{2,1,0:T(4,128)S(1)}, f32[3,3,256]{2,1,0:T(4,128)S(1)}, u32[]{:S(2)}, u32[]{:S(2)}) collective-permute-start(f32[3,3,256]{2,1,0:T(4,128)S(1)} %get-tuple-element.56), channel_id=1, source_target_pairs={{3,0},{0,1},{1,2},{2,3},{7,4},{4,5},{5,6},{6,7},{11,8},{8,9},{9,10... | collective-permute-start | bytes 27656 | tf_op jit(solution)/shard_map/ppermute | solution.py:25
  272.4 4.2 %collective-permute-start.37 = (f32[3,3,256]{2,1,0:T(4,128)S(1)}, f32[3,3,256]{2,1,0:T(4,128)S(1)}, u32[]{:S(2)}, u32[]{:S(2)}) collective-permute-start(f32[3,3,256]{2,1,0:T(4,128)S(1)} %get-tuple-element.57), channel_id=1, source_target_pairs={{1,0},{2,1},{3,2},{0,3},{5,4},{6,5},{7,6},{4,7},{9,8},{10,9},{11,1... | collective-permute-start | bytes 27656 | tf_op jit(solution)/shard_map/ppermute | solution.py:25
  276.7 4.9 %collective-permute-start.38 = (f32[3,256]{1,0:T(4,128)S(1)}, f32[3,256]{1,0:T(4,128)S(1)}, u32[]{:S(2)}, u32[]{:S(2)}) collective-permute-start(f32[3,256]{1,0:T(4,128)S(1)} %get-tuple-element.62), channel_id=1, source_target_pairs={{28,0},{0,4},{4,8},{8,12},{12,16},{16,20},{20,24},{24,28},{29,1},{... | collective-permute-start | bytes 9224 | tf_op jit(solution)/shard_map/ppermute | solution.py:25
  276.8 4.9 %collective-permute-start.39 = (f32[3,256]{1,0:T(4,128)S(1)}, f32[3,256]{1,0:T(4,128)S(1)}, u32[]{:S(2)}, u32[]{:S(2)}) collective-permute-start(f32[3,256]{1,0:T(4,128)S(1)} %get-tuple-element.63), channel_id=1, source_target_pairs={{4,0},{8,4},{12,8},{16,12},{20,16},{24,20},{28,24},{0,28},{5,1},{9... | collective-permute-start | bytes 9224 | tf_op jit(solution)/shard_map/ppermute | solution.py:25
  (35 other events, 117.8 us)

commit v2 on v1

v2 whole, which is shorter than its diff:
```python
import functools
import math

import jax
import jax.numpy as jnp
import numpy as np
from jax import lax
from jax.experimental import pallas as pl
from jax.experimental.pallas import tpu as pltpu
from jax.sharding import PartitionSpec as P

cell_width = 10.0
box_height = 30.0
cut_radius = 50.0
soften = 0.25
screen = 0.5
smear_width = 0.5
WAVE_REACH = 8
F32 = jnp.float32
BF16 = jnp.bfloat16
OFFSETS = [(a, b) for a in (-1, 0, 1) for b in (-1, 0, 1)]
CENTRE = 4


def shifted(block, along_x, along_y):
    count_x, count_y = lax.axis_size("gx"), lax.axis_size("gy")
    route = []
    for i in range(count_x):
        for j in range(count_y):
            source = ((i + along_x) % count_x) * count_y + (j + along_y) % count_y
            route.append((source, i * count_y + j))
    return lax.ppermute(block, ("gx", "gy"), route)


def whole(space=pltpu.VMEM):
    return pl.BlockSpec(memory_space=space)


def run(kernel, outs, args, scratch=(), smem=0, flops=1_000_000, name=None):
    specs = [whole(pltpu.SMEM)] * smem + [whole()] * (len(args) - smem)
    return pl.pallas_call(
        kernel,
        out_shape=outs,
        in_specs=specs,
        out_specs=jax.tree.map(lambda _: whole(), outs),
        scratch_shapes=list(scratch),
        compiler_params=pltpu.CompilerParams(vmem_limit_bytes=48 * 1024 * 1024),
        cost_estimate=pl.CostEstimate(flops=flops, bytes_accessed=1_000_000, transcendentals=0),
        name=name,
    )(*args)


def shape(*dims, dtype=F32):
    return jax.ShapeDtypeStruct(dims, dtype)


def split(value):
    high = value.astype(BF16)
    return high, (value - high.astype(F32)).astype(BF16)


def dot(left, right, contract=((1,), (0,))):
    return lax.dot_general(left, right, (contract, ((), ())), preferred_element_type=F32)


def dot3(left, right):
    left_high, left_low = split(left)
    right_high, right_low = split(right)
    return dot(left_high, right_high) + (dot(left_high, right_low) + dot(left_low, right_high))


def stacked_left(value):
    high = value.astype(BF16).astype(F32)
    rows = jnp.concatenate([high, high, value - high, jnp.zeros_like(high)], axis=0)
    return rows.T.astype(BF16)


def stacked_right(value):
    high = value.astype(BF16).astype(F32)
    return jnp.concatenate([high, value - high, high, jnp.zeros_like(high)], axis=0).astype(BF16)


def silu_pair(value):
    gate = 1.0 / (1.0 + jnp.exp(-value))
    return value * gate, gate * (1.0 + value * (1.0 - gate))


def flat_row(block):
    return jnp.concatenate([block[n : n + 1] for n in range(block.shape[0])], axis=1)


def onehot_kinds(kinds, rows):
    levels = lax.broadcasted_iota(jnp.int32, (rows, kinds.shape[1]), 0).astype(F32)
    return jnp.where(kinds == levels, 1.0, 0.0)


def embedding_stack(embed):
    high = embed.astype(BF16).astype(F32)
    rest = embed - high
    middle = rest.astype(BF16).astype(F32)
    rows = jnp.concatenate([high, middle, rest - middle, jnp.zeros_like(high)], axis=0)
    return rows.T.astype(BF16)


def embedded(stack, kinds):
    hot = onehot_kinds(kinds, 8)
    return dot(stack, jnp.concatenate([hot, hot, hot, jnp.zeros_like(hot)], axis=0).astype(BF16))


def messages(edge_rows, radial_ref, layer, slots, atoms, source):
    scalar = stacked_left(radial_ref[layer, 0])
    vector = stacked_left(radial_ref[layer, 1])
    sums = [None] * 4
    for n in range(slots):
        lanes = slice(n * atoms, (n + 1) * atoms)
        feature = source(n)
        for part in range(4):
            weight = dot(vector if part else scalar, stacked_right(edge_rows[part][:, lanes]))
            term = weight * feature
            sums[part] = term if sums[part] is None else sums[part] + term
    norm = 1.0 / math.sqrt(slots)
    return [total * norm for total in sums]


def mixed(sums, mixing_ref, layer):
    squares = sums[1] * sums[1] + sums[2] * sums[2] + sums[3] * sums[3]
    pre = dot3(mixing_ref[layer, 0].T, sums[0]) + dot3(mixing_ref[layer, 1].T, squares)
    return silu_pair(pre)


def edge_parts(basis_ref, unit_ref):
    basis = basis_ref[...]
    unit = unit_ref[...]
    return [basis] + [basis * unit[i : i + 1] for i in range(3)]


def first_kernel(slots, neighbour_ref, count_ref, embed_ref, radial_ref, mixing_ref, *refs):
    frame, (low_ref, basis_ref, slope_ref, unit_ref, sums_ref, gate_ref) = refs[:9], refs[9:]
    atoms = frame[0].shape[1]
    ids = flat_row(neighbour_ref[...])
    halves = []
    for cell, (a, b) in enumerate(OFFSETS):
        block = frame[cell][...]
        if (a, b) != (0, 0):
            block = jnp.concatenate(
                [block[0:1] + a * cell_width, block[1:2] + b * cell_width, block[2:]], axis=0
            )
        halves += [block[:, s : s + 128] for s in range(0, atoms, 128)]
    pieces = []
    for start in range(0, ids.shape[1], 128):
        part = jnp.broadcast_to(ids[:, start : start + 128], (8, 128))
        lane, half = part & 127, part >> 7
        found = jnp.zeros((8, 128), F32)
        for h, rows in enumerate(halves):
            found = jnp.where(half == h, jnp.take_along_axis(rows, lane, axis=1), found)
        pieces.append(found)
    found = jnp.concatenate(pieces, axis=1)
    own = frame[CENTRE][...]
    relative = found - jnp.concatenate([own] * slots, axis=1)
    rel = [relative[i : i + 1] for i in range(3)]
    distance = jnp.sqrt(rel[0] * rel[0] + rel[1] * rel[1] + rel[2] * rel[2] + soften)
    inverse = 1.0 / distance
    orders = radial_ref.shape[2]
    order = (lax.broadcasted_iota(jnp.int32, (orders, 1), 0) + 1).astype(F32)
    phase = (order * (math.pi / cut_radius)) * distance
    wave = jnp.sin(phase) / phase
    count = count_ref[...]
    live = jnp.concatenate([jnp.where(count > n, 1.0, 0.0) for n in range(slots)], axis=1)
    basis_ref[...] = wave * live
    slope_ref[...] = (jnp.cos(phase) - wave) * (inverse * live)
    kinds = found[3:4]
    unit_ref[...] = jnp.concatenate(
        [r * inverse for r in rel] + [inverse, kinds] + [jnp.zeros_like(kinds)] * 3, axis=0
    )
    stack = embedding_stack(embed_ref[...])
    sums = messages(
        edge_parts(basis_ref, unit_ref),
        radial_ref,
        0,
        slots,
        atoms,
        lambda n: embedded(stack, kinds[:, n * atoms : (n + 1) * atoms]),
    )
    step, gate = mixed(sums, mixing_ref, 0)
    low_ref[...] = (embedded(stack, own[3:4]) + step).astype(BF16)
    for part in range(3):
        sums_ref[part] = sums[part + 1]
    gate_ref[...] = gate


def hot_columns(ids, rows):
    place = lax.broadcasted_iota(jnp.int32, (rows, ids.shape[1]), 0)
    return jnp.where(ids == place, 1.0, 0.0).astype(BF16)


def second_kernel(slots, neighbour_ref, basis_ref, unit_ref, radial_ref, mixing_ref, hidden_ref,
                  out_ref, charge_ref, *refs):
    frame, refs = refs[:9], refs[9:]
    feature_ref, sums_ref, gate_ref, low_charge_ref, full_charge_ref, energy_ref, slope_ref = refs[:7]
    (source_ref,) = refs[7:]
    atoms = frame[0].shape[1]
    for cell in range(9):
        source_ref[:, cell * atoms : (cell + 1) * atoms] = frame[cell][...]

    def gathered(n):
        hot = hot_columns(neighbour_ref[n : n + 1, :], 9 * atoms)
        feature = dot(source_ref[...], hot)
        feature_ref[:, n * atoms : (n + 1) * atoms] = feature.astype(BF16)
        return feature

    sums = messages(edge_parts(basis_ref, unit_ref), radial_ref, 1, slots, atoms, gathered)
    step, gate = mixed(sums, mixing_ref, 1)
    hidden = frame[CENTRE][...].astype(F32) + step
    for part in range(3):
        sums_ref[part] = sums[part + 1]
    gate_ref[...] = gate
    charge = dot3(charge_ref[...].T, hidden)
    full_charge_ref[...] = charge
    low_charge_ref[...] = charge.astype(low_charge_ref.dtype)
    value, slope = silu_pair(dot3(hidden_ref[...].T, hidden))
    out = out_ref[...].T
    energy_ref[...] = jnp.sum(value * out, axis=0, keepdims=True)
    slope_ref[...] = dot3(hidden_ref[...], slope * out)


def message_grads(cotangent, gate_ref, sums_ref, mixing_ref, layer, slots):
    pre = cotangent * gate_ref[...]
    norm = 1.0 / math.sqrt(slots)
    scalar = dot3(mixing_ref[layer, 0], pre) * norm
    squares = dot3(mixing_ref[layer, 1], pre) * (2.0 * norm)
    return [scalar] + [squares * sums_ref[i] for i in range(3)]


def radial_left(radial_ref, layer, path):
    high, low = split(radial_ref[layer, path])
    top = jnp.concatenate([high.astype(F32), high.astype(F32)], axis=1)
    end = jnp.concatenate([low.astype(F32), jnp.zeros(low.shape, F32)], axis=1)
    return jnp.concatenate([top, end], axis=0).astype(BF16)


def radial_grad(left, value):
    high, low = split(value)
    both = dot(left, jnp.concatenate([high, low], axis=0))
    half = both.shape[0] // 2
    return both[:half] + both[half:]


def second_back_kernel(slots, scale, grid_x, neighbour_ref, basis_ref, unit_ref, radial_ref,
                       mixing_ref, charge_ref, feature_ref, sums_ref, gate_ref, full_charge_ref,
                       energy_ref, slope_ref, *refs):
    folds, refs = refs[:grid_x], refs[grid_x:]
    site_ref, long_ref, edge_ref, centre_ref = refs[:4]
    ghosts, (term_ref,) = refs[4:12], refs[12:]
    atoms = gate_ref.shape[1]
    total = folds[0][...]
    for fold in folds[1:]:
        total = total + fold[...]
    wide = full_charge_ref.shape[0]
    potential = total[:wide]
    long_ref[...] = total[wide:] * (2.0 * scale)
    site_ref[...] = energy_ref[...] + scale * jnp.sum(
        full_charge_ref[...] * potential, axis=0, keepdims=True
    )
    cotangent = slope_ref[...] + dot3(charge_ref[...], potential * (2.0 * scale))
    grads = message_grads(cotangent, gate_ref, sums_ref, mixing_ref, 1, slots)
    left = [stacked_left(radial_ref[1, path]) for path in range(2)]
    back = [radial_left(radial_ref, 1, path) for path in range(2)]
    parts = edge_parts(basis_ref, unit_ref)
    for n in range(slots):
        lanes = slice(n * atoms, (n + 1) * atoms)
        feature = feature_ref[:, lanes].astype(F32)
        term = None
        for part in range(4):
            path = 1 if part else 0
            edge_ref[8 * part : 8 * part + 8, lanes] = radial_grad(back[path], grads[part] * feature)
            weight = dot(left[path], stacked_right(parts[part][:, lanes])) * grads[part]
            term = weight if term is None else term + weight
        high, low = split(term)
        term_ref[:, lanes] = jnp.concatenate([high, low], axis=0)
    ids = flat_row(neighbour_ref[...])
    features = centre_ref.shape[0]
    for cell in range(9):
        hot = hot_columns(ids - cell * atoms, atoms)
        both = dot(term_ref[...], hot, ((1,), (1,)))
        grad = both[:features] + both[features:]
        if cell == CENTRE:
            centre_ref[...] = grad + cotangent
        else:
            ghosts[cell - (cell > CENTRE)][...] = grad.astype(BF16)


def first_back_kernel(slots, neighbour_ref, basis_ref, slope_ref, unit_ref, embed_ref, radial_ref,
                      mixing_ref, sums_ref, gate_ref, edge_ref, long_ref, centre_ref, *refs):
    ghosts, refs = refs[:8], refs[8:]
    own_ref, outs = refs[0], refs[1:]
    atoms = gate_ref.shape[1]
    cotangent = centre_ref[...]
    for ghost in ghosts:
        cotangent = cotangent + ghost[...].astype(F32)
    grads = message_grads(cotangent, gate_ref, sums_ref, mixing_ref, 0, slots)
    back = [radial_left(radial_ref, 0, path) for path in range(2)]
    stack = embedding_stack(embed_ref[...])
    unit = unit_ref[...]
    kinds = unit[4:5]
    edges = [[] for _ in range(4)]
    for n in range(slots):
        lanes = slice(n * atoms, (n + 1) * atoms)
        feature = embedded(stack, kinds[:, lanes])
        for part in range(4):
            edges[part].append(radial_grad(back[1 if part else 0], grads[part] * feature))
    edges = [
        edge_ref[8 * part : 8 * part + 8] + jnp.concatenate(edges[part], axis=1) for part in range(4)
    ]
    basis = basis_ref[...]
    units = [unit[i : i + 1] for i in range(3)]
    inverse = unit[3:4]
    by_basis = edges[0]
    for i in range(3):
        by_basis = by_basis + edges[i + 1] * units[i]
    by_unit = [jnp.sum(edges[i + 1] * basis, axis=0, keepdims=True) * inverse for i in range(3)]
    by_distance = jnp.sum(by_basis * slope_ref[...], axis=0, keepdims=True)
    for i in range(3):
        by_distance = by_distance - by_unit[i] * units[i]
    moves = [by_unit[i] + by_distance * units[i] for i in range(3)]
    zero = jnp.zeros_like(moves[0])
    move = jnp.concatenate(moves + [zero] * 5, axis=0)
    own = long_ref[...]
    for n in range(slots):
        own = own - move[:, n * atoms : (n + 1) * atoms]
    ids = flat_row(neighbour_ref[...])
    lane_hot = hot_columns(ids & 127, 128)
    half = ids >> 7
    high = move.astype(BF16).astype(F32)
    both = jnp.concatenate([high, move - high], axis=0)
    per_cell = atoms // 128
    rows = jnp.concatenate(
        [jnp.where(half == h, both, 0.0).astype(BF16) for h in range(9 * per_cell)], axis=0
    )
    spread = dot(rows, lane_hot, ((1,), (1,)))
    for cell in range(9):
        found = []
        for h in range(cell * per_cell, (cell + 1) * per_cell):
            found.append(spread[16 * h : 16 * h + 8] + spread[16 * h + 8 : 16 * h + 16])
        grad = jnp.concatenate(found, axis=1)
        if cell == CENTRE:
            own_ref[...] = own + grad
        else:
            outs[cell - (cell > CENTRE)][...] = grad


def pair_tables(parts):
    reach = WAVE_REACH
    pairs = [(0, y) for y in range(1, reach + 1)]
    pairs += [(x, y) for x in range(1, reach + 1) for y in range(-reach, reach + 1)]
    share = -(-len(pairs) // parts)
    padded = -(-share // 8) * 8
    side = 2 * reach + 1
    pair_rows = np.zeros((parts, padded, 8), np.float32)
    wave_rows = np.zeros((parts, 2 * 8 * share + padded, 8), np.float32)
    for part in range(parts):
        for slot, (x, y) in enumerate(pairs[part * share : (part + 1) * share]):
            pair_rows[part, slot, :2] = (x, y)
            rows = [(8 * slot + z - 1, z) for z in range(1, 9)]
            rows += [(8 * share + 8 * slot + z - 1, -z) for z in range(1, 9)]
            rows += [(16 * share + slot, 0)]
            for row, z in rows:
                code = ((x + reach) * side + y + reach) * side + z + reach
                wave_rows[part, row, :5] = (x, y, z, code, 1.0)
    return share, padded, pair_rows, wave_rows


def table_kernel(share, padded, grid, pos_ref, pair_ref, wave_ref, vec_ref, *refs):
    grid_x, grid_y = grid
    blocks, (ca_ref, sa_ref, cb_ref, sb_ref, weight_ref) = refs[:grid_x], refs[grid_x:]
    turn = 2.0 * math.pi
    col = pos_ref[1].astype(jnp.float32) * (1.0 / grid_y)
    kx = pair_ref[:, 0:1]
    ky = pair_ref[:, 1:2]
    kz = (lax.broadcasted_iota(jnp.int32, (8, 1), 0) + 1).astype(jnp.float32)
    for d in range(grid_x):
        row_id = lax.rem(pos_ref[0] + d, grid_x).astype(jnp.float32) * (1.0 / grid_x)
        block = blocks[d]
        lanes = pl.ds(d * block.shape[1], block.shape[1])
        x = block[0:1, :] * (1.0 / (grid_x * cell_width)) + row_id
        y = block[1:2, :] * (1.0 / (grid_y * cell_width)) + col
        z = block[2:3, :] * (1.0 / box_height)
        alpha = kx * x + ky * y
        alpha = (alpha - jnp.round(alpha)) * turn
        beta = kz * z
        beta = (beta - jnp.round(beta)) * turn
        ca_ref[:, lanes] = jnp.cos(alpha)
        sa_ref[:, lanes] = jnp.sin(alpha)
        cb_ref[:, lanes] = jnp.cos(beta)
        sb_ref[:, lanes] = jnp.sin(beta)
    side = 2 * WAVE_REACH + 1
    top = side * side * side - 1
    vec = vec_ref[...].astype(jnp.float32) + WAVE_REACH
    code = (vec[0:1] * side + vec[1:2]) * side + vec[2:3]
    code = jnp.maximum(code, top - code)
    wave = wave_ref[...]
    own = wave[:, 3:4]
    width = code.shape[1]
    seen = jnp.zeros((own.shape[0], 128), jnp.float32)
    for start in range(0, width, 128):
        seen = seen + jnp.where(own == code[:, start : start + 128], 1.0, 0.0)
    count = jnp.sum(seen, axis=1, keepdims=True) * wave[:, 4:5]
    sq = (
        (wave[:, 0:1] * (turn / (grid_x * cell_width))) ** 2
        + (wave[:, 1:2] * (turn / (grid_y * cell_width))) ** 2
        + (wave[:, 2:3] * (turn / box_height)) ** 2
    )
    green = jnp.exp(-smear_width * sq) / (sq + screen * screen) * count
    weight_ref[...] = jnp.broadcast_to(green, weight_ref.shape)


def basis_rows(share, ca, sa, cb, sb):
    cc, ss, sc, cs = [], [], [], []
    for p in range(share):
        c, s = ca[p : p + 1], sa[p : p + 1]
        cc.append(c * cb)
        ss.append(s * sb)
        sc.append(s * cb)
        cs.append(c * sb)
    return cc, ss, sc, cs


def unpack_rows(block):
    half = block.shape[1] // 2
    return jnp.concatenate([block[:, :half], block[:, half:]], axis=0)


def pack_rows(block):
    half = block.shape[0] // 2
    return jnp.concatenate([block[:half], block[half:]], axis=1)


def structure_kernel(share, padded, grid_x, *refs):
    ca_ref, sa_ref, cb_ref, sb_ref = refs[:4]
    blocks, (out_ref,) = refs[4 : 4 + grid_x], refs[4 + grid_x :]
    total = None
    for d in range(grid_x):
        charge = blocks[d][...]
        atoms = charge.shape[1]
        lanes = pl.ds(d * atoms, atoms)
        ca, sa, cb, sb = ca_ref[:, lanes], sa_ref[:, lanes], cb_ref[:, lanes], sb_ref[:, lanes]
        cc, ss, sc, cs = basis_rows(share, ca, sa, cb, sb)
        high, low = split(jnp.concatenate(cc + ss + sc + cs + [ca, sa], axis=0))
        term = dot(high, charge, ((1,), (1,))) + dot(low, charge, ((1,), (1,)))
        total = term if total is None else total + term
    out_ref[...] = pack_rows(total).astype(out_ref.dtype)


def fold_kernel(share, padded, grid, *refs):
    grid_x, grid_y = grid
    ca_ref, sa_ref, cb_ref, sb_ref, weight_ref, pair_ref = refs[:6]
    blocks = refs[6 : 6 + grid_x]
    parts = refs[6 + grid_x : 6 + grid_x + grid_y]
    outs = refs[6 + grid_x + grid_y :]
    turn = 2.0 * math.pi
    packed = parts[0][...].astype(jnp.float32)
    for part in parts[1:]:
        packed = packed + part[...].astype(jnp.float32)
    struct = unpack_rows(packed)
    wide = struct.shape[1]
    span = 8 * share
    cc, ss, sc, cs = (struct[i * span : (i + 1) * span] for i in range(4))
    weight = weight_ref[:, :wide]
    plus, minus, flat = weight[:span], weight[span : 2 * span], weight[2 * span :]
    re_plus, im_plus = plus * (cc - ss), plus * (sc + cs)
    re_minus, im_minus = minus * (cc + ss), minus * (sc - cs)
    rows = jnp.concatenate(
        [
            re_plus + re_minus,
            re_minus - re_plus,
            im_plus + im_minus,
            im_plus - im_minus,
            flat * struct[4 * span : 4 * span + padded],
            flat * struct[4 * span + padded :],
        ],
        axis=0,
    )
    row_high, row_low = split(rows)
    row_pair = jnp.concatenate([row_high, row_low], axis=1)
    turned = rows.T
    t_high, t_low = split(turned)
    t_both = jnp.concatenate([t_high, t_low], axis=0)
    kx = pair_ref[:, 0:1] * (turn / (grid_x * cell_width))
    ky = pair_ref[:, 1:2] * (turn / (grid_y * cell_width))
    kz = (lax.broadcasted_iota(jnp.int32, (8, 1), 0) + 1).astype(jnp.float32) * (turn / box_height)
    for d in range(grid_x):
        charge = blocks[d][...]
        atoms = charge.shape[1]
        lanes = pl.ds(d * atoms, atoms)
        ca, sa, cb, sb = ca_ref[:, lanes], sa_ref[:, lanes], cb_ref[:, lanes], sb_ref[:, lanes]
        bcc, bss, bsc, bcs = basis_rows(share, ca, sa, cb, sb)
        high, low = split(jnp.concatenate(bcc + bss + bsc + bcs + [ca, sa], axis=0))
        both = dot(t_both, high)
        pot = both[:wide] + both[wide:] + dot(t_high, low)
        proj = dot(row_pair, jnp.concatenate([charge, charge], axis=0))
        by_x = jnp.zeros((8, atoms), jnp.float32)
        by_y = jnp.zeros((8, atoms), jnp.float32)
        by_z = jnp.zeros((8, atoms), jnp.float32)
        for p in range(share):
            pcc, pss, psc, pcs = (
                proj[i * span + 8 * p : i * span + 8 * p + 8] for i in range(4)
            )
            slope = bcs[p] * pss - bsc[p] * pcc + bcc[p] * psc - bss[p] * pcs
            by_x = by_x + kx[p : p + 1] * slope
            by_y = by_y + ky[p : p + 1] * slope
            by_z = by_z + (bsc[p] * pss - bcs[p] * pcc - bss[p] * psc + bcc[p] * pcs)
        flat_slope = ca * proj[4 * span + padded :] - sa * proj[4 * span : 4 * span + padded]
        grad_x = jnp.sum(by_x, axis=0, keepdims=True) + jnp.sum(kx * flat_slope, axis=0, keepdims=True)
        grad_y = jnp.sum(by_y, axis=0, keepdims=True) + jnp.sum(ky * flat_slope, axis=0, keepdims=True)
        grad_z = jnp.sum(kz * by_z, axis=0, keepdims=True)
        zero = jnp.zeros((5, atoms), jnp.float32)
        outs[d][...] = jnp.concatenate([pot, grad_x, grad_y, grad_z, zero], axis=0)


def per_device(
    positions,
    species,
    neighbours,
    counts,
    species_embed,
    radial,
    mixing,
    read_hidden,
    read_out,
    charge_map,
    wavevectors,
):
    atoms = positions.shape[3]
    slots = neighbours.shape[3]
    features, lat_width = charge_map.shape
    wave_count = wavevectors.shape[1]
    grid = lax.axis_size("gx"), lax.axis_size("gy")
    grid_x, grid_y = grid
    edges = slots * atoms
    scale = 1.0 / math.sqrt(wave_count * lat_width * atoms * grid_x * grid_y)
    ids = neighbours[0, 0].T
    count = counts[0]
    embed = jnp.pad(species_embed, ((0, 8 - species_embed.shape[0]), (0, 0)))
    kinds = species[0].astype(F32)
    own = jnp.concatenate([positions[0, 0], kinds, jnp.zeros((4, atoms), F32)], axis=0)

    frame = [own if cell == CENTRE else shifted(own, *at) for cell, at in enumerate(OFFSETS)]
    row = {0: own, 1: frame[7], grid_x - 1: frame[1]}
    row = [row[d] if d in row else shifted(own, d, 0) for d in range(grid_x)]

    low, basis, slope, unit, sums_one, gate_one = run(
        functools.partial(first_kernel, slots),
        [
            shape(features, atoms, dtype=BF16),
            shape(8, edges),
            shape(8, edges),
            shape(8, edges),
            shape(3, features, atoms),
            shape(features, atoms),
        ],
        [ids, count, embed, radial, mixing] + frame,
        name="first",
    )
    hidden = [low if cell == CENTRE else shifted(low, *at) for cell, at in enumerate(OFFSETS)]

    share, padded, pair_np, wave_np = pair_tables(grid_x)
    place = jnp.stack([lax.axis_index("gx"), lax.axis_index("gy")]).astype(jnp.int32)
    pair_rows = lax.dynamic_index_in_dim(jnp.asarray(pair_np), place[0], 0, keepdims=False)
    wave_rows = lax.dynamic_index_in_dim(jnp.asarray(wave_np), place[0], 0, keepdims=False)
    span = grid_x * atoms
    *phases, weight = run(
        functools.partial(table_kernel, share, padded, grid),
        [
            shape(padded, span),
            shape(padded, span),
            shape(8, span),
            shape(8, span),
            shape(wave_np.shape[1], 128),
        ],
        [place, pair_rows, wave_rows, wavevectors] + row,
        smem=1,
        name="tables",
    )

    feature, sums_two, gate_two, low_charge, charge, energy, energy_slope = run(
        functools.partial(second_kernel, slots),
        [
            shape(features, edges, dtype=BF16),
            shape(3, features, atoms),
            shape(features, atoms),
            shape(lat_width, atoms, dtype=BF16),
            shape(lat_width, atoms),
            shape(1, atoms),
            shape(features, atoms),
        ],
        [ids, basis, unit, radial, mixing, read_hidden, read_out[None, :], charge_map] + hidden,
        scratch=[pltpu.VMEM((features, 9 * atoms), BF16)],
        name="second",
    )
    charges = [low_charge] + [shifted(low_charge, d, 0) for d in range(1, grid_x)]
    rows = 32 * share + 2 * padded
    (part,) = run(
        functools.partial(structure_kernel, share, padded, grid_x),
        [shape(rows // 2, 2 * lat_width)],
        phases + charges,
        name="structure",
    )
    parts = [part] + [shifted(part, 0, d) for d in range(1, grid_y)]
    folds = run(
        functools.partial(fold_kernel, share, padded, grid),
        [shape(lat_width + 8, atoms)] * grid_x,
        phases + [weight, pair_rows] + charges + parts,
        name="fold",
    )
    folds = [folds[0]] + [shifted(folds[d], -d, 0) for d in range(1, grid_x)]

    site, long, edge, centre, *ghosts = run(
        functools.partial(second_back_kernel, slots, scale, grid_x),
        [shape(1, atoms), shape(8, atoms), shape(32, edges), shape(features, atoms)]
        + [shape(features, atoms, dtype=BF16)] * 8,
        [ids, basis, unit, radial, mixing, charge_map, feature, sums_two, gate_two, charge, energy,
         energy_slope] + folds,
        scratch=[pltpu.VMEM((2 * features, edges), BF16)],
        name="second_back",
    )
    around = [at for at in OFFSETS if at != (0, 0)]
    ghosts = [shifted(ghost, -a, -b) for ghost, (a, b) in zip(ghosts, around)]
    mine, *moves = run(
        functools.partial(first_back_kernel, slots),
        [shape(8, atoms)] * 9,
        [ids, basis, slope, unit, embed, radial, mixing, sums_one, gate_one, edge, long, centre]
        + ghosts,
        name="first_back",
    )
    for move, (a, b) in zip(moves, around):
        mine = mine + shifted(move, -a, -b)
    return (-mine[None, None, :3], site[None])


def solution(mesh):
    in_specs = (
        P("gx", "gy", None, None),
        P("gx", "gy", None),
        P("gx", "gy", None, None),
        P("gx", "gy", None),
        P(),
        P(),
        P(),
        P(),
        P(),
        P(),
        P(),
    )
    out_specs = (P("gx", "gy", None, None), P("gx", "gy", None))
    return jax.shard_map(
        per_device, mesh=mesh, in_specs=in_specs, out_specs=out_specs, check_vma=False
    )
```

time: 287 us -> 136 us (0.47); the launches traced: 283 us -> 135 us
  matrix products: 62.9 us -> 0 us
  other arithmetic: 61.7 us -> 0.88 us
  local copies, waits for them, and re-layouts: 55.6 us -> 10.8 us
  Pallas kernels: 6.87 us -> 23.3 us
  starting transfers between devices: 55.3 us -> 64.6 us
  waiting for transfers between devices: 38.1 us -> 34.6 us
    dot_general x28 -> x0, matrix products: 62.9 us -> none  [the longest x6 26.3 us: interact(): jnp.einsum('anc,xan->xac', weight_one * source, unit_vec, precision=highest)]
    scatter-add x3 -> x0, other arithmetic: 52.1 us -> none  [the longest x2 34.7 us: interact(): relative = src_pos[:, neighbour_ids] - own_pos[:, :, None]]
    gather x7 -> x0, local copies, waits for them, and re-layouts: 35 us -> none  [the longest x4 26 us: interact(): source = h_src[neighbour_ids]]
    pallas_call x3 -> x7, Pallas kernels: 6.87 us -> 23.3 us  [run(): pl.pallas_call(kernel, out_shape=outs, in_specs=specs, out_specs=jax.tree...]
    ppermute x40 -> x54, starting transfers between devices: 55.3 us -> 64.6 us  [shifted(): return lax.ppermute(block, ('gx', 'gy'), route)]
    add_any x8 -> x0, local copies, waits for them, and re-layouts: 6.63 us -> none  [the longest x2 3.87 us: interact(): msg_zero = jnp.sum(weight_zero * source, axis=1) * norm_factor]
    unnamed x122 -> x24, local copies, waits for them, and re-layouts: 3.41 us -> 8.35 us
    reduce_sum x3 -> x0, other arithmetic: 3.66 us -> none  [the longest x1 3.1 us: interact(): relative = src_pos[:, neighbour_ids] - own_pos[:, :, None]]
  transfers between devices with their start and end apart: 40 -> 54, of which waited for: 16 -> 21; matrix products, arithmetic and copies ran while one was open for 29% -> 3% of each run, Pallas kernels for 1% -> 5%
where the time goes in v2:
time: 136 us; the launch traced here: 135 us
  starting transfers between devices  64.6 us (47%)
  waiting for transfers between devices  34.6 us (25%)
  Pallas kernels  23.3 us (17%)
  local copies, waits for them, and re-layouts  10.8 us (8%)
    ppermute x54, starting transfers between devices, shifted(): return lax.ppermute(block, ('gx', 'gy'), route)  64.6 us
    ppermute x54, waiting for transfers between devices, shifted(): return lax.ppermute(block, ('gx', 'gy'), route)  34.6 us
    pallas_call x7, Pallas kernels, run(): pl.pallas_call(kernel, out_shape=outs, in_specs=specs, out_specs=jax.tree...  23.3 us
    unnamed x24, local copies, waits for them, and re-layouts  8.35 us
  transfers between devices with their start and end apart: 54, of which 21 were waited for; matrix products, arithmetic and copies ran while one was open for 3% of the time, Pallas kernels for 5%

profile of v2, /device:TPU:0, one launch (start us, length us, event | category | flops | bytes accessed | tf_op | source)
XLA Modules:
  0.0 135.0 jit_solution(9858282644366899728)
XLA Ops:
  0.6 0.7 convert_bitcast_fusion
  1.4 0.7 copy.23
  2.2 6.4 %collective-permute-start.7 = (f32[8,256]{1,0:T(8,128)S(1)}, f32[8,256]{1,0:T(8,128)S(1)}, u32[]{:S(2)}, u32[]{:S(2)}) collective-permute-start(f32[8,256]{1,0:T(8,128)S(1)} %maximum_maximum_fusion.refs_4_.refs_0_), channel_id=1, source_target_pairs={{5,0},{6,1},{7,2},{4,3},{9,4},{10,5},{11,6},{8,7},{13,8},{14,9},{1... | collective-permute-start | bytes 24584 | tf_op jit(solution)/shard_map/ppermute | solution.py:32
  8.6 0.8 collective-permute-start.6
  9.4 2.4 %collective-permute-start.4 = (f32[8,256]{1,0:T(8,128)S(1)}, f32[8,256]{1,0:T(8,128)S(1)}, u32[]{:S(2)}, u32[]{:S(2)}) collective-permute-start(f32[8,256]{1,0:T(8,128)S(1)} %maximum_maximum_fusion.refs_4_.refs_0_), channel_id=1, source_target_pairs={{1,0},{2,1},{3,2},{0,3},{5,4},{6,5},{7,6},{4,7},{9,8},{10,9},{11,1... | collective-permute-start | bytes 24584 | tf_op jit(solution)/shard_map/ppermute | solution.py:32
  11.8 2.7 %collective-permute-start.2 = (f32[8,256]{1,0:T(8,128)S(1)}, f32[8,256]{1,0:T(8,128)S(1)}, u32[]{:S(2)}, u32[]{:S(2)}) collective-permute-start(f32[8,256]{1,0:T(8,128)S(1)} %maximum_maximum_fusion.refs_4_.refs_0_), channel_id=1, source_target_pairs={{29,0},{30,1},{31,2},{28,3},{1,4},{2,5},{3,6},{0,7},{5,8},{6,9},{7... | collective-permute-start | bytes 24584 | tf_op jit(solution)/shard_map/ppermute | solution.py:32
  14.5 1.1 collective-permute-start.1
  15.6 0.7 pad.4.embed_ref
  16.3 0.7 copy.22
  17.6 1.8 %collective-permute-done.1.refs_1_.refs_7_ = f32[8,256]{1,0:T(8,128)S(1)} collective-permute-done((f32[8,256]{1,0:T(8,128)S(1)}, f32[8,256]{1,0:T(8,128)S(1)}, u32[]{:S(2)}, u32[]{:S(2)}) %collective-permute-start.1) | collective-permute-done | bytes 8224 | tf_op jit(solution)/shard_map/ppermute | solution.py:32
  19.3 2.9 %collective-permute-done.refs_0_ = f32[8,256]{1,0:T(8,128)S(1)} collective-permute-done((f32[8,256]{1,0:T(8,128)S(1)}, f32[8,256]{1,0:T(8,128)S(1)}, u32[]{:S(2)}, u32[]{:S(2)}) %collective-permute-start) | collective-permute-done | bytes 8224 | tf_op jit(solution)/shard_map/ppermute | solution.py:32
  22.2 0.9 copy-done
  23.2 0.7 copy-done.3
  24.6 2.0 %first.1 = (bf16[128,256]{1,0:T(8,128)(2,1)S(1)}, f32[8,3072]{1,0:T(8,128)S(1)}, f32[8,3072]{1,0:T(8,128)S(1)}, f32[8,3072]{1,0:T(8,128)S(1)}, f32[3,128,256]{2,1,0:T(8,128)S(1)}, /*index=5*/f32[128,256]{1,0:T(8,128)S(1)}) custom-call(s32[12,256]{1,0:T(8,128)S(1)} %bitcast.21, s32[1,256]{1,0:T(1,128)S(1)} %bitcast.25, f32[8,128]{1,0:T(8,128)S(1)} %pad.4.embed_ref, ...), custom_call_target="tpu_custom_call" | custom-call | flops 1000000 | bytes 1000000 | tf_op jit(solution)/shard_map/first/pallas_call | solution.py:41
  26.7 1.8 %collective-permute-start.13 = (bf16[128,256]{1,0:T(8,128)(2,1)S(1)}, bf16[128,256]{1,0:T(8,128)(2,1)S(1)}, u32[]{:S(2)}, u32[]{:S(2)}) collective-permute-start(bf16[128,256]{1,0:T(8,128)(2,1)S(1)} %get-tuple-element.54.refs_4_), channel_id=1, source_target_pairs={{7,0},{4,1},{5,2},{6,3},{11,4},{8,5},{9,6},{10,7},{15,8},{12,9},{1... | collective-permute-start | bytes 196616 | tf_op jit(solution)/shard_map/ppermute | solution.py:32
  28.5 1.4 %collective-permute-start.12 = (bf16[128,256]{1,0:T(8,128)(2,1)S(1)}, bf16[128,256]{1,0:T(8,128)(2,1)S(1)}, u32[]{:S(2)}, u32[]{:S(2)}) collective-permute-start(bf16[128,256]{1,0:T(8,128)(2,1)S(1)} %get-tuple-element.54.refs_4_), channel_id=1, source_target_pairs={{1,0},{2,1},{3,2},{0,3},{5,4},{6,5},{7,6},{4,7},{9,8},{10,9},{11,1... | collective-permute-start | bytes 196616 | tf_op jit(solution)/shard_map/ppermute | solution.py:32
  30.6 1.3 collective-permute-start.20
  31.9 1.1 collective-permute-start.10
  33.0 1.2 collective-permute-done.12.refs_5_
  34.2 0.9 collective-permute-start.9
  35.3 1.2 collective-permute-start.8
  36.4 0.9 dynamic-slice_bitcast_fusion.wave_ref
  37.4 0.8 copy.16.charge_ref
  38.3 0.9 collective-permute-start.18
  39.8 1.4 %collective-permute-start.17 = (f32[8,256]{1,0:T(8,128)S(1)}, f32[8,256]{1,0:T(8,128)S(1)}, u32[]{:S(2)}, u32[]{:S(2)}) collective-permute-start(f32[8,256]{1,0:T(8,128)S(1)} %maximum_maximum_fusion.refs_4_.refs_0_), channel_id=1, source_target_pairs={{12,0},{13,1},{14,2},{15,3},{16,4},{17,5},{18,6},{19,7},{20,8},{21... | collective-permute-start | bytes 24584 | tf_op jit(solution)/shard_map/ppermute | solution.py:32
  41.2 1.4 %collective-permute-done.8.refs_0_ = bf16[128,256]{1,0:T(8,128)(2,1)S(1)} collective-permute-done((bf16[128,256]{1,0:T(8,128)(2,1)S(1)}, bf16[128,256]{1,0:T(8,128)(2,1)S(1)}, u32[]{:S(2)}, u32[]{:S(2)}) %collective-permute-start.8) | collective-permute-done | bytes 65568 | tf_op jit(solution)/shard_map/ppermute | solution.py:32
  42.6 1.2 collective-permute-start.16
  43.8 0.9 copy-done.1
  44.7 0.7 copy-done.4
  45.5 0.8 copy-done.6
  47.0 4.6 %second.1 = (bf16[128,3072]{1,0:T(8,128)(2,1)S(1)}, f32[3,128,256]{2,1,0:T(8,128)S(1)}, f32[128,256]{1,0:T(8,128)S(1)}, bf16[64,256]{1,0:T(8,128)(2,1)S(1)}, f32...) custom-call(s32[12,256]{1,0:T(8,128)S(1)} %bitcast.22, ...), custom_call_target="tpu_custom_call" | custom-call | flops 1000000 | bytes 1000000 | tf_op jit(solution)/shard_map/second/pallas_call | solution.py:41
  51.6 0.9 collective-permute-start.26
  52.5 0.7 dynamic-slice_bitcast_fusion.1.pair_ref.refs_5_
  53.2 3.8 %collective-permute-start.24 = (bf16[64,256]{1,0:T(8,128)(2,1)S(1)}, bf16[64,256]{1,0:T(8,128)(2,1)S(1)}, u32[]{:S(2)}, u32[]{:S(2)}) collective-permute-start(bf16[64,256]{1,0:T(8,128)(2,1)S(1)} %get-tuple-element.66.refs_4_.refs_6_), channel_id=1, source_target_pairs={{16,0},{17,1},{18,2},{19,3},{20,4},{21,5},{22,6},{23,7},{24,8},{25... | collective-permute-start | bytes 98312 | tf_op jit(solution)/shard_map/ppermute | solution.py:32
  57.0 2.2 %collective-permute-start.22 = (bf16[64,256]{1,0:T(8,128)(2,1)S(1)}, bf16[64,256]{1,0:T(8,128)(2,1)S(1)}, u32[]{:S(2)}, u32[]{:S(2)}) collective-permute-start(bf16[64,256]{1,0:T(8,128)(2,1)S(1)} %get-tuple-element.66.refs_4_.refs_6_), channel_id=1, source_target_pairs={{8,0},{9,1},{10,2},{11,3},{12,4},{13,5},{14,6},{15,7},{16,8},{17,9... | collective-permute-start | bytes 98312 | tf_op jit(solution)/shard_map/ppermute | solution.py:32
  59.7 2.3 %tables.1 = (f32[24,2048]{1,0:T(8,128)S(1)}, f32[24,2048]{1,0:T(8,128)S(1)}, f32[8,2048]{1,0:T(8,128)S(1)}, f32[8,2048]{1,0:T(8,128)S(1)}, f32[312,128]{1,0:T(8,128)S(1)}) custom-call(s32[2]{0:T(128)S(1)} %pad_add_fusion.pos_ref, f32[24,8]{1,0:T(8,128)S(1)} %dynamic-slice_bitcast_fusion.1.pair_ref.refs_5_, f32[312,8]{1,0:T(8,128)S(1)} %dynamic-slice_bitcast_fusion.wave_ref, ...), custom_call_target="tpu_custom_call" | custom-call | flops 1000000 | bytes 1000000 | tf_op jit(solution)/shard_map/tables/pallas_call | solution.py:41
  62.1 1.5 %structure.1.refs_14_ = f32[312,128]{1,0:T(8,128)S(1)} custom-call(f32[24,2048]{1,0:T(8,128)S(1)} %get-tuple-element.61.refs_0_, f32[24,2048]{1,0:T(8,128)S(1)} %get-tuple-element.62.refs_1_, f32[8,2048]{1,0:T(8,128)S(1)} %get-tuple-element.63.refs_2_, f32[8,2048]{1,0:T(8,128)S(1)} %get-tuple-element.64.refs_3_, ...), custom_call_target="tpu_custom_call" | custom-call | flops 1000000 | bytes 1000000 | tf_op jit(solution)/shard_map/structure/pallas_call | solution.py:41
  63.6 1.6 %collective-permute-start.30 = (f32[312,128]{1,0:T(8,128)S(1)}, f32[312,128]{1,0:T(8,128)S(1)}, u32[]{:S(2)}, u32[]{:S(2)}) collective-permute-start(f32[312,128]{1,0:T(8,128)S(1)} %structure.1.refs_14_), channel_id=1, source_target_pairs={{3,0},{0,1},{1,2},{2,3},{7,4},{4,5},{5,6},{6,7},{11,8},{8,9},{9,10... | collective-permute-start | bytes 479240 | tf_op jit(solution)/shard_map/ppermute | solution.py:32
  65.8 2.3 %collective-permute-start.28 = (f32[312,128]{1,0:T(8,128)S(1)}, f32[312,128]{1,0:T(8,128)S(1)}, u32[]{:S(2)}, u32[]{:S(2)}) collective-permute-start(f32[312,128]{1,0:T(8,128)S(1)} %structure.1.refs_14_), channel_id=1, source_target_pairs={{1,0},{2,1},{3,2},{0,3},{5,4},{6,5},{7,6},{4,7},{9,8},{10,9},{11,1... | collective-permute-start | bytes 479240 | tf_op jit(solution)/shard_map/ppermute | solution.py:32
  68.1 3.5 %collective-permute-done.30.refs_17_ = f32[312,128]{1,0:T(8,128)S(1)} collective-permute-done((f32[312,128]{1,0:T(8,128)S(1)}, f32[312,128]{1,0:T(8,128)S(1)}, u32[]{:S(2)}, u32[]{:S(2)}) %collective-permute-start.30) | collective-permute-done | bytes 159776 | tf_op jit(solution)/shard_map/ppermute | solution.py:32
  71.6 3.1 %collective-permute-done.29.refs_16_ = f32[312,128]{1,0:T(8,128)S(1)} collective-permute-done((f32[312,128]{1,0:T(8,128)S(1)}, f32[312,128]{1,0:T(8,128)S(1)}, u32[]{:S(2)}, u32[]{:S(2)}) %collective-permute-start.29) | collective-permute-done | bytes 159776 | tf_op jit(solution)/shard_map/ppermute | solution.py:32
  74.7 2.4 %fold.1 = (f32[72,256]{1,0:T(8,128)S(1)}, f32[72,256]{1,0:T(8,128)S(1)}, f32[72,256]{1,0:T(8,128)S(1)}, f32[72,256]{1,0:T(8,128)S(1)}, f32[72,256]{1,0:T(8,128)S...) custom-call(f32[24,2048]{1,0:T(8,128)S(1)} %get-tuple-element.61.refs_0_, ...), custom_call_target="tpu_custom_call" | custom-call | flops 1000000 | bytes 1000000 | tf_op jit(solution)/shard_map/fold/pallas_call | solution.py:41
  77.3 1.5 %collective-permute-start.32 = (f32[72,256]{1,0:T(8,128)S(1)}, f32[72,256]{1,0:T(8,128)S(1)}, u32[]{:S(2)}, u32[]{:S(2)}) collective-permute-start(f32[72,256]{1,0:T(8,128)S(1)} %get-tuple-element.69), channel_id=1, source_target_pairs={{24,0},{25,1},{26,2},{27,3},{28,4},{29,5},{30,6},{31,7},{0,8},{1,9... | collective-permute-start | bytes 221192 | tf_op jit(solution)/shard_map/ppermute | solution.py:32
  78.8 1.4 %collective-permute-start.33 = (f32[72,256]{1,0:T(8,128)S(1)}, f32[72,256]{1,0:T(8,128)S(1)}, u32[]{:S(2)}, u32[]{:S(2)}) collective-permute-start(f32[72,256]{1,0:T(8,128)S(1)} %get-tuple-element.70), channel_id=1, source_target_pairs={{20,0},{21,1},{22,2},{23,3},{24,4},{25,5},{26,6},{27,7},{28,8},{29... | collective-permute-start | bytes 221192 | tf_op jit(solution)/shard_map/ppermute | solution.py:32
  80.2 2.3 %collective-permute-start.34 = (f32[72,256]{1,0:T(8,128)S(1)}, f32[72,256]{1,0:T(8,128)S(1)}, u32[]{:S(2)}, u32[]{:S(2)}) collective-permute-start(f32[72,256]{1,0:T(8,128)S(1)} %get-tuple-element.71), channel_id=1, source_target_pairs={{16,0},{17,1},{18,2},{19,3},{20,4},{21,5},{22,6},{23,7},{24,8},{25... | collective-permute-start | bytes 221192 | tf_op jit(solution)/shard_map/ppermute | solution.py:32
  83.0 1.7 %collective-permute-start.36 = (f32[72,256]{1,0:T(8,128)S(1)}, f32[72,256]{1,0:T(8,128)S(1)}, u32[]{:S(2)}, u32[]{:S(2)}) collective-permute-start(f32[72,256]{1,0:T(8,128)S(1)} %get-tuple-element.73), channel_id=1, source_target_pairs={{8,0},{9,1},{10,2},{11,3},{12,4},{13,5},{14,6},{15,7},{16,8},{17,9... | collective-permute-start | bytes 221192 | tf_op jit(solution)/shard_map/ppermute | solution.py:32
  85.3 4.7 %collective-permute-done.33.refs_3_ = f32[72,256]{1,0:T(8,128)S(1)} collective-permute-done((f32[72,256]{1,0:T(8,128)S(1)}, f32[72,256]{1,0:T(8,128)S(1)}, u32[]{:S(2)}, u32[]{:S(2)}) %collective-permute-start.33) | collective-permute-done | bytes 73760 | tf_op jit(solution)/shard_map/ppermute | solution.py:32
  90.1 7.0 %second_back.1 = (f32[1,256]{1,0:T(1,128)}, f32[8,256]{1,0:T(8,128)S(1)}, f32[32,3072]{1,0:T(8,128)S(1)}, f32[128,256]{1,0:T(8,128)S(1)}, bf16[128,256]{1,0:T(8,...) custom-call(s32[12,256]{1,0:T(8,128)S(1)} %bitcast.23, ...), custom_call_target="tpu_custom_call" | custom-call | flops 1000000 | bytes 1000000 | tf_op jit(solution)/shard_map/second_back/pallas_call | solution.py:41
  97.1 5.7 %collective-permute-start.38 = (bf16[128,256]{1,0:T(8,128)(2,1)S(1)}, bf16[128,256]{1,0:T(8,128)(2,1)S(1)}, u32[]{:S(2)}, u32[]{:S(2)}) collective-permute-start(bf16[128,256]{1,0:T(8,128)(2,1)S(1)} %get-tuple-element.78), channel_id=1, source_target_pairs={{5,0},{6,1},{7,2},{4,3},{9,4},{10,5},{11,6},{8,7},{13,8},{14,9},{1... | collective-permute-start | bytes 196616 | tf_op jit(solution)/shard_map/ppermute | solution.py:32
  103.3 2.5 %collective-permute-start.41 = (bf16[128,256]{1,0:T(8,128)(2,1)S(1)}, bf16[128,256]{1,0:T(8,128)(2,1)S(1)}, u32[]{:S(2)}, u32[]{:S(2)}) collective-permute-start(bf16[128,256]{1,0:T(8,128)(2,1)S(1)} %get-tuple-element.81), channel_id=1, source_target_pairs={{1,0},{2,1},{3,2},{0,3},{5,4},{6,5},{7,6},{4,7},{9,8},{10,9},{11,1... | collective-permute-start | bytes 196616 | tf_op jit(solution)/shard_map/ppermute | solution.py:32
  105.8 2.1 %collective-permute-start.43 = (bf16[128,256]{1,0:T(8,128)(2,1)S(1)}, bf16[128,256]{1,0:T(8,128)(2,1)S(1)}, u32[]{:S(2)}, u32[]{:S(2)}) collective-permute-start(bf16[128,256]{1,0:T(8,128)(2,1)S(1)} %get-tuple-element.83), channel_id=1, source_target_pairs={{29,0},{30,1},{31,2},{28,3},{1,4},{2,5},{3,6},{0,7},{5,8},{6,9},{7... | collective-permute-start | bytes 196616 | tf_op jit(solution)/shard_map/ppermute | solution.py:32
  107.9 1.9 %collective-permute-start.44 = (bf16[128,256]{1,0:T(8,128)(2,1)S(1)}, bf16[128,256]{1,0:T(8,128)(2,1)S(1)}, u32[]{:S(2)}, u32[]{:S(2)}) collective-permute-start(bf16[128,256]{1,0:T(8,128)(2,1)S(1)} %get-tuple-element.84), channel_id=1, source_target_pairs={{28,0},{29,1},{30,2},{31,3},{0,4},{1,5},{2,6},{3,7},{4,8},{5,9},{6... | collective-permute-start | bytes 196616 | tf_op jit(solution)/shard_map/ppermute | solution.py:32
  109.8 1.2 collective-permute-done.42.refs_4_
  111.0 1.2 collective-permute-done.43.refs_5_
  112.2 2.2 %collective-permute-done.44.refs_6_ = bf16[128,256]{1,0:T(8,128)(2,1)S(1)} collective-permute-done((bf16[128,256]{1,0:T(8,128)(2,1)S(1)}, bf16[128,256]{1,0:T(8,128)(2,1)S(1)}, u32[]{:S(2)}, u32[]{:S(2)}) %collective-permute-start.44) | collective-permute-done | bytes 65568 | tf_op jit(solution)/shard_map/ppermute | solution.py:32
  114.4 2.7 %collective-permute-done.45.refs_7_ = bf16[128,256]{1,0:T(8,128)(2,1)S(1)} collective-permute-done((bf16[128,256]{1,0:T(8,128)(2,1)S(1)}, bf16[128,256]{1,0:T(8,128)(2,1)S(1)}, u32[]{:S(2)}, u32[]{:S(2)}) %collective-permute-start.45) | collective-permute-done | bytes 65568 | tf_op jit(solution)/shard_map/ppermute | solution.py:32
  117.1 3.5 %first_back.1 = (f32[8,256]{1,0:T(8,128)S(1)}, f32[8,256]{1,0:T(8,128)S(1)}, f32[8,256]{1,0:T(8,128)S(1)}, f32[8,256]{1,0:T(8,128)S(1)}, f32[8,256]{1,0:T(8,128)...) custom-call(s32[12,256]{1,0:T(8,128)S(1)} %bitcast.24, ...), custom_call_target="tpu_custom_call" | custom-call | flops 1000000 | bytes 1000000 | tf_op jit(solution)/shard_map/first_back/pallas_call | solution.py:41
  120.8 1.6 %collective-permute-start.48 = (f32[8,256]{1,0:T(8,128)S(1)}, f32[8,256]{1,0:T(8,128)S(1)}, u32[]{:S(2)}, u32[]{:S(2)}) collective-permute-start(f32[8,256]{1,0:T(8,128)S(1)} %get-tuple-element.89), channel_id=1, source_target_pairs={{7,0},{4,1},{5,2},{6,3},{11,4},{8,5},{9,6},{10,7},{15,8},{12,9},{1... | collective-permute-start | bytes 24584 | tf_op jit(solution)/shard_map/ppermute | solution.py:32
  122.5 1.4 %collective-permute-start.49 = (f32[8,256]{1,0:T(8,128)S(1)}, f32[8,256]{1,0:T(8,128)S(1)}, u32[]{:S(2)}, u32[]{:S(2)}) collective-permute-start(f32[8,256]{1,0:T(8,128)S(1)} %get-tuple-element.90), channel_id=1, source_target_pairs={{1,0},{2,1},{3,2},{0,3},{5,4},{6,5},{7,6},{4,7},{9,8},{10,9},{11,1... | collective-permute-start | bytes 24584 | tf_op jit(solution)/shard_map/ppermute | solution.py:32
  124.5 1.3 collective-permute-start.51
  125.8 1.9 %collective-permute-start.52 = (f32[8,256]{1,0:T(8,128)S(1)}, f32[8,256]{1,0:T(8,128)S(1)}, u32[]{:S(2)}, u32[]{:S(2)}) collective-permute-start(f32[8,256]{1,0:T(8,128)S(1)} %get-tuple-element.93), channel_id=1, source_target_pairs={{28,0},{29,1},{30,2},{31,3},{0,4},{1,5},{2,6},{3,7},{4,8},{5,9},{6... | collective-permute-start | bytes 24584 | tf_op jit(solution)/shard_map/ppermute | solution.py:32
  128.4 1.9 %collective-permute-done.51 = f32[8,256]{1,0:T(8,128)S(1)} collective-permute-done((f32[8,256]{1,0:T(8,128)S(1)}, f32[8,256]{1,0:T(8,128)S(1)}, u32[]{:S(2)}, u32[]{:S(2)}) %collective-permute-start.51) | collective-permute-done | bytes 8224 | tf_op jit(solution)/shard_map/ppermute | solution.py:32
  130.3 0.9 collective-permute-done.52
  131.1 3.3 %collective-permute-done.53 = f32[8,256]{1,0:T(8,128)S(1)} collective-permute-done((f32[8,256]{1,0:T(8,128)S(1)}, f32[8,256]{1,0:T(8,128)S(1)}, u32[]{:S(2)}, u32[]{:S(2)}) %collective-permute-start.53) | collective-permute-done | bytes 8224 | tf_op jit(solution)/shard_map/ppermute | solution.py:32
  (85 shorter events, 9.1 us)
Async XLA Ops:
  0.6 59.1 %copy-start.7 = (s32[3,4096]{1,0:T(4,128)S(1)}, s32[3,4096]{1,0:T(4,128)}, u32[]{:S(2)}) copy-start(s32[3,4096]{1,0:T(4,128)} %vec_ref.1) | copy-start | bytes 147460
  2.2 9.6 %collective-permute-start.7 = (f32[8,256]{1,0:T(8,128)S(1)}, f32[8,256]{1,0:T(8,128)S(1)}, u32[]{:S(2)}, u32[]{:S(2)}) collective-permute-start(f32[8,256]{1,0:T(8,128)S(1)} %maximum_maximum_fusion.refs_4_.refs_0_), channel_id=1, source_target_pairs={{5,0},{6,1},{7,2},{4,3},{9,4},{10,5},{11,6},{8,7},{13,8},{14,9},{1... | collective-permute-start | bytes 24584 | tf_op jit(solution)/shard_map/ppermute | solution.py:32
  8.6 5.9 %collective-permute-start.6 = (f32[8,256]{1,0:T(8,128)S(1)}, f32[8,256]{1,0:T(8,128)S(1)}, u32[]{:S(2)}, u32[]{:S(2)}) collective-permute-start(f32[8,256]{1,0:T(8,128)S(1)} %maximum_maximum_fusion.refs_4_.refs_0_), channel_id=1, source_target_pairs={{4,0},{5,1},{6,2},{7,3},{8,4},{9,5},{10,6},{11,7},{12,8},{13,9},{1... | collective-permute-start | bytes 24584 | tf_op jit(solution)/shard_map/ppermute | solution.py:32
  9.4 6.1 %collective-permute-start.5 = (f32[8,256]{1,0:T(8,128)S(1)}, f32[8,256]{1,0:T(8,128)S(1)}, u32[]{:S(2)}, u32[]{:S(2)}) collective-permute-start(f32[8,256]{1,0:T(8,128)S(1)} %maximum_maximum_fusion.refs_4_.refs_0_), channel_id=1, source_target_pairs={{7,0},{4,1},{5,2},{6,3},{11,4},{8,5},{9,6},{10,7},{15,8},{12,9},{1... | collective-permute-start | bytes 24584 | tf_op jit(solution)/shard_map/ppermute | solution.py:32
  9.4 7.6 %collective-permute-start.4 = (f32[8,256]{1,0:T(8,128)S(1)}, f32[8,256]{1,0:T(8,128)S(1)}, u32[]{:S(2)}, u32[]{:S(2)}) collective-permute-start(f32[8,256]{1,0:T(8,128)S(1)} %maximum_maximum_fusion.refs_4_.refs_0_), channel_id=1, source_target_pairs={{1,0},{2,1},{3,2},{0,3},{5,4},{6,5},{7,6},{4,7},{9,8},{10,9},{11,1... | collective-permute-start | bytes 24584 | tf_op jit(solution)/shard_map/ppermute | solution.py:32
  11.8 5.2 %collective-permute-start.3 = (f32[8,256]{1,0:T(8,128)S(1)}, f32[8,256]{1,0:T(8,128)S(1)}, u32[]{:S(2)}, u32[]{:S(2)}) collective-permute-start(f32[8,256]{1,0:T(8,128)S(1)} %maximum_maximum_fusion.refs_4_.refs_0_), channel_id=1, source_target_pairs={{3,0},{0,1},{1,2},{2,3},{7,4},{4,5},{5,6},{6,7},{11,8},{8,9},{9,10... | collective-permute-start | bytes 24584 | tf_op jit(solution)/shard_map/ppermute | solution.py:32
  11.8 5.8 %collective-permute-start.2 = (f32[8,256]{1,0:T(8,128)S(1)}, f32[8,256]{1,0:T(8,128)S(1)}, u32[]{:S(2)}, u32[]{:S(2)}) collective-permute-start(f32[8,256]{1,0:T(8,128)S(1)} %maximum_maximum_fusion.refs_4_.refs_0_), channel_id=1, source_target_pairs={{29,0},{30,1},{31,2},{28,3},{1,4},{2,5},{3,6},{0,7},{5,8},{6,9},{7... | collective-permute-start | bytes 24584 | tf_op jit(solution)/shard_map/ppermute | solution.py:32
  14.5 4.9 %collective-permute-start.1 = (f32[8,256]{1,0:T(8,128)S(1)}, f32[8,256]{1,0:T(8,128)S(1)}, u32[]{:S(2)}, u32[]{:S(2)}) collective-permute-start(f32[8,256]{1,0:T(8,128)S(1)} %maximum_maximum_fusion.refs_4_.refs_0_), channel_id=1, source_target_pairs={{28,0},{29,1},{30,2},{31,3},{0,4},{1,5},{2,6},{3,7},{4,8},{5,9},{6... | collective-permute-start | bytes 24584 | tf_op jit(solution)/shard_map/ppermute | solution.py:32
  15.6 6.7 %collective-permute-start = (f32[8,256]{1,0:T(8,128)S(1)}, f32[8,256]{1,0:T(8,128)S(1)}, u32[]{:S(2)}, u32[]{:S(2)}) collective-permute-start(f32[8,256]{1,0:T(8,128)S(1)} %maximum_maximum_fusion.refs_4_.refs_0_), channel_id=1, source_target_pairs={{31,0},{28,1},{29,2},{30,3},{3,4},{0,5},{1,6},{2,7},{7,8},{4,9},{5... | collective-permute-start | bytes 24584 | tf_op jit(solution)/shard_map/ppermute | solution.py:32
  22.2 1.0 copy-start
  23.2 0.7 copy-start.3
  23.9 0.7 copy-start.8
  26.6 4.0 %collective-permute-start.15 = (bf16[128,256]{1,0:T(8,128)(2,1)S(1)}, bf16[128,256]{1,0:T(8,128)(2,1)S(1)}, u32[]{:S(2)}, u32[]{:S(2)}) collective-permute-start(bf16[128,256]{1,0:T(8,128)(2,1)S(1)} %get-tuple-element.54.refs_4_), channel_id=1, source_target_pairs={{5,0},{6,1},{7,2},{4,3},{9,4},{10,5},{11,6},{8,7},{13,8},{14,9},{1... | collective-permute-start | bytes 196616 | tf_op jit(solution)/shard_map/ppermute | solution.py:32
  26.7 5.1 %collective-permute-start.14 = (bf16[128,256]{1,0:T(8,128)(2,1)S(1)}, bf16[128,256]{1,0:T(8,128)(2,1)S(1)}, u32[]{:S(2)}, u32[]{:S(2)}) collective-permute-start(bf16[128,256]{1,0:T(8,128)(2,1)S(1)} %get-tuple-element.54.refs_4_), channel_id=1, source_target_pairs={{4,0},{5,1},{6,2},{7,3},{8,4},{9,5},{10,6},{11,7},{12,8},{13,9},{1... | collective-permute-start | bytes 196616 | tf_op jit(solution)/shard_map/ppermute | solution.py:32
  26.7 5.1 %collective-permute-start.13 = (bf16[128,256]{1,0:T(8,128)(2,1)S(1)}, bf16[128,256]{1,0:T(8,128)(2,1)S(1)}, u32[]{:S(2)}, u32[]{:S(2)}) collective-permute-start(bf16[128,256]{1,0:T(8,128)(2,1)S(1)} %get-tuple-element.54.refs_4_), channel_id=1, source_target_pairs={{7,0},{4,1},{5,2},{6,3},{11,4},{8,5},{9,6},{10,7},{15,8},{12,9},{1... | collective-permute-start | bytes 196616 | tf_op jit(solution)/shard_map/ppermute | solution.py:32
  28.5 5.7 %collective-permute-start.12 = (bf16[128,256]{1,0:T(8,128)(2,1)S(1)}, bf16[128,256]{1,0:T(8,128)(2,1)S(1)}, u32[]{:S(2)}, u32[]{:S(2)}) collective-permute-start(bf16[128,256]{1,0:T(8,128)(2,1)S(1)} %get-tuple-element.54.refs_4_), channel_id=1, source_target_pairs={{1,0},{2,1},{3,2},{0,3},{5,4},{6,5},{7,6},{4,7},{9,8},{10,9},{11,1... | collective-permute-start | bytes 196616 | tf_op jit(solution)/shard_map/ppermute | solution.py:32
  29.9 5.3 %collective-permute-start.11 = (bf16[128,256]{1,0:T(8,128)(2,1)S(1)}, bf16[128,256]{1,0:T(8,128)(2,1)S(1)}, u32[]{:S(2)}, u32[]{:S(2)}) collective-permute-start(bf16[128,256]{1,0:T(8,128)(2,1)S(1)} %get-tuple-element.54.refs_4_), channel_id=1, source_target_pairs={{3,0},{0,1},{1,2},{2,3},{7,4},{4,5},{5,6},{6,7},{11,8},{8,9},{9,10... | collective-permute-start | bytes 196616 | tf_op jit(solution)/shard_map/ppermute | solution.py:32
  30.6 21.0 %collective-permute-start.20 = (f32[8,256]{1,0:T(8,128)S(1)}, f32[8,256]{1,0:T(8,128)S(1)}, u32[]{:S(2)}, u32[]{:S(2)}) collective-permute-start(f32[8,256]{1,0:T(8,128)S(1)} %maximum_maximum_fusion.refs_4_.refs_0_), channel_id=1, source_target_pairs={{24,0},{25,1},{26,2},{27,3},{28,4},{29,5},{30,6},{31,7},{0,8},{1,9... | collective-permute-start | bytes 24584 | tf_op jit(solution)/shard_map/ppermute | solution.py:32
  31.9 19.8 %collective-permute-start.19 = (f32[8,256]{1,0:T(8,128)S(1)}, f32[8,256]{1,0:T(8,128)S(1)}, u32[]{:S(2)}, u32[]{:S(2)}) collective-permute-start(f32[8,256]{1,0:T(8,128)S(1)} %maximum_maximum_fusion.refs_4_.refs_0_), channel_id=1, source_target_pairs={{20,0},{21,1},{22,2},{23,3},{24,4},{25,5},{26,6},{27,7},{28,8},{29... | collective-permute-start | bytes 24584 | tf_op jit(solution)/shard_map/ppermute | solution.py:32
  31.9 6.4 %collective-permute-start.10 = (bf16[128,256]{1,0:T(8,128)(2,1)S(1)}, bf16[128,256]{1,0:T(8,128)(2,1)S(1)}, u32[]{:S(2)}, u32[]{:S(2)}) collective-permute-start(bf16[128,256]{1,0:T(8,128)(2,1)S(1)} %get-tuple-element.54.refs_4_), channel_id=1, source_target_pairs={{29,0},{30,1},{31,2},{28,3},{1,4},{2,5},{3,6},{0,7},{5,8},{6,9},{7... | collective-permute-start | bytes 196616 | tf_op jit(solution)/shard_map/ppermute | solution.py:32
  34.2 5.7 %collective-permute-start.9 = (bf16[128,256]{1,0:T(8,128)(2,1)S(1)}, bf16[128,256]{1,0:T(8,128)(2,1)S(1)}, u32[]{:S(2)}, u32[]{:S(2)}) collective-permute-start(bf16[128,256]{1,0:T(8,128)(2,1)S(1)} %get-tuple-element.54.refs_4_), channel_id=1, source_target_pairs={{28,0},{29,1},{30,2},{31,3},{0,4},{1,5},{2,6},{3,7},{4,8},{5,9},{6... | collective-permute-start | bytes 196616 | tf_op jit(solution)/shard_map/ppermute | solution.py:32
  35.3 7.3 %collective-permute-start.8 = (bf16[128,256]{1,0:T(8,128)(2,1)S(1)}, bf16[128,256]{1,0:T(8,128)(2,1)S(1)}, u32[]{:S(2)}, u32[]{:S(2)}) collective-permute-start(bf16[128,256]{1,0:T(8,128)(2,1)S(1)} %get-tuple-element.54.refs_4_), channel_id=1, source_target_pairs={{31,0},{28,1},{29,2},{30,3},{3,4},{0,5},{1,6},{2,7},{7,8},{4,9},{5... | collective-permute-start | bytes 196616 | tf_op jit(solution)/shard_map/ppermute | solution.py:32
  38.3 14.9 %collective-permute-start.18 = (f32[8,256]{1,0:T(8,128)S(1)}, f32[8,256]{1,0:T(8,128)S(1)}, u32[]{:S(2)}, u32[]{:S(2)}) collective-permute-start(f32[8,256]{1,0:T(8,128)S(1)} %maximum_maximum_fusion.refs_4_.refs_0_), channel_id=1, source_target_pairs={{16,0},{17,1},{18,2},{19,3},{20,4},{21,5},{22,6},{23,7},{24,8},{25... | collective-permute-start | bytes 24584 | tf_op jit(solution)/shard_map/ppermute | solution.py:32
  39.8 13.4 %collective-permute-start.17 = (f32[8,256]{1,0:T(8,128)S(1)}, f32[8,256]{1,0:T(8,128)S(1)}, u32[]{:S(2)}, u32[]{:S(2)}) collective-permute-start(f32[8,256]{1,0:T(8,128)S(1)} %maximum_maximum_fusion.refs_4_.refs_0_), channel_id=1, source_target_pairs={{12,0},{13,1},{14,2},{15,3},{16,4},{17,5},{18,6},{19,7},{20,8},{21... | collective-permute-start | bytes 24584 | tf_op jit(solution)/shard_map/ppermute | solution.py:32
  42.6 14.4 %collective-permute-start.16 = (f32[8,256]{1,0:T(8,128)S(1)}, f32[8,256]{1,0:T(8,128)S(1)}, u32[]{:S(2)}, u32[]{:S(2)}) collective-permute-start(f32[8,256]{1,0:T(8,128)S(1)} %maximum_maximum_fusion.refs_4_.refs_0_), channel_id=1, source_target_pairs={{8,0},{9,1},{10,2},{11,3},{12,4},{13,5},{14,6},{15,7},{16,8},{17,9... | collective-permute-start | bytes 24584 | tf_op jit(solution)/shard_map/ppermute | solution.py:32
  43.8 0.9 copy-start.1
  44.7 0.7 copy-start.4
  45.5 0.8 copy-start.6
  46.3 0.7 copy-start.9
  51.6 5.4 %collective-permute-start.27 = (bf16[64,256]{1,0:T(8,128)(2,1)S(1)}, bf16[64,256]{1,0:T(8,128)(2,1)S(1)}, u32[]{:S(2)}, u32[]{:S(2)}) collective-permute-start(bf16[64,256]{1,0:T(8,128)(2,1)S(1)} %get-tuple-element.66.refs_4_.refs_6_), channel_id=1, source_target_pairs={{28,0},{29,1},{30,2},{31,3},{0,4},{1,5},{2,6},{3,7},{4,8},{5,9},{6... | collective-permute-start | bytes 98312 | tf_op jit(solution)/shard_map/ppermute | solution.py:32
  51.6 7.5 %collective-permute-start.26 = (bf16[64,256]{1,0:T(8,128)(2,1)S(1)}, bf16[64,256]{1,0:T(8,128)(2,1)S(1)}, u32[]{:S(2)}, u32[]{:S(2)}) collective-permute-start(bf16[64,256]{1,0:T(8,128)(2,1)S(1)} %get-tuple-element.66.refs_4_.refs_6_), channel_id=1, source_target_pairs={{24,0},{25,1},{26,2},{27,3},{28,4},{29,5},{30,6},{31,7},{0,8},{1,9... | collective-permute-start | bytes 98312 | tf_op jit(solution)/shard_map/ppermute | solution.py:32
  53.2 8.8 %collective-permute-start.25 = (bf16[64,256]{1,0:T(8,128)(2,1)S(1)}, bf16[64,256]{1,0:T(8,128)(2,1)S(1)}, u32[]{:S(2)}, u32[]{:S(2)}) collective-permute-start(bf16[64,256]{1,0:T(8,128)(2,1)S(1)} %get-tuple-element.66.refs_4_.refs_6_), channel_id=1, source_target_pairs={{20,0},{21,1},{22,2},{23,3},{24,4},{25,5},{26,6},{27,7},{28,8},{29... | collective-permute-start | bytes 98312 | tf_op jit(solution)/shard_map/ppermute | solution.py:32
  53.2 8.8 %collective-permute-start.24 = (bf16[64,256]{1,0:T(8,128)(2,1)S(1)}, bf16[64,256]{1,0:T(8,128)(2,1)S(1)}, u32[]{:S(2)}, u32[]{:S(2)}) collective-permute-start(bf16[64,256]{1,0:T(8,128)(2,1)S(1)} %get-tuple-element.66.refs_4_.refs_6_), channel_id=1, source_target_pairs={{16,0},{17,1},{18,2},{19,3},{20,4},{21,5},{22,6},{23,7},{24,8},{25... | collective-permute-start | bytes 98312 | tf_op jit(solution)/shard_map/ppermute | solution.py:32
  57.0 5.0 %collective-permute-start.23 = (bf16[64,256]{1,0:T(8,128)(2,1)S(1)}, bf16[64,256]{1,0:T(8,128)(2,1)S(1)}, u32[]{:S(2)}, u32[]{:S(2)}) collective-permute-start(bf16[64,256]{1,0:T(8,128)(2,1)S(1)} %get-tuple-element.66.refs_4_.refs_6_), channel_id=1, source_target_pairs={{12,0},{13,1},{14,2},{15,3},{16,4},{17,5},{18,6},{19,7},{20,8},{21... | collective-permute-start | bytes 98312 | tf_op jit(solution)/shard_map/ppermute | solution.py:32
  57.0 5.0 %collective-permute-start.22 = (bf16[64,256]{1,0:T(8,128)(2,1)S(1)}, bf16[64,256]{1,0:T(8,128)(2,1)S(1)}, u32[]{:S(2)}, u32[]{:S(2)}) collective-permute-start(bf16[64,256]{1,0:T(8,128)(2,1)S(1)} %get-tuple-element.66.refs_4_.refs_6_), channel_id=1, source_target_pairs={{8,0},{9,1},{10,2},{11,3},{12,4},{13,5},{14,6},{15,7},{16,8},{17,9... | collective-permute-start | bytes 98312 | tf_op jit(solution)/shard_map/ppermute | solution.py:32
  59.2 2.9 %collective-permute-start.21 = (bf16[64,256]{1,0:T(8,128)(2,1)S(1)}, bf16[64,256]{1,0:T(8,128)(2,1)S(1)}, u32[]{:S(2)}, u32[]{:S(2)}) collective-permute-start(bf16[64,256]{1,0:T(8,128)(2,1)S(1)} %get-tuple-element.66.refs_4_.refs_6_), channel_id=1, source_target_pairs={{4,0},{5,1},{6,2},{7,3},{8,4},{9,5},{10,6},{11,7},{12,8},{13,9},{1... | collective-permute-start | bytes 98312 | tf_op jit(solution)/shard_map/ppermute | solution.py:32
  62.0 28.1 %copy-start.2 = (f32[2,2,128,128]{3,2,1,0:T(8,128)S(1)}, f32[2,2,128,128]{3,2,1,0:T(8,128)}, u32[]{:S(2)}) copy-start(f32[2,2,128,128]{3,2,1,0:T(8,128)} %mixing_ref.7) | copy-start | bytes 786436
  62.0 28.1 %copy-start.5 = (f32[2,2,8,128]{3,2,1,0:T(8,128)S(1)}, f32[2,2,8,128]{3,2,1,0:T(8,128)}, u32[]{:S(2)}) copy-start(f32[2,2,8,128]{3,2,1,0:T(8,128)} %radial_ref.7) | copy-start | bytes 49156
  63.6 8.0 %collective-permute-start.30 = (f32[312,128]{1,0:T(8,128)S(1)}, f32[312,128]{1,0:T(8,128)S(1)}, u32[]{:S(2)}, u32[]{:S(2)}) collective-permute-start(f32[312,128]{1,0:T(8,128)S(1)} %structure.1.refs_14_), channel_id=1, source_target_pairs={{3,0},{0,1},{1,2},{2,3},{7,4},{4,5},{5,6},{6,7},{11,8},{8,9},{9,10... | collective-permute-start | bytes 479240 | tf_op jit(solution)/shard_map/ppermute | solution.py:32
  65.2 9.5 %collective-permute-start.29 = (f32[312,128]{1,0:T(8,128)S(1)}, f32[312,128]{1,0:T(8,128)S(1)}, u32[]{:S(2)}, u32[]{:S(2)}) collective-permute-start(f32[312,128]{1,0:T(8,128)S(1)} %structure.1.refs_14_), channel_id=1, source_target_pairs={{2,0},{3,1},{0,2},{1,3},{6,4},{7,5},{4,6},{5,7},{10,8},{11,9},{8,1... | collective-permute-start | bytes 479240 | tf_op jit(solution)/shard_map/ppermute | solution.py:32
  65.8 8.9 %collective-permute-start.28 = (f32[312,128]{1,0:T(8,128)S(1)}, f32[312,128]{1,0:T(8,128)S(1)}, u32[]{:S(2)}, u32[]{:S(2)}) collective-permute-start(f32[312,128]{1,0:T(8,128)S(1)} %structure.1.refs_14_), channel_id=1, source_target_pairs={{1,0},{2,1},{3,2},{0,3},{5,4},{6,5},{7,6},{4,7},{9,8},{10,9},{11,1... | collective-permute-start | bytes 479240 | tf_op jit(solution)/shard_map/ppermute | solution.py:32
  77.2 5.8 %collective-permute-start.31 = (f32[72,256]{1,0:T(8,128)S(1)}, f32[72,256]{1,0:T(8,128)S(1)}, u32[]{:S(2)}, u32[]{:S(2)}) collective-permute-start(f32[72,256]{1,0:T(8,128)S(1)} %get-tuple-element.68), channel_id=1, source_target_pairs={{28,0},{29,1},{30,2},{31,3},{0,4},{1,5},{2,6},{3,7},{4,8},{5,9},{6... | collective-permute-start | bytes 221192 | tf_op jit(solution)/shard_map/ppermute | solution.py:32
  77.3 7.3 %collective-permute-start.32 = (f32[72,256]{1,0:T(8,128)S(1)}, f32[72,256]{1,0:T(8,128)S(1)}, u32[]{:S(2)}, u32[]{:S(2)}) collective-permute-start(f32[72,256]{1,0:T(8,128)S(1)} %get-tuple-element.69), channel_id=1, source_target_pairs={{24,0},{25,1},{26,2},{27,3},{28,4},{29,5},{30,6},{31,7},{0,8},{1,9... | collective-permute-start | bytes 221192 | tf_op jit(solution)/shard_map/ppermute | solution.py:32
  78.8 11.1 %collective-permute-start.33 = (f32[72,256]{1,0:T(8,128)S(1)}, f32[72,256]{1,0:T(8,128)S(1)}, u32[]{:S(2)}, u32[]{:S(2)}) collective-permute-start(f32[72,256]{1,0:T(8,128)S(1)} %get-tuple-element.70), channel_id=1, source_target_pairs={{20,0},{21,1},{22,2},{23,3},{24,4},{25,5},{26,6},{27,7},{28,8},{29... | collective-permute-start | bytes 221192 | tf_op jit(solution)/shard_map/ppermute | solution.py:32
  80.2 9.9 %collective-permute-start.34 = (f32[72,256]{1,0:T(8,128)S(1)}, f32[72,256]{1,0:T(8,128)S(1)}, u32[]{:S(2)}, u32[]{:S(2)}) collective-permute-start(f32[72,256]{1,0:T(8,128)S(1)} %get-tuple-element.71), channel_id=1, source_target_pairs={{16,0},{17,1},{18,2},{19,3},{20,4},{21,5},{22,6},{23,7},{24,8},{25... | collective-permute-start | bytes 221192 | tf_op jit(solution)/shard_map/ppermute | solution.py:32
  82.6 7.5 %collective-permute-start.35 = (f32[72,256]{1,0:T(8,128)S(1)}, f32[72,256]{1,0:T(8,128)S(1)}, u32[]{:S(2)}, u32[]{:S(2)}) collective-permute-start(f32[72,256]{1,0:T(8,128)S(1)} %get-tuple-element.72), channel_id=1, source_target_pairs={{12,0},{13,1},{14,2},{15,3},{16,4},{17,5},{18,6},{19,7},{20,8},{21... | collective-permute-start | bytes 221192 | tf_op jit(solution)/shard_map/ppermute | solution.py:32
  83.0 7.1 %collective-permute-start.36 = (f32[72,256]{1,0:T(8,128)S(1)}, f32[72,256]{1,0:T(8,128)S(1)}, u32[]{:S(2)}, u32[]{:S(2)}) collective-permute-start(f32[72,256]{1,0:T(8,128)S(1)} %get-tuple-element.73), channel_id=1, source_target_pairs={{8,0},{9,1},{10,2},{11,3},{12,4},{13,5},{14,6},{15,7},{16,8},{17,9... | collective-permute-start | bytes 221192 | tf_op jit(solution)/shard_map/ppermute | solution.py:32
  84.7 5.5 %collective-permute-start.37 = (f32[72,256]{1,0:T(8,128)S(1)}, f32[72,256]{1,0:T(8,128)S(1)}, u32[]{:S(2)}, u32[]{:S(2)}) collective-permute-start(f32[72,256]{1,0:T(8,128)S(1)} %get-tuple-element.74), channel_id=1, source_target_pairs={{4,0},{5,1},{6,2},{7,3},{8,4},{9,5},{10,6},{11,7},{12,8},{13,9},{1... | collective-permute-start | bytes 221192 | tf_op jit(solution)/shard_map/ppermute | solution.py:32
  97.1 8.7 %collective-permute-start.38 = (bf16[128,256]{1,0:T(8,128)(2,1)S(1)}, bf16[128,256]{1,0:T(8,128)(2,1)S(1)}, u32[]{:S(2)}, u32[]{:S(2)}) collective-permute-start(bf16[128,256]{1,0:T(8,128)(2,1)S(1)} %get-tuple-element.78), channel_id=1, source_target_pairs={{5,0},{6,1},{7,2},{4,3},{9,4},{10,5},{11,6},{8,7},{13,8},{14,9},{1... | collective-permute-start | bytes 196616 | tf_op jit(solution)/shard_map/ppermute | solution.py:32
  102.8 5.1 %collective-permute-start.39 = (bf16[128,256]{1,0:T(8,128)(2,1)S(1)}, bf16[128,256]{1,0:T(8,128)(2,1)S(1)}, u32[]{:S(2)}, u32[]{:S(2)}) collective-permute-start(bf16[128,256]{1,0:T(8,128)(2,1)S(1)} %get-tuple-element.79), channel_id=1, source_target_pairs={{4,0},{5,1},{6,2},{7,3},{8,4},{9,5},{10,6},{11,7},{12,8},{13,9},{1... | collective-permute-start | bytes 196616 | tf_op jit(solution)/shard_map/ppermute | solution.py:32
  102.9 6.9 %collective-permute-start.40 = (bf16[128,256]{1,0:T(8,128)(2,1)S(1)}, bf16[128,256]{1,0:T(8,128)(2,1)S(1)}, u32[]{:S(2)}, u32[]{:S(2)}) collective-permute-start(bf16[128,256]{1,0:T(8,128)(2,1)S(1)} %get-tuple-element.80), channel_id=1, source_target_pairs={{7,0},{4,1},{5,2},{6,3},{11,4},{8,5},{9,6},{10,7},{15,8},{12,9},{1... | collective-permute-start | bytes 196616 | tf_op jit(solution)/shard_map/ppermute | solution.py:32
  103.3 6.5 %collective-permute-start.41 = (bf16[128,256]{1,0:T(8,128)(2,1)S(1)}, bf16[128,256]{1,0:T(8,128)(2,1)S(1)}, u32[]{:S(2)}, u32[]{:S(2)}) collective-permute-start(bf16[128,256]{1,0:T(8,128)(2,1)S(1)} %get-tuple-element.81), channel_id=1, source_target_pairs={{1,0},{2,1},{3,2},{0,3},{5,4},{6,5},{7,6},{4,7},{9,8},{10,9},{11,1... | collective-permute-start | bytes 196616 | tf_op jit(solution)/shard_map/ppermute | solution.py:32
  105.8 5.2 %collective-permute-start.42 = (bf16[128,256]{1,0:T(8,128)(2,1)S(1)}, bf16[128,256]{1,0:T(8,128)(2,1)S(1)}, u32[]{:S(2)}, u32[]{:S(2)}) collective-permute-start(bf16[128,256]{1,0:T(8,128)(2,1)S(1)} %get-tuple-element.82), channel_id=1, source_target_pairs={{3,0},{0,1},{1,2},{2,3},{7,4},{4,5},{5,6},{6,7},{11,8},{8,9},{9,10... | collective-permute-start | bytes 196616 | tf_op jit(solution)/shard_map/ppermute | solution.py:32
  105.8 6.4 %collective-permute-start.43 = (bf16[128,256]{1,0:T(8,128)(2,1)S(1)}, bf16[128,256]{1,0:T(8,128)(2,1)S(1)}, u32[]{:S(2)}, u32[]{:S(2)}) collective-permute-start(bf16[128,256]{1,0:T(8,128)(2,1)S(1)} %get-tuple-element.83), channel_id=1, source_target_pairs={{29,0},{30,1},{31,2},{28,3},{1,4},{2,5},{3,6},{0,7},{5,8},{6,9},{7... | collective-permute-start | bytes 196616 | tf_op jit(solution)/shard_map/ppermute | solution.py:32
  107.9 6.5 %collective-permute-start.44 = (bf16[128,256]{1,0:T(8,128)(2,1)S(1)}, bf16[128,256]{1,0:T(8,128)(2,1)S(1)}, u32[]{:S(2)}, u32[]{:S(2)}) collective-permute-start(bf16[128,256]{1,0:T(8,128)(2,1)S(1)} %get-tuple-element.84), channel_id=1, source_target_pairs={{28,0},{29,1},{30,2},{31,3},{0,4},{1,5},{2,6},{3,7},{4,8},{5,9},{6... | collective-permute-start | bytes 196616 | tf_op jit(solution)/shard_map/ppermute | solution.py:32
  109.8 7.3 %collective-permute-start.45 = (bf16[128,256]{1,0:T(8,128)(2,1)S(1)}, bf16[128,256]{1,0:T(8,128)(2,1)S(1)}, u32[]{:S(2)}, u32[]{:S(2)}) collective-permute-start(bf16[128,256]{1,0:T(8,128)(2,1)S(1)} %get-tuple-element.85), channel_id=1, source_target_pairs={{31,0},{28,1},{29,2},{30,3},{3,4},{0,5},{1,6},{2,7},{7,8},{4,9},{5... | collective-permute-start | bytes 196616 | tf_op jit(solution)/shard_map/ppermute | solution.py:32
  120.6 3.9 %collective-permute-start.46 = (f32[8,256]{1,0:T(8,128)S(1)}, f32[8,256]{1,0:T(8,128)S(1)}, u32[]{:S(2)}, u32[]{:S(2)}) collective-permute-start(f32[8,256]{1,0:T(8,128)S(1)} %get-tuple-element.87), channel_id=1, source_target_pairs={{5,0},{6,1},{7,2},{4,3},{9,4},{10,5},{11,6},{8,7},{13,8},{14,9},{1... | collective-permute-start | bytes 24584 | tf_op jit(solution)/shard_map/ppermute | solution.py:32
  120.7 5.1 %collective-permute-start.47 = (f32[8,256]{1,0:T(8,128)S(1)}, f32[8,256]{1,0:T(8,128)S(1)}, u32[]{:S(2)}, u32[]{:S(2)}) collective-permute-start(f32[8,256]{1,0:T(8,128)S(1)} %get-tuple-element.88), channel_id=1, source_target_pairs={{4,0},{5,1},{6,2},{7,3},{8,4},{9,5},{10,6},{11,7},{12,8},{13,9},{1... | collective-permute-start | bytes 24584 | tf_op jit(solution)/shard_map/ppermute | solution.py:32
  120.8 6.9 %collective-permute-start.48 = (f32[8,256]{1,0:T(8,128)S(1)}, f32[8,256]{1,0:T(8,128)S(1)}, u32[]{:S(2)}, u32[]{:S(2)}) collective-permute-start(f32[8,256]{1,0:T(8,128)S(1)} %get-tuple-element.89), channel_id=1, source_target_pairs={{7,0},{4,1},{5,2},{6,3},{11,4},{8,5},{9,6},{10,7},{15,8},{12,9},{1... | collective-permute-start | bytes 24584 | tf_op jit(solution)/shard_map/ppermute | solution.py:32
  122.5 5.3 %collective-permute-start.49 = (f32[8,256]{1,0:T(8,128)S(1)}, f32[8,256]{1,0:T(8,128)S(1)}, u32[]{:S(2)}, u32[]{:S(2)}) collective-permute-start(f32[8,256]{1,0:T(8,128)S(1)} %get-tuple-element.90), channel_id=1, source_target_pairs={{1,0},{2,1},{3,2},{0,3},{5,4},{6,5},{7,6},{4,7},{9,8},{10,9},{11,1... | collective-permute-start | bytes 24584 | tf_op jit(solution)/shard_map/ppermute | solution.py:32
  123.8 4.5 %collective-permute-start.50 = (f32[8,256]{1,0:T(8,128)S(1)}, f32[8,256]{1,0:T(8,128)S(1)}, u32[]{:S(2)}, u32[]{:S(2)}) collective-permute-start(f32[8,256]{1,0:T(8,128)S(1)} %get-tuple-element.91), channel_id=1, source_target_pairs={{3,0},{0,1},{1,2},{2,3},{7,4},{4,5},{5,6},{6,7},{11,8},{8,9},{9,10... | collective-permute-start | bytes 24584 | tf_op jit(solution)/shard_map/ppermute | solution.py:32
  124.5 5.8 %collective-permute-start.51 = (f32[8,256]{1,0:T(8,128)S(1)}, f32[8,256]{1,0:T(8,128)S(1)}, u32[]{:S(2)}, u32[]{:S(2)}) collective-permute-start(f32[8,256]{1,0:T(8,128)S(1)} %get-tuple-element.92), channel_id=1, source_target_pairs={{29,0},{30,1},{31,2},{28,3},{1,4},{2,5},{3,6},{0,7},{5,8},{6,9},{7... | collective-permute-start | bytes 24584 | tf_op jit(solution)/shard_map/ppermute | solution.py:32
  125.8 5.3 %collective-permute-start.52 = (f32[8,256]{1,0:T(8,128)S(1)}, f32[8,256]{1,0:T(8,128)S(1)}, u32[]{:S(2)}, u32[]{:S(2)}) collective-permute-start(f32[8,256]{1,0:T(8,128)S(1)} %get-tuple-element.93), channel_id=1, source_target_pairs={{28,0},{29,1},{30,2},{31,3},{0,4},{1,5},{2,6},{3,7},{4,8},{5,9},{6... | collective-permute-start | bytes 24584 | tf_op jit(solution)/shard_map/ppermute | solution.py:32
  127.7 6.7 %collective-permute-start.53 = (f32[8,256]{1,0:T(8,128)S(1)}, f32[8,256]{1,0:T(8,128)S(1)}, u32[]{:S(2)}, u32[]{:S(2)}) collective-permute-start(f32[8,256]{1,0:T(8,128)S(1)} %get-tuple-element.94), channel_id=1, source_target_pairs={{31,0},{28,1},{29,2},{30,3},{3,4},{0,5},{1,6},{2,7},{7,8},{4,9},{5... | collective-permute-start | bytes 24584 | tf_op jit(solution)/shard_map/ppermute | solution.py:32

commit v3 on v2

--- a/solution.py
+++ b/solution.py
@@ -30,6 +30,15 @@
             source = ((i + along_x) % count_x) * count_y + (j + along_y) % count_y
             route.append((source, i * count_y + j))
     return lax.ppermute(block, ("gx", "gy"), route)
+
+
+def exchanged(blocks, axis):
+    return lax.all_to_all(blocks, axis, 0, 0)
+
+
+def around(block):
+    column = jnp.stack([shifted(block, 0, -1), block, shifted(block, 0, 1)])
+    return [shifted(column, -1, 0), column, shifted(column, 1, 0)]
 
 
 def whole(space=pltpu.VMEM):
@@ -134,18 +143,52 @@
     return [basis] + [basis * unit[i : i + 1] for i in range(3)]
 
 
-def first_kernel(slots, neighbour_ref, count_ref, embed_ref, radial_ref, mixing_ref, *refs):
-    frame, (low_ref, basis_ref, slope_ref, unit_ref, sums_ref, gate_ref) = refs[:9], refs[9:]
-    atoms = frame[0].shape[1]
+def pack_kernel(position_ref, species_ref, out_ref):
+    rows = jnp.concatenate([position_ref[0, 0], species_ref[0].astype(F32)], axis=0)
+    block = jnp.concatenate([rows[:, s : s + 128] for s in range(0, rows.shape[1], 128)], axis=0)
+    for copy in range(out_ref.shape[0]):
+        out_ref[copy] = block
+
+
+def prep_kernel(grid, neighbour_ref, embed_ref, radial_ref, mixing_ref, hidden_ref, charge_ref,
+                wave_ref, vec_ref, id_ref, rows_ref, radial_out, mixing_out, hidden_out, charge_out,
+                weight_ref):
+    id_ref[...] = neighbour_ref[0, 0].astype(F32).T.astype(jnp.int32)
+    kinds = embed_ref.shape[0]
+    rows_ref[...] = jnp.concatenate(
+        [embed_ref[...], jnp.zeros((8 - kinds, embed_ref.shape[1]), F32)], axis=0
+    )
+    radial_out[...] = radial_ref[...]
+    mixing_out[...] = mixing_ref[...]
+    hidden_out[...] = hidden_ref[...]
+    charge_out[...] = charge_ref[...]
+    green_weights(grid, wave_ref, vec_ref, weight_ref)
+
+
+def unfold_block(block, atoms):
+    parts = atoms // 128
+    return jnp.concatenate([block[4 * s : 4 * s + 4] for s in range(parts)], axis=1)
+
+
+def first_kernel(slots, grid, place_ref, neighbour_ref, count_ref, embed_ref, radial_ref,
+                 mixing_ref, all_ref, low_ref, basis_ref, slope_ref, unit_ref, sums_ref, gate_ref):
+    atoms = low_ref.shape[1]
     ids = flat_row(neighbour_ref[...])
     halves = []
     for cell, (a, b) in enumerate(OFFSETS):
-        block = frame[cell][...]
-        if (a, b) != (0, 0):
-            block = jnp.concatenate(
-                [block[0:1] + a * cell_width, block[1:2] + b * cell_width, block[2:]], axis=0
+        block = all_ref[lax.rem(place_ref[0] + (a + grid[0]), grid[0]),
+                        lax.rem(place_ref[1] + (b + grid[1]), grid[1])]
+        if cell == CENTRE:
+            own = unfold_block(block, atoms)
+            own = jnp.concatenate([own, jnp.zeros_like(own)], axis=0)
+        for s in range(atoms // 128):
+            rows = block[4 * s : 4 * s + 4]
+            halves.append(
+                jnp.concatenate(
+                    [rows[0:1] + a * cell_width, rows[1:2] + b * cell_width, rows[2:4], rows],
+                    axis=0,
+                )
             )
-        halves += [block[:, s : s + 128] for s in range(0, atoms, 128)]
     pieces = []
     for start in range(0, ids.shape[1], 128):
         part = jnp.broadcast_to(ids[:, start : start + 128], (8, 128))
@@ -155,7 +198,6 @@
             found = jnp.where(half == h, jnp.take_along_axis(rows, lane, axis=1), found)
         pieces.append(found)
     found = jnp.concatenate(pieces, axis=1)
-    own = frame[CENTRE][...]
     relative = found - jnp.concatenate([own] * slots, axis=1)
     rel = [relative[i : i + 1] for i in range(3)]
     distance = jnp.sqrt(rel[0] * rel[0] + rel[1] * rel[1] + rel[2] * rel[2] + soften)
@@ -195,12 +237,12 @@
 
 def second_kernel(slots, neighbour_ref, basis_ref, unit_ref, radial_ref, mixing_ref, hidden_ref,
                   out_ref, charge_ref, *refs):
-    frame, refs = refs[:9], refs[9:]
+    frame, refs = refs[:3], refs[3:]
     feature_ref, sums_ref, gate_ref, low_charge_ref, full_charge_ref, energy_ref, slope_ref = refs[:7]
     (source_ref,) = refs[7:]
-    atoms = frame[0].shape[1]
+    atoms = frame[0].shape[2]
     for cell in range(9):
-        source_ref[:, cell * atoms : (cell + 1) * atoms] = frame[cell][...]
+        source_ref[:, cell * atoms : (cell + 1) * atoms] = frame[cell // 3][cell % 3]
 
     def gathered(n):
         hot = hot_columns(neighbour_ref[n : n + 1, :], 9 * atoms)
@@ -210,13 +252,14 @@
 
     sums = messages(edge_parts(basis_ref, unit_ref), radial_ref, 1, slots, atoms, gathered)
     step, gate = mixed(sums, mixing_ref, 1)
-    hidden = frame[CENTRE][...].astype(F32) + step
+    hidden = frame[1][1].astype(F32) + step
     for part in range(3):
         sums_ref[part] = sums[part + 1]
     gate_ref[...] = gate
     charge = dot3(charge_ref[...].T, hidden)
     full_charge_ref[...] = charge
-    low_charge_ref[...] = charge.astype(low_charge_ref.dtype)
+    for copy in range(low_charge_ref.shape[0]):
+        low_charge_ref[copy] = charge.astype(low_charge_ref.dtype)
     value, slope = silu_pair(dot3(hidden_ref[...].T, hidden))
     out = out_ref[...].T
     energy_ref[...] = jnp.sum(value * out, axis=0, keepdims=True)
@@ -247,14 +290,13 @@
 
 def second_back_kernel(slots, scale, grid_x, neighbour_ref, basis_ref, unit_ref, radial_ref,
                        mixing_ref, charge_ref, feature_ref, sums_ref, gate_ref, full_charge_ref,
-                       energy_ref, slope_ref, *refs):
-    folds, refs = refs[:grid_x], refs[grid_x:]
-    site_ref, long_ref, edge_ref, centre_ref = refs[:4]
-    ghosts, (term_ref,) = refs[4:12], refs[12:]
+                       energy_ref, slope_ref, fold_ref, site_ref, long_ref, edge_ref, before_ref,
+                       middle_ref, after_ref, term_ref):
+    ghosts = [before_ref, middle_ref, after_ref]
     atoms = gate_ref.shape[1]
-    total = folds[0][...]
-    for fold in folds[1:]:
-        total = total + fold[...]
+    total = fold_ref[0]
+    for part in range(1, grid_x):
+        total = total + fold_ref[part]
     wide = full_charge_ref.shape[0]
     potential = total[:wide]
     long_ref[...] = total[wide:] * (2.0 * scale)
@@ -278,25 +320,23 @@
         high, low = split(term)
         term_ref[:, lanes] = jnp.concatenate([high, low], axis=0)
     ids = flat_row(neighbour_ref[...])
-    features = centre_ref.shape[0]
+    features = middle_ref.shape[1]
     for cell in range(9):
         hot = hot_columns(ids - cell * atoms, atoms)
         both = dot(term_ref[...], hot, ((1,), (1,)))
         grad = both[:features] + both[features:]
         if cell == CENTRE:
-            centre_ref[...] = grad + cotangent
-        else:
-            ghosts[cell - (cell > CENTRE)][...] = grad.astype(BF16)
+            grad = grad + cotangent
+        ghosts[cell // 3][cell % 3] = grad.astype(ghosts[cell // 3].dtype)
 
 
 def first_back_kernel(slots, neighbour_ref, basis_ref, slope_ref, unit_ref, embed_ref, radial_ref,
-                      mixing_ref, sums_ref, gate_ref, edge_ref, long_ref, centre_ref, *refs):
-    ghosts, refs = refs[:8], refs[8:]
-    own_ref, outs = refs[0], refs[1:]
+                      mixing_ref, sums_ref, gate_ref, edge_ref, long_ref, middle_ref, *refs):
+    from_x, from_y, outs = refs[:2], refs[2:4], refs[4:]
     atoms = gate_ref.shape[1]
-    cotangent = centre_ref[...]
-    for ghost in ghosts:
-        cotangent = cotangent + ghost[...].astype(F32)
+    cotangent = middle_ref[1]
+    for block in (from_x[0][1], from_x[1][1], from_y[0][...], from_y[1][...]):
+        cotangent = cotangent + block.astype(F32)
     grads = message_grads(cotangent, gate_ref, sums_ref, mixing_ref, 0, slots)
     back = [radial_left(radial_ref, 0, path) for path in range(2)]
     stack = embedding_stack(embed_ref[...])
@@ -343,9 +383,8 @@
             found.append(spread[16 * h : 16 * h + 8] + spread[16 * h + 8 : 16 * h + 16])
         grad = jnp.concatenate(found, axis=1)
         if cell == CENTRE:
-            own_ref[...] = own + grad
-        else:
-            outs[cell - (cell > CENTRE)][...] = grad
+            grad = own + grad
+        outs[cell // 3][cell % 3] = grad
 
 
 def pair_tables(parts):
@@ -369,21 +408,43 @@
     return share, padded, pair_rows, wave_rows
 
 
-def table_kernel(share, padded, grid, pos_ref, pair_ref, wave_ref, vec_ref, *refs):
+def green_weights(grid, wave_ref, vec_ref, weight_ref):
     grid_x, grid_y = grid
-    blocks, (ca_ref, sa_ref, cb_ref, sb_ref, weight_ref) = refs[:grid_x], refs[grid_x:]
     turn = 2.0 * math.pi
-    col = pos_ref[1].astype(jnp.float32) * (1.0 / grid_y)
+    side = 2 * WAVE_REACH + 1
+    top = side * side * side - 1
+    vec = vec_ref[...].astype(F32) + WAVE_REACH
+    code = (vec[0:1] * side + vec[1:2]) * side + vec[2:3]
+    code = jnp.maximum(code, top - code)
+    wave = wave_ref[...]
+    own = wave[:, 3:4]
+    seen = jnp.zeros((own.shape[0], 128), F32)
+    for start in range(0, code.shape[1], 128):
+        seen = seen + jnp.where(own == code[:, start : start + 128], 1.0, 0.0)
+    count = jnp.sum(seen, axis=1, keepdims=True) * wave[:, 4:5]
+    sq = (
+        (wave[:, 0:1] * (turn / (grid_x * cell_width))) ** 2
+        + (wave[:, 1:2] * (turn / (grid_y * cell_width))) ** 2
+        + (wave[:, 2:3] * (turn / box_height)) ** 2
+    )
+    green = jnp.exp(-smear_width * sq) / (sq + screen * screen) * count
+    weight_ref[...] = jnp.broadcast_to(green, weight_ref.shape)
+
+
+def table_kernel(grid, place_ref, pair_ref, all_ref, ca_ref, sa_ref, cb_ref, sb_ref):
+    grid_x, grid_y = grid
+    turn = 2.0 * math.pi
+    col = place_ref[1].astype(F32) * (1.0 / grid_y)
     kx = pair_ref[:, 0:1]
     ky = pair_ref[:, 1:2]
-    kz = (lax.broadcasted_iota(jnp.int32, (8, 1), 0) + 1).astype(jnp.float32)
+    kz = (lax.broadcasted_iota(jnp.int32, (8, 1), 0) + 1).astype(F32)
+    atoms = ca_ref.shape[1] // grid_x
     for d in range(grid_x):
-        row_id = lax.rem(pos_ref[0] + d, grid_x).astype(jnp.float32) * (1.0 / grid_x)
-        block = blocks[d]
-        lanes = pl.ds(d * block.shape[1], block.shape[1])
-        x = block[0:1, :] * (1.0 / (grid_x * cell_width)) + row_id
-        y = block[1:2, :] * (1.0 / (grid_y * cell_width)) + col
-        z = block[2:3, :] * (1.0 / box_height)
+        block = unfold_block(all_ref[d, place_ref[1]], atoms)
+        lanes = pl.ds(d * atoms, atoms)
+        x = block[0:1] * (1.0 / (grid_x * cell_width)) + d / grid_x
+        y = block[1:2] * (1.0 / (grid_y * cell_width)) + col
+        z = block[2:3] * (1.0 / box_height)
         alpha = kx * x + ky * y
         alpha = (alpha - jnp.round(alpha)) * turn
         beta = kz * z
@@ -392,25 +453,6 @@
         sa_ref[:, lanes] = jnp.sin(alpha)
         cb_ref[:, lanes] = jnp.cos(beta)
         sb_ref[:, lanes] = jnp.sin(beta)
-    side = 2 * WAVE_REACH + 1
-    top = side * side * side - 1
-    vec = vec_ref[...].astype(jnp.float32) + WAVE_REACH
-    code = (vec[0:1] * side + vec[1:2]) * side + vec[2:3]
-    code = jnp.maximum(code, top - code)
-    wave = wave_ref[...]
-    own = wave[:, 3:4]
-    width = code.shape[1]
-    seen = jnp.zeros((own.shape[0], 128), jnp.float32)
-    for start in range(0, width, 128):
-        seen = seen + jnp.where(own == code[:, start : start + 128], 1.0, 0.0)
-    count = jnp.sum(seen, axis=1, keepdims=True) * wave[:, 4:5]
-    sq = (
-        (wave[:, 0:1] * (turn / (grid_x * cell_width))) ** 2
-        + (wave[:, 1:2] * (turn / (grid_y * cell_width))) ** 2
-        + (wave[:, 2:3] * (turn / box_height)) ** 2
-    )
-    green = jnp.exp(-smear_width * sq) / (sq + screen * screen) * count
-    weight_ref[...] = jnp.broadcast_to(green, weight_ref.shape)
 
 
 def basis_rows(share, ca, sa, cb, sb):
@@ -434,12 +476,10 @@
     return jnp.concatenate([block[:half], block[half:]], axis=1)
 
 
-def structure_kernel(share, padded, grid_x, *refs):
-    ca_ref, sa_ref, cb_ref, sb_ref = refs[:4]
-    blocks, (out_ref,) = refs[4 : 4 + grid_x], refs[4 + grid_x :]
+def structure_kernel(share, grid_x, ca_ref, sa_ref, cb_ref, sb_ref, blocks, out_ref):
     total = None
     for d in range(grid_x):
-        charge = blocks[d][...]
+        charge = blocks[d]
         atoms = charge.shape[1]
         lanes = pl.ds(d * atoms, atoms)
         ca, sa, cb, sb = ca_ref[:, lanes], sa_ref[:, lanes], cb_ref[:, lanes], sb_ref[:, lanes]
@@ -447,19 +487,18 @@
         high, low = split(jnp.concatenate(cc + ss + sc + cs + [ca, sa], axis=0))
         term = dot(high, charge, ((1,), (1,))) + dot(low, charge, ((1,), (1,)))
         total = term if total is None else total + term
-    out_ref[...] = pack_rows(total).astype(out_ref.dtype)
-
-
-def fold_kernel(share, padded, grid, *refs):
+    packed = pack_rows(total).astype(out_ref.dtype)
+    for copy in range(out_ref.shape[0]):
+        out_ref[copy] = packed
+
+
+def fold_kernel(share, padded, grid, ca_ref, sa_ref, cb_ref, sb_ref, weight_ref, pair_ref, blocks,
+                parts, outs):
     grid_x, grid_y = grid
-    ca_ref, sa_ref, cb_ref, sb_ref, weight_ref, pair_ref = refs[:6]
-    blocks = refs[6 : 6 + grid_x]
-    parts = refs[6 + grid_x : 6 + grid_x + grid_y]
-    outs = refs[6 + grid_x + grid_y :]
     turn = 2.0 * math.pi
-    packed = parts[0][...].astype(jnp.float32)
-    for part in parts[1:]:
-        packed = packed + part[...].astype(jnp.float32)
+    packed = parts[0].astype(F32)
+    for part in range(1, grid_y):
+        packed = packed + parts[part].astype(F32)
     struct = unpack_rows(packed)
     wide = struct.shape[1]
     span = 8 * share
@@ -488,7 +527,7 @@
     ky = pair_ref[:, 1:2] * (turn / (grid_y * cell_width))
     kz = (lax.broadcasted_iota(jnp.int32, (8, 1), 0) + 1).astype(jnp.float32) * (turn / box_height)
     for d in range(grid_x):
-        charge = blocks[d][...]
+        charge = blocks[d]
         atoms = charge.shape[1]
         lanes = pl.ds(d * atoms, atoms)
         ca, sa, cb, sb = ca_ref[:, lanes], sa_ref[:, lanes], cb_ref[:, lanes], sb_ref[:, lanes]
@@ -513,7 +552,7 @@
         grad_y = jnp.sum(by_y, axis=0, keepdims=True) + jnp.sum(ky * flat_slope, axis=0, keepdims=True)
         grad_z = jnp.sum(kz * by_z, axis=0, keepdims=True)
         zero = jnp.zeros((5, atoms), jnp.float32)
-        outs[d][...] = jnp.concatenate([pot, grad_x, grad_y, grad_z, zero], axis=0)
+        outs[d] = jnp.concatenate([pot, grad_x, grad_y, grad_z, zero], axis=0)
 
 
 def per_device(
@@ -537,18 +576,33 @@
     grid_x, grid_y = grid
     edges = slots * atoms
     scale = 1.0 / math.sqrt(wave_count * lat_width * atoms * grid_x * grid_y)
-    ids = neighbours[0, 0].T
-    count = counts[0]
-    embed = jnp.pad(species_embed, ((0, 8 - species_embed.shape[0]), (0, 0)))
-    kinds = species[0].astype(F32)
-    own = jnp.concatenate([positions[0, 0], kinds, jnp.zeros((4, atoms), F32)], axis=0)
-
-    frame = [own if cell == CENTRE else shifted(own, *at) for cell, at in enumerate(OFFSETS)]
-    row = {0: own, 1: frame[7], grid_x - 1: frame[1]}
-    row = [row[d] if d in row else shifted(own, d, 0) for d in range(grid_x)]
-
+    place = jnp.stack([lax.axis_index("gx"), lax.axis_index("gy")]).astype(jnp.int32)
+    share, padded, pair_np, wave_np = pair_tables(grid_x)
+    pair_rows = lax.dynamic_index_in_dim(jnp.asarray(pair_np), place[0], 0, keepdims=False)
+    wave_rows = lax.dynamic_index_in_dim(jnp.asarray(wave_np), place[0], 0, keepdims=False)
+    cell_rows = 4 * atoms // 128
+
+    (own,) = run(pack_kernel, [shape(grid_y, cell_rows, 128)], [positions, species], name="pack")
+    column = exchanged(own, "gy")
+    everywhere = exchanged(jnp.broadcast_to(column[None], (grid_x,) + column.shape), "gx")
+
+    ids, embed, radial, mixing, read_hidden, charge_map, weight = run(
+        functools.partial(prep_kernel, grid),
+        [
+            shape(slots, atoms, dtype=jnp.int32),
+            shape(8, features),
+            shape(*radial.shape),
+            shape(*mixing.shape),
+            shape(*read_hidden.shape),
+            shape(*charge_map.shape),
+            shape(wave_np.shape[1], 128),
+        ],
+        [neighbours, species_embed, radial, mixing, read_hidden, charge_map, wave_rows,
+         wavevectors],
+        name="prep",
+    )
     low, basis, slope, unit, sums_one, gate_one = run(
-        functools.partial(first_kernel, slots),
+        functools.partial(first_kernel, slots, grid),
         [
             shape(features, atoms, dtype=BF16),
             shape(8, edges),
@@ -557,37 +611,27 @@
             shape(3, features, atoms),
             shape(features, atoms),
         ],
-        [ids, count, embed, radial, mixing] + frame,
+        [place, ids, counts[0], embed, radial, mixing, everywhere],
+        smem=1,
         name="first",
     )
-    hidden = [low if cell == CENTRE else shifted(low, *at) for cell, at in enumerate(OFFSETS)]
-
-    share, padded, pair_np, wave_np = pair_tables(grid_x)
-    place = jnp.stack([lax.axis_index("gx"), lax.axis_index("gy")]).astype(jnp.int32)
-    pair_rows = lax.dynamic_index_in_dim(jnp.asarray(pair_np), place[0], 0, keepdims=False)
-    wave_rows = lax.dynamic_index_in_dim(jnp.asarray(wave_np), place[0], 0, keepdims=False)
+    hidden = around(low)
+
     span = grid_x * atoms
-    *phases, weight = run(
-        functools.partial(table_kernel, share, padded, grid),
-        [
-            shape(padded, span),
-            shape(padded, span),
-            shape(8, span),
-            shape(8, span),
-            shape(wave_np.shape[1], 128),
-        ],
-        [place, pair_rows, wave_rows, wavevectors] + row,
+    phases = run(
+        functools.partial(table_kernel, grid),
+        [shape(padded, span), shape(padded, span), shape(8, span), shape(8, span)],
+        [place, pair_rows, everywhere],
         smem=1,
         name="tables",
     )
-
     feature, sums_two, gate_two, low_charge, charge, energy, energy_slope = run(
         functools.partial(second_kernel, slots),
         [
             shape(features, edges, dtype=BF16),
             shape(3, features, atoms),
             shape(features, atoms),
-            shape(lat_width, atoms, dtype=BF16),
+            shape(grid_x, lat_width, atoms, dtype=BF16),
             shape(lat_width, atoms),
             shape(1, atoms),
             shape(features, atoms),
@@ -596,44 +640,54 @@
         scratch=[pltpu.VMEM((features, 9 * atoms), BF16)],
         name="second",
     )
-    charges = [low_charge] + [shifted(low_charge, d, 0) for d in range(1, grid_x)]
+    charges = exchanged(low_charge, "gx")
     rows = 32 * share + 2 * padded
     (part,) = run(
-        functools.partial(structure_kernel, share, padded, grid_x),
-        [shape(rows // 2, 2 * lat_width)],
-        phases + charges,
+        functools.partial(structure_kernel, share, grid_x),
+        [shape(grid_y, rows // 2, 2 * lat_width)],
+        list(phases) + [charges],
         name="structure",
     )
-    parts = [part] + [shifted(part, 0, d) for d in range(1, grid_y)]
-    folds = run(
+    parts = exchanged(part, "gy")
+    (folds,) = run(
         functools.partial(fold_kernel, share, padded, grid),
-        [shape(lat_width + 8, atoms)] * grid_x,
-        phases + [weight, pair_rows] + charges + parts,
+        [shape(grid_x, lat_width + 8, atoms)],
+        list(phases) + [weight, pair_rows, charges, parts],
         name="fold",
     )
-    folds = [folds[0]] + [shifted(folds[d], -d, 0) for d in range(1, grid_x)]
-
-    site, long, edge, centre, *ghosts = run(
+    folds = exchanged(folds, "gx")
+
+    site, long, edge, before, middle, after = run(
         functools.partial(second_back_kernel, slots, scale, grid_x),
-        [shape(1, atoms), shape(8, atoms), shape(32, edges), shape(features, atoms)]
-        + [shape(features, atoms, dtype=BF16)] * 8,
+        [
+            shape(1, atoms),
+            shape(8, atoms),
+            shape(32, edges),
+            shape(3, features, atoms, dtype=BF16),
+            shape(3, features, atoms),
+            shape(3, features, atoms, dtype=BF16),
+        ],
         [ids, basis, unit, radial, mixing, charge_map, feature, sums_two, gate_two, charge, energy,
-         energy_slope] + folds,
+         energy_slope, folds],
         scratch=[pltpu.VMEM((2 * features, edges), BF16)],
         name="second_back",
     )
-    around = [at for at in OFFSETS if at != (0, 0)]
-    ghosts = [shifted(ghost, -a, -b) for ghost, (a, b) in zip(ghosts, around)]
-    mine, *moves = run(
+    from_x = [shifted(after, -1, 0), shifted(before, 1, 0)]
+    sides = [
+        (middle[b] + from_x[0][b].astype(F32) + from_x[1][b].astype(F32)).astype(BF16)
+        for b in (0, 2)
+    ]
+    from_y = [shifted(sides[1], 0, -1), shifted(sides[0], 0, 1)]
+    before, middle, after = run(
         functools.partial(first_back_kernel, slots),
-        [shape(8, atoms)] * 9,
-        [ids, basis, slope, unit, embed, radial, mixing, sums_one, gate_one, edge, long, centre]
-        + ghosts,
+        [shape(3, 8, atoms)] * 3,
+        [ids, basis, slope, unit, embed, radial, mixing, sums_one, gate_one, edge, long, middle]
+        + from_x + from_y,
         name="first_back",
     )
-    for move, (a, b) in zip(moves, around):
-        mine = mine + shifted(move, -a, -b)
-    return (-mine[None, None, :3], site[None])
+    total = middle + shifted(after, -1, 0) + shifted(before, 1, 0)
+    total = total[1] + shifted(total[2], 0, -1) + shifted(total[0], 0, 1)
+    return (-total[None, None, :3], site[None])
 
 
 def solution(mesh):

time: 136 us -> 135 us (level)
  starting transfers between devices: 64.6 us -> 29.2 us
  blocking collectives: 0 us -> 31.8 us
  waiting for transfers between devices: 34.6 us -> 37 us
  Pallas kernels: 23.3 us -> 25.2 us
    ppermute x54 -> x12, starting transfers between devices: 64.6 us -> 15.7 us  [shifted(): return lax.ppermute(block, ('gx', 'gy'), route)]
    all_to_all x0 -> x2, blocking collectives: none -> 31.8 us  [exchanged(): return lax.all_to_all(blocks, axis, 0, 0)]
    all_to_all x0 -> x3, starting transfers between devices: none -> 13.5 us  [exchanged(): return lax.all_to_all(blocks, axis, 0, 0)]
    all_to_all x0 -> x3, waiting for transfers between devices: none -> 12 us  [exchanged(): return lax.all_to_all(blocks, axis, 0, 0)]
    ppermute x54 -> x12, waiting for transfers between devices: 34.6 us -> 24.9 us  [shifted(): return lax.ppermute(block, ('gx', 'gy'), route)]
    pallas_call x7 -> x9, Pallas kernels: 23.3 us -> 25.2 us  [run(): pl.pallas_call(kernel, out_shape=outs, in_specs=specs, out_specs=jax.tree...]
    unnamed x24 -> x32, local copies, waits for them, and re-layouts: 8.35 us -> 8.24 us
  transfers between devices with their start and end apart: 54 -> 15, of which waited for: 21 -> 12; matrix products, arithmetic and copies ran while one was open for 3% -> 3% of each run, Pallas kernels for 5% -> 2%
where the time goes in v3:
time: 135 us
  waiting for transfers between devices  37 us (27%)
  blocking collectives  31.8 us (24%)
  starting transfers between devices  29.2 us (22%)
  Pallas kernels  25.2 us (19%)
  local copies, waits for them, and re-layouts  10.5 us (8%)
    all_to_all x2, blocking collectives, exchanged(): return lax.all_to_all(blocks, axis, 0, 0)  31.8 us
    pallas_call x9, Pallas kernels, run(): pl.pallas_call(kernel, out_shape=outs, in_specs=specs, out_specs=jax.tree...  25.2 us
    ppermute x12, waiting for transfers between devices, shifted(): return lax.ppermute(block, ('gx', 'gy'), route)  24.9 us
    ppermute x12, starting transfers between devices, shifted(): return lax.ppermute(block, ('gx', 'gy'), route)  15.7 us
    all_to_all x3, starting transfers between devices, exchanged(): return lax.all_to_all(blocks, axis, 0, 0)  13.5 us
    all_to_all x3, waiting for transfers between devices, exchanged(): return lax.all_to_all(blocks, axis, 0, 0)  12 us
    unnamed x32, local copies, waits for them, and re-layouts  8.24 us
  transfers between devices with their start and end apart: 15, of which 12 were waited for; matrix products, arithmetic and copies ran while one was open for 3% of the time, Pallas kernels for 2%

profile of v3, /device:TPU:0, one launch (start us, length us, event | category | flops | bytes accessed | tf_op | source)
XLA Modules:
  0.0 134.6 jit_solution(13765216259564681983)
XLA Ops:
  0.6 0.0 copy-start.11
  0.6 0.7 copy.17.position_ref
  1.3 0.7 copy-done.12
  2.0 0.6 pack.1
  2.6 5.2 %all-to-all-start = ((f32[4,8,128]{2,1,0:T(8,128)}), f32[4,8,128]{2,1,0:T(8,128)S(1)}, u32[]{:S(2)}, u32[]{:S(2)}) async-start(f32[4,8,128]{2,1,0:T(8,128)} %pack.1), calls=%async_computation | async-start | bytes 32768 | tf_op jit(solution)/shard_map/all_to_all | solution.py:36
  7.8 4.7 %all-to-all-done = f32[4,8,128]{2,1,0:T(8,128)S(1)} async-done(((f32[4,8,128]{2,1,0:T(8,128)}), f32[4,8,128]{2,1,0:T(8,128)S(1)}, u32[]{:S(2)}, u32[]{:S(2)}) %all-to-all-start) | async-done | bytes 16416 | tf_op jit(solution)/shard_map/all_to_all | solution.py:36
  12.5 0.6 broadcast_in_dim.6
  13.1 4.9 %all-to-all-start.1 = ((f32[8,4,8,128]{3,2,1,0:T(8,128)}), f32[8,4,8,128]{3,2,1,0:T(8,128)S(1)}, u32[]{:S(2)}, u32[]{:S(2)}) async-start(f32[8,4,8,128]{3,2,1,0:T(8,128)} %broadcast_in_dim.6), calls=%async_computation.1 | async-start | bytes 262144 | tf_op jit(solution)/shard_map/all_to_all | solution.py:36
  18.0 0.8 copy.16.charge_ref
  18.9 0.8 copy.15.neighbour_ref
  19.7 0.9 dynamic-slice_bitcast_fusion.wave_ref
  20.6 0.0 copy-start
  20.6 0.9 copy-done
  21.6 0.8 copy-done.5
  22.4 0.8 copy-done.6
  23.3 0.7 copy-done.7
  24.0 0.7 copy-done.8
  24.7 0.9 prep.1
  25.5 0.1 pad_add_fusion.place_ref
  25.6 0.0 all-to-all-done.1.all_ref
  25.6 0.0 copy-done.11
  25.6 2.5 %first.1 = (bf16[128,256]{1,0:T(8,128)(2,1)S(1)}, f32[8,3072]{1,0:T(8,128)S(1)}, f32[8,3072]{1,0:T(8,128)S(1)}, f32[8,3072]{1,0:T(8,128)S(1)}, f32[3,128,256]{2,1,0:T(8,128)S(1)}, /*index=5*/f32[128,256]{1,0:T(8,128)S(1)}) custom-call(s32[2]{0:T(128)S(1)} %pad_add_fusion.place_ref, s32[12,256]{1,0:T(8,128)S(1)} %get-tuple-element.35.neighbour_ref, ...), custom_call_target="tpu_custom_call" | custom-call | flops 1000000 | bytes 1000000 | tf_op jit(solution)/shard_map/first/pallas_call | solution.py:50
  28.1 0.0 copy-start.3
  28.1 0.6 collective-permute-start.1
  28.8 1.5 %collective-permute-start = (bf16[128,256]{1,0:T(8,128)(2,1)S(1)}, bf16[128,256]{1,0:T(8,128)(2,1)S(1)}, u32[]{:S(2)}, u32[]{:S(2)}) collective-permute-start(bf16[128,256]{1,0:T(8,128)(2,1)S(1)} %get-tuple-element.46), channel_id=1, source_target_pairs={{3,0},{0,1},{1,2},{2,3},{7,4},{4,5},{5,6},{6,7},{11,8},{8,9},{9,10... | collective-permute-start | bytes 196616 | tf_op jit(solution)/shard_map/ppermute | solution.py:32
  30.2 2.7 %collective-permute-done.1 = bf16[128,256]{1,0:T(8,128)(2,1)S(1)} collective-permute-done((bf16[128,256]{1,0:T(8,128)(2,1)S(1)}, bf16[128,256]{1,0:T(8,128)(2,1)S(1)}, u32[]{:S(2)}, u32[]{:S(2)}) %collective-permute-start.1) | collective-permute-done | bytes 65568 | tf_op jit(solution)/shard_map/ppermute | solution.py:32
  32.9 1.2 collective-permute-done
  34.2 2.4 %collective-permute-start.3 = (bf16[3,128,256]{2,1,0:T(8,128)(2,1)S(1)}, bf16[3,128,256]{2,1,0:T(8,128)(2,1)S(1)}, u32[]{:S(2)}, u32[]{:S(2)}) collective-permute-start(bf16[3,128,256]{2,1,0:T(8,128)(2,1)S(1)} %pad_maximum_fusion.refs_1_), channel_id=1, source_target_pairs={{4,0},{5,1},{6,2},{7,3},{8,4},{9,5},{10,6},{11,7},{12,8},{13,9},{1... | collective-permute-start | bytes 589832 | tf_op jit(solution)/shard_map/ppermute | solution.py:32
  36.5 0.0 collective-permute-start.2
  36.5 4.3 %collective-permute-done.3.refs_2_ = bf16[3,128,256]{2,1,0:T(8,128)(2,1)S(1)} collective-permute-done((bf16[3,128,256]{2,1,0:T(8,128)(2,1)S(1)}, bf16[3,128,256]{2,1,0:T(8,128)(2,1)S(1)}, u32[]{:S(2)}, u32[]{:S(2)}) %collective-permute-start.3) | collective-permute-done | bytes 196640 | tf_op jit(solution)/shard_map/ppermute | solution.py:32
  40.8 2.8 %collective-permute-done.2.refs_0_ = bf16[3,128,256]{2,1,0:T(8,128)(2,1)S(1)} collective-permute-done((bf16[3,128,256]{2,1,0:T(8,128)(2,1)S(1)}, bf16[3,128,256]{2,1,0:T(8,128)(2,1)S(1)}, u32[]{:S(2)}, u32[]{:S(2)}) %collective-permute-start.2) | collective-permute-done | bytes 196640 | tf_op jit(solution)/shard_map/ppermute | solution.py:32
  43.6 0.0 copy-done.3
  43.6 0.0 copy-done.13
  43.6 5.4 %second.1 = (bf16[128,3072]{1,0:T(8,128)(2,1)S(1)}, f32[3,128,256]{2,1,0:T(8,128)S(1)}, f32[128,256]{1,0:T(8,128)S(1)}, bf16[8,64,256]{2,1,0:T(8,128)(2,1)}, f32...) custom-call(s32[12,256]{1,0:T(8,128)S(1)} %get-tuple-element.35.neighbour_ref, ...), custom_call_target="tpu_custom_call" | custom-call | flops 1000000 | bytes 1000000 | tf_op jit(solution)/shard_map/second/pallas_call | solution.py:50
  49.0 0.6 copy-done.9
  49.6 3.4 %all-to-all-start.2 = ((bf16[8,64,256]{2,1,0:T(8,128)(2,1)}), bf16[8,64,256]{2,1,0:T(8,128)(2,1)S(1)}, u32[]{:S(2)}, u32[]{:S(2)}) async-start(bf16[8,64,256]{2,1,0:T(8,128)(2,1)} %get-tuple-element.58), calls=%async_computation.2 | async-start | bytes 524288 | tf_op jit(solution)/shard_map/all_to_all | solution.py:36
  53.0 0.0 copy-done.1
  53.0 0.7 dynamic-slice_bitcast_fusion.1.pair_ref
  53.7 1.6 %tables.1 = (f32[24,2048]{1,0:T(8,128)S(1)}, f32[24,2048]{1,0:T(8,128)S(1)}, f32[8,2048]{1,0:T(8,128)S(1)}, f32[8,2048]{1,0:T(8,128)S(1)}) custom-call(s32[2]{0:T(128)S(1)} %pad_add_fusion.place_ref, f32[24,8]{1,0:T(8,128)S(1)} %dynamic-slice_bitcast_fusion.1.pair_ref, f32[8,4,8,128]{3,2,1,0:T(8,128)S(1)} %all-to-all-done.1.all_ref), custom_call_target="tpu_custom_call" | custom-call | flops 1000000 | bytes 1000000 | tf_op jit(solution)/shard_map/tables/pallas_call | solution.py:50
  55.3 7.3 %all-to-all-done.2.blocks = bf16[8,64,256]{2,1,0:T(8,128)(2,1)S(1)} async-done(((bf16[8,64,256]{2,1,0:T(8,128)(2,1)}), bf16[8,64,256]{2,1,0:T(8,128)(2,1)S(1)}, u32[]{:S(2)}, u32[]{:S(2)}) %all-to-all-start.2) | async-done | bytes 262176 | tf_op jit(solution)/shard_map/all_to_all | solution.py:36
  62.7 1.5 %structure.1 = f32[4,312,128]{2,1,0:T(8,128)S(1)} custom-call(f32[24,2048]{1,0:T(8,128)S(1)} %get-tuple-element.53.ca_ref, f32[24,2048]{1,0:T(8,128)S(1)} %get-tuple-element.54.sa_ref, f32[8,2048]{1,0:T(8,128)S(1)} %get-tuple-element.55.cb_ref, f32[8,2048]{1,0:T(8,128)S(1)} %get-tuple-element.56.sb_ref, bf16[8,64,256]{2,1,0:T(8,128)(2,1)S(1)} %all-to-all-done.2.blocks), custom_call_target="tpu_custom_call" | custom-call | flops 1000000 | bytes 1000000 | tf_op jit(solution)/shard_map/structure/pallas_call | solution.py:50
  64.2 12.1 %all_to_all.25.parts = f32[4,312,128]{2,1,0:T(8,128)S(1)} all-to-all(f32[4,312,128]{2,1,0:T(8,128)S(1)} %structure.1), channel_id=1, replica_groups=mesh['gx'=8,'gy'=4] {'gy'}, dimensions={0} | all-to-all | bytes 1277952 | tf_op jit(solution)/shard_map/all_to_all | solution.py:36
  76.3 2.3 %fold.1 = f32[8,72,256]{2,1,0:T(8,128)S(1)} custom-call(f32[24,2048]{1,0:T(8,128)S(1)} %get-tuple-element.53.ca_ref, f32[24,2048]{1,0:T(8,128)S(1)} %get-tuple-element.54.sa_ref, f32[8,2048]{1,0:T(8,128)S(1)} %get-tuple-element.55.cb_ref, f32[8,2048]{1,0:T(8,128)S(1)} %get-tuple-element.56.sb_ref, f32[312,128]{1,0:T(8,128)S(1)} %get-tuple-element.57.weight_ref, ...), custom_call_target="tpu_custom_call" | custom-call | flops 1000000 | bytes 1000000 | tf_op jit(solution)/shard_map/fold/pallas_call | solution.py:50
  78.7 19.7 %all_to_all.26.fold_ref = f32[8,72,256]{2,1,0:T(8,128)S(1)} all-to-all(f32[8,72,256]{2,1,0:T(8,128)S(1)} %fold.1), channel_id=1, replica_groups=mesh['gx'=8,'gy'=4] {'gx'}, dimensions={0} | all-to-all | bytes 1179648 | tf_op jit(solution)/shard_map/all_to_all | solution.py:36
  98.3 6.8 %second_back.1 = (f32[1,256]{1,0:T(1,128)}, f32[8,256]{1,0:T(8,128)S(1)}, f32[32,3072]{1,0:T(8,128)S(1)}, bf16[3,128,256]{2,1,0:T(8,128)(2,1)S(1)}, f32[3,128,25...) custom-call(s32[12,256]{1,0:T(8,128)S(1)} %get-tuple-element.35.neighbour_ref, ...), custom_call_target="tpu_custom_call" | custom-call | flops 1000000 | bytes 1000000 | tf_op jit(solution)/shard_map/second_back/pallas_call | solution.py:50
  105.1 0.0 collective-permute-start.4
  105.1 3.5 %collective-permute-start.5 = (bf16[3,128,256]{2,1,0:T(8,128)(2,1)S(1)}, bf16[3,128,256]{2,1,0:T(8,128)(2,1)S(1)}, u32[]{:S(2)}, u32[]{:S(2)}) collective-permute-start(bf16[3,128,256]{2,1,0:T(8,128)(2,1)S(1)} %get-tuple-element.63), channel_id=1, source_target_pairs={{4,0},{5,1},{6,2},{7,3},{8,4},{9,5},{10,6},{11,7},{12,8},{13,9},{1... | collective-permute-start | bytes 589832 | tf_op jit(solution)/shard_map/ppermute | solution.py:32
  108.7 5.2 %collective-permute-done.4.refs_0_ = bf16[3,128,256]{2,1,0:T(8,128)(2,1)S(1)} collective-permute-done((bf16[3,128,256]{2,1,0:T(8,128)(2,1)S(1)}, bf16[3,128,256]{2,1,0:T(8,128)(2,1)S(1)}, u32[]{:S(2)}, u32[]{:S(2)}) %collective-permute-start.4) | collective-permute-done | bytes 196640 | tf_op jit(solution)/shard_map/ppermute | solution.py:32
  113.9 0.0 collective-permute-done.5.refs_1_
  113.9 0.1 fusion.1
  114.0 0.9 collective-permute-start.7
  114.9 1.2 collective-permute-start.6
  116.0 2.2 %collective-permute-done.7.refs_3_ = bf16[128,256]{1,0:T(8,128)(2,1)S(1)} collective-permute-done((bf16[128,256]{1,0:T(8,128)(2,1)S(1)}, bf16[128,256]{1,0:T(8,128)(2,1)S(1)}, u32[]{:S(2)}, u32[]{:S(2)}) %collective-permute-start.7) | collective-permute-done | bytes 65568 | tf_op jit(solution)/shard_map/ppermute | solution.py:32
  118.3 1.8 %collective-permute-done.6.refs_2_ = bf16[128,256]{1,0:T(8,128)(2,1)S(1)} collective-permute-done((bf16[128,256]{1,0:T(8,128)(2,1)S(1)}, bf16[128,256]{1,0:T(8,128)(2,1)S(1)}, u32[]{:S(2)}, u32[]{:S(2)}) %collective-permute-start.6) | collective-permute-done | bytes 65568 | tf_op jit(solution)/shard_map/ppermute | solution.py:32
  120.1 3.5 %first_back.1 = (f32[3,8,256]{2,1,0:T(8,128)S(1)}, f32[3,8,256]{2,1,0:T(8,128)S(1)}, f32[3,8,256]{2,1,0:T(8,128)S(1)}) custom-call(s32[12,256]{1,0:T(8,128)S(1)} %get-tuple-element.35.neighbour_ref, f32[8,3072]{1,0:T(8,128)S(1)} %get-tuple-element.39.basis_ref, f32[8,3072]{1,0:T(8,128)S(1)} %copy-done.4, f32[8,3072]{1,0:T(8,128)S(1)} %get-tuple-element.41.unit_ref, ...), custom_call_target="tpu_custom_call" | custom-call | flops 1000000 | bytes 1000000 | tf_op jit(solution)/shard_map/first_back/pallas_call | solution.py:50
  123.6 0.1 collective-permute-start.8
  123.6 3.5 %collective-permute-start.9 = (f32[3,8,256]{2,1,0:T(8,128)S(1)}, f32[3,8,256]{2,1,0:T(8,128)S(1)}, u32[]{:S(2)}, u32[]{:S(2)}) collective-permute-start(f32[3,8,256]{2,1,0:T(8,128)S(1)} %get-tuple-element.66), channel_id=1, source_target_pairs={{4,0},{5,1},{6,2},{7,3},{8,4},{9,5},{10,6},{11,7},{12,8},{13,9},{1... | collective-permute-start | bytes 73736 | tf_op jit(solution)/shard_map/ppermute | solution.py:32
  127.2 1.5 %collective-permute-done.8 = f32[3,8,256]{2,1,0:T(8,128)S(1)} collective-permute-done((f32[3,8,256]{2,1,0:T(8,128)S(1)}, f32[3,8,256]{2,1,0:T(8,128)S(1)}, u32[]{:S(2)}, u32[]{:S(2)}) %collective-permute-start.8) | collective-permute-done | bytes 24608 | tf_op jit(solution)/shard_map/ppermute | solution.py:32
  128.7 0.0 collective-permute-done.9
  128.7 0.8 collective-permute-start.11
  129.4 1.3 collective-permute-start.10
  130.8 1.6 %collective-permute-done.11 = f32[8,256]{1,0:T(8,128)S(1)} collective-permute-done((f32[8,256]{1,0:T(8,128)S(1)}, f32[8,256]{1,0:T(8,128)S(1)}, u32[]{:S(2)}, u32[]{:S(2)}) %collective-permute-start.11) | collective-permute-done | bytes 8224 | tf_op jit(solution)/shard_map/ppermute | solution.py:32
  132.4 1.6 %collective-permute-done.10 = f32[8,256]{1,0:T(8,128)S(1)} collective-permute-done((f32[8,256]{1,0:T(8,128)S(1)}, f32[8,256]{1,0:T(8,128)S(1)}, u32[]{:S(2)}, u32[]{:S(2)}) %collective-permute-start.10) | collective-permute-done | bytes 8224 | tf_op jit(solution)/shard_map/ppermute | solution.py:32
  134.0 0.6 copy.18
  (18 shorter events, 0.1 us)
Async XLA Ops:
  0.6 25.0 %copy-start.11 = (s32[1,1,256]{2,1,0:T(1,128)S(1)}, s32[1,1,256]{2,1,0:T(1,128)}, u32[]{:S(2)}) copy-start(s32[1,1,256]{2,1,0:T(1,128)} %param.16) | copy-start | bytes 3076
  1.3 0.7 copy-start.12
  2.6 9.9 %all-to-all-start = ((f32[4,8,128]{2,1,0:T(8,128)}), f32[4,8,128]{2,1,0:T(8,128)S(1)}, u32[]{:S(2)}, u32[]{:S(2)}) async-start(f32[4,8,128]{2,1,0:T(8,128)} %pack.1), calls=%async_computation | async-start | bytes 32768 | tf_op jit(solution)/shard_map/all_to_all | solution.py:36
  7.8 35.8 %copy-start.13 = (f32[128]{0:T(128)S(1)}, f32[128]{0:T(128)}, u32[]{:S(2)}) copy-start(f32[128]{0:T(128)} %param.21) | copy-start | bytes 1540
  13.1 12.5 %all-to-all-start.1 = ((f32[8,4,8,128]{3,2,1,0:T(8,128)}), f32[8,4,8,128]{3,2,1,0:T(8,128)S(1)}, u32[]{:S(2)}, u32[]{:S(2)}) async-start(f32[8,4,8,128]{3,2,1,0:T(8,128)} %broadcast_in_dim.6), calls=%async_computation.1 | async-start | bytes 262144 | tf_op jit(solution)/shard_map/all_to_all | solution.py:36
  20.6 1.0 copy-start
  21.6 0.8 copy-start.5
  22.4 0.8 copy-start.6
  23.3 0.7 copy-start.7
  24.0 0.7 copy-start.8
  28.1 15.5 %copy-start.3 = (f32[8,3072]{1,0:T(8,128)}, f32[8,3072]{1,0:T(8,128)S(1)}, u32[]{:S(2)}) copy-start(f32[8,3072]{1,0:T(8,128)S(1)} %get-tuple-element.40.slope_ref) | copy-start | bytes 294916
  28.1 4.8 %collective-permute-start.1 = (bf16[128,256]{1,0:T(8,128)(2,1)S(1)}, bf16[128,256]{1,0:T(8,128)(2,1)S(1)}, u32[]{:S(2)}, u32[]{:S(2)}) collective-permute-start(bf16[128,256]{1,0:T(8,128)(2,1)S(1)} %get-tuple-element.46), channel_id=1, source_target_pairs={{1,0},{2,1},{3,2},{0,3},{5,4},{6,5},{7,6},{4,7},{9,8},{10,9},{11,1... | collective-permute-start | bytes 196616 | tf_op jit(solution)/shard_map/ppermute | solution.py:32
  28.8 5.4 %collective-permute-start = (bf16[128,256]{1,0:T(8,128)(2,1)S(1)}, bf16[128,256]{1,0:T(8,128)(2,1)S(1)}, u32[]{:S(2)}, u32[]{:S(2)}) collective-permute-start(bf16[128,256]{1,0:T(8,128)(2,1)S(1)} %get-tuple-element.46), channel_id=1, source_target_pairs={{3,0},{0,1},{1,2},{2,3},{7,4},{4,5},{5,6},{6,7},{11,8},{8,9},{9,10... | collective-permute-start | bytes 196616 | tf_op jit(solution)/shard_map/ppermute | solution.py:32
  34.2 6.6 %collective-permute-start.3 = (bf16[3,128,256]{2,1,0:T(8,128)(2,1)S(1)}, bf16[3,128,256]{2,1,0:T(8,128)(2,1)S(1)}, u32[]{:S(2)}, u32[]{:S(2)}) collective-permute-start(bf16[3,128,256]{2,1,0:T(8,128)(2,1)S(1)} %pad_maximum_fusion.refs_1_), channel_id=1, source_target_pairs={{4,0},{5,1},{6,2},{7,3},{8,4},{9,5},{10,6},{11,7},{12,8},{13,9},{1... | collective-permute-start | bytes 589832 | tf_op jit(solution)/shard_map/ppermute | solution.py:32
  36.5 7.1 %collective-permute-start.2 = (bf16[3,128,256]{2,1,0:T(8,128)(2,1)S(1)}, bf16[3,128,256]{2,1,0:T(8,128)(2,1)S(1)}, u32[]{:S(2)}, u32[]{:S(2)}) collective-permute-start(bf16[3,128,256]{2,1,0:T(8,128)(2,1)S(1)} %pad_maximum_fusion.refs_1_), channel_id=1, source_target_pairs={{28,0},{29,1},{30,2},{31,3},{0,4},{1,5},{2,6},{3,7},{4,8},{5,9},{6... | collective-permute-start | bytes 589832 | tf_op jit(solution)/shard_map/ppermute | solution.py:32
  49.0 0.6 copy-start.9
  49.0 4.0 %copy-start.1 = (f32[128,256]{1,0:T(8,128)}, f32[128,256]{1,0:T(8,128)S(1)}, u32[]{:S(2)}) copy-start(f32[128,256]{1,0:T(8,128)S(1)} %get-tuple-element.52.slope_ref) | copy-start | bytes 393220
  49.6 13.1 %all-to-all-start.2 = ((bf16[8,64,256]{2,1,0:T(8,128)(2,1)}), bf16[8,64,256]{2,1,0:T(8,128)(2,1)S(1)}, u32[]{:S(2)}, u32[]{:S(2)}) async-start(bf16[8,64,256]{2,1,0:T(8,128)(2,1)} %get-tuple-element.58), calls=%async_computation.2 | async-start | bytes 524288 | tf_op jit(solution)/shard_map/all_to_all | solution.py:36
  76.3 22.0 %copy-start.2 = (f32[128,256]{1,0:T(8,128)S(1)}, f32[128,256]{1,0:T(8,128)}, u32[]{:S(2)}) copy-start(f32[128,256]{1,0:T(8,128)} %copy-done.1) | copy-start | bytes 393220
  76.3 22.0 %copy-start.10 = (f32[1,256]{1,0:T(1,128)S(1)}, f32[1,256]{1,0:T(1,128)}, u32[]{:S(2)}) copy-start(f32[1,256]{1,0:T(1,128)} %copy-done.9) | copy-start | bytes 3076
  98.3 21.7 %copy-start.4 = (f32[8,3072]{1,0:T(8,128)S(1)}, f32[8,3072]{1,0:T(8,128)}, u32[]{:S(2)}) copy-start(f32[8,3072]{1,0:T(8,128)} %copy-done.3) | copy-start | bytes 294916
  105.1 8.8 %collective-permute-start.4 = (bf16[3,128,256]{2,1,0:T(8,128)(2,1)S(1)}, bf16[3,128,256]{2,1,0:T(8,128)(2,1)S(1)}, u32[]{:S(2)}, u32[]{:S(2)}) collective-permute-start(bf16[3,128,256]{2,1,0:T(8,128)(2,1)S(1)} %get-tuple-element.62), channel_id=1, source_target_pairs={{28,0},{29,1},{30,2},{31,3},{0,4},{1,5},{2,6},{3,7},{4,8},{5,9},{6... | collective-permute-start | bytes 589832 | tf_op jit(solution)/shard_map/ppermute | solution.py:32
  105.1 8.8 %collective-permute-start.5 = (bf16[3,128,256]{2,1,0:T(8,128)(2,1)S(1)}, bf16[3,128,256]{2,1,0:T(8,128)(2,1)S(1)}, u32[]{:S(2)}, u32[]{:S(2)}) collective-permute-start(bf16[3,128,256]{2,1,0:T(8,128)(2,1)S(1)} %get-tuple-element.63), channel_id=1, source_target_pairs={{4,0},{5,1},{6,2},{7,3},{8,4},{9,5},{10,6},{11,7},{12,8},{13,9},{1... | collective-permute-start | bytes 589832 | tf_op jit(solution)/shard_map/ppermute | solution.py:32
  114.0 4.3 %collective-permute-start.7 = (bf16[128,256]{1,0:T(8,128)(2,1)S(1)}, bf16[128,256]{1,0:T(8,128)(2,1)S(1)}, u32[]{:S(2)}, u32[]{:S(2)}) collective-permute-start(bf16[128,256]{1,0:T(8,128)(2,1)S(1)} %get-tuple-element.70), channel_id=1, source_target_pairs={{1,0},{2,1},{3,2},{0,3},{5,4},{6,5},{7,6},{4,7},{9,8},{10,9},{11,1... | collective-permute-start | bytes 196616 | tf_op jit(solution)/shard_map/ppermute | solution.py:32
  114.9 5.2 %collective-permute-start.6 = (bf16[128,256]{1,0:T(8,128)(2,1)S(1)}, bf16[128,256]{1,0:T(8,128)(2,1)S(1)}, u32[]{:S(2)}, u32[]{:S(2)}) collective-permute-start(bf16[128,256]{1,0:T(8,128)(2,1)S(1)} %get-tuple-element.71), channel_id=1, source_target_pairs={{3,0},{0,1},{1,2},{2,3},{7,4},{4,5},{5,6},{6,7},{11,8},{8,9},{9,10... | collective-permute-start | bytes 196616 | tf_op jit(solution)/shard_map/ppermute | solution.py:32
  123.6 5.1 %collective-permute-start.8 = (f32[3,8,256]{2,1,0:T(8,128)S(1)}, f32[3,8,256]{2,1,0:T(8,128)S(1)}, u32[]{:S(2)}, u32[]{:S(2)}) collective-permute-start(f32[3,8,256]{2,1,0:T(8,128)S(1)} %get-tuple-element.65), channel_id=1, source_target_pairs={{28,0},{29,1},{30,2},{31,3},{0,4},{1,5},{2,6},{3,7},{4,8},{5,9},{6... | collective-permute-start | bytes 73736 | tf_op jit(solution)/shard_map/ppermute | solution.py:32
  123.6 5.1 %collective-permute-start.9 = (f32[3,8,256]{2,1,0:T(8,128)S(1)}, f32[3,8,256]{2,1,0:T(8,128)S(1)}, u32[]{:S(2)}, u32[]{:S(2)}) collective-permute-start(f32[3,8,256]{2,1,0:T(8,128)S(1)} %get-tuple-element.66), channel_id=1, source_target_pairs={{4,0},{5,1},{6,2},{7,3},{8,4},{9,5},{10,6},{11,7},{12,8},{13,9},{1... | collective-permute-start | bytes 73736 | tf_op jit(solution)/shard_map/ppermute | solution.py:32
  128.7 3.7 %collective-permute-start.11 = (f32[8,256]{1,0:T(8,128)S(1)}, f32[8,256]{1,0:T(8,128)S(1)}, u32[]{:S(2)}, u32[]{:S(2)}) collective-permute-start(f32[8,256]{1,0:T(8,128)S(1)} %get-tuple-element.73), channel_id=1, source_target_pairs={{1,0},{2,1},{3,2},{0,3},{5,4},{6,5},{7,6},{4,7},{9,8},{10,9},{11,1... | collective-permute-start | bytes 24584 | tf_op jit(solution)/shard_map/ppermute | solution.py:32
  129.4 4.5 %collective-permute-start.10 = (f32[8,256]{1,0:T(8,128)S(1)}, f32[8,256]{1,0:T(8,128)S(1)}, u32[]{:S(2)}, u32[]{:S(2)}) collective-permute-start(f32[8,256]{1,0:T(8,128)S(1)} %get-tuple-element.74), channel_id=1, source_target_pairs={{3,0},{0,1},{1,2},{2,3},{7,4},{4,5},{5,6},{6,7},{11,8},{8,9},{9,10... | collective-permute-start | bytes 24584 | tf_op jit(solution)/shard_map/ppermute | solution.py:32

commit v4 on v3

v4 whole, which is shorter than its diff:
```python
import functools
import math

import jax
import jax.numpy as jnp
import numpy as np
from jax import lax
from jax.experimental import pallas as pl
from jax.experimental.pallas import tpu as pltpu
from jax.sharding import PartitionSpec as P

cell_width = 10.0
box_height = 30.0
cut_radius = 50.0
soften = 0.25
screen = 0.5
smear_width = 0.5
WAVE_REACH = 8
F32 = jnp.float32
BF16 = jnp.bfloat16
OFFSETS = [(a, b) for a in (-1, 0, 1) for b in (-1, 0, 1)]
CENTRE = 4


def shifted(block, along_x, along_y):
    count_x, count_y = lax.axis_size("gx"), lax.axis_size("gy")
    route = []
    for i in range(count_x):
        for j in range(count_y):
            source = ((i + along_x) % count_x) * count_y + (j + along_y) % count_y
            route.append((source, i * count_y + j))
    return lax.ppermute(block, ("gx", "gy"), route)


def around(block):
    column = jnp.stack([shifted(block, 0, -1), block, shifted(block, 0, 1)])
    return [shifted(column, -1, 0), column, shifted(column, 1, 0)]


def whole(space=pltpu.VMEM):
    return pl.BlockSpec(memory_space=space)


def run(kernel, outs, args, scratch=(), smem=0, hbm=0, flops=10_000_000, name=None):
    specs = [whole(pltpu.SMEM)] * smem + [whole(pl.ANY)] * hbm
    specs += [whole()] * (len(args) - smem - hbm)
    return list(
        pl.pallas_call(
            kernel,
            out_shape=outs,
            in_specs=specs,
            out_specs=[whole() for _ in outs],
            scratch_shapes=list(scratch),
            compiler_params=pltpu.CompilerParams(vmem_limit_bytes=32 * 1024 * 1024),
            cost_estimate=pl.CostEstimate(
                flops=flops, bytes_accessed=1_000_000, transcendentals=0
            ),
            name=name,
        )(*args)
    )


def shape(*dims, dtype=F32):
    return jax.ShapeDtypeStruct(dims, dtype)


def split(value):
    high = value.astype(BF16)
    return high, (value - high.astype(F32)).astype(BF16)


def dot(left, right, contract=((1,), (0,))):
    return lax.dot_general(left, right, (contract, ((), ())), preferred_element_type=F32)


def dot3(left, right):
    left_high, left_low = split(left)
    right_high, right_low = split(right)
    return dot(left_high, right_high) + (dot(left_high, right_low) + dot(left_low, right_high))


def dot_split(left, right):
    right_high, right_low = split(right)
    return dot(left[0], right_high) + (dot(left[0], right_low) + dot(left[1], right_high))


def sin_cos(turns):
    quarter = jnp.round(turns * 4.0)
    x = (turns - quarter * 0.25) * (2.0 * math.pi)
    z = x * x
    sine = ((-1.9515295891e-4 * z + 8.3321608736e-3) * z - 1.6666654611e-1) * (z * x) + x
    cosine = (2.443315711809948e-5 * z - 1.388731625493765e-3) * z + 4.166664568298827e-2
    cosine = cosine * (z * z) - 0.5 * z + 1.0
    k = quarter.astype(jnp.int32) & 3
    odd = (k & 1) == 1
    by_sine = jnp.where(odd, cosine, sine)
    by_cosine = jnp.where(odd, sine, cosine)
    return (
        jnp.where(k >= 2, -by_sine, by_sine),
        jnp.where((k == 1) | (k == 2), -by_cosine, by_cosine),
    )


def stacked_left(value):
    high = value.astype(BF16).astype(F32)
    rows = jnp.concatenate([high, high, value - high, jnp.zeros_like(high)], axis=0)
    return rows.T.astype(BF16)


def stacked_right(value):
    high = value.astype(BF16).astype(F32)
    return jnp.concatenate([high, value - high, high, jnp.zeros_like(high)], axis=0).astype(BF16)


def silu_pair(value):
    gate = 1.0 / (1.0 + jnp.exp(-value))
    return value * gate, gate * (1.0 + value * (1.0 - gate))


def onehot_kinds(kinds, rows):
    levels = lax.broadcasted_iota(jnp.int32, (rows, kinds.shape[1]), 0).astype(F32)
    return jnp.where(kinds == levels, 1.0, 0.0)


def embedding_stack(embed):
    high = embed.astype(BF16).astype(F32)
    rest = embed - high
    middle = rest.astype(BF16).astype(F32)
    rows = jnp.concatenate([high, middle, rest - middle, jnp.zeros_like(high)], axis=0)
    return rows.T.astype(BF16)


def embedded(stack, kinds):
    hot = onehot_kinds(kinds, 8)
    return dot(stack, jnp.concatenate([hot, hot, hot, jnp.zeros_like(hot)], axis=0).astype(BF16))


def weights_of(stack_ref, layer, part, rows):
    return dot(stack_ref[layer, 1 if part else 0], stacked_right(rows))


def mixed(sums, high_ref, low_ref, layer):
    squares = sums[1] * sums[1] + sums[2] * sums[2] + sums[3] * sums[3]
    both = jnp.concatenate([sums[0], squares], axis=0)
    return silu_pair(dot_split((high_ref[layer], low_ref[layer]), both))


def edge_parts(basis, unit):
    return [basis] + [basis * unit[i : i + 1] for i in range(3)]


def pack_kernel(position_ref, species_ref, out_ref, place, kind, sems):
    copies = [
        pltpu.make_async_copy(position_ref, place, sems.at[0]),
        pltpu.make_async_copy(species_ref, kind, sems.at[1]),
    ]
    for copy in copies:
        copy.start()
    for copy in copies:
        copy.wait()
    rows = [place[0, i] for i in range(3)] + [kind[0].astype(F32)]
    atoms = rows[0].shape[1]
    out_ref[...] = jnp.concatenate(
        [row[:, s : s + 128] for s in range(0, atoms, 128) for row in rows], axis=0
    )


def radial_left(radial):
    high = radial.astype(BF16).astype(F32)
    low = radial - high
    top = jnp.concatenate([high, high], axis=1)
    end = jnp.concatenate([low, jnp.zeros_like(low)], axis=1)
    return jnp.concatenate([top, end], axis=0).astype(BF16)


def put_split(value, high_ref, low_ref, *at):
    high, low = split(value)
    high_ref[at] = high
    low_ref[at] = low


def prep_kernel(share, padded, grid, norm, place_ref, *refs):
    sources, outs, scratch = refs[:9], refs[9:25], refs[25:]
    id_ref, count_ref, read_ref = outs[:3]
    (embed_out, left_out, back_out, mix_high, mix_low, turn_high, turn_low, hidden_high, hidden_low,
     hidden_turn_high, hidden_turn_low, charge_pair, weight_ref) = outs[3:]
    embed_ref, radial_ref, mixing_ref, hidden_ref, charge_ref, vec_ref, sems = scratch
    targets = [id_ref, count_ref, read_ref, embed_ref, radial_ref, mixing_ref, hidden_ref,
               charge_ref, vec_ref]
    copies = [
        pltpu.make_async_copy(source, target, sems.at[i])
        for i, (source, target) in enumerate(zip(sources, targets))
    ]
    for copy in copies:
        copy.start()
    for copy in copies:
        copy.wait()
    embed = embed_ref[...]
    embed = jnp.concatenate([embed, jnp.zeros((8 - embed.shape[0], embed.shape[1]), F32)], axis=0)
    embed_out[...] = embedding_stack(embed)
    for layer in range(2):
        for path in range(2):
            radial = radial_ref[layer, path] * norm
            left_out[layer, path] = stacked_left(radial)
            back_out[layer, path] = radial_left(radial)
        scalar, vector = mixing_ref[layer, 0], mixing_ref[layer, 1]
        put_split(jnp.concatenate([scalar.T, vector.T], axis=1), mix_high, mix_low, layer)
        put_split(jnp.concatenate([scalar, 2.0 * vector], axis=0), turn_high, turn_low, layer)
    put_split(hidden_ref[...].T, hidden_high, hidden_low, Ellipsis)
    put_split(hidden_ref[...], hidden_turn_high, hidden_turn_low, Ellipsis)
    charge = charge_ref[...]
    high = charge.astype(BF16).astype(F32)
    charge_pair[0] = high.astype(BF16)
    charge_pair[1] = (charge - high).astype(BF16)
    green_weights(share, padded, grid, place_ref, vec_ref, weight_ref)


def unfold_block(block, atoms):
    parts = atoms // 128
    return jnp.concatenate([block[4 * s : 4 * s + 4] for s in range(parts)], axis=1)


def first_kernel(slots, ids_ref, count_ref, embed_ref, left_ref, mix_high, mix_low, before_ref,
                 column_ref, after_ref, low_ref, basis_ref, slope_ref, unit_ref, sums_ref,
                 gate_ref):
    atoms = low_ref.shape[1]
    ids = ids_ref[...]
    frame = [before_ref, column_ref, after_ref]
    own = unfold_block(column_ref[1], atoms)
    own = jnp.concatenate([own, jnp.zeros_like(own)], axis=0)
    halves = []
    for a, b in OFFSETS:
        block = frame[a + 1][b + 1]
        for s in range(atoms // 128):
            rows = block[4 * s : 4 * s + 4]
            halves.append(
                jnp.concatenate(
                    [rows[0:1] + a * cell_width, rows[1:2] + b * cell_width, rows[2:4], rows],
                    axis=0,
                )
            )
    pieces = []
    for start in range(0, ids.shape[1], 128):
        part = jnp.broadcast_to(ids[:, start : start + 128], (8, 128))
        lane, half = part & 127, part >> 7
        found = jnp.zeros((8, 128), F32)
        for h, rows in enumerate(halves):
            found = jnp.where(half == h, jnp.take_along_axis(rows, lane, axis=1), found)
        pieces.append(found)
    found = jnp.concatenate(pieces, axis=1)
    relative = found - jnp.concatenate([own] * slots, axis=1)
    rel = [relative[i : i + 1] for i in range(3)]
    distance = jnp.sqrt(rel[0] * rel[0] + rel[1] * rel[1] + rel[2] * rel[2] + soften)
    inverse = 1.0 / distance
    order = (lax.broadcasted_iota(jnp.int32, (8, 1), 0) + 1).astype(F32)
    sine, cosine = sin_cos((order * (0.5 / cut_radius)) * distance)
    wave = sine / ((order * (math.pi / cut_radius)) * distance)
    count = count_ref[0]
    live = jnp.concatenate([jnp.where(count > n, 1.0, 0.0) for n in range(slots)], axis=1)
    basis = wave * live
    basis_ref[...] = basis
    slope_ref[...] = (cosine - wave) * (inverse * live)
    kinds = found[3:4]
    unit = jnp.concatenate(
        [r * inverse for r in rel] + [inverse, kinds] + [jnp.zeros_like(kinds)] * 3, axis=0
    )
    unit_ref[...] = unit
    stack = embed_ref[...]
    parts = edge_parts(basis, unit)
    sums = [None] * 4
    for n in range(slots):
        lanes = slice(n * atoms, (n + 1) * atoms)
        feature = embedded(stack, kinds[:, lanes])
        for part in range(4):
            term = weights_of(left_ref, 0, part, parts[part][:, lanes]) * feature
            sums[part] = term if sums[part] is None else sums[part] + term
    step, gate = mixed(sums, mix_high, mix_low, 0)
    low_ref[...] = (embedded(stack, own[3:4]) + step).astype(BF16)
    for part in range(3):
        sums_ref[part] = sums[part + 1]
    gate_ref[...] = gate


def hot_columns(ids, rows):
    place = lax.broadcasted_iota(jnp.int32, (rows, ids.shape[1]), 0)
    return jnp.where(ids == place, 1.0, 0.0).astype(BF16)


def second_near_kernel(slots, ids_ref, basis_ref, unit_ref, left_ref, column_ref, weight_ref,
                       near_ref):
    atoms = column_ref.shape[2]
    parts = edge_parts(basis_ref[...], unit_ref[...])
    source = jnp.concatenate([column_ref[b] for b in range(3)], axis=1)
    for n in range(slots):
        lanes = slice(n * atoms, (n + 1) * atoms)
        for part in range(4):
            weight_ref[part, :, lanes] = weights_of(left_ref, 1, part, parts[part][:, lanes])
        hot = hot_columns(ids_ref[:, lanes] - 3 * atoms, 3 * atoms)
        near_ref[:, lanes] = dot(source, hot)


def second_kernel(slots, ids_ref, weight_ref, near_ref, mix_high, mix_low, hidden_high, hidden_low,
                  turn_high, turn_low, out_ref, charge_ref, cell_ref, before_ref, column_ref,
                  after_ref, feature_ref, sums_ref, gate_ref, packed_ref, full_charge_ref,
                  energy_ref, slope_ref):
    atoms = column_ref.shape[2]
    source = jnp.concatenate(
        [before_ref[b] for b in range(3)] + [after_ref[b] for b in range(3)], axis=1
    )
    sums = [None] * 4
    for n in range(slots):
        lanes = slice(n * atoms, (n + 1) * atoms)
        ids = ids_ref[:, lanes]
        ids = jnp.where(ids >= 6 * atoms, ids - 3 * atoms, jnp.where(ids >= 3 * atoms, -1, ids))
        feature = near_ref[:, lanes] + dot(source, hot_columns(ids, 6 * atoms))
        feature_ref[:, lanes] = feature.astype(BF16)
        for part in range(4):
            term = weight_ref[part, :, lanes] * feature
            sums[part] = term if sums[part] is None else sums[part] + term
    step, gate = mixed(sums, mix_high, mix_low, 1)
    hidden = column_ref[1].astype(F32) + step
    for part in range(3):
        sums_ref[part] = sums[part + 1]
    gate_ref[...] = gate
    charge = dot_split((charge_ref[0], charge_ref[1]), hidden)
    full_charge_ref[...] = charge
    place = unfold_block(cell_ref[1], atoms)[:3]
    high = place.astype(BF16).astype(F32)
    rest = place - high
    middle = rest.astype(BF16).astype(F32)
    zero = jnp.zeros((packed_ref.shape[0] - charge.shape[0] - 9, atoms), F32)
    packed_ref[...] = jnp.concatenate([charge, high, middle, rest - middle, zero], axis=0).astype(
        BF16
    )
    value, slope = silu_pair(dot_split((hidden_high[...], hidden_low[...]), hidden))
    out = out_ref[...].T
    energy_ref[...] = jnp.sum(value * out, axis=0, keepdims=True)
    slope_ref[...] = dot_split((turn_high[...], turn_low[...]), slope * out)


def message_grads(cotangent, gate_ref, sums_ref, high_ref, low_ref, layer):
    pre = cotangent * gate_ref[...]
    both = dot_split((high_ref[layer], low_ref[layer]), pre)
    half = both.shape[0] // 2
    return [both[:half]] + [both[half:] * sums_ref[i] for i in range(3)]


def radial_grad(left, value):
    high, low = split(value)
    both = dot(left, jnp.concatenate([high, low], axis=0))
    half = both.shape[0] // 2
    return both[:half] + both[half:]


def second_back_kernel(slots, scale, grid_x, ids_ref, weight_ref, turn_high, turn_low, charge_ref,
                       sums_ref, gate_ref, full_charge_ref, energy_ref, slope_ref, *refs):
    folds, refs = refs[:grid_x], refs[grid_x:]
    site_ref, long_ref, cotangent_ref, grad_ref, term_ref, before_ref, after_ref = refs
    atoms = gate_ref.shape[1]
    total = folds[0][...].astype(F32)
    for part in folds[1:]:
        total = total + part[...].astype(F32)
    wide = full_charge_ref.shape[0]
    potential = total[:wide] * (2.0 * scale)
    slopes = total[wide : wide + 3] + total[wide + 3 : wide + 6] + total[wide + 6 : wide + 9]
    long_ref[...] = jnp.concatenate(
        [slopes * (2.0 * scale), jnp.zeros((5, atoms), F32)], axis=0
    )
    site_ref[0] = energy_ref[...] + 0.5 * jnp.sum(
        full_charge_ref[...] * potential, axis=0, keepdims=True
    )
    high, low = split(potential)
    turned = ((0,), (0,))
    cotangent = slope_ref[...] + (
        dot(charge_ref[0], high, turned)
        + (dot(charge_ref[0], low, turned) + dot(charge_ref[1], high, turned))
    )
    cotangent_ref[...] = cotangent
    grads = message_grads(cotangent, gate_ref, sums_ref, turn_high, turn_low, 1)
    for part in range(4):
        grad_ref[part] = grads[part]
    for n in range(slots):
        lanes = slice(n * atoms, (n + 1) * atoms)
        term = weight_ref[0, :, lanes] * grads[0]
        for part in range(1, 4):
            term = term + weight_ref[part, :, lanes] * grads[part]
        term_ref[:, lanes] = term.astype(BF16)
    ids = ids_ref[...]
    for side, out_ref in ((0, before_ref), (2, after_ref)):
        for b in range(3):
            hot = hot_columns(ids - (3 * side + b) * atoms, atoms)
            out_ref[b] = dot(term_ref[...], hot, ((1,), (1,))).astype(BF16)


def second_middle_kernel(ids_ref, term_ref, cotangent_ref, middle_ref):
    ids = ids_ref[...]
    atoms = cotangent_ref.shape[1]
    for b in range(3):
        hot = hot_columns(ids - (3 + b) * atoms, atoms)
        grad = dot(term_ref[...], hot, ((1,), (1,)))
        middle_ref[b] = grad + cotangent_ref[...] if b == 1 else grad


def second_edge_kernel(slots, back_ref, feature_ref, grad_ref, edge_ref):
    atoms = grad_ref.shape[2]
    for n in range(slots):
        lanes = slice(n * atoms, (n + 1) * atoms)
        feature = feature_ref[:, lanes].astype(F32)
        for part in range(4):
            edge_ref[8 * part : 8 * part + 8, lanes] = radial_grad(
                back_ref[1, 1 if part else 0], grad_ref[part] * feature
            )


def first_back_kernel(slots, ids_ref, basis_ref, slope_ref, unit_ref, embed_ref, back_ref,
                      turn_high, turn_low, sums_ref, gate_ref, edge_ref, long_ref, middle_ref,
                      *refs):
    from_x, from_y, outs = refs[:2], refs[2:4], refs[4:]
    atoms = gate_ref.shape[1]
    cotangent = middle_ref[1]
    for block in (from_x[0][1], from_x[1][1], from_y[0][...], from_y[1][...]):
        cotangent = cotangent + block.astype(F32)
    grads = message_grads(cotangent, gate_ref, sums_ref, turn_high, turn_low, 0)
    stack = embed_ref[...]
    unit = unit_ref[...]
    kinds = unit[4:5]
    edges = [[] for _ in range(4)]
    for n in range(slots):
        lanes = slice(n * atoms, (n + 1) * atoms)
        feature = embedded(stack, kinds[:, lanes])
        for part in range(4):
            edges[part].append(radial_grad(back_ref[0, 1 if part else 0], grads[part] * feature))
    edges = [
        edge_ref[8 * part : 8 * part + 8] + jnp.concatenate(edges[part], axis=1) for part in range(4)
    ]
    basis = basis_ref[...]
    units = [unit[i : i + 1] for i in range(3)]
    inverse = unit[3:4]
    by_basis = edges[0]
    for i in range(3):
        by_basis = by_basis + edges[i + 1] * units[i]
    by_unit = [jnp.sum(edges[i + 1] * basis, axis=0, keepdims=True) * inverse for i in range(3)]
    by_distance = jnp.sum(by_basis * slope_ref[...], axis=0, keepdims=True)
    for i in range(3):
        by_distance = by_distance - by_unit[i] * units[i]
    moves = [by_unit[i] + by_distance * units[i] for i in range(3)]
    zero = jnp.zeros_like(moves[0])
    move = jnp.concatenate(moves + [zero] * 5, axis=0)
    own = long_ref[...]
    for n in range(slots):
        own = own - move[:, n * atoms : (n + 1) * atoms]
    ids = ids_ref[...]
    lane_hot = hot_columns(ids & 127, 128)
    half = ids >> 7
    high = move.astype(BF16).astype(F32)
    both = jnp.concatenate([high, move - high], axis=0)
    per_cell = atoms // 128
    rows = jnp.concatenate(
        [jnp.where(half == h, both, 0.0).astype(BF16) for h in range(9 * per_cell)], axis=0
    )
    spread = dot(rows, lane_hot, ((1,), (1,)))
    for cell in range(9):
        found = []
        for h in range(cell * per_cell, (cell + 1) * per_cell):
            found.append(spread[16 * h : 16 * h + 8] + spread[16 * h + 8 : 16 * h + 16])
        grad = jnp.concatenate(found, axis=1)
        if cell == CENTRE:
            grad = own + grad
        outs[cell // 3][cell % 3] = grad


def pair_counts(parts):
    total = WAVE_REACH + WAVE_REACH * (2 * WAVE_REACH + 1)
    share = -(-total // parts)
    return total, share, -(-share // 16) * 16


def pair_vectors(slot, share, part):
    side = 2 * WAVE_REACH + 1
    total = WAVE_REACH + WAVE_REACH * side
    index = slot + part.astype(F32) * share
    later = index - WAVE_REACH
    row = jnp.floor((later + 0.5) * (1.0 / side))
    first = index < WAVE_REACH
    kx = jnp.where(first, 0.0, row + 1.0)
    ky = jnp.where(first, index + 1.0, later - row * side - WAVE_REACH)
    valid = jnp.where((slot < share) & (index < total), 1.0, 0.0)
    return kx, ky, valid


def count_up(rows):
    return lax.broadcasted_iota(jnp.int32, (rows, 1), 0).astype(F32)


def green_weights(share, padded, grid, place_ref, vec_ref, weight_ref):
    grid_x, grid_y = grid
    turn = 2.0 * math.pi
    side = 2 * WAVE_REACH + 1
    top = side * side * side - 1
    vec = vec_ref[...].astype(F32) + WAVE_REACH
    code = (vec[0:1] * side + vec[1:2]) * side + vec[2:3]
    code = jnp.maximum(code, top - code)
    span = 8 * share
    row = count_up(span)
    slot = jnp.floor(row * 0.125)
    height = row - 8.0 * slot + 1.0
    flat = count_up(padded)
    slot = jnp.concatenate([slot, slot, flat], axis=0)
    kz = jnp.concatenate([height, -height, jnp.zeros_like(flat)], axis=0)
    kx, ky, valid = pair_vectors(slot, share, place_ref[0])
    own = ((kx + WAVE_REACH) * side + ky + WAVE_REACH) * side + kz + WAVE_REACH
    seen = jnp.zeros((own.shape[0], 128), F32)
    for start in range(0, code.shape[1], 128):
        seen = seen + jnp.where(own == code[:, start : start + 128], 1.0, 0.0)
    count = jnp.sum(seen, axis=1, keepdims=True) * valid
    sq = (
        (kx * (turn / (grid_x * cell_width))) ** 2
        + (ky * (turn / (grid_y * cell_width))) ** 2
        + (kz * (turn / box_height)) ** 2
    )
    green = jnp.exp(-smear_width * sq) / (sq + screen * screen) * count
    weight_ref[...] = jnp.broadcast_to(green, weight_ref.shape)


def basis_rows(share, ca, sa, cb, sb):
    cc, ss, sc, cs = [], [], [], []
    for p in range(share):
        c, s = ca[p : p + 1], sa[p : p + 1]
        cc.append(c * cb)
        ss.append(s * sb)
        sc.append(s * cb)
        cs.append(c * sb)
    return cc, ss, sc, cs


def unpack_rows(block):
    half = block.shape[1] // 2
    return jnp.concatenate([block[:, :half], block[:, half:]], axis=0)


def pack_rows(block):
    half = block.shape[0] // 2
    return jnp.concatenate([block[:half], block[half:]], axis=1)


def structure_kernel(share, padded, grid, wide, place_ref, *refs):
    grid_x, grid_y = grid
    blocks, (ca_ref, sa_ref, cb_ref, sb_ref, out_ref) = refs[:grid_x], refs[grid_x:]
    col = place_ref[1].astype(F32) * (1.0 / grid_y)
    kx, ky, _ = pair_vectors(count_up(padded), share, place_ref[0])
    kz = count_up(8) + 1.0
    total = None
    for d in range(grid_x):
        block = blocks[d][...]
        charge = block[:wide]
        atoms = charge.shape[1]
        pieces = block[wide:].astype(F32)
        place = pieces[0:3] + (pieces[3:6] + pieces[6:9])
        row = lax.rem(place_ref[0] + d, grid_x).astype(F32) * (1.0 / grid_x)
        x = place[0:1] * (1.0 / (grid_x * cell_width)) + row
        y = place[1:2] * (1.0 / (grid_y * cell_width)) + col
        sa, ca = sin_cos(kx * x + ky * y)
        sb, cb = sin_cos(kz * (place[2:3] * (1.0 / box_height)))
        lanes = pl.ds(d * atoms, atoms)
        ca_ref[:, lanes] = ca
        sa_ref[:, lanes] = sa
        cb_ref[:, lanes] = cb
        sb_ref[:, lanes] = sb
        cc, ss, sc, cs = basis_rows(share, ca, sa, cb, sb)
        high, low = split(jnp.concatenate(cc + ss + sc + cs + [ca, sa], axis=0))
        term = dot(high, charge, ((1,), (1,))) + dot(low, charge, ((1,), (1,)))
        total = term if total is None else total + term
    out_ref[...] = pack_rows(total).astype(BF16)


def fold_kernel(share, padded, grid, wide, place_ref, ca_ref, sa_ref, cb_ref, sb_ref, weight_ref,
                *refs):
    grid_x, grid_y = grid
    blocks, parts, outs = refs[:grid_x], refs[grid_x : grid_x + grid_y], refs[grid_x + grid_y :]
    turn = 2.0 * math.pi
    packed = parts[0][...].astype(F32)
    for part in parts[1:]:
        packed = packed + part[...].astype(F32)
    struct = unpack_rows(packed)
    span = 8 * share
    cc, ss, sc, cs = (struct[i * span : (i + 1) * span] for i in range(4))
    weight = weight_ref[:, :wide]
    plus, minus, flat = weight[:span], weight[span : 2 * span], weight[2 * span :]
    re_plus, im_plus = plus * (cc - ss), plus * (sc + cs)
    re_minus, im_minus = minus * (cc + ss), minus * (sc - cs)
    rows = jnp.concatenate(
        [
            re_plus + re_minus,
            re_minus - re_plus,
            im_plus + im_minus,
            im_plus - im_minus,
            flat * struct[4 * span : 4 * span + padded],
            flat * struct[4 * span + padded :],
        ],
        axis=0,
    )
    row_high, row_low = split(rows)
    row_pair = jnp.concatenate([row_high, row_low], axis=1)
    turned = rows.T
    t_high, t_low = split(turned)
    t_both = jnp.concatenate([t_high, t_low], axis=0)
    kx, ky, _ = pair_vectors(count_up(padded), share, place_ref[0])
    kx = kx * (turn / (grid_x * cell_width))
    ky = ky * (turn / (grid_y * cell_width))
    kz = (count_up(8) + 1.0) * (turn / box_height)
    for d in range(grid_x):
        charge = blocks[d][:wide]
        atoms = charge.shape[1]
        lanes = pl.ds(d * atoms, atoms)
        ca, sa, cb, sb = ca_ref[:, lanes], sa_ref[:, lanes], cb_ref[:, lanes], sb_ref[:, lanes]
        bcc, bss, bsc, bcs = basis_rows(share, ca, sa, cb, sb)
        high, low = split(jnp.concatenate(bcc + bss + bsc + bcs + [ca, sa], axis=0))
        both = dot(t_both, high)
        pot = both[:wide] + both[wide:] + dot(t_high, low)
        proj = dot(row_pair, jnp.concatenate([charge, charge], axis=0))
        by_x = jnp.zeros((8, atoms), jnp.float32)
        by_y = jnp.zeros((8, atoms), jnp.float32)
        by_z = jnp.zeros((8, atoms), jnp.float32)
        for p in range(share):
            pcc, pss, psc, pcs = (
                proj[i * span + 8 * p : i * span + 8 * p + 8] for i in range(4)
            )
            slope = bcs[p] * pss - bsc[p] * pcc + bcc[p] * psc - bss[p] * pcs
            by_x = by_x + kx[p : p + 1] * slope
            by_y = by_y + ky[p : p + 1] * slope
            by_z = by_z + (bsc[p] * pss - bcs[p] * pcc - bss[p] * psc + bcc[p] * pcs)
        flat_slope = ca * proj[4 * span + padded :] - sa * proj[4 * span : 4 * span + padded]
        grad_x = jnp.sum(by_x, axis=0, keepdims=True) + jnp.sum(kx * flat_slope, axis=0, keepdims=True)
        grad_y = jnp.sum(by_y, axis=0, keepdims=True) + jnp.sum(ky * flat_slope, axis=0, keepdims=True)
        grad_z = jnp.sum(kz * by_z, axis=0, keepdims=True)
        slopes = jnp.concatenate([grad_x, grad_y, grad_z], axis=0)
        high = slopes.astype(BF16).astype(F32)
        rest = slopes - high
        middle = rest.astype(BF16).astype(F32)
        zero = jnp.zeros((outs[d].shape[0] - wide - 9, atoms), F32)
        outs[d][...] = jnp.concatenate([pot, high, middle, rest - middle, zero], axis=0).astype(
            BF16
        )


def per_device(
    positions,
    species,
    neighbours,
    counts,
    species_embed,
    radial,
    mixing,
    read_hidden,
    read_out,
    charge_map,
    wavevectors,
):
    atoms = positions.shape[3]
    slots = neighbours.shape[3]
    features, lat_width = charge_map.shape
    wave_count = wavevectors.shape[1]
    grid = lax.axis_size("gx"), lax.axis_size("gy")
    grid_x, grid_y = grid
    edges = slots * atoms
    scale = 1.0 / math.sqrt(wave_count * lat_width * atoms * grid_x * grid_y)
    place = jnp.stack([lax.axis_index("gx"), lax.axis_index("gy")]).astype(jnp.int32)
    _, share, padded = pair_counts(grid_x)
    ids = neighbours.transpose(0, 3, 1, 2).reshape(1, edges)
    dma = pltpu.SemaphoreType.DMA
    shown = positions.transpose(0, 2, 1, 3)

    (own,) = run(
        pack_kernel,
        [shape(4 * atoms // 128, 128)],
        [shown, species],
        scratch=[
            pltpu.VMEM(shown.shape, F32),
            pltpu.VMEM(species.shape, jnp.int32),
            dma((2,)),
        ],
        hbm=2,
        name="pack",
    )
    cells = around(own)

    pair = [shape(features, features, dtype=BF16)] * 2
    (ids, counts, read_out, embed, left, back, mix_high, mix_low, turn_high, turn_low, hidden_high,
     hidden_low, hidden_turn_high, hidden_turn_low, charge_pair, weight) = run(
        functools.partial(prep_kernel, share, padded, grid, 1.0 / math.sqrt(slots)),
        [
            shape(1, edges, dtype=jnp.int32),
            shape(*counts.shape, dtype=jnp.int32),
            shape(1, features),
            shape(features, 32, dtype=BF16),
            shape(2, 2, features, 32, dtype=BF16),
            shape(2, 2, 16, 2 * features, dtype=BF16),
            shape(2, features, 2 * features, dtype=BF16),
            shape(2, features, 2 * features, dtype=BF16),
            shape(2, 2 * features, features, dtype=BF16),
            shape(2, 2 * features, features, dtype=BF16),
        ]
        + pair + pair
        + [
            shape(2, lat_width, features, dtype=BF16),
            shape(16 * share + padded, 128),
        ],
        [place, ids, counts, read_out[None, :], species_embed, radial, mixing, read_hidden,
         charge_map.T, wavevectors],
        scratch=[
            pltpu.VMEM(species_embed.shape, F32),
            pltpu.VMEM(radial.shape, F32),
            pltpu.VMEM(mixing.shape, F32),
            pltpu.VMEM(read_hidden.shape, F32),
            pltpu.VMEM((lat_width, features), F32),
            pltpu.VMEM(wavevectors.shape, jnp.int32),
            dma((9,)),
        ],
        smem=1,
        hbm=9,
        name="prep",
    )
    low, basis, slope, unit, sums_one, gate_one = run(
        functools.partial(first_kernel, slots),
        [
            shape(features, atoms, dtype=BF16),
            shape(8, edges),
            shape(8, edges),
            shape(8, edges),
            shape(3, features, atoms),
            shape(features, atoms),
        ],
        [ids, counts, embed, left, mix_high, mix_low] + cells,
        name="first",
    )
    hidden = around(low)
    edge_weights, near = run(
        functools.partial(second_near_kernel, slots),
        [shape(4, features, edges), shape(features, edges)],
        [ids, basis, unit, left, hidden[1]],
        flops=2_000_000_000,
        name="second_near",
    )
    block_rows = -(-(lat_width + 9) // 16) * 16
    feature, sums_two, gate_two, packed, charge, energy, energy_slope = run(
        functools.partial(second_kernel, slots),
        [
            shape(features, edges, dtype=BF16),
            shape(3, features, atoms),
            shape(features, atoms),
            shape(block_rows, atoms, dtype=BF16),
            shape(lat_width, atoms),
            shape(1, atoms),
            shape(features, atoms),
        ],
        [ids, edge_weights, near, mix_high, mix_low, hidden_high, hidden_low, hidden_turn_high,
         hidden_turn_low, read_out, charge_pair, cells[1]] + hidden,
        name="second",
    )
    charges = [packed] + [shifted(packed, d, 0) for d in range(1, grid_x)]
    span = grid_x * atoms
    rows = 32 * share + 2 * padded
    *phases, part = run(
        functools.partial(structure_kernel, share, padded, grid, lat_width),
        [
            shape(padded, span),
            shape(padded, span),
            shape(8, span),
            shape(8, span),
            shape(rows // 2, 2 * lat_width, dtype=BF16),
        ],
        [place] + charges,
        smem=1,
        name="structure",
    )
    parts = [part] + [shifted(part, 0, d) for d in range(1, grid_y)]
    folds = run(
        functools.partial(fold_kernel, share, padded, grid, lat_width),
        [shape(block_rows, atoms, dtype=BF16)] * grid_x,
        [place] + phases + [weight] + charges + parts,
        smem=1,
        name="fold",
    )
    folds = [folds[0]] + [shifted(folds[d], -d, 0) for d in range(1, grid_x)]

    site, long, cotangent, grads, term, before, after = run(
        functools.partial(second_back_kernel, slots, scale, grid_x),
        [
            shape(1, 1, atoms),
            shape(8, atoms),
            shape(features, atoms),
            shape(4, features, atoms),
            shape(features, edges, dtype=BF16),
            shape(3, features, atoms, dtype=BF16),
            shape(3, features, atoms, dtype=BF16),
        ],
        [ids, edge_weights, turn_high, turn_low, charge_pair, sums_two, gate_two, charge, energy,
         energy_slope] + folds,
        name="second_back",
    )
    from_x = [shifted(after, -1, 0), shifted(before, 1, 0)]
    (middle,) = run(
        second_middle_kernel,
        [shape(3, features, atoms)],
        [ids, term, cotangent],
        flops=1_000_000_000,
        name="second_middle",
    )
    sides = [
        (middle[b] + from_x[0][b].astype(F32) + from_x[1][b].astype(F32)).astype(BF16)
        for b in (0, 2)
    ]
    from_y = [shifted(sides[1], 0, -1), shifted(sides[0], 0, 1)]
    (edge,) = run(
        functools.partial(second_edge_kernel, slots),
        [shape(32, edges)],
        [back, feature, grads],
        flops=1_000_000_000,
        name="second_edge",
    )
    before, middle, after = run(
        functools.partial(first_back_kernel, slots),
        [shape(3, 8, atoms)] * 3,
        [ids, basis, slope, unit, embed, back, turn_high, turn_low, sums_one, gate_one, edge, long,
         middle] + from_x + from_y,
        name="first_back",
    )
    total = middle + shifted(after, -1, 0) + shifted(before, 1, 0)
    total = total[1] + shifted(total[2], 0, -1) + shifted(total[0], 0, 1)
    forces = -total[None, :3, None, :]
    return (forces.transpose(0, 2, 1, 3), site)


def solution(mesh):
    in_specs = (
        P("gx", "gy", None, None),
        P("gx", "gy", None),
        P("gx", "gy", None, None),
        P("gx", "gy", None),
        P(),
        P(),
        P(),
        P(),
        P(),
        P(),
        P(),
    )
    out_specs = (P("gx", "gy", None, None), P("gx", "gy", None))
    return jax.shard_map(
        per_device, mesh=mesh, in_specs=in_specs, out_specs=out_specs, check_vma=False
    )
```

time: 135 us -> 111 us (0.82)
  blocking collectives: 31.8 us -> 0 us
  starting transfers between devices: 29.2 us -> 40.4 us
  local copies, waits for them, and re-layouts: 10.5 us -> 8.77 us
  waiting for transfers between devices: 37 us -> 35.3 us
    all_to_all x2 -> x0, blocking collectives: 31.8 us -> none  [exchanged(): return lax.all_to_all(blocks, axis, 0, 0)]
    ppermute x12 -> x33, starting transfers between devices: 15.7 us -> 40.4 us  [shifted(): return lax.ppermute(block, ('gx', 'gy'), route)]
    all_to_all x3 -> x0, starting transfers between devices: 13.5 us -> none  [exchanged(): return lax.all_to_all(blocks, axis, 0, 0)]
    all_to_all x3 -> x0, waiting for transfers between devices: 12 us -> none  [exchanged(): return lax.all_to_all(blocks, axis, 0, 0)]
    ppermute x12 -> x33, waiting for transfers between devices: 24.9 us -> 35.3 us  [shifted(): return lax.ppermute(block, ('gx', 'gy'), route)]
    squeeze x2 -> x0, local copies, waits for them, and re-layouts: 1.64 us -> none  [the longest x1 0.93 us: per_device(): lax.dynamic_index_in_dim(jnp.asarray(wave_np), place[0], 0, keepdims=False)]
    unnamed x32 -> x23, local copies, waits for them, and re-layouts: 8.24 us -> 8.77 us
    pallas_call x9 -> x11, Pallas kernels: 25.2 us -> 24.9 us  [run(): pl.pallas_call(kernel, out_shape=outs, in_specs=specs, out_specs=[whole()...]
  transfers between devices with their start and end apart: 15 -> 33, of which waited for: 12 -> 22; matrix products, arithmetic and copies ran while one was open for 3% -> 0% of each run, Pallas kernels for 2% -> 6%
where the time goes in v4:
time: 111 us; the launch traced here: 110 us
  starting transfers between devices  40.4 us (36%)
  waiting for transfers between devices  35.3 us (32%)
  Pallas kernels  24.9 us (22%)
  local copies, waits for them, and re-layouts  8.77 us (8%)
    ppermute x33, starting transfers between devices, shifted(): return lax.ppermute(block, ('gx', 'gy'), route)  40.4 us
    ppermute x33, waiting for transfers between devices, shifted(): return lax.ppermute(block, ('gx', 'gy'), route)  35.3 us
    pallas_call x11, Pallas kernels, run(): pl.pallas_call(kernel, out_shape=outs, in_specs=specs, out_specs=[whole()...  24.9 us
    unnamed x23, local copies, waits for them, and re-layouts  8.77 us
  transfers between devices with their start and end apart: 33, of which 22 were waited for; matrix products, arithmetic and copies ran while one was open for 0% of the time, Pallas kernels for 6%

profile of v4, /device:TPU:0, one launch (start us, length us, event | category | flops | bytes accessed | tf_op | source)
XLA Modules:
  0.0 110.2 jit_solution(18287848144561534044)
XLA Ops:
  0.6 0.7 copy-done.9
  1.3 0.7 copy-done.10
  2.0 3.9 %collective-permute-start.1 = (f32[8,128]{1,0:T(8,128)S(1)}, f32[8,128]{1,0:T(8,128)S(1)}, u32[]{:S(2)}, u32[]{:S(2)}) collective-permute-start(f32[8,128]{1,0:T(8,128)S(1)} %pack.1), channel_id=1, source_target_pairs={{1,0},{2,1},{3,2},{0,3},{5,4},{6,5},{7,6},{4,7},{9,8},{10,9},{11,1... | collective-permute-start | bytes 12296 | tf_op jit(solution)/shard_map/ppermute | solution.py:32
  6.0 1.3 %collective-permute-done.1 = f32[8,128]{1,0:T(8,128)S(1)} collective-permute-done((f32[8,128]{1,0:T(8,128)S(1)}, f32[8,128]{1,0:T(8,128)S(1)}, u32[]{:S(2)}, u32[]{:S(2)}) %collective-permute-start.1) | collective-permute-done | bytes 4128 | tf_op jit(solution)/shard_map/ppermute | solution.py:32
  7.3 3.2 %collective-permute-done = f32[8,128]{1,0:T(8,128)S(1)} collective-permute-done((f32[8,128]{1,0:T(8,128)S(1)}, f32[8,128]{1,0:T(8,128)S(1)}, u32[]{:S(2)}, u32[]{:S(2)}) %collective-permute-start) | collective-permute-done | bytes 4128 | tf_op jit(solution)/shard_map/ppermute | solution.py:32
  10.5 1.6 %collective-permute-start.3 = (f32[3,8,128]{2,1,0:T(8,128)S(1)}, f32[3,8,128]{2,1,0:T(8,128)S(1)}, u32[]{:S(2)}, u32[]{:S(2)}) collective-permute-start(f32[3,8,128]{2,1,0:T(8,128)S(1)} %pad_maximum_fusion.1.column_ref.cell_ref), channel_id=1, source_target_pairs={{4,0},{5,1},{6,2},{7,3},{8,4},{9,5},{10,6},{11,7},{12,8},{13,9},{1... | collective-permute-start | bytes 36872 | tf_op jit(solution)/shard_map/ppermute | solution.py:32
  12.2 0.9 copy-done
  13.1 0.8 copy-done.1
  14.0 0.8 copy-done.2
  14.8 0.8 copy-done.3
  15.6 0.7 copy-done.4
  16.3 0.7 copy-done.5
  17.0 0.7 copy-done.6
  17.7 0.7 copy-done.7
  18.4 0.7 copy-done.8
  19.0 1.9 %prep.1 = (s32[1,3072]{1,0:T(1,128)S(1)}, s32[1,1,256]{2,1,0:T(1,128)S(1)}, f32[1,128]{1,0:T(1,128)S(1)}, bf16[128,32]{1,0:T(8,128)(2,1)S(1)}, bf16[2,2,128,32]{...) custom-call(s32[2]{0:T(128)S(1)} %pad_add_fusion.place_ref, ...), custom_call_target="tpu_custom_call" | custom-call | flops 10000000 | bytes 1000000 | tf_op jit(solution)/shard_map/prep/pallas_call | solution.py:48
  21.0 1.6 %first.1 = (bf16[128,256]{1,0:T(8,128)(2,1)S(1)}, f32[8,3072]{1,0:T(8,128)S(1)}, f32[8,3072]{1,0:T(8,128)S(1)}, f32[8,3072]{1,0:T(8,128)S(1)}, f32[3,128,256]{2,1,0:T(8,128)S(1)}, /*index=5*/f32[128,256]{1,0:T(8,128)S(1)}) custom-call(s32[1,3072]{1,0:T(1,128)S(1)} %get-tuple-element.56.ids_ref, s32[1,1,256]{2,1,0:T(1,128)S(1)} %get-tuple-element.57.count_ref, ...), custom_call_target="tpu_custom_call" | custom-call | flops 10000000 | bytes 1000000 | tf_op jit(solution)/shard_map/first/pallas_call | solution.py:48
  22.6 0.3 collective-permute-start.5
  22.9 1.7 %collective-permute-start.4 = (bf16[128,256]{1,0:T(8,128)(2,1)S(1)}, bf16[128,256]{1,0:T(8,128)(2,1)S(1)}, u32[]{:S(2)}, u32[]{:S(2)}) collective-permute-start(bf16[128,256]{1,0:T(8,128)(2,1)S(1)} %get-tuple-element.70), channel_id=1, source_target_pairs={{3,0},{0,1},{1,2},{2,3},{7,4},{4,5},{5,6},{6,7},{11,8},{8,9},{9,10... | collective-permute-start | bytes 196616 | tf_op jit(solution)/shard_map/ppermute | solution.py:32
  24.7 2.7 %collective-permute-done.5 = bf16[128,256]{1,0:T(8,128)(2,1)S(1)} collective-permute-done((bf16[128,256]{1,0:T(8,128)(2,1)S(1)}, bf16[128,256]{1,0:T(8,128)(2,1)S(1)}, u32[]{:S(2)}, u32[]{:S(2)}) %collective-permute-start.5) | collective-permute-done | bytes 65568 | tf_op jit(solution)/shard_map/ppermute | solution.py:32
  27.4 0.8 collective-permute-done.4
  28.3 2.7 %collective-permute-start.7 = (bf16[3,128,256]{2,1,0:T(8,128)(2,1)S(1)}, bf16[3,128,256]{2,1,0:T(8,128)(2,1)S(1)}, u32[]{:S(2)}, u32[]{:S(2)}) collective-permute-start(bf16[3,128,256]{2,1,0:T(8,128)(2,1)S(1)} %pad_maximum_fusion.column_ref), channel_id=1, source_target_pairs={{4,0},{5,1},{6,2},{7,3},{8,4},{9,5},{10,6},{11,7},{12,8},{13,9},{1... | collective-permute-start | bytes 589832 | tf_op jit(solution)/shard_map/ppermute | solution.py:32
  31.0 1.7 %second_near.1 = (f32[4,128,3072]{2,1,0:T(8,128)S(1)}, f32[128,3072]{1,0:T(8,128)S(1)}) custom-call(s32[1,3072]{1,0:T(1,128)S(1)} %get-tuple-element.56.ids_ref, f32[8,3072]{1,0:T(8,128)S(1)} %get-tuple-element.62.basis_ref, f32[8,3072]{1,0:T(8,128)S(1)} %get-tuple-element.64.unit_ref, bf16[2,2,128,32]{3,2,1,0:T(8,128)(2,1)S(1)} %get-tuple-element.59.left_ref, ...), custom_call_target="tpu_custom_call" | custom-call | flops 2000000000 | bytes 1000000 | tf_op jit(solution)/shard_map/second_near/pallas_call | solution.py:48
  32.7 1.5 %collective-permute-done.7.after_ref = bf16[3,128,256]{2,1,0:T(8,128)(2,1)S(1)} collective-permute-done((bf16[3,128,256]{2,1,0:T(8,128)(2,1)S(1)}, bf16[3,128,256]{2,1,0:T(8,128)(2,1)S(1)}, u32[]{:S(2)}, u32[]{:S(2)}) %collective-permute-start.7) | collective-permute-done | bytes 196640 | tf_op jit(solution)/shard_map/ppermute | solution.py:32
  34.3 3.6 %collective-permute-done.6.before_ref = bf16[3,128,256]{2,1,0:T(8,128)(2,1)S(1)} collective-permute-done((bf16[3,128,256]{2,1,0:T(8,128)(2,1)S(1)}, bf16[3,128,256]{2,1,0:T(8,128)(2,1)S(1)}, u32[]{:S(2)}, u32[]{:S(2)}) %collective-permute-start.6) | collective-permute-done | bytes 196640 | tf_op jit(solution)/shard_map/ppermute | solution.py:32
  37.9 3.3 %second.1 = (bf16[128,3072]{1,0:T(8,128)(2,1)S(1)}, f32[3,128,256]{2,1,0:T(8,128)S(1)}, f32[128,256]{1,0:T(8,128)S(1)}, bf16[80,256]{1,0:T(8,128)(2,1)S(1)}, f32...) custom-call(s32[1,3072]{1,0:T(1,128)S(1)} %get-tuple-element.56.ids_ref, ...), custom_call_target="tpu_custom_call" | custom-call | flops 10000000 | bytes 1000000 | tf_op jit(solution)/shard_map/second/pallas_call | solution.py:48
  41.3 1.3 %collective-permute-start.12 = (bf16[80,256]{1,0:T(8,128)(2,1)S(1)}, bf16[80,256]{1,0:T(8,128)(2,1)S(1)}, u32[]{:S(2)}, u32[]{:S(2)}) collective-permute-start(bf16[80,256]{1,0:T(8,128)(2,1)S(1)} %get-tuple-element.85.refs_0_), channel_id=1, source_target_pairs={{20,0},{21,1},{22,2},{23,3},{24,4},{25,5},{26,6},{27,7},{28,8},{29... | collective-permute-start | bytes 122888 | tf_op jit(solution)/shard_map/ppermute | solution.py:32
  42.6 2.7 %collective-permute-start.11 = (bf16[80,256]{1,0:T(8,128)(2,1)S(1)}, bf16[80,256]{1,0:T(8,128)(2,1)S(1)}, u32[]{:S(2)}, u32[]{:S(2)}) collective-permute-start(bf16[80,256]{1,0:T(8,128)(2,1)S(1)} %get-tuple-element.85.refs_0_), channel_id=1, source_target_pairs={{16,0},{17,1},{18,2},{19,3},{20,4},{21,5},{22,6},{23,7},{24,8},{25... | collective-permute-start | bytes 122888 | tf_op jit(solution)/shard_map/ppermute | solution.py:32
  45.4 1.1 collective-permute-done.14.refs_7_
  46.4 1.6 %collective-permute-start.9 = (bf16[80,256]{1,0:T(8,128)(2,1)S(1)}, bf16[80,256]{1,0:T(8,128)(2,1)S(1)}, u32[]{:S(2)}, u32[]{:S(2)}) collective-permute-start(bf16[80,256]{1,0:T(8,128)(2,1)S(1)} %get-tuple-element.85.refs_0_), channel_id=1, source_target_pairs={{8,0},{9,1},{10,2},{11,3},{12,4},{13,5},{14,6},{15,7},{16,8},{17,9... | collective-permute-start | bytes 122888 | tf_op jit(solution)/shard_map/ppermute | solution.py:32
  48.1 1.4 %collective-permute-done.12.refs_5_ = bf16[80,256]{1,0:T(8,128)(2,1)S(1)} collective-permute-done((bf16[80,256]{1,0:T(8,128)(2,1)S(1)}, bf16[80,256]{1,0:T(8,128)(2,1)S(1)}, u32[]{:S(2)}, u32[]{:S(2)}) %collective-permute-start.12) | collective-permute-done | bytes 40992 | tf_op jit(solution)/shard_map/ppermute | solution.py:32
  49.7 1.2 %collective-permute-done.9.refs_2_ = bf16[80,256]{1,0:T(8,128)(2,1)S(1)} collective-permute-done((bf16[80,256]{1,0:T(8,128)(2,1)S(1)}, bf16[80,256]{1,0:T(8,128)(2,1)S(1)}, u32[]{:S(2)}, u32[]{:S(2)}) %collective-permute-start.9) | collective-permute-done | bytes 40992 | tf_op jit(solution)/shard_map/ppermute | solution.py:32
  50.8 2.5 %structure.1 = (f32[32,2048]{1,0:T(8,128)S(1)}, f32[32,2048]{1,0:T(8,128)S(1)}, f32[8,2048]{1,0:T(8,128)S(1)}, f32[8,2048]{1,0:T(8,128)S(1)}, bf16[320,128]{1,0:T(8,128)(2,1)S(1)}) custom-call(s32[2]{0:T(128)S(1)} %pad_add_fusion.place_ref, bf16[80,256]{1,0:T(8,128)(2,1)S(1)} %get-tuple-element.85.refs_0_, ...), custom_call_target="tpu_custom_call" | custom-call | flops 10000000 | bytes 1000000 | tf_op jit(solution)/shard_map/structure/pallas_call | solution.py:48
  53.4 0.8 collective-permute-start.17
  54.2 0.8 collective-permute-start.16
  55.0 2.9 %collective-permute-start.15 = (bf16[320,128]{1,0:T(8,128)(2,1)S(1)}, bf16[320,128]{1,0:T(8,128)(2,1)S(1)}, u32[]{:S(2)}, u32[]{:S(2)}) collective-permute-start(bf16[320,128]{1,0:T(8,128)(2,1)S(1)} %get-tuple-element.91.refs_8_), channel_id=1, source_target_pairs={{1,0},{2,1},{3,2},{0,3},{5,4},{6,5},{7,6},{4,7},{9,8},{10,9},{11,1... | collective-permute-start | bytes 245768 | tf_op jit(solution)/shard_map/ppermute | solution.py:32
  57.9 1.8 %collective-permute-done.17.refs_11_ = bf16[320,128]{1,0:T(8,128)(2,1)S(1)} collective-permute-done((bf16[320,128]{1,0:T(8,128)(2,1)S(1)}, bf16[320,128]{1,0:T(8,128)(2,1)S(1)}, u32[]{:S(2)}, u32[]{:S(2)}) %collective-permute-start.17) | collective-permute-done | bytes 81952 | tf_op jit(solution)/shard_map/ppermute | solution.py:32
  59.7 1.3 %collective-permute-done.16.refs_10_ = bf16[320,128]{1,0:T(8,128)(2,1)S(1)} collective-permute-done((bf16[320,128]{1,0:T(8,128)(2,1)S(1)}, bf16[320,128]{1,0:T(8,128)(2,1)S(1)}, u32[]{:S(2)}, u32[]{:S(2)}) %collective-permute-start.16) | collective-permute-done | bytes 81952 | tf_op jit(solution)/shard_map/ppermute | solution.py:32
  61.0 0.5 collective-permute-done.15.refs_9_
  61.5 3.0 %fold.1 = (bf16[80,256]{1,0:T(8,128)(2,1)S(1)}, bf16[80,256]{1,0:T(8,128)(2,1)S(1)}, bf16[80,256]{1,0:T(8,128)(2,1)S(1)}, bf16[80,256]{1,0:T(8,128)(2,1)S(1)}, b...) custom-call(s32[2]{0:T(128)S(1)} %pad_add_fusion.place_ref, ...), custom_call_target="tpu_custom_call" | custom-call | flops 10000000 | bytes 1000000 | tf_op jit(solution)/shard_map/fold/pallas_call | solution.py:48
  64.7 1.6 %collective-permute-start.19 = (bf16[80,256]{1,0:T(8,128)(2,1)S(1)}, bf16[80,256]{1,0:T(8,128)(2,1)S(1)}, u32[]{:S(2)}, u32[]{:S(2)}) collective-permute-start(bf16[80,256]{1,0:T(8,128)(2,1)S(1)} %get-tuple-element.94), channel_id=1, source_target_pairs={{24,0},{25,1},{26,2},{27,3},{28,4},{29,5},{30,6},{31,7},{0,8},{1,9... | collective-permute-start | bytes 122888 | tf_op jit(solution)/shard_map/ppermute | solution.py:32
  66.2 1.4 %collective-permute-start.20 = (bf16[80,256]{1,0:T(8,128)(2,1)S(1)}, bf16[80,256]{1,0:T(8,128)(2,1)S(1)}, u32[]{:S(2)}, u32[]{:S(2)}) collective-permute-start(bf16[80,256]{1,0:T(8,128)(2,1)S(1)} %get-tuple-element.95), channel_id=1, source_target_pairs={{20,0},{21,1},{22,2},{23,3},{24,4},{25,5},{26,6},{27,7},{28,8},{29... | collective-permute-start | bytes 122888 | tf_op jit(solution)/shard_map/ppermute | solution.py:32
  67.7 2.3 %collective-permute-start.21 = (bf16[80,256]{1,0:T(8,128)(2,1)S(1)}, bf16[80,256]{1,0:T(8,128)(2,1)S(1)}, u32[]{:S(2)}, u32[]{:S(2)}) collective-permute-start(bf16[80,256]{1,0:T(8,128)(2,1)S(1)} %get-tuple-element.96), channel_id=1, source_target_pairs={{16,0},{17,1},{18,2},{19,3},{20,4},{21,5},{22,6},{23,7},{24,8},{25... | collective-permute-start | bytes 122888 | tf_op jit(solution)/shard_map/ppermute | solution.py:32
  70.1 2.0 %collective-permute-start.23 = (bf16[80,256]{1,0:T(8,128)(2,1)S(1)}, bf16[80,256]{1,0:T(8,128)(2,1)S(1)}, u32[]{:S(2)}, u32[]{:S(2)}) collective-permute-start(bf16[80,256]{1,0:T(8,128)(2,1)S(1)} %get-tuple-element.98), channel_id=1, source_target_pairs={{8,0},{9,1},{10,2},{11,3},{12,4},{13,5},{14,6},{15,7},{16,8},{17,9... | collective-permute-start | bytes 122888 | tf_op jit(solution)/shard_map/ppermute | solution.py:32
  72.1 0.6 collective-permute-start.24
  72.8 1.4 %collective-permute-done.21.refs_4_ = bf16[80,256]{1,0:T(8,128)(2,1)S(1)} collective-permute-done((bf16[80,256]{1,0:T(8,128)(2,1)S(1)}, bf16[80,256]{1,0:T(8,128)(2,1)S(1)}, u32[]{:S(2)}, u32[]{:S(2)}) %collective-permute-start.21) | collective-permute-done | bytes 40992 | tf_op jit(solution)/shard_map/ppermute | solution.py:32
  74.1 1.2 %collective-permute-done.23.refs_6_ = bf16[80,256]{1,0:T(8,128)(2,1)S(1)} collective-permute-done((bf16[80,256]{1,0:T(8,128)(2,1)S(1)}, bf16[80,256]{1,0:T(8,128)(2,1)S(1)}, u32[]{:S(2)}, u32[]{:S(2)}) %collective-permute-start.23) | collective-permute-done | bytes 40992 | tf_op jit(solution)/shard_map/ppermute | solution.py:32
  75.3 4.3 %second_back.1 = (f32[1,1,256]{2,1,0:T(1,128)}, f32[8,256]{1,0:T(8,128)S(1)}, f32[128,256]{1,0:T(8,128)S(1)}, f32[4,128,256]{2,1,0:T(8,128)S(1)}, bf16[128,3072]...) custom-call(s32[1,3072]{1,0:T(1,128)S(1)} %get-tuple-element.56.ids_ref, ...), custom_call_target="tpu_custom_call" | custom-call | flops 10000000 | bytes 1000000 | tf_op jit(solution)/shard_map/second_back/pallas_call | solution.py:48
  79.6 0.4 collective-permute-start.25
  80.0 3.2 %collective-permute-start.26 = (bf16[3,128,256]{2,1,0:T(8,128)(2,1)S(1)}, bf16[3,128,256]{2,1,0:T(8,128)(2,1)S(1)}, u32[]{:S(2)}, u32[]{:S(2)}) collective-permute-start(bf16[3,128,256]{2,1,0:T(8,128)(2,1)S(1)} %get-tuple-element.105), channel_id=1, source_target_pairs={{4,0},{5,1},{6,2},{7,3},{8,4},{9,5},{10,6},{11,7},{12,8},{13,9},{1... | collective-permute-start | bytes 589832 | tf_op jit(solution)/shard_map/ppermute | solution.py:32
  83.1 1.7 %second_middle.1.middle_ref = f32[3,128,256]{2,1,0:T(8,128)S(1)} custom-call(s32[1,3072]{1,0:T(1,128)S(1)} %get-tuple-element.56.ids_ref, bf16[128,3072]{1,0:T(8,128)(2,1)S(1)} %get-tuple-element.102.term_ref, f32[128,256]{1,0:T(8,128)S(1)} %get-tuple-element.103.cotangent_ref), custom_call_target="tpu_custom_call" | custom-call | flops 1000000000 | bytes 1000000 | tf_op jit(solution)/shard_map/second_middle/pallas_call | solution.py:48
  84.8 2.8 %collective-permute-done.25.refs_0_ = bf16[3,128,256]{2,1,0:T(8,128)(2,1)S(1)} collective-permute-done((bf16[3,128,256]{2,1,0:T(8,128)(2,1)S(1)}, bf16[3,128,256]{2,1,0:T(8,128)(2,1)S(1)}, u32[]{:S(2)}, u32[]{:S(2)}) %collective-permute-start.25) | collective-permute-done | bytes 196640 | tf_op jit(solution)/shard_map/ppermute | solution.py:32
  87.6 2.3 %collective-permute-start.28 = (bf16[128,256]{1,0:T(8,128)(2,1)S(1)}, bf16[128,256]{1,0:T(8,128)(2,1)S(1)}, u32[]{:S(2)}, u32[]{:S(2)}) collective-permute-start(bf16[128,256]{1,0:T(8,128)(2,1)S(1)} %get-tuple-element.112), channel_id=1, source_target_pairs={{1,0},{2,1},{3,2},{0,3},{5,4},{6,5},{7,6},{4,7},{9,8},{10,9},{11,1... | collective-permute-start | bytes 196616 | tf_op jit(solution)/shard_map/ppermute | solution.py:32
  90.0 1.2 %second_edge.1.edge_ref = f32[32,3072]{1,0:T(8,128)S(1)} custom-call(bf16[2,2,16,256]{3,2,1,0:T(8,128)(2,1)S(1)} %get-tuple-element.65.back_ref, bf16[128,3072]{1,0:T(8,128)(2,1)S(1)} %get-tuple-element.79.feature_ref, f32[4,128,256]{2,1,0:T(8,128)S(1)} %get-tuple-element.100.grad_ref), custom_call_target="tpu_custom_call" | custom-call | flops 1000000000 | bytes 1000000 | tf_op jit(solution)/shard_map/second_edge/pallas_call | solution.py:48
  91.2 1.2 %collective-permute-done.28.refs_3_ = bf16[128,256]{1,0:T(8,128)(2,1)S(1)} collective-permute-done((bf16[128,256]{1,0:T(8,128)(2,1)S(1)}, bf16[128,256]{1,0:T(8,128)(2,1)S(1)}, u32[]{:S(2)}, u32[]{:S(2)}) %collective-permute-start.28) | collective-permute-done | bytes 65568 | tf_op jit(solution)/shard_map/ppermute | solution.py:32
  92.4 2.7 %collective-permute-done.27.refs_2_ = bf16[128,256]{1,0:T(8,128)(2,1)S(1)} collective-permute-done((bf16[128,256]{1,0:T(8,128)(2,1)S(1)}, bf16[128,256]{1,0:T(8,128)(2,1)S(1)}, u32[]{:S(2)}, u32[]{:S(2)}) %collective-permute-start.27) | collective-permute-done | bytes 65568 | tf_op jit(solution)/shard_map/ppermute | solution.py:32
  95.2 3.6 %first_back.1 = (f32[3,8,256]{2,1,0:T(8,128)S(1)}, f32[3,8,256]{2,1,0:T(8,128)S(1)}, f32[3,8,256]{2,1,0:T(8,128)S(1)}) custom-call(s32[1,3072]{1,0:T(1,128)S(1)} %get-tuple-element.56.ids_ref, f32[8,3072]{1,0:T(8,128)S(1)} %get-tuple-element.62.basis_ref, f32[8,3072]{1,0:T(8,128)S(1)} %get-tuple-element.63.slope_ref, ...), custom_call_target="tpu_custom_call" | custom-call | flops 10000000 | bytes 1000000 | tf_op jit(solution)/shard_map/first_back/pallas_call | solution.py:48
  98.8 3.5 %collective-permute-start.30 = (f32[3,8,256]{2,1,0:T(8,128)S(1)}, f32[3,8,256]{2,1,0:T(8,128)S(1)}, u32[]{:S(2)}, u32[]{:S(2)}) collective-permute-start(f32[3,8,256]{2,1,0:T(8,128)S(1)} %get-tuple-element.108), channel_id=1, source_target_pairs={{4,0},{5,1},{6,2},{7,3},{8,4},{9,5},{10,6},{11,7},{12,8},{13,9},{1... | collective-permute-start | bytes 73736 | tf_op jit(solution)/shard_map/ppermute | solution.py:32
  102.3 1.5 %collective-permute-done.29 = f32[3,8,256]{2,1,0:T(8,128)S(1)} collective-permute-done((f32[3,8,256]{2,1,0:T(8,128)S(1)}, f32[3,8,256]{2,1,0:T(8,128)S(1)}, u32[]{:S(2)}, u32[]{:S(2)}) %collective-permute-start.29) | collective-permute-done | bytes 24608 | tf_op jit(solution)/shard_map/ppermute | solution.py:32
  103.9 1.2 %collective-permute-start.32 = (f32[8,256]{1,0:T(8,128)S(1)}, f32[8,256]{1,0:T(8,128)S(1)}, u32[]{:S(2)}, u32[]{:S(2)}) collective-permute-start(f32[8,256]{1,0:T(8,128)S(1)} %get-tuple-element.115), channel_id=1, source_target_pairs={{1,0},{2,1},{3,2},{0,3},{5,4},{6,5},{7,6},{4,7},{9,8},{10,9},{11,1... | collective-permute-start | bytes 24584 | tf_op jit(solution)/shard_map/ppermute | solution.py:32
  105.1 0.9 collective-permute-start.31
  105.9 1.6 %collective-permute-done.32 = f32[8,256]{1,0:T(8,128)S(1)} collective-permute-done((f32[8,256]{1,0:T(8,128)S(1)}, f32[8,256]{1,0:T(8,128)S(1)}, u32[]{:S(2)}, u32[]{:S(2)}) %collective-permute-start.32) | collective-permute-done | bytes 8224 | tf_op jit(solution)/shard_map/ppermute | solution.py:32
  107.6 2.1 %collective-permute-done.31 = f32[8,256]{1,0:T(8,128)S(1)} collective-permute-done((f32[8,256]{1,0:T(8,128)S(1)}, f32[8,256]{1,0:T(8,128)S(1)}, u32[]{:S(2)}, u32[]{:S(2)}) %collective-permute-start.31) | collective-permute-done | bytes 8224 | tf_op jit(solution)/shard_map/ppermute | solution.py:32
  109.6 0.6 copy.13
  (43 shorter events, 1.1 us)
Async XLA Ops:
  0.6 0.7 copy-start.9
  1.3 0.7 copy-start.10
  2.0 5.3 %collective-permute-start.1 = (f32[8,128]{1,0:T(8,128)S(1)}, f32[8,128]{1,0:T(8,128)S(1)}, u32[]{:S(2)}, u32[]{:S(2)}) collective-permute-start(f32[8,128]{1,0:T(8,128)S(1)} %pack.1), channel_id=1, source_target_pairs={{1,0},{2,1},{3,2},{0,3},{5,4},{6,5},{7,6},{4,7},{9,8},{10,9},{11,1... | collective-permute-start | bytes 12296 | tf_op jit(solution)/shard_map/ppermute | solution.py:32
  6.0 4.5 %collective-permute-start = (f32[8,128]{1,0:T(8,128)S(1)}, f32[8,128]{1,0:T(8,128)S(1)}, u32[]{:S(2)}, u32[]{:S(2)}) collective-permute-start(f32[8,128]{1,0:T(8,128)S(1)} %pack.1), channel_id=1, source_target_pairs={{3,0},{0,1},{1,2},{2,3},{7,4},{4,5},{5,6},{6,7},{11,8},{8,9},{9,10... | collective-permute-start | bytes 12296 | tf_op jit(solution)/shard_map/ppermute | solution.py:32
  10.5 10.5 %collective-permute-start.3 = (f32[3,8,128]{2,1,0:T(8,128)S(1)}, f32[3,8,128]{2,1,0:T(8,128)S(1)}, u32[]{:S(2)}, u32[]{:S(2)}) collective-permute-start(f32[3,8,128]{2,1,0:T(8,128)S(1)} %pad_maximum_fusion.1.column_ref.cell_ref), channel_id=1, source_target_pairs={{4,0},{5,1},{6,2},{7,3},{8,4},{9,5},{10,6},{11,7},{12,8},{13,9},{1... | collective-permute-start | bytes 36872 | tf_op jit(solution)/shard_map/ppermute | solution.py:32
  12.1 8.9 %collective-permute-start.2 = (f32[3,8,128]{2,1,0:T(8,128)S(1)}, f32[3,8,128]{2,1,0:T(8,128)S(1)}, u32[]{:S(2)}, u32[]{:S(2)}) collective-permute-start(f32[3,8,128]{2,1,0:T(8,128)S(1)} %pad_maximum_fusion.1.column_ref.cell_ref), channel_id=1, source_target_pairs={{28,0},{29,1},{30,2},{31,3},{0,4},{1,5},{2,6},{3,7},{4,8},{5,9},{6... | collective-permute-start | bytes 36872 | tf_op jit(solution)/shard_map/ppermute | solution.py:32
  12.2 1.0 copy-start
  13.1 0.8 copy-start.1
  14.0 0.8 copy-start.2
  14.8 0.8 copy-start.3
  15.6 0.7 copy-start.4
  16.3 0.7 copy-start.5
  17.0 0.7 copy-start.6
  17.7 0.7 copy-start.7
  18.4 0.7 copy-start.8
  22.6 4.8 %collective-permute-start.5 = (bf16[128,256]{1,0:T(8,128)(2,1)S(1)}, bf16[128,256]{1,0:T(8,128)(2,1)S(1)}, u32[]{:S(2)}, u32[]{:S(2)}) collective-permute-start(bf16[128,256]{1,0:T(8,128)(2,1)S(1)} %get-tuple-element.70), channel_id=1, source_target_pairs={{1,0},{2,1},{3,2},{0,3},{5,4},{6,5},{7,6},{4,7},{9,8},{10,9},{11,1... | collective-permute-start | bytes 196616 | tf_op jit(solution)/shard_map/ppermute | solution.py:32
  22.9 5.3 %collective-permute-start.4 = (bf16[128,256]{1,0:T(8,128)(2,1)S(1)}, bf16[128,256]{1,0:T(8,128)(2,1)S(1)}, u32[]{:S(2)}, u32[]{:S(2)}) collective-permute-start(bf16[128,256]{1,0:T(8,128)(2,1)S(1)} %get-tuple-element.70), channel_id=1, source_target_pairs={{3,0},{0,1},{1,2},{2,3},{7,4},{4,5},{5,6},{6,7},{11,8},{8,9},{9,10... | collective-permute-start | bytes 196616 | tf_op jit(solution)/shard_map/ppermute | solution.py:32
  28.3 6.0 %collective-permute-start.7 = (bf16[3,128,256]{2,1,0:T(8,128)(2,1)S(1)}, bf16[3,128,256]{2,1,0:T(8,128)(2,1)S(1)}, u32[]{:S(2)}, u32[]{:S(2)}) collective-permute-start(bf16[3,128,256]{2,1,0:T(8,128)(2,1)S(1)} %pad_maximum_fusion.column_ref), channel_id=1, source_target_pairs={{4,0},{5,1},{6,2},{7,3},{8,4},{9,5},{10,6},{11,7},{12,8},{13,9},{1... | collective-permute-start | bytes 589832 | tf_op jit(solution)/shard_map/ppermute | solution.py:32
  31.0 6.9 %collective-permute-start.6 = (bf16[3,128,256]{2,1,0:T(8,128)(2,1)S(1)}, bf16[3,128,256]{2,1,0:T(8,128)(2,1)S(1)}, u32[]{:S(2)}, u32[]{:S(2)}) collective-permute-start(bf16[3,128,256]{2,1,0:T(8,128)(2,1)S(1)} %pad_maximum_fusion.column_ref), channel_id=1, source_target_pairs={{28,0},{29,1},{30,2},{31,3},{0,4},{1,5},{2,6},{3,7},{4,8},{5,9},{6... | collective-permute-start | bytes 589832 | tf_op jit(solution)/shard_map/ppermute | solution.py:32
  41.2 5.3 %collective-permute-start.14 = (bf16[80,256]{1,0:T(8,128)(2,1)S(1)}, bf16[80,256]{1,0:T(8,128)(2,1)S(1)}, u32[]{:S(2)}, u32[]{:S(2)}) collective-permute-start(bf16[80,256]{1,0:T(8,128)(2,1)S(1)} %get-tuple-element.85.refs_0_), channel_id=1, source_target_pairs={{28,0},{29,1},{30,2},{31,3},{0,4},{1,5},{2,6},{3,7},{4,8},{5,9},{6... | collective-permute-start | bytes 122888 | tf_op jit(solution)/shard_map/ppermute | solution.py:32
  41.2 6.8 %collective-permute-start.13 = (bf16[80,256]{1,0:T(8,128)(2,1)S(1)}, bf16[80,256]{1,0:T(8,128)(2,1)S(1)}, u32[]{:S(2)}, u32[]{:S(2)}) collective-permute-start(bf16[80,256]{1,0:T(8,128)(2,1)S(1)} %get-tuple-element.85.refs_0_), channel_id=1, source_target_pairs={{24,0},{25,1},{26,2},{27,3},{28,4},{29,5},{30,6},{31,7},{0,8},{1,9... | collective-permute-start | bytes 122888 | tf_op jit(solution)/shard_map/ppermute | solution.py:32
  41.3 8.1 %collective-permute-start.12 = (bf16[80,256]{1,0:T(8,128)(2,1)S(1)}, bf16[80,256]{1,0:T(8,128)(2,1)S(1)}, u32[]{:S(2)}, u32[]{:S(2)}) collective-permute-start(bf16[80,256]{1,0:T(8,128)(2,1)S(1)} %get-tuple-element.85.refs_0_), channel_id=1, source_target_pairs={{20,0},{21,1},{22,2},{23,3},{24,4},{25,5},{26,6},{27,7},{28,8},{29... | collective-permute-start | bytes 122888 | tf_op jit(solution)/shard_map/ppermute | solution.py:32
  42.6 7.1 %collective-permute-start.11 = (bf16[80,256]{1,0:T(8,128)(2,1)S(1)}, bf16[80,256]{1,0:T(8,128)(2,1)S(1)}, u32[]{:S(2)}, u32[]{:S(2)}) collective-permute-start(bf16[80,256]{1,0:T(8,128)(2,1)S(1)} %get-tuple-element.85.refs_0_), channel_id=1, source_target_pairs={{16,0},{17,1},{18,2},{19,3},{20,4},{21,5},{22,6},{23,7},{24,8},{25... | collective-permute-start | bytes 122888 | tf_op jit(solution)/shard_map/ppermute | solution.py:32
  45.3 4.3 %collective-permute-start.10 = (bf16[80,256]{1,0:T(8,128)(2,1)S(1)}, bf16[80,256]{1,0:T(8,128)(2,1)S(1)}, u32[]{:S(2)}, u32[]{:S(2)}) collective-permute-start(bf16[80,256]{1,0:T(8,128)(2,1)S(1)} %get-tuple-element.85.refs_0_), channel_id=1, source_target_pairs={{12,0},{13,1},{14,2},{15,3},{16,4},{17,5},{18,6},{19,7},{20,8},{21... | collective-permute-start | bytes 122888 | tf_op jit(solution)/shard_map/ppermute | solution.py:32
  46.4 4.4 %collective-permute-start.9 = (bf16[80,256]{1,0:T(8,128)(2,1)S(1)}, bf16[80,256]{1,0:T(8,128)(2,1)S(1)}, u32[]{:S(2)}, u32[]{:S(2)}) collective-permute-start(bf16[80,256]{1,0:T(8,128)(2,1)S(1)} %get-tuple-element.85.refs_0_), channel_id=1, source_target_pairs={{8,0},{9,1},{10,2},{11,3},{12,4},{13,5},{14,6},{15,7},{16,8},{17,9... | collective-permute-start | bytes 122888 | tf_op jit(solution)/shard_map/ppermute | solution.py:32
  48.0 2.8 %collective-permute-start.8 = (bf16[80,256]{1,0:T(8,128)(2,1)S(1)}, bf16[80,256]{1,0:T(8,128)(2,1)S(1)}, u32[]{:S(2)}, u32[]{:S(2)}) collective-permute-start(bf16[80,256]{1,0:T(8,128)(2,1)S(1)} %get-tuple-element.85.refs_0_), channel_id=1, source_target_pairs={{4,0},{5,1},{6,2},{7,3},{8,4},{9,5},{10,6},{11,7},{12,8},{13,9},{1... | collective-permute-start | bytes 122888 | tf_op jit(solution)/shard_map/ppermute | solution.py:32
  53.4 6.4 %collective-permute-start.17 = (bf16[320,128]{1,0:T(8,128)(2,1)S(1)}, bf16[320,128]{1,0:T(8,128)(2,1)S(1)}, u32[]{:S(2)}, u32[]{:S(2)}) collective-permute-start(bf16[320,128]{1,0:T(8,128)(2,1)S(1)} %get-tuple-element.91.refs_8_), channel_id=1, source_target_pairs={{3,0},{0,1},{1,2},{2,3},{7,4},{4,5},{5,6},{6,7},{11,8},{8,9},{9,10... | collective-permute-start | bytes 245768 | tf_op jit(solution)/shard_map/ppermute | solution.py:32
  54.2 6.8 %collective-permute-start.16 = (bf16[320,128]{1,0:T(8,128)(2,1)S(1)}, bf16[320,128]{1,0:T(8,128)(2,1)S(1)}, u32[]{:S(2)}, u32[]{:S(2)}) collective-permute-start(bf16[320,128]{1,0:T(8,128)(2,1)S(1)} %get-tuple-element.91.refs_8_), channel_id=1, source_target_pairs={{2,0},{3,1},{0,2},{1,3},{6,4},{7,5},{4,6},{5,7},{10,8},{11,9},{8,1... | collective-permute-start | bytes 245768 | tf_op jit(solution)/shard_map/ppermute | solution.py:32
  55.0 6.5 %collective-permute-start.15 = (bf16[320,128]{1,0:T(8,128)(2,1)S(1)}, bf16[320,128]{1,0:T(8,128)(2,1)S(1)}, u32[]{:S(2)}, u32[]{:S(2)}) collective-permute-start(bf16[320,128]{1,0:T(8,128)(2,1)S(1)} %get-tuple-element.91.refs_8_), channel_id=1, source_target_pairs={{1,0},{2,1},{3,2},{0,3},{5,4},{6,5},{7,6},{4,7},{9,8},{10,9},{11,1... | collective-permute-start | bytes 245768 | tf_op jit(solution)/shard_map/ppermute | solution.py:32
  64.5 5.6 %collective-permute-start.18 = (bf16[80,256]{1,0:T(8,128)(2,1)S(1)}, bf16[80,256]{1,0:T(8,128)(2,1)S(1)}, u32[]{:S(2)}, u32[]{:S(2)}) collective-permute-start(bf16[80,256]{1,0:T(8,128)(2,1)S(1)} %get-tuple-element.93), channel_id=1, source_target_pairs={{28,0},{29,1},{30,2},{31,3},{0,4},{1,5},{2,6},{3,7},{4,8},{5,9},{6... | collective-permute-start | bytes 122888 | tf_op jit(solution)/shard_map/ppermute | solution.py:32
  64.7 7.4 %collective-permute-start.19 = (bf16[80,256]{1,0:T(8,128)(2,1)S(1)}, bf16[80,256]{1,0:T(8,128)(2,1)S(1)}, u32[]{:S(2)}, u32[]{:S(2)}) collective-permute-start(bf16[80,256]{1,0:T(8,128)(2,1)S(1)} %get-tuple-element.94), channel_id=1, source_target_pairs={{24,0},{25,1},{26,2},{27,3},{28,4},{29,5},{30,6},{31,7},{0,8},{1,9... | collective-permute-start | bytes 122888 | tf_op jit(solution)/shard_map/ppermute | solution.py:32
  66.2 6.5 %collective-permute-start.20 = (bf16[80,256]{1,0:T(8,128)(2,1)S(1)}, bf16[80,256]{1,0:T(8,128)(2,1)S(1)}, u32[]{:S(2)}, u32[]{:S(2)}) collective-permute-start(bf16[80,256]{1,0:T(8,128)(2,1)S(1)} %get-tuple-element.95), channel_id=1, source_target_pairs={{20,0},{21,1},{22,2},{23,3},{24,4},{25,5},{26,6},{27,7},{28,8},{29... | collective-permute-start | bytes 122888 | tf_op jit(solution)/shard_map/ppermute | solution.py:32
  67.7 6.5 %collective-permute-start.21 = (bf16[80,256]{1,0:T(8,128)(2,1)S(1)}, bf16[80,256]{1,0:T(8,128)(2,1)S(1)}, u32[]{:S(2)}, u32[]{:S(2)}) collective-permute-start(bf16[80,256]{1,0:T(8,128)(2,1)S(1)} %get-tuple-element.96), channel_id=1, source_target_pairs={{16,0},{17,1},{18,2},{19,3},{20,4},{21,5},{22,6},{23,7},{24,8},{25... | collective-permute-start | bytes 122888 | tf_op jit(solution)/shard_map/ppermute | solution.py:32
  70.0 4.1 %collective-permute-start.22 = (bf16[80,256]{1,0:T(8,128)(2,1)S(1)}, bf16[80,256]{1,0:T(8,128)(2,1)S(1)}, u32[]{:S(2)}, u32[]{:S(2)}) collective-permute-start(bf16[80,256]{1,0:T(8,128)(2,1)S(1)} %get-tuple-element.97), channel_id=1, source_target_pairs={{12,0},{13,1},{14,2},{15,3},{16,4},{17,5},{18,6},{19,7},{20,8},{21... | collective-permute-start | bytes 122888 | tf_op jit(solution)/shard_map/ppermute | solution.py:32
  70.1 5.2 %collective-permute-start.23 = (bf16[80,256]{1,0:T(8,128)(2,1)S(1)}, bf16[80,256]{1,0:T(8,128)(2,1)S(1)}, u32[]{:S(2)}, u32[]{:S(2)}) collective-permute-start(bf16[80,256]{1,0:T(8,128)(2,1)S(1)} %get-tuple-element.98), channel_id=1, source_target_pairs={{8,0},{9,1},{10,2},{11,3},{12,4},{13,5},{14,6},{15,7},{16,8},{17,9... | collective-permute-start | bytes 122888 | tf_op jit(solution)/shard_map/ppermute | solution.py:32
  72.1 3.2 %collective-permute-start.24 = (bf16[80,256]{1,0:T(8,128)(2,1)S(1)}, bf16[80,256]{1,0:T(8,128)(2,1)S(1)}, u32[]{:S(2)}, u32[]{:S(2)}) collective-permute-start(bf16[80,256]{1,0:T(8,128)(2,1)S(1)} %get-tuple-element.99), channel_id=1, source_target_pairs={{4,0},{5,1},{6,2},{7,3},{8,4},{9,5},{10,6},{11,7},{12,8},{13,9},{1... | collective-permute-start | bytes 122888 | tf_op jit(solution)/shard_map/ppermute | solution.py:32
  79.6 8.0 %collective-permute-start.25 = (bf16[3,128,256]{2,1,0:T(8,128)(2,1)S(1)}, bf16[3,128,256]{2,1,0:T(8,128)(2,1)S(1)}, u32[]{:S(2)}, u32[]{:S(2)}) collective-permute-start(bf16[3,128,256]{2,1,0:T(8,128)(2,1)S(1)} %get-tuple-element.104), channel_id=1, source_target_pairs={{28,0},{29,1},{30,2},{31,3},{0,4},{1,5},{2,6},{3,7},{4,8},{5,9},{6... | collective-permute-start | bytes 589832 | tf_op jit(solution)/shard_map/ppermute | solution.py:32
  80.0 7.6 %collective-permute-start.26 = (bf16[3,128,256]{2,1,0:T(8,128)(2,1)S(1)}, bf16[3,128,256]{2,1,0:T(8,128)(2,1)S(1)}, u32[]{:S(2)}, u32[]{:S(2)}) collective-permute-start(bf16[3,128,256]{2,1,0:T(8,128)(2,1)S(1)} %get-tuple-element.105), channel_id=1, source_target_pairs={{4,0},{5,1},{6,2},{7,3},{8,4},{9,5},{10,6},{11,7},{12,8},{13,9},{1... | collective-permute-start | bytes 589832 | tf_op jit(solution)/shard_map/ppermute | solution.py:32
  87.6 4.8 %collective-permute-start.28 = (bf16[128,256]{1,0:T(8,128)(2,1)S(1)}, bf16[128,256]{1,0:T(8,128)(2,1)S(1)}, u32[]{:S(2)}, u32[]{:S(2)}) collective-permute-start(bf16[128,256]{1,0:T(8,128)(2,1)S(1)} %get-tuple-element.112), channel_id=1, source_target_pairs={{1,0},{2,1},{3,2},{0,3},{5,4},{6,5},{7,6},{4,7},{9,8},{10,9},{11,1... | collective-permute-start | bytes 196616 | tf_op jit(solution)/shard_map/ppermute | solution.py:32
  90.0 5.2 %collective-permute-start.27 = (bf16[128,256]{1,0:T(8,128)(2,1)S(1)}, bf16[128,256]{1,0:T(8,128)(2,1)S(1)}, u32[]{:S(2)}, u32[]{:S(2)}) collective-permute-start(bf16[128,256]{1,0:T(8,128)(2,1)S(1)} %get-tuple-element.113), channel_id=1, source_target_pairs={{3,0},{0,1},{1,2},{2,3},{7,4},{4,5},{5,6},{6,7},{11,8},{8,9},{9,10... | collective-permute-start | bytes 196616 | tf_op jit(solution)/shard_map/ppermute | solution.py:32
  98.7 5.1 %collective-permute-start.29 = (f32[3,8,256]{2,1,0:T(8,128)S(1)}, f32[3,8,256]{2,1,0:T(8,128)S(1)}, u32[]{:S(2)}, u32[]{:S(2)}) collective-permute-start(f32[3,8,256]{2,1,0:T(8,128)S(1)} %get-tuple-element.107), channel_id=1, source_target_pairs={{28,0},{29,1},{30,2},{31,3},{0,4},{1,5},{2,6},{3,7},{4,8},{5,9},{6... | collective-permute-start | bytes 73736 | tf_op jit(solution)/shard_map/ppermute | solution.py:32
  98.8 5.1 %collective-permute-start.30 = (f32[3,8,256]{2,1,0:T(8,128)S(1)}, f32[3,8,256]{2,1,0:T(8,128)S(1)}, u32[]{:S(2)}, u32[]{:S(2)}) collective-permute-start(f32[3,8,256]{2,1,0:T(8,128)S(1)} %get-tuple-element.108), channel_id=1, source_target_pairs={{4,0},{5,1},{6,2},{7,3},{8,4},{9,5},{10,6},{11,7},{12,8},{13,9},{1... | collective-permute-start | bytes 73736 | tf_op jit(solution)/shard_map/ppermute | solution.py:32
  103.9 3.7 %collective-permute-start.32 = (f32[8,256]{1,0:T(8,128)S(1)}, f32[8,256]{1,0:T(8,128)S(1)}, u32[]{:S(2)}, u32[]{:S(2)}) collective-permute-start(f32[8,256]{1,0:T(8,128)S(1)} %get-tuple-element.115), channel_id=1, source_target_pairs={{1,0},{2,1},{3,2},{0,3},{5,4},{6,5},{7,6},{4,7},{9,8},{10,9},{11,1... | collective-permute-start | bytes 24584 | tf_op jit(solution)/shard_map/ppermute | solution.py:32
  105.1 4.5 %collective-permute-start.31 = (f32[8,256]{1,0:T(8,128)S(1)}, f32[8,256]{1,0:T(8,128)S(1)}, u32[]{:S(2)}, u32[]{:S(2)}) collective-permute-start(f32[8,256]{1,0:T(8,128)S(1)} %get-tuple-element.116), channel_id=1, source_target_pairs={{3,0},{0,1},{1,2},{2,3},{7,4},{4,5},{5,6},{6,7},{11,8},{8,9},{9,10... | collective-permute-start | bytes 24584 | tf_op jit(solution)/shard_map/ppermute | solution.py:32

commit v5 on v4

--- a/solution.py
+++ b/solution.py
@@ -32,17 +32,18 @@
     return lax.ppermute(block, ("gx", "gy"), route)
 
 
-def around(block):
+def around(block, beside):
     column = jnp.stack([shifted(block, 0, -1), block, shifted(block, 0, 1)])
-    return [shifted(column, -1, 0), column, shifted(column, 1, 0)]
+    column, beside = lax.optimization_barrier((column, beside))
+    return [shifted(column, -1, 0), column, shifted(column, 1, 0)], beside
 
 
 def whole(space=pltpu.VMEM):
     return pl.BlockSpec(memory_space=space)
 
 
-def run(kernel, outs, args, scratch=(), smem=0, hbm=0, flops=10_000_000, name=None):
-    specs = [whole(pltpu.SMEM)] * smem + [whole(pl.ANY)] * hbm
+def run(kernel, outs, args, scratch=(), smem=0, hbm=0, flops=10_000_000, grant=16, name=None):
+    specs = [whole(pltpu.SMEM)] * smem + [whole(pltpu.HBM)] * hbm
     specs += [whole()] * (len(args) - smem - hbm)
     return list(
         pl.pallas_call(
@@ -51,7 +52,7 @@
             in_specs=specs,
             out_specs=[whole() for _ in outs],
             scratch_shapes=list(scratch),
-            compiler_params=pltpu.CompilerParams(vmem_limit_bytes=32 * 1024 * 1024),
+            compiler_params=pltpu.CompilerParams(vmem_limit_bytes=grant * 1024 * 1024),
             cost_estimate=pl.CostEstimate(
                 flops=flops, bytes_accessed=1_000_000, transcendentals=0
             ),
@@ -135,8 +136,8 @@
     return dot(stack, jnp.concatenate([hot, hot, hot, jnp.zeros_like(hot)], axis=0).astype(BF16))
 
 
-def weights_of(stack_ref, layer, part, rows):
-    return dot(stack_ref[layer, 1 if part else 0], stacked_right(rows))
+def weights_of(stack_ref, part, rows):
+    return dot(stack_ref[1 if part else 0], stacked_right(rows))
 
 
 def mixed(sums, high_ref, low_ref, layer):
@@ -179,14 +180,7 @@
     low_ref[at] = low
 
 
-def prep_kernel(share, padded, grid, norm, place_ref, *refs):
-    sources, outs, scratch = refs[:9], refs[9:25], refs[25:]
-    id_ref, count_ref, read_ref = outs[:3]
-    (embed_out, left_out, back_out, mix_high, mix_low, turn_high, turn_low, hidden_high, hidden_low,
-     hidden_turn_high, hidden_turn_low, charge_pair, weight_ref) = outs[3:]
-    embed_ref, radial_ref, mixing_ref, hidden_ref, charge_ref, vec_ref, sems = scratch
-    targets = [id_ref, count_ref, read_ref, embed_ref, radial_ref, mixing_ref, hidden_ref,
-               charge_ref, vec_ref]
+def fetch(sources, targets, sems):
     copies = [
         pltpu.make_async_copy(source, target, sems.at[i])
         for i, (source, target) in enumerate(zip(sources, targets))
@@ -195,24 +189,50 @@
         copy.start()
     for copy in copies:
         copy.wait()
+
+
+def prep_first_kernel(norm, ids_in, count_in, embed_in, radial_in, mixing_in, id_ref, count_ref,
+                      embed_out, kind_left, left_out, back_out, kind_high, kind_low, mix_high,
+                      mix_low, turn_high, turn_low, embed_ref, radial_ref, mixing_ref, sems):
+    fetch(
+        [ids_in, count_in, embed_in, radial_in, mixing_in],
+        [id_ref, count_ref, embed_ref, radial_ref, mixing_ref],
+        sems,
+    )
     embed = embed_ref[...]
-    embed = jnp.concatenate([embed, jnp.zeros((8 - embed.shape[0], embed.shape[1]), F32)], axis=0)
-    embed_out[...] = embedding_stack(embed)
+    kinds = embed.shape[0]
+    for path in range(2):
+        radial = radial_ref[0, path] * norm
+        rows = jnp.concatenate([radial * embed[s : s + 1] for s in range(kinds)], axis=0)
+        kind_left[path] = stacked_left(rows)
+        put_split(rows, kind_high, kind_low, path)
+        radial = radial_ref[1, path] * norm
+        left_out[path] = stacked_left(radial)
+        back_out[path] = radial_left(radial)
     for layer in range(2):
-        for path in range(2):
-            radial = radial_ref[layer, path] * norm
-            left_out[layer, path] = stacked_left(radial)
-            back_out[layer, path] = radial_left(radial)
         scalar, vector = mixing_ref[layer, 0], mixing_ref[layer, 1]
         put_split(jnp.concatenate([scalar.T, vector.T], axis=1), mix_high, mix_low, layer)
         put_split(jnp.concatenate([scalar, 2.0 * vector], axis=0), turn_high, turn_low, layer)
+    embed = jnp.concatenate([embed, jnp.zeros((8 - kinds, embed.shape[1]), F32)], axis=0)
+    embed_out[...] = embedding_stack(embed)
+
+
+def prep_second_kernel(read_in, hidden_in, charge_in, read_ref, hidden_high, hidden_low,
+                       hidden_turn_high, hidden_turn_low, charge_pair, hidden_ref, charge_ref, sems):
+    fetch([read_in, hidden_in, charge_in], [read_ref, hidden_ref, charge_ref], sems)
     put_split(hidden_ref[...].T, hidden_high, hidden_low, Ellipsis)
     put_split(hidden_ref[...], hidden_turn_high, hidden_turn_low, Ellipsis)
     charge = charge_ref[...]
     high = charge.astype(BF16).astype(F32)
     charge_pair[0] = high.astype(BF16)
     charge_pair[1] = (charge - high).astype(BF16)
-    green_weights(share, padded, grid, place_ref, vec_ref, weight_ref)
+
+
+def hot_kernel(ids_ref, hot_ref):
+    edges = ids_ref.shape[1]
+    for start in range(0, edges, 256):
+        lanes = slice(start, start + 256)
+        hot_ref[:, lanes] = hot_columns(ids_ref[:, lanes], hot_ref.shape[0])
 
 
 def unfold_block(block, atoms):
@@ -220,7 +240,7 @@
     return jnp.concatenate([block[4 * s : 4 * s + 4] for s in range(parts)], axis=1)
 
 
-def first_kernel(slots, ids_ref, count_ref, embed_ref, left_ref, mix_high, mix_low, before_ref,
+def first_kernel(slots, ids_ref, count_ref, embed_ref, kind_left, mix_high, mix_low, before_ref,
                  column_ref, after_ref, low_ref, basis_ref, slope_ref, unit_ref, sums_ref,
                  gate_ref):
     atoms = low_ref.shape[1]
@@ -267,13 +287,21 @@
     unit_ref[...] = unit
     stack = embed_ref[...]
     parts = edge_parts(basis, unit)
-    sums = [None] * 4
+    species = kind_left.shape[2] // 32
+    by_kind = [[None] * species for _ in range(4)]
     for n in range(slots):
         lanes = slice(n * atoms, (n + 1) * atoms)
-        feature = embedded(stack, kinds[:, lanes])
-        for part in range(4):
-            term = weights_of(left_ref, 0, part, parts[part][:, lanes]) * feature
-            sums[part] = term if sums[part] is None else sums[part] + term
+        kind = jnp.broadcast_to(kinds[:, lanes], (8, atoms))
+        for k in range(species):
+            match = kind == float(k)
+            for part in range(4):
+                term = jnp.where(match, parts[part][:, lanes], 0.0)
+                old = by_kind[part][k]
+                by_kind[part][k] = term if old is None else old + term
+    stacks = [stacked_right(jnp.concatenate(rows, axis=0)) for rows in by_kind]
+    vectors = dot(kind_left[1], jnp.concatenate(stacks[1:], axis=1))
+    sums = [dot(kind_left[0], stacks[0])]
+    sums += [vectors[:, i * atoms : (i + 1) * atoms] for i in range(3)]
     step, gate = mixed(sums, mix_high, mix_low, 0)
     low_ref[...] = (embedded(stack, own[3:4]) + step).astype(BF16)
     for part in range(3):
@@ -286,7 +314,7 @@
     return jnp.where(ids == place, 1.0, 0.0).astype(BF16)
 
 
-def second_near_kernel(slots, ids_ref, basis_ref, unit_ref, left_ref, column_ref, weight_ref,
+def second_near_kernel(slots, basis_ref, unit_ref, left_ref, hot_ref, column_ref, weight_ref,
                        near_ref):
     atoms = column_ref.shape[2]
     parts = edge_parts(basis_ref[...], unit_ref[...])
@@ -294,25 +322,28 @@
     for n in range(slots):
         lanes = slice(n * atoms, (n + 1) * atoms)
         for part in range(4):
-            weight_ref[part, :, lanes] = weights_of(left_ref, 1, part, parts[part][:, lanes])
-        hot = hot_columns(ids_ref[:, lanes] - 3 * atoms, 3 * atoms)
-        near_ref[:, lanes] = dot(source, hot)
-
-
-def second_kernel(slots, ids_ref, weight_ref, near_ref, mix_high, mix_low, hidden_high, hidden_low,
-                  turn_high, turn_low, out_ref, charge_ref, cell_ref, before_ref, column_ref,
-                  after_ref, feature_ref, sums_ref, gate_ref, packed_ref, full_charge_ref,
-                  energy_ref, slope_ref):
+            weight_ref[part, :, lanes] = weights_of(left_ref, part, parts[part][:, lanes])
+        near_ref[:, lanes] = dot(source, hot_ref[3 * atoms : 6 * atoms, lanes])
+
+
+def second_side_kernel(slots, hot_ref, near_ref, after_ref, out_ref):
+    atoms = after_ref.shape[2]
+    source = jnp.concatenate([after_ref[b] for b in range(3)], axis=1)
+    for n in range(slots):
+        lanes = slice(n * atoms, (n + 1) * atoms)
+        out_ref[:, lanes] = near_ref[:, lanes] + dot(source, hot_ref[6 * atoms :, lanes])
+
+
+def second_kernel(slots, hot_ref, weight_ref, near_ref, mix_high, mix_low, hidden_high, hidden_low,
+                  turn_high, turn_low, out_ref, charge_ref, cell_ref, column_ref, before_ref,
+                  feature_ref, sums_ref, gate_ref, packed_ref, full_charge_ref, energy_ref,
+                  slope_ref):
     atoms = column_ref.shape[2]
-    source = jnp.concatenate(
-        [before_ref[b] for b in range(3)] + [after_ref[b] for b in range(3)], axis=1
-    )
+    source = jnp.concatenate([before_ref[b] for b in range(3)], axis=1)
     sums = [None] * 4
     for n in range(slots):
         lanes = slice(n * atoms, (n + 1) * atoms)
-        ids = ids_ref[:, lanes]
-        ids = jnp.where(ids >= 6 * atoms, ids - 3 * atoms, jnp.where(ids >= 3 * atoms, -1, ids))
-        feature = near_ref[:, lanes] + dot(source, hot_columns(ids, 6 * atoms))
+        feature = near_ref[:, lanes] + dot(source, hot_ref[: 3 * atoms, lanes])
         feature_ref[:, lanes] = feature.astype(BF16)
         for part in range(4):
             term = weight_ref[part, :, lanes] * feature
@@ -352,7 +383,7 @@
     return both[:half] + both[half:]
 
 
-def second_back_kernel(slots, scale, grid_x, ids_ref, weight_ref, turn_high, turn_low, charge_ref,
+def second_back_kernel(slots, scale, grid_x, hot_ref, weight_ref, turn_high, turn_low, charge_ref,
                        sums_ref, gate_ref, full_charge_ref, energy_ref, slope_ref, *refs):
     folds, refs = refs[:grid_x], refs[grid_x:]
     site_ref, long_ref, cotangent_ref, grad_ref, term_ref, before_ref, after_ref = refs
@@ -385,18 +416,17 @@
         for part in range(1, 4):
             term = term + weight_ref[part, :, lanes] * grads[part]
         term_ref[:, lanes] = term.astype(BF16)
-    ids = ids_ref[...]
     for side, out_ref in ((0, before_ref), (2, after_ref)):
         for b in range(3):
-            hot = hot_columns(ids - (3 * side + b) * atoms, atoms)
+            start = (3 * side + b) * atoms
+            hot = hot_ref[start : start + atoms]
             out_ref[b] = dot(term_ref[...], hot, ((1,), (1,))).astype(BF16)
 
 
-def second_middle_kernel(ids_ref, term_ref, cotangent_ref, middle_ref):
-    ids = ids_ref[...]
+def second_middle_kernel(hot_ref, term_ref, cotangent_ref, middle_ref):
     atoms = cotangent_ref.shape[1]
     for b in range(3):
-        hot = hot_columns(ids - (3 + b) * atoms, atoms)
+        hot = hot_ref[(3 + b) * atoms : (4 + b) * atoms]
         grad = dot(term_ref[...], hot, ((1,), (1,)))
         middle_ref[b] = grad + cotangent_ref[...] if b == 1 else grad
 
@@ -408,11 +438,11 @@
         feature = feature_ref[:, lanes].astype(F32)
         for part in range(4):
             edge_ref[8 * part : 8 * part + 8, lanes] = radial_grad(
-                back_ref[1, 1 if part else 0], grad_ref[part] * feature
+                back_ref[1 if part else 0], grad_ref[part] * feature
             )
 
 
-def first_back_kernel(slots, ids_ref, basis_ref, slope_ref, unit_ref, embed_ref, back_ref,
+def first_back_kernel(slots, ids_ref, basis_ref, slope_ref, unit_ref, kind_high, kind_low,
                       turn_high, turn_low, sums_ref, gate_ref, edge_ref, long_ref, middle_ref,
                       *refs):
     from_x, from_y, outs = refs[:2], refs[2:4], refs[4:]
@@ -421,15 +451,21 @@
     for block in (from_x[0][1], from_x[1][1], from_y[0][...], from_y[1][...]):
         cotangent = cotangent + block.astype(F32)
     grads = message_grads(cotangent, gate_ref, sums_ref, turn_high, turn_low, 0)
-    stack = embed_ref[...]
     unit = unit_ref[...]
     kinds = unit[4:5]
+    by_kind = [dot_split((kind_high[0], kind_low[0]), grads[0])]
+    by_kind += [dot_split((kind_high[1], kind_low[1]), grads[i]) for i in range(1, 4)]
+    species = by_kind[0].shape[0] // 8
     edges = [[] for _ in range(4)]
     for n in range(slots):
-        lanes = slice(n * atoms, (n + 1) * atoms)
-        feature = embedded(stack, kinds[:, lanes])
+        kind = jnp.broadcast_to(kinds[:, n * atoms : (n + 1) * atoms], (8, atoms))
+        matches = [kind == float(k) for k in range(1, species)]
         for part in range(4):
-            edges[part].append(radial_grad(back_ref[0, 1 if part else 0], grads[part] * feature))
+            rows = by_kind[part]
+            found = rows[:8]
+            for k, match in enumerate(matches):
+                found = jnp.where(match, rows[8 * k + 8 : 8 * k + 16], found)
+            edges[part].append(found)
     edges = [
         edge_ref[8 * part : 8 * part + 8] + jnp.concatenate(edges[part], axis=1) for part in range(4)
     ]
@@ -545,7 +581,7 @@
 
 def structure_kernel(share, padded, grid, wide, place_ref, *refs):
     grid_x, grid_y = grid
-    blocks, (ca_ref, sa_ref, cb_ref, sb_ref, out_ref) = refs[:grid_x], refs[grid_x:]
+    blocks, (ca_ref, sa_ref, cb_ref, sb_ref, own_ref, out_ref) = refs[:grid_x], refs[grid_x:]
     col = place_ref[1].astype(F32) * (1.0 / grid_y)
     kx, ky, _ = pair_vectors(count_up(padded), share, place_ref[0])
     kz = count_up(8) + 1.0
@@ -570,7 +606,9 @@
         high, low = split(jnp.concatenate(cc + ss + sc + cs + [ca, sa], axis=0))
         term = dot(high, charge, ((1,), (1,))) + dot(low, charge, ((1,), (1,)))
         total = term if total is None else total + term
-    out_ref[...] = pack_rows(total).astype(BF16)
+    packed = pack_rows(total)
+    own_ref[...] = packed
+    out_ref[...] = packed.astype(BF16)
 
 
 def fold_kernel(share, padded, grid, wide, place_ref, ca_ref, sa_ref, cb_ref, sb_ref, weight_ref,
@@ -638,9 +676,8 @@
         rest = slopes - high
         middle = rest.astype(BF16).astype(F32)
         zero = jnp.zeros((outs[d].shape[0] - wide - 9, atoms), F32)
-        outs[d][...] = jnp.concatenate([pot, high, middle, rest - middle, zero], axis=0).astype(
-            BF16
-        )
+        block = jnp.concatenate([pot, high, middle, rest - middle, zero], axis=0)
+        outs[d][...] = block.astype(outs[d].dtype)
 
 
 def per_device(
@@ -680,45 +717,61 @@
             dma((2,)),
         ],
         hbm=2,
+        grant=60,
         name="pack",
     )
-    cells = around(own)
-
-    pair = [shape(features, features, dtype=BF16)] * 2
-    (ids, counts, read_out, embed, left, back, mix_high, mix_low, turn_high, turn_low, hidden_high,
-     hidden_low, hidden_turn_high, hidden_turn_low, charge_pair, weight) = run(
-        functools.partial(prep_kernel, share, padded, grid, 1.0 / math.sqrt(slots)),
+    norm = 1.0 / math.sqrt(slots)
+    kind_rows = 8 * species_embed.shape[0]
+    low_pair = lambda *dims: [shape(*dims, dtype=BF16)] * 2
+    (ids, counts, embed, kind_left, left, back, kind_high, kind_low, mix_high, mix_low, turn_high,
+     turn_low) = run(
+        functools.partial(prep_first_kernel, norm),
         [
             shape(1, edges, dtype=jnp.int32),
             shape(*counts.shape, dtype=jnp.int32),
-            shape(1, features),
             shape(features, 32, dtype=BF16),
-            shape(2, 2, features, 32, dtype=BF16),
-            shape(2, 2, 16, 2 * features, dtype=BF16),
-            shape(2, features, 2 * features, dtype=BF16),
-            shape(2, features, 2 * features, dtype=BF16),
-            shape(2, 2 * features, features, dtype=BF16),
-            shape(2, 2 * features, features, dtype=BF16),
+            shape(2, features, 4 * kind_rows, dtype=BF16),
+            shape(2, features, 32, dtype=BF16),
+            shape(2, 16, 2 * features, dtype=BF16),
         ]
-        + pair + pair
-        + [
-            shape(2, lat_width, features, dtype=BF16),
-            shape(16 * share + padded, 128),
-        ],
-        [place, ids, counts, read_out[None, :], species_embed, radial, mixing, read_hidden,
-         charge_map.T, wavevectors],
+        + low_pair(2, kind_rows, features)
+        + low_pair(2, features, 2 * features)
+        + low_pair(2, 2 * features, features),
+        [ids, counts, species_embed, radial, mixing],
         scratch=[
             pltpu.VMEM(species_embed.shape, F32),
             pltpu.VMEM(radial.shape, F32),
             pltpu.VMEM(mixing.shape, F32),
+            dma((5,)),
+        ],
+        hbm=5,
+        name="prep_first",
+    )
+    cells, ids = around(own, ids)
+    (hot,) = run(
+        hot_kernel, [shape(9 * atoms, edges, dtype=BF16)], [ids], flops=2_000_000_000, name="hot"
+    )
+    read_out, hidden_high, hidden_low, hidden_turn_high, hidden_turn_low, charge_pair = run(
+        prep_second_kernel,
+        [shape(1, features)]
+        + low_pair(features, features)
+        + low_pair(features, features)
+        + [shape(2, lat_width, features, dtype=BF16)],
+        [read_out[None, :], read_hidden, charge_map.T],
+        scratch=[
             pltpu.VMEM(read_hidden.shape, F32),
             pltpu.VMEM((lat_width, features), F32),
-            pltpu.VMEM(wavevectors.shape, jnp.int32),
-            dma((9,)),
+            dma((3,)),
         ],
+        hbm=3,
+        name="prep_second",
+    )
+    (weight,) = run(
+        functools.partial(green_weights, share, padded, grid),
+        [shape(16 * share + padded, 128)],
+        [place, wavevectors],
         smem=1,
-        hbm=9,
-        name="prep",
+        name="green",
     )
     low, basis, slope, unit, sums_one, gate_one = run(
         functools.partial(first_kernel, slots),
@@ -730,16 +783,23 @@
             shape(3, features, atoms),
             shape(features, atoms),
         ],
-        [ids, counts, embed, left, mix_high, mix_low] + cells,
+        [ids, counts, embed, kind_left, mix_high, mix_low] + cells,
         name="first",
     )
-    hidden = around(low)
+    hidden, hot = around(low, hot)
     edge_weights, near = run(
         functools.partial(second_near_kernel, slots),
         [shape(4, features, edges), shape(features, edges)],
-        [ids, basis, unit, left, hidden[1]],
+        [basis, unit, left, hot, hidden[1]],
         flops=2_000_000_000,
         name="second_near",
+    )
+    (near,) = run(
+        functools.partial(second_side_kernel, slots),
+        [shape(features, edges)],
+        [hot, near, hidden[2]],
+        flops=1_000_000_000,
+        name="second_side",
     )
     block_rows = -(-(lat_width + 9) // 16) * 16
     feature, sums_two, gate_two, packed, charge, energy, energy_slope = run(
@@ -753,30 +813,31 @@
             shape(1, atoms),
             shape(features, atoms),
         ],
-        [ids, edge_weights, near, mix_high, mix_low, hidden_high, hidden_low, hidden_turn_high,
-         hidden_turn_low, read_out, charge_pair, cells[1]] + hidden,
+        [hot, edge_weights, near, mix_high, mix_low, hidden_high, hidden_low, hidden_turn_high,
+         hidden_turn_low, read_out, charge_pair, cells[1], hidden[1], hidden[0]],
         name="second",
     )
     charges = [packed] + [shifted(packed, d, 0) for d in range(1, grid_x)]
     span = grid_x * atoms
     rows = 32 * share + 2 * padded
-    *phases, part = run(
+    *phases, own_part, part = run(
         functools.partial(structure_kernel, share, padded, grid, lat_width),
         [
             shape(padded, span),
             shape(padded, span),
             shape(8, span),
             shape(8, span),
+            shape(rows // 2, 2 * lat_width),
             shape(rows // 2, 2 * lat_width, dtype=BF16),
         ],
         [place] + charges,
         smem=1,
         name="structure",
     )
-    parts = [part] + [shifted(part, 0, d) for d in range(1, grid_y)]
+    parts = [own_part] + [shifted(part, 0, d) for d in range(1, grid_y)]
     folds = run(
         functools.partial(fold_kernel, share, padded, grid, lat_width),
-        [shape(block_rows, atoms, dtype=BF16)] * grid_x,
+        [shape(block_rows, atoms)] + [shape(block_rows, atoms, dtype=BF16)] * (grid_x - 1),
         [place] + phases + [weight] + charges + parts,
         smem=1,
         name="fold",
@@ -794,7 +855,7 @@
             shape(3, features, atoms, dtype=BF16),
             shape(3, features, atoms, dtype=BF16),
         ],
-        [ids, edge_weights, turn_high, turn_low, charge_pair, sums_two, gate_two, charge, energy,
+        [hot, edge_weights, turn_high, turn_low, charge_pair, sums_two, gate_two, charge, energy,
          energy_slope] + folds,
         name="second_back",
     )
@@ -802,7 +863,7 @@
     (middle,) = run(
         second_middle_kernel,
         [shape(3, features, atoms)],
-        [ids, term, cotangent],
+        [hot, term, cotangent],
         flops=1_000_000_000,
         name="second_middle",
     )
@@ -821,8 +882,8 @@
     before, middle, after = run(
         functools.partial(first_back_kernel, slots),
         [shape(3, 8, atoms)] * 3,
-        [ids, basis, slope, unit, embed, back, turn_high, turn_low, sums_one, gate_one, edge, long,
-         middle] + from_x + from_y,
+        [ids, basis, slope, unit, kind_high, kind_low, turn_high, turn_low, sums_one, gate_one, edge,
+         long, middle] + from_x + from_y,
         name="first_back",
     )
     total = middle + shifted(after, -1, 0) + shifted(before, 1, 0)

time: 111 us -> 113 us (1.018)
  starting transfers between devices: 40.4 us -> 36.3 us
  local copies, waits for them, and re-layouts: 8.77 us -> 12.2 us
  Pallas kernels: 24.9 us -> 26.9 us
    ppermute x33, starting transfers between devices: 40.4 us -> 36.3 us  [shifted(): return lax.ppermute(block, ('gx', 'gy'), route)]
    unnamed x23 -> x29, local copies, waits for them, and re-layouts: 8.77 us -> 12.2 us
    pallas_call x11 -> x15, Pallas kernels: 24.9 us -> 26.9 us  [run(): pl.pallas_call(kernel, out_shape=outs, in_specs=specs, out_specs=[whole()...]
  transfers between devices with their start and end apart: 33 -> 33, of which waited for: 22 -> 22; matrix products, arithmetic and copies ran while one was open for 0% -> 0% of each run, Pallas kernels for 6% -> 9%
where the time goes in v5:
time: 113 us; the launch traced here: 112 us
  starting transfers between devices  36.3 us (32%)
  waiting for transfers between devices  35.2 us (31%)
  Pallas kernels  26.9 us (24%)
  local copies, waits for them, and re-layouts  12.2 us (11%)
    ppermute x33, starting transfers between devices, shifted(): return lax.ppermute(block, ('gx', 'gy'), route)  36.3 us
    ppermute x33, waiting for transfers between devices, shifted(): return lax.ppermute(block, ('gx', 'gy'), route)  35.2 us
    pallas_call x15, Pallas kernels, run(): pl.pallas_call(kernel, out_shape=outs, in_specs=specs, out_specs=[whole()...  26.9 us
    unnamed x29, local copies, waits for them, and re-layouts  12.2 us
  transfers between devices with their start and end apart: 33, of which 22 were waited for; matrix products, arithmetic and copies ran while one was open for 0% of the time, Pallas kernels for 9%

profile of v5, /device:TPU:0, one launch (start us, length us, event | category | flops | bytes accessed | tf_op | source)
XLA Modules:
  0.0 112.3 jit_solution(10971842516393711615)
XLA Ops:
  0.6 1.3 %pack.1 = f32[8,128]{1,0:T(8,128)} custom-call(f32[1,3,1,256]{3,2,1,0:T(1,128)} %bitcast.35, s32[1,1,256]{2,1,0:T(1,128)} %species_ref.1), custom_call_target="tpu_custom_call" | custom-call | flops 10000000 | bytes 1000000 | tf_op jit(solution)/shard_map/pack/pallas_call | solution.py:49
  1.9 3.9 %collective-permute-start.1 = (f32[8,128]{1,0:T(8,128)}, f32[8,128]{1,0:T(8,128)S(1)}, u32[]{:S(2)}, u32[]{:S(2)}) collective-permute-start(f32[8,128]{1,0:T(8,128)} %pack.1), channel_id=1, source_target_pairs={{1,0},{2,1},{3,2},{0,3},{5,4},{6,5},{7,6},{4,7},{9,8},{10,9},{11,1... | collective-permute-start | bytes 12296 | tf_op jit(solution)/shard_map/ppermute | solution.py:32
  5.9 0.9 copy-done.5
  6.8 0.7 copy-done.9
  7.6 0.7 copy-done.10
  8.3 0.7 copy-done.11
  9.0 0.7 copy-done.12
  9.6 0.3 prep_first.1
  10.0 0.6 collective-permute-done
  10.6 0.7 pad_maximum_fusion.1.column_ref.cell_ref
  11.3 3.5 %collective-permute-start.3 = (f32[3,8,128]{2,1,0:T(8,128)S(1)}, f32[3,8,128]{2,1,0:T(8,128)S(1)}, u32[]{:S(2)}, u32[]{:S(2)}) collective-permute-start(f32[3,8,128]{2,1,0:T(8,128)S(1)} %pad_maximum_fusion.1.column_ref.cell_ref), channel_id=1, source_target_pairs={{4,0},{5,1},{6,2},{7,3},{8,4},{9,5},{10,6},{11,7},{12,8},{13,9},{1... | collective-permute-start | bytes 36872 | tf_op jit(solution)/shard_map/ppermute | solution.py:32
  14.8 1.4 %collective-permute-done.2.before_ref = f32[3,8,128]{2,1,0:T(8,128)S(1)} collective-permute-done((f32[3,8,128]{2,1,0:T(8,128)S(1)}, f32[3,8,128]{2,1,0:T(8,128)S(1)}, u32[]{:S(2)}, u32[]{:S(2)}) %collective-permute-start.2) | collective-permute-done | bytes 12320 | tf_op jit(solution)/shard_map/ppermute | solution.py:32
  16.2 1.6 %first.1 = (bf16[128,256]{1,0:T(8,128)(2,1)S(1)}, f32[8,3072]{1,0:T(8,128)S(1)}, f32[8,3072]{1,0:T(8,128)S(1)}, f32[8,3072]{1,0:T(8,128)S(1)}, f32[3,128,256]{2,1,0:T(8,128)S(1)}, /*index=5*/f32[128,256]{1,0:T(8,128)S(1)}) custom-call(s32[1,3072]{1,0:T(1,128)S(1)} %get-tuple-element.64.ids_ref, s32[1,1,256]{2,1,0:T(1,128)S(1)} %get-tuple-element.65.count_ref, ...), custom_call_target="tpu_custom_call" | custom-call | flops 10000000 | bytes 1000000 | tf_op jit(solution)/shard_map/first/pallas_call | solution.py:49
  17.9 2.3 %collective-permute-start.5 = (bf16[128,256]{1,0:T(8,128)(2,1)S(1)}, bf16[128,256]{1,0:T(8,128)(2,1)S(1)}, u32[]{:S(2)}, u32[]{:S(2)}) collective-permute-start(bf16[128,256]{1,0:T(8,128)(2,1)S(1)} %get-tuple-element.81), channel_id=1, source_target_pairs={{1,0},{2,1},{3,2},{0,3},{5,4},{6,5},{7,6},{4,7},{9,8},{10,9},{11,1... | collective-permute-start | bytes 196616 | tf_op jit(solution)/shard_map/ppermute | solution.py:32
  20.2 3.2 %hot.1.hot_ref = bf16[2304,3072]{1,0:T(8,128)(2,1)S(1)} custom-call(s32[1,3072]{1,0:T(1,128)S(1)} %get-tuple-element.64.ids_ref), custom_call_target="tpu_custom_call" | custom-call | flops 2000000000 | bytes 1000000 | tf_op jit(solution)/shard_map/hot/pallas_call | solution.py:49
  23.5 1.9 %collective-permute-done.4 = bf16[128,256]{1,0:T(8,128)(2,1)S(1)} collective-permute-done((bf16[128,256]{1,0:T(8,128)(2,1)S(1)}, bf16[128,256]{1,0:T(8,128)(2,1)S(1)}, u32[]{:S(2)}, u32[]{:S(2)}) %collective-permute-start.4) | collective-permute-done | bytes 65568 | tf_op jit(solution)/shard_map/ppermute | solution.py:32
  25.4 2.1 %collective-permute-start.6 = (bf16[3,128,256]{2,1,0:T(8,128)(2,1)S(1)}, bf16[3,128,256]{2,1,0:T(8,128)(2,1)S(1)}, u32[]{:S(2)}, u32[]{:S(2)}) collective-permute-start(bf16[3,128,256]{2,1,0:T(8,128)(2,1)S(1)} %pad_maximum_fusion.column_ref), channel_id=1, source_target_pairs={{4,0},{5,1},{6,2},{7,3},{8,4},{9,5},{10,6},{11,7},{12,8},{13,9},{1... | collective-permute-start | bytes 589832 | tf_op jit(solution)/shard_map/ppermute | solution.py:32
  27.9 1.6 %second_near.1 = (f32[4,128,3072]{2,1,0:T(8,128)S(1)}, f32[128,3072]{1,0:T(8,128)S(1)}) custom-call(f32[8,3072]{1,0:T(8,128)S(1)} %get-tuple-element.71.basis_ref, f32[8,3072]{1,0:T(8,128)S(1)} %get-tuple-element.73.unit_ref, bf16[2,128,32]{2,1,0:T(8,128)(2,1)S(1)} %get-tuple-element.83.left_ref, bf16[2304,3072]{1,0:T(8,128)(2,1)S(1)} %hot.1.hot_ref, ...), custom_call_target="tpu_custom_call" | custom-call | flops 2000000000 | bytes 1000000 | tf_op jit(solution)/shard_map/second_near/pallas_call | solution.py:49
  29.5 1.4 %collective-permute-done.6.after_ref = bf16[3,128,256]{2,1,0:T(8,128)(2,1)S(1)} collective-permute-done((bf16[3,128,256]{2,1,0:T(8,128)(2,1)S(1)}, bf16[3,128,256]{2,1,0:T(8,128)(2,1)S(1)}, u32[]{:S(2)}, u32[]{:S(2)}) %collective-permute-start.6) | collective-permute-done | bytes 196640 | tf_op jit(solution)/shard_map/ppermute | solution.py:32
  30.9 0.8 second_side.1.near_ref
  31.8 3.0 %collective-permute-done.7.before_ref = bf16[3,128,256]{2,1,0:T(8,128)(2,1)S(1)} collective-permute-done((bf16[3,128,256]{2,1,0:T(8,128)(2,1)S(1)}, bf16[3,128,256]{2,1,0:T(8,128)(2,1)S(1)}, u32[]{:S(2)}, u32[]{:S(2)}) %collective-permute-start.7) | collective-permute-done | bytes 196640 | tf_op jit(solution)/shard_map/ppermute | solution.py:32
  34.8 2.2 %second.1 = (bf16[128,3072]{1,0:T(8,128)(2,1)S(1)}, f32[3,128,256]{2,1,0:T(8,128)S(1)}, f32[128,256]{1,0:T(8,128)S(1)}, bf16[80,256]{1,0:T(8,128)(2,1)S(1)}, f32...) custom-call(bf16[2304,3072]{1,0:T(8,128)(2,1)S(1)} %hot.1.hot_ref, ...), custom_call_target="tpu_custom_call" | custom-call | flops 10000000 | bytes 1000000 | tf_op jit(solution)/shard_map/second/pallas_call | solution.py:49
  37.0 0.9 collective-permute-start.8
  37.9 2.7 %collective-permute-start.11 = (bf16[80,256]{1,0:T(8,128)(2,1)S(1)}, bf16[80,256]{1,0:T(8,128)(2,1)S(1)}, u32[]{:S(2)}, u32[]{:S(2)}) collective-permute-start(bf16[80,256]{1,0:T(8,128)(2,1)S(1)} %get-tuple-element.99.refs_0_), channel_id=1, source_target_pairs={{16,0},{17,1},{18,2},{19,3},{20,4},{21,5},{22,6},{23,7},{24,8},{25... | collective-permute-start | bytes 122888 | tf_op jit(solution)/shard_map/ppermute | solution.py:32
  40.6 1.2 %collective-permute-start.13 = (bf16[80,256]{1,0:T(8,128)(2,1)S(1)}, bf16[80,256]{1,0:T(8,128)(2,1)S(1)}, u32[]{:S(2)}, u32[]{:S(2)}) collective-permute-start(bf16[80,256]{1,0:T(8,128)(2,1)S(1)} %get-tuple-element.99.refs_0_), channel_id=1, source_target_pairs={{24,0},{25,1},{26,2},{27,3},{28,4},{29,5},{30,6},{31,7},{0,8},{1,9... | collective-permute-start | bytes 122888 | tf_op jit(solution)/shard_map/ppermute | solution.py:32
  41.9 0.8 collective-permute-start.14
  42.8 2.2 %collective-permute-done.11.refs_4_ = bf16[80,256]{1,0:T(8,128)(2,1)S(1)} collective-permute-done((bf16[80,256]{1,0:T(8,128)(2,1)S(1)}, bf16[80,256]{1,0:T(8,128)(2,1)S(1)}, u32[]{:S(2)}, u32[]{:S(2)}) %collective-permute-start.11) | collective-permute-done | bytes 40992 | tf_op jit(solution)/shard_map/ppermute | solution.py:32
  45.0 2.8 %collective-permute-done.12.refs_5_ = bf16[80,256]{1,0:T(8,128)(2,1)S(1)} collective-permute-done((bf16[80,256]{1,0:T(8,128)(2,1)S(1)}, bf16[80,256]{1,0:T(8,128)(2,1)S(1)}, u32[]{:S(2)}, u32[]{:S(2)}) %collective-permute-start.12) | collective-permute-done | bytes 40992 | tf_op jit(solution)/shard_map/ppermute | solution.py:32
  47.9 2.5 %structure.1 = (f32[32,2048]{1,0:T(8,128)S(1)}, f32[32,2048]{1,0:T(8,128)S(1)}, f32[8,2048]{1,0:T(8,128)S(1)}, f32[8,2048]{1,0:T(8,128)S(1)}, f32[320,128]{1,0:T(8,128)S(1)}, /*index=5*/bf16[320,128]{1,0:T(8,128)(2,1)S(1)}) custom-call(s32[2]{0:T(128)S(1)} %pad_add_fusion.place_ref, bf16[80,256]{1,0:T(8,128)(2,1)S(1)} %get-tuple-element.99.refs_0_, ...), custom_call_target="tpu_custom_call" | custom-call | flops 10000000 | bytes 1000000 | tf_op jit(solution)/shard_map/structure/pallas_call | solution.py:49
  50.4 1.9 %collective-permute-start.15 = (bf16[320,128]{1,0:T(8,128)(2,1)S(1)}, bf16[320,128]{1,0:T(8,128)(2,1)S(1)}, u32[]{:S(2)}, u32[]{:S(2)}) collective-permute-start(bf16[320,128]{1,0:T(8,128)(2,1)S(1)} %get-tuple-element.105), channel_id=1, source_target_pairs={{1,0},{2,1},{3,2},{0,3},{5,4},{6,5},{7,6},{4,7},{9,8},{10,9},{11,1... | collective-permute-start | bytes 245768 | tf_op jit(solution)/shard_map/ppermute | solution.py:32
  52.3 0.5 collective-permute-start.16
  53.0 1.3 %green.1.weight_ref = f32[320,128]{1,0:T(8,128)S(1)} custom-call(s32[2]{0:T(128)S(1)} %pad_add_fusion.place_ref, s32[3,4096]{1,0:T(4,128)S(1)} %copy-done.6), custom_call_target="tpu_custom_call" | custom-call | flops 10000000 | bytes 1000000 | tf_op jit(solution)/shard_map/green/pallas_call | solution.py:49
  54.3 1.2 %collective-permute-done.15.refs_9_ = bf16[320,128]{1,0:T(8,128)(2,1)S(1)} collective-permute-done((bf16[320,128]{1,0:T(8,128)(2,1)S(1)}, bf16[320,128]{1,0:T(8,128)(2,1)S(1)}, u32[]{:S(2)}, u32[]{:S(2)}) %collective-permute-start.15) | collective-permute-done | bytes 81952 | tf_op jit(solution)/shard_map/ppermute | solution.py:32
  55.5 1.2 %collective-permute-done.16.refs_10_ = bf16[320,128]{1,0:T(8,128)(2,1)S(1)} collective-permute-done((bf16[320,128]{1,0:T(8,128)(2,1)S(1)}, bf16[320,128]{1,0:T(8,128)(2,1)S(1)}, u32[]{:S(2)}, u32[]{:S(2)}) %collective-permute-start.16) | collective-permute-done | bytes 81952 | tf_op jit(solution)/shard_map/ppermute | solution.py:32
  56.7 1.4 %collective-permute-done.17.refs_11_ = bf16[320,128]{1,0:T(8,128)(2,1)S(1)} collective-permute-done((bf16[320,128]{1,0:T(8,128)(2,1)S(1)}, bf16[320,128]{1,0:T(8,128)(2,1)S(1)}, u32[]{:S(2)}, u32[]{:S(2)}) %collective-permute-start.17) | collective-permute-done | bytes 81952 | tf_op jit(solution)/shard_map/ppermute | solution.py:32
  58.1 3.0 %fold.1 = (f32[80,256]{1,0:T(8,128)S(1)}, bf16[80,256]{1,0:T(8,128)(2,1)S(1)}, bf16[80,256]{1,0:T(8,128)(2,1)S(1)}, bf16[80,256]{1,0:T(8,128)(2,1)S(1)}, bf16[80...) custom-call(s32[2]{0:T(128)S(1)} %pad_add_fusion.place_ref, ...), custom_call_target="tpu_custom_call" | custom-call | flops 10000000 | bytes 1000000 | tf_op jit(solution)/shard_map/fold/pallas_call | solution.py:49
  61.3 1.6 %collective-permute-start.20 = (bf16[80,256]{1,0:T(8,128)(2,1)S(1)}, bf16[80,256]{1,0:T(8,128)(2,1)S(1)}, u32[]{:S(2)}, u32[]{:S(2)}) collective-permute-start(bf16[80,256]{1,0:T(8,128)(2,1)S(1)} %get-tuple-element.109), channel_id=1, source_target_pairs={{20,0},{21,1},{22,2},{23,3},{24,4},{25,5},{26,6},{27,7},{28,8},{29... | collective-permute-start | bytes 122888 | tf_op jit(solution)/shard_map/ppermute | solution.py:32
  62.9 2.5 %collective-permute-start.21 = (bf16[80,256]{1,0:T(8,128)(2,1)S(1)}, bf16[80,256]{1,0:T(8,128)(2,1)S(1)}, u32[]{:S(2)}, u32[]{:S(2)}) collective-permute-start(bf16[80,256]{1,0:T(8,128)(2,1)S(1)} %get-tuple-element.110), channel_id=1, source_target_pairs={{16,0},{17,1},{18,2},{19,3},{20,4},{21,5},{22,6},{23,7},{24,8},{25... | collective-permute-start | bytes 122888 | tf_op jit(solution)/shard_map/ppermute | solution.py:32
  65.4 1.1 collective-permute-done.18.refs_1_
  66.4 1.6 %collective-permute-start.23 = (bf16[80,256]{1,0:T(8,128)(2,1)S(1)}, bf16[80,256]{1,0:T(8,128)(2,1)S(1)}, u32[]{:S(2)}, u32[]{:S(2)}) collective-permute-start(bf16[80,256]{1,0:T(8,128)(2,1)S(1)} %get-tuple-element.112), channel_id=1, source_target_pairs={{8,0},{9,1},{10,2},{11,3},{12,4},{13,5},{14,6},{15,7},{16,8},{17,9... | collective-permute-start | bytes 122888 | tf_op jit(solution)/shard_map/ppermute | solution.py:32
  68.0 1.0 collective-permute-start.24
  69.0 0.4 collective-permute-done.20.refs_3_
  69.4 0.8 collective-permute-done.21.refs_4_
  70.2 0.9 collective-permute-done.23.refs_6_
  71.1 5.0 %copy-done.1 = bf16[2304,3072]{1,0:T(8,128)(2,1)S(1)} copy-done((bf16[2304,3072]{1,0:T(8,128)(2,1)S(1)}, bf16[2304,3072]{1,0:T(8,128)(2,1)}, u32[]{:S(2)}) %copy-start.1) | copy-done | bytes 14155800
  76.1 2.8 %copy-done.4 = f32[4,128,3072]{2,1,0:T(8,128)S(1)} copy-done((f32[4,128,3072]{2,1,0:T(8,128)S(1)}, f32[4,128,3072]{2,1,0:T(8,128)}, u32[]{:S(2)}) %copy-start.4) | copy-done | bytes 6291480
  78.9 4.3 %second_back.1 = (f32[1,1,256]{2,1,0:T(1,128)}, f32[8,256]{1,0:T(8,128)S(1)}, f32[128,256]{1,0:T(8,128)S(1)}, f32[4,128,256]{2,1,0:T(8,128)S(1)}, bf16[128,3072]...) custom-call(bf16[2304,3072]{1,0:T(8,128)(2,1)S(1)} %copy-done.1, ...), custom_call_target="tpu_custom_call" | custom-call | flops 10000000 | bytes 1000000 | tf_op jit(solution)/shard_map/second_back/pallas_call | solution.py:49
  83.3 0.8 collective-permute-start.25
  84.1 2.7 %collective-permute-start.26 = (bf16[3,128,256]{2,1,0:T(8,128)(2,1)S(1)}, bf16[3,128,256]{2,1,0:T(8,128)(2,1)S(1)}, u32[]{:S(2)}, u32[]{:S(2)}) collective-permute-start(bf16[3,128,256]{2,1,0:T(8,128)(2,1)S(1)} %get-tuple-element.119), channel_id=1, source_target_pairs={{4,0},{5,1},{6,2},{7,3},{8,4},{9,5},{10,6},{11,7},{12,8},{13,9},{1... | collective-permute-start | bytes 589832 | tf_op jit(solution)/shard_map/ppermute | solution.py:32
  86.8 1.6 %second_middle.1.middle_ref = f32[3,128,256]{2,1,0:T(8,128)S(1)} custom-call(bf16[2304,3072]{1,0:T(8,128)(2,1)S(1)} %copy-done.2, bf16[128,3072]{1,0:T(8,128)(2,1)S(1)} %get-tuple-element.116.term_ref, f32[128,256]{1,0:T(8,128)S(1)} %get-tuple-element.117.cotangent_ref), custom_call_target="tpu_custom_call" | custom-call | flops 1000000000 | bytes 1000000 | tf_op jit(solution)/shard_map/second_middle/pallas_call | solution.py:49
  88.5 2.3 %collective-permute-done.25.refs_0_ = bf16[3,128,256]{2,1,0:T(8,128)(2,1)S(1)} collective-permute-done((bf16[3,128,256]{2,1,0:T(8,128)(2,1)S(1)}, bf16[3,128,256]{2,1,0:T(8,128)(2,1)S(1)}, u32[]{:S(2)}, u32[]{:S(2)}) %collective-permute-start.25) | collective-permute-done | bytes 196640 | tf_op jit(solution)/shard_map/ppermute | solution.py:32
  90.9 2.9 %collective-permute-start.28 = (bf16[128,256]{1,0:T(8,128)(2,1)S(1)}, bf16[128,256]{1,0:T(8,128)(2,1)S(1)}, u32[]{:S(2)}, u32[]{:S(2)}) collective-permute-start(bf16[128,256]{1,0:T(8,128)(2,1)S(1)} %get-tuple-element.126), channel_id=1, source_target_pairs={{1,0},{2,1},{3,2},{0,3},{5,4},{6,5},{7,6},{4,7},{9,8},{10,9},{11,1... | collective-permute-start | bytes 196616 | tf_op jit(solution)/shard_map/ppermute | solution.py:32
  93.8 1.2 %second_edge.1.edge_ref = f32[32,3072]{1,0:T(8,128)S(1)} custom-call(bf16[2,16,256]{2,1,0:T(8,128)(2,1)S(1)} %get-tuple-element.80.back_ref, bf16[128,3072]{1,0:T(8,128)(2,1)S(1)} %get-tuple-element.93.feature_ref, f32[4,128,256]{2,1,0:T(8,128)S(1)} %get-tuple-element.114.grad_ref), custom_call_target="tpu_custom_call" | custom-call | flops 1000000000 | bytes 1000000 | tf_op jit(solution)/shard_map/second_edge/pallas_call | solution.py:49
  95.0 1.5 %collective-permute-done.27.refs_2_ = bf16[128,256]{1,0:T(8,128)(2,1)S(1)} collective-permute-done((bf16[128,256]{1,0:T(8,128)(2,1)S(1)}, bf16[128,256]{1,0:T(8,128)(2,1)S(1)}, u32[]{:S(2)}, u32[]{:S(2)}) %collective-permute-start.27) | collective-permute-done | bytes 65568 | tf_op jit(solution)/shard_map/ppermute | solution.py:32
  96.5 1.6 %collective-permute-done.28.refs_3_ = bf16[128,256]{1,0:T(8,128)(2,1)S(1)} collective-permute-done((bf16[128,256]{1,0:T(8,128)(2,1)S(1)}, bf16[128,256]{1,0:T(8,128)(2,1)S(1)}, u32[]{:S(2)}, u32[]{:S(2)}) %collective-permute-start.28) | collective-permute-done | bytes 65568 | tf_op jit(solution)/shard_map/ppermute | solution.py:32
  98.1 1.5 %first_back.1 = (f32[3,8,256]{2,1,0:T(8,128)S(1)}, f32[3,8,256]{2,1,0:T(8,128)S(1)}, f32[3,8,256]{2,1,0:T(8,128)S(1)}) custom-call(s32[1,3072]{1,0:T(1,128)S(1)} %get-tuple-element.64.ids_ref, f32[8,3072]{1,0:T(8,128)S(1)} %get-tuple-element.71.basis_ref, f32[8,3072]{1,0:T(8,128)S(1)} %get-tuple-element.72.slope_ref, ...), custom_call_target="tpu_custom_call" | custom-call | flops 10000000 | bytes 1000000 | tf_op jit(solution)/shard_map/first_back/pallas_call | solution.py:49
  99.6 0.7 collective-permute-start.30
  100.3 1.5 %collective-permute-done.30 = f32[3,8,256]{2,1,0:T(8,128)S(1)} collective-permute-done((f32[3,8,256]{2,1,0:T(8,128)S(1)}, f32[3,8,256]{2,1,0:T(8,128)S(1)}, u32[]{:S(2)}, u32[]{:S(2)}) %collective-permute-start.30) | collective-permute-done | bytes 24608 | tf_op jit(solution)/shard_map/ppermute | solution.py:32
  101.9 3.5 %collective-permute-done.29 = f32[3,8,256]{2,1,0:T(8,128)S(1)} collective-permute-done((f32[3,8,256]{2,1,0:T(8,128)S(1)}, f32[3,8,256]{2,1,0:T(8,128)S(1)}, u32[]{:S(2)}, u32[]{:S(2)}) %collective-permute-start.29) | collective-permute-done | bytes 24608 | tf_op jit(solution)/shard_map/ppermute | solution.py:32
  105.4 1.8 %collective-permute-start.32 = (f32[8,256]{1,0:T(8,128)S(1)}, f32[8,256]{1,0:T(8,128)S(1)}, u32[]{:S(2)}, u32[]{:S(2)}) collective-permute-start(f32[8,256]{1,0:T(8,128)S(1)} %get-tuple-element.129), channel_id=1, source_target_pairs={{1,0},{2,1},{3,2},{0,3},{5,4},{6,5},{7,6},{4,7},{9,8},{10,9},{11,1... | collective-permute-start | bytes 24584 | tf_op jit(solution)/shard_map/ppermute | solution.py:32
  107.2 0.3 collective-permute-start.31
  107.5 1.6 %collective-permute-done.32 = f32[8,256]{1,0:T(8,128)S(1)} collective-permute-done((f32[8,256]{1,0:T(8,128)S(1)}, f32[8,256]{1,0:T(8,128)S(1)}, u32[]{:S(2)}, u32[]{:S(2)}) %collective-permute-start.32) | collective-permute-done | bytes 8224 | tf_op jit(solution)/shard_map/ppermute | solution.py:32
  109.1 2.6 %collective-permute-done.31 = f32[8,256]{1,0:T(8,128)S(1)} collective-permute-done((f32[8,256]{1,0:T(8,128)S(1)}, f32[8,256]{1,0:T(8,128)S(1)}, u32[]{:S(2)}, u32[]{:S(2)}) %collective-permute-start.31) | collective-permute-done | bytes 8224 | tf_op jit(solution)/shard_map/ppermute | solution.py:32
  111.7 0.6 copy.13
  (53 shorter events, 1.0 us)
Async XLA Ops:
  1.9 8.0 %collective-permute-start.1 = (f32[8,128]{1,0:T(8,128)}, f32[8,128]{1,0:T(8,128)S(1)}, u32[]{:S(2)}, u32[]{:S(2)}) collective-permute-start(f32[8,128]{1,0:T(8,128)} %pack.1), channel_id=1, source_target_pairs={{1,0},{2,1},{3,2},{0,3},{5,4},{6,5},{7,6},{4,7},{9,8},{10,9},{11,1... | collective-permute-start | bytes 12296 | tf_op jit(solution)/shard_map/ppermute | solution.py:32
  5.9 4.7 %collective-permute-start = (f32[8,128]{1,0:T(8,128)}, f32[8,128]{1,0:T(8,128)S(1)}, u32[]{:S(2)}, u32[]{:S(2)}) collective-permute-start(f32[8,128]{1,0:T(8,128)} %pack.1), channel_id=1, source_target_pairs={{3,0},{0,1},{1,2},{2,3},{7,4},{4,5},{5,6},{6,7},{11,8},{8,9},{9,10... | collective-permute-start | bytes 12296 | tf_op jit(solution)/shard_map/ppermute | solution.py:32
  5.9 1.0 copy-start.5
  6.8 0.7 copy-start.9
  7.6 0.7 copy-start.10
  8.3 0.7 copy-start.11
  9.0 0.7 copy-start.12
  11.3 4.9 %collective-permute-start.2 = (f32[3,8,128]{2,1,0:T(8,128)S(1)}, f32[3,8,128]{2,1,0:T(8,128)S(1)}, u32[]{:S(2)}, u32[]{:S(2)}) collective-permute-start(f32[3,8,128]{2,1,0:T(8,128)S(1)} %pad_maximum_fusion.1.column_ref.cell_ref), channel_id=1, source_target_pairs={{28,0},{29,1},{30,2},{31,3},{0,4},{1,5},{2,6},{3,7},{4,8},{5,9},{6... | collective-permute-start | bytes 36872 | tf_op jit(solution)/shard_map/ppermute | solution.py:32
  11.3 4.9 %collective-permute-start.3 = (f32[3,8,128]{2,1,0:T(8,128)S(1)}, f32[3,8,128]{2,1,0:T(8,128)S(1)}, u32[]{:S(2)}, u32[]{:S(2)}) collective-permute-start(f32[3,8,128]{2,1,0:T(8,128)S(1)} %pad_maximum_fusion.1.column_ref.cell_ref), channel_id=1, source_target_pairs={{4,0},{5,1},{6,2},{7,3},{8,4},{9,5},{10,6},{11,7},{12,8},{13,9},{1... | collective-permute-start | bytes 36872 | tf_op jit(solution)/shard_map/ppermute | solution.py:32
  17.9 9.7 %copy-start.7 = (f32[128,128]{1,0:T(8,128)S(1)}, f32[128,128]{1,0:T(8,128)}, u32[]{:S(2)}) copy-start(f32[128,128]{1,0:T(8,128)} %hidden_in.1) | copy-start | bytes 196612
  17.9 9.7 %copy-start.8 = (f32[128,64]{0,1:T(8,128)S(1)}, f32[128,64]{0,1:T(8,128)}, u32[]{:S(2)}) copy-start(f32[128,64]{0,1:T(8,128)} %param.20) | copy-start | bytes 98308
  17.9 9.7 %copy-start.13 = (f32[128]{0:T(128)S(1)}, f32[128]{0:T(128)}, u32[]{:S(2)}) copy-start(f32[128]{0:T(128)} %param.19) | copy-start | bytes 1540
  17.9 5.6 %collective-permute-start.5 = (bf16[128,256]{1,0:T(8,128)(2,1)S(1)}, bf16[128,256]{1,0:T(8,128)(2,1)S(1)}, u32[]{:S(2)}, u32[]{:S(2)}) collective-permute-start(bf16[128,256]{1,0:T(8,128)(2,1)S(1)} %get-tuple-element.81), channel_id=1, source_target_pairs={{1,0},{2,1},{3,2},{0,3},{5,4},{6,5},{7,6},{4,7},{9,8},{10,9},{11,1... | collective-permute-start | bytes 196616 | tf_op jit(solution)/shard_map/ppermute | solution.py:32
  20.2 5.2 %collective-permute-start.4 = (bf16[128,256]{1,0:T(8,128)(2,1)S(1)}, bf16[128,256]{1,0:T(8,128)(2,1)S(1)}, u32[]{:S(2)}, u32[]{:S(2)}) collective-permute-start(bf16[128,256]{1,0:T(8,128)(2,1)S(1)} %get-tuple-element.81), channel_id=1, source_target_pairs={{3,0},{0,1},{1,2},{2,3},{7,4},{4,5},{5,6},{6,7},{11,8},{8,9},{9,10... | collective-permute-start | bytes 196616 | tf_op jit(solution)/shard_map/ppermute | solution.py:32
  23.5 11.3 %copy-start = (bf16[2304,3072]{1,0:T(8,128)(2,1)}, bf16[2304,3072]{1,0:T(8,128)(2,1)S(1)}, u32[]{:S(2)}) copy-start(bf16[2304,3072]{1,0:T(8,128)(2,1)S(1)} %hot.1.hot_ref) | copy-start | bytes 42467332
  25.4 5.5 %collective-permute-start.6 = (bf16[3,128,256]{2,1,0:T(8,128)(2,1)S(1)}, bf16[3,128,256]{2,1,0:T(8,128)(2,1)S(1)}, u32[]{:S(2)}, u32[]{:S(2)}) collective-permute-start(bf16[3,128,256]{2,1,0:T(8,128)(2,1)S(1)} %pad_maximum_fusion.column_ref), channel_id=1, source_target_pairs={{4,0},{5,1},{6,2},{7,3},{8,4},{9,5},{10,6},{11,7},{12,8},{13,9},{1... | collective-permute-start | bytes 589832 | tf_op jit(solution)/shard_map/ppermute | solution.py:32
  27.8 6.9 %collective-permute-start.7 = (bf16[3,128,256]{2,1,0:T(8,128)(2,1)S(1)}, bf16[3,128,256]{2,1,0:T(8,128)(2,1)S(1)}, u32[]{:S(2)}, u32[]{:S(2)}) collective-permute-start(bf16[3,128,256]{2,1,0:T(8,128)(2,1)S(1)} %pad_maximum_fusion.column_ref), channel_id=1, source_target_pairs={{28,0},{29,1},{30,2},{31,3},{0,4},{1,5},{2,6},{3,7},{4,8},{5,9},{6... | collective-permute-start | bytes 589832 | tf_op jit(solution)/shard_map/ppermute | solution.py:32
  29.5 5.3 %copy-start.3 = (f32[4,128,3072]{2,1,0:T(8,128)}, f32[4,128,3072]{2,1,0:T(8,128)S(1)}, u32[]{:S(2)}) copy-start(f32[4,128,3072]{2,1,0:T(8,128)S(1)} %get-tuple-element.85.weight_ref) | copy-start | bytes 18874372
  34.8 18.2 %copy-start.6 = (s32[3,4096]{1,0:T(4,128)S(1)}, s32[3,4096]{1,0:T(4,128)}, u32[]{:S(2)}) copy-start(s32[3,4096]{1,0:T(4,128)} %vec_ref.1) | copy-start | bytes 147460
  37.0 3.6 %collective-permute-start.8 = (bf16[80,256]{1,0:T(8,128)(2,1)S(1)}, bf16[80,256]{1,0:T(8,128)(2,1)S(1)}, u32[]{:S(2)}, u32[]{:S(2)}) collective-permute-start(bf16[80,256]{1,0:T(8,128)(2,1)S(1)} %get-tuple-element.99.refs_0_), channel_id=1, source_target_pairs={{4,0},{5,1},{6,2},{7,3},{8,4},{9,5},{10,6},{11,7},{12,8},{13,9},{1... | collective-permute-start | bytes 122888 | tf_op jit(solution)/shard_map/ppermute | solution.py:32
  37.9 4.0 %collective-permute-start.9 = (bf16[80,256]{1,0:T(8,128)(2,1)S(1)}, bf16[80,256]{1,0:T(8,128)(2,1)S(1)}, u32[]{:S(2)}, u32[]{:S(2)}) collective-permute-start(bf16[80,256]{1,0:T(8,128)(2,1)S(1)} %get-tuple-element.99.refs_0_), channel_id=1, source_target_pairs={{8,0},{9,1},{10,2},{11,3},{12,4},{13,5},{14,6},{15,7},{16,8},{17,9... | collective-permute-start | bytes 122888 | tf_op jit(solution)/shard_map/ppermute | solution.py:32
  37.9 4.9 %collective-permute-start.10 = (bf16[80,256]{1,0:T(8,128)(2,1)S(1)}, bf16[80,256]{1,0:T(8,128)(2,1)S(1)}, u32[]{:S(2)}, u32[]{:S(2)}) collective-permute-start(bf16[80,256]{1,0:T(8,128)(2,1)S(1)} %get-tuple-element.99.refs_0_), channel_id=1, source_target_pairs={{12,0},{13,1},{14,2},{15,3},{16,4},{17,5},{18,6},{19,7},{20,8},{21... | collective-permute-start | bytes 122888 | tf_op jit(solution)/shard_map/ppermute | solution.py:32
  37.9 7.1 %collective-permute-start.11 = (bf16[80,256]{1,0:T(8,128)(2,1)S(1)}, bf16[80,256]{1,0:T(8,128)(2,1)S(1)}, u32[]{:S(2)}, u32[]{:S(2)}) collective-permute-start(bf16[80,256]{1,0:T(8,128)(2,1)S(1)} %get-tuple-element.99.refs_0_), channel_id=1, source_target_pairs={{16,0},{17,1},{18,2},{19,3},{20,4},{21,5},{22,6},{23,7},{24,8},{25... | collective-permute-start | bytes 122888 | tf_op jit(solution)/shard_map/ppermute | solution.py:32
  40.6 7.2 %collective-permute-start.12 = (bf16[80,256]{1,0:T(8,128)(2,1)S(1)}, bf16[80,256]{1,0:T(8,128)(2,1)S(1)}, u32[]{:S(2)}, u32[]{:S(2)}) collective-permute-start(bf16[80,256]{1,0:T(8,128)(2,1)S(1)} %get-tuple-element.99.refs_0_), channel_id=1, source_target_pairs={{20,0},{21,1},{22,2},{23,3},{24,4},{25,5},{26,6},{27,7},{28,8},{29... | collective-permute-start | bytes 122888 | tf_op jit(solution)/shard_map/ppermute | solution.py:32
  40.6 7.2 %collective-permute-start.13 = (bf16[80,256]{1,0:T(8,128)(2,1)S(1)}, bf16[80,256]{1,0:T(8,128)(2,1)S(1)}, u32[]{:S(2)}, u32[]{:S(2)}) collective-permute-start(bf16[80,256]{1,0:T(8,128)(2,1)S(1)} %get-tuple-element.99.refs_0_), channel_id=1, source_target_pairs={{24,0},{25,1},{26,2},{27,3},{28,4},{29,5},{30,6},{31,7},{0,8},{1,9... | collective-permute-start | bytes 122888 | tf_op jit(solution)/shard_map/ppermute | solution.py:32
  41.9 6.0 %collective-permute-start.14 = (bf16[80,256]{1,0:T(8,128)(2,1)S(1)}, bf16[80,256]{1,0:T(8,128)(2,1)S(1)}, u32[]{:S(2)}, u32[]{:S(2)}) collective-permute-start(bf16[80,256]{1,0:T(8,128)(2,1)S(1)} %get-tuple-element.99.refs_0_), channel_id=1, source_target_pairs={{28,0},{29,1},{30,2},{31,3},{0,4},{1,5},{2,6},{3,7},{4,8},{5,9},{6... | collective-permute-start | bytes 122888 | tf_op jit(solution)/shard_map/ppermute | solution.py:32
  50.4 5.1 %collective-permute-start.15 = (bf16[320,128]{1,0:T(8,128)(2,1)S(1)}, bf16[320,128]{1,0:T(8,128)(2,1)S(1)}, u32[]{:S(2)}, u32[]{:S(2)}) collective-permute-start(bf16[320,128]{1,0:T(8,128)(2,1)S(1)} %get-tuple-element.105), channel_id=1, source_target_pairs={{1,0},{2,1},{3,2},{0,3},{5,4},{6,5},{7,6},{4,7},{9,8},{10,9},{11,1... | collective-permute-start | bytes 245768 | tf_op jit(solution)/shard_map/ppermute | solution.py:32
  52.3 4.4 %collective-permute-start.16 = (bf16[320,128]{1,0:T(8,128)(2,1)S(1)}, bf16[320,128]{1,0:T(8,128)(2,1)S(1)}, u32[]{:S(2)}, u32[]{:S(2)}) collective-permute-start(bf16[320,128]{1,0:T(8,128)(2,1)S(1)} %get-tuple-element.105), channel_id=1, source_target_pairs={{2,0},{3,1},{0,2},{1,3},{6,4},{7,5},{4,6},{5,7},{10,8},{11,9},{8,1... | collective-permute-start | bytes 245768 | tf_op jit(solution)/shard_map/ppermute | solution.py:32
  52.8 5.3 %collective-permute-start.17 = (bf16[320,128]{1,0:T(8,128)(2,1)S(1)}, bf16[320,128]{1,0:T(8,128)(2,1)S(1)}, u32[]{:S(2)}, u32[]{:S(2)}) collective-permute-start(bf16[320,128]{1,0:T(8,128)(2,1)S(1)} %get-tuple-element.105), channel_id=1, source_target_pairs={{3,0},{0,1},{1,2},{2,3},{7,4},{4,5},{5,6},{6,7},{11,8},{8,9},{9,10... | collective-permute-start | bytes 245768 | tf_op jit(solution)/shard_map/ppermute | solution.py:32
  61.1 5.3 %collective-permute-start.18 = (bf16[80,256]{1,0:T(8,128)(2,1)S(1)}, bf16[80,256]{1,0:T(8,128)(2,1)S(1)}, u32[]{:S(2)}, u32[]{:S(2)}) collective-permute-start(bf16[80,256]{1,0:T(8,128)(2,1)S(1)} %get-tuple-element.107), channel_id=1, source_target_pairs={{28,0},{29,1},{30,2},{31,3},{0,4},{1,5},{2,6},{3,7},{4,8},{5,9},{6... | collective-permute-start | bytes 122888 | tf_op jit(solution)/shard_map/ppermute | solution.py:32
  61.2 6.8 %collective-permute-start.19 = (bf16[80,256]{1,0:T(8,128)(2,1)S(1)}, bf16[80,256]{1,0:T(8,128)(2,1)S(1)}, u32[]{:S(2)}, u32[]{:S(2)}) collective-permute-start(bf16[80,256]{1,0:T(8,128)(2,1)S(1)} %get-tuple-element.108), channel_id=1, source_target_pairs={{24,0},{25,1},{26,2},{27,3},{28,4},{29,5},{30,6},{31,7},{0,8},{1,9... | collective-permute-start | bytes 122888 | tf_op jit(solution)/shard_map/ppermute | solution.py:32
  61.3 8.1 %collective-permute-start.20 = (bf16[80,256]{1,0:T(8,128)(2,1)S(1)}, bf16[80,256]{1,0:T(8,128)(2,1)S(1)}, u32[]{:S(2)}, u32[]{:S(2)}) collective-permute-start(bf16[80,256]{1,0:T(8,128)(2,1)S(1)} %get-tuple-element.109), channel_id=1, source_target_pairs={{20,0},{21,1},{22,2},{23,3},{24,4},{25,5},{26,6},{27,7},{28,8},{29... | collective-permute-start | bytes 122888 | tf_op jit(solution)/shard_map/ppermute | solution.py:32
  62.9 7.3 %collective-permute-start.21 = (bf16[80,256]{1,0:T(8,128)(2,1)S(1)}, bf16[80,256]{1,0:T(8,128)(2,1)S(1)}, u32[]{:S(2)}, u32[]{:S(2)}) collective-permute-start(bf16[80,256]{1,0:T(8,128)(2,1)S(1)} %get-tuple-element.110), channel_id=1, source_target_pairs={{16,0},{17,1},{18,2},{19,3},{20,4},{21,5},{22,6},{23,7},{24,8},{25... | collective-permute-start | bytes 122888 | tf_op jit(solution)/shard_map/ppermute | solution.py:32
  65.4 4.9 %collective-permute-start.22 = (bf16[80,256]{1,0:T(8,128)(2,1)S(1)}, bf16[80,256]{1,0:T(8,128)(2,1)S(1)}, u32[]{:S(2)}, u32[]{:S(2)}) collective-permute-start(bf16[80,256]{1,0:T(8,128)(2,1)S(1)} %get-tuple-element.111), channel_id=1, source_target_pairs={{12,0},{13,1},{14,2},{15,3},{16,4},{17,5},{18,6},{19,7},{20,8},{21... | collective-permute-start | bytes 122888 | tf_op jit(solution)/shard_map/ppermute | solution.py:32
  66.4 4.7 %collective-permute-start.23 = (bf16[80,256]{1,0:T(8,128)(2,1)S(1)}, bf16[80,256]{1,0:T(8,128)(2,1)S(1)}, u32[]{:S(2)}, u32[]{:S(2)}) collective-permute-start(bf16[80,256]{1,0:T(8,128)(2,1)S(1)} %get-tuple-element.112), channel_id=1, source_target_pairs={{8,0},{9,1},{10,2},{11,3},{12,4},{13,5},{14,6},{15,7},{16,8},{17,9... | collective-permute-start | bytes 122888 | tf_op jit(solution)/shard_map/ppermute | solution.py:32
  68.0 3.1 %collective-permute-start.24 = (bf16[80,256]{1,0:T(8,128)(2,1)S(1)}, bf16[80,256]{1,0:T(8,128)(2,1)S(1)}, u32[]{:S(2)}, u32[]{:S(2)}) collective-permute-start(bf16[80,256]{1,0:T(8,128)(2,1)S(1)} %get-tuple-element.113), channel_id=1, source_target_pairs={{4,0},{5,1},{6,2},{7,3},{8,4},{9,5},{10,6},{11,7},{12,8},{13,9},{1... | collective-permute-start | bytes 122888 | tf_op jit(solution)/shard_map/ppermute | solution.py:32
  71.1 5.0 %copy-start.1 = (bf16[2304,3072]{1,0:T(8,128)(2,1)S(1)}, bf16[2304,3072]{1,0:T(8,128)(2,1)}, u32[]{:S(2)}) copy-start(bf16[2304,3072]{1,0:T(8,128)(2,1)} %copy-done) | copy-start | bytes 42467332
  76.1 2.8 %copy-start.4 = (f32[4,128,3072]{2,1,0:T(8,128)S(1)}, f32[4,128,3072]{2,1,0:T(8,128)}, u32[]{:S(2)}) copy-start(f32[4,128,3072]{2,1,0:T(8,128)} %copy-done.3) | copy-start | bytes 18874372
  78.9 7.9 %copy-start.2 = (bf16[2304,3072]{1,0:T(8,128)(2,1)S(1)}, bf16[2304,3072]{1,0:T(8,128)(2,1)}, u32[]{:S(2)}) copy-start(bf16[2304,3072]{1,0:T(8,128)(2,1)} %copy-done) | copy-start | bytes 42467332
  83.3 7.5 %collective-permute-start.25 = (bf16[3,128,256]{2,1,0:T(8,128)(2,1)S(1)}, bf16[3,128,256]{2,1,0:T(8,128)(2,1)S(1)}, u32[]{:S(2)}, u32[]{:S(2)}) collective-permute-start(bf16[3,128,256]{2,1,0:T(8,128)(2,1)S(1)} %get-tuple-element.118), channel_id=1, source_target_pairs={{28,0},{29,1},{30,2},{31,3},{0,4},{1,5},{2,6},{3,7},{4,8},{5,9},{6... | collective-permute-start | bytes 589832 | tf_op jit(solution)/shard_map/ppermute | solution.py:32
  84.1 6.7 %collective-permute-start.26 = (bf16[3,128,256]{2,1,0:T(8,128)(2,1)S(1)}, bf16[3,128,256]{2,1,0:T(8,128)(2,1)S(1)}, u32[]{:S(2)}, u32[]{:S(2)}) collective-permute-start(bf16[3,128,256]{2,1,0:T(8,128)(2,1)S(1)} %get-tuple-element.119), channel_id=1, source_target_pairs={{4,0},{5,1},{6,2},{7,3},{8,4},{9,5},{10,6},{11,7},{12,8},{13,9},{1... | collective-permute-start | bytes 589832 | tf_op jit(solution)/shard_map/ppermute | solution.py:32
  90.8 5.7 %collective-permute-start.27 = (bf16[128,256]{1,0:T(8,128)(2,1)S(1)}, bf16[128,256]{1,0:T(8,128)(2,1)S(1)}, u32[]{:S(2)}, u32[]{:S(2)}) collective-permute-start(bf16[128,256]{1,0:T(8,128)(2,1)S(1)} %get-tuple-element.127), channel_id=1, source_target_pairs={{3,0},{0,1},{1,2},{2,3},{7,4},{4,5},{5,6},{6,7},{11,8},{8,9},{9,10... | collective-permute-start | bytes 196616 | tf_op jit(solution)/shard_map/ppermute | solution.py:32
  90.9 7.2 %collective-permute-start.28 = (bf16[128,256]{1,0:T(8,128)(2,1)S(1)}, bf16[128,256]{1,0:T(8,128)(2,1)S(1)}, u32[]{:S(2)}, u32[]{:S(2)}) collective-permute-start(bf16[128,256]{1,0:T(8,128)(2,1)S(1)} %get-tuple-element.126), channel_id=1, source_target_pairs={{1,0},{2,1},{3,2},{0,3},{5,4},{6,5},{7,6},{4,7},{9,8},{10,9},{11,1... | collective-permute-start | bytes 196616 | tf_op jit(solution)/shard_map/ppermute | solution.py:32
  99.6 2.2 %collective-permute-start.30 = (f32[3,8,256]{2,1,0:T(8,128)S(1)}, f32[3,8,256]{2,1,0:T(8,128)S(1)}, u32[]{:S(2)}, u32[]{:S(2)}) collective-permute-start(f32[3,8,256]{2,1,0:T(8,128)S(1)} %get-tuple-element.122), channel_id=1, source_target_pairs={{4,0},{5,1},{6,2},{7,3},{8,4},{9,5},{10,6},{11,7},{12,8},{13,9},{1... | collective-permute-start | bytes 73736 | tf_op jit(solution)/shard_map/ppermute | solution.py:32
  100.3 5.0 %collective-permute-start.29 = (f32[3,8,256]{2,1,0:T(8,128)S(1)}, f32[3,8,256]{2,1,0:T(8,128)S(1)}, u32[]{:S(2)}, u32[]{:S(2)}) collective-permute-start(f32[3,8,256]{2,1,0:T(8,128)S(1)} %get-tuple-element.121), channel_id=1, source_target_pairs={{28,0},{29,1},{30,2},{31,3},{0,4},{1,5},{2,6},{3,7},{4,8},{5,9},{6... | collective-permute-start | bytes 73736 | tf_op jit(solution)/shard_map/ppermute | solution.py:32
  105.4 3.7 %collective-permute-start.32 = (f32[8,256]{1,0:T(8,128)S(1)}, f32[8,256]{1,0:T(8,128)S(1)}, u32[]{:S(2)}, u32[]{:S(2)}) collective-permute-start(f32[8,256]{1,0:T(8,128)S(1)} %get-tuple-element.129), channel_id=1, source_target_pairs={{1,0},{2,1},{3,2},{0,3},{5,4},{6,5},{7,6},{4,7},{9,8},{10,9},{11,1... | collective-permute-start | bytes 24584 | tf_op jit(solution)/shard_map/ppermute | solution.py:32
  107.2 4.5 %collective-permute-start.31 = (f32[8,256]{1,0:T(8,128)S(1)}, f32[8,256]{1,0:T(8,128)S(1)}, u32[]{:S(2)}, u32[]{:S(2)}) collective-permute-start(f32[8,256]{1,0:T(8,128)S(1)} %get-tuple-element.130), channel_id=1, source_target_pairs={{3,0},{0,1},{1,2},{2,3},{7,4},{4,5},{5,6},{6,7},{11,8},{8,9},{9,10... | collective-permute-start | bytes 24584 | tf_op jit(solution)/shard_map/ppermute | solution.py:32

commit v6 on v5

--- a/solution.py
+++ b/solution.py
@@ -235,6 +235,15 @@
         hot_ref[:, lanes] = hot_columns(ids_ref[:, lanes], hot_ref.shape[0])
 
 
+def hot_back_kernel(ids_ref, hot_ref):
+    edges = ids_ref.shape[1]
+    entry = lax.broadcasted_iota(jnp.int32, (128, hot_ref.shape[1]), 1).astype(F32)
+    for start in range(0, edges, 128):
+        row = jnp.broadcast_to(ids_ref[:, start : start + 128].astype(F32), (8, 128))
+        column = row.T[:, 0:1]
+        hot_ref[start : start + 128] = jnp.where(column == entry, 1.0, 0.0).astype(BF16)
+
+
 def unfold_block(block, atoms):
     parts = atoms // 128
     return jnp.concatenate([block[4 * s : 4 * s + 4] for s in range(parts)], axis=1)
@@ -248,25 +257,27 @@
     frame = [before_ref, column_ref, after_ref]
     own = unfold_block(column_ref[1], atoms)
     own = jnp.concatenate([own, jnp.zeros_like(own)], axis=0)
-    halves = []
+    per_cell = atoms // 128
+    places = lax.broadcasted_iota(jnp.int32, (4 * per_cell, 128), 0)
+    upper = places >> 2
+    kind_of_row = places & 3
+    rows = []
     for a, b in OFFSETS:
-        block = frame[a + 1][b + 1]
-        for s in range(atoms // 128):
-            rows = block[4 * s : 4 * s + 4]
-            halves.append(
-                jnp.concatenate(
-                    [rows[0:1] + a * cell_width, rows[1:2] + b * cell_width, rows[2:4], rows],
-                    axis=0,
-                )
-            )
+        move = jnp.where(kind_of_row == 0, a * cell_width, 0.0)
+        move = move + jnp.where(kind_of_row == 1, b * cell_width, 0.0)
+        rows.append(frame[a + 1][b + 1] + move)
     pieces = []
     for start in range(0, ids.shape[1], 128):
-        part = jnp.broadcast_to(ids[:, start : start + 128], (8, 128))
-        lane, half = part & 127, part >> 7
-        found = jnp.zeros((8, 128), F32)
-        for h, rows in enumerate(halves):
-            found = jnp.where(half == h, jnp.take_along_axis(rows, lane, axis=1), found)
-        pieces.append(found)
+        part = jnp.broadcast_to(ids[:, start : start + 128], places.shape)
+        lane, half = part & 127, (part >> 7) - upper
+        found = jnp.zeros(places.shape, F32)
+        for cell, block in enumerate(rows):
+            value = jnp.take_along_axis(block, lane, axis=1)
+            found = jnp.where(half == per_cell * cell, value, found)
+        total = found[:4]
+        for s in range(1, per_cell):
+            total = total + found[4 * s : 4 * s + 4]
+        pieces.append(jnp.concatenate([total, total], axis=0))
     found = jnp.concatenate(pieces, axis=1)
     relative = found - jnp.concatenate([own] * slots, axis=1)
     rel = [relative[i : i + 1] for i in range(3)]
@@ -419,15 +430,13 @@
     for side, out_ref in ((0, before_ref), (2, after_ref)):
         for b in range(3):
             start = (3 * side + b) * atoms
-            hot = hot_ref[start : start + atoms]
-            out_ref[b] = dot(term_ref[...], hot, ((1,), (1,))).astype(BF16)
+            out_ref[b] = dot(term_ref[...], hot_ref[:, start : start + atoms]).astype(BF16)
 
 
 def second_middle_kernel(hot_ref, term_ref, cotangent_ref, middle_ref):
     atoms = cotangent_ref.shape[1]
     for b in range(3):
-        hot = hot_ref[(3 + b) * atoms : (4 + b) * atoms]
-        grad = dot(term_ref[...], hot, ((1,), (1,)))
+        grad = dot(term_ref[...], hot_ref[:, (3 + b) * atoms : (4 + b) * atoms])
         middle_ref[b] = grad + cotangent_ref[...] if b == 1 else grad
 
 
@@ -581,7 +590,10 @@
 
 def structure_kernel(share, padded, grid, wide, place_ref, *refs):
     grid_x, grid_y = grid
-    blocks, (ca_ref, sa_ref, cb_ref, sb_ref, own_ref, out_ref) = refs[:grid_x], refs[grid_x:]
+    blocks, (ca_ref, sa_ref, cb_ref, sb_ref, high_ref, low_ref, own_ref, out_ref) = (
+        refs[:grid_x],
+        refs[grid_x:],
+    )
     col = place_ref[1].astype(F32) * (1.0 / grid_y)
     kx, ky, _ = pair_vectors(count_up(padded), share, place_ref[0])
     kz = count_up(8) + 1.0
@@ -604,6 +616,8 @@
         sb_ref[:, lanes] = sb
         cc, ss, sc, cs = basis_rows(share, ca, sa, cb, sb)
         high, low = split(jnp.concatenate(cc + ss + sc + cs + [ca, sa], axis=0))
+        high_ref[:, lanes] = high
+        low_ref[:, lanes] = low
         term = dot(high, charge, ((1,), (1,))) + dot(low, charge, ((1,), (1,)))
         total = term if total is None else total + term
     packed = pack_rows(total)
@@ -611,8 +625,8 @@
     out_ref[...] = packed.astype(BF16)
 
 
-def fold_kernel(share, padded, grid, wide, place_ref, ca_ref, sa_ref, cb_ref, sb_ref, weight_ref,
-                *refs):
+def fold_kernel(share, padded, grid, wide, place_ref, ca_ref, sa_ref, cb_ref, sb_ref, high_ref,
+                low_ref, weight_ref, *refs):
     grid_x, grid_y = grid
     blocks, parts, outs = refs[:grid_x], refs[grid_x : grid_x + grid_y], refs[grid_x + grid_y :]
     turn = 2.0 * math.pi
@@ -652,7 +666,7 @@
         lanes = pl.ds(d * atoms, atoms)
         ca, sa, cb, sb = ca_ref[:, lanes], sa_ref[:, lanes], cb_ref[:, lanes], sb_ref[:, lanes]
         bcc, bss, bsc, bcs = basis_rows(share, ca, sa, cb, sb)
-        high, low = split(jnp.concatenate(bcc + bss + bsc + bcs + [ca, sa], axis=0))
+        high, low = high_ref[:, lanes], low_ref[:, lanes]
         both = dot(t_both, high)
         pot = both[:wide] + both[wide:] + dot(t_high, low)
         proj = dot(row_pair, jnp.concatenate([charge, charge], axis=0))
@@ -747,7 +761,7 @@
         hbm=5,
         name="prep_first",
     )
-    cells, ids = around(own, ids)
+    cells, (ids, place) = around(own, (ids, place))
     (hot,) = run(
         hot_kernel, [shape(9 * atoms, edges, dtype=BF16)], [ids], flops=2_000_000_000, name="hot"
     )
@@ -818,6 +832,14 @@
         name="second",
     )
     charges = [packed] + [shifted(packed, d, 0) for d in range(1, grid_x)]
+    (hot_back,) = run(
+        hot_back_kernel,
+        [shape(edges, 9 * atoms, dtype=BF16)],
+        [ids],
+        flops=2_000_000_000,
+        name="hot_back",
+    )
+    charges, hot_back = lax.optimization_barrier((charges, hot_back))
     span = grid_x * atoms
     rows = 32 * share + 2 * padded
     *phases, own_part, part = run(
@@ -827,6 +849,8 @@
             shape(padded, span),
             shape(8, span),
             shape(8, span),
+            shape(rows, span, dtype=BF16),
+            shape(rows, span, dtype=BF16),
             shape(rows // 2, 2 * lat_width),
             shape(rows // 2, 2 * lat_width, dtype=BF16),
         ],
@@ -855,7 +879,7 @@
             shape(3, features, atoms, dtype=BF16),
             shape(3, features, atoms, dtype=BF16),
         ],
-        [hot, edge_weights, turn_high, turn_low, charge_pair, sums_two, gate_two, charge, energy,
+        [hot_back, edge_weights, turn_high, turn_low, charge_pair, sums_two, gate_two, charge, energy,
          energy_slope] + folds,
         name="second_back",
     )
@@ -863,7 +887,7 @@
     (middle,) = run(
         second_middle_kernel,
         [shape(3, features, atoms)],
-        [hot, term, cotangent],
+        [hot_back, term, cotangent],
         flops=1_000_000_000,
         name="second_middle",
     )

time: 113 us -> 103 us (0.912)
  local copies, waits for them, and re-layouts: 12.2 us -> 4.35 us
  waiting for transfers between devices: 35.2 us -> 31.5 us
  starting transfers between devices: 36.3 us -> 37.5 us
    unnamed x29 -> x19, local copies, waits for them, and re-layouts: 12.2 us -> 4.35 us
    ppermute x33, waiting for transfers between devices: 35.2 us -> 31.5 us  [shifted(): return lax.ppermute(block, ('gx', 'gy'), route)]
    ppermute x33, starting transfers between devices: 36.3 us -> 37.5 us  [shifted(): return lax.ppermute(block, ('gx', 'gy'), route)]
    pallas_call x15 -> x16, Pallas kernels: 26.9 us -> 27.4 us  [run(): pl.pallas_call(kernel, out_shape=outs, in_specs=specs, out_specs=[whole()...]
  transfers between devices with their start and end apart: 33 -> 33, of which waited for: 22 -> 22; matrix products, arithmetic and copies ran while one was open for 0% -> 0% of each run, Pallas kernels for 9% -> 12%
where the time goes in v6:
time: 103 us; the launch traced here: 102 us
  starting transfers between devices  37.5 us (36%)
  waiting for transfers between devices  31.5 us (31%)
  Pallas kernels  27.4 us (27%)
  local copies, waits for them, and re-layouts  4.35 us (4%)
    ppermute x33, starting transfers between devices, shifted(): return lax.ppermute(block, ('gx', 'gy'), route)  37.5 us
    ppermute x33, waiting for transfers between devices, shifted(): return lax.ppermute(block, ('gx', 'gy'), route)  31.5 us
    pallas_call x16, Pallas kernels, run(): pl.pallas_call(kernel, out_shape=outs, in_specs=specs, out_specs=[whole()...  27.4 us
    unnamed x19, local copies, waits for them, and re-layouts  4.35 us
  transfers between devices with their start and end apart: 33, of which 22 were waited for; matrix products, arithmetic and copies ran while one was open for 0% of the time, Pallas kernels for 12%

profile of v6, /device:TPU:0, one launch (start us, length us, event | category | flops | bytes accessed | tf_op | source)
XLA Modules:
  0.0 102.5 jit_solution(161984429771697983)
XLA Ops:
  0.6 1.3 %pack.1 = f32[8,128]{1,0:T(8,128)} custom-call(f32[1,3,1,256]{3,2,1,0:T(1,128)} %bitcast.35, s32[1,1,256]{2,1,0:T(1,128)} %species_ref.1), custom_call_target="tpu_custom_call" | custom-call | flops 10000000 | bytes 1000000 | tf_op jit(solution)/shard_map/pack/pallas_call | solution.py:49
  1.9 3.9 %collective-permute-start.1 = (f32[8,128]{1,0:T(8,128)}, f32[8,128]{1,0:T(8,128)S(1)}, u32[]{:S(2)}, u32[]{:S(2)}) collective-permute-start(f32[8,128]{1,0:T(8,128)} %pack.1), channel_id=1, source_target_pairs={{1,0},{2,1},{3,2},{0,3},{5,4},{6,5},{7,6},{4,7},{9,8},{10,9},{11,1... | collective-permute-start | bytes 12296 | tf_op jit(solution)/shard_map/ppermute | solution.py:32
  6.0 0.9 copy-done
  6.9 0.7 copy-done.4
  7.6 0.7 copy-done.5
  8.4 0.7 copy-done.6
  9.0 0.7 copy-done.7
  9.7 0.3 prep_first.1
  10.0 0.6 collective-permute-done
  10.6 0.7 pad_maximum_fusion.1.column_ref.cell_ref
  11.3 3.5 %collective-permute-start.3 = (f32[3,8,128]{2,1,0:T(8,128)S(1)}, f32[3,8,128]{2,1,0:T(8,128)S(1)}, u32[]{:S(2)}, u32[]{:S(2)}) collective-permute-start(f32[3,8,128]{2,1,0:T(8,128)S(1)} %pad_maximum_fusion.1.column_ref.cell_ref), channel_id=1, source_target_pairs={{4,0},{5,1},{6,2},{7,3},{8,4},{9,5},{10,6},{11,7},{12,8},{13,9},{1... | collective-permute-start | bytes 36872 | tf_op jit(solution)/shard_map/ppermute | solution.py:32
  14.8 1.4 %collective-permute-done.2.before_ref = f32[3,8,128]{2,1,0:T(8,128)S(1)} collective-permute-done((f32[3,8,128]{2,1,0:T(8,128)S(1)}, f32[3,8,128]{2,1,0:T(8,128)S(1)}, u32[]{:S(2)}, u32[]{:S(2)}) %collective-permute-start.2) | collective-permute-done | bytes 12320 | tf_op jit(solution)/shard_map/ppermute | solution.py:32
  16.2 1.3 %first.1 = (bf16[128,256]{1,0:T(8,128)(2,1)S(1)}, f32[8,3072]{1,0:T(8,128)S(1)}, f32[8,3072]{1,0:T(8,128)S(1)}, f32[8,3072]{1,0:T(8,128)S(1)}, f32[3,128,256]{2,1,0:T(8,128)S(1)}, /*index=5*/f32[128,256]{1,0:T(8,128)S(1)}) custom-call(s32[1,3072]{1,0:T(1,128)S(1)} %get-tuple-element.76.ids_ref, s32[1,1,256]{2,1,0:T(1,128)S(1)} %get-tuple-element.77.count_ref, ...), custom_call_target="tpu_custom_call" | custom-call | flops 10000000 | bytes 1000000 | tf_op jit(solution)/shard_map/first/pallas_call | solution.py:49
  17.6 2.4 %collective-permute-start.5 = (bf16[128,256]{1,0:T(8,128)(2,1)S(1)}, bf16[128,256]{1,0:T(8,128)(2,1)S(1)}, u32[]{:S(2)}, u32[]{:S(2)}) collective-permute-start(bf16[128,256]{1,0:T(8,128)(2,1)S(1)} %get-tuple-element.93), channel_id=1, source_target_pairs={{1,0},{2,1},{3,2},{0,3},{5,4},{6,5},{7,6},{4,7},{9,8},{10,9},{11,1... | collective-permute-start | bytes 196616 | tf_op jit(solution)/shard_map/ppermute | solution.py:32
  20.0 3.2 %hot.1.hot_ref = bf16[2304,3072]{1,0:T(8,128)(2,1)S(1)} custom-call(s32[1,3072]{1,0:T(1,128)S(1)} %get-tuple-element.76.ids_ref), custom_call_target="tpu_custom_call" | custom-call | flops 2000000000 | bytes 1000000 | tf_op jit(solution)/shard_map/hot/pallas_call | solution.py:49
  23.3 1.9 %collective-permute-done.4 = bf16[128,256]{1,0:T(8,128)(2,1)S(1)} collective-permute-done((bf16[128,256]{1,0:T(8,128)(2,1)S(1)}, bf16[128,256]{1,0:T(8,128)(2,1)S(1)}, u32[]{:S(2)}, u32[]{:S(2)}) %collective-permute-start.4) | collective-permute-done | bytes 65568 | tf_op jit(solution)/shard_map/ppermute | solution.py:32
  25.2 2.1 %collective-permute-start.6 = (bf16[3,128,256]{2,1,0:T(8,128)(2,1)S(1)}, bf16[3,128,256]{2,1,0:T(8,128)(2,1)S(1)}, u32[]{:S(2)}, u32[]{:S(2)}) collective-permute-start(bf16[3,128,256]{2,1,0:T(8,128)(2,1)S(1)} %pad_maximum_fusion.column_ref), channel_id=1, source_target_pairs={{4,0},{5,1},{6,2},{7,3},{8,4},{9,5},{10,6},{11,7},{12,8},{13,9},{1... | collective-permute-start | bytes 589832 | tf_op jit(solution)/shard_map/ppermute | solution.py:32
  27.4 0.3 prep_second.1
  27.7 1.6 %second_near.1 = (f32[4,128,3072]{2,1,0:T(8,128)S(1)}, f32[128,3072]{1,0:T(8,128)S(1)}) custom-call(f32[8,3072]{1,0:T(8,128)S(1)} %get-tuple-element.83.basis_ref, f32[8,3072]{1,0:T(8,128)S(1)} %get-tuple-element.85.unit_ref, bf16[2,128,32]{2,1,0:T(8,128)(2,1)S(1)} %get-tuple-element.95.left_ref, bf16[2304,3072]{1,0:T(8,128)(2,1)S(1)} %hot.1.hot_ref, ...), custom_call_target="tpu_custom_call" | custom-call | flops 2000000000 | bytes 1000000 | tf_op jit(solution)/shard_map/second_near/pallas_call | solution.py:49
  29.3 1.4 %collective-permute-done.6.after_ref = bf16[3,128,256]{2,1,0:T(8,128)(2,1)S(1)} collective-permute-done((bf16[3,128,256]{2,1,0:T(8,128)(2,1)S(1)}, bf16[3,128,256]{2,1,0:T(8,128)(2,1)S(1)}, u32[]{:S(2)}, u32[]{:S(2)}) %collective-permute-start.6) | collective-permute-done | bytes 196640 | tf_op jit(solution)/shard_map/ppermute | solution.py:32
  30.7 0.8 second_side.1.near_ref
  31.6 3.0 %collective-permute-done.7.before_ref = bf16[3,128,256]{2,1,0:T(8,128)(2,1)S(1)} collective-permute-done((bf16[3,128,256]{2,1,0:T(8,128)(2,1)S(1)}, bf16[3,128,256]{2,1,0:T(8,128)(2,1)S(1)}, u32[]{:S(2)}, u32[]{:S(2)}) %collective-permute-start.7) | collective-permute-done | bytes 196640 | tf_op jit(solution)/shard_map/ppermute | solution.py:32
  34.6 2.2 %second.1 = (bf16[128,3072]{1,0:T(8,128)(2,1)S(1)}, f32[3,128,256]{2,1,0:T(8,128)S(1)}, f32[128,256]{1,0:T(8,128)S(1)}, bf16[80,256]{1,0:T(8,128)(2,1)S(1)}, f32...) custom-call(bf16[2304,3072]{1,0:T(8,128)(2,1)S(1)} %hot.1.hot_ref, ...), custom_call_target="tpu_custom_call" | custom-call | flops 10000000 | bytes 1000000 | tf_op jit(solution)/shard_map/second/pallas_call | solution.py:49
  36.8 0.9 collective-permute-start.8
  37.7 2.7 %collective-permute-start.11 = (bf16[80,256]{1,0:T(8,128)(2,1)S(1)}, bf16[80,256]{1,0:T(8,128)(2,1)S(1)}, u32[]{:S(2)}, u32[]{:S(2)}) collective-permute-start(bf16[80,256]{1,0:T(8,128)(2,1)S(1)} %get-tuple-element.114.refs_0_), channel_id=1, source_target_pairs={{16,0},{17,1},{18,2},{19,3},{20,4},{21,5},{22,6},{23,7},{24,8},{25... | collective-permute-start | bytes 122888 | tf_op jit(solution)/shard_map/ppermute | solution.py:32
  40.4 1.2 %collective-permute-start.13 = (bf16[80,256]{1,0:T(8,128)(2,1)S(1)}, bf16[80,256]{1,0:T(8,128)(2,1)S(1)}, u32[]{:S(2)}, u32[]{:S(2)}) collective-permute-start(bf16[80,256]{1,0:T(8,128)(2,1)S(1)} %get-tuple-element.114.refs_0_), channel_id=1, source_target_pairs={{24,0},{25,1},{26,2},{27,3},{28,4},{29,5},{30,6},{31,7},{0,8},{1,9... | collective-permute-start | bytes 122888 | tf_op jit(solution)/shard_map/ppermute | solution.py:32
  41.7 0.8 collective-permute-start.14
  42.5 2.8 %hot_back.1.hot_ref = bf16[3072,2304]{1,0:T(8,128)(2,1)S(1)} custom-call(s32[1,3072]{1,0:T(1,128)S(1)} %get-tuple-element.76.ids_ref), custom_call_target="tpu_custom_call" | custom-call | flops 2000000000 | bytes 1000000 | tf_op jit(solution)/shard_map/hot_back/pallas_call | solution.py:49
  45.3 2.3 %collective-permute-done.12.refs_5_ = bf16[80,256]{1,0:T(8,128)(2,1)S(1)} collective-permute-done((bf16[80,256]{1,0:T(8,128)(2,1)S(1)}, bf16[80,256]{1,0:T(8,128)(2,1)S(1)}, u32[]{:S(2)}, u32[]{:S(2)}) %collective-permute-start.12) | collective-permute-done | bytes 40992 | tf_op jit(solution)/shard_map/ppermute | solution.py:32
  47.6 2.8 %structure.1 = (f32[32,2048]{1,0:T(8,128)S(1)}, f32[32,2048]{1,0:T(8,128)S(1)}, f32[8,2048]{1,0:T(8,128)S(1)}, f32[8,2048]{1,0:T(8,128)S(1)}, bf16[640,2048]{1,0...) custom-call(s32[2]{0:T(128)S(1)} %pad_add_fusion.place_ref, ...), custom_call_target="tpu_custom_call" | custom-call | flops 10000000 | bytes 1000000 | tf_op jit(solution)/shard_map/structure/pallas_call | solution.py:49
  50.4 1.7 %collective-permute-start.15 = (bf16[320,128]{1,0:T(8,128)(2,1)S(1)}, bf16[320,128]{1,0:T(8,128)(2,1)S(1)}, u32[]{:S(2)}, u32[]{:S(2)}) collective-permute-start(bf16[320,128]{1,0:T(8,128)(2,1)S(1)} %get-tuple-element.129), channel_id=1, source_target_pairs={{1,0},{2,1},{3,2},{0,3},{5,4},{6,5},{7,6},{4,7},{9,8},{10,9},{11,1... | collective-permute-start | bytes 245768 | tf_op jit(solution)/shard_map/ppermute | solution.py:32
  52.1 0.5 collective-permute-start.16
  52.6 0.4 collective-permute-start.17
  53.0 1.3 %green.1.weight_ref = f32[320,128]{1,0:T(8,128)S(1)} custom-call(s32[2]{0:T(128)S(1)} %pad_add_fusion.place_ref, s32[3,4096]{1,0:T(4,128)S(1)} %copy-done.1), custom_call_target="tpu_custom_call" | custom-call | flops 10000000 | bytes 1000000 | tf_op jit(solution)/shard_map/green/pallas_call | solution.py:49
  54.3 1.2 %collective-permute-done.15.refs_9_ = bf16[320,128]{1,0:T(8,128)(2,1)S(1)} collective-permute-done((bf16[320,128]{1,0:T(8,128)(2,1)S(1)}, bf16[320,128]{1,0:T(8,128)(2,1)S(1)}, u32[]{:S(2)}, u32[]{:S(2)}) %collective-permute-start.15) | collective-permute-done | bytes 81952 | tf_op jit(solution)/shard_map/ppermute | solution.py:32
  55.5 1.1 %collective-permute-done.16.refs_10_ = bf16[320,128]{1,0:T(8,128)(2,1)S(1)} collective-permute-done((bf16[320,128]{1,0:T(8,128)(2,1)S(1)}, bf16[320,128]{1,0:T(8,128)(2,1)S(1)}, u32[]{:S(2)}, u32[]{:S(2)}) %collective-permute-start.16) | collective-permute-done | bytes 81952 | tf_op jit(solution)/shard_map/ppermute | solution.py:32
  56.6 1.4 %collective-permute-done.17.refs_11_ = bf16[320,128]{1,0:T(8,128)(2,1)S(1)} collective-permute-done((bf16[320,128]{1,0:T(8,128)(2,1)S(1)}, bf16[320,128]{1,0:T(8,128)(2,1)S(1)}, u32[]{:S(2)}, u32[]{:S(2)}) %collective-permute-start.17) | collective-permute-done | bytes 81952 | tf_op jit(solution)/shard_map/ppermute | solution.py:32
  57.9 2.9 %fold.1 = (f32[80,256]{1,0:T(8,128)S(1)}, bf16[80,256]{1,0:T(8,128)(2,1)S(1)}, bf16[80,256]{1,0:T(8,128)(2,1)S(1)}, bf16[80,256]{1,0:T(8,128)(2,1)S(1)}, bf16[80...) custom-call(s32[2]{0:T(128)S(1)} %pad_add_fusion.place_ref, ...), custom_call_target="tpu_custom_call" | custom-call | flops 10000000 | bytes 1000000 | tf_op jit(solution)/shard_map/fold/pallas_call | solution.py:49
  60.9 0.3 collective-permute-start.19
  61.3 1.6 %collective-permute-start.20 = (bf16[80,256]{1,0:T(8,128)(2,1)S(1)}, bf16[80,256]{1,0:T(8,128)(2,1)S(1)}, u32[]{:S(2)}, u32[]{:S(2)}) collective-permute-start(bf16[80,256]{1,0:T(8,128)(2,1)S(1)} %get-tuple-element.133), channel_id=1, source_target_pairs={{20,0},{21,1},{22,2},{23,3},{24,4},{25,5},{26,6},{27,7},{28,8},{29... | collective-permute-start | bytes 122888 | tf_op jit(solution)/shard_map/ppermute | solution.py:32
  62.8 2.2 %collective-permute-start.21 = (bf16[80,256]{1,0:T(8,128)(2,1)S(1)}, bf16[80,256]{1,0:T(8,128)(2,1)S(1)}, u32[]{:S(2)}, u32[]{:S(2)}) collective-permute-start(bf16[80,256]{1,0:T(8,128)(2,1)S(1)} %get-tuple-element.134), channel_id=1, source_target_pairs={{16,0},{17,1},{18,2},{19,3},{20,4},{21,5},{22,6},{23,7},{24,8},{25... | collective-permute-start | bytes 122888 | tf_op jit(solution)/shard_map/ppermute | solution.py:32
  65.3 0.9 collective-permute-done.18.refs_1_
  66.2 1.6 %collective-permute-start.23 = (bf16[80,256]{1,0:T(8,128)(2,1)S(1)}, bf16[80,256]{1,0:T(8,128)(2,1)S(1)}, u32[]{:S(2)}, u32[]{:S(2)}) collective-permute-start(bf16[80,256]{1,0:T(8,128)(2,1)S(1)} %get-tuple-element.136), channel_id=1, source_target_pairs={{8,0},{9,1},{10,2},{11,3},{12,4},{13,5},{14,6},{15,7},{16,8},{17,9... | collective-permute-start | bytes 122888 | tf_op jit(solution)/shard_map/ppermute | solution.py:32
  67.7 1.1 %collective-permute-start.24 = (bf16[80,256]{1,0:T(8,128)(2,1)S(1)}, bf16[80,256]{1,0:T(8,128)(2,1)S(1)}, u32[]{:S(2)}, u32[]{:S(2)}) collective-permute-start(bf16[80,256]{1,0:T(8,128)(2,1)S(1)} %get-tuple-element.137), channel_id=1, source_target_pairs={{4,0},{5,1},{6,2},{7,3},{8,4},{9,5},{10,6},{11,7},{12,8},{13,9},{1... | collective-permute-start | bytes 122888 | tf_op jit(solution)/shard_map/ppermute | solution.py:32
  68.8 0.3 collective-permute-done.20.refs_3_
  69.1 0.9 collective-permute-done.21.refs_4_
  70.0 0.3 collective-permute-done.23.refs_6_
  70.5 2.9 %second_back.1 = (f32[1,1,256]{2,1,0:T(1,128)}, f32[8,256]{1,0:T(8,128)S(1)}, f32[128,256]{1,0:T(8,128)S(1)}, f32[4,128,256]{2,1,0:T(8,128)S(1)}, bf16[128,3072]...) custom-call(bf16[3072,2304]{1,0:T(8,128)(2,1)S(1)} %hot_back.1.hot_ref, ...), custom_call_target="tpu_custom_call" | custom-call | flops 10000000 | bytes 1000000 | tf_op jit(solution)/shard_map/second_back/pallas_call | solution.py:49
  73.4 1.2 %collective-permute-start.25 = (bf16[3,128,256]{2,1,0:T(8,128)(2,1)S(1)}, bf16[3,128,256]{2,1,0:T(8,128)(2,1)S(1)}, u32[]{:S(2)}, u32[]{:S(2)}) collective-permute-start(bf16[3,128,256]{2,1,0:T(8,128)(2,1)S(1)} %get-tuple-element.142), channel_id=1, source_target_pairs={{28,0},{29,1},{30,2},{31,3},{0,4},{1,5},{2,6},{3,7},{4,8},{5,9},{6... | collective-permute-start | bytes 589832 | tf_op jit(solution)/shard_map/ppermute | solution.py:32
  74.6 2.3 %collective-permute-start.26 = (bf16[3,128,256]{2,1,0:T(8,128)(2,1)S(1)}, bf16[3,128,256]{2,1,0:T(8,128)(2,1)S(1)}, u32[]{:S(2)}, u32[]{:S(2)}) collective-permute-start(bf16[3,128,256]{2,1,0:T(8,128)(2,1)S(1)} %get-tuple-element.143), channel_id=1, source_target_pairs={{4,0},{5,1},{6,2},{7,3},{8,4},{9,5},{10,6},{11,7},{12,8},{13,9},{1... | collective-permute-start | bytes 589832 | tf_op jit(solution)/shard_map/ppermute | solution.py:32
  76.9 0.8 second_middle.1.middle_ref
  77.7 2.8 %collective-permute-done.25.refs_0_ = bf16[3,128,256]{2,1,0:T(8,128)(2,1)S(1)} collective-permute-done((bf16[3,128,256]{2,1,0:T(8,128)(2,1)S(1)}, bf16[3,128,256]{2,1,0:T(8,128)(2,1)S(1)}, u32[]{:S(2)}, u32[]{:S(2)}) %collective-permute-start.25) | collective-permute-done | bytes 196640 | tf_op jit(solution)/shard_map/ppermute | solution.py:32
  80.6 2.9 %collective-permute-start.28 = (bf16[128,256]{1,0:T(8,128)(2,1)S(1)}, bf16[128,256]{1,0:T(8,128)(2,1)S(1)}, u32[]{:S(2)}, u32[]{:S(2)}) collective-permute-start(bf16[128,256]{1,0:T(8,128)(2,1)S(1)} %get-tuple-element.150), channel_id=1, source_target_pairs={{1,0},{2,1},{3,2},{0,3},{5,4},{6,5},{7,6},{4,7},{9,8},{10,9},{11,1... | collective-permute-start | bytes 196616 | tf_op jit(solution)/shard_map/ppermute | solution.py:32
  83.5 1.2 %second_edge.1.edge_ref = f32[32,3072]{1,0:T(8,128)S(1)} custom-call(bf16[2,16,256]{2,1,0:T(8,128)(2,1)S(1)} %get-tuple-element.92.back_ref, bf16[128,3072]{1,0:T(8,128)(2,1)S(1)} %get-tuple-element.105.feature_ref, f32[4,128,256]{2,1,0:T(8,128)S(1)} %get-tuple-element.138.grad_ref), custom_call_target="tpu_custom_call" | custom-call | flops 1000000000 | bytes 1000000 | tf_op jit(solution)/shard_map/second_edge/pallas_call | solution.py:49
  84.8 1.0 collective-permute-done.27.refs_2_
  85.8 1.5 %collective-permute-done.28.refs_3_ = bf16[128,256]{1,0:T(8,128)(2,1)S(1)} collective-permute-done((bf16[128,256]{1,0:T(8,128)(2,1)S(1)}, bf16[128,256]{1,0:T(8,128)(2,1)S(1)}, u32[]{:S(2)}, u32[]{:S(2)}) %collective-permute-start.28) | collective-permute-done | bytes 65568 | tf_op jit(solution)/shard_map/ppermute | solution.py:32
  87.2 1.5 %first_back.1 = (f32[3,8,256]{2,1,0:T(8,128)S(1)}, f32[3,8,256]{2,1,0:T(8,128)S(1)}, f32[3,8,256]{2,1,0:T(8,128)S(1)}) custom-call(s32[1,3072]{1,0:T(1,128)S(1)} %get-tuple-element.76.ids_ref, f32[8,3072]{1,0:T(8,128)S(1)} %get-tuple-element.83.basis_ref, f32[8,3072]{1,0:T(8,128)S(1)} %get-tuple-element.84.slope_ref, ...), custom_call_target="tpu_custom_call" | custom-call | flops 10000000 | bytes 1000000 | tf_op jit(solution)/shard_map/first_back/pallas_call | solution.py:49
  88.8 1.6 %collective-permute-start.30 = (f32[3,8,256]{2,1,0:T(8,128)S(1)}, f32[3,8,256]{2,1,0:T(8,128)S(1)}, u32[]{:S(2)}, u32[]{:S(2)}) collective-permute-start(f32[3,8,256]{2,1,0:T(8,128)S(1)} %get-tuple-element.146), channel_id=1, source_target_pairs={{4,0},{5,1},{6,2},{7,3},{8,4},{9,5},{10,6},{11,7},{12,8},{13,9},{1... | collective-permute-start | bytes 73736 | tf_op jit(solution)/shard_map/ppermute | solution.py:32
  90.4 1.6 %collective-permute-done.30 = f32[3,8,256]{2,1,0:T(8,128)S(1)} collective-permute-done((f32[3,8,256]{2,1,0:T(8,128)S(1)}, f32[3,8,256]{2,1,0:T(8,128)S(1)}, u32[]{:S(2)}, u32[]{:S(2)}) %collective-permute-start.30) | collective-permute-done | bytes 24608 | tf_op jit(solution)/shard_map/ppermute | solution.py:32
  92.0 3.5 %collective-permute-done.29 = f32[3,8,256]{2,1,0:T(8,128)S(1)} collective-permute-done((f32[3,8,256]{2,1,0:T(8,128)S(1)}, f32[3,8,256]{2,1,0:T(8,128)S(1)}, u32[]{:S(2)}, u32[]{:S(2)}) %collective-permute-start.29) | collective-permute-done | bytes 24608 | tf_op jit(solution)/shard_map/ppermute | solution.py:32
  95.4 1.9 %collective-permute-start.32 = (f32[8,256]{1,0:T(8,128)S(1)}, f32[8,256]{1,0:T(8,128)S(1)}, u32[]{:S(2)}, u32[]{:S(2)}) collective-permute-start(f32[8,256]{1,0:T(8,128)S(1)} %get-tuple-element.153), channel_id=1, source_target_pairs={{1,0},{2,1},{3,2},{0,3},{5,4},{6,5},{7,6},{4,7},{9,8},{10,9},{11,1... | collective-permute-start | bytes 24584 | tf_op jit(solution)/shard_map/ppermute | solution.py:32
  97.5 1.6 %collective-permute-done.32 = f32[8,256]{1,0:T(8,128)S(1)} collective-permute-done((f32[8,256]{1,0:T(8,128)S(1)}, f32[8,256]{1,0:T(8,128)S(1)}, u32[]{:S(2)}, u32[]{:S(2)}) %collective-permute-start.32) | collective-permute-done | bytes 8224 | tf_op jit(solution)/shard_map/ppermute | solution.py:32
  99.1 2.7 %collective-permute-done.31 = f32[8,256]{1,0:T(8,128)S(1)} collective-permute-done((f32[8,256]{1,0:T(8,128)S(1)}, f32[8,256]{1,0:T(8,128)S(1)}, u32[]{:S(2)}, u32[]{:S(2)}) %collective-permute-start.31) | collective-permute-done | bytes 8224 | tf_op jit(solution)/shard_map/ppermute | solution.py:32
  101.9 0.6 copy.13
  (44 shorter events, 1.0 us)
Async XLA Ops:
  1.9 8.1 %collective-permute-start.1 = (f32[8,128]{1,0:T(8,128)}, f32[8,128]{1,0:T(8,128)S(1)}, u32[]{:S(2)}, u32[]{:S(2)}) collective-permute-start(f32[8,128]{1,0:T(8,128)} %pack.1), channel_id=1, source_target_pairs={{1,0},{2,1},{3,2},{0,3},{5,4},{6,5},{7,6},{4,7},{9,8},{10,9},{11,1... | collective-permute-start | bytes 12296 | tf_op jit(solution)/shard_map/ppermute | solution.py:32
  5.9 4.7 %collective-permute-start = (f32[8,128]{1,0:T(8,128)}, f32[8,128]{1,0:T(8,128)S(1)}, u32[]{:S(2)}, u32[]{:S(2)}) collective-permute-start(f32[8,128]{1,0:T(8,128)} %pack.1), channel_id=1, source_target_pairs={{3,0},{0,1},{1,2},{2,3},{7,4},{4,5},{5,6},{6,7},{11,8},{8,9},{9,10... | collective-permute-start | bytes 12296 | tf_op jit(solution)/shard_map/ppermute | solution.py:32
  6.0 1.0 copy-start
  6.9 0.7 copy-start.4
  7.6 0.7 copy-start.5
  8.3 0.7 copy-start.6
  9.0 0.7 copy-start.7
  11.3 4.9 %collective-permute-start.2 = (f32[3,8,128]{2,1,0:T(8,128)S(1)}, f32[3,8,128]{2,1,0:T(8,128)S(1)}, u32[]{:S(2)}, u32[]{:S(2)}) collective-permute-start(f32[3,8,128]{2,1,0:T(8,128)S(1)} %pad_maximum_fusion.1.column_ref.cell_ref), channel_id=1, source_target_pairs={{28,0},{29,1},{30,2},{31,3},{0,4},{1,5},{2,6},{3,7},{4,8},{5,9},{6... | collective-permute-start | bytes 36872 | tf_op jit(solution)/shard_map/ppermute | solution.py:32
  11.3 4.9 %collective-permute-start.3 = (f32[3,8,128]{2,1,0:T(8,128)S(1)}, f32[3,8,128]{2,1,0:T(8,128)S(1)}, u32[]{:S(2)}, u32[]{:S(2)}) collective-permute-start(f32[3,8,128]{2,1,0:T(8,128)S(1)} %pad_maximum_fusion.1.column_ref.cell_ref), channel_id=1, source_target_pairs={{4,0},{5,1},{6,2},{7,3},{8,4},{9,5},{10,6},{11,7},{12,8},{13,9},{1... | collective-permute-start | bytes 36872 | tf_op jit(solution)/shard_map/ppermute | solution.py:32
  17.6 9.8 %copy-start.2 = (f32[128,128]{1,0:T(8,128)S(1)}, f32[128,128]{1,0:T(8,128)}, u32[]{:S(2)}) copy-start(f32[128,128]{1,0:T(8,128)} %hidden_in.1) | copy-start | bytes 196612
  17.6 9.8 %copy-start.3 = (f32[128,64]{0,1:T(8,128)S(1)}, f32[128,64]{0,1:T(8,128)}, u32[]{:S(2)}) copy-start(f32[128,64]{0,1:T(8,128)} %param.20) | copy-start | bytes 98308
  17.6 9.8 %copy-start.8 = (f32[128]{0:T(128)S(1)}, f32[128]{0:T(128)}, u32[]{:S(2)}) copy-start(f32[128]{0:T(128)} %param.19) | copy-start | bytes 1540
  17.6 5.7 %collective-permute-start.5 = (bf16[128,256]{1,0:T(8,128)(2,1)S(1)}, bf16[128,256]{1,0:T(8,128)(2,1)S(1)}, u32[]{:S(2)}, u32[]{:S(2)}) collective-permute-start(bf16[128,256]{1,0:T(8,128)(2,1)S(1)} %get-tuple-element.93), channel_id=1, source_target_pairs={{1,0},{2,1},{3,2},{0,3},{5,4},{6,5},{7,6},{4,7},{9,8},{10,9},{11,1... | collective-permute-start | bytes 196616 | tf_op jit(solution)/shard_map/ppermute | solution.py:32
  20.0 5.2 %collective-permute-start.4 = (bf16[128,256]{1,0:T(8,128)(2,1)S(1)}, bf16[128,256]{1,0:T(8,128)(2,1)S(1)}, u32[]{:S(2)}, u32[]{:S(2)}) collective-permute-start(bf16[128,256]{1,0:T(8,128)(2,1)S(1)} %get-tuple-element.93), channel_id=1, source_target_pairs={{3,0},{0,1},{1,2},{2,3},{7,4},{4,5},{5,6},{6,7},{11,8},{8,9},{9,10... | collective-permute-start | bytes 196616 | tf_op jit(solution)/shard_map/ppermute | solution.py:32
  25.2 5.5 %collective-permute-start.6 = (bf16[3,128,256]{2,1,0:T(8,128)(2,1)S(1)}, bf16[3,128,256]{2,1,0:T(8,128)(2,1)S(1)}, u32[]{:S(2)}, u32[]{:S(2)}) collective-permute-start(bf16[3,128,256]{2,1,0:T(8,128)(2,1)S(1)} %pad_maximum_fusion.column_ref), channel_id=1, source_target_pairs={{4,0},{5,1},{6,2},{7,3},{8,4},{9,5},{10,6},{11,7},{12,8},{13,9},{1... | collective-permute-start | bytes 589832 | tf_op jit(solution)/shard_map/ppermute | solution.py:32
  27.6 6.9 %collective-permute-start.7 = (bf16[3,128,256]{2,1,0:T(8,128)(2,1)S(1)}, bf16[3,128,256]{2,1,0:T(8,128)(2,1)S(1)}, u32[]{:S(2)}, u32[]{:S(2)}) collective-permute-start(bf16[3,128,256]{2,1,0:T(8,128)(2,1)S(1)} %pad_maximum_fusion.column_ref), channel_id=1, source_target_pairs={{28,0},{29,1},{30,2},{31,3},{0,4},{1,5},{2,6},{3,7},{4,8},{5,9},{6... | collective-permute-start | bytes 589832 | tf_op jit(solution)/shard_map/ppermute | solution.py:32
  36.7 16.2 %copy-start.1 = (s32[3,4096]{1,0:T(4,128)S(1)}, s32[3,4096]{1,0:T(4,128)}, u32[]{:S(2)}) copy-start(s32[3,4096]{1,0:T(4,128)} %vec_ref.1) | copy-start | bytes 147460
  36.8 3.6 %collective-permute-start.8 = (bf16[80,256]{1,0:T(8,128)(2,1)S(1)}, bf16[80,256]{1,0:T(8,128)(2,1)S(1)}, u32[]{:S(2)}, u32[]{:S(2)}) collective-permute-start(bf16[80,256]{1,0:T(8,128)(2,1)S(1)} %get-tuple-element.114.refs_0_), channel_id=1, source_target_pairs={{4,0},{5,1},{6,2},{7,3},{8,4},{9,5},{10,6},{11,7},{12,8},{13,9},{1... | collective-permute-start | bytes 122888 | tf_op jit(solution)/shard_map/ppermute | solution.py:32
  37.7 4.0 %collective-permute-start.9 = (bf16[80,256]{1,0:T(8,128)(2,1)S(1)}, bf16[80,256]{1,0:T(8,128)(2,1)S(1)}, u32[]{:S(2)}, u32[]{:S(2)}) collective-permute-start(bf16[80,256]{1,0:T(8,128)(2,1)S(1)} %get-tuple-element.114.refs_0_), channel_id=1, source_target_pairs={{8,0},{9,1},{10,2},{11,3},{12,4},{13,5},{14,6},{15,7},{16,8},{17,9... | collective-permute-start | bytes 122888 | tf_op jit(solution)/shard_map/ppermute | solution.py:32
  37.7 7.7 %collective-permute-start.10 = (bf16[80,256]{1,0:T(8,128)(2,1)S(1)}, bf16[80,256]{1,0:T(8,128)(2,1)S(1)}, u32[]{:S(2)}, u32[]{:S(2)}) collective-permute-start(bf16[80,256]{1,0:T(8,128)(2,1)S(1)} %get-tuple-element.114.refs_0_), channel_id=1, source_target_pairs={{12,0},{13,1},{14,2},{15,3},{16,4},{17,5},{18,6},{19,7},{20,8},{21... | collective-permute-start | bytes 122888 | tf_op jit(solution)/shard_map/ppermute | solution.py:32
  37.7 7.7 %collective-permute-start.11 = (bf16[80,256]{1,0:T(8,128)(2,1)S(1)}, bf16[80,256]{1,0:T(8,128)(2,1)S(1)}, u32[]{:S(2)}, u32[]{:S(2)}) collective-permute-start(bf16[80,256]{1,0:T(8,128)(2,1)S(1)} %get-tuple-element.114.refs_0_), channel_id=1, source_target_pairs={{16,0},{17,1},{18,2},{19,3},{20,4},{21,5},{22,6},{23,7},{24,8},{25... | collective-permute-start | bytes 122888 | tf_op jit(solution)/shard_map/ppermute | solution.py:32
  40.4 7.2 %collective-permute-start.12 = (bf16[80,256]{1,0:T(8,128)(2,1)S(1)}, bf16[80,256]{1,0:T(8,128)(2,1)S(1)}, u32[]{:S(2)}, u32[]{:S(2)}) collective-permute-start(bf16[80,256]{1,0:T(8,128)(2,1)S(1)} %get-tuple-element.114.refs_0_), channel_id=1, source_target_pairs={{20,0},{21,1},{22,2},{23,3},{24,4},{25,5},{26,6},{27,7},{28,8},{29... | collective-permute-start | bytes 122888 | tf_op jit(solution)/shard_map/ppermute | solution.py:32
  40.4 7.2 %collective-permute-start.13 = (bf16[80,256]{1,0:T(8,128)(2,1)S(1)}, bf16[80,256]{1,0:T(8,128)(2,1)S(1)}, u32[]{:S(2)}, u32[]{:S(2)}) collective-permute-start(bf16[80,256]{1,0:T(8,128)(2,1)S(1)} %get-tuple-element.114.refs_0_), channel_id=1, source_target_pairs={{24,0},{25,1},{26,2},{27,3},{28,4},{29,5},{30,6},{31,7},{0,8},{1,9... | collective-permute-start | bytes 122888 | tf_op jit(solution)/shard_map/ppermute | solution.py:32
  41.7 6.0 %collective-permute-start.14 = (bf16[80,256]{1,0:T(8,128)(2,1)S(1)}, bf16[80,256]{1,0:T(8,128)(2,1)S(1)}, u32[]{:S(2)}, u32[]{:S(2)}) collective-permute-start(bf16[80,256]{1,0:T(8,128)(2,1)S(1)} %get-tuple-element.114.refs_0_), channel_id=1, source_target_pairs={{28,0},{29,1},{30,2},{31,3},{0,4},{1,5},{2,6},{3,7},{4,8},{5,9},{6... | collective-permute-start | bytes 122888 | tf_op jit(solution)/shard_map/ppermute | solution.py:32
  50.4 5.1 %collective-permute-start.15 = (bf16[320,128]{1,0:T(8,128)(2,1)S(1)}, bf16[320,128]{1,0:T(8,128)(2,1)S(1)}, u32[]{:S(2)}, u32[]{:S(2)}) collective-permute-start(bf16[320,128]{1,0:T(8,128)(2,1)S(1)} %get-tuple-element.129), channel_id=1, source_target_pairs={{1,0},{2,1},{3,2},{0,3},{5,4},{6,5},{7,6},{4,7},{9,8},{10,9},{11,1... | collective-permute-start | bytes 245768 | tf_op jit(solution)/shard_map/ppermute | solution.py:32
  52.1 4.5 %collective-permute-start.16 = (bf16[320,128]{1,0:T(8,128)(2,1)S(1)}, bf16[320,128]{1,0:T(8,128)(2,1)S(1)}, u32[]{:S(2)}, u32[]{:S(2)}) collective-permute-start(bf16[320,128]{1,0:T(8,128)(2,1)S(1)} %get-tuple-element.129), channel_id=1, source_target_pairs={{2,0},{3,1},{0,2},{1,3},{6,4},{7,5},{4,6},{5,7},{10,8},{11,9},{8,1... | collective-permute-start | bytes 245768 | tf_op jit(solution)/shard_map/ppermute | solution.py:32
  52.6 5.3 %collective-permute-start.17 = (bf16[320,128]{1,0:T(8,128)(2,1)S(1)}, bf16[320,128]{1,0:T(8,128)(2,1)S(1)}, u32[]{:S(2)}, u32[]{:S(2)}) collective-permute-start(bf16[320,128]{1,0:T(8,128)(2,1)S(1)} %get-tuple-element.129), channel_id=1, source_target_pairs={{3,0},{0,1},{1,2},{2,3},{7,4},{4,5},{5,6},{6,7},{11,8},{8,9},{9,10... | collective-permute-start | bytes 245768 | tf_op jit(solution)/shard_map/ppermute | solution.py:32
  60.9 5.3 %collective-permute-start.18 = (bf16[80,256]{1,0:T(8,128)(2,1)S(1)}, bf16[80,256]{1,0:T(8,128)(2,1)S(1)}, u32[]{:S(2)}, u32[]{:S(2)}) collective-permute-start(bf16[80,256]{1,0:T(8,128)(2,1)S(1)} %get-tuple-element.131), channel_id=1, source_target_pairs={{28,0},{29,1},{30,2},{31,3},{0,4},{1,5},{2,6},{3,7},{4,8},{5,9},{6... | collective-permute-start | bytes 122888 | tf_op jit(solution)/shard_map/ppermute | solution.py:32
  60.9 6.8 %collective-permute-start.19 = (bf16[80,256]{1,0:T(8,128)(2,1)S(1)}, bf16[80,256]{1,0:T(8,128)(2,1)S(1)}, u32[]{:S(2)}, u32[]{:S(2)}) collective-permute-start(bf16[80,256]{1,0:T(8,128)(2,1)S(1)} %get-tuple-element.132), channel_id=1, source_target_pairs={{24,0},{25,1},{26,2},{27,3},{28,4},{29,5},{30,6},{31,7},{0,8},{1,9... | collective-permute-start | bytes 122888 | tf_op jit(solution)/shard_map/ppermute | solution.py:32
  61.3 7.8 %collective-permute-start.20 = (bf16[80,256]{1,0:T(8,128)(2,1)S(1)}, bf16[80,256]{1,0:T(8,128)(2,1)S(1)}, u32[]{:S(2)}, u32[]{:S(2)}) collective-permute-start(bf16[80,256]{1,0:T(8,128)(2,1)S(1)} %get-tuple-element.133), channel_id=1, source_target_pairs={{20,0},{21,1},{22,2},{23,3},{24,4},{25,5},{26,6},{27,7},{28,8},{29... | collective-permute-start | bytes 122888 | tf_op jit(solution)/shard_map/ppermute | solution.py:32
  62.8 7.2 %collective-permute-start.21 = (bf16[80,256]{1,0:T(8,128)(2,1)S(1)}, bf16[80,256]{1,0:T(8,128)(2,1)S(1)}, u32[]{:S(2)}, u32[]{:S(2)}) collective-permute-start(bf16[80,256]{1,0:T(8,128)(2,1)S(1)} %get-tuple-element.134), channel_id=1, source_target_pairs={{16,0},{17,1},{18,2},{19,3},{20,4},{21,5},{22,6},{23,7},{24,8},{25... | collective-permute-start | bytes 122888 | tf_op jit(solution)/shard_map/ppermute | solution.py:32
  65.1 5.0 %collective-permute-start.22 = (bf16[80,256]{1,0:T(8,128)(2,1)S(1)}, bf16[80,256]{1,0:T(8,128)(2,1)S(1)}, u32[]{:S(2)}, u32[]{:S(2)}) collective-permute-start(bf16[80,256]{1,0:T(8,128)(2,1)S(1)} %get-tuple-element.135), channel_id=1, source_target_pairs={{12,0},{13,1},{14,2},{15,3},{16,4},{17,5},{18,6},{19,7},{20,8},{21... | collective-permute-start | bytes 122888 | tf_op jit(solution)/shard_map/ppermute | solution.py:32
  66.2 4.2 %collective-permute-start.23 = (bf16[80,256]{1,0:T(8,128)(2,1)S(1)}, bf16[80,256]{1,0:T(8,128)(2,1)S(1)}, u32[]{:S(2)}, u32[]{:S(2)}) collective-permute-start(bf16[80,256]{1,0:T(8,128)(2,1)S(1)} %get-tuple-element.136), channel_id=1, source_target_pairs={{8,0},{9,1},{10,2},{11,3},{12,4},{13,5},{14,6},{15,7},{16,8},{17,9... | collective-permute-start | bytes 122888 | tf_op jit(solution)/shard_map/ppermute | solution.py:32
  67.7 2.7 %collective-permute-start.24 = (bf16[80,256]{1,0:T(8,128)(2,1)S(1)}, bf16[80,256]{1,0:T(8,128)(2,1)S(1)}, u32[]{:S(2)}, u32[]{:S(2)}) collective-permute-start(bf16[80,256]{1,0:T(8,128)(2,1)S(1)} %get-tuple-element.137), channel_id=1, source_target_pairs={{4,0},{5,1},{6,2},{7,3},{8,4},{9,5},{10,6},{11,7},{12,8},{13,9},{1... | collective-permute-start | bytes 122888 | tf_op jit(solution)/shard_map/ppermute | solution.py:32
  73.4 7.1 %collective-permute-start.25 = (bf16[3,128,256]{2,1,0:T(8,128)(2,1)S(1)}, bf16[3,128,256]{2,1,0:T(8,128)(2,1)S(1)}, u32[]{:S(2)}, u32[]{:S(2)}) collective-permute-start(bf16[3,128,256]{2,1,0:T(8,128)(2,1)S(1)} %get-tuple-element.142), channel_id=1, source_target_pairs={{28,0},{29,1},{30,2},{31,3},{0,4},{1,5},{2,6},{3,7},{4,8},{5,9},{6... | collective-permute-start | bytes 589832 | tf_op jit(solution)/shard_map/ppermute | solution.py:32
  74.6 5.9 %collective-permute-start.26 = (bf16[3,128,256]{2,1,0:T(8,128)(2,1)S(1)}, bf16[3,128,256]{2,1,0:T(8,128)(2,1)S(1)}, u32[]{:S(2)}, u32[]{:S(2)}) collective-permute-start(bf16[3,128,256]{2,1,0:T(8,128)(2,1)S(1)} %get-tuple-element.143), channel_id=1, source_target_pairs={{4,0},{5,1},{6,2},{7,3},{8,4},{9,5},{10,6},{11,7},{12,8},{13,9},{1... | collective-permute-start | bytes 589832 | tf_op jit(solution)/shard_map/ppermute | solution.py:32
  80.5 5.2 %collective-permute-start.27 = (bf16[128,256]{1,0:T(8,128)(2,1)S(1)}, bf16[128,256]{1,0:T(8,128)(2,1)S(1)}, u32[]{:S(2)}, u32[]{:S(2)}) collective-permute-start(bf16[128,256]{1,0:T(8,128)(2,1)S(1)} %get-tuple-element.151), channel_id=1, source_target_pairs={{3,0},{0,1},{1,2},{2,3},{7,4},{4,5},{5,6},{6,7},{11,8},{8,9},{9,10... | collective-permute-start | bytes 196616 | tf_op jit(solution)/shard_map/ppermute | solution.py:32
  80.6 6.6 %collective-permute-start.28 = (bf16[128,256]{1,0:T(8,128)(2,1)S(1)}, bf16[128,256]{1,0:T(8,128)(2,1)S(1)}, u32[]{:S(2)}, u32[]{:S(2)}) collective-permute-start(bf16[128,256]{1,0:T(8,128)(2,1)S(1)} %get-tuple-element.150), channel_id=1, source_target_pairs={{1,0},{2,1},{3,2},{0,3},{5,4},{6,5},{7,6},{4,7},{9,8},{10,9},{11,1... | collective-permute-start | bytes 196616 | tf_op jit(solution)/shard_map/ppermute | solution.py:32
  88.8 3.2 %collective-permute-start.30 = (f32[3,8,256]{2,1,0:T(8,128)S(1)}, f32[3,8,256]{2,1,0:T(8,128)S(1)}, u32[]{:S(2)}, u32[]{:S(2)}) collective-permute-start(f32[3,8,256]{2,1,0:T(8,128)S(1)} %get-tuple-element.146), channel_id=1, source_target_pairs={{4,0},{5,1},{6,2},{7,3},{8,4},{9,5},{10,6},{11,7},{12,8},{13,9},{1... | collective-permute-start | bytes 73736 | tf_op jit(solution)/shard_map/ppermute | solution.py:32
  90.4 5.0 %collective-permute-start.29 = (f32[3,8,256]{2,1,0:T(8,128)S(1)}, f32[3,8,256]{2,1,0:T(8,128)S(1)}, u32[]{:S(2)}, u32[]{:S(2)}) collective-permute-start(f32[3,8,256]{2,1,0:T(8,128)S(1)} %get-tuple-element.145), channel_id=1, source_target_pairs={{28,0},{29,1},{30,2},{31,3},{0,4},{1,5},{2,6},{3,7},{4,8},{5,9},{6... | collective-permute-start | bytes 73736 | tf_op jit(solution)/shard_map/ppermute | solution.py:32
  95.4 3.7 %collective-permute-start.32 = (f32[8,256]{1,0:T(8,128)S(1)}, f32[8,256]{1,0:T(8,128)S(1)}, u32[]{:S(2)}, u32[]{:S(2)}) collective-permute-start(f32[8,256]{1,0:T(8,128)S(1)} %get-tuple-element.153), channel_id=1, source_target_pairs={{1,0},{2,1},{3,2},{0,3},{5,4},{6,5},{7,6},{4,7},{9,8},{10,9},{11,1... | collective-permute-start | bytes 24584 | tf_op jit(solution)/shard_map/ppermute | solution.py:32
  97.3 4.5 %collective-permute-start.31 = (f32[8,256]{1,0:T(8,128)S(1)}, f32[8,256]{1,0:T(8,128)S(1)}, u32[]{:S(2)}, u32[]{:S(2)}) collective-permute-start(f32[8,256]{1,0:T(8,128)S(1)} %get-tuple-element.154), channel_id=1, source_target_pairs={{3,0},{0,1},{1,2},{2,3},{7,4},{4,5},{5,6},{6,7},{11,8},{8,9},{9,10... | collective-permute-start | bytes 24584 | tf_op jit(solution)/shard_map/ppermute | solution.py:32

commit v7 on v6

--- a/solution.py
+++ b/solution.py
@@ -30,6 +30,11 @@
             source = ((i + along_x) % count_x) * count_y + (j + along_y) % count_y
             route.append((source, i * count_y + j))
     return lax.ppermute(block, ("gx", "gy"), route)
+
+
+def swapped(block):
+    count = lax.axis_size("gx")
+    return lax.ppermute(block, "gx", [(i ^ 1, i) for i in range(count)])
 
 
 def around(block, beside):
@@ -150,7 +155,7 @@
     return [basis] + [basis * unit[i : i + 1] for i in range(3)]
 
 
-def pack_kernel(position_ref, species_ref, out_ref, place, kind, sems):
+def pack_kernel(place_ref, position_ref, species_ref, out_ref, place, kind, sems):
     copies = [
         pltpu.make_async_copy(position_ref, place, sems.at[0]),
         pltpu.make_async_copy(species_ref, kind, sems.at[1]),
@@ -394,9 +399,9 @@
     return both[:half] + both[half:]
 
 
-def second_back_kernel(slots, scale, grid_x, hot_ref, weight_ref, turn_high, turn_low, charge_ref,
+def second_back_kernel(slots, scale, count, hot_ref, weight_ref, turn_high, turn_low, charge_ref,
                        sums_ref, gate_ref, full_charge_ref, energy_ref, slope_ref, *refs):
-    folds, refs = refs[:grid_x], refs[grid_x:]
+    folds, refs = refs[:count], refs[count:]
     site_ref, long_ref, cotangent_ref, grad_ref, term_ref, before_ref, after_ref = refs
     atoms = gate_ref.shape[1]
     total = folds[0][...].astype(F32)
@@ -588,23 +593,28 @@
     return jnp.concatenate([block[:half], block[half:]], axis=1)
 
 
-def structure_kernel(share, padded, grid, wide, place_ref, *refs):
+def structure_kernel(share, padded, grid, wide, flip, place_ref, blocks, *refs):
     grid_x, grid_y = grid
-    blocks, (ca_ref, sa_ref, cb_ref, sb_ref, high_ref, low_ref, own_ref, out_ref) = (
-        refs[:grid_x],
-        refs[grid_x:],
-    )
+    if flip:
+        near_ref, (ca_ref, sa_ref, cb_ref, sb_ref, high_ref, low_ref, own_ref, out_ref) = (
+            refs[0],
+            refs[1:],
+        )
+        total = near_ref[...]
+    else:
+        ca_ref, sa_ref, cb_ref, sb_ref, high_ref, low_ref, total_ref = refs
+        total = None
     col = place_ref[1].astype(F32) * (1.0 / grid_y)
+    first = place_ref[0] ^ flip
     kx, ky, _ = pair_vectors(count_up(padded), share, place_ref[0])
     kz = count_up(8) + 1.0
-    total = None
-    for d in range(grid_x):
-        block = blocks[d][...]
+    for d in range(grid_x // 2):
+        block = blocks[d]
         charge = block[:wide]
         atoms = charge.shape[1]
         pieces = block[wide:].astype(F32)
         place = pieces[0:3] + (pieces[3:6] + pieces[6:9])
-        row = lax.rem(place_ref[0] + d, grid_x).astype(F32) * (1.0 / grid_x)
+        row = lax.rem(first + 2 * d, grid_x).astype(F32) * (1.0 / grid_x)
         x = place[0:1] * (1.0 / (grid_x * cell_width)) + row
         y = place[1:2] * (1.0 / (grid_y * cell_width)) + col
         sa, ca = sin_cos(kx * x + ky * y)
@@ -620,16 +630,15 @@
         low_ref[:, lanes] = low
         term = dot(high, charge, ((1,), (1,))) + dot(low, charge, ((1,), (1,)))
         total = term if total is None else total + term
-    packed = pack_rows(total)
-    own_ref[...] = packed
-    out_ref[...] = packed.astype(BF16)
-
-
-def fold_kernel(share, padded, grid, wide, place_ref, ca_ref, sa_ref, cb_ref, sb_ref, high_ref,
-                low_ref, weight_ref, *refs):
-    grid_x, grid_y = grid
-    blocks, parts, outs = refs[:grid_x], refs[grid_x : grid_x + grid_y], refs[grid_x + grid_y :]
-    turn = 2.0 * math.pi
+    if flip:
+        packed = pack_rows(total)
+        own_ref[...] = packed
+        out_ref[...] = packed.astype(BF16)
+    else:
+        total_ref[...] = total
+
+
+def weighted_rows(share, padded, wide, weight_ref, parts):
     packed = parts[0][...].astype(F32)
     for part in parts[1:]:
         packed = packed + part[...].astype(F32)
@@ -651,16 +660,31 @@
         ],
         axis=0,
     )
+    return rows
+
+
+def fold_kernel(share, padded, grid, wide, flip, place_ref, *refs):
+    grid_x, grid_y = grid
+    turn = 2.0 * math.pi
+    if flip:
+        weight_ref, parts, refs = refs[0], refs[1 : 1 + grid_y], refs[1 + grid_y :]
+        rows = weighted_rows(share, padded, wide, weight_ref, parts)
+        refs, rows_ref = refs[:-1], refs[-1]
+        rows_ref[...] = rows
+    else:
+        rows, refs = refs[0][...], refs[1:]
+    ca_ref, sa_ref, cb_ref, sb_ref, high_ref, low_ref, blocks, out_ref = refs
     row_high, row_low = split(rows)
     row_pair = jnp.concatenate([row_high, row_low], axis=1)
     turned = rows.T
     t_high, t_low = split(turned)
     t_both = jnp.concatenate([t_high, t_low], axis=0)
+    span = 8 * share
     kx, ky, _ = pair_vectors(count_up(padded), share, place_ref[0])
     kx = kx * (turn / (grid_x * cell_width))
     ky = ky * (turn / (grid_y * cell_width))
     kz = (count_up(8) + 1.0) * (turn / box_height)
-    for d in range(grid_x):
+    for d in range(grid_x // 2):
         charge = blocks[d][:wide]
         atoms = charge.shape[1]
         lanes = pl.ds(d * atoms, atoms)
@@ -686,12 +710,31 @@
         grad_y = jnp.sum(by_y, axis=0, keepdims=True) + jnp.sum(ky * flat_slope, axis=0, keepdims=True)
         grad_z = jnp.sum(kz * by_z, axis=0, keepdims=True)
         slopes = jnp.concatenate([grad_x, grad_y, grad_z], axis=0)
-        high = slopes.astype(BF16).astype(F32)
-        rest = slopes - high
-        middle = rest.astype(BF16).astype(F32)
-        zero = jnp.zeros((outs[d].shape[0] - wide - 9, atoms), F32)
-        block = jnp.concatenate([pot, high, middle, rest - middle, zero], axis=0)
-        outs[d][...] = block.astype(outs[d].dtype)
+        out_ref[d] = pieced(pot, slopes, out_ref.shape[1]).astype(out_ref.dtype)
+
+
+def pieced(pot, slopes, rows):
+    high = slopes.astype(BF16).astype(F32)
+    rest = slopes - high
+    middle = rest.astype(BF16).astype(F32)
+    zero = jnp.zeros((rows - pot.shape[0] - 9, pot.shape[1]), F32)
+    return jnp.concatenate([pot, high, middle, rest - middle, zero], axis=0)
+
+
+def unpieced(block, wide):
+    slopes = block[wide : wide + 3] + (block[wide + 3 : wide + 6] + block[wide + 6 : wide + 9])
+    return block[:wide], slopes
+
+
+def join_kernel(wide, near_ref, far_ref, own_ref, *outs):
+    for d in range(near_ref.shape[0]):
+        pot, slopes = unpieced(near_ref[d], wide)
+        pot_far, slopes_far = unpieced(far_ref[d].astype(F32), wide)
+        block = pieced(pot + pot_far, slopes + slopes_far, near_ref.shape[1])
+        if d:
+            outs[d - 1][...] = block.astype(BF16)
+        else:
+            own_ref[...] = block
 
 
 def per_device(
@@ -724,14 +767,14 @@
     (own,) = run(
         pack_kernel,
         [shape(4 * atoms // 128, 128)],
-        [shown, species],
+        [place, shown, species],
         scratch=[
             pltpu.VMEM(shown.shape, F32),
             pltpu.VMEM(species.shape, jnp.int32),
             dma((2,)),
         ],
+        smem=1,
         hbm=2,
-        grant=60,
         name="pack",
     )
     norm = 1.0 / math.sqrt(slots)
@@ -761,7 +804,7 @@
         hbm=5,
         name="prep_first",
     )
-    cells, (ids, place) = around(own, (ids, place))
+    cells, ids = around(own, ids)
     (hot,) = run(
         hot_kernel, [shape(9 * atoms, edges, dtype=BF16)], [ids], flops=2_000_000_000, name="hot"
     )
@@ -831,7 +874,8 @@
          hidden_turn_low, read_out, charge_pair, cells[1], hidden[1], hidden[0]],
         name="second",
     )
-    charges = [packed] + [shifted(packed, d, 0) for d in range(1, grid_x)]
+    half = grid_x // 2
+    near_charges = jnp.stack([packed] + [shifted(packed, 2 * d, 0) for d in range(1, half)])
     (hot_back,) = run(
         hot_back_kernel,
         [shape(edges, 9 * atoms, dtype=BF16)],
@@ -839,37 +883,64 @@
         flops=2_000_000_000,
         name="hot_back",
     )
-    charges, hot_back = lax.optimization_barrier((charges, hot_back))
-    span = grid_x * atoms
+    near_charges, hot_back = lax.optimization_barrier((near_charges, hot_back))
+    far_charges = swapped(near_charges)
+    span = half * atoms
     rows = 32 * share + 2 * padded
-    *phases, own_part, part = run(
-        functools.partial(structure_kernel, share, padded, grid, lat_width),
-        [
-            shape(padded, span),
-            shape(padded, span),
-            shape(8, span),
-            shape(8, span),
-            shape(rows, span, dtype=BF16),
-            shape(rows, span, dtype=BF16),
+    phase_shapes = [
+        shape(padded, span),
+        shape(padded, span),
+        shape(8, span),
+        shape(8, span),
+        shape(rows, span, dtype=BF16),
+        shape(rows, span, dtype=BF16),
+    ]
+    *near_phases, near_total = run(
+        functools.partial(structure_kernel, share, padded, grid, lat_width, 0),
+        phase_shapes + [shape(rows, lat_width)],
+        [place, near_charges],
+        smem=1,
+        flops=1_000_000_000,
+        name="structure_near",
+    )
+    *far_phases, own_part, part = run(
+        functools.partial(structure_kernel, share, padded, grid, lat_width, 1),
+        phase_shapes
+        + [
             shape(rows // 2, 2 * lat_width),
             shape(rows // 2, 2 * lat_width, dtype=BF16),
         ],
-        [place] + charges,
+        [place, far_charges, near_total],
         smem=1,
-        name="structure",
+        name="structure_far",
     )
     parts = [own_part] + [shifted(part, 0, d) for d in range(1, grid_y)]
+    far_folds, wave_rows = run(
+        functools.partial(fold_kernel, share, padded, grid, lat_width, 1),
+        [shape(half, block_rows, atoms, dtype=BF16), shape(rows, lat_width)],
+        [place, weight] + parts + far_phases + [far_charges],
+        smem=1,
+        name="fold_far",
+    )
+    far_folds = swapped(far_folds)
+    (near_folds,) = run(
+        functools.partial(fold_kernel, share, padded, grid, lat_width, 0),
+        [shape(half, block_rows, atoms)],
+        [place, wave_rows] + near_phases + [near_charges],
+        smem=1,
+        flops=1_000_000_000,
+        name="fold_near",
+    )
     folds = run(
-        functools.partial(fold_kernel, share, padded, grid, lat_width),
-        [shape(block_rows, atoms)] + [shape(block_rows, atoms, dtype=BF16)] * (grid_x - 1),
-        [place] + phases + [weight] + charges + parts,
-        smem=1,
-        name="fold",
-    )
-    folds = [folds[0]] + [shifted(folds[d], -d, 0) for d in range(1, grid_x)]
+        functools.partial(join_kernel, lat_width),
+        [shape(block_rows, atoms)] + [shape(block_rows, atoms, dtype=BF16)] * (half - 1),
+        [near_folds, far_folds],
+        name="fold_join",
+    )
+    folds = [folds[0]] + [shifted(folds[d], -2 * d, 0) for d in range(1, half)]
 
     site, long, cotangent, grads, term, before, after = run(
-        functools.partial(second_back_kernel, slots, scale, grid_x),
+        functools.partial(second_back_kernel, slots, scale, half),
         [
             shape(1, 1, atoms),
             shape(8, atoms),

time: 103 us -> 99.4 us (0.965)
  starting transfers between devices: 37.5 us -> 33.3 us
  local copies, waits for them, and re-layouts: 4.35 us -> 5.72 us
    ppermute x33 -> x25, starting transfers between devices: 37.5 us -> 33.2 us  [shifted(): return lax.ppermute(block, ('gx', 'gy'), route)]
    unnamed x19 -> x23, local copies, waits for them, and re-layouts: 4.35 us -> 5.71 us
    ppermute x33 -> x25, waiting for transfers between devices: 31.5 us -> 30.8 us  [shifted(): return lax.ppermute(block, ('gx', 'gy'), route)]
    pallas_call x16 -> x19, Pallas kernels: 27.4 us -> 28.1 us  [run(): pl.pallas_call(kernel, out_shape=outs, in_specs=specs, out_specs=[whole()...]
  transfers between devices with their start and end apart: 33 -> 27, of which waited for: 22 -> 17; matrix products, arithmetic and copies ran while one was open for 0% -> 0% of each run, Pallas kernels for 12% -> 16%
where the time goes in v7:
time: 99.4 us; the launch traced here: 99 us
  starting transfers between devices  33.3 us (34%)
  waiting for transfers between devices  30.8 us (31%)
  Pallas kernels  28.1 us (28%)
  local copies, waits for them, and re-layouts  5.72 us (6%)
    ppermute x25, starting transfers between devices, shifted(): return lax.ppermute(block, ('gx', 'gy'), route)  33.2 us
    ppermute x25, waiting for transfers between devices, shifted(): return lax.ppermute(block, ('gx', 'gy'), route)  30.8 us
    pallas_call x19, Pallas kernels, run(): pl.pallas_call(kernel, out_shape=outs, in_specs=specs, out_specs=[whole()...  28.1 us
    unnamed x23, local copies, waits for them, and re-layouts  5.71 us
  transfers between devices with their start and end apart: 27, of which 17 were waited for; matrix products, arithmetic and copies ran while one was open for 0% of the time, Pallas kernels for 16%

profile of v7, /device:TPU:0, one launch (start us, length us, event | category | flops | bytes accessed | tf_op | source)
XLA Modules:
  0.0 99.0 jit_solution(15299187541726006433)
XLA Ops:
  0.6 0.1 pad_add_fusion.place_ref
  0.7 0.7 copy-done.9
  1.4 0.7 copy-done.10
  2.1 0.6 pack.1
  2.7 3.9 %collective-permute-start.1 = (f32[8,128]{1,0:T(8,128)S(1)}, f32[8,128]{1,0:T(8,128)S(1)}, u32[]{:S(2)}, u32[]{:S(2)}) collective-permute-start(f32[8,128]{1,0:T(8,128)S(1)} %pack.1), channel_id=1, source_target_pairs={{1,0},{2,1},{3,2},{0,3},{5,4},{6,5},{7,6},{4,7},{9,8},{10,9},{11,1... | collective-permute-start | bytes 12296 | tf_op jit(solution)/shard_map/ppermute | solution.py:32
  6.6 0.9 copy-done
  7.6 0.7 copy-done.4
  8.3 0.7 copy-done.5
  9.0 0.7 copy-done.6
  9.7 0.7 copy-done.7
  10.3 0.3 prep_first.1
  10.7 0.4 collective-permute-done
  11.1 3.5 %collective-permute-start.3 = (f32[3,8,128]{2,1,0:T(8,128)S(1)}, f32[3,8,128]{2,1,0:T(8,128)S(1)}, u32[]{:S(2)}, u32[]{:S(2)}) collective-permute-start(f32[3,8,128]{2,1,0:T(8,128)S(1)} %pad_maximum_fusion.2.column_ref.cell_ref), channel_id=1, source_target_pairs={{4,0},{5,1},{6,2},{7,3},{8,4},{9,5},{10,6},{11,7},{12,8},{13,9},{1... | collective-permute-start | bytes 36872 | tf_op jit(solution)/shard_map/ppermute | solution.py:32
  14.7 1.4 %collective-permute-done.2.before_ref = f32[3,8,128]{2,1,0:T(8,128)S(1)} collective-permute-done((f32[3,8,128]{2,1,0:T(8,128)S(1)}, f32[3,8,128]{2,1,0:T(8,128)S(1)}, u32[]{:S(2)}, u32[]{:S(2)}) %collective-permute-start.2) | collective-permute-done | bytes 12320 | tf_op jit(solution)/shard_map/ppermute | solution.py:32
  16.1 1.3 %first.1 = (bf16[128,256]{1,0:T(8,128)(2,1)S(1)}, f32[8,3072]{1,0:T(8,128)S(1)}, f32[8,3072]{1,0:T(8,128)S(1)}, f32[8,3072]{1,0:T(8,128)S(1)}, f32[3,128,256]{2,1,0:T(8,128)S(1)}, /*index=5*/f32[128,256]{1,0:T(8,128)S(1)}) custom-call(s32[1,3072]{1,0:T(1,128)S(1)} %get-tuple-element.73.ids_ref, s32[1,1,256]{2,1,0:T(1,128)S(1)} %get-tuple-element.74.count_ref, ...), custom_call_target="tpu_custom_call" | custom-call | flops 10000000 | bytes 1000000 | tf_op jit(solution)/shard_map/first/pallas_call | solution.py:54
  17.4 2.6 %collective-permute-start.5 = (bf16[128,256]{1,0:T(8,128)(2,1)S(1)}, bf16[128,256]{1,0:T(8,128)(2,1)S(1)}, u32[]{:S(2)}, u32[]{:S(2)}) collective-permute-start(bf16[128,256]{1,0:T(8,128)(2,1)S(1)} %get-tuple-element.90), channel_id=1, source_target_pairs={{1,0},{2,1},{3,2},{0,3},{5,4},{6,5},{7,6},{4,7},{9,8},{10,9},{11,1... | collective-permute-start | bytes 196616 | tf_op jit(solution)/shard_map/ppermute | solution.py:32
  20.0 3.2 %hot.1.hot_ref = bf16[2304,3072]{1,0:T(8,128)(2,1)S(1)} custom-call(s32[1,3072]{1,0:T(1,128)S(1)} %get-tuple-element.73.ids_ref), custom_call_target="tpu_custom_call" | custom-call | flops 2000000000 | bytes 1000000 | tf_op jit(solution)/shard_map/hot/pallas_call | solution.py:54
  23.3 1.9 %collective-permute-done.4 = bf16[128,256]{1,0:T(8,128)(2,1)S(1)} collective-permute-done((bf16[128,256]{1,0:T(8,128)(2,1)S(1)}, bf16[128,256]{1,0:T(8,128)(2,1)S(1)}, u32[]{:S(2)}, u32[]{:S(2)}) %collective-permute-start.4) | collective-permute-done | bytes 65568 | tf_op jit(solution)/shard_map/ppermute | solution.py:32
  25.2 2.1 %collective-permute-start.6 = (bf16[3,128,256]{2,1,0:T(8,128)(2,1)S(1)}, bf16[3,128,256]{2,1,0:T(8,128)(2,1)S(1)}, u32[]{:S(2)}, u32[]{:S(2)}) collective-permute-start(bf16[3,128,256]{2,1,0:T(8,128)(2,1)S(1)} %pad_maximum_fusion.column_ref), channel_id=1, source_target_pairs={{4,0},{5,1},{6,2},{7,3},{8,4},{9,5},{10,6},{11,7},{12,8},{13,9},{1... | collective-permute-start | bytes 589832 | tf_op jit(solution)/shard_map/ppermute | solution.py:32
  27.4 0.3 prep_second.1
  27.7 1.6 %second_near.1 = (f32[4,128,3072]{2,1,0:T(8,128)S(1)}, f32[128,3072]{1,0:T(8,128)S(1)}) custom-call(f32[8,3072]{1,0:T(8,128)S(1)} %get-tuple-element.80.basis_ref, f32[8,3072]{1,0:T(8,128)S(1)} %get-tuple-element.82.unit_ref, bf16[2,128,32]{2,1,0:T(8,128)(2,1)S(1)} %get-tuple-element.92.left_ref, bf16[2304,3072]{1,0:T(8,128)(2,1)S(1)} %hot.1.hot_ref, ...), custom_call_target="tpu_custom_call" | custom-call | flops 2000000000 | bytes 1000000 | tf_op jit(solution)/shard_map/second_near/pallas_call | solution.py:54
  29.3 1.4 %collective-permute-done.6.after_ref = bf16[3,128,256]{2,1,0:T(8,128)(2,1)S(1)} collective-permute-done((bf16[3,128,256]{2,1,0:T(8,128)(2,1)S(1)}, bf16[3,128,256]{2,1,0:T(8,128)(2,1)S(1)}, u32[]{:S(2)}, u32[]{:S(2)}) %collective-permute-start.6) | collective-permute-done | bytes 196640 | tf_op jit(solution)/shard_map/ppermute | solution.py:32
  30.7 0.8 second_side.1.near_ref
  31.6 3.0 %collective-permute-done.7.before_ref = bf16[3,128,256]{2,1,0:T(8,128)(2,1)S(1)} collective-permute-done((bf16[3,128,256]{2,1,0:T(8,128)(2,1)S(1)}, bf16[3,128,256]{2,1,0:T(8,128)(2,1)S(1)}, u32[]{:S(2)}, u32[]{:S(2)}) %collective-permute-start.7) | collective-permute-done | bytes 196640 | tf_op jit(solution)/shard_map/ppermute | solution.py:32
  34.6 2.2 %second.1 = (bf16[128,3072]{1,0:T(8,128)(2,1)S(1)}, f32[3,128,256]{2,1,0:T(8,128)S(1)}, f32[128,256]{1,0:T(8,128)S(1)}, bf16[80,256]{1,0:T(8,128)(2,1)S(1)}, f32...) custom-call(bf16[2304,3072]{1,0:T(8,128)(2,1)S(1)} %hot.1.hot_ref, ...), custom_call_target="tpu_custom_call" | custom-call | flops 10000000 | bytes 1000000 | tf_op jit(solution)/shard_map/second/pallas_call | solution.py:54
  36.9 1.2 %collective-permute-start.9 = (bf16[80,256]{1,0:T(8,128)(2,1)S(1)}, bf16[80,256]{1,0:T(8,128)(2,1)S(1)}, u32[]{:S(2)}, u32[]{:S(2)}) collective-permute-start(bf16[80,256]{1,0:T(8,128)(2,1)S(1)} %get-tuple-element.103), channel_id=1, source_target_pairs={{16,0},{17,1},{18,2},{19,3},{20,4},{21,5},{22,6},{23,7},{24,8},{25... | collective-permute-start | bytes 122888 | tf_op jit(solution)/shard_map/ppermute | solution.py:32
  38.0 2.6 %collective-permute-start.8 = (bf16[80,256]{1,0:T(8,128)(2,1)S(1)}, bf16[80,256]{1,0:T(8,128)(2,1)S(1)}, u32[]{:S(2)}, u32[]{:S(2)}) collective-permute-start(bf16[80,256]{1,0:T(8,128)(2,1)S(1)} %get-tuple-element.103), channel_id=1, source_target_pairs={{8,0},{9,1},{10,2},{11,3},{12,4},{13,5},{14,6},{15,7},{16,8},{17,9... | collective-permute-start | bytes 122888 | tf_op jit(solution)/shard_map/ppermute | solution.py:32
  40.7 2.8 %hot_back.1.hot_ref = bf16[3072,2304]{1,0:T(8,128)(2,1)S(1)} custom-call(s32[1,3072]{1,0:T(1,128)S(1)} %get-tuple-element.73.ids_ref), custom_call_target="tpu_custom_call" | custom-call | flops 2000000000 | bytes 1000000 | tf_op jit(solution)/shard_map/hot_back/pallas_call | solution.py:54
  43.6 0.1 collective-permute-start.11
  43.7 1.7 %structure_near.1 = (f32[32,1024]{1,0:T(8,128)S(1)}, f32[32,1024]{1,0:T(8,128)S(1)}, f32[8,1024]{1,0:T(8,128)S(1)}, f32[8,1024]{1,0:T(8,128)S(1)}, bf16[640,1024...) custom-call(s32[2]{0:T(128)S(1)} %pad_add_fusion.place_ref, ...), custom_call_target="tpu_custom_call" | custom-call | flops 1000000000 | bytes 1000000 | tf_op jit(solution)/shard_map/structure_near/pallas_call | solution.py:54
  45.4 1.8 %structure_far.1 = (f32[32,1024]{1,0:T(8,128)S(1)}, f32[32,1024]{1,0:T(8,128)S(1)}, f32[8,1024]{1,0:T(8,128)S(1)}, f32[8,1024]{1,0:T(8,128)S(1)}, bf16[640,1024]...) custom-call(s32[2]{0:T(128)S(1)} %pad_add_fusion.place_ref, ...), custom_call_target="tpu_custom_call" | custom-call | flops 10000000 | bytes 1000000 | tf_op jit(solution)/shard_map/structure_far/pallas_call | solution.py:54
  47.3 2.0 %collective-permute-start.12 = (bf16[320,128]{1,0:T(8,128)(2,1)S(1)}, bf16[320,128]{1,0:T(8,128)(2,1)S(1)}, u32[]{:S(2)}, u32[]{:S(2)}) collective-permute-start(bf16[320,128]{1,0:T(8,128)(2,1)S(1)} %get-tuple-element.113), channel_id=1, source_target_pairs={{1,0},{2,1},{3,2},{0,3},{5,4},{6,5},{7,6},{4,7},{9,8},{10,9},{11,1... | collective-permute-start | bytes 245768 | tf_op jit(solution)/shard_map/ppermute | solution.py:32
  49.2 0.5 collective-permute-start.13
  49.7 0.1 collective-permute-start.14
  49.9 1.3 %green.1.refs_0_ = f32[320,128]{1,0:T(8,128)S(1)} custom-call(s32[2]{0:T(128)S(1)} %pad_add_fusion.place_ref, s32[3,4096]{1,0:T(4,128)S(1)} %copy-done.1), custom_call_target="tpu_custom_call" | custom-call | flops 10000000 | bytes 1000000 | tf_op jit(solution)/shard_map/green/pallas_call | solution.py:54
  51.2 0.9 collective-permute-done.12.refs_2_
  52.1 3.4 %collective-permute-done.13.refs_3_ = bf16[320,128]{1,0:T(8,128)(2,1)S(1)} collective-permute-done((bf16[320,128]{1,0:T(8,128)(2,1)S(1)}, bf16[320,128]{1,0:T(8,128)(2,1)S(1)}, u32[]{:S(2)}, u32[]{:S(2)}) %collective-permute-start.13) | collective-permute-done | bytes 81952 | tf_op jit(solution)/shard_map/ppermute | solution.py:32
  55.5 1.9 %fold_far.1 = (bf16[4,80,256]{2,1,0:T(8,128)(2,1)S(1)}, f32[640,64]{1,0:T(8,128)S(1)}) custom-call(s32[2]{0:T(128)S(1)} %pad_add_fusion.place_ref, f32[320,128]{1,0:T(8,128)S(1)} %green.1.refs_0_, f32[320,128]{1,0:T(8,128)S(1)} %get-tuple-element.112.refs_1_, bf16[320,128]{1,0:T(8,128)(2,1)S(1)} %collective-permute-done.12.refs_2_, ...), custom_call_target="tpu_custom_call" | custom-call | flops 10000000 | bytes 1000000 | tf_op jit(solution)/shard_map/fold_far/pallas_call | solution.py:54
  57.4 0.1 collective-permute-start.15
  57.5 1.8 %fold_near.1.near_ref = f32[4,80,256]{2,1,0:T(8,128)S(1)} custom-call(s32[2]{0:T(128)S(1)} %pad_add_fusion.place_ref, f32[640,64]{1,0:T(8,128)S(1)} %get-tuple-element.120.refs_0_, f32[32,1024]{1,0:T(8,128)S(1)} %get-tuple-element.121.refs_1_, f32[32,1024]{1,0:T(8,128)S(1)} %get-tuple-element.122.refs_2_, f32[8,1024]{1,0:T(8,128)S(1)} %get-tuple-element.123.refs_3_, ...), custom_call_target="tpu_custom_call" | custom-call | flops 1000000000 | bytes 1000000 | tf_op jit(solution)/shard_map/fold_near/pallas_call | solution.py:54
  59.3 0.1 fold_join.1
  59.4 1.7 %collective-permute-start.16 = (bf16[80,256]{1,0:T(8,128)(2,1)S(1)}, bf16[80,256]{1,0:T(8,128)(2,1)S(1)}, u32[]{:S(2)}, u32[]{:S(2)}) collective-permute-start(bf16[80,256]{1,0:T(8,128)(2,1)S(1)} %get-tuple-element.129), channel_id=1, source_target_pairs={{24,0},{25,1},{26,2},{27,3},{28,4},{29,5},{30,6},{31,7},{0,8},{1,9... | collective-permute-start | bytes 122888 | tf_op jit(solution)/shard_map/ppermute | solution.py:32
  61.1 1.8 %collective-permute-start.17 = (bf16[80,256]{1,0:T(8,128)(2,1)S(1)}, bf16[80,256]{1,0:T(8,128)(2,1)S(1)}, u32[]{:S(2)}, u32[]{:S(2)}) collective-permute-start(bf16[80,256]{1,0:T(8,128)(2,1)S(1)} %get-tuple-element.130), channel_id=1, source_target_pairs={{16,0},{17,1},{18,2},{19,3},{20,4},{21,5},{22,6},{23,7},{24,8},{25... | collective-permute-start | bytes 122888 | tf_op jit(solution)/shard_map/ppermute | solution.py:32
  62.9 1.5 %collective-permute-start.18 = (bf16[80,256]{1,0:T(8,128)(2,1)S(1)}, bf16[80,256]{1,0:T(8,128)(2,1)S(1)}, u32[]{:S(2)}, u32[]{:S(2)}) collective-permute-start(bf16[80,256]{1,0:T(8,128)(2,1)S(1)} %get-tuple-element.131), channel_id=1, source_target_pairs={{8,0},{9,1},{10,2},{11,3},{12,4},{13,5},{14,6},{15,7},{16,8},{17,9... | collective-permute-start | bytes 122888 | tf_op jit(solution)/shard_map/ppermute | solution.py:32
  64.4 1.1 %collective-permute-done.16.refs_1_ = bf16[80,256]{1,0:T(8,128)(2,1)S(1)} collective-permute-done((bf16[80,256]{1,0:T(8,128)(2,1)S(1)}, bf16[80,256]{1,0:T(8,128)(2,1)S(1)}, u32[]{:S(2)}, u32[]{:S(2)}) %collective-permute-start.16) | collective-permute-done | bytes 40992 | tf_op jit(solution)/shard_map/ppermute | solution.py:32
  65.4 1.6 %collective-permute-done.17.refs_2_ = bf16[80,256]{1,0:T(8,128)(2,1)S(1)} collective-permute-done((bf16[80,256]{1,0:T(8,128)(2,1)S(1)}, bf16[80,256]{1,0:T(8,128)(2,1)S(1)}, u32[]{:S(2)}, u32[]{:S(2)}) %collective-permute-start.17) | collective-permute-done | bytes 40992 | tf_op jit(solution)/shard_map/ppermute | solution.py:32
  67.0 0.2 collective-permute-done.18.refs_3_
  67.3 2.7 %second_back.1 = (f32[1,1,256]{2,1,0:T(1,128)}, f32[8,256]{1,0:T(8,128)S(1)}, f32[128,256]{1,0:T(8,128)S(1)}, f32[4,128,256]{2,1,0:T(8,128)S(1)}, bf16[128,3072]...) custom-call(bf16[3072,2304]{1,0:T(8,128)(2,1)S(1)} %hot_back.1.hot_ref, ...), custom_call_target="tpu_custom_call" | custom-call | flops 10000000 | bytes 1000000 | tf_op jit(solution)/shard_map/second_back/pallas_call | solution.py:54
  70.0 3.5 %collective-permute-start.20 = (bf16[3,128,256]{2,1,0:T(8,128)(2,1)S(1)}, bf16[3,128,256]{2,1,0:T(8,128)(2,1)S(1)}, u32[]{:S(2)}, u32[]{:S(2)}) collective-permute-start(bf16[3,128,256]{2,1,0:T(8,128)(2,1)S(1)} %get-tuple-element.137), channel_id=1, source_target_pairs={{4,0},{5,1},{6,2},{7,3},{8,4},{9,5},{10,6},{11,7},{12,8},{13,9},{1... | collective-permute-start | bytes 589832 | tf_op jit(solution)/shard_map/ppermute | solution.py:32
  73.5 0.8 second_middle.1.middle_ref
  74.4 3.3 %collective-permute-done.19.refs_0_ = bf16[3,128,256]{2,1,0:T(8,128)(2,1)S(1)} collective-permute-done((bf16[3,128,256]{2,1,0:T(8,128)(2,1)S(1)}, bf16[3,128,256]{2,1,0:T(8,128)(2,1)S(1)}, u32[]{:S(2)}, u32[]{:S(2)}) %collective-permute-start.19) | collective-permute-done | bytes 196640 | tf_op jit(solution)/shard_map/ppermute | solution.py:32
  77.7 0.4 collective-permute-start.21
  78.1 2.6 %collective-permute-start.22 = (bf16[128,256]{1,0:T(8,128)(2,1)S(1)}, bf16[128,256]{1,0:T(8,128)(2,1)S(1)}, u32[]{:S(2)}, u32[]{:S(2)}) collective-permute-start(bf16[128,256]{1,0:T(8,128)(2,1)S(1)} %get-tuple-element.144), channel_id=1, source_target_pairs={{1,0},{2,1},{3,2},{0,3},{5,4},{6,5},{7,6},{4,7},{9,8},{10,9},{11,1... | collective-permute-start | bytes 196616 | tf_op jit(solution)/shard_map/ppermute | solution.py:32
  80.7 1.2 %second_edge.1.edge_ref = f32[32,3072]{1,0:T(8,128)S(1)} custom-call(bf16[2,16,256]{2,1,0:T(8,128)(2,1)S(1)} %get-tuple-element.89.back_ref, bf16[128,3072]{1,0:T(8,128)(2,1)S(1)} %get-tuple-element.102.feature_ref, f32[4,128,256]{2,1,0:T(8,128)S(1)} %get-tuple-element.132.grad_ref), custom_call_target="tpu_custom_call" | custom-call | flops 1000000000 | bytes 1000000 | tf_op jit(solution)/shard_map/second_edge/pallas_call | solution.py:54
  81.9 1.7 %collective-permute-done.21.refs_2_ = bf16[128,256]{1,0:T(8,128)(2,1)S(1)} collective-permute-done((bf16[128,256]{1,0:T(8,128)(2,1)S(1)}, bf16[128,256]{1,0:T(8,128)(2,1)S(1)}, u32[]{:S(2)}, u32[]{:S(2)}) %collective-permute-start.21) | collective-permute-done | bytes 65568 | tf_op jit(solution)/shard_map/ppermute | solution.py:32
  83.6 0.8 collective-permute-done.22.refs_3_
  84.4 1.5 %first_back.1 = (f32[3,8,256]{2,1,0:T(8,128)S(1)}, f32[3,8,256]{2,1,0:T(8,128)S(1)}, f32[3,8,256]{2,1,0:T(8,128)S(1)}) custom-call(s32[1,3072]{1,0:T(1,128)S(1)} %get-tuple-element.73.ids_ref, f32[8,3072]{1,0:T(8,128)S(1)} %get-tuple-element.80.basis_ref, f32[8,3072]{1,0:T(8,128)S(1)} %get-tuple-element.81.slope_ref, ...), custom_call_target="tpu_custom_call" | custom-call | flops 10000000 | bytes 1000000 | tf_op jit(solution)/shard_map/first_back/pallas_call | solution.py:54
  85.9 0.6 collective-permute-start.24
  86.5 1.5 %collective-permute-done.24 = f32[3,8,256]{2,1,0:T(8,128)S(1)} collective-permute-done((f32[3,8,256]{2,1,0:T(8,128)S(1)}, f32[3,8,256]{2,1,0:T(8,128)S(1)}, u32[]{:S(2)}, u32[]{:S(2)}) %collective-permute-start.24) | collective-permute-done | bytes 24608 | tf_op jit(solution)/shard_map/ppermute | solution.py:32
  88.1 3.5 %collective-permute-done.23 = f32[3,8,256]{2,1,0:T(8,128)S(1)} collective-permute-done((f32[3,8,256]{2,1,0:T(8,128)S(1)}, f32[3,8,256]{2,1,0:T(8,128)S(1)}, u32[]{:S(2)}, u32[]{:S(2)}) %collective-permute-start.23) | collective-permute-done | bytes 24608 | tf_op jit(solution)/shard_map/ppermute | solution.py:32
  91.6 2.3 %collective-permute-start.26 = (f32[8,256]{1,0:T(8,128)S(1)}, f32[8,256]{1,0:T(8,128)S(1)}, u32[]{:S(2)}, u32[]{:S(2)}) collective-permute-start(f32[8,256]{1,0:T(8,128)S(1)} %get-tuple-element.147), channel_id=1, source_target_pairs={{1,0},{2,1},{3,2},{0,3},{5,4},{6,5},{7,6},{4,7},{9,8},{10,9},{11,1... | collective-permute-start | bytes 24584 | tf_op jit(solution)/shard_map/ppermute | solution.py:32
  93.9 1.4 %collective-permute-done.26 = f32[8,256]{1,0:T(8,128)S(1)} collective-permute-done((f32[8,256]{1,0:T(8,128)S(1)}, f32[8,256]{1,0:T(8,128)S(1)}, u32[]{:S(2)}, u32[]{:S(2)}) %collective-permute-start.26) | collective-permute-done | bytes 8224 | tf_op jit(solution)/shard_map/ppermute | solution.py:32
  95.3 3.1 %collective-permute-done.25 = f32[8,256]{1,0:T(8,128)S(1)} collective-permute-done((f32[8,256]{1,0:T(8,128)S(1)}, f32[8,256]{1,0:T(8,128)S(1)}, u32[]{:S(2)}, u32[]{:S(2)}) %collective-permute-start.25) | collective-permute-done | bytes 8224 | tf_op jit(solution)/shard_map/ppermute | solution.py:32
  98.4 0.6 copy.13
  (40 shorter events, 0.3 us)
Async XLA Ops:
  0.7 0.7 copy-start.9
  1.4 0.7 copy-start.10
  2.7 8.0 %collective-permute-start.1 = (f32[8,128]{1,0:T(8,128)S(1)}, f32[8,128]{1,0:T(8,128)S(1)}, u32[]{:S(2)}, u32[]{:S(2)}) collective-permute-start(f32[8,128]{1,0:T(8,128)S(1)} %pack.1), channel_id=1, source_target_pairs={{1,0},{2,1},{3,2},{0,3},{5,4},{6,5},{7,6},{4,7},{9,8},{10,9},{11,1... | collective-permute-start | bytes 12296 | tf_op jit(solution)/shard_map/ppermute | solution.py:32
  6.6 4.5 %collective-permute-start = (f32[8,128]{1,0:T(8,128)S(1)}, f32[8,128]{1,0:T(8,128)S(1)}, u32[]{:S(2)}, u32[]{:S(2)}) collective-permute-start(f32[8,128]{1,0:T(8,128)S(1)} %pack.1), channel_id=1, source_target_pairs={{3,0},{0,1},{1,2},{2,3},{7,4},{4,5},{5,6},{6,7},{11,8},{8,9},{9,10... | collective-permute-start | bytes 12296 | tf_op jit(solution)/shard_map/ppermute | solution.py:32
  6.6 1.0 copy-start
  7.6 0.7 copy-start.4
  8.3 0.7 copy-start.5
  9.0 0.7 copy-start.6
  9.7 0.7 copy-start.7
  11.1 4.9 %collective-permute-start.2 = (f32[3,8,128]{2,1,0:T(8,128)S(1)}, f32[3,8,128]{2,1,0:T(8,128)S(1)}, u32[]{:S(2)}, u32[]{:S(2)}) collective-permute-start(f32[3,8,128]{2,1,0:T(8,128)S(1)} %pad_maximum_fusion.2.column_ref.cell_ref), channel_id=1, source_target_pairs={{28,0},{29,1},{30,2},{31,3},{0,4},{1,5},{2,6},{3,7},{4,8},{5,9},{6... | collective-permute-start | bytes 36872 | tf_op jit(solution)/shard_map/ppermute | solution.py:32
  11.1 4.9 %collective-permute-start.3 = (f32[3,8,128]{2,1,0:T(8,128)S(1)}, f32[3,8,128]{2,1,0:T(8,128)S(1)}, u32[]{:S(2)}, u32[]{:S(2)}) collective-permute-start(f32[3,8,128]{2,1,0:T(8,128)S(1)} %pad_maximum_fusion.2.column_ref.cell_ref), channel_id=1, source_target_pairs={{4,0},{5,1},{6,2},{7,3},{8,4},{9,5},{10,6},{11,7},{12,8},{13,9},{1... | collective-permute-start | bytes 36872 | tf_op jit(solution)/shard_map/ppermute | solution.py:32
  17.4 10.0 %copy-start.2 = (f32[128,128]{1,0:T(8,128)S(1)}, f32[128,128]{1,0:T(8,128)}, u32[]{:S(2)}) copy-start(f32[128,128]{1,0:T(8,128)} %hidden_in.1) | copy-start | bytes 196612
  17.4 10.0 %copy-start.3 = (f32[128,64]{0,1:T(8,128)S(1)}, f32[128,64]{0,1:T(8,128)}, u32[]{:S(2)}) copy-start(f32[128,64]{0,1:T(8,128)} %param.20) | copy-start | bytes 98308
  17.4 10.0 %copy-start.8 = (f32[128]{0:T(128)S(1)}, f32[128]{0:T(128)}, u32[]{:S(2)}) copy-start(f32[128]{0:T(128)} %param.19) | copy-start | bytes 1540
  17.4 5.9 %collective-permute-start.5 = (bf16[128,256]{1,0:T(8,128)(2,1)S(1)}, bf16[128,256]{1,0:T(8,128)(2,1)S(1)}, u32[]{:S(2)}, u32[]{:S(2)}) collective-permute-start(bf16[128,256]{1,0:T(8,128)(2,1)S(1)} %get-tuple-element.90), channel_id=1, source_target_pairs={{1,0},{2,1},{3,2},{0,3},{5,4},{6,5},{7,6},{4,7},{9,8},{10,9},{11,1... | collective-permute-start | bytes 196616 | tf_op jit(solution)/shard_map/ppermute | solution.py:32
  20.0 5.2 %collective-permute-start.4 = (bf16[128,256]{1,0:T(8,128)(2,1)S(1)}, bf16[128,256]{1,0:T(8,128)(2,1)S(1)}, u32[]{:S(2)}, u32[]{:S(2)}) collective-permute-start(bf16[128,256]{1,0:T(8,128)(2,1)S(1)} %get-tuple-element.90), channel_id=1, source_target_pairs={{3,0},{0,1},{1,2},{2,3},{7,4},{4,5},{5,6},{6,7},{11,8},{8,9},{9,10... | collective-permute-start | bytes 196616 | tf_op jit(solution)/shard_map/ppermute | solution.py:32
  25.2 5.5 %collective-permute-start.6 = (bf16[3,128,256]{2,1,0:T(8,128)(2,1)S(1)}, bf16[3,128,256]{2,1,0:T(8,128)(2,1)S(1)}, u32[]{:S(2)}, u32[]{:S(2)}) collective-permute-start(bf16[3,128,256]{2,1,0:T(8,128)(2,1)S(1)} %pad_maximum_fusion.column_ref), channel_id=1, source_target_pairs={{4,0},{5,1},{6,2},{7,3},{8,4},{9,5},{10,6},{11,7},{12,8},{13,9},{1... | collective-permute-start | bytes 589832 | tf_op jit(solution)/shard_map/ppermute | solution.py:32
  27.6 6.9 %collective-permute-start.7 = (bf16[3,128,256]{2,1,0:T(8,128)(2,1)S(1)}, bf16[3,128,256]{2,1,0:T(8,128)(2,1)S(1)}, u32[]{:S(2)}, u32[]{:S(2)}) collective-permute-start(bf16[3,128,256]{2,1,0:T(8,128)(2,1)S(1)} %pad_maximum_fusion.column_ref), channel_id=1, source_target_pairs={{28,0},{29,1},{30,2},{31,3},{0,4},{1,5},{2,6},{3,7},{4,8},{5,9},{6... | collective-permute-start | bytes 589832 | tf_op jit(solution)/shard_map/ppermute | solution.py:32
  36.8 6.7 %collective-permute-start.10 = (bf16[80,256]{1,0:T(8,128)(2,1)S(1)}, bf16[80,256]{1,0:T(8,128)(2,1)S(1)}, u32[]{:S(2)}, u32[]{:S(2)}) collective-permute-start(bf16[80,256]{1,0:T(8,128)(2,1)S(1)} %get-tuple-element.103), channel_id=1, source_target_pairs={{24,0},{25,1},{26,2},{27,3},{28,4},{29,5},{30,6},{31,7},{0,8},{1,9... | collective-permute-start | bytes 122888 | tf_op jit(solution)/shard_map/ppermute | solution.py:32
  36.9 6.7 %collective-permute-start.9 = (bf16[80,256]{1,0:T(8,128)(2,1)S(1)}, bf16[80,256]{1,0:T(8,128)(2,1)S(1)}, u32[]{:S(2)}, u32[]{:S(2)}) collective-permute-start(bf16[80,256]{1,0:T(8,128)(2,1)S(1)} %get-tuple-element.103), channel_id=1, source_target_pairs={{16,0},{17,1},{18,2},{19,3},{20,4},{21,5},{22,6},{23,7},{24,8},{25... | collective-permute-start | bytes 122888 | tf_op jit(solution)/shard_map/ppermute | solution.py:32
  38.0 5.5 %collective-permute-start.8 = (bf16[80,256]{1,0:T(8,128)(2,1)S(1)}, bf16[80,256]{1,0:T(8,128)(2,1)S(1)}, u32[]{:S(2)}, u32[]{:S(2)}) collective-permute-start(bf16[80,256]{1,0:T(8,128)(2,1)S(1)} %get-tuple-element.103), channel_id=1, source_target_pairs={{8,0},{9,1},{10,2},{11,3},{12,4},{13,5},{14,6},{15,7},{16,8},{17,9... | collective-permute-start | bytes 122888 | tf_op jit(solution)/shard_map/ppermute | solution.py:32
  43.6 6.3 %copy-start.1 = (s32[3,4096]{1,0:T(4,128)S(1)}, s32[3,4096]{1,0:T(4,128)}, u32[]{:S(2)}) copy-start(s32[3,4096]{1,0:T(4,128)} %vec_ref.1) | copy-start | bytes 147460
  43.6 1.8 %collective-permute-start.11 = (bf16[4,80,256]{2,1,0:T(8,128)(2,1)S(1)}, bf16[4,80,256]{2,1,0:T(8,128)(2,1)S(1)}, u32[]{:S(2)}, u32[]{:S(2)}) collective-permute-start(bf16[4,80,256]{2,1,0:T(8,128)(2,1)S(1)} %pad_maximum_fusion.1.blocks.refs_7_), channel_id=1, source_target_pairs={{4,0},{0,4},{12,8},{8,12},{20,16},{16,20},{28,24},{24,28},{5,1},{1... | collective-permute-start | bytes 491528 | tf_op jit(solution)/shard_map/ppermute | solution.py:37
  47.3 4.9 %collective-permute-start.12 = (bf16[320,128]{1,0:T(8,128)(2,1)S(1)}, bf16[320,128]{1,0:T(8,128)(2,1)S(1)}, u32[]{:S(2)}, u32[]{:S(2)}) collective-permute-start(bf16[320,128]{1,0:T(8,128)(2,1)S(1)} %get-tuple-element.113), channel_id=1, source_target_pairs={{1,0},{2,1},{3,2},{0,3},{5,4},{6,5},{7,6},{4,7},{9,8},{10,9},{11,1... | collective-permute-start | bytes 245768 | tf_op jit(solution)/shard_map/ppermute | solution.py:32
  49.2 6.3 %collective-permute-start.13 = (bf16[320,128]{1,0:T(8,128)(2,1)S(1)}, bf16[320,128]{1,0:T(8,128)(2,1)S(1)}, u32[]{:S(2)}, u32[]{:S(2)}) collective-permute-start(bf16[320,128]{1,0:T(8,128)(2,1)S(1)} %get-tuple-element.113), channel_id=1, source_target_pairs={{2,0},{3,1},{0,2},{1,3},{6,4},{7,5},{4,6},{5,7},{10,8},{11,9},{8,1... | collective-permute-start | bytes 245768 | tf_op jit(solution)/shard_map/ppermute | solution.py:32
  49.7 5.8 %collective-permute-start.14 = (bf16[320,128]{1,0:T(8,128)(2,1)S(1)}, bf16[320,128]{1,0:T(8,128)(2,1)S(1)}, u32[]{:S(2)}, u32[]{:S(2)}) collective-permute-start(bf16[320,128]{1,0:T(8,128)(2,1)S(1)} %get-tuple-element.113), channel_id=1, source_target_pairs={{3,0},{0,1},{1,2},{2,3},{7,4},{4,5},{5,6},{6,7},{11,8},{8,9},{9,10... | collective-permute-start | bytes 245768 | tf_op jit(solution)/shard_map/ppermute | solution.py:32
  57.4 1.9 %collective-permute-start.15 = (bf16[4,80,256]{2,1,0:T(8,128)(2,1)S(1)}, bf16[4,80,256]{2,1,0:T(8,128)(2,1)S(1)}, u32[]{:S(2)}, u32[]{:S(2)}) collective-permute-start(bf16[4,80,256]{2,1,0:T(8,128)(2,1)S(1)} %get-tuple-element.127), channel_id=1, source_target_pairs={{4,0},{0,4},{12,8},{8,12},{20,16},{16,20},{28,24},{24,28},{5,1},{1... | collective-permute-start | bytes 491528 | tf_op jit(solution)/shard_map/ppermute | solution.py:37
  59.4 6.1 %collective-permute-start.16 = (bf16[80,256]{1,0:T(8,128)(2,1)S(1)}, bf16[80,256]{1,0:T(8,128)(2,1)S(1)}, u32[]{:S(2)}, u32[]{:S(2)}) collective-permute-start(bf16[80,256]{1,0:T(8,128)(2,1)S(1)} %get-tuple-element.129), channel_id=1, source_target_pairs={{24,0},{25,1},{26,2},{27,3},{28,4},{29,5},{30,6},{31,7},{0,8},{1,9... | collective-permute-start | bytes 122888 | tf_op jit(solution)/shard_map/ppermute | solution.py:32
  61.1 5.9 %collective-permute-start.17 = (bf16[80,256]{1,0:T(8,128)(2,1)S(1)}, bf16[80,256]{1,0:T(8,128)(2,1)S(1)}, u32[]{:S(2)}, u32[]{:S(2)}) collective-permute-start(bf16[80,256]{1,0:T(8,128)(2,1)S(1)} %get-tuple-element.130), channel_id=1, source_target_pairs={{16,0},{17,1},{18,2},{19,3},{20,4},{21,5},{22,6},{23,7},{24,8},{25... | collective-permute-start | bytes 122888 | tf_op jit(solution)/shard_map/ppermute | solution.py:32
  62.9 4.4 %collective-permute-start.18 = (bf16[80,256]{1,0:T(8,128)(2,1)S(1)}, bf16[80,256]{1,0:T(8,128)(2,1)S(1)}, u32[]{:S(2)}, u32[]{:S(2)}) collective-permute-start(bf16[80,256]{1,0:T(8,128)(2,1)S(1)} %get-tuple-element.131), channel_id=1, source_target_pairs={{8,0},{9,1},{10,2},{11,3},{12,4},{13,5},{14,6},{15,7},{16,8},{17,9... | collective-permute-start | bytes 122888 | tf_op jit(solution)/shard_map/ppermute | solution.py:32
  70.0 7.7 %collective-permute-start.19 = (bf16[3,128,256]{2,1,0:T(8,128)(2,1)S(1)}, bf16[3,128,256]{2,1,0:T(8,128)(2,1)S(1)}, u32[]{:S(2)}, u32[]{:S(2)}) collective-permute-start(bf16[3,128,256]{2,1,0:T(8,128)(2,1)S(1)} %get-tuple-element.136), channel_id=1, source_target_pairs={{28,0},{29,1},{30,2},{31,3},{0,4},{1,5},{2,6},{3,7},{4,8},{5,9},{6... | collective-permute-start | bytes 589832 | tf_op jit(solution)/shard_map/ppermute | solution.py:32
  70.0 7.7 %collective-permute-start.20 = (bf16[3,128,256]{2,1,0:T(8,128)(2,1)S(1)}, bf16[3,128,256]{2,1,0:T(8,128)(2,1)S(1)}, u32[]{:S(2)}, u32[]{:S(2)}) collective-permute-start(bf16[3,128,256]{2,1,0:T(8,128)(2,1)S(1)} %get-tuple-element.137), channel_id=1, source_target_pairs={{4,0},{5,1},{6,2},{7,3},{8,4},{9,5},{10,6},{11,7},{12,8},{13,9},{1... | collective-permute-start | bytes 589832 | tf_op jit(solution)/shard_map/ppermute | solution.py:32
  77.7 5.9 %collective-permute-start.21 = (bf16[128,256]{1,0:T(8,128)(2,1)S(1)}, bf16[128,256]{1,0:T(8,128)(2,1)S(1)}, u32[]{:S(2)}, u32[]{:S(2)}) collective-permute-start(bf16[128,256]{1,0:T(8,128)(2,1)S(1)} %get-tuple-element.145), channel_id=1, source_target_pairs={{3,0},{0,1},{1,2},{2,3},{7,4},{4,5},{5,6},{6,7},{11,8},{8,9},{9,10... | collective-permute-start | bytes 196616 | tf_op jit(solution)/shard_map/ppermute | solution.py:32
  78.1 6.3 %collective-permute-start.22 = (bf16[128,256]{1,0:T(8,128)(2,1)S(1)}, bf16[128,256]{1,0:T(8,128)(2,1)S(1)}, u32[]{:S(2)}, u32[]{:S(2)}) collective-permute-start(bf16[128,256]{1,0:T(8,128)(2,1)S(1)} %get-tuple-element.144), channel_id=1, source_target_pairs={{1,0},{2,1},{3,2},{0,3},{5,4},{6,5},{7,6},{4,7},{9,8},{10,9},{11,1... | collective-permute-start | bytes 196616 | tf_op jit(solution)/shard_map/ppermute | solution.py:32
  85.9 2.1 %collective-permute-start.24 = (f32[3,8,256]{2,1,0:T(8,128)S(1)}, f32[3,8,256]{2,1,0:T(8,128)S(1)}, u32[]{:S(2)}, u32[]{:S(2)}) collective-permute-start(f32[3,8,256]{2,1,0:T(8,128)S(1)} %get-tuple-element.140), channel_id=1, source_target_pairs={{4,0},{5,1},{6,2},{7,3},{8,4},{9,5},{10,6},{11,7},{12,8},{13,9},{1... | collective-permute-start | bytes 73736 | tf_op jit(solution)/shard_map/ppermute | solution.py:32
  86.5 5.0 %collective-permute-start.23 = (f32[3,8,256]{2,1,0:T(8,128)S(1)}, f32[3,8,256]{2,1,0:T(8,128)S(1)}, u32[]{:S(2)}, u32[]{:S(2)}) collective-permute-start(f32[3,8,256]{2,1,0:T(8,128)S(1)} %get-tuple-element.139), channel_id=1, source_target_pairs={{28,0},{29,1},{30,2},{31,3},{0,4},{1,5},{2,6},{3,7},{4,8},{5,9},{6... | collective-permute-start | bytes 73736 | tf_op jit(solution)/shard_map/ppermute | solution.py:32
  91.6 3.7 %collective-permute-start.26 = (f32[8,256]{1,0:T(8,128)S(1)}, f32[8,256]{1,0:T(8,128)S(1)}, u32[]{:S(2)}, u32[]{:S(2)}) collective-permute-start(f32[8,256]{1,0:T(8,128)S(1)} %get-tuple-element.147), channel_id=1, source_target_pairs={{1,0},{2,1},{3,2},{0,3},{5,4},{6,5},{7,6},{4,7},{9,8},{10,9},{11,1... | collective-permute-start | bytes 24584 | tf_op jit(solution)/shard_map/ppermute | solution.py:32
  93.9 4.5 %collective-permute-start.25 = (f32[8,256]{1,0:T(8,128)S(1)}, f32[8,256]{1,0:T(8,128)S(1)}, u32[]{:S(2)}, u32[]{:S(2)}) collective-permute-start(f32[8,256]{1,0:T(8,128)S(1)} %get-tuple-element.148), channel_id=1, source_target_pairs={{3,0},{0,1},{1,2},{2,3},{7,4},{4,5},{5,6},{6,7},{11,8},{8,9},{9,10... | collective-permute-start | bytes 24584 | tf_op jit(solution)/shard_map/ppermute | solution.py:32

commit v8 on v7

--- a/solution.py
+++ b/solution.py
@@ -18,29 +18,23 @@
 WAVE_REACH = 8
 F32 = jnp.float32
 BF16 = jnp.bfloat16
-OFFSETS = [(a, b) for a in (-1, 0, 1) for b in (-1, 0, 1)]
 CENTRE = 4
 
 
-def shifted(block, along_x, along_y):
-    count_x, count_y = lax.axis_size("gx"), lax.axis_size("gy")
-    route = []
-    for i in range(count_x):
-        for j in range(count_y):
-            source = ((i + along_x) % count_x) * count_y + (j + along_y) % count_y
-            route.append((source, i * count_y + j))
-    return lax.ppermute(block, ("gx", "gy"), route)
-
-
-def swapped(block):
-    count = lax.axis_size("gx")
-    return lax.ppermute(block, "gx", [(i ^ 1, i) for i in range(count)])
+def paired(block, axis, mask):
+    return lax.ppermute(block, axis, [(i ^ mask, i) for i in range(lax.axis_size(axis))])
+
+
+def beyond(block, axis):
+    count = lax.axis_size(axis)
+    route = [((i + (1 if i % 2 else -1)) % count, i) for i in range(count)]
+    return lax.ppermute(block, axis, route)
 
 
 def around(block, beside):
-    column = jnp.stack([shifted(block, 0, -1), block, shifted(block, 0, 1)])
+    column = jnp.stack([paired(block, "gy", 1), block, beyond(block, "gy")])
     column, beside = lax.optimization_barrier((column, beside))
-    return [shifted(column, -1, 0), column, shifted(column, 1, 0)], beside
+    return [paired(column, "gx", 1), column, beyond(column, "gx")], beside
 
 
 def whole(space=pltpu.VMEM):
@@ -185,6 +179,15 @@
     low_ref[at] = low
 
 
+def slot_order(ids, place_ref, atoms):
+    cell = ids // atoms
+    a = (cell * 11) >> 5
+    b = cell - 3 * a
+    a = jnp.where((place_ref[0] & 1) == 0, 2 - a, a)
+    b = jnp.where((place_ref[1] & 1) == 0, 2 - b, b)
+    return ids + (3 * a + b - cell) * atoms
+
+
 def fetch(sources, targets, sems):
     copies = [
         pltpu.make_async_copy(source, target, sems.at[i])
@@ -196,7 +199,7 @@
         copy.wait()
 
 
-def prep_first_kernel(norm, ids_in, count_in, embed_in, radial_in, mixing_in, id_ref, count_ref,
+def prep_first_kernel(norm, place_ref, ids_in, count_in, embed_in, radial_in, mixing_in, id_ref, count_ref,
                       embed_out, kind_left, left_out, back_out, kind_high, kind_low, mix_high,
                       mix_low, turn_high, turn_low, embed_ref, radial_ref, mixing_ref, sems):
     fetch(
@@ -204,6 +207,7 @@
         [id_ref, count_ref, embed_ref, radial_ref, mixing_ref],
         sems,
     )
+    id_ref[...] = slot_order(id_ref[...], place_ref, count_ref.shape[2])
     embed = embed_ref[...]
     kinds = embed.shape[0]
     for path in range(2):
@@ -254,12 +258,12 @@
     return jnp.concatenate([block[4 * s : 4 * s + 4] for s in range(parts)], axis=1)
 
 
-def first_kernel(slots, ids_ref, count_ref, embed_ref, kind_left, mix_high, mix_low, before_ref,
-                 column_ref, after_ref, low_ref, basis_ref, slope_ref, unit_ref, sums_ref,
+def first_kernel(slots, place_ref, ids_ref, count_ref, embed_ref, kind_left, mix_high, mix_low,
+                 pair_ref, column_ref, beyond_ref, low_ref, basis_ref, slope_ref, unit_ref, sums_ref,
                  gate_ref):
     atoms = low_ref.shape[1]
     ids = ids_ref[...]
-    frame = [before_ref, column_ref, after_ref]
+    frame = [pair_ref, column_ref, beyond_ref]
     own = unfold_block(column_ref[1], atoms)
     own = jnp.concatenate([own, jnp.zeros_like(own)], axis=0)
     per_cell = atoms // 128
@@ -267,10 +271,13 @@
     upper = places >> 2
     kind_of_row = places & 3
     rows = []
-    for a, b in OFFSETS:
-        move = jnp.where(kind_of_row == 0, a * cell_width, 0.0)
-        move = move + jnp.where(kind_of_row == 1, b * cell_width, 0.0)
-        rows.append(frame[a + 1][b + 1] + move)
+    to_x = jnp.where(kind_of_row == 0, cell_width, 0.0)
+    to_x = jnp.where((place_ref[0] & 1) == 0, to_x, -to_x)
+    to_y = jnp.where(kind_of_row == 1, cell_width, 0.0)
+    to_y = jnp.where((place_ref[1] & 1) == 0, to_y, -to_y)
+    for a in range(3):
+        for b in range(3):
+            rows.append(frame[a][b] + ((1 - a) * to_x + (1 - b) * to_y))
     pieces = []
     for start in range(0, ids.shape[1], 128):
         part = jnp.broadcast_to(ids[:, start : start + 128], places.shape)
@@ -342,24 +349,24 @@
         near_ref[:, lanes] = dot(source, hot_ref[3 * atoms : 6 * atoms, lanes])
 
 
-def second_side_kernel(slots, hot_ref, near_ref, after_ref, out_ref):
-    atoms = after_ref.shape[2]
-    source = jnp.concatenate([after_ref[b] for b in range(3)], axis=1)
+def second_side_kernel(slots, hot_ref, near_ref, pair_ref, out_ref):
+    atoms = pair_ref.shape[2]
+    source = jnp.concatenate([pair_ref[b] for b in range(3)], axis=1)
     for n in range(slots):
         lanes = slice(n * atoms, (n + 1) * atoms)
-        out_ref[:, lanes] = near_ref[:, lanes] + dot(source, hot_ref[6 * atoms :, lanes])
+        out_ref[:, lanes] = near_ref[:, lanes] + dot(source, hot_ref[: 3 * atoms, lanes])
 
 
 def second_kernel(slots, hot_ref, weight_ref, near_ref, mix_high, mix_low, hidden_high, hidden_low,
-                  turn_high, turn_low, out_ref, charge_ref, cell_ref, column_ref, before_ref,
+                  turn_high, turn_low, out_ref, charge_ref, cell_ref, column_ref, beyond_ref,
                   feature_ref, sums_ref, gate_ref, packed_ref, full_charge_ref, energy_ref,
                   slope_ref):
     atoms = column_ref.shape[2]
-    source = jnp.concatenate([before_ref[b] for b in range(3)], axis=1)
+    source = jnp.concatenate([beyond_ref[b] for b in range(3)], axis=1)
     sums = [None] * 4
     for n in range(slots):
         lanes = slice(n * atoms, (n + 1) * atoms)
-        feature = near_ref[:, lanes] + dot(source, hot_ref[: 3 * atoms, lanes])
+        feature = near_ref[:, lanes] + dot(source, hot_ref[6 * atoms :, lanes])
         feature_ref[:, lanes] = feature.astype(BF16)
         for part in range(4):
             term = weight_ref[part, :, lanes] * feature
@@ -402,7 +409,7 @@
 def second_back_kernel(slots, scale, count, hot_ref, weight_ref, turn_high, turn_low, charge_ref,
                        sums_ref, gate_ref, full_charge_ref, energy_ref, slope_ref, *refs):
     folds, refs = refs[:count], refs[count:]
-    site_ref, long_ref, cotangent_ref, grad_ref, term_ref, before_ref, after_ref = refs
+    site_ref, long_ref, cotangent_ref, grad_ref, term_ref, beyond_ref = refs
     atoms = gate_ref.shape[1]
     total = folds[0][...].astype(F32)
     for part in folds[1:]:
@@ -432,17 +439,17 @@
         for part in range(1, 4):
             term = term + weight_ref[part, :, lanes] * grads[part]
         term_ref[:, lanes] = term.astype(BF16)
-    for side, out_ref in ((0, before_ref), (2, after_ref)):
-        for b in range(3):
-            start = (3 * side + b) * atoms
-            out_ref[b] = dot(term_ref[...], hot_ref[:, start : start + atoms]).astype(BF16)
-
-
-def second_middle_kernel(hot_ref, term_ref, cotangent_ref, middle_ref):
+    for b in range(3):
+        start = (6 + b) * atoms
+        beyond_ref[b] = dot(term_ref[...], hot_ref[:, start : start + atoms]).astype(BF16)
+
+
+def second_middle_kernel(hot_ref, term_ref, cotangent_ref, pair_ref, middle_ref):
     atoms = cotangent_ref.shape[1]
     for b in range(3):
         grad = dot(term_ref[...], hot_ref[:, (3 + b) * atoms : (4 + b) * atoms])
         middle_ref[b] = grad + cotangent_ref[...] if b == 1 else grad
+        pair_ref[b] = dot(term_ref[...], hot_ref[:, b * atoms : (b + 1) * atoms]).astype(BF16)
 
 
 def second_edge_kernel(slots, back_ref, feature_ref, grad_ref, edge_ref):
@@ -614,7 +621,7 @@
         atoms = charge.shape[1]
         pieces = block[wide:].astype(F32)
         place = pieces[0:3] + (pieces[3:6] + pieces[6:9])
-        row = lax.rem(first + 2 * d, grid_x).astype(F32) * (1.0 / grid_x)
+        row = (first ^ (2 * d)).astype(F32) * (1.0 / grid_x)
         x = place[0:1] * (1.0 / (grid_x * cell_width)) + row
         y = place[1:2] * (1.0 / (grid_y * cell_width)) + col
         sa, ca = sin_cos(kx * x + ky * y)
@@ -794,13 +801,14 @@
         + low_pair(2, kind_rows, features)
         + low_pair(2, features, 2 * features)
         + low_pair(2, 2 * features, features),
-        [ids, counts, species_embed, radial, mixing],
+        [place, ids, counts, species_embed, radial, mixing],
         scratch=[
             pltpu.VMEM(species_embed.shape, F32),
             pltpu.VMEM(radial.shape, F32),
             pltpu.VMEM(mixing.shape, F32),
             dma((5,)),
         ],
+        smem=1,
         hbm=5,
         name="prep_first",
     )
@@ -823,13 +831,6 @@
         hbm=3,
         name="prep_second",
     )
-    (weight,) = run(
-        functools.partial(green_weights, share, padded, grid),
-        [shape(16 * share + padded, 128)],
-        [place, wavevectors],
-        smem=1,
-        name="green",
-    )
     low, basis, slope, unit, sums_one, gate_one = run(
         functools.partial(first_kernel, slots),
         [
@@ -840,7 +841,8 @@
             shape(3, features, atoms),
             shape(features, atoms),
         ],
-        [ids, counts, embed, kind_left, mix_high, mix_low] + cells,
+        [place, ids, counts, embed, kind_left, mix_high, mix_low] + cells,
+        smem=1,
         name="first",
     )
     hidden, hot = around(low, hot)
@@ -854,7 +856,7 @@
     (near,) = run(
         functools.partial(second_side_kernel, slots),
         [shape(features, edges)],
-        [hot, near, hidden[2]],
+        [hot, near, hidden[0]],
         flops=1_000_000_000,
         name="second_side",
     )
@@ -871,20 +873,20 @@
             shape(features, atoms),
         ],
         [hot, edge_weights, near, mix_high, mix_low, hidden_high, hidden_low, hidden_turn_high,
-         hidden_turn_low, read_out, charge_pair, cells[1], hidden[1], hidden[0]],
+         hidden_turn_low, read_out, charge_pair, cells[1], hidden[1], hidden[2]],
         name="second",
     )
     half = grid_x // 2
-    near_charges = jnp.stack([packed] + [shifted(packed, 2 * d, 0) for d in range(1, half)])
-    (hot_back,) = run(
-        hot_back_kernel,
-        [shape(edges, 9 * atoms, dtype=BF16)],
-        [ids],
-        flops=2_000_000_000,
-        name="hot_back",
-    )
-    near_charges, hot_back = lax.optimization_barrier((near_charges, hot_back))
-    far_charges = swapped(near_charges)
+    near_charges = jnp.stack([packed] + [paired(packed, "gx", 2 * d) for d in range(1, half)])
+    (weight,) = run(
+        functools.partial(green_weights, share, padded, grid),
+        [shape(16 * share + padded, 128)],
+        [place, wavevectors],
+        smem=1,
+        name="green",
+    )
+    near_charges, weight = lax.optimization_barrier((near_charges, weight))
+    far_charges = paired(near_charges, "gx", 1)
     span = half * atoms
     rows = 32 * share + 2 * padded
     phase_shapes = [
@@ -914,7 +916,15 @@
         smem=1,
         name="structure_far",
     )
-    parts = [own_part] + [shifted(part, 0, d) for d in range(1, grid_y)]
+    parts = [own_part] + [paired(part, "gy", d) for d in range(1, grid_y)]
+    (hot_back,) = run(
+        hot_back_kernel,
+        [shape(edges, 9 * atoms, dtype=BF16)],
+        [ids],
+        flops=2_000_000_000,
+        name="hot_back",
+    )
+    parts, hot_back = lax.optimization_barrier((parts, hot_back))
     far_folds, wave_rows = run(
         functools.partial(fold_kernel, share, padded, grid, lat_width, 1),
         [shape(half, block_rows, atoms, dtype=BF16), shape(rows, lat_width)],
@@ -922,7 +932,7 @@
         smem=1,
         name="fold_far",
     )
-    far_folds = swapped(far_folds)
+    far_folds = paired(far_folds, "gx", 1)
     (near_folds,) = run(
         functools.partial(fold_kernel, share, padded, grid, lat_width, 0),
         [shape(half, block_rows, atoms)],
@@ -937,9 +947,9 @@
         [near_folds, far_folds],
         name="fold_join",
     )
-    folds = [folds[0]] + [shifted(folds[d], -2 * d, 0) for d in range(1, half)]
-
-    site, long, cotangent, grads, term, before, after = run(
+    folds = [folds[0]] + [paired(folds[d], "gx", 2 * d) for d in range(1, half)]
+
+    site, long, cotangent, grads, term, to_beyond = run(
         functools.partial(second_back_kernel, slots, scale, half),
         [
             shape(1, 1, atoms),
@@ -948,25 +958,25 @@
             shape(4, features, atoms),
             shape(features, edges, dtype=BF16),
             shape(3, features, atoms, dtype=BF16),
-            shape(3, features, atoms, dtype=BF16),
         ],
-        [hot_back, edge_weights, turn_high, turn_low, charge_pair, sums_two, gate_two, charge, energy,
-         energy_slope] + folds,
+        [hot_back, edge_weights, turn_high, turn_low, charge_pair, sums_two, gate_two, charge,
+         energy, energy_slope] + folds,
         name="second_back",
     )
-    from_x = [shifted(after, -1, 0), shifted(before, 1, 0)]
-    (middle,) = run(
+    from_beyond = beyond(to_beyond, "gx")
+    to_pair, middle = run(
         second_middle_kernel,
-        [shape(3, features, atoms)],
+        [shape(3, features, atoms, dtype=BF16), shape(3, features, atoms)],
         [hot_back, term, cotangent],
         flops=1_000_000_000,
         name="second_middle",
     )
+    from_x = [paired(to_pair, "gx", 1), from_beyond]
     sides = [
         (middle[b] + from_x[0][b].astype(F32) + from_x[1][b].astype(F32)).astype(BF16)
         for b in (0, 2)
     ]
-    from_y = [shifted(sides[1], 0, -1), shifted(sides[0], 0, 1)]
+    from_y = [paired(sides[0], "gy", 1), beyond(sides[1], "gy")]
     (edge,) = run(
         functools.partial(second_edge_kernel, slots),
         [shape(32, edges)],
@@ -974,15 +984,15 @@
         flops=1_000_000_000,
         name="second_edge",
     )
-    before, middle, after = run(
+    to_pair, middle, to_beyond = run(
         functools.partial(first_back_kernel, slots),
         [shape(3, 8, atoms)] * 3,
         [ids, basis, slope, unit, kind_high, kind_low, turn_high, turn_low, sums_one, gate_one, edge,
          long, middle] + from_x + from_y,
         name="first_back",
     )
-    total = middle + shifted(after, -1, 0) + shifted(before, 1, 0)
-    total = total[1] + shifted(total[2], 0, -1) + shifted(total[0], 0, 1)
+    total = middle + paired(to_pair, "gx", 1) + beyond(to_beyond, "gx")
+    total = total[1] + paired(total[0], "gy", 1) + beyond(total[2], "gy")
     forces = -total[None, :3, None, :]
     return (forces.transpose(0, 2, 1, 3), site)
 

time: 99.4 us -> 98.5 us (level)
  waiting for transfers between devices: 30.8 us -> 29 us
  Pallas kernels: 28.1 us -> 29.8 us
    ppermute x27, waiting for transfers between devices: 30.8 us -> 29 us  [the longest x8 20.2 us: beyond(): return lax.ppermute(block, axis, route)]
    pallas_call x19, Pallas kernels: 28.1 us -> 29.8 us  [run(): pl.pallas_call(kernel, out_shape=outs, in_specs=specs, out_specs=[whole()...]
  transfers between devices with their start and end apart: 27 -> 27, of which waited for: 17 -> 15; matrix products, arithmetic and copies ran while one was open for 0% -> 0% of each run, Pallas kernels for 16% -> 16%
where the time goes in v8:
time: 98.5 us; the launch traced here: 98.1 us
  starting transfers between devices  32.4 us (33%)
  Pallas kernels  29.8 us (30%)
  waiting for transfers between devices  29 us (29%)
  local copies, waits for them, and re-layouts  5.71 us (6%)
    pallas_call x19, Pallas kernels, run(): pl.pallas_call(kernel, out_shape=outs, in_specs=specs, out_specs=[whole()...  29.8 us
    ppermute x8, waiting for transfers between devices, beyond(): return lax.ppermute(block, axis, route)  20.2 us
    ppermute x8, starting transfers between devices, beyond(): return lax.ppermute(block, axis, route)  16.9 us
    ppermute x19, starting transfers between devices, paired(): lax.ppermute(block, axis, [(i ^ mask, i) for i in range(lax.axis_size(axi...  15.4 us
    ppermute x19, waiting for transfers between devices, paired(): lax.ppermute(block, axis, [(i ^ mask, i) for i in range(lax.axis_size(axi...  8.81 us
    unnamed x23, local copies, waits for them, and re-layouts  5.71 us
  transfers between devices with their start and end apart: 27, of which 15 were waited for; matrix products, arithmetic and copies ran while one was open for 0% of the time, Pallas kernels for 16%

profile of v8, /device:TPU:0, one launch (start us, length us, event | category | flops | bytes accessed | tf_op | source)
XLA Modules:
  0.0 98.1 jit_solution(3767152780914071847)
XLA Ops:
  0.6 0.1 pad_add_fusion.place_ref
  0.7 0.7 copy-done.9
  1.4 0.7 copy-done.10
  2.1 0.6 pack.1
  2.7 4.0 %collective-permute-start.1 = (f32[8,128]{1,0:T(8,128)S(1)}, f32[8,128]{1,0:T(8,128)S(1)}, u32[]{:S(2)}, u32[]{:S(2)}) collective-permute-start(f32[8,128]{1,0:T(8,128)S(1)} %pack.1), channel_id=1, source_target_pairs={{3,0},{2,1},{1,2},{0,3},{7,4},{6,5},{5,6},{4,7},{11,8},{10,9},{9,1... | collective-permute-start | bytes 12296 | tf_op jit(solution)/shard_map/ppermute | solution.py:31
  6.6 0.5 collective-permute-start
  7.1 0.9 copy-done
  8.1 0.7 copy-done.4
  8.8 0.7 copy-done.5
  9.5 0.7 copy-done.6
  10.2 0.7 copy-done.7
  10.9 0.9 prep_first.1
  11.8 0.1 collective-permute-start.2
  11.9 3.7 %collective-permute-start.3 = (f32[3,8,128]{2,1,0:T(8,128)S(1)}, f32[3,8,128]{2,1,0:T(8,128)S(1)}, u32[]{:S(2)}, u32[]{:S(2)}) collective-permute-start(f32[3,8,128]{2,1,0:T(8,128)S(1)} %pad_maximum_fusion.2.column_ref.cell_ref), channel_id=1, source_target_pairs={{28,0},{8,4},{4,8},{16,12},{12,16},{24,20},{20,24},{0,28},{29,1},{... | collective-permute-start | bytes 36872 | tf_op jit(solution)/shard_map/ppermute | solution.py:31
  15.6 1.4 %collective-permute-done.3.beyond_ref = f32[3,8,128]{2,1,0:T(8,128)S(1)} collective-permute-done((f32[3,8,128]{2,1,0:T(8,128)S(1)}, f32[3,8,128]{2,1,0:T(8,128)S(1)}, u32[]{:S(2)}, u32[]{:S(2)}) %collective-permute-start.3) | collective-permute-done | bytes 12320 | tf_op jit(solution)/shard_map/ppermute | solution.py:31
  17.0 1.9 %first.1 = (bf16[128,256]{1,0:T(8,128)(2,1)S(1)}, f32[8,3072]{1,0:T(8,128)S(1)}, f32[8,3072]{1,0:T(8,128)S(1)}, f32[8,3072]{1,0:T(8,128)S(1)}, f32[3,128,256]{2,1,0:T(8,128)S(1)}, /*index=5*/f32[128,256]{1,0:T(8,128)S(1)}) custom-call(s32[2]{0:T(128)S(1)} %pad_add_fusion.place_ref, s32[1,3072]{1,0:T(1,128)S(1)} %get-tuple-element.79.ids_ref, ...), custom_call_target="tpu_custom_call" | custom-call | flops 10000000 | bytes 1000000 | tf_op jit(solution)/shard_map/first/pallas_call | solution.py:48
  18.9 1.5 %collective-permute-start.5 = (bf16[128,256]{1,0:T(8,128)(2,1)S(1)}, bf16[128,256]{1,0:T(8,128)(2,1)S(1)}, u32[]{:S(2)}, u32[]{:S(2)}) collective-permute-start(bf16[128,256]{1,0:T(8,128)(2,1)S(1)} %get-tuple-element.96), channel_id=1, source_target_pairs={{3,0},{2,1},{1,2},{0,3},{7,4},{6,5},{5,6},{4,7},{11,8},{10,9},{9,1... | collective-permute-start | bytes 196616 | tf_op jit(solution)/shard_map/ppermute | solution.py:31
  20.4 0.5 collective-permute-start.4
  20.9 3.2 %hot.1.hot_ref = bf16[2304,3072]{1,0:T(8,128)(2,1)S(1)} custom-call(s32[1,3072]{1,0:T(1,128)S(1)} %get-tuple-element.79.ids_ref), custom_call_target="tpu_custom_call" | custom-call | flops 2000000000 | bytes 1000000 | tf_op jit(solution)/shard_map/hot/pallas_call | solution.py:48
  24.2 0.5 collective-permute-done.4
  24.7 0.1 collective-permute-start.6
  24.8 0.4 prep_second.1
  25.3 2.6 %collective-permute-start.7 = (bf16[3,128,256]{2,1,0:T(8,128)(2,1)S(1)}, bf16[3,128,256]{2,1,0:T(8,128)(2,1)S(1)}, u32[]{:S(2)}, u32[]{:S(2)}) collective-permute-start(bf16[3,128,256]{2,1,0:T(8,128)(2,1)S(1)} %pad_maximum_fusion.column_ref), channel_id=1, source_target_pairs={{28,0},{8,4},{4,8},{16,12},{12,16},{24,20},{20,24},{0,28},{29,1},{... | collective-permute-start | bytes 589832 | tf_op jit(solution)/shard_map/ppermute | solution.py:31
  27.8 1.6 %second_near.1 = (f32[4,128,3072]{2,1,0:T(8,128)S(1)}, f32[128,3072]{1,0:T(8,128)S(1)}) custom-call(f32[8,3072]{1,0:T(8,128)S(1)} %get-tuple-element.86.basis_ref, f32[8,3072]{1,0:T(8,128)S(1)} %get-tuple-element.88.unit_ref, bf16[2,128,32]{2,1,0:T(8,128)(2,1)S(1)} %get-tuple-element.98.left_ref, bf16[2304,3072]{1,0:T(8,128)(2,1)S(1)} %hot.1.hot_ref, ...), custom_call_target="tpu_custom_call" | custom-call | flops 2000000000 | bytes 1000000 | tf_op jit(solution)/shard_map/second_near/pallas_call | solution.py:48
  29.4 0.8 second_side.1.near_ref
  30.3 3.6 %collective-permute-done.7.beyond_ref = bf16[3,128,256]{2,1,0:T(8,128)(2,1)S(1)} collective-permute-done((bf16[3,128,256]{2,1,0:T(8,128)(2,1)S(1)}, bf16[3,128,256]{2,1,0:T(8,128)(2,1)S(1)}, u32[]{:S(2)}, u32[]{:S(2)}) %collective-permute-start.7) | collective-permute-done | bytes 196640 | tf_op jit(solution)/shard_map/ppermute | solution.py:31
  33.9 2.2 %second.1 = (bf16[128,3072]{1,0:T(8,128)(2,1)S(1)}, f32[3,128,256]{2,1,0:T(8,128)S(1)}, f32[128,256]{1,0:T(8,128)S(1)}, bf16[80,256]{1,0:T(8,128)(2,1)S(1)}, f32...) custom-call(bf16[2304,3072]{1,0:T(8,128)(2,1)S(1)} %hot.1.hot_ref, ...), custom_call_target="tpu_custom_call" | custom-call | flops 10000000 | bytes 1000000 | tf_op jit(solution)/shard_map/second/pallas_call | solution.py:48
  36.2 0.1 collective-permute-start.9
  36.3 4.3 %collective-permute-start.8 = (bf16[80,256]{1,0:T(8,128)(2,1)S(1)}, bf16[80,256]{1,0:T(8,128)(2,1)S(1)}, u32[]{:S(2)}, u32[]{:S(2)}) collective-permute-start(bf16[80,256]{1,0:T(8,128)(2,1)S(1)} %get-tuple-element.109), channel_id=1, source_target_pairs={{8,0},{12,4},{0,8},{4,12},{24,16},{28,20},{16,24},{20,28},{9,1},{1... | collective-permute-start | bytes 122888 | tf_op jit(solution)/shard_map/ppermute | solution.py:25
  40.6 1.3 %green.1.refs_0_ = f32[320,128]{1,0:T(8,128)S(1)} custom-call(s32[2]{0:T(128)S(1)} %pad_add_fusion.place_ref, s32[3,4096]{1,0:T(4,128)S(1)} %copy-done.1), custom_call_target="tpu_custom_call" | custom-call | flops 10000000 | bytes 1000000 | tf_op jit(solution)/shard_map/green/pallas_call | solution.py:48
  42.0 0.2 collective-permute-done.10
  42.2 0.4 collective-permute-done.8
  42.7 1.7 %structure_near.1 = (f32[32,1024]{1,0:T(8,128)S(1)}, f32[32,1024]{1,0:T(8,128)S(1)}, f32[8,1024]{1,0:T(8,128)S(1)}, f32[8,1024]{1,0:T(8,128)S(1)}, bf16[640,1024...) custom-call(s32[2]{0:T(128)S(1)} %pad_add_fusion.place_ref, ...), custom_call_target="tpu_custom_call" | custom-call | flops 1000000000 | bytes 1000000 | tf_op jit(solution)/shard_map/structure_near/pallas_call | solution.py:48
  44.5 1.8 %structure_far.1 = (f32[32,1024]{1,0:T(8,128)S(1)}, f32[32,1024]{1,0:T(8,128)S(1)}, f32[8,1024]{1,0:T(8,128)S(1)}, f32[8,1024]{1,0:T(8,128)S(1)}, bf16[640,1024]...) custom-call(s32[2]{0:T(128)S(1)} %pad_add_fusion.place_ref, ...), custom_call_target="tpu_custom_call" | custom-call | flops 10000000 | bytes 1000000 | tf_op jit(solution)/shard_map/structure_far/pallas_call | solution.py:48
  46.3 1.4 %collective-permute-start.12 = (bf16[320,128]{1,0:T(8,128)(2,1)S(1)}, bf16[320,128]{1,0:T(8,128)(2,1)S(1)}, u32[]{:S(2)}, u32[]{:S(2)}) collective-permute-start(bf16[320,128]{1,0:T(8,128)(2,1)S(1)} %get-tuple-element.113), channel_id=1, source_target_pairs={{1,0},{0,1},{3,2},{2,3},{5,4},{4,5},{7,6},{6,7},{9,8},{8,9},{11,10... | collective-permute-start | bytes 245768 | tf_op jit(solution)/shard_map/ppermute | solution.py:25
  47.7 1.5 %collective-permute-start.13 = (bf16[320,128]{1,0:T(8,128)(2,1)S(1)}, bf16[320,128]{1,0:T(8,128)(2,1)S(1)}, u32[]{:S(2)}, u32[]{:S(2)}) collective-permute-start(bf16[320,128]{1,0:T(8,128)(2,1)S(1)} %get-tuple-element.113), channel_id=1, source_target_pairs={{2,0},{3,1},{0,2},{1,3},{6,4},{7,5},{4,6},{5,7},{10,8},{11,9},{8,1... | collective-permute-start | bytes 245768 | tf_op jit(solution)/shard_map/ppermute | solution.py:25
  49.2 0.6 collective-permute-start.14
  49.8 2.8 %hot_back.1.hot_ref = bf16[3072,2304]{1,0:T(8,128)(2,1)S(1)} custom-call(s32[1,3072]{1,0:T(1,128)S(1)} %get-tuple-element.79.ids_ref), custom_call_target="tpu_custom_call" | custom-call | flops 2000000000 | bytes 1000000 | tf_op jit(solution)/shard_map/hot_back/pallas_call | solution.py:48
  52.7 0.4 collective-permute-done.13.refs_3_
  53.1 1.5 %collective-permute-done.14.refs_4_ = bf16[320,128]{1,0:T(8,128)(2,1)S(1)} collective-permute-done((bf16[320,128]{1,0:T(8,128)(2,1)S(1)}, bf16[320,128]{1,0:T(8,128)(2,1)S(1)}, u32[]{:S(2)}, u32[]{:S(2)}) %collective-permute-start.14) | collective-permute-done | bytes 81952 | tf_op jit(solution)/shard_map/ppermute | solution.py:25
  54.5 1.9 %fold_far.1 = (bf16[4,80,256]{2,1,0:T(8,128)(2,1)S(1)}, f32[640,64]{1,0:T(8,128)S(1)}) custom-call(s32[2]{0:T(128)S(1)} %pad_add_fusion.place_ref, f32[320,128]{1,0:T(8,128)S(1)} %green.1.refs_0_, f32[320,128]{1,0:T(8,128)S(1)} %get-tuple-element.121.refs_1_, bf16[320,128]{1,0:T(8,128)(2,1)S(1)} %collective-permute-done.12.refs_2_, ...), custom_call_target="tpu_custom_call" | custom-call | flops 10000000 | bytes 1000000 | tf_op jit(solution)/shard_map/fold_far/pallas_call | solution.py:48
  56.4 0.1 collective-permute-start.15
  56.5 2.0 %fold_near.1.near_ref = f32[4,80,256]{2,1,0:T(8,128)S(1)} custom-call(s32[2]{0:T(128)S(1)} %pad_add_fusion.place_ref, f32[640,64]{1,0:T(8,128)S(1)} %get-tuple-element.131.refs_0_, f32[32,1024]{1,0:T(8,128)S(1)} %get-tuple-element.132.refs_1_, f32[32,1024]{1,0:T(8,128)S(1)} %get-tuple-element.133.refs_2_, f32[8,1024]{1,0:T(8,128)S(1)} %get-tuple-element.134.refs_3_, ...), custom_call_target="tpu_custom_call" | custom-call | flops 1000000000 | bytes 1000000 | tf_op jit(solution)/shard_map/fold_near/pallas_call | solution.py:48
  58.6 2.1 %collective-permute-start.16 = (bf16[80,256]{1,0:T(8,128)(2,1)S(1)}, bf16[80,256]{1,0:T(8,128)(2,1)S(1)}, u32[]{:S(2)}, u32[]{:S(2)}) collective-permute-start(bf16[80,256]{1,0:T(8,128)(2,1)S(1)} %get-tuple-element.140), channel_id=1, source_target_pairs={{8,0},{12,4},{0,8},{4,12},{24,16},{28,20},{16,24},{20,28},{9,1},{1... | collective-permute-start | bytes 122888 | tf_op jit(solution)/shard_map/ppermute | solution.py:25
  60.7 0.9 collective-permute-start.17
  61.6 1.5 %collective-permute-start.18 = (bf16[80,256]{1,0:T(8,128)(2,1)S(1)}, bf16[80,256]{1,0:T(8,128)(2,1)S(1)}, u32[]{:S(2)}, u32[]{:S(2)}) collective-permute-start(bf16[80,256]{1,0:T(8,128)(2,1)S(1)} %get-tuple-element.142), channel_id=1, source_target_pairs={{24,0},{28,4},{16,8},{20,12},{8,16},{12,20},{0,24},{4,28},{25,1},{... | collective-permute-start | bytes 122888 | tf_op jit(solution)/shard_map/ppermute | solution.py:25
  63.1 3.3 %collective-permute-done.17.refs_2_ = bf16[80,256]{1,0:T(8,128)(2,1)S(1)} collective-permute-done((bf16[80,256]{1,0:T(8,128)(2,1)S(1)}, bf16[80,256]{1,0:T(8,128)(2,1)S(1)}, u32[]{:S(2)}, u32[]{:S(2)}) %collective-permute-start.17) | collective-permute-done | bytes 40992 | tf_op jit(solution)/shard_map/ppermute | solution.py:25
  66.5 1.0 %collective-permute-done.18.refs_3_ = bf16[80,256]{1,0:T(8,128)(2,1)S(1)} collective-permute-done((bf16[80,256]{1,0:T(8,128)(2,1)S(1)}, bf16[80,256]{1,0:T(8,128)(2,1)S(1)}, u32[]{:S(2)}, u32[]{:S(2)}) %collective-permute-start.18) | collective-permute-done | bytes 40992 | tf_op jit(solution)/shard_map/ppermute | solution.py:25
  67.5 2.3 %second_back.1 = (f32[1,1,256]{2,1,0:T(1,128)}, f32[8,256]{1,0:T(8,128)S(1)}, f32[128,256]{1,0:T(8,128)S(1)}, f32[4,128,256]{2,1,0:T(8,128)S(1)}, bf16[128,3072]...) custom-call(bf16[3072,2304]{1,0:T(8,128)(2,1)S(1)} %hot_back.1.hot_ref, ...), custom_call_target="tpu_custom_call" | custom-call | flops 10000000 | bytes 1000000 | tf_op jit(solution)/shard_map/second_back/pallas_call | solution.py:48
  69.8 1.5 %second_middle.1 = (bf16[3,128,256]{2,1,0:T(8,128)(2,1)S(1)}, f32[3,128,256]{2,1,0:T(8,128)S(1)}) custom-call(bf16[3072,2304]{1,0:T(8,128)(2,1)S(1)} %hot_back.1.hot_ref, bf16[128,3072]{1,0:T(8,128)(2,1)S(1)} %get-tuple-element.145.term_ref, f32[128,256]{1,0:T(8,128)S(1)} %get-tuple-element.146.cotangent_ref), custom_call_target="tpu_custom_call" | custom-call | flops 1000000000 | bytes 1000000 | tf_op jit(solution)/shard_map/second_middle/pallas_call | solution.py:48
  71.3 1.6 %collective-permute-start.20 = (bf16[3,128,256]{2,1,0:T(8,128)(2,1)S(1)}, bf16[3,128,256]{2,1,0:T(8,128)(2,1)S(1)}, u32[]{:S(2)}, u32[]{:S(2)}) collective-permute-start(bf16[3,128,256]{2,1,0:T(8,128)(2,1)S(1)} %get-tuple-element.149), channel_id=1, source_target_pairs={{28,0},{8,4},{4,8},{16,12},{12,16},{24,20},{20,24},{0,28},{29,1},{... | collective-permute-start | bytes 589832 | tf_op jit(solution)/shard_map/ppermute | solution.py:31
  72.9 6.5 %collective-permute-done.20.refs_1_ = bf16[3,128,256]{2,1,0:T(8,128)(2,1)S(1)} collective-permute-done((bf16[3,128,256]{2,1,0:T(8,128)(2,1)S(1)}, bf16[3,128,256]{2,1,0:T(8,128)(2,1)S(1)}, u32[]{:S(2)}, u32[]{:S(2)}) %collective-permute-start.20) | collective-permute-done | bytes 196640 | tf_op jit(solution)/shard_map/ppermute | solution.py:31
  79.4 0.8 collective-permute-start.21
  80.2 1.7 %collective-permute-start.22 = (bf16[128,256]{1,0:T(8,128)(2,1)S(1)}, bf16[128,256]{1,0:T(8,128)(2,1)S(1)}, u32[]{:S(2)}, u32[]{:S(2)}) collective-permute-start(bf16[128,256]{1,0:T(8,128)(2,1)S(1)} %get-tuple-element.156), channel_id=1, source_target_pairs={{3,0},{2,1},{1,2},{0,3},{7,4},{6,5},{5,6},{4,7},{11,8},{10,9},{9,1... | collective-permute-start | bytes 196616 | tf_op jit(solution)/shard_map/ppermute | solution.py:31
  81.9 1.2 %second_edge.1.edge_ref = f32[32,3072]{1,0:T(8,128)S(1)} custom-call(bf16[2,16,256]{2,1,0:T(8,128)(2,1)S(1)} %get-tuple-element.95.back_ref, bf16[128,3072]{1,0:T(8,128)(2,1)S(1)} %get-tuple-element.108.feature_ref, f32[4,128,256]{2,1,0:T(8,128)S(1)} %get-tuple-element.143.grad_ref), custom_call_target="tpu_custom_call" | custom-call | flops 1000000000 | bytes 1000000 | tf_op jit(solution)/shard_map/second_edge/pallas_call | solution.py:48
  83.2 0.6 collective-permute-done.21.refs_2_
  83.8 1.6 %collective-permute-done.22.refs_3_ = bf16[128,256]{1,0:T(8,128)(2,1)S(1)} collective-permute-done((bf16[128,256]{1,0:T(8,128)(2,1)S(1)}, bf16[128,256]{1,0:T(8,128)(2,1)S(1)}, u32[]{:S(2)}, u32[]{:S(2)}) %collective-permute-start.22) | collective-permute-done | bytes 65568 | tf_op jit(solution)/shard_map/ppermute | solution.py:31
  85.4 1.5 %first_back.1 = (f32[3,8,256]{2,1,0:T(8,128)S(1)}, f32[3,8,256]{2,1,0:T(8,128)S(1)}, f32[3,8,256]{2,1,0:T(8,128)S(1)}) custom-call(s32[1,3072]{1,0:T(1,128)S(1)} %get-tuple-element.79.ids_ref, f32[8,3072]{1,0:T(8,128)S(1)} %get-tuple-element.86.basis_ref, f32[8,3072]{1,0:T(8,128)S(1)} %get-tuple-element.87.slope_ref, ...), custom_call_target="tpu_custom_call" | custom-call | flops 10000000 | bytes 1000000 | tf_op jit(solution)/shard_map/first_back/pallas_call | solution.py:48
  87.1 5.0 %collective-permute-done.24 = f32[3,8,256]{2,1,0:T(8,128)S(1)} collective-permute-done((f32[3,8,256]{2,1,0:T(8,128)S(1)}, f32[3,8,256]{2,1,0:T(8,128)S(1)}, u32[]{:S(2)}, u32[]{:S(2)}) %collective-permute-start.24) | collective-permute-done | bytes 24608 | tf_op jit(solution)/shard_map/ppermute | solution.py:31
  92.0 1.8 %collective-permute-start.26 = (f32[8,256]{1,0:T(8,128)S(1)}, f32[8,256]{1,0:T(8,128)S(1)}, u32[]{:S(2)}, u32[]{:S(2)}) collective-permute-start(f32[8,256]{1,0:T(8,128)S(1)} %get-tuple-element.159), channel_id=1, source_target_pairs={{3,0},{2,1},{1,2},{0,3},{7,4},{6,5},{5,6},{4,7},{11,8},{10,9},{9,1... | collective-permute-start | bytes 24584 | tf_op jit(solution)/shard_map/ppermute | solution.py:31
  93.8 0.7 collective-permute-start.25
  94.5 2.1 %collective-permute-done.26 = f32[8,256]{1,0:T(8,128)S(1)} collective-permute-done((f32[8,256]{1,0:T(8,128)S(1)}, f32[8,256]{1,0:T(8,128)S(1)}, u32[]{:S(2)}, u32[]{:S(2)}) %collective-permute-start.26) | collective-permute-done | bytes 8224 | tf_op jit(solution)/shard_map/ppermute | solution.py:31
  96.7 0.8 collective-permute-done.25
  97.5 0.6 copy.13
  (40 shorter events, 0.6 us)
Async XLA Ops:
  0.7 0.7 copy-start.9
  1.4 0.7 copy-start.10
  2.7 9.1 %collective-permute-start.1 = (f32[8,128]{1,0:T(8,128)S(1)}, f32[8,128]{1,0:T(8,128)S(1)}, u32[]{:S(2)}, u32[]{:S(2)}) collective-permute-start(f32[8,128]{1,0:T(8,128)S(1)} %pack.1), channel_id=1, source_target_pairs={{3,0},{2,1},{1,2},{0,3},{7,4},{6,5},{5,6},{4,7},{11,8},{10,9},{9,1... | collective-permute-start | bytes 12296 | tf_op jit(solution)/shard_map/ppermute | solution.py:31
  6.6 5.2 %collective-permute-start = (f32[8,128]{1,0:T(8,128)S(1)}, f32[8,128]{1,0:T(8,128)S(1)}, u32[]{:S(2)}, u32[]{:S(2)}) collective-permute-start(f32[8,128]{1,0:T(8,128)S(1)} %pack.1), channel_id=1, source_target_pairs={{1,0},{0,1},{3,2},{2,3},{5,4},{4,5},{7,6},{6,7},{9,8},{8,9},{11,10... | collective-permute-start | bytes 12296 | tf_op jit(solution)/shard_map/ppermute | solution.py:25
  7.1 0.9 copy-start
  8.1 0.7 copy-start.4
  8.8 0.7 copy-start.5
  9.5 0.7 copy-start.6
  10.2 0.7 copy-start.7
  11.8 3.8 %collective-permute-start.2 = (f32[3,8,128]{2,1,0:T(8,128)S(1)}, f32[3,8,128]{2,1,0:T(8,128)S(1)}, u32[]{:S(2)}, u32[]{:S(2)}) collective-permute-start(f32[3,8,128]{2,1,0:T(8,128)S(1)} %pad_maximum_fusion.2.column_ref.cell_ref), channel_id=1, source_target_pairs={{4,0},{0,4},{12,8},{8,12},{20,16},{16,20},{28,24},{24,28},{5,1},{1... | collective-permute-start | bytes 36872 | tf_op jit(solution)/shard_map/ppermute | solution.py:25
  11.9 5.1 %collective-permute-start.3 = (f32[3,8,128]{2,1,0:T(8,128)S(1)}, f32[3,8,128]{2,1,0:T(8,128)S(1)}, u32[]{:S(2)}, u32[]{:S(2)}) collective-permute-start(f32[3,8,128]{2,1,0:T(8,128)S(1)} %pad_maximum_fusion.2.column_ref.cell_ref), channel_id=1, source_target_pairs={{28,0},{8,4},{4,8},{16,12},{12,16},{24,20},{20,24},{0,28},{29,1},{... | collective-permute-start | bytes 36872 | tf_op jit(solution)/shard_map/ppermute | solution.py:31
  18.9 5.9 %copy-start.2 = (f32[128,128]{1,0:T(8,128)S(1)}, f32[128,128]{1,0:T(8,128)}, u32[]{:S(2)}) copy-start(f32[128,128]{1,0:T(8,128)} %hidden_in.1) | copy-start | bytes 196612
  18.9 5.9 %copy-start.3 = (f32[128,64]{0,1:T(8,128)S(1)}, f32[128,64]{0,1:T(8,128)}, u32[]{:S(2)}) copy-start(f32[128,64]{0,1:T(8,128)} %param.20) | copy-start | bytes 98308
  18.9 5.9 %copy-start.8 = (f32[128]{0:T(128)S(1)}, f32[128]{0:T(128)}, u32[]{:S(2)}) copy-start(f32[128]{0:T(128)} %param.19) | copy-start | bytes 1540
  18.9 5.3 %collective-permute-start.5 = (bf16[128,256]{1,0:T(8,128)(2,1)S(1)}, bf16[128,256]{1,0:T(8,128)(2,1)S(1)}, u32[]{:S(2)}, u32[]{:S(2)}) collective-permute-start(bf16[128,256]{1,0:T(8,128)(2,1)S(1)} %get-tuple-element.96), channel_id=1, source_target_pairs={{3,0},{2,1},{1,2},{0,3},{7,4},{6,5},{5,6},{4,7},{11,8},{10,9},{9,1... | collective-permute-start | bytes 196616 | tf_op jit(solution)/shard_map/ppermute | solution.py:31
  20.4 4.3 %collective-permute-start.4 = (bf16[128,256]{1,0:T(8,128)(2,1)S(1)}, bf16[128,256]{1,0:T(8,128)(2,1)S(1)}, u32[]{:S(2)}, u32[]{:S(2)}) collective-permute-start(bf16[128,256]{1,0:T(8,128)(2,1)S(1)} %get-tuple-element.96), channel_id=1, source_target_pairs={{1,0},{0,1},{3,2},{2,3},{5,4},{4,5},{7,6},{6,7},{9,8},{8,9},{11,10... | collective-permute-start | bytes 196616 | tf_op jit(solution)/shard_map/ppermute | solution.py:25
  24.7 4.7 %collective-permute-start.6 = (bf16[3,128,256]{2,1,0:T(8,128)(2,1)S(1)}, bf16[3,128,256]{2,1,0:T(8,128)(2,1)S(1)}, u32[]{:S(2)}, u32[]{:S(2)}) collective-permute-start(bf16[3,128,256]{2,1,0:T(8,128)(2,1)S(1)} %pad_maximum_fusion.column_ref), channel_id=1, source_target_pairs={{4,0},{0,4},{12,8},{8,12},{20,16},{16,20},{28,24},{24,28},{5,1},{1... | collective-permute-start | bytes 589832 | tf_op jit(solution)/shard_map/ppermute | solution.py:25
  25.3 8.7 %collective-permute-start.7 = (bf16[3,128,256]{2,1,0:T(8,128)(2,1)S(1)}, bf16[3,128,256]{2,1,0:T(8,128)(2,1)S(1)}, u32[]{:S(2)}, u32[]{:S(2)}) collective-permute-start(bf16[3,128,256]{2,1,0:T(8,128)(2,1)S(1)} %pad_maximum_fusion.column_ref), channel_id=1, source_target_pairs={{28,0},{8,4},{4,8},{16,12},{12,16},{24,20},{20,24},{0,28},{29,1},{... | collective-permute-start | bytes 589832 | tf_op jit(solution)/shard_map/ppermute | solution.py:31
  33.9 6.7 %copy-start.1 = (s32[3,4096]{1,0:T(4,128)S(1)}, s32[3,4096]{1,0:T(4,128)}, u32[]{:S(2)}) copy-start(s32[3,4096]{1,0:T(4,128)} %vec_ref.1) | copy-start | bytes 147460
  36.2 6.0 %collective-permute-start.10 = (bf16[80,256]{1,0:T(8,128)(2,1)S(1)}, bf16[80,256]{1,0:T(8,128)(2,1)S(1)}, u32[]{:S(2)}, u32[]{:S(2)}) collective-permute-start(bf16[80,256]{1,0:T(8,128)(2,1)S(1)} %get-tuple-element.109), channel_id=1, source_target_pairs={{24,0},{28,4},{16,8},{20,12},{8,16},{12,20},{0,24},{4,28},{25,1},{... | collective-permute-start | bytes 122888 | tf_op jit(solution)/shard_map/ppermute | solution.py:25
  36.2 5.9 %collective-permute-start.9 = (bf16[80,256]{1,0:T(8,128)(2,1)S(1)}, bf16[80,256]{1,0:T(8,128)(2,1)S(1)}, u32[]{:S(2)}, u32[]{:S(2)}) collective-permute-start(bf16[80,256]{1,0:T(8,128)(2,1)S(1)} %get-tuple-element.109), channel_id=1, source_target_pairs={{16,0},{20,4},{24,8},{28,12},{0,16},{4,20},{8,24},{12,28},{17,1},{... | collective-permute-start | bytes 122888 | tf_op jit(solution)/shard_map/ppermute | solution.py:25
  36.3 6.3 %collective-permute-start.8 = (bf16[80,256]{1,0:T(8,128)(2,1)S(1)}, bf16[80,256]{1,0:T(8,128)(2,1)S(1)}, u32[]{:S(2)}, u32[]{:S(2)}) collective-permute-start(bf16[80,256]{1,0:T(8,128)(2,1)S(1)} %get-tuple-element.109), channel_id=1, source_target_pairs={{8,0},{12,4},{0,8},{4,12},{24,16},{28,20},{16,24},{20,28},{9,1},{1... | collective-permute-start | bytes 122888 | tf_op jit(solution)/shard_map/ppermute | solution.py:25
  42.6 1.8 %collective-permute-start.11 = (bf16[4,80,256]{2,1,0:T(8,128)(2,1)S(1)}, bf16[4,80,256]{2,1,0:T(8,128)(2,1)S(1)}, u32[]{:S(2)}, u32[]{:S(2)}) collective-permute-start(bf16[4,80,256]{2,1,0:T(8,128)(2,1)S(1)} %pad_maximum_fusion.1.blocks.refs_7_), channel_id=1, source_target_pairs={{4,0},{0,4},{12,8},{8,12},{20,16},{16,20},{28,24},{24,28},{5,1},{1... | collective-permute-start | bytes 491528 | tf_op jit(solution)/shard_map/ppermute | solution.py:25
  46.3 6.4 %collective-permute-start.12 = (bf16[320,128]{1,0:T(8,128)(2,1)S(1)}, bf16[320,128]{1,0:T(8,128)(2,1)S(1)}, u32[]{:S(2)}, u32[]{:S(2)}) collective-permute-start(bf16[320,128]{1,0:T(8,128)(2,1)S(1)} %get-tuple-element.113), channel_id=1, source_target_pairs={{1,0},{0,1},{3,2},{2,3},{5,4},{4,5},{7,6},{6,7},{9,8},{8,9},{11,10... | collective-permute-start | bytes 245768 | tf_op jit(solution)/shard_map/ppermute | solution.py:25
  47.7 5.4 %collective-permute-start.13 = (bf16[320,128]{1,0:T(8,128)(2,1)S(1)}, bf16[320,128]{1,0:T(8,128)(2,1)S(1)}, u32[]{:S(2)}, u32[]{:S(2)}) collective-permute-start(bf16[320,128]{1,0:T(8,128)(2,1)S(1)} %get-tuple-element.113), channel_id=1, source_target_pairs={{2,0},{3,1},{0,2},{1,3},{6,4},{7,5},{4,6},{5,7},{10,8},{11,9},{8,1... | collective-permute-start | bytes 245768 | tf_op jit(solution)/shard_map/ppermute | solution.py:25
  49.2 5.3 %collective-permute-start.14 = (bf16[320,128]{1,0:T(8,128)(2,1)S(1)}, bf16[320,128]{1,0:T(8,128)(2,1)S(1)}, u32[]{:S(2)}, u32[]{:S(2)}) collective-permute-start(bf16[320,128]{1,0:T(8,128)(2,1)S(1)} %get-tuple-element.113), channel_id=1, source_target_pairs={{3,0},{2,1},{1,2},{0,3},{7,4},{6,5},{5,6},{4,7},{11,8},{10,9},{9,1... | collective-permute-start | bytes 245768 | tf_op jit(solution)/shard_map/ppermute | solution.py:25
  56.4 2.1 %collective-permute-start.15 = (bf16[4,80,256]{2,1,0:T(8,128)(2,1)S(1)}, bf16[4,80,256]{2,1,0:T(8,128)(2,1)S(1)}, u32[]{:S(2)}, u32[]{:S(2)}) collective-permute-start(bf16[4,80,256]{2,1,0:T(8,128)(2,1)S(1)} %get-tuple-element.138), channel_id=1, source_target_pairs={{4,0},{0,4},{12,8},{8,12},{20,16},{16,20},{28,24},{24,28},{5,1},{1... | collective-permute-start | bytes 491528 | tf_op jit(solution)/shard_map/ppermute | solution.py:25
  58.6 4.5 %collective-permute-start.16 = (bf16[80,256]{1,0:T(8,128)(2,1)S(1)}, bf16[80,256]{1,0:T(8,128)(2,1)S(1)}, u32[]{:S(2)}, u32[]{:S(2)}) collective-permute-start(bf16[80,256]{1,0:T(8,128)(2,1)S(1)} %get-tuple-element.140), channel_id=1, source_target_pairs={{8,0},{12,4},{0,8},{4,12},{24,16},{28,20},{16,24},{20,28},{9,1},{1... | collective-permute-start | bytes 122888 | tf_op jit(solution)/shard_map/ppermute | solution.py:25
  60.7 5.8 %collective-permute-start.17 = (bf16[80,256]{1,0:T(8,128)(2,1)S(1)}, bf16[80,256]{1,0:T(8,128)(2,1)S(1)}, u32[]{:S(2)}, u32[]{:S(2)}) collective-permute-start(bf16[80,256]{1,0:T(8,128)(2,1)S(1)} %get-tuple-element.141), channel_id=1, source_target_pairs={{16,0},{20,4},{24,8},{28,12},{0,16},{4,20},{8,24},{12,28},{17,1},{... | collective-permute-start | bytes 122888 | tf_op jit(solution)/shard_map/ppermute | solution.py:25
  61.6 5.9 %collective-permute-start.18 = (bf16[80,256]{1,0:T(8,128)(2,1)S(1)}, bf16[80,256]{1,0:T(8,128)(2,1)S(1)}, u32[]{:S(2)}, u32[]{:S(2)}) collective-permute-start(bf16[80,256]{1,0:T(8,128)(2,1)S(1)} %get-tuple-element.142), channel_id=1, source_target_pairs={{24,0},{28,4},{16,8},{20,12},{8,16},{12,20},{0,24},{4,28},{25,1},{... | collective-permute-start | bytes 122888 | tf_op jit(solution)/shard_map/ppermute | solution.py:25
  71.2 1.7 %collective-permute-start.19 = (bf16[3,128,256]{2,1,0:T(8,128)(2,1)S(1)}, bf16[3,128,256]{2,1,0:T(8,128)(2,1)S(1)}, u32[]{:S(2)}, u32[]{:S(2)}) collective-permute-start(bf16[3,128,256]{2,1,0:T(8,128)(2,1)S(1)} %get-tuple-element.148), channel_id=1, source_target_pairs={{4,0},{0,4},{12,8},{8,12},{20,16},{16,20},{28,24},{24,28},{5,1},{1... | collective-permute-start | bytes 589832 | tf_op jit(solution)/shard_map/ppermute | solution.py:25
  71.3 8.1 %collective-permute-start.20 = (bf16[3,128,256]{2,1,0:T(8,128)(2,1)S(1)}, bf16[3,128,256]{2,1,0:T(8,128)(2,1)S(1)}, u32[]{:S(2)}, u32[]{:S(2)}) collective-permute-start(bf16[3,128,256]{2,1,0:T(8,128)(2,1)S(1)} %get-tuple-element.149), channel_id=1, source_target_pairs={{28,0},{8,4},{4,8},{16,12},{12,16},{24,20},{20,24},{0,28},{29,1},{... | collective-permute-start | bytes 589832 | tf_op jit(solution)/shard_map/ppermute | solution.py:31
  79.4 4.3 %collective-permute-start.21 = (bf16[128,256]{1,0:T(8,128)(2,1)S(1)}, bf16[128,256]{1,0:T(8,128)(2,1)S(1)}, u32[]{:S(2)}, u32[]{:S(2)}) collective-permute-start(bf16[128,256]{1,0:T(8,128)(2,1)S(1)} %get-tuple-element.157), channel_id=1, source_target_pairs={{1,0},{0,1},{3,2},{2,3},{5,4},{4,5},{7,6},{6,7},{9,8},{8,9},{11,10... | collective-permute-start | bytes 196616 | tf_op jit(solution)/shard_map/ppermute | solution.py:25
  80.2 5.2 %collective-permute-start.22 = (bf16[128,256]{1,0:T(8,128)(2,1)S(1)}, bf16[128,256]{1,0:T(8,128)(2,1)S(1)}, u32[]{:S(2)}, u32[]{:S(2)}) collective-permute-start(bf16[128,256]{1,0:T(8,128)(2,1)S(1)} %get-tuple-element.156), channel_id=1, source_target_pairs={{3,0},{2,1},{1,2},{0,3},{7,4},{6,5},{5,6},{4,7},{11,8},{10,9},{9,1... | collective-permute-start | bytes 196616 | tf_op jit(solution)/shard_map/ppermute | solution.py:31
  86.9 5.1 %collective-permute-start.24 = (f32[3,8,256]{2,1,0:T(8,128)S(1)}, f32[3,8,256]{2,1,0:T(8,128)S(1)}, u32[]{:S(2)}, u32[]{:S(2)}) collective-permute-start(f32[3,8,256]{2,1,0:T(8,128)S(1)} %get-tuple-element.152), channel_id=1, source_target_pairs={{28,0},{8,4},{4,8},{16,12},{12,16},{24,20},{20,24},{0,28},{29,1},{... | collective-permute-start | bytes 73736 | tf_op jit(solution)/shard_map/ppermute | solution.py:31
  87.0 5.0 %collective-permute-start.23 = (f32[3,8,256]{2,1,0:T(8,128)S(1)}, f32[3,8,256]{2,1,0:T(8,128)S(1)}, u32[]{:S(2)}, u32[]{:S(2)}) collective-permute-start(f32[3,8,256]{2,1,0:T(8,128)S(1)} %get-tuple-element.151), channel_id=1, source_target_pairs={{4,0},{0,4},{12,8},{8,12},{20,16},{16,20},{28,24},{24,28},{5,1},{1... | collective-permute-start | bytes 73736 | tf_op jit(solution)/shard_map/ppermute | solution.py:25
  92.0 4.6 %collective-permute-start.26 = (f32[8,256]{1,0:T(8,128)S(1)}, f32[8,256]{1,0:T(8,128)S(1)}, u32[]{:S(2)}, u32[]{:S(2)}) collective-permute-start(f32[8,256]{1,0:T(8,128)S(1)} %get-tuple-element.159), channel_id=1, source_target_pairs={{3,0},{2,1},{1,2},{0,3},{7,4},{6,5},{5,6},{4,7},{11,8},{10,9},{9,1... | collective-permute-start | bytes 24584 | tf_op jit(solution)/shard_map/ppermute | solution.py:31
  93.8 3.7 %collective-permute-start.25 = (f32[8,256]{1,0:T(8,128)S(1)}, f32[8,256]{1,0:T(8,128)S(1)}, u32[]{:S(2)}, u32[]{:S(2)}) collective-permute-start(f32[8,256]{1,0:T(8,128)S(1)} %get-tuple-element.160), channel_id=1, source_target_pairs={{1,0},{0,1},{3,2},{2,3},{5,4},{4,5},{7,6},{6,7},{9,8},{8,9},{11,10... | collective-permute-start | bytes 24584 | tf_op jit(solution)/shard_map/ppermute | solution.py:25

commit v9 on v8

--- a/solution.py
+++ b/solution.py
@@ -180,7 +180,7 @@
 
 
 def slot_order(ids, place_ref, atoms):
-    cell = ids // atoms
+    cell = ids >> (atoms.bit_length() - 1) if atoms & (atoms - 1) == 0 else ids // atoms
     a = (cell * 11) >> 5
     b = cell - 3 * a
     a = jnp.where((place_ref[0] & 1) == 0, 2 - a, a)
@@ -237,11 +237,11 @@
     charge_pair[1] = (charge - high).astype(BF16)
 
 
-def hot_kernel(ids_ref, hot_ref):
+def hot_kernel(first, ids_ref, hot_ref):
     edges = ids_ref.shape[1]
     for start in range(0, edges, 256):
         lanes = slice(start, start + 256)
-        hot_ref[:, lanes] = hot_columns(ids_ref[:, lanes], hot_ref.shape[0])
+        hot_ref[:, lanes] = hot_columns(ids_ref[:, lanes] - first, hot_ref.shape[0])
 
 
 def hot_back_kernel(ids_ref, hot_ref):
@@ -366,7 +366,7 @@
     sums = [None] * 4
     for n in range(slots):
         lanes = slice(n * atoms, (n + 1) * atoms)
-        feature = near_ref[:, lanes] + dot(source, hot_ref[6 * atoms :, lanes])
+        feature = near_ref[:, lanes] + dot(source, hot_ref[:, lanes])
         feature_ref[:, lanes] = feature.astype(BF16)
         for part in range(4):
             term = weight_ref[part, :, lanes] * feature
@@ -409,7 +409,7 @@
 def second_back_kernel(slots, scale, count, hot_ref, weight_ref, turn_high, turn_low, charge_ref,
                        sums_ref, gate_ref, full_charge_ref, energy_ref, slope_ref, *refs):
     folds, refs = refs[:count], refs[count:]
-    site_ref, long_ref, cotangent_ref, grad_ref, term_ref, beyond_ref = refs
+    site_ref, long_ref, cotangent_ref, grad_ref, term_ref, sides_ref, beyond_ref, pair_ref = refs
     atoms = gate_ref.shape[1]
     total = folds[0][...].astype(F32)
     for part in folds[1:]:
@@ -441,15 +441,20 @@
         term_ref[:, lanes] = term.astype(BF16)
     for b in range(3):
         start = (6 + b) * atoms
-        beyond_ref[b] = dot(term_ref[...], hot_ref[:, start : start + atoms]).astype(BF16)
-
-
-def second_middle_kernel(hot_ref, term_ref, cotangent_ref, pair_ref, middle_ref):
+        grad = dot(term_ref[...], hot_ref[:, start : start + atoms]).astype(BF16)
+        if b == 1:
+            beyond_ref[...] = grad
+        else:
+            sides_ref[b // 2] = grad
+    for b in range(3):
+        pair_ref[b] = dot(term_ref[...], hot_ref[:, b * atoms : (b + 1) * atoms]).astype(BF16)
+
+
+def second_middle_kernel(hot_ref, term_ref, cotangent_ref, middle_ref):
     atoms = cotangent_ref.shape[1]
     for b in range(3):
         grad = dot(term_ref[...], hot_ref[:, (3 + b) * atoms : (4 + b) * atoms])
         middle_ref[b] = grad + cotangent_ref[...] if b == 1 else grad
-        pair_ref[b] = dot(term_ref[...], hot_ref[:, b * atoms : (b + 1) * atoms]).astype(BF16)
 
 
 def second_edge_kernel(slots, back_ref, feature_ref, grad_ref, edge_ref):
@@ -469,7 +474,7 @@
     from_x, from_y, outs = refs[:2], refs[2:4], refs[4:]
     atoms = gate_ref.shape[1]
     cotangent = middle_ref[1]
-    for block in (from_x[0][1], from_x[1][1], from_y[0][...], from_y[1][...]):
+    for block in (from_x[0][1], from_x[1][...], from_y[0][...], from_y[1][...]):
         cotangent = cotangent + block.astype(F32)
     grads = message_grads(cotangent, gate_ref, sums_ref, turn_high, turn_low, 0)
     unit = unit_ref[...]
@@ -782,6 +787,7 @@
         ],
         smem=1,
         hbm=2,
+        flops=10_000_000_000,
         name="pack",
     )
     norm = 1.0 / math.sqrt(slots)
@@ -814,7 +820,18 @@
     )
     cells, ids = around(own, ids)
     (hot,) = run(
-        hot_kernel, [shape(9 * atoms, edges, dtype=BF16)], [ids], flops=2_000_000_000, name="hot"
+        functools.partial(hot_kernel, 0),
+        [shape(6 * atoms, edges, dtype=BF16)],
+        [ids],
+        flops=1_000_000,
+        name="hot",
+    )
+    (hot_beyond,) = run(
+        functools.partial(hot_kernel, 6 * atoms),
+        [shape(3 * atoms, edges, dtype=BF16)],
+        [ids],
+        flops=1_000_000_000,
+        name="hot_beyond",
     )
     read_out, hidden_high, hidden_low, hidden_turn_high, hidden_turn_low, charge_pair = run(
         prep_second_kernel,
@@ -872,7 +889,7 @@
             shape(1, atoms),
             shape(features, atoms),
         ],
-        [hot, edge_weights, near, mix_high, mix_low, hidden_high, hidden_low, hidden_turn_high,
+        [hot_beyond, edge_weights, near, mix_high, mix_low, hidden_high, hidden_low, hidden_turn_high,
          hidden_turn_low, read_out, charge_pair, cells[1], hidden[1], hidden[2]],
         name="second",
     )
@@ -949,7 +966,7 @@
     )
     folds = [folds[0]] + [paired(folds[d], "gx", 2 * d) for d in range(1, half)]
 
-    site, long, cotangent, grads, term, to_beyond = run(
+    site, long, cotangent, grads, term, to_sides, to_beyond, to_pair = run(
         functools.partial(second_back_kernel, slots, scale, half),
         [
             shape(1, 1, atoms),
@@ -957,25 +974,28 @@
             shape(features, atoms),
             shape(4, features, atoms),
             shape(features, edges, dtype=BF16),
+            shape(2, features, atoms, dtype=BF16),
+            shape(features, atoms, dtype=BF16),
             shape(3, features, atoms, dtype=BF16),
         ],
         [hot_back, edge_weights, turn_high, turn_low, charge_pair, sums_two, gate_two, charge,
          energy, energy_slope] + folds,
         name="second_back",
     )
-    from_beyond = beyond(to_beyond, "gx")
-    to_pair, middle = run(
+    from_pair, from_sides = paired(to_pair, "gx", 1), beyond(to_sides, "gx")
+    (middle,) = run(
         second_middle_kernel,
-        [shape(3, features, atoms, dtype=BF16), shape(3, features, atoms)],
+        [shape(3, features, atoms)],
         [hot_back, term, cotangent],
         flops=1_000_000_000,
         name="second_middle",
     )
-    from_x = [paired(to_pair, "gx", 1), from_beyond]
     sides = [
-        (middle[b] + from_x[0][b].astype(F32) + from_x[1][b].astype(F32)).astype(BF16)
-        for b in (0, 2)
+        (middle[2 * b] + from_pair[2 * b].astype(F32) + from_sides[b].astype(F32)).astype(BF16)
+        for b in range(2)
     ]
+    sides, to_beyond = lax.optimization_barrier((sides, to_beyond))
+    from_beyond = beyond(to_beyond, "gx")
     from_y = [paired(sides[0], "gy", 1), beyond(sides[1], "gy")]
     (edge,) = run(
         functools.partial(second_edge_kernel, slots),
@@ -988,7 +1008,7 @@
         functools.partial(first_back_kernel, slots),
         [shape(3, 8, atoms)] * 3,
         [ids, basis, slope, unit, kind_high, kind_low, turn_high, turn_low, sums_one, gate_one, edge,
-         long, middle] + from_x + from_y,
+         long, middle, from_pair, from_beyond] + from_y,
         name="first_back",
     )
     total = middle + paired(to_pair, "gx", 1) + beyond(to_beyond, "gx")

time: 98.5 us -> 94.3 us (0.957)
  local copies, waits for them, and re-layouts: 5.71 us -> 2 us
    unnamed x23, local copies, waits for them, and re-layouts: 5.71 us -> 1.99 us
    pallas_call x19 -> x20, Pallas kernels: 29.8 us -> 29.1 us  [run(): pl.pallas_call(kernel, out_shape=outs, in_specs=specs, out_specs=[whole()...]
    ppermute x8 -> x9, waiting for transfers between devices: 20.2 us -> 19.9 us  [beyond(): return lax.ppermute(block, axis, route)]
    ppermute x8 -> x9, starting transfers between devices: 16.9 us -> 16.7 us  [beyond(): return lax.ppermute(block, axis, route)]
  transfers between devices with their start and end apart: 27 -> 28, of which waited for: 15 -> 17; matrix products, arithmetic and copies ran while one was open for 0% -> 0% of each run, Pallas kernels for 16% -> 18%
where the time goes in v9:
time: 94.3 us; the launch traced here: 94.1 us
  starting transfers between devices  32.9 us (35%)
  Pallas kernels  29.1 us (31%)
  waiting for transfers between devices  28.9 us (31%)
  local copies, waits for them, and re-layouts  2 us (2%)
    pallas_call x20, Pallas kernels, run(): pl.pallas_call(kernel, out_shape=outs, in_specs=specs, out_specs=[whole()...  29.1 us
    ppermute x9, waiting for transfers between devices, beyond(): return lax.ppermute(block, axis, route)  19.9 us
    ppermute x9, starting transfers between devices, beyond(): return lax.ppermute(block, axis, route)  16.7 us
    ppermute x19, starting transfers between devices, paired(): lax.ppermute(block, axis, [(i ^ mask, i) for i in range(lax.axis_size(axi...  16.2 us
    ppermute x19, waiting for transfers between devices, paired(): lax.ppermute(block, axis, [(i ^ mask, i) for i in range(lax.axis_size(axi...  9 us
    unnamed x23, local copies, waits for them, and re-layouts  1.99 us
  transfers between devices with their start and end apart: 28, of which 17 were waited for; matrix products, arithmetic and copies ran while one was open for 0% of the time, Pallas kernels for 18%

profile of v9, /device:TPU:0, one launch (start us, length us, event | category | flops | bytes accessed | tf_op | source)
XLA Modules:
  0.0 94.1 jit_solution(3367547795633935897)
XLA Ops:
  0.6 0.1 pad_add_fusion.place_ref
  0.7 0.7 copy-done.9
  1.4 0.7 copy-done.10
  2.1 0.6 pack.1
  2.7 4.0 %collective-permute-start.1 = (f32[8,128]{1,0:T(8,128)S(1)}, f32[8,128]{1,0:T(8,128)S(1)}, u32[]{:S(2)}, u32[]{:S(2)}) collective-permute-start(f32[8,128]{1,0:T(8,128)S(1)} %pack.1), channel_id=1, source_target_pairs={{3,0},{2,1},{1,2},{0,3},{7,4},{6,5},{5,6},{4,7},{11,8},{10,9},{9,1... | collective-permute-start | bytes 12296 | tf_op jit(solution)/shard_map/ppermute | solution.py:31
  6.7 0.5 collective-permute-start
  7.2 0.9 prep_first.1
  8.1 0.1 collective-permute-done.1
  8.3 2.0 %collective-permute-done = f32[8,128]{1,0:T(8,128)S(1)} collective-permute-done((f32[8,128]{1,0:T(8,128)S(1)}, f32[8,128]{1,0:T(8,128)S(1)}, u32[]{:S(2)}, u32[]{:S(2)}) %collective-permute-start) | collective-permute-done | bytes 4128 | tf_op jit(solution)/shard_map/ppermute | solution.py:25
  10.3 1.8 %collective-permute-start.3 = (f32[3,8,128]{2,1,0:T(8,128)S(1)}, f32[3,8,128]{2,1,0:T(8,128)S(1)}, u32[]{:S(2)}, u32[]{:S(2)}) collective-permute-start(f32[3,8,128]{2,1,0:T(8,128)S(1)} %pad_maximum_fusion.2.column_ref.cell_ref), channel_id=1, source_target_pairs={{28,0},{8,4},{4,8},{16,12},{12,16},{24,20},{20,24},{0,28},{29,1},{... | collective-permute-start | bytes 36872 | tf_op jit(solution)/shard_map/ppermute | solution.py:31
  12.1 3.1 %collective-permute-done.3.beyond_ref = f32[3,8,128]{2,1,0:T(8,128)S(1)} collective-permute-done((f32[3,8,128]{2,1,0:T(8,128)S(1)}, f32[3,8,128]{2,1,0:T(8,128)S(1)}, u32[]{:S(2)}, u32[]{:S(2)}) %collective-permute-start.3) | collective-permute-done | bytes 12320 | tf_op jit(solution)/shard_map/ppermute | solution.py:31
  15.2 1.9 %first.1 = (bf16[128,256]{1,0:T(8,128)(2,1)S(1)}, f32[8,3072]{1,0:T(8,128)S(1)}, f32[8,3072]{1,0:T(8,128)S(1)}, f32[8,3072]{1,0:T(8,128)S(1)}, f32[3,128,256]{2,1,0:T(8,128)S(1)}, /*index=5*/f32[128,256]{1,0:T(8,128)S(1)}) custom-call(s32[2]{0:T(128)S(1)} %pad_add_fusion.place_ref, s32[1,3072]{1,0:T(1,128)S(1)} %get-tuple-element.82.ids_ref, ...), custom_call_target="tpu_custom_call" | custom-call | flops 10000000 | bytes 1000000 | tf_op jit(solution)/shard_map/first/pallas_call | solution.py:48
  17.1 1.0 %collective-permute-start.5 = (bf16[128,256]{1,0:T(8,128)(2,1)S(1)}, bf16[128,256]{1,0:T(8,128)(2,1)S(1)}, u32[]{:S(2)}, u32[]{:S(2)}) collective-permute-start(bf16[128,256]{1,0:T(8,128)(2,1)S(1)} %get-tuple-element.100), channel_id=1, source_target_pairs={{3,0},{2,1},{1,2},{0,3},{7,4},{6,5},{5,6},{4,7},{11,8},{10,9},{9,1... | collective-permute-start | bytes 196616 | tf_op jit(solution)/shard_map/ppermute | solution.py:31
  18.0 1.1 %collective-permute-start.4 = (bf16[128,256]{1,0:T(8,128)(2,1)S(1)}, bf16[128,256]{1,0:T(8,128)(2,1)S(1)}, u32[]{:S(2)}, u32[]{:S(2)}) collective-permute-start(bf16[128,256]{1,0:T(8,128)(2,1)S(1)} %get-tuple-element.100), channel_id=1, source_target_pairs={{1,0},{0,1},{3,2},{2,3},{5,4},{4,5},{7,6},{6,7},{9,8},{8,9},{11,10... | collective-permute-start | bytes 196616 | tf_op jit(solution)/shard_map/ppermute | solution.py:25
  19.1 0.3 prep_second.1
  19.4 2.1 %hot.1.hot_ref = bf16[1536,3072]{1,0:T(8,128)(2,1)S(1)} custom-call(s32[1,3072]{1,0:T(1,128)S(1)} %get-tuple-element.82.ids_ref), custom_call_target="tpu_custom_call" | custom-call | flops 1000000 | bytes 1000000 | tf_op jit(solution)/shard_map/hot/pallas_call | solution.py:48
  21.5 0.8 collective-permute-done.5
  22.3 0.1 collective-permute-start.6
  22.4 1.0 %hot_beyond.1.hot_ref = bf16[768,3072]{1,0:T(8,128)(2,1)S(1)} custom-call(s32[1,3072]{1,0:T(1,128)S(1)} %get-tuple-element.82.ids_ref), custom_call_target="tpu_custom_call" | custom-call | flops 1000000000 | bytes 1000000 | tf_op jit(solution)/shard_map/hot_beyond/pallas_call | solution.py:48
  23.4 2.6 %collective-permute-start.7 = (bf16[3,128,256]{2,1,0:T(8,128)(2,1)S(1)}, bf16[3,128,256]{2,1,0:T(8,128)(2,1)S(1)}, u32[]{:S(2)}, u32[]{:S(2)}) collective-permute-start(bf16[3,128,256]{2,1,0:T(8,128)(2,1)S(1)} %pad_maximum_fusion.column_ref), channel_id=1, source_target_pairs={{28,0},{8,4},{4,8},{16,12},{12,16},{24,20},{20,24},{0,28},{29,1},{... | collective-permute-start | bytes 589832 | tf_op jit(solution)/shard_map/ppermute | solution.py:31
  26.0 1.6 %second_near.1 = (f32[4,128,3072]{2,1,0:T(8,128)S(1)}, f32[128,3072]{1,0:T(8,128)S(1)}) custom-call(f32[8,3072]{1,0:T(8,128)S(1)} %get-tuple-element.89.basis_ref, f32[8,3072]{1,0:T(8,128)S(1)} %get-tuple-element.91.unit_ref, bf16[2,128,32]{2,1,0:T(8,128)(2,1)S(1)} %get-tuple-element.99.left_ref, bf16[1536,3072]{1,0:T(8,128)(2,1)S(1)} %hot.1.hot_ref, ...), custom_call_target="tpu_custom_call" | custom-call | flops 2000000000 | bytes 1000000 | tf_op jit(solution)/shard_map/second_near/pallas_call | solution.py:48
  27.6 0.8 second_side.1.near_ref
  28.4 3.7 %collective-permute-done.7.beyond_ref = bf16[3,128,256]{2,1,0:T(8,128)(2,1)S(1)} collective-permute-done((bf16[3,128,256]{2,1,0:T(8,128)(2,1)S(1)}, bf16[3,128,256]{2,1,0:T(8,128)(2,1)S(1)}, u32[]{:S(2)}, u32[]{:S(2)}) %collective-permute-start.7) | collective-permute-done | bytes 196640 | tf_op jit(solution)/shard_map/ppermute | solution.py:31
  32.1 2.2 %second.1 = (bf16[128,3072]{1,0:T(8,128)(2,1)S(1)}, f32[3,128,256]{2,1,0:T(8,128)S(1)}, f32[128,256]{1,0:T(8,128)S(1)}, bf16[80,256]{1,0:T(8,128)(2,1)S(1)}, f32...) custom-call(bf16[768,3072]{1,0:T(8,128)(2,1)S(1)} %hot_beyond.1.hot_ref, ...), custom_call_target="tpu_custom_call" | custom-call | flops 10000000 | bytes 1000000 | tf_op jit(solution)/shard_map/second/pallas_call | solution.py:48
  34.3 0.1 collective-permute-start.10
  34.4 0.1 collective-permute-start.9
  34.5 4.3 %collective-permute-start.8 = (bf16[80,256]{1,0:T(8,128)(2,1)S(1)}, bf16[80,256]{1,0:T(8,128)(2,1)S(1)}, u32[]{:S(2)}, u32[]{:S(2)}) collective-permute-start(bf16[80,256]{1,0:T(8,128)(2,1)S(1)} %get-tuple-element.112), channel_id=1, source_target_pairs={{8,0},{12,4},{0,8},{4,12},{24,16},{28,20},{16,24},{20,28},{9,1},{1... | collective-permute-start | bytes 122888 | tf_op jit(solution)/shard_map/ppermute | solution.py:25
  38.8 1.3 %green.1.refs_0_ = f32[320,128]{1,0:T(8,128)S(1)} custom-call(s32[2]{0:T(128)S(1)} %pad_add_fusion.place_ref, s32[3,4096]{1,0:T(4,128)S(1)} %copy-done.1), custom_call_target="tpu_custom_call" | custom-call | flops 10000000 | bytes 1000000 | tf_op jit(solution)/shard_map/green/pallas_call | solution.py:48
  40.1 0.3 collective-permute-done.10
  40.4 0.4 collective-permute-done.8
  40.9 1.7 %structure_near.1 = (f32[32,1024]{1,0:T(8,128)S(1)}, f32[32,1024]{1,0:T(8,128)S(1)}, f32[8,1024]{1,0:T(8,128)S(1)}, f32[8,1024]{1,0:T(8,128)S(1)}, bf16[640,1024...) custom-call(s32[2]{0:T(128)S(1)} %pad_add_fusion.place_ref, ...), custom_call_target="tpu_custom_call" | custom-call | flops 1000000000 | bytes 1000000 | tf_op jit(solution)/shard_map/structure_near/pallas_call | solution.py:48
  42.7 1.8 %structure_far.1 = (f32[32,1024]{1,0:T(8,128)S(1)}, f32[32,1024]{1,0:T(8,128)S(1)}, f32[8,1024]{1,0:T(8,128)S(1)}, f32[8,1024]{1,0:T(8,128)S(1)}, bf16[640,1024]...) custom-call(s32[2]{0:T(128)S(1)} %pad_add_fusion.place_ref, ...), custom_call_target="tpu_custom_call" | custom-call | flops 10000000 | bytes 1000000 | tf_op jit(solution)/shard_map/structure_far/pallas_call | solution.py:48
  44.5 1.6 %collective-permute-start.14 = (bf16[320,128]{1,0:T(8,128)(2,1)S(1)}, bf16[320,128]{1,0:T(8,128)(2,1)S(1)}, u32[]{:S(2)}, u32[]{:S(2)}) collective-permute-start(bf16[320,128]{1,0:T(8,128)(2,1)S(1)} %get-tuple-element.116), channel_id=1, source_target_pairs={{3,0},{2,1},{1,2},{0,3},{7,4},{6,5},{5,6},{4,7},{11,8},{10,9},{9,1... | collective-permute-start | bytes 245768 | tf_op jit(solution)/shard_map/ppermute | solution.py:25
  46.1 0.7 collective-permute-start.13
  46.7 1.3 %collective-permute-start.12 = (bf16[320,128]{1,0:T(8,128)(2,1)S(1)}, bf16[320,128]{1,0:T(8,128)(2,1)S(1)}, u32[]{:S(2)}, u32[]{:S(2)}) collective-permute-start(bf16[320,128]{1,0:T(8,128)(2,1)S(1)} %get-tuple-element.116), channel_id=1, source_target_pairs={{1,0},{0,1},{3,2},{2,3},{5,4},{4,5},{7,6},{6,7},{9,8},{8,9},{11,10... | collective-permute-start | bytes 245768 | tf_op jit(solution)/shard_map/ppermute | solution.py:25
  48.0 3.0 %hot_back.1.hot_ref = bf16[3072,2304]{1,0:T(8,128)(2,1)S(1)} custom-call(s32[1,3072]{1,0:T(1,128)S(1)} %get-tuple-element.82.ids_ref), custom_call_target="tpu_custom_call" | custom-call | flops 2000000000 | bytes 1000000 | tf_op jit(solution)/shard_map/hot_back/pallas_call | solution.py:48
  51.1 1.0 %collective-permute-done.13.refs_3_ = bf16[320,128]{1,0:T(8,128)(2,1)S(1)} collective-permute-done((bf16[320,128]{1,0:T(8,128)(2,1)S(1)}, bf16[320,128]{1,0:T(8,128)(2,1)S(1)}, u32[]{:S(2)}, u32[]{:S(2)}) %collective-permute-start.13) | collective-permute-done | bytes 81952 | tf_op jit(solution)/shard_map/ppermute | solution.py:25
  52.0 1.9 %fold_far.1 = (bf16[4,80,256]{2,1,0:T(8,128)(2,1)S(1)}, f32[640,64]{1,0:T(8,128)S(1)}) custom-call(s32[2]{0:T(128)S(1)} %pad_add_fusion.place_ref, f32[320,128]{1,0:T(8,128)S(1)} %green.1.refs_0_, f32[320,128]{1,0:T(8,128)S(1)} %get-tuple-element.124.refs_1_, bf16[320,128]{1,0:T(8,128)(2,1)S(1)} %collective-permute-done.12.refs_2_, ...), custom_call_target="tpu_custom_call" | custom-call | flops 10000000 | bytes 1000000 | tf_op jit(solution)/shard_map/fold_far/pallas_call | solution.py:48
  53.9 0.1 collective-permute-start.15
  54.0 1.8 %fold_near.1.near_ref = f32[4,80,256]{2,1,0:T(8,128)S(1)} custom-call(s32[2]{0:T(128)S(1)} %pad_add_fusion.place_ref, f32[640,64]{1,0:T(8,128)S(1)} %get-tuple-element.134.refs_0_, f32[32,1024]{1,0:T(8,128)S(1)} %get-tuple-element.135.refs_1_, f32[32,1024]{1,0:T(8,128)S(1)} %get-tuple-element.136.refs_2_, f32[8,1024]{1,0:T(8,128)S(1)} %get-tuple-element.137.refs_3_, ...), custom_call_target="tpu_custom_call" | custom-call | flops 1000000000 | bytes 1000000 | tf_op jit(solution)/shard_map/fold_near/pallas_call | solution.py:48
  55.9 2.0 %collective-permute-start.16 = (bf16[80,256]{1,0:T(8,128)(2,1)S(1)}, bf16[80,256]{1,0:T(8,128)(2,1)S(1)}, u32[]{:S(2)}, u32[]{:S(2)}) collective-permute-start(bf16[80,256]{1,0:T(8,128)(2,1)S(1)} %get-tuple-element.143), channel_id=1, source_target_pairs={{8,0},{12,4},{0,8},{4,12},{24,16},{28,20},{16,24},{20,28},{9,1},{1... | collective-permute-start | bytes 122888 | tf_op jit(solution)/shard_map/ppermute | solution.py:25
  57.9 0.9 collective-permute-start.17
  58.8 1.5 %collective-permute-start.18 = (bf16[80,256]{1,0:T(8,128)(2,1)S(1)}, bf16[80,256]{1,0:T(8,128)(2,1)S(1)}, u32[]{:S(2)}, u32[]{:S(2)}) collective-permute-start(bf16[80,256]{1,0:T(8,128)(2,1)S(1)} %get-tuple-element.145), channel_id=1, source_target_pairs={{24,0},{28,4},{16,8},{20,12},{8,16},{12,20},{0,24},{4,28},{25,1},{... | collective-permute-start | bytes 122888 | tf_op jit(solution)/shard_map/ppermute | solution.py:25
  60.4 3.3 %collective-permute-done.17.refs_2_ = bf16[80,256]{1,0:T(8,128)(2,1)S(1)} collective-permute-done((bf16[80,256]{1,0:T(8,128)(2,1)S(1)}, bf16[80,256]{1,0:T(8,128)(2,1)S(1)}, u32[]{:S(2)}, u32[]{:S(2)}) %collective-permute-start.17) | collective-permute-done | bytes 40992 | tf_op jit(solution)/shard_map/ppermute | solution.py:25
  63.7 1.0 %collective-permute-done.18.refs_3_ = bf16[80,256]{1,0:T(8,128)(2,1)S(1)} collective-permute-done((bf16[80,256]{1,0:T(8,128)(2,1)S(1)}, bf16[80,256]{1,0:T(8,128)(2,1)S(1)}, u32[]{:S(2)}, u32[]{:S(2)}) %collective-permute-start.18) | collective-permute-done | bytes 40992 | tf_op jit(solution)/shard_map/ppermute | solution.py:25
  64.7 2.7 %second_back.1 = (f32[1,1,256]{2,1,0:T(1,128)}, f32[8,256]{1,0:T(8,128)S(1)}, f32[128,256]{1,0:T(8,128)S(1)}, f32[4,128,256]{2,1,0:T(8,128)S(1)}, bf16[128,3072]...) custom-call(bf16[3072,2304]{1,0:T(8,128)(2,1)S(1)} %hot_back.1.hot_r, ...), custom_call_target="tpu_custom_call" | custom-call | flops 10000000 | bytes 1000000 | tf_op jit(solution)/shard_map/second_back/pallas_call | solution.py:48
  67.5 1.6 %collective-permute-start.20 = (bf16[2,128,256]{2,1,0:T(8,128)(2,1)S(1)}, bf16[2,128,256]{2,1,0:T(8,128)(2,1)S(1)}, u32[]{:S(2)}, u32[]{:S(2)}) collective-permute-start(bf16[2,128,256]{2,1,0:T(8,128)(2,1)S(1)} %get-tuple-element.151), channel_id=1, source_target_pairs={{28,0},{8,4},{4,8},{16,12},{12,16},{24,20},{20,24},{0,28},{29,1},{... | collective-permute-start | bytes 393224 | tf_op jit(solution)/shard_map/ppermute | solution.py:31
  69.1 0.8 second_middle.1.middle_ref
  69.9 4.2 %collective-permute-done.20 = bf16[2,128,256]{2,1,0:T(8,128)(2,1)S(1)} collective-permute-done((bf16[2,128,256]{2,1,0:T(8,128)(2,1)S(1)}, bf16[2,128,256]{2,1,0:T(8,128)(2,1)S(1)}, u32[]{:S(2)}, u32[]{:S(2)}) %collective-permute-start.20) | collective-permute-done | bytes 131104 | tf_op jit(solution)/shard_map/ppermute | solution.py:31
  74.2 1.2 %collective-permute-start.21 = (bf16[128,256]{1,0:T(8,128)(2,1)S(1)}, bf16[128,256]{1,0:T(8,128)(2,1)S(1)}, u32[]{:S(2)}, u32[]{:S(2)}) collective-permute-start(bf16[128,256]{1,0:T(8,128)(2,1)S(1)} %get-tuple-element.153), channel_id=1, source_target_pairs={{28,0},{8,4},{4,8},{16,12},{12,16},{24,20},{20,24},{0,28},{29,1},{... | collective-permute-start | bytes 196616 | tf_op jit(solution)/shard_map/ppermute | solution.py:31
  75.4 0.8 collective-permute-start.22
  76.1 1.8 %collective-permute-start.23 = (bf16[128,256]{1,0:T(8,128)(2,1)S(1)}, bf16[128,256]{1,0:T(8,128)(2,1)S(1)}, u32[]{:S(2)}, u32[]{:S(2)}) collective-permute-start(bf16[128,256]{1,0:T(8,128)(2,1)S(1)} %get-tuple-element.155), channel_id=1, source_target_pairs={{3,0},{2,1},{1,2},{0,3},{7,4},{6,5},{5,6},{4,7},{11,8},{10,9},{9,1... | collective-permute-start | bytes 196616 | tf_op jit(solution)/shard_map/ppermute | solution.py:31
  77.9 1.2 %second_edge.1.edge_ref = f32[32,3072]{1,0:T(8,128)S(1)} custom-call(bf16[2,16,256]{2,1,0:T(8,128)(2,1)S(1)} %get-tuple-element.98.back_ref, bf16[128,3072]{1,0:T(8,128)(2,1)S(1)} %get-tuple-element.111.feature_ref, f32[4,128,256]{2,1,0:T(8,128)S(1)} %get-tuple-element.146.grad_ref), custom_call_target="tpu_custom_call" | custom-call | flops 1000000000 | bytes 1000000 | tf_op jit(solution)/shard_map/second_edge/pallas_call | solution.py:48
  79.1 0.6 collective-permute-done.21.refs_1_
  79.7 1.6 %collective-permute-done.23.refs_3_ = bf16[128,256]{1,0:T(8,128)(2,1)S(1)} collective-permute-done((bf16[128,256]{1,0:T(8,128)(2,1)S(1)}, bf16[128,256]{1,0:T(8,128)(2,1)S(1)}, u32[]{:S(2)}, u32[]{:S(2)}) %collective-permute-start.23) | collective-permute-done | bytes 65568 | tf_op jit(solution)/shard_map/ppermute | solution.py:31
  81.3 1.5 %first_back.1 = (f32[3,8,256]{2,1,0:T(8,128)S(1)}, f32[3,8,256]{2,1,0:T(8,128)S(1)}, f32[3,8,256]{2,1,0:T(8,128)S(1)}) custom-call(s32[1,3072]{1,0:T(1,128)S(1)} %get-tuple-element.82.ids_ref, f32[8,3072]{1,0:T(8,128)S(1)} %get-tuple-element.89.basis_ref, f32[8,3072]{1,0:T(8,128)S(1)} %get-tuple-element.90.slope_ref, ...), custom_call_target="tpu_custom_call" | custom-call | flops 10000000 | bytes 1000000 | tf_op jit(solution)/shard_map/first_back/pallas_call | solution.py:48
  82.9 1.1 %collective-permute-start.25 = (f32[3,8,256]{2,1,0:T(8,128)S(1)}, f32[3,8,256]{2,1,0:T(8,128)S(1)}, u32[]{:S(2)}, u32[]{:S(2)}) collective-permute-start(f32[3,8,256]{2,1,0:T(8,128)S(1)} %get-tuple-element.158), channel_id=1, source_target_pairs={{28,0},{8,4},{4,8},{16,12},{12,16},{24,20},{20,24},{0,28},{29,1},{... | collective-permute-start | bytes 73736 | tf_op jit(solution)/shard_map/ppermute | solution.py:31
  84.0 0.1 collective-permute-done.24
  84.1 3.9 %collective-permute-done.25 = f32[3,8,256]{2,1,0:T(8,128)S(1)} collective-permute-done((f32[3,8,256]{2,1,0:T(8,128)S(1)}, f32[3,8,256]{2,1,0:T(8,128)S(1)}, u32[]{:S(2)}, u32[]{:S(2)}) %collective-permute-start.25) | collective-permute-done | bytes 24608 | tf_op jit(solution)/shard_map/ppermute | solution.py:31
  88.0 1.8 %collective-permute-start.27 = (f32[8,256]{1,0:T(8,128)S(1)}, f32[8,256]{1,0:T(8,128)S(1)}, u32[]{:S(2)}, u32[]{:S(2)}) collective-permute-start(f32[8,256]{1,0:T(8,128)S(1)} %get-tuple-element.165), channel_id=1, source_target_pairs={{3,0},{2,1},{1,2},{0,3},{7,4},{6,5},{5,6},{4,7},{11,8},{10,9},{9,1... | collective-permute-start | bytes 24584 | tf_op jit(solution)/shard_map/ppermute | solution.py:31
  89.9 1.0 %collective-permute-start.26 = (f32[8,256]{1,0:T(8,128)S(1)}, f32[8,256]{1,0:T(8,128)S(1)}, u32[]{:S(2)}, u32[]{:S(2)}) collective-permute-start(f32[8,256]{1,0:T(8,128)S(1)} %get-tuple-element.166), channel_id=1, source_target_pairs={{1,0},{0,1},{3,2},{2,3},{5,4},{4,5},{7,6},{6,7},{9,8},{8,9},{11,10... | collective-permute-start | bytes 24584 | tf_op jit(solution)/shard_map/ppermute | solution.py:25
  90.8 1.8 %collective-permute-done.27 = f32[8,256]{1,0:T(8,128)S(1)} collective-permute-done((f32[8,256]{1,0:T(8,128)S(1)}, f32[8,256]{1,0:T(8,128)S(1)}, u32[]{:S(2)}, u32[]{:S(2)}) %collective-permute-start.27) | collective-permute-done | bytes 8224 | tf_op jit(solution)/shard_map/ppermute | solution.py:31
  92.6 0.9 collective-permute-done.26
  93.5 0.6 copy.13
  (43 shorter events, 0.4 us)
Async XLA Ops:
  0.7 0.7 copy-start.9
  1.4 0.7 copy-start.10
  2.1 5.1 %copy-start = (f32[2,2,128,128]{3,2,1,0:T(8,128)S(1)}, f32[2,2,128,128]{3,2,1,0:T(8,128)}, u32[]{:S(2)}) copy-start(f32[2,2,128,128]{3,2,1,0:T(8,128)} %mixing_in.1) | copy-start | bytes 786436
  2.1 5.1 %copy-start.4 = (f32[2,2,8,128]{3,2,1,0:T(8,128)S(1)}, f32[2,2,8,128]{3,2,1,0:T(8,128)}, u32[]{:S(2)}) copy-start(f32[2,2,8,128]{3,2,1,0:T(8,128)} %radial_in.1) | copy-start | bytes 49156
  2.1 5.1 %copy-start.5 = (s32[1,1,256,12]{2,1,3,0:T(1,128)S(1)}, s32[1,1,256,12]{2,1,3,0:T(1,128)}, u32[]{:S(2)}) copy-start(s32[1,1,256,12]{2,1,3,0:T(1,128)} %param.13) | copy-start | bytes 36868
  2.1 5.1 %copy-start.6 = (f32[6,128]{1,0:T(8,128)S(1)}, f32[6,128]{1,0:T(8,128)}, u32[]{:S(2)}) copy-start(f32[6,128]{1,0:T(8,128)} %embed_in.1) | copy-start | bytes 9220
  2.1 5.1 %copy-start.7 = (s32[1,1,256]{2,1,0:T(1,128)S(1)}, s32[1,1,256]{2,1,0:T(1,128)}, u32[]{:S(2)}) copy-start(s32[1,1,256]{2,1,0:T(1,128)} %count_in.1) | copy-start | bytes 3076
  2.1 17.0 %copy-start.2 = (f32[128,128]{1,0:T(8,128)S(1)}, f32[128,128]{1,0:T(8,128)}, u32[]{:S(2)}) copy-start(f32[128,128]{1,0:T(8,128)} %hidden_in.1) | copy-start | bytes 196612
  2.1 17.0 %copy-start.3 = (f32[128,64]{0,1:T(8,128)S(1)}, f32[128,64]{0,1:T(8,128)}, u32[]{:S(2)}) copy-start(f32[128,64]{0,1:T(8,128)} %param.20) | copy-start | bytes 98308
  2.1 17.0 %copy-start.8 = (f32[128]{0:T(128)S(1)}, f32[128]{0:T(128)}, u32[]{:S(2)}) copy-start(f32[128]{0:T(128)} %param.19) | copy-start | bytes 1540
  2.7 5.5 %collective-permute-start.1 = (f32[8,128]{1,0:T(8,128)S(1)}, f32[8,128]{1,0:T(8,128)S(1)}, u32[]{:S(2)}, u32[]{:S(2)}) collective-permute-start(f32[8,128]{1,0:T(8,128)S(1)} %pack.1), channel_id=1, source_target_pairs={{3,0},{2,1},{1,2},{0,3},{7,4},{6,5},{5,6},{4,7},{11,8},{10,9},{9,1... | collective-permute-start | bytes 12296 | tf_op jit(solution)/shard_map/ppermute | solution.py:31
  6.7 3.6 %collective-permute-start = (f32[8,128]{1,0:T(8,128)S(1)}, f32[8,128]{1,0:T(8,128)S(1)}, u32[]{:S(2)}, u32[]{:S(2)}) collective-permute-start(f32[8,128]{1,0:T(8,128)S(1)} %pack.1), channel_id=1, source_target_pairs={{1,0},{0,1},{3,2},{2,3},{5,4},{4,5},{7,6},{6,7},{9,8},{8,9},{11,10... | collective-permute-start | bytes 12296 | tf_op jit(solution)/shard_map/ppermute | solution.py:25
  10.3 4.9 %collective-permute-start.3 = (f32[3,8,128]{2,1,0:T(8,128)S(1)}, f32[3,8,128]{2,1,0:T(8,128)S(1)}, u32[]{:S(2)}, u32[]{:S(2)}) collective-permute-start(f32[3,8,128]{2,1,0:T(8,128)S(1)} %pad_maximum_fusion.2.column_ref.cell_ref), channel_id=1, source_target_pairs={{28,0},{8,4},{4,8},{16,12},{12,16},{24,20},{20,24},{0,28},{29,1},{... | collective-permute-start | bytes 36872 | tf_op jit(solution)/shard_map/ppermute | solution.py:31
  12.1 3.1 %collective-permute-start.2 = (f32[3,8,128]{2,1,0:T(8,128)S(1)}, f32[3,8,128]{2,1,0:T(8,128)S(1)}, u32[]{:S(2)}, u32[]{:S(2)}) collective-permute-start(f32[3,8,128]{2,1,0:T(8,128)S(1)} %pad_maximum_fusion.2.column_ref.cell_ref), channel_id=1, source_target_pairs={{4,0},{0,4},{12,8},{8,12},{20,16},{16,20},{28,24},{24,28},{5,1},{1... | collective-permute-start | bytes 36872 | tf_op jit(solution)/shard_map/ppermute | solution.py:25
  17.1 5.2 %collective-permute-start.5 = (bf16[128,256]{1,0:T(8,128)(2,1)S(1)}, bf16[128,256]{1,0:T(8,128)(2,1)S(1)}, u32[]{:S(2)}, u32[]{:S(2)}) collective-permute-start(bf16[128,256]{1,0:T(8,128)(2,1)S(1)} %get-tuple-element.100), channel_id=1, source_target_pairs={{3,0},{2,1},{1,2},{0,3},{7,4},{6,5},{5,6},{4,7},{11,8},{10,9},{9,1... | collective-permute-start | bytes 196616 | tf_op jit(solution)/shard_map/ppermute | solution.py:31
  18.0 4.3 %collective-permute-start.4 = (bf16[128,256]{1,0:T(8,128)(2,1)S(1)}, bf16[128,256]{1,0:T(8,128)(2,1)S(1)}, u32[]{:S(2)}, u32[]{:S(2)}) collective-permute-start(bf16[128,256]{1,0:T(8,128)(2,1)S(1)} %get-tuple-element.100), channel_id=1, source_target_pairs={{1,0},{0,1},{3,2},{2,3},{5,4},{4,5},{7,6},{6,7},{9,8},{8,9},{11,10... | collective-permute-start | bytes 196616 | tf_op jit(solution)/shard_map/ppermute | solution.py:25
  22.3 5.3 %collective-permute-start.6 = (bf16[3,128,256]{2,1,0:T(8,128)(2,1)S(1)}, bf16[3,128,256]{2,1,0:T(8,128)(2,1)S(1)}, u32[]{:S(2)}, u32[]{:S(2)}) collective-permute-start(bf16[3,128,256]{2,1,0:T(8,128)(2,1)S(1)} %pad_maximum_fusion.column_ref), channel_id=1, source_target_pairs={{4,0},{0,4},{12,8},{8,12},{20,16},{16,20},{28,24},{24,28},{5,1},{1... | collective-permute-start | bytes 589832 | tf_op jit(solution)/shard_map/ppermute | solution.py:25
  23.4 8.7 %collective-permute-start.7 = (bf16[3,128,256]{2,1,0:T(8,128)(2,1)S(1)}, bf16[3,128,256]{2,1,0:T(8,128)(2,1)S(1)}, u32[]{:S(2)}, u32[]{:S(2)}) collective-permute-start(bf16[3,128,256]{2,1,0:T(8,128)(2,1)S(1)} %pad_maximum_fusion.column_ref), channel_id=1, source_target_pairs={{28,0},{8,4},{4,8},{16,12},{12,16},{24,20},{20,24},{0,28},{29,1},{... | collective-permute-start | bytes 589832 | tf_op jit(solution)/shard_map/ppermute | solution.py:31
  32.1 6.7 %copy-start.1 = (s32[3,4096]{1,0:T(4,128)S(1)}, s32[3,4096]{1,0:T(4,128)}, u32[]{:S(2)}) copy-start(s32[3,4096]{1,0:T(4,128)} %vec_ref.1) | copy-start | bytes 147460
  34.3 6.1 %collective-permute-start.10 = (bf16[80,256]{1,0:T(8,128)(2,1)S(1)}, bf16[80,256]{1,0:T(8,128)(2,1)S(1)}, u32[]{:S(2)}, u32[]{:S(2)}) collective-permute-start(bf16[80,256]{1,0:T(8,128)(2,1)S(1)} %get-tuple-element.112), channel_id=1, source_target_pairs={{24,0},{28,4},{16,8},{20,12},{8,16},{12,20},{0,24},{4,28},{25,1},{... | collective-permute-start | bytes 122888 | tf_op jit(solution)/shard_map/ppermute | solution.py:25
  34.4 6.0 %collective-permute-start.9 = (bf16[80,256]{1,0:T(8,128)(2,1)S(1)}, bf16[80,256]{1,0:T(8,128)(2,1)S(1)}, u32[]{:S(2)}, u32[]{:S(2)}) collective-permute-start(bf16[80,256]{1,0:T(8,128)(2,1)S(1)} %get-tuple-element.112), channel_id=1, source_target_pairs={{16,0},{20,4},{24,8},{28,12},{0,16},{4,20},{8,24},{12,28},{17,1},{... | collective-permute-start | bytes 122888 | tf_op jit(solution)/shard_map/ppermute | solution.py:25
  34.5 6.3 %collective-permute-start.8 = (bf16[80,256]{1,0:T(8,128)(2,1)S(1)}, bf16[80,256]{1,0:T(8,128)(2,1)S(1)}, u32[]{:S(2)}, u32[]{:S(2)}) collective-permute-start(bf16[80,256]{1,0:T(8,128)(2,1)S(1)} %get-tuple-element.112), channel_id=1, source_target_pairs={{8,0},{12,4},{0,8},{4,12},{24,16},{28,20},{16,24},{20,28},{9,1},{1... | collective-permute-start | bytes 122888 | tf_op jit(solution)/shard_map/ppermute | solution.py:25
  40.8 1.8 %collective-permute-start.11 = (bf16[4,80,256]{2,1,0:T(8,128)(2,1)S(1)}, bf16[4,80,256]{2,1,0:T(8,128)(2,1)S(1)}, u32[]{:S(2)}, u32[]{:S(2)}) collective-permute-start(bf16[4,80,256]{2,1,0:T(8,128)(2,1)S(1)} %pad_maximum_fusion.1.blocks.refs_7_), channel_id=1, source_target_pairs={{4,0},{0,4},{12,8},{8,12},{20,16},{16,20},{28,24},{24,28},{5,1},{1... | collective-permute-start | bytes 491528 | tf_op jit(solution)/shard_map/ppermute | solution.py:25
  44.5 6.6 %collective-permute-start.14 = (bf16[320,128]{1,0:T(8,128)(2,1)S(1)}, bf16[320,128]{1,0:T(8,128)(2,1)S(1)}, u32[]{:S(2)}, u32[]{:S(2)}) collective-permute-start(bf16[320,128]{1,0:T(8,128)(2,1)S(1)} %get-tuple-element.116), channel_id=1, source_target_pairs={{3,0},{2,1},{1,2},{0,3},{7,4},{6,5},{5,6},{4,7},{11,8},{10,9},{9,1... | collective-permute-start | bytes 245768 | tf_op jit(solution)/shard_map/ppermute | solution.py:25
  46.1 6.0 %collective-permute-start.13 = (bf16[320,128]{1,0:T(8,128)(2,1)S(1)}, bf16[320,128]{1,0:T(8,128)(2,1)S(1)}, u32[]{:S(2)}, u32[]{:S(2)}) collective-permute-start(bf16[320,128]{1,0:T(8,128)(2,1)S(1)} %get-tuple-element.116), channel_id=1, source_target_pairs={{2,0},{3,1},{0,2},{1,3},{6,4},{7,5},{4,6},{5,7},{10,8},{11,9},{8,1... | collective-permute-start | bytes 245768 | tf_op jit(solution)/shard_map/ppermute | solution.py:25
  46.7 5.3 %collective-permute-start.12 = (bf16[320,128]{1,0:T(8,128)(2,1)S(1)}, bf16[320,128]{1,0:T(8,128)(2,1)S(1)}, u32[]{:S(2)}, u32[]{:S(2)}) collective-permute-start(bf16[320,128]{1,0:T(8,128)(2,1)S(1)} %get-tuple-element.116), channel_id=1, source_target_pairs={{1,0},{0,1},{3,2},{2,3},{5,4},{4,5},{7,6},{6,7},{9,8},{8,9},{11,10... | collective-permute-start | bytes 245768 | tf_op jit(solution)/shard_map/ppermute | solution.py:25
  53.9 1.9 %collective-permute-start.15 = (bf16[4,80,256]{2,1,0:T(8,128)(2,1)S(1)}, bf16[4,80,256]{2,1,0:T(8,128)(2,1)S(1)}, u32[]{:S(2)}, u32[]{:S(2)}) collective-permute-start(bf16[4,80,256]{2,1,0:T(8,128)(2,1)S(1)} %get-tuple-element.141), channel_id=1, source_target_pairs={{4,0},{0,4},{12,8},{8,12},{20,16},{16,20},{28,24},{24,28},{5,1},{1... | collective-permute-start | bytes 491528 | tf_op jit(solution)/shard_map/ppermute | solution.py:25
  55.9 4.5 %collective-permute-start.16 = (bf16[80,256]{1,0:T(8,128)(2,1)S(1)}, bf16[80,256]{1,0:T(8,128)(2,1)S(1)}, u32[]{:S(2)}, u32[]{:S(2)}) collective-permute-start(bf16[80,256]{1,0:T(8,128)(2,1)S(1)} %get-tuple-element.143), channel_id=1, source_target_pairs={{8,0},{12,4},{0,8},{4,12},{24,16},{28,20},{16,24},{20,28},{9,1},{1... | collective-permute-start | bytes 122888 | tf_op jit(solution)/shard_map/ppermute | solution.py:25
  57.9 5.8 %collective-permute-start.17 = (bf16[80,256]{1,0:T(8,128)(2,1)S(1)}, bf16[80,256]{1,0:T(8,128)(2,1)S(1)}, u32[]{:S(2)}, u32[]{:S(2)}) collective-permute-start(bf16[80,256]{1,0:T(8,128)(2,1)S(1)} %get-tuple-element.144), channel_id=1, source_target_pairs={{16,0},{20,4},{24,8},{28,12},{0,16},{4,20},{8,24},{12,28},{17,1},{... | collective-permute-start | bytes 122888 | tf_op jit(solution)/shard_map/ppermute | solution.py:25
  58.8 5.9 %collective-permute-start.18 = (bf16[80,256]{1,0:T(8,128)(2,1)S(1)}, bf16[80,256]{1,0:T(8,128)(2,1)S(1)}, u32[]{:S(2)}, u32[]{:S(2)}) collective-permute-start(bf16[80,256]{1,0:T(8,128)(2,1)S(1)} %get-tuple-element.145), channel_id=1, source_target_pairs={{24,0},{28,4},{16,8},{20,12},{8,16},{12,20},{0,24},{4,28},{25,1},{... | collective-permute-start | bytes 122888 | tf_op jit(solution)/shard_map/ppermute | solution.py:25
  67.5 6.7 %collective-permute-start.19 = (bf16[3,128,256]{2,1,0:T(8,128)(2,1)S(1)}, bf16[3,128,256]{2,1,0:T(8,128)(2,1)S(1)}, u32[]{:S(2)}, u32[]{:S(2)}) collective-permute-start(bf16[3,128,256]{2,1,0:T(8,128)(2,1)S(1)} %get-tuple-element.150), channel_id=1, source_target_pairs={{4,0},{0,4},{12,8},{8,12},{20,16},{16,20},{28,24},{24,28},{5,1},{1... | collective-permute-start | bytes 589832 | tf_op jit(solution)/shard_map/ppermute | solution.py:25
  67.5 6.7 %collective-permute-start.20 = (bf16[2,128,256]{2,1,0:T(8,128)(2,1)S(1)}, bf16[2,128,256]{2,1,0:T(8,128)(2,1)S(1)}, u32[]{:S(2)}, u32[]{:S(2)}) collective-permute-start(bf16[2,128,256]{2,1,0:T(8,128)(2,1)S(1)} %get-tuple-element.151), channel_id=1, source_target_pairs={{28,0},{8,4},{4,8},{16,12},{12,16},{24,20},{20,24},{0,28},{29,1},{... | collective-permute-start | bytes 393224 | tf_op jit(solution)/shard_map/ppermute | solution.py:31
  74.2 5.6 %collective-permute-start.21 = (bf16[128,256]{1,0:T(8,128)(2,1)S(1)}, bf16[128,256]{1,0:T(8,128)(2,1)S(1)}, u32[]{:S(2)}, u32[]{:S(2)}) collective-permute-start(bf16[128,256]{1,0:T(8,128)(2,1)S(1)} %get-tuple-element.153), channel_id=1, source_target_pairs={{28,0},{8,4},{4,8},{16,12},{12,16},{24,20},{20,24},{0,28},{29,1},{... | collective-permute-start | bytes 196616 | tf_op jit(solution)/shard_map/ppermute | solution.py:31
  75.4 4.4 %collective-permute-start.22 = (bf16[128,256]{1,0:T(8,128)(2,1)S(1)}, bf16[128,256]{1,0:T(8,128)(2,1)S(1)}, u32[]{:S(2)}, u32[]{:S(2)}) collective-permute-start(bf16[128,256]{1,0:T(8,128)(2,1)S(1)} %get-tuple-element.154), channel_id=1, source_target_pairs={{1,0},{0,1},{3,2},{2,3},{5,4},{4,5},{7,6},{6,7},{9,8},{8,9},{11,10... | collective-permute-start | bytes 196616 | tf_op jit(solution)/shard_map/ppermute | solution.py:25
  76.1 5.2 %collective-permute-start.23 = (bf16[128,256]{1,0:T(8,128)(2,1)S(1)}, bf16[128,256]{1,0:T(8,128)(2,1)S(1)}, u32[]{:S(2)}, u32[]{:S(2)}) collective-permute-start(bf16[128,256]{1,0:T(8,128)(2,1)S(1)} %get-tuple-element.155), channel_id=1, source_target_pairs={{3,0},{2,1},{1,2},{0,3},{7,4},{6,5},{5,6},{4,7},{11,8},{10,9},{9,1... | collective-permute-start | bytes 196616 | tf_op jit(solution)/shard_map/ppermute | solution.py:31
  82.8 1.3 %collective-permute-start.24 = (f32[3,8,256]{2,1,0:T(8,128)S(1)}, f32[3,8,256]{2,1,0:T(8,128)S(1)}, u32[]{:S(2)}, u32[]{:S(2)}) collective-permute-start(f32[3,8,256]{2,1,0:T(8,128)S(1)} %get-tuple-element.157), channel_id=1, source_target_pairs={{4,0},{0,4},{12,8},{8,12},{20,16},{16,20},{28,24},{24,28},{5,1},{1... | collective-permute-start | bytes 73736 | tf_op jit(solution)/shard_map/ppermute | solution.py:25
  82.9 5.1 %collective-permute-start.25 = (f32[3,8,256]{2,1,0:T(8,128)S(1)}, f32[3,8,256]{2,1,0:T(8,128)S(1)}, u32[]{:S(2)}, u32[]{:S(2)}) collective-permute-start(f32[3,8,256]{2,1,0:T(8,128)S(1)} %get-tuple-element.158), channel_id=1, source_target_pairs={{28,0},{8,4},{4,8},{16,12},{12,16},{24,20},{20,24},{0,28},{29,1},{... | collective-permute-start | bytes 73736 | tf_op jit(solution)/shard_map/ppermute | solution.py:31
  88.0 4.6 %collective-permute-start.27 = (f32[8,256]{1,0:T(8,128)S(1)}, f32[8,256]{1,0:T(8,128)S(1)}, u32[]{:S(2)}, u32[]{:S(2)}) collective-permute-start(f32[8,256]{1,0:T(8,128)S(1)} %get-tuple-element.165), channel_id=1, source_target_pairs={{3,0},{2,1},{1,2},{0,3},{7,4},{6,5},{5,6},{4,7},{11,8},{10,9},{9,1... | collective-permute-start | bytes 24584 | tf_op jit(solution)/shard_map/ppermute | solution.py:31
  89.9 3.7 %collective-permute-start.26 = (f32[8,256]{1,0:T(8,128)S(1)}, f32[8,256]{1,0:T(8,128)S(1)}, u32[]{:S(2)}, u32[]{:S(2)}) collective-permute-start(f32[8,256]{1,0:T(8,128)S(1)} %get-tuple-element.166), channel_id=1, source_target_pairs={{1,0},{0,1},{3,2},{2,3},{5,4},{4,5},{7,6},{6,7},{9,8},{8,9},{11,10... | collective-permute-start | bytes 24584 | tf_op jit(solution)/shard_map/ppermute | solution.py:25

commit v10 on v9

--- a/solution.py
+++ b/solution.py
@@ -41,9 +41,8 @@
     return pl.BlockSpec(memory_space=space)
 
 
-def run(kernel, outs, args, scratch=(), smem=0, hbm=0, flops=10_000_000, grant=16, name=None):
-    specs = [whole(pltpu.SMEM)] * smem + [whole(pltpu.HBM)] * hbm
-    specs += [whole()] * (len(args) - smem - hbm)
+def run(kernel, outs, args, scratch=(), hbm=0, flops=10_000_000, grant=16, name=None):
+    specs = [whole()] * (len(args) - hbm) + [whole(pltpu.HBM)] * hbm
     return list(
         pl.pallas_call(
             kernel,
@@ -149,19 +148,11 @@
     return [basis] + [basis * unit[i : i + 1] for i in range(3)]
 
 
-def pack_kernel(place_ref, position_ref, species_ref, out_ref, place, kind, sems):
-    copies = [
-        pltpu.make_async_copy(position_ref, place, sems.at[0]),
-        pltpu.make_async_copy(species_ref, kind, sems.at[1]),
-    ]
-    for copy in copies:
-        copy.start()
-    for copy in copies:
-        copy.wait()
-    rows = [place[0, i] for i in range(3)] + [kind[0].astype(F32)]
+def pack_kernel(place_ref, position_ref, species_ref, out_ref):
+    rows = [position_ref[0, i] for i in range(3)] + [species_ref[0].astype(F32)]
     atoms = rows[0].shape[1]
     out_ref[...] = jnp.concatenate(
-        [row[:, s : s + 128] for s in range(0, atoms, 128) for row in rows], axis=0
+        [row[:, s : s + 128] for row in rows for s in range(0, atoms, 128)], axis=0
     )
 
 
@@ -183,8 +174,8 @@
     cell = ids >> (atoms.bit_length() - 1) if atoms & (atoms - 1) == 0 else ids // atoms
     a = (cell * 11) >> 5
     b = cell - 3 * a
-    a = jnp.where((place_ref[0] & 1) == 0, 2 - a, a)
-    b = jnp.where((place_ref[1] & 1) == 0, 2 - b, b)
+    a = jnp.where((place_ref[0, 0:1, 0:1] & 1) == 0, 2 - a, a)
+    b = jnp.where((place_ref[1, 0:1, 0:1] & 1) == 0, 2 - b, b)
     return ids + (3 * a + b - cell) * atoms
 
 
@@ -237,11 +228,11 @@
     charge_pair[1] = (charge - high).astype(BF16)
 
 
-def hot_kernel(first, ids_ref, hot_ref):
+def hot_kernel(ids_ref, hot_ref):
     edges = ids_ref.shape[1]
     for start in range(0, edges, 256):
         lanes = slice(start, start + 256)
-        hot_ref[:, lanes] = hot_columns(ids_ref[:, lanes] - first, hot_ref.shape[0])
+        hot_ref[:, lanes] = hot_columns(ids_ref[:, lanes], hot_ref.shape[0])
 
 
 def hot_back_kernel(ids_ref, hot_ref):
@@ -255,7 +246,8 @@
 
 def unfold_block(block, atoms):
     parts = atoms // 128
-    return jnp.concatenate([block[4 * s : 4 * s + 4] for s in range(parts)], axis=1)
+    rows = [block[r : r + 1] for r in range(4 * parts)]
+    return [jnp.concatenate(rows[q * parts : (q + 1) * parts], axis=1) for q in range(4)]
 
 
 def first_kernel(slots, place_ref, ids_ref, count_ref, embed_ref, kind_left, mix_high, mix_low,
@@ -265,11 +257,10 @@
     ids = ids_ref[...]
     frame = [pair_ref, column_ref, beyond_ref]
     own = unfold_block(column_ref[1], atoms)
-    own = jnp.concatenate([own, jnp.zeros_like(own)], axis=0)
     per_cell = atoms // 128
     places = lax.broadcasted_iota(jnp.int32, (4 * per_cell, 128), 0)
-    upper = places >> 2
-    kind_of_row = places & 3
+    upper = places % per_cell
+    kind_of_row = places // per_cell
     rows = []
     to_x = jnp.where(kind_of_row == 0, cell_width, 0.0)
     to_x = jnp.where((place_ref[0] & 1) == 0, to_x, -to_x)
@@ -286,13 +277,13 @@
         for cell, block in enumerate(rows):
             value = jnp.take_along_axis(block, lane, axis=1)
             found = jnp.where(half == per_cell * cell, value, found)
-        total = found[:4]
+        total = found
         for s in range(1, per_cell):
-            total = total + found[4 * s : 4 * s + 4]
-        pieces.append(jnp.concatenate([total, total], axis=0))
+            total = total + pltpu.roll(found, 4 * per_cell - s, 0)
+        pieces.append(total)
     found = jnp.concatenate(pieces, axis=1)
-    relative = found - jnp.concatenate([own] * slots, axis=1)
-    rel = [relative[i : i + 1] for i in range(3)]
+    found = [found[q * per_cell : q * per_cell + 1] for q in range(4)]
+    rel = [found[q] - jnp.concatenate([own[q]] * slots, axis=1) for q in range(3)]
     distance = jnp.sqrt(rel[0] * rel[0] + rel[1] * rel[1] + rel[2] * rel[2] + soften)
     inverse = 1.0 / distance
     order = (lax.broadcasted_iota(jnp.int32, (8, 1), 0) + 1).astype(F32)
@@ -303,7 +294,7 @@
     basis = wave * live
     basis_ref[...] = basis
     slope_ref[...] = (cosine - wave) * (inverse * live)
-    kinds = found[3:4]
+    kinds = found[3]
     unit = jnp.concatenate(
         [r * inverse for r in rel] + [inverse, kinds] + [jnp.zeros_like(kinds)] * 3, axis=0
     )
@@ -326,7 +317,7 @@
     sums = [dot(kind_left[0], stacks[0])]
     sums += [vectors[:, i * atoms : (i + 1) * atoms] for i in range(3)]
     step, gate = mixed(sums, mix_high, mix_low, 0)
-    low_ref[...] = (embedded(stack, own[3:4]) + step).astype(BF16)
+    low_ref[...] = (embedded(stack, own[3]) + step).astype(BF16)
     for part in range(3):
         sums_ref[part] = sums[part + 1]
     gate_ref[...] = gate
@@ -337,8 +328,8 @@
     return jnp.where(ids == place, 1.0, 0.0).astype(BF16)
 
 
-def second_near_kernel(slots, basis_ref, unit_ref, left_ref, hot_ref, column_ref, weight_ref,
-                       near_ref):
+def second_near_kernel(slots, ids_ref, basis_ref, unit_ref, left_ref, hot_ref, column_ref,
+                       weight_ref, near_ref, beyond_ref):
     atoms = column_ref.shape[2]
     parts = edge_parts(basis_ref[...], unit_ref[...])
     source = jnp.concatenate([column_ref[b] for b in range(3)], axis=1)
@@ -347,6 +338,7 @@
         for part in range(4):
             weight_ref[part, :, lanes] = weights_of(left_ref, part, parts[part][:, lanes])
         near_ref[:, lanes] = dot(source, hot_ref[3 * atoms : 6 * atoms, lanes])
+        beyond_ref[:, lanes] = hot_columns(ids_ref[:, lanes] - 6 * atoms, 3 * atoms)
 
 
 def second_side_kernel(slots, hot_ref, near_ref, pair_ref, out_ref):
@@ -357,10 +349,9 @@
         out_ref[:, lanes] = near_ref[:, lanes] + dot(source, hot_ref[: 3 * atoms, lanes])
 
 
-def second_kernel(slots, hot_ref, weight_ref, near_ref, mix_high, mix_low, hidden_high, hidden_low,
-                  turn_high, turn_low, out_ref, charge_ref, cell_ref, column_ref, beyond_ref,
-                  feature_ref, sums_ref, gate_ref, packed_ref, full_charge_ref, energy_ref,
-                  slope_ref):
+def second_kernel(slots, hot_ref, weight_ref, near_ref, mix_high, mix_low, charge_ref, cell_ref,
+                  column_ref, beyond_ref, feature_ref, sums_ref, gate_ref, packed_ref,
+                  full_charge_ref, hidden_ref):
     atoms = column_ref.shape[2]
     source = jnp.concatenate([beyond_ref[b] for b in range(3)], axis=1)
     sums = [None] * 4
@@ -373,12 +364,13 @@
             sums[part] = term if sums[part] is None else sums[part] + term
     step, gate = mixed(sums, mix_high, mix_low, 1)
     hidden = column_ref[1].astype(F32) + step
+    hidden_ref[...] = hidden
     for part in range(3):
         sums_ref[part] = sums[part + 1]
     gate_ref[...] = gate
     charge = dot_split((charge_ref[0], charge_ref[1]), hidden)
     full_charge_ref[...] = charge
-    place = unfold_block(cell_ref[1], atoms)[:3]
+    place = jnp.concatenate(unfold_block(cell_ref[1], atoms)[:3], axis=0)
     high = place.astype(BF16).astype(F32)
     rest = place - high
     middle = rest.astype(BF16).astype(F32)
@@ -386,6 +378,11 @@
     packed_ref[...] = jnp.concatenate([charge, high, middle, rest - middle, zero], axis=0).astype(
         BF16
     )
+
+
+def readout_kernel(hidden_high, hidden_low, turn_high, turn_low, out_ref, hidden_ref, energy_ref,
+                   slope_ref):
+    hidden = hidden_ref[...]
     value, slope = silu_pair(dot_split((hidden_high[...], hidden_low[...]), hidden))
     out = out_ref[...].T
     energy_ref[...] = jnp.sum(value * out, axis=0, keepdims=True)
@@ -569,7 +566,7 @@
     flat = count_up(padded)
     slot = jnp.concatenate([slot, slot, flat], axis=0)
     kz = jnp.concatenate([height, -height, jnp.zeros_like(flat)], axis=0)
-    kx, ky, valid = pair_vectors(slot, share, place_ref[0])
+    kx, ky, valid = pair_vectors(slot, share, place_ref[0, 0:1, 0:1])
     own = ((kx + WAVE_REACH) * side + ky + WAVE_REACH) * side + kz + WAVE_REACH
     seen = jnp.zeros((own.shape[0], 128), F32)
     for start in range(0, code.shape[1], 128):
@@ -616,9 +613,9 @@
     else:
         ca_ref, sa_ref, cb_ref, sb_ref, high_ref, low_ref, total_ref = refs
         total = None
-    col = place_ref[1].astype(F32) * (1.0 / grid_y)
-    first = place_ref[0] ^ flip
-    kx, ky, _ = pair_vectors(count_up(padded), share, place_ref[0])
+    col = place_ref[1, 0:1, 0:1].astype(F32) * (1.0 / grid_y)
+    first = place_ref[0, 0:1, 0:1] ^ flip
+    kx, ky, _ = pair_vectors(count_up(padded), share, place_ref[0, 0:1, 0:1])
     kz = count_up(8) + 1.0
     for d in range(grid_x // 2):
         block = blocks[d]
@@ -692,7 +689,7 @@
     t_high, t_low = split(turned)
     t_both = jnp.concatenate([t_high, t_low], axis=0)
     span = 8 * share
-    kx, ky, _ = pair_vectors(count_up(padded), share, place_ref[0])
+    kx, ky, _ = pair_vectors(count_up(padded), share, place_ref[0, 0:1, 0:1])
     kx = kx * (turn / (grid_x * cell_width))
     ky = ky * (turn / (grid_y * cell_width))
     kz = (count_up(8) + 1.0) * (turn / box_height)
@@ -771,22 +768,14 @@
     edges = slots * atoms
     scale = 1.0 / math.sqrt(wave_count * lat_width * atoms * grid_x * grid_y)
     place = jnp.stack([lax.axis_index("gx"), lax.axis_index("gy")]).astype(jnp.int32)
+    place = jnp.broadcast_to(place[:, None, None], (2, 8, 128))
     _, share, padded = pair_counts(grid_x)
     ids = neighbours.transpose(0, 3, 1, 2).reshape(1, edges)
     dma = pltpu.SemaphoreType.DMA
-    shown = positions.transpose(0, 2, 1, 3)
-
     (own,) = run(
         pack_kernel,
         [shape(4 * atoms // 128, 128)],
-        [place, shown, species],
-        scratch=[
-            pltpu.VMEM(shown.shape, F32),
-            pltpu.VMEM(species.shape, jnp.int32),
-            dma((2,)),
-        ],
-        smem=1,
-        hbm=2,
+        [place, positions.transpose(0, 2, 1, 3), species],
         flops=10_000_000_000,
         name="pack",
     )
@@ -814,24 +803,16 @@
             pltpu.VMEM(mixing.shape, F32),
             dma((5,)),
         ],
-        smem=1,
         hbm=5,
         name="prep_first",
     )
     cells, ids = around(own, ids)
     (hot,) = run(
-        functools.partial(hot_kernel, 0),
+        hot_kernel,
         [shape(6 * atoms, edges, dtype=BF16)],
         [ids],
         flops=1_000_000,
         name="hot",
-    )
-    (hot_beyond,) = run(
-        functools.partial(hot_kernel, 6 * atoms),
-        [shape(3 * atoms, edges, dtype=BF16)],
-        [ids],
-        flops=1_000_000_000,
-        name="hot_beyond",
     )
     read_out, hidden_high, hidden_low, hidden_turn_high, hidden_turn_low, charge_pair = run(
         prep_second_kernel,
@@ -859,14 +840,17 @@
             shape(features, atoms),
         ],
         [place, ids, counts, embed, kind_left, mix_high, mix_low] + cells,
-        smem=1,
         name="first",
     )
     hidden, hot = around(low, hot)
-    edge_weights, near = run(
+    edge_weights, near, hot_beyond = run(
         functools.partial(second_near_kernel, slots),
-        [shape(4, features, edges), shape(features, edges)],
-        [basis, unit, left, hot, hidden[1]],
+        [
+            shape(4, features, edges),
+            shape(features, edges),
+            shape(3 * atoms, edges, dtype=BF16),
+        ],
+        [ids, basis, unit, left, hot, hidden[1]],
         flops=2_000_000_000,
         name="second_near",
     )
@@ -878,7 +862,7 @@
         name="second_side",
     )
     block_rows = -(-(lat_width + 9) // 16) * 16
-    feature, sums_two, gate_two, packed, charge, energy, energy_slope = run(
+    feature, sums_two, gate_two, packed, charge, hidden_two = run(
         functools.partial(second_kernel, slots),
         [
             shape(features, edges, dtype=BF16),
@@ -886,12 +870,17 @@
             shape(features, atoms),
             shape(block_rows, atoms, dtype=BF16),
             shape(lat_width, atoms),
-            shape(1, atoms),
             shape(features, atoms),
         ],
-        [hot_beyond, edge_weights, near, mix_high, mix_low, hidden_high, hidden_low, hidden_turn_high,
-         hidden_turn_low, read_out, charge_pair, cells[1], hidden[1], hidden[2]],
+        [hot_beyond, edge_weights, near, mix_high, mix_low, charge_pair, cells[1], hidden[1],
+         hidden[2]],
         name="second",
+    )
+    energy, energy_slope = run(
+        readout_kernel,
+        [shape(1, atoms), shape(features, atoms)],
+        [hidden_high, hidden_low, hidden_turn_high, hidden_turn_low, read_out, hidden_two],
+        name="readout",
     )
     half = grid_x // 2
     near_charges = jnp.stack([packed] + [paired(packed, "gx", 2 * d) for d in range(1, half)])
@@ -899,7 +888,6 @@
         functools.partial(green_weights, share, padded, grid),
         [shape(16 * share + padded, 128)],
         [place, wavevectors],
-        smem=1,
         name="green",
     )
     near_charges, weight = lax.optimization_barrier((near_charges, weight))
@@ -918,7 +906,6 @@
         functools.partial(structure_kernel, share, padded, grid, lat_width, 0),
         phase_shapes + [shape(rows, lat_width)],
         [place, near_charges],
-        smem=1,
         flops=1_000_000_000,
         name="structure_near",
     )
@@ -930,7 +917,6 @@
             shape(rows // 2, 2 * lat_width, dtype=BF16),
         ],
         [place, far_charges, near_total],
-        smem=1,
         name="structure_far",
     )
     parts = [own_part] + [paired(part, "gy", d) for d in range(1, grid_y)]
@@ -946,7 +932,6 @@
         functools.partial(fold_kernel, share, padded, grid, lat_width, 1),
         [shape(half, block_rows, atoms, dtype=BF16), shape(rows, lat_width)],
         [place, weight] + parts + far_phases + [far_charges],
-        smem=1,
         name="fold_far",
     )
     far_folds = paired(far_folds, "gx", 1)
@@ -954,7 +939,6 @@
         functools.partial(fold_kernel, share, padded, grid, lat_width, 0),
         [shape(half, block_rows, atoms)],
         [place, wave_rows] + near_phases + [near_charges],
-        smem=1,
         flops=1_000_000_000,
         name="fold_near",
     )

time: 94.3 us -> 90.9 us (0.964)
  Pallas kernels: 29.1 us -> 26.5 us
    pallas_call x20, Pallas kernels: 29.1 us -> 26.5 us  [run(): pl.pallas_call(kernel, out_shape=outs, in_specs=specs, out_specs=[whole()...]
    ppermute x9, waiting for transfers between devices: 19.9 us -> 18.7 us  [beyond(): return lax.ppermute(block, axis, route)]
  transfers between devices with their start and end apart: 28 -> 28, of which waited for: 17 -> 19; matrix products, arithmetic and copies ran while one was open for 0% -> 0% of each run, Pallas kernels for 18% -> 17%
where the time goes in v10:
time: 90.9 us; the launch traced here: 90.7 us
  starting transfers between devices  32.9 us (36%)
  waiting for transfers between devices  28.1 us (31%)
  Pallas kernels  26.5 us (29%)
  local copies, waits for them, and re-layouts  2.07 us (2%)
  between operations  0.92 us (1%)
    pallas_call x20, Pallas kernels, run(): pl.pallas_call(kernel, out_shape=outs, in_specs=specs, out_specs=[whole()...  26.5 us
    ppermute x9, waiting for transfers between devices, beyond(): return lax.ppermute(block, axis, route)  18.7 us
    ppermute x9, starting transfers between devices, beyond(): return lax.ppermute(block, axis, route)  16.7 us
    ppermute x19, starting transfers between devices, paired(): lax.ppermute(block, axis, [(i ^ mask, i) for i in range(lax.axis_size(axi...  16.2 us
    ppermute x19, waiting for transfers between devices, paired(): lax.ppermute(block, axis, [(i ^ mask, i) for i in range(lax.axis_size(axi...  9.4 us
    unnamed x23, local copies, waits for them, and re-layouts  1.99 us
  transfers between devices with their start and end apart: 28, of which 19 were waited for; matrix products, arithmetic and copies ran while one was open for 0% of the time, Pallas kernels for 17%

profile of v10, /device:TPU:0, one launch (start us, length us, event | category | flops | bytes accessed | tf_op | source)
XLA Modules:
  0.0 90.7 jit_solution(11004368097154908495)
XLA Ops:
  0.6 0.1 pad_add_fusion
  0.7 0.1 broadcast_in_dim.4.place_ref
  0.8 0.7 copy-done.9
  1.5 0.7 copy-done.10
  2.2 4.0 %collective-permute-start.1 = (f32[8,128]{1,0:T(8,128)S(1)}, f32[8,128]{1,0:T(8,128)S(1)}, u32[]{:S(2)}, u32[]{:S(2)}) collective-permute-start(f32[8,128]{1,0:T(8,128)S(1)} %pack.1), channel_id=1, source_target_pairs={{3,0},{2,1},{1,2},{0,3},{7,4},{6,5},{5,6},{4,7},{11,8},{10,9},{9,1... | collective-permute-start | bytes 12296 | tf_op jit(solution)/shard_map/ppermute | solution.py:31
  6.1 0.5 collective-permute-start
  6.7 0.4 prep_first.1
  7.1 0.7 collective-permute-done.1
  7.7 2.0 %collective-permute-done = f32[8,128]{1,0:T(8,128)S(1)} collective-permute-done((f32[8,128]{1,0:T(8,128)S(1)}, f32[8,128]{1,0:T(8,128)S(1)}, u32[]{:S(2)}, u32[]{:S(2)}) %collective-permute-start) | collective-permute-done | bytes 4128 | tf_op jit(solution)/shard_map/ppermute | solution.py:25
  9.8 1.8 %collective-permute-start.3 = (f32[3,8,128]{2,1,0:T(8,128)S(1)}, f32[3,8,128]{2,1,0:T(8,128)S(1)}, u32[]{:S(2)}, u32[]{:S(2)}) collective-permute-start(f32[3,8,128]{2,1,0:T(8,128)S(1)} %pad_maximum_fusion.2.column_ref.cell_ref), channel_id=1, source_target_pairs={{28,0},{8,4},{4,8},{16,12},{12,16},{24,20},{20,24},{0,28},{29,1},{... | collective-permute-start | bytes 36872 | tf_op jit(solution)/shard_map/ppermute | solution.py:31
  11.5 3.1 %collective-permute-done.3.beyond_ref = f32[3,8,128]{2,1,0:T(8,128)S(1)} collective-permute-done((f32[3,8,128]{2,1,0:T(8,128)S(1)}, f32[3,8,128]{2,1,0:T(8,128)S(1)}, u32[]{:S(2)}, u32[]{:S(2)}) %collective-permute-start.3) | collective-permute-done | bytes 12320 | tf_op jit(solution)/shard_map/ppermute | solution.py:31
  14.7 1.3 %first.1 = (bf16[128,256]{1,0:T(8,128)(2,1)S(1)}, f32[8,3072]{1,0:T(8,128)S(1)}, f32[8,3072]{1,0:T(8,128)S(1)}, f32[8,3072]{1,0:T(8,128)S(1)}, f32[3,128,256]{2,1,0:T(8,128)S(1)}, /*index=5*/f32[128,256]{1,0:T(8,128)S(1)}) custom-call(s32[2,8,128]{2,1,0:T(8,128)S(1)} %broadcast_in_dim.4.place_ref, s32[1,3072]{1,0:T(1,128)S(1)} %get-tuple-element.84.ids_ref, ...), custom_call_target="tpu_custom_call" | custom-call | flops 10000000 | bytes 1000000 | tf_op jit(solution)/shard_map/first/pallas_call | solution.py:47
  16.0 1.0 %collective-permute-start.5 = (bf16[128,256]{1,0:T(8,128)(2,1)S(1)}, bf16[128,256]{1,0:T(8,128)(2,1)S(1)}, u32[]{:S(2)}, u32[]{:S(2)}) collective-permute-start(bf16[128,256]{1,0:T(8,128)(2,1)S(1)} %get-tuple-element.102), channel_id=1, source_target_pairs={{3,0},{2,1},{1,2},{0,3},{7,4},{6,5},{5,6},{4,7},{11,8},{10,9},{9,1... | collective-permute-start | bytes 196616 | tf_op jit(solution)/shard_map/ppermute | solution.py:31
  17.0 1.1 %collective-permute-start.4 = (bf16[128,256]{1,0:T(8,128)(2,1)S(1)}, bf16[128,256]{1,0:T(8,128)(2,1)S(1)}, u32[]{:S(2)}, u32[]{:S(2)}) collective-permute-start(bf16[128,256]{1,0:T(8,128)(2,1)S(1)} %get-tuple-element.102), channel_id=1, source_target_pairs={{1,0},{0,1},{3,2},{2,3},{5,4},{4,5},{7,6},{6,7},{9,8},{8,9},{11,10... | collective-permute-start | bytes 196616 | tf_op jit(solution)/shard_map/ppermute | solution.py:25
  18.1 2.1 %hot.1.hot_ref = bf16[1536,3072]{1,0:T(8,128)(2,1)S(1)} custom-call(s32[1,3072]{1,0:T(1,128)S(1)} %get-tuple-element.84.ids_ref), custom_call_target="tpu_custom_call" | custom-call | flops 1000000 | bytes 1000000 | tf_op jit(solution)/shard_map/hot/pallas_call | solution.py:47
  20.2 1.1 %collective-permute-done.5 = bf16[128,256]{1,0:T(8,128)(2,1)S(1)} collective-permute-done((bf16[128,256]{1,0:T(8,128)(2,1)S(1)}, bf16[128,256]{1,0:T(8,128)(2,1)S(1)}, u32[]{:S(2)}, u32[]{:S(2)}) %collective-permute-start.5) | collective-permute-done | bytes 65568 | tf_op jit(solution)/shard_map/ppermute | solution.py:31
  21.4 0.4 prep_second.1
  21.9 2.6 %collective-permute-start.7 = (bf16[3,128,256]{2,1,0:T(8,128)(2,1)S(1)}, bf16[3,128,256]{2,1,0:T(8,128)(2,1)S(1)}, u32[]{:S(2)}, u32[]{:S(2)}) collective-permute-start(bf16[3,128,256]{2,1,0:T(8,128)(2,1)S(1)} %pad_maximum_fusion.column_ref), channel_id=1, source_target_pairs={{28,0},{8,4},{4,8},{16,12},{12,16},{24,20},{20,24},{0,28},{29,1},{... | collective-permute-start | bytes 589832 | tf_op jit(solution)/shard_map/ppermute | solution.py:31
  24.5 3.5 %second_near.1 = (f32[4,128,3072]{2,1,0:T(8,128)S(1)}, f32[128,3072]{1,0:T(8,128)S(1)}, bf16[768,3072]{1,0:T(8,128)(2,1)S(1)}) custom-call(s32[1,3072]{1,0:T(1,128)S(1)} %get-tuple-element.84.ids_ref, f32[8,3072]{1,0:T(8,128)S(1)} %get-tuple-element.91.basis_ref, f32[8,3072]{1,0:T(8,128)S(1)} %get-tuple-element.93.unit_ref, ...), custom_call_target="tpu_custom_call" | custom-call | flops 2000000000 | bytes 1000000 | tf_op jit(solution)/shard_map/second_near/pallas_call | solution.py:47
  28.0 0.8 second_side.1.near_ref
  28.8 1.7 %collective-permute-done.7.beyond_ref = bf16[3,128,256]{2,1,0:T(8,128)(2,1)S(1)} collective-permute-done((bf16[3,128,256]{2,1,0:T(8,128)(2,1)S(1)}, bf16[3,128,256]{2,1,0:T(8,128)(2,1)S(1)}, u32[]{:S(2)}, u32[]{:S(2)}) %collective-permute-start.7) | collective-permute-done | bytes 196640 | tf_op jit(solution)/shard_map/ppermute | solution.py:31
  30.6 1.9 %second.1 = (bf16[128,3072]{1,0:T(8,128)(2,1)S(1)}, f32[3,128,256]{2,1,0:T(8,128)S(1)}, f32[128,256]{1,0:T(8,128)S(1)}, bf16[80,256]{1,0:T(8,128)(2,1)S(1)}, f32...) custom-call(bf16[768,3072]{1,0:T(8,128)(2,1)S(1)} %get-tuple-element.105.hot_ref, ...), custom_call_target="tpu_custom_call" | custom-call | flops 10000000 | bytes 1000000 | tf_op jit(solution)/shard_map/second/pallas_call | solution.py:47
  32.5 0.1 collective-permute-start.10
  32.6 4.3 %collective-permute-start.8 = (bf16[80,256]{1,0:T(8,128)(2,1)S(1)}, bf16[80,256]{1,0:T(8,128)(2,1)S(1)}, u32[]{:S(2)}, u32[]{:S(2)}) collective-permute-start(bf16[80,256]{1,0:T(8,128)(2,1)S(1)} %get-tuple-element.110), channel_id=1, source_target_pairs={{8,0},{12,4},{0,8},{4,12},{24,16},{28,20},{16,24},{20,28},{9,1},{1... | collective-permute-start | bytes 122888 | tf_op jit(solution)/shard_map/ppermute | solution.py:25
  36.9 0.8 green.1.refs_0_
  37.7 0.8 collective-permute-done.10
  38.6 0.4 collective-permute-done.8
  39.0 1.2 %structure_near.1 = (f32[32,1024]{1,0:T(8,128)S(1)}, f32[32,1024]{1,0:T(8,128)S(1)}, f32[8,1024]{1,0:T(8,128)S(1)}, f32[8,1024]{1,0:T(8,128)S(1)}, bf16[640,1024...) custom-call(s32[2,8,128]{2,1,0:T(8,128)S(1)} %broadcast_in_dim.4.place_ref, ...), custom_call_target="tpu_custom_call" | custom-call | flops 1000000000 | bytes 1000000 | tf_op jit(solution)/shard_map/structure_near/pallas_call | solution.py:47
  40.3 0.2 collective-permute-done.11.blocks.refs_11_
  40.4 1.3 %structure_far.1 = (f32[32,1024]{1,0:T(8,128)S(1)}, f32[32,1024]{1,0:T(8,128)S(1)}, f32[8,1024]{1,0:T(8,128)S(1)}, f32[8,1024]{1,0:T(8,128)S(1)}, bf16[640,1024]...) custom-call(s32[2,8,128]{2,1,0:T(8,128)S(1)} %broadcast_in_dim.4.place_r, ...), custom_call_target="tpu_custom_call" | custom-call | flops 10000000 | bytes 1000000 | tf_op jit(solution)/shard_map/structure_far/pallas_call | solution.py:47
  41.7 1.6 %collective-permute-start.14 = (bf16[320,128]{1,0:T(8,128)(2,1)S(1)}, bf16[320,128]{1,0:T(8,128)(2,1)S(1)}, u32[]{:S(2)}, u32[]{:S(2)}) collective-permute-start(bf16[320,128]{1,0:T(8,128)(2,1)S(1)} %get-tuple-element.114), channel_id=1, source_target_pairs={{3,0},{2,1},{1,2},{0,3},{7,4},{6,5},{5,6},{4,7},{11,8},{10,9},{9,1... | collective-permute-start | bytes 245768 | tf_op jit(solution)/shard_map/ppermute | solution.py:25
  43.3 0.7 collective-permute-start.13
  43.9 1.3 %collective-permute-start.12 = (bf16[320,128]{1,0:T(8,128)(2,1)S(1)}, bf16[320,128]{1,0:T(8,128)(2,1)S(1)}, u32[]{:S(2)}, u32[]{:S(2)}) collective-permute-start(bf16[320,128]{1,0:T(8,128)(2,1)S(1)} %get-tuple-element.114), channel_id=1, source_target_pairs={{1,0},{0,1},{3,2},{2,3},{5,4},{4,5},{7,6},{6,7},{9,8},{8,9},{11,10... | collective-permute-start | bytes 245768 | tf_op jit(solution)/shard_map/ppermute | solution.py:25
  45.2 2.8 %hot_back.1.hot_ref = bf16[3072,2304]{1,0:T(8,128)(2,1)S(1)} custom-call(s32[1,3072]{1,0:T(1,128)S(1)} %get-tuple-element.84.ids_ref), custom_call_target="tpu_custom_call" | custom-call | flops 2000000000 | bytes 1000000 | tf_op jit(solution)/shard_map/hot_back/pallas_call | solution.py:47
  48.1 1.0 %collective-permute-done.13.refs_3_ = bf16[320,128]{1,0:T(8,128)(2,1)S(1)} collective-permute-done((bf16[320,128]{1,0:T(8,128)(2,1)S(1)}, bf16[320,128]{1,0:T(8,128)(2,1)S(1)}, u32[]{:S(2)}, u32[]{:S(2)}) %collective-permute-start.13) | collective-permute-done | bytes 81952 | tf_op jit(solution)/shard_map/ppermute | solution.py:25
  49.1 1.5 %fold_far.1 = (bf16[4,80,256]{2,1,0:T(8,128)(2,1)S(1)}, f32[640,64]{1,0:T(8,128)S(1)}) custom-call(s32[2,8,128]{2,1,0:T(8,128)S(1)} %broadcast_in_dim.4.place_ref, f32[320,128]{1,0:T(8,128)S(1)} %green.1.refs_0_, f32[320,128]{1,0:T(8,128)S(1)} %get-tuple-element.128.refs_1_, bf16[320,128]{1,0:T(8,128)(2,1)S(1)} %collective-permute-done.12.refs_2_, ...), custom_call_target="tpu_custom_call" | custom-call | flops 10000000 | bytes 1000000 | tf_op jit(solution)/shard_map/fold_far/pallas_call | solution.py:47
  50.7 0.1 collective-permute-start.15
  50.8 1.2 %fold_near.1.near_ref = f32[4,80,256]{2,1,0:T(8,128)S(1)} custom-call(s32[2,8,128]{2,1,0:T(8,128)S(1)} %broadcast_in_dim.4.place_ref, f32[640,64]{1,0:T(8,128)S(1)} %get-tuple-element.138.refs_0_, f32[32,1024]{1,0:T(8,128)S(1)} %get-tuple-element.139.refs_1_, f32[32,1024]{1,0:T(8,128)S(1)} %get-tuple-element.140.refs_2_, ...), custom_call_target="tpu_custom_call" | custom-call | flops 1000000000 | bytes 1000000 | tf_op jit(solution)/shard_map/fold_near/pallas_call | solution.py:47
  52.0 0.1 collective-permute-done.15.far_ref
  52.2 2.0 %collective-permute-start.16 = (bf16[80,256]{1,0:T(8,128)(2,1)S(1)}, bf16[80,256]{1,0:T(8,128)(2,1)S(1)}, u32[]{:S(2)}, u32[]{:S(2)}) collective-permute-start(bf16[80,256]{1,0:T(8,128)(2,1)S(1)} %get-tuple-element.147), channel_id=1, source_target_pairs={{8,0},{12,4},{0,8},{4,12},{24,16},{28,20},{16,24},{20,28},{9,1},{1... | collective-permute-start | bytes 122888 | tf_op jit(solution)/shard_map/ppermute | solution.py:25
  54.2 0.9 %collective-permute-start.17 = (bf16[80,256]{1,0:T(8,128)(2,1)S(1)}, bf16[80,256]{1,0:T(8,128)(2,1)S(1)}, u32[]{:S(2)}, u32[]{:S(2)}) collective-permute-start(bf16[80,256]{1,0:T(8,128)(2,1)S(1)} %get-tuple-element.148), channel_id=1, source_target_pairs={{16,0},{20,4},{24,8},{28,12},{0,16},{4,20},{8,24},{12,28},{17,1},{... | collective-permute-start | bytes 122888 | tf_op jit(solution)/shard_map/ppermute | solution.py:25
  55.2 1.5 %collective-permute-start.18 = (bf16[80,256]{1,0:T(8,128)(2,1)S(1)}, bf16[80,256]{1,0:T(8,128)(2,1)S(1)}, u32[]{:S(2)}, u32[]{:S(2)}) collective-permute-start(bf16[80,256]{1,0:T(8,128)(2,1)S(1)} %get-tuple-element.149), channel_id=1, source_target_pairs={{24,0},{28,4},{16,8},{20,12},{8,16},{12,20},{0,24},{4,28},{25,1},{... | collective-permute-start | bytes 122888 | tf_op jit(solution)/shard_map/ppermute | solution.py:25
  56.7 0.5 readout.1
  57.2 2.8 %collective-permute-done.17.refs_2_ = bf16[80,256]{1,0:T(8,128)(2,1)S(1)} collective-permute-done((bf16[80,256]{1,0:T(8,128)(2,1)S(1)}, bf16[80,256]{1,0:T(8,128)(2,1)S(1)}, u32[]{:S(2)}, u32[]{:S(2)}) %collective-permute-start.17) | collective-permute-done | bytes 40992 | tf_op jit(solution)/shard_map/ppermute | solution.py:25
  60.0 1.1 %collective-permute-done.18.refs_3_ = bf16[80,256]{1,0:T(8,128)(2,1)S(1)} collective-permute-done((bf16[80,256]{1,0:T(8,128)(2,1)S(1)}, bf16[80,256]{1,0:T(8,128)(2,1)S(1)}, u32[]{:S(2)}, u32[]{:S(2)}) %collective-permute-start.18) | collective-permute-done | bytes 40992 | tf_op jit(solution)/shard_map/ppermute | solution.py:25
  61.1 3.1 %second_back.1 = (f32[1,1,256]{2,1,0:T(1,128)}, f32[8,256]{1,0:T(8,128)S(1)}, f32[128,256]{1,0:T(8,128)S(1)}, f32[4,128,256]{2,1,0:T(8,128)S(1)}, bf16[128,3072]...) custom-call(bf16[3072,2304]{1,0:T(8,128)(2,1)S(1)} %hot_back.1.hot_r, ...), custom_call_target="tpu_custom_call" | custom-call | flops 10000000 | bytes 1000000 | tf_op jit(solution)/shard_map/second_back/pallas_call | solution.py:47
  64.1 1.6 %collective-permute-start.20 = (bf16[2,128,256]{2,1,0:T(8,128)(2,1)S(1)}, bf16[2,128,256]{2,1,0:T(8,128)(2,1)S(1)}, u32[]{:S(2)}, u32[]{:S(2)}) collective-permute-start(bf16[2,128,256]{2,1,0:T(8,128)(2,1)S(1)} %get-tuple-element.155), channel_id=1, source_target_pairs={{28,0},{8,4},{4,8},{16,12},{12,16},{24,20},{20,24},{0,28},{29,1},{... | collective-permute-start | bytes 393224 | tf_op jit(solution)/shard_map/ppermute | solution.py:31
  65.7 0.8 second_middle.1.middle_ref
  66.5 4.2 %collective-permute-done.20 = bf16[2,128,256]{2,1,0:T(8,128)(2,1)S(1)} collective-permute-done((bf16[2,128,256]{2,1,0:T(8,128)(2,1)S(1)}, bf16[2,128,256]{2,1,0:T(8,128)(2,1)S(1)}, u32[]{:S(2)}, u32[]{:S(2)}) %collective-permute-start.20) | collective-permute-done | bytes 131104 | tf_op jit(solution)/shard_map/ppermute | solution.py:31
  70.8 1.2 %collective-permute-start.21 = (bf16[128,256]{1,0:T(8,128)(2,1)S(1)}, bf16[128,256]{1,0:T(8,128)(2,1)S(1)}, u32[]{:S(2)}, u32[]{:S(2)}) collective-permute-start(bf16[128,256]{1,0:T(8,128)(2,1)S(1)} %get-tuple-element.157), channel_id=1, source_target_pairs={{28,0},{8,4},{4,8},{16,12},{12,16},{24,20},{20,24},{0,28},{29,1},{... | collective-permute-start | bytes 196616 | tf_op jit(solution)/shard_map/ppermute | solution.py:31
  72.0 0.8 collective-permute-start.22
  72.8 1.7 %collective-permute-start.23 = (bf16[128,256]{1,0:T(8,128)(2,1)S(1)}, bf16[128,256]{1,0:T(8,128)(2,1)S(1)}, u32[]{:S(2)}, u32[]{:S(2)}) collective-permute-start(bf16[128,256]{1,0:T(8,128)(2,1)S(1)} %get-tuple-element.159), channel_id=1, source_target_pairs={{3,0},{2,1},{1,2},{0,3},{7,4},{6,5},{5,6},{4,7},{11,8},{10,9},{9,1... | collective-permute-start | bytes 196616 | tf_op jit(solution)/shard_map/ppermute | solution.py:31
  74.5 1.2 %second_edge.1.edge_ref = f32[32,3072]{1,0:T(8,128)S(1)} custom-call(bf16[2,16,256]{2,1,0:T(8,128)(2,1)S(1)} %get-tuple-element.100.back_ref, bf16[128,3072]{1,0:T(8,128)(2,1)S(1)} %get-tuple-element.109.feature_ref, f32[4,128,256]{2,1,0:T(8,128)S(1)} %get-tuple-element.150.grad_ref), custom_call_target="tpu_custom_call" | custom-call | flops 1000000000 | bytes 1000000 | tf_op jit(solution)/shard_map/second_edge/pallas_call | solution.py:47
  75.7 0.6 collective-permute-done.21.refs_1_
  76.4 1.6 %collective-permute-done.23.refs_3_ = bf16[128,256]{1,0:T(8,128)(2,1)S(1)} collective-permute-done((bf16[128,256]{1,0:T(8,128)(2,1)S(1)}, bf16[128,256]{1,0:T(8,128)(2,1)S(1)}, u32[]{:S(2)}, u32[]{:S(2)}) %collective-permute-start.23) | collective-permute-done | bytes 65568 | tf_op jit(solution)/shard_map/ppermute | solution.py:31
  78.0 1.5 %first_back.1 = (f32[3,8,256]{2,1,0:T(8,128)S(1)}, f32[3,8,256]{2,1,0:T(8,128)S(1)}, f32[3,8,256]{2,1,0:T(8,128)S(1)}) custom-call(s32[1,3072]{1,0:T(1,128)S(1)} %get-tuple-element.84.ids_ref, f32[8,3072]{1,0:T(8,128)S(1)} %get-tuple-element.91.basis_ref, f32[8,3072]{1,0:T(8,128)S(1)} %get-tuple-element.92.slope_ref, ...), custom_call_target="tpu_custom_call" | custom-call | flops 10000000 | bytes 1000000 | tf_op jit(solution)/shard_map/first_back/pallas_call | solution.py:47
  79.6 1.0 %collective-permute-start.25 = (f32[3,8,256]{2,1,0:T(8,128)S(1)}, f32[3,8,256]{2,1,0:T(8,128)S(1)}, u32[]{:S(2)}, u32[]{:S(2)}) collective-permute-start(f32[3,8,256]{2,1,0:T(8,128)S(1)} %get-tuple-element.162), channel_id=1, source_target_pairs={{28,0},{8,4},{4,8},{16,12},{12,16},{24,20},{20,24},{0,28},{29,1},{... | collective-permute-start | bytes 73736 | tf_op jit(solution)/shard_map/ppermute | solution.py:31
  80.6 0.1 collective-permute-done.24
  80.7 3.9 %collective-permute-done.25 = f32[3,8,256]{2,1,0:T(8,128)S(1)} collective-permute-done((f32[3,8,256]{2,1,0:T(8,128)S(1)}, f32[3,8,256]{2,1,0:T(8,128)S(1)}, u32[]{:S(2)}, u32[]{:S(2)}) %collective-permute-start.25) | collective-permute-done | bytes 24608 | tf_op jit(solution)/shard_map/ppermute | solution.py:31
  84.7 1.8 %collective-permute-start.27 = (f32[8,256]{1,0:T(8,128)S(1)}, f32[8,256]{1,0:T(8,128)S(1)}, u32[]{:S(2)}, u32[]{:S(2)}) collective-permute-start(f32[8,256]{1,0:T(8,128)S(1)} %get-tuple-element.169), channel_id=1, source_target_pairs={{3,0},{2,1},{1,2},{0,3},{7,4},{6,5},{5,6},{4,7},{11,8},{10,9},{9,1... | collective-permute-start | bytes 24584 | tf_op jit(solution)/shard_map/ppermute | solution.py:31
  86.5 1.1 %collective-permute-start.26 = (f32[8,256]{1,0:T(8,128)S(1)}, f32[8,256]{1,0:T(8,128)S(1)}, u32[]{:S(2)}, u32[]{:S(2)}) collective-permute-start(f32[8,256]{1,0:T(8,128)S(1)} %get-tuple-element.170), channel_id=1, source_target_pairs={{1,0},{0,1},{3,2},{2,3},{5,4},{4,5},{7,6},{6,7},{9,8},{8,9},{11,10... | collective-permute-start | bytes 24584 | tf_op jit(solution)/shard_map/ppermute | solution.py:25
  87.6 1.7 %collective-permute-done.27 = f32[8,256]{1,0:T(8,128)S(1)} collective-permute-done((f32[8,256]{1,0:T(8,128)S(1)}, f32[8,256]{1,0:T(8,128)S(1)}, u32[]{:S(2)}, u32[]{:S(2)}) %collective-permute-start.27) | collective-permute-done | bytes 8224 | tf_op jit(solution)/shard_map/ppermute | solution.py:31
  89.3 0.8 collective-permute-done.26
  90.2 0.6 copy.13
  (44 shorter events, 0.6 us)
Async XLA Ops:
  0.8 0.7 copy-start.9
  1.5 0.7 copy-start.10
  2.1 4.5 %copy-start = (f32[2,2,128,128]{3,2,1,0:T(8,128)S(1)}, f32[2,2,128,128]{3,2,1,0:T(8,128)}, u32[]{:S(2)}) copy-start(f32[2,2,128,128]{3,2,1,0:T(8,128)} %mixing_in.1) | copy-start | bytes 786436
  2.2 4.5 %copy-start.4 = (f32[2,2,8,128]{3,2,1,0:T(8,128)S(1)}, f32[2,2,8,128]{3,2,1,0:T(8,128)}, u32[]{:S(2)}) copy-start(f32[2,2,8,128]{3,2,1,0:T(8,128)} %radial_in.1) | copy-start | bytes 49156
  2.2 4.5 %copy-start.5 = (s32[1,1,256,12]{2,1,3,0:T(1,128)S(1)}, s32[1,1,256,12]{2,1,3,0:T(1,128)}, u32[]{:S(2)}) copy-start(s32[1,1,256,12]{2,1,3,0:T(1,128)} %param.13) | copy-start | bytes 36868
  2.2 4.5 %copy-start.6 = (f32[6,128]{1,0:T(8,128)S(1)}, f32[6,128]{1,0:T(8,128)}, u32[]{:S(2)}) copy-start(f32[6,128]{1,0:T(8,128)} %embed_in.1) | copy-start | bytes 9220
  2.2 4.5 %copy-start.7 = (s32[1,1,256]{2,1,0:T(1,128)S(1)}, s32[1,1,256]{2,1,0:T(1,128)}, u32[]{:S(2)}) copy-start(s32[1,1,256]{2,1,0:T(1,128)} %count_in.1) | copy-start | bytes 3076
  2.2 5.5 %collective-permute-start.1 = (f32[8,128]{1,0:T(8,128)S(1)}, f32[8,128]{1,0:T(8,128)S(1)}, u32[]{:S(2)}, u32[]{:S(2)}) collective-permute-start(f32[8,128]{1,0:T(8,128)S(1)} %pack.1), channel_id=1, source_target_pairs={{3,0},{2,1},{1,2},{0,3},{7,4},{6,5},{5,6},{4,7},{11,8},{10,9},{9,1... | collective-permute-start | bytes 12296 | tf_op jit(solution)/shard_map/ppermute | solution.py:31
  6.1 3.6 %collective-permute-start = (f32[8,128]{1,0:T(8,128)S(1)}, f32[8,128]{1,0:T(8,128)S(1)}, u32[]{:S(2)}, u32[]{:S(2)}) collective-permute-start(f32[8,128]{1,0:T(8,128)S(1)} %pack.1), channel_id=1, source_target_pairs={{1,0},{0,1},{3,2},{2,3},{5,4},{4,5},{7,6},{6,7},{9,8},{8,9},{11,10... | collective-permute-start | bytes 12296 | tf_op jit(solution)/shard_map/ppermute | solution.py:25
  9.8 4.9 %collective-permute-start.3 = (f32[3,8,128]{2,1,0:T(8,128)S(1)}, f32[3,8,128]{2,1,0:T(8,128)S(1)}, u32[]{:S(2)}, u32[]{:S(2)}) collective-permute-start(f32[3,8,128]{2,1,0:T(8,128)S(1)} %pad_maximum_fusion.2.column_ref.cell_ref), channel_id=1, source_target_pairs={{28,0},{8,4},{4,8},{16,12},{12,16},{24,20},{20,24},{0,28},{29,1},{... | collective-permute-start | bytes 36872 | tf_op jit(solution)/shard_map/ppermute | solution.py:31
  11.5 3.1 %collective-permute-start.2 = (f32[3,8,128]{2,1,0:T(8,128)S(1)}, f32[3,8,128]{2,1,0:T(8,128)S(1)}, u32[]{:S(2)}, u32[]{:S(2)}) collective-permute-start(f32[3,8,128]{2,1,0:T(8,128)S(1)} %pad_maximum_fusion.2.column_ref.cell_ref), channel_id=1, source_target_pairs={{4,0},{0,4},{12,8},{8,12},{20,16},{16,20},{28,24},{24,28},{5,1},{1... | collective-permute-start | bytes 36872 | tf_op jit(solution)/shard_map/ppermute | solution.py:25
  16.0 5.4 %copy-start.1 = (f32[128,128]{1,0:T(8,128)S(1)}, f32[128,128]{1,0:T(8,128)}, u32[]{:S(2)}) copy-start(f32[128,128]{1,0:T(8,128)} %hidden_in.1) | copy-start | bytes 196612
  16.0 5.4 %copy-start.3 = (f32[128,64]{0,1:T(8,128)S(1)}, f32[128,64]{0,1:T(8,128)}, u32[]{:S(2)}) copy-start(f32[128,64]{0,1:T(8,128)} %param.20) | copy-start | bytes 98308
  16.0 5.4 %copy-start.8 = (f32[128]{0:T(128)S(1)}, f32[128]{0:T(128)}, u32[]{:S(2)}) copy-start(f32[128]{0:T(128)} %param.19) | copy-start | bytes 1540
  16.0 5.2 %collective-permute-start.5 = (bf16[128,256]{1,0:T(8,128)(2,1)S(1)}, bf16[128,256]{1,0:T(8,128)(2,1)S(1)}, u32[]{:S(2)}, u32[]{:S(2)}) collective-permute-start(bf16[128,256]{1,0:T(8,128)(2,1)S(1)} %get-tuple-element.102), channel_id=1, source_target_pairs={{3,0},{2,1},{1,2},{0,3},{7,4},{6,5},{5,6},{4,7},{11,8},{10,9},{9,1... | collective-permute-start | bytes 196616 | tf_op jit(solution)/shard_map/ppermute | solution.py:31
  17.0 4.3 %collective-permute-start.4 = (bf16[128,256]{1,0:T(8,128)(2,1)S(1)}, bf16[128,256]{1,0:T(8,128)(2,1)S(1)}, u32[]{:S(2)}, u32[]{:S(2)}) collective-permute-start(bf16[128,256]{1,0:T(8,128)(2,1)S(1)} %get-tuple-element.102), channel_id=1, source_target_pairs={{1,0},{0,1},{3,2},{2,3},{5,4},{4,5},{7,6},{6,7},{9,8},{8,9},{11,10... | collective-permute-start | bytes 196616 | tf_op jit(solution)/shard_map/ppermute | solution.py:25
  21.3 6.7 %collective-permute-start.6 = (bf16[3,128,256]{2,1,0:T(8,128)(2,1)S(1)}, bf16[3,128,256]{2,1,0:T(8,128)(2,1)S(1)}, u32[]{:S(2)}, u32[]{:S(2)}) collective-permute-start(bf16[3,128,256]{2,1,0:T(8,128)(2,1)S(1)} %pad_maximum_fusion.column_ref), channel_id=1, source_target_pairs={{4,0},{0,4},{12,8},{8,12},{20,16},{16,20},{28,24},{24,28},{5,1},{1... | collective-permute-start | bytes 589832 | tf_op jit(solution)/shard_map/ppermute | solution.py:25
  21.9 8.7 %collective-permute-start.7 = (bf16[3,128,256]{2,1,0:T(8,128)(2,1)S(1)}, bf16[3,128,256]{2,1,0:T(8,128)(2,1)S(1)}, u32[]{:S(2)}, u32[]{:S(2)}) collective-permute-start(bf16[3,128,256]{2,1,0:T(8,128)(2,1)S(1)} %pad_maximum_fusion.column_ref), channel_id=1, source_target_pairs={{28,0},{8,4},{4,8},{16,12},{12,16},{24,20},{20,24},{0,28},{29,1},{... | collective-permute-start | bytes 589832 | tf_op jit(solution)/shard_map/ppermute | solution.py:31
  30.6 6.4 %copy-start.2 = (s32[3,4096]{1,0:T(4,128)S(1)}, s32[3,4096]{1,0:T(4,128)}, u32[]{:S(2)}) copy-start(s32[3,4096]{1,0:T(4,128)} %vec_ref.1) | copy-start | bytes 147460
  32.5 6.1 %collective-permute-start.10 = (bf16[80,256]{1,0:T(8,128)(2,1)S(1)}, bf16[80,256]{1,0:T(8,128)(2,1)S(1)}, u32[]{:S(2)}, u32[]{:S(2)}) collective-permute-start(bf16[80,256]{1,0:T(8,128)(2,1)S(1)} %get-tuple-element.110), channel_id=1, source_target_pairs={{24,0},{28,4},{16,8},{20,12},{8,16},{12,20},{0,24},{4,28},{25,1},{... | collective-permute-start | bytes 122888 | tf_op jit(solution)/shard_map/ppermute | solution.py:25
  32.5 6.0 %collective-permute-start.9 = (bf16[80,256]{1,0:T(8,128)(2,1)S(1)}, bf16[80,256]{1,0:T(8,128)(2,1)S(1)}, u32[]{:S(2)}, u32[]{:S(2)}) collective-permute-start(bf16[80,256]{1,0:T(8,128)(2,1)S(1)} %get-tuple-element.110), channel_id=1, source_target_pairs={{16,0},{20,4},{24,8},{28,12},{0,16},{4,20},{8,24},{12,28},{17,1},{... | collective-permute-start | bytes 122888 | tf_op jit(solution)/shard_map/ppermute | solution.py:25
  32.6 6.3 %collective-permute-start.8 = (bf16[80,256]{1,0:T(8,128)(2,1)S(1)}, bf16[80,256]{1,0:T(8,128)(2,1)S(1)}, u32[]{:S(2)}, u32[]{:S(2)}) collective-permute-start(bf16[80,256]{1,0:T(8,128)(2,1)S(1)} %get-tuple-element.110), channel_id=1, source_target_pairs={{8,0},{12,4},{0,8},{4,12},{24,16},{28,20},{16,24},{20,28},{9,1},{1... | collective-permute-start | bytes 122888 | tf_op jit(solution)/shard_map/ppermute | solution.py:25
  39.0 1.5 %collective-permute-start.11 = (bf16[4,80,256]{2,1,0:T(8,128)(2,1)S(1)}, bf16[4,80,256]{2,1,0:T(8,128)(2,1)S(1)}, u32[]{:S(2)}, u32[]{:S(2)}) collective-permute-start(bf16[4,80,256]{2,1,0:T(8,128)(2,1)S(1)} %pad_maximum_fusion.1.blocks.refs_7_), channel_id=1, source_target_pairs={{4,0},{0,4},{12,8},{8,12},{20,16},{16,20},{28,24},{24,28},{5,1},{1... | collective-permute-start | bytes 491528 | tf_op jit(solution)/shard_map/ppermute | solution.py:25
  41.7 6.4 %collective-permute-start.14 = (bf16[320,128]{1,0:T(8,128)(2,1)S(1)}, bf16[320,128]{1,0:T(8,128)(2,1)S(1)}, u32[]{:S(2)}, u32[]{:S(2)}) collective-permute-start(bf16[320,128]{1,0:T(8,128)(2,1)S(1)} %get-tuple-element.114), channel_id=1, source_target_pairs={{3,0},{2,1},{1,2},{0,3},{7,4},{6,5},{5,6},{4,7},{11,8},{10,9},{9,1... | collective-permute-start | bytes 245768 | tf_op jit(solution)/shard_map/ppermute | solution.py:25
  43.3 5.8 %collective-permute-start.13 = (bf16[320,128]{1,0:T(8,128)(2,1)S(1)}, bf16[320,128]{1,0:T(8,128)(2,1)S(1)}, u32[]{:S(2)}, u32[]{:S(2)}) collective-permute-start(bf16[320,128]{1,0:T(8,128)(2,1)S(1)} %get-tuple-element.114), channel_id=1, source_target_pairs={{2,0},{3,1},{0,2},{1,3},{6,4},{7,5},{4,6},{5,7},{10,8},{11,9},{8,1... | collective-permute-start | bytes 245768 | tf_op jit(solution)/shard_map/ppermute | solution.py:25
  43.9 5.2 %collective-permute-start.12 = (bf16[320,128]{1,0:T(8,128)(2,1)S(1)}, bf16[320,128]{1,0:T(8,128)(2,1)S(1)}, u32[]{:S(2)}, u32[]{:S(2)}) collective-permute-start(bf16[320,128]{1,0:T(8,128)(2,1)S(1)} %get-tuple-element.114), channel_id=1, source_target_pairs={{1,0},{0,1},{3,2},{2,3},{5,4},{4,5},{7,6},{6,7},{9,8},{8,9},{11,10... | collective-permute-start | bytes 245768 | tf_op jit(solution)/shard_map/ppermute | solution.py:25
  50.7 1.5 %collective-permute-start.15 = (bf16[4,80,256]{2,1,0:T(8,128)(2,1)S(1)}, bf16[4,80,256]{2,1,0:T(8,128)(2,1)S(1)}, u32[]{:S(2)}, u32[]{:S(2)}) collective-permute-start(bf16[4,80,256]{2,1,0:T(8,128)(2,1)S(1)} %get-tuple-element.145), channel_id=1, source_target_pairs={{4,0},{0,4},{12,8},{8,12},{20,16},{16,20},{28,24},{24,28},{5,1},{1... | collective-permute-start | bytes 491528 | tf_op jit(solution)/shard_map/ppermute | solution.py:25
  52.2 5.0 %collective-permute-start.16 = (bf16[80,256]{1,0:T(8,128)(2,1)S(1)}, bf16[80,256]{1,0:T(8,128)(2,1)S(1)}, u32[]{:S(2)}, u32[]{:S(2)}) collective-permute-start(bf16[80,256]{1,0:T(8,128)(2,1)S(1)} %get-tuple-element.147), channel_id=1, source_target_pairs={{8,0},{12,4},{0,8},{4,12},{24,16},{28,20},{16,24},{20,28},{9,1},{1... | collective-permute-start | bytes 122888 | tf_op jit(solution)/shard_map/ppermute | solution.py:25
  54.2 5.8 %collective-permute-start.17 = (bf16[80,256]{1,0:T(8,128)(2,1)S(1)}, bf16[80,256]{1,0:T(8,128)(2,1)S(1)}, u32[]{:S(2)}, u32[]{:S(2)}) collective-permute-start(bf16[80,256]{1,0:T(8,128)(2,1)S(1)} %get-tuple-element.148), channel_id=1, source_target_pairs={{16,0},{20,4},{24,8},{28,12},{0,16},{4,20},{8,24},{12,28},{17,1},{... | collective-permute-start | bytes 122888 | tf_op jit(solution)/shard_map/ppermute | solution.py:25
  55.2 5.9 %collective-permute-start.18 = (bf16[80,256]{1,0:T(8,128)(2,1)S(1)}, bf16[80,256]{1,0:T(8,128)(2,1)S(1)}, u32[]{:S(2)}, u32[]{:S(2)}) collective-permute-start(bf16[80,256]{1,0:T(8,128)(2,1)S(1)} %get-tuple-element.149), channel_id=1, source_target_pairs={{24,0},{28,4},{16,8},{20,12},{8,16},{12,20},{0,24},{4,28},{25,1},{... | collective-permute-start | bytes 122888 | tf_op jit(solution)/shard_map/ppermute | solution.py:25
  64.1 6.6 %collective-permute-start.19 = (bf16[3,128,256]{2,1,0:T(8,128)(2,1)S(1)}, bf16[3,128,256]{2,1,0:T(8,128)(2,1)S(1)}, u32[]{:S(2)}, u32[]{:S(2)}) collective-permute-start(bf16[3,128,256]{2,1,0:T(8,128)(2,1)S(1)} %get-tuple-element.154), channel_id=1, source_target_pairs={{4,0},{0,4},{12,8},{8,12},{20,16},{16,20},{28,24},{24,28},{5,1},{1... | collective-permute-start | bytes 589832 | tf_op jit(solution)/shard_map/ppermute | solution.py:25
  64.1 6.6 %collective-permute-start.20 = (bf16[2,128,256]{2,1,0:T(8,128)(2,1)S(1)}, bf16[2,128,256]{2,1,0:T(8,128)(2,1)S(1)}, u32[]{:S(2)}, u32[]{:S(2)}) collective-permute-start(bf16[2,128,256]{2,1,0:T(8,128)(2,1)S(1)} %get-tuple-element.155), channel_id=1, source_target_pairs={{28,0},{8,4},{4,8},{16,12},{12,16},{24,20},{20,24},{0,28},{29,1},{... | collective-permute-start | bytes 393224 | tf_op jit(solution)/shard_map/ppermute | solution.py:31
  70.8 5.6 %collective-permute-start.21 = (bf16[128,256]{1,0:T(8,128)(2,1)S(1)}, bf16[128,256]{1,0:T(8,128)(2,1)S(1)}, u32[]{:S(2)}, u32[]{:S(2)}) collective-permute-start(bf16[128,256]{1,0:T(8,128)(2,1)S(1)} %get-tuple-element.157), channel_id=1, source_target_pairs={{28,0},{8,4},{4,8},{16,12},{12,16},{24,20},{20,24},{0,28},{29,1},{... | collective-permute-start | bytes 196616 | tf_op jit(solution)/shard_map/ppermute | solution.py:31
  72.0 4.3 %collective-permute-start.22 = (bf16[128,256]{1,0:T(8,128)(2,1)S(1)}, bf16[128,256]{1,0:T(8,128)(2,1)S(1)}, u32[]{:S(2)}, u32[]{:S(2)}) collective-permute-start(bf16[128,256]{1,0:T(8,128)(2,1)S(1)} %get-tuple-element.158), channel_id=1, source_target_pairs={{1,0},{0,1},{3,2},{2,3},{5,4},{4,5},{7,6},{6,7},{9,8},{8,9},{11,10... | collective-permute-start | bytes 196616 | tf_op jit(solution)/shard_map/ppermute | solution.py:25
  72.8 5.2 %collective-permute-start.23 = (bf16[128,256]{1,0:T(8,128)(2,1)S(1)}, bf16[128,256]{1,0:T(8,128)(2,1)S(1)}, u32[]{:S(2)}, u32[]{:S(2)}) collective-permute-start(bf16[128,256]{1,0:T(8,128)(2,1)S(1)} %get-tuple-element.159), channel_id=1, source_target_pairs={{3,0},{2,1},{1,2},{0,3},{7,4},{6,5},{5,6},{4,7},{11,8},{10,9},{9,1... | collective-permute-start | bytes 196616 | tf_op jit(solution)/shard_map/ppermute | solution.py:31
  79.5 1.3 %collective-permute-start.24 = (f32[3,8,256]{2,1,0:T(8,128)S(1)}, f32[3,8,256]{2,1,0:T(8,128)S(1)}, u32[]{:S(2)}, u32[]{:S(2)}) collective-permute-start(f32[3,8,256]{2,1,0:T(8,128)S(1)} %get-tuple-element.161), channel_id=1, source_target_pairs={{4,0},{0,4},{12,8},{8,12},{20,16},{16,20},{28,24},{24,28},{5,1},{1... | collective-permute-start | bytes 73736 | tf_op jit(solution)/shard_map/ppermute | solution.py:25
  79.6 5.1 %collective-permute-start.25 = (f32[3,8,256]{2,1,0:T(8,128)S(1)}, f32[3,8,256]{2,1,0:T(8,128)S(1)}, u32[]{:S(2)}, u32[]{:S(2)}) collective-permute-start(f32[3,8,256]{2,1,0:T(8,128)S(1)} %get-tuple-element.162), channel_id=1, source_target_pairs={{28,0},{8,4},{4,8},{16,12},{12,16},{24,20},{20,24},{0,28},{29,1},{... | collective-permute-start | bytes 73736 | tf_op jit(solution)/shard_map/ppermute | solution.py:31
  84.7 4.6 %collective-permute-start.27 = (f32[8,256]{1,0:T(8,128)S(1)}, f32[8,256]{1,0:T(8,128)S(1)}, u32[]{:S(2)}, u32[]{:S(2)}) collective-permute-start(f32[8,256]{1,0:T(8,128)S(1)} %get-tuple-element.169), channel_id=1, source_target_pairs={{3,0},{2,1},{1,2},{0,3},{7,4},{6,5},{5,6},{4,7},{11,8},{10,9},{9,1... | collective-permute-start | bytes 24584 | tf_op jit(solution)/shard_map/ppermute | solution.py:31
  86.5 3.7 %collective-permute-start.26 = (f32[8,256]{1,0:T(8,128)S(1)}, f32[8,256]{1,0:T(8,128)S(1)}, u32[]{:S(2)}, u32[]{:S(2)}) collective-permute-start(f32[8,256]{1,0:T(8,128)S(1)} %get-tuple-element.170), channel_id=1, source_target_pairs={{1,0},{0,1},{3,2},{2,3},{5,4},{4,5},{7,6},{6,7},{9,8},{8,9},{11,10... | collective-permute-start | bytes 24584 | tf_op jit(solution)/shard_map/ppermute | solution.py:25

commit v11 on v10

--- a/solution.py
+++ b/solution.py
@@ -350,10 +350,10 @@
 
 
 def second_kernel(slots, hot_ref, weight_ref, near_ref, mix_high, mix_low, charge_ref, cell_ref,
-                  column_ref, beyond_ref, feature_ref, sums_ref, gate_ref, packed_ref,
-                  full_charge_ref, hidden_ref):
+                  column_ref, beyond_ref, corner_pair, corner_beyond, feature_ref, sums_ref, gate_ref,
+                  packed_ref, full_charge_ref, hidden_ref):
     atoms = column_ref.shape[2]
-    source = jnp.concatenate([beyond_ref[b] for b in range(3)], axis=1)
+    source = jnp.concatenate([corner_pair[...], beyond_ref[...], corner_beyond[...]], axis=1)
     sums = [None] * 4
     for n in range(slots):
         lanes = slice(n * atoms, (n + 1) * atoms)
@@ -406,7 +406,7 @@
 def second_back_kernel(slots, scale, count, hot_ref, weight_ref, turn_high, turn_low, charge_ref,
                        sums_ref, gate_ref, full_charge_ref, energy_ref, slope_ref, *refs):
     folds, refs = refs[:count], refs[count:]
-    site_ref, long_ref, cotangent_ref, grad_ref, term_ref, sides_ref, beyond_ref, pair_ref = refs
+    site_ref, long_ref, cotangent_ref, grad_ref, term_ref, pair_ref, *beyond_refs = refs
     atoms = gate_ref.shape[1]
     total = folds[0][...].astype(F32)
     for part in folds[1:]:
@@ -438,11 +438,7 @@
         term_ref[:, lanes] = term.astype(BF16)
     for b in range(3):
         start = (6 + b) * atoms
-        grad = dot(term_ref[...], hot_ref[:, start : start + atoms]).astype(BF16)
-        if b == 1:
-            beyond_ref[...] = grad
-        else:
-            sides_ref[b // 2] = grad
+        beyond_refs[b][...] = dot(term_ref[...], hot_ref[:, start : start + atoms]).astype(BF16)
     for b in range(3):
         pair_ref[b] = dot(term_ref[...], hot_ref[:, b * atoms : (b + 1) * atoms]).astype(BF16)
 
@@ -842,7 +838,12 @@
         [place, ids, counts, embed, kind_left, mix_high, mix_low] + cells,
         name="first",
     )
-    hidden, hot = around(low, hot)
+    y_pair, y_beyond = paired(low, "gy", 1), beyond(low, "gy")
+    x_beyond = beyond(low, "gx")
+    column = jnp.stack([y_pair, low, y_beyond])
+    column, x_beyond, hot = lax.optimization_barrier((column, x_beyond, hot))
+    hidden_pair = paired(column, "gx", 1)
+    corners = [paired(x_beyond, "gy", 1), beyond(x_beyond, "gy")]
     edge_weights, near, hot_beyond = run(
         functools.partial(second_near_kernel, slots),
         [
@@ -850,14 +851,14 @@
             shape(features, edges),
             shape(3 * atoms, edges, dtype=BF16),
         ],
-        [ids, basis, unit, left, hot, hidden[1]],
+        [ids, basis, unit, left, hot, column],
         flops=2_000_000_000,
         name="second_near",
     )
     (near,) = run(
         functools.partial(second_side_kernel, slots),
         [shape(features, edges)],
-        [hot, near, hidden[0]],
+        [hot, near, hidden_pair],
         flops=1_000_000_000,
         name="second_side",
     )
@@ -872,8 +873,8 @@
             shape(lat_width, atoms),
             shape(features, atoms),
         ],
-        [hot_beyond, edge_weights, near, mix_high, mix_low, charge_pair, cells[1], hidden[1],
-         hidden[2]],
+        [hot_beyond, edge_weights, near, mix_high, mix_low, charge_pair, cells[1], column, x_beyond]
+        + corners,
         name="second",
     )
     energy, energy_slope = run(
@@ -950,7 +951,7 @@
     )
     folds = [folds[0]] + [paired(folds[d], "gx", 2 * d) for d in range(1, half)]
 
-    site, long, cotangent, grads, term, to_sides, to_beyond, to_pair = run(
+    site, long, cotangent, grads, term, to_pair, *to_beyond = run(
         functools.partial(second_back_kernel, slots, scale, half),
         [
             shape(1, 1, atoms),
@@ -958,15 +959,15 @@
             shape(features, atoms),
             shape(4, features, atoms),
             shape(features, edges, dtype=BF16),
-            shape(2, features, atoms, dtype=BF16),
-            shape(features, atoms, dtype=BF16),
             shape(3, features, atoms, dtype=BF16),
-        ],
+        ]
+        + [shape(features, atoms, dtype=BF16)] * 3,
         [hot_back, edge_weights, turn_high, turn_low, charge_pair, sums_two, gate_two, charge,
          energy, energy_slope] + folds,
         name="second_back",
     )
-    from_pair, from_sides = paired(to_pair, "gx", 1), beyond(to_sides, "gx")
+    corners = [paired(to_beyond[0], "gy", 1), beyond(to_beyond[2], "gy")]
+    from_pair = paired(to_pair, "gx", 1)
     (middle,) = run(
         second_middle_kernel,
         [shape(3, features, atoms)],
@@ -974,11 +975,10 @@
         flops=1_000_000_000,
         name="second_middle",
     )
-    sides = [
-        (middle[2 * b] + from_pair[2 * b].astype(F32) + from_sides[b].astype(F32)).astype(BF16)
-        for b in range(2)
-    ]
-    sides, to_beyond = lax.optimization_barrier((sides, to_beyond))
+    sides = [(middle[b] + from_pair[b].astype(F32)).astype(BF16) for b in (0, 2)]
+    to_beyond = (to_beyond[1].astype(F32) + corners[0].astype(F32) + corners[1].astype(F32)).astype(
+        BF16
+    )
     from_beyond = beyond(to_beyond, "gx")
     from_y = [paired(sides[0], "gy", 1), beyond(sides[1], "gy")]
     (edge,) = run(

time: 90.9 us -> 92.8 us (1.021)
  starting transfers between devices: 32.9 us -> 34.5 us
    ppermute x19 -> x21, starting transfers between devices: 16.2 us -> 18.4 us  [paired(): lax.ppermute(block, axis, [(i ^ mask, i) for i in range(lax.axis_size(axi...]
    ppermute x19 -> x21, waiting for transfers between devices: 9.4 us -> 10.8 us  [paired(): lax.ppermute(block, axis, [(i ^ mask, i) for i in range(lax.axis_size(axi...]
    ppermute x9 -> x10, waiting for transfers between devices: 18.7 us -> 17.5 us  [beyond(): return lax.ppermute(block, axis, route)]
    ppermute x9 -> x10, starting transfers between devices: 16.7 us -> 16.1 us  [beyond(): return lax.ppermute(block, axis, route)]
  transfers between devices with their start and end apart: 28 -> 31, of which waited for: 19 -> 19; matrix products, arithmetic and copies ran while one was open for 0% -> 0% of each run, Pallas kernels for 17% -> 17%
where the time goes in v11:
time: 92.8 us; the launch traced here: 92.6 us
  starting transfers between devices  34.5 us (37%)
  waiting for transfers between devices  28.3 us (30%)
  Pallas kernels  26.5 us (29%)
  local copies, waits for them, and re-layouts  2.07 us (2%)
  between operations  0.93 us (1%)
    pallas_call x20, Pallas kernels, run(): pl.pallas_call(kernel, out_shape=outs, in_specs=specs, out_specs=[whole()...  26.5 us
    ppermute x21, starting transfers between devices, paired(): lax.ppermute(block, axis, [(i ^ mask, i) for i in range(lax.axis_size(axi...  18.4 us
    ppermute x10, waiting for transfers between devices, beyond(): return lax.ppermute(block, axis, route)  17.5 us
    ppermute x10, starting transfers between devices, beyond(): return lax.ppermute(block, axis, route)  16.1 us
    ppermute x21, waiting for transfers between devices, paired(): lax.ppermute(block, axis, [(i ^ mask, i) for i in range(lax.axis_size(axi...  10.8 us
    unnamed x23, local copies, waits for them, and re-layouts  2 us
  transfers between devices with their start and end apart: 31, of which 19 were waited for; matrix products, arithmetic and copies ran while one was open for 0% of the time, Pallas kernels for 17%

profile of v11, /device:TPU:0, one launch (start us, length us, event | category | flops | bytes accessed | tf_op | source)
XLA Modules:
  0.0 92.6 jit_solution(6741582891408789327)
XLA Ops:
  0.8 0.7 copy-done.9
  1.5 0.7 copy-done.10
  2.2 4.0 %collective-permute-start.1 = (f32[8,128]{1,0:T(8,128)S(1)}, f32[8,128]{1,0:T(8,128)S(1)}, u32[]{:S(2)}, u32[]{:S(2)}) collective-permute-start(f32[8,128]{1,0:T(8,128)S(1)} %pack.1), channel_id=1, source_target_pairs={{3,0},{2,1},{1,2},{0,3},{7,4},{6,5},{5,6},{4,7},{11,8},{10,9},{9,1... | collective-permute-start | bytes 12296 | tf_op jit(solution)/shard_map/ppermute | solution.py:31
  6.1 0.5 collective-permute-start
  6.7 0.4 prep_first.1
  7.1 0.7 collective-permute-done.1
  7.7 2.0 %collective-permute-done = f32[8,128]{1,0:T(8,128)S(1)} collective-permute-done((f32[8,128]{1,0:T(8,128)S(1)}, f32[8,128]{1,0:T(8,128)S(1)}, u32[]{:S(2)}, u32[]{:S(2)}) %collective-permute-start) | collective-permute-done | bytes 4128 | tf_op jit(solution)/shard_map/ppermute | solution.py:25
  9.8 1.8 %collective-permute-start.3 = (f32[3,8,128]{2,1,0:T(8,128)S(1)}, f32[3,8,128]{2,1,0:T(8,128)S(1)}, u32[]{:S(2)}, u32[]{:S(2)}) collective-permute-start(f32[3,8,128]{2,1,0:T(8,128)S(1)} %pad_maximum_fusion.2.column_ref.cell_ref), channel_id=1, source_target_pairs={{28,0},{8,4},{4,8},{16,12},{12,16},{24,20},{20,24},{0,28},{29,1},{... | collective-permute-start | bytes 36872 | tf_op jit(solution)/shard_map/ppermute | solution.py:31
  11.5 3.1 %collective-permute-done.3.beyond_ref = f32[3,8,128]{2,1,0:T(8,128)S(1)} collective-permute-done((f32[3,8,128]{2,1,0:T(8,128)S(1)}, f32[3,8,128]{2,1,0:T(8,128)S(1)}, u32[]{:S(2)}, u32[]{:S(2)}) %collective-permute-start.3) | collective-permute-done | bytes 12320 | tf_op jit(solution)/shard_map/ppermute | solution.py:31
  14.7 1.3 %first.1 = (bf16[128,256]{1,0:T(8,128)(2,1)S(1)}, f32[8,3072]{1,0:T(8,128)S(1)}, f32[8,3072]{1,0:T(8,128)S(1)}, f32[8,3072]{1,0:T(8,128)S(1)}, f32[3,128,256]{2,1,0:T(8,128)S(1)}, /*index=5*/f32[128,256]{1,0:T(8,128)S(1)}) custom-call(s32[2,8,128]{2,1,0:T(8,128)S(1)} %broadcast_in_dim.4.place_ref, s32[1,3072]{1,0:T(1,128)S(1)} %get-tuple-element.83.ids_ref, ...), custom_call_target="tpu_custom_call" | custom-call | flops 10000000 | bytes 1000000 | tf_op jit(solution)/shard_map/first/pallas_call | solution.py:47
  16.0 1.0 %collective-permute-start.5 = (bf16[128,256]{1,0:T(8,128)(2,1)S(1)}, bf16[128,256]{1,0:T(8,128)(2,1)S(1)}, u32[]{:S(2)}, u32[]{:S(2)}) collective-permute-start(bf16[128,256]{1,0:T(8,128)(2,1)S(1)} %get-tuple-element.101), channel_id=1, source_target_pairs={{3,0},{2,1},{1,2},{0,3},{7,4},{6,5},{5,6},{4,7},{11,8},{10,9},{9,1... | collective-permute-start | bytes 196616 | tf_op jit(solution)/shard_map/ppermute | solution.py:31
  17.0 1.1 %collective-permute-start.4 = (bf16[128,256]{1,0:T(8,128)(2,1)S(1)}, bf16[128,256]{1,0:T(8,128)(2,1)S(1)}, u32[]{:S(2)}, u32[]{:S(2)}) collective-permute-start(bf16[128,256]{1,0:T(8,128)(2,1)S(1)} %get-tuple-element.101), channel_id=1, source_target_pairs={{1,0},{0,1},{3,2},{2,3},{5,4},{4,5},{7,6},{6,7},{9,8},{8,9},{11,10... | collective-permute-start | bytes 196616 | tf_op jit(solution)/shard_map/ppermute | solution.py:25
  18.1 2.1 %hot.1.hot_ref = bf16[1536,3072]{1,0:T(8,128)(2,1)S(1)} custom-call(s32[1,3072]{1,0:T(1,128)S(1)} %get-tuple-element.83.ids_ref), custom_call_target="tpu_custom_call" | custom-call | flops 1000000 | bytes 1000000 | tf_op jit(solution)/shard_map/hot/pallas_call | solution.py:47
  20.2 1.1 %collective-permute-start.6 = (bf16[128,256]{1,0:T(8,128)(2,1)S(1)}, bf16[128,256]{1,0:T(8,128)(2,1)S(1)}, u32[]{:S(2)}, u32[]{:S(2)}) collective-permute-start(bf16[128,256]{1,0:T(8,128)(2,1)S(1)} %get-tuple-element.101), channel_id=1, source_target_pairs={{28,0},{8,4},{4,8},{16,12},{12,16},{24,20},{20,24},{0,28},{29,1},{... | collective-permute-start | bytes 196616 | tf_op jit(solution)/shard_map/ppermute | solution.py:31
  21.3 4.4 %collective-permute-done.6.beyond_ref = bf16[128,256]{1,0:T(8,128)(2,1)S(1)} collective-permute-done((bf16[128,256]{1,0:T(8,128)(2,1)S(1)}, bf16[128,256]{1,0:T(8,128)(2,1)S(1)}, u32[]{:S(2)}, u32[]{:S(2)}) %collective-permute-start.6) | collective-permute-done | bytes 65568 | tf_op jit(solution)/shard_map/ppermute | solution.py:31
  25.8 0.4 prep_second.1
  26.2 1.6 %collective-permute-start.9 = (bf16[128,256]{1,0:T(8,128)(2,1)S(1)}, bf16[128,256]{1,0:T(8,128)(2,1)S(1)}, u32[]{:S(2)}, u32[]{:S(2)}) collective-permute-start(bf16[128,256]{1,0:T(8,128)(2,1)S(1)} %collective-permute-done.6.beyond_ref), channel_id=1, source_target_pairs={{3,0},{2,1},{1,2},{0,3},{7,4},{6,5},{5,6},{4,7},{11,8},{10,9},{9,1... | collective-permute-start | bytes 196616 | tf_op jit(solution)/shard_map/ppermute | solution.py:31
  27.8 1.5 %collective-permute-start.8 = (bf16[128,256]{1,0:T(8,128)(2,1)S(1)}, bf16[128,256]{1,0:T(8,128)(2,1)S(1)}, u32[]{:S(2)}, u32[]{:S(2)}) collective-permute-start(bf16[128,256]{1,0:T(8,128)(2,1)S(1)} %collective-permute-done.6.beyond_ref), channel_id=1, source_target_pairs={{1,0},{0,1},{3,2},{2,3},{5,4},{4,5},{7,6},{6,7},{9,8},{8,9},{11,10... | collective-permute-start | bytes 196616 | tf_op jit(solution)/shard_map/ppermute | solution.py:25
  29.3 3.5 %second_near.1 = (f32[4,128,3072]{2,1,0:T(8,128)S(1)}, f32[128,3072]{1,0:T(8,128)S(1)}, bf16[768,3072]{1,0:T(8,128)(2,1)S(1)}) custom-call(s32[1,3072]{1,0:T(1,128)S(1)} %get-tuple-element.83.ids_ref, f32[8,3072]{1,0:T(8,128)S(1)} %get-tuple-element.90.basis_ref, f32[8,3072]{1,0:T(8,128)S(1)} %get-tuple-element.92.unit_ref, ...), custom_call_target="tpu_custom_call" | custom-call | flops 2000000000 | bytes 1000000 | tf_op jit(solution)/shard_map/second_near/pallas_call | solution.py:47
  32.8 0.8 second_side.1.near_ref
  33.6 1.9 %second.1 = (bf16[128,3072]{1,0:T(8,128)(2,1)S(1)}, f32[3,128,256]{2,1,0:T(8,128)S(1)}, f32[128,256]{1,0:T(8,128)S(1)}, bf16[80,256]{1,0:T(8,128)(2,1)S(1)}, f32...) custom-call(bf16[768,3072]{1,0:T(8,128)(2,1)S(1)} %get-tuple-element.104.hot_ref, ...), custom_call_target="tpu_custom_call" | custom-call | flops 10000000 | bytes 1000000 | tf_op jit(solution)/shard_map/second/pallas_call | solution.py:47
  35.5 1.7 %collective-permute-start.12 = (bf16[80,256]{1,0:T(8,128)(2,1)S(1)}, bf16[80,256]{1,0:T(8,128)(2,1)S(1)}, u32[]{:S(2)}, u32[]{:S(2)}) collective-permute-start(bf16[80,256]{1,0:T(8,128)(2,1)S(1)} %get-tuple-element.110), channel_id=1, source_target_pairs={{24,0},{28,4},{16,8},{20,12},{8,16},{12,20},{0,24},{4,28},{25,1},{... | collective-permute-start | bytes 122888 | tf_op jit(solution)/shard_map/ppermute | solution.py:25
  37.2 2.8 %collective-permute-start.10 = (bf16[80,256]{1,0:T(8,128)(2,1)S(1)}, bf16[80,256]{1,0:T(8,128)(2,1)S(1)}, u32[]{:S(2)}, u32[]{:S(2)}) collective-permute-start(bf16[80,256]{1,0:T(8,128)(2,1)S(1)} %get-tuple-element.110), channel_id=1, source_target_pairs={{8,0},{12,4},{0,8},{4,12},{24,16},{28,20},{16,24},{20,28},{9,1},{1... | collective-permute-start | bytes 122888 | tf_op jit(solution)/shard_map/ppermute | solution.py:25
  40.0 0.8 green.1.refs_0_
  40.8 1.0 %collective-permute-done.12 = bf16[80,256]{1,0:T(8,128)(2,1)S(1)} collective-permute-done((bf16[80,256]{1,0:T(8,128)(2,1)S(1)}, bf16[80,256]{1,0:T(8,128)(2,1)S(1)}, u32[]{:S(2)}, u32[]{:S(2)}) %collective-permute-start.12) | collective-permute-done | bytes 40992 | tf_op jit(solution)/shard_map/ppermute | solution.py:25
  41.7 0.8 collective-permute-done.11
  42.7 1.2 %structure_near.1 = (f32[32,1024]{1,0:T(8,128)S(1)}, f32[32,1024]{1,0:T(8,128)S(1)}, f32[8,1024]{1,0:T(8,128)S(1)}, f32[8,1024]{1,0:T(8,128)S(1)}, bf16[640,1024...) custom-call(s32[2,8,128]{2,1,0:T(8,128)S(1)} %broadcast_in_dim.4.place_ref, ...), custom_call_target="tpu_custom_call" | custom-call | flops 1000000000 | bytes 1000000 | tf_op jit(solution)/shard_map/structure_near/pallas_call | solution.py:47
  43.9 0.2 collective-permute-done.13.blocks.refs_11_
  44.1 1.3 %structure_far.1 = (f32[32,1024]{1,0:T(8,128)S(1)}, f32[32,1024]{1,0:T(8,128)S(1)}, f32[8,1024]{1,0:T(8,128)S(1)}, f32[8,1024]{1,0:T(8,128)S(1)}, bf16[640,1024]...) custom-call(s32[2,8,128]{2,1,0:T(8,128)S(1)} %broadcast_in_dim.4.place_r, ...), custom_call_target="tpu_custom_call" | custom-call | flops 10000000 | bytes 1000000 | tf_op jit(solution)/shard_map/structure_far/pallas_call | solution.py:47
  45.3 1.0 %collective-permute-start.16 = (bf16[320,128]{1,0:T(8,128)(2,1)S(1)}, bf16[320,128]{1,0:T(8,128)(2,1)S(1)}, u32[]{:S(2)}, u32[]{:S(2)}) collective-permute-start(bf16[320,128]{1,0:T(8,128)(2,1)S(1)} %get-tuple-element.114), channel_id=1, source_target_pairs={{3,0},{2,1},{1,2},{0,3},{7,4},{6,5},{5,6},{4,7},{11,8},{10,9},{9,1... | collective-permute-start | bytes 245768 | tf_op jit(solution)/shard_map/ppermute | solution.py:25
  46.3 1.1 %collective-permute-start.15 = (bf16[320,128]{1,0:T(8,128)(2,1)S(1)}, bf16[320,128]{1,0:T(8,128)(2,1)S(1)}, u32[]{:S(2)}, u32[]{:S(2)}) collective-permute-start(bf16[320,128]{1,0:T(8,128)(2,1)S(1)} %get-tuple-element.114), channel_id=1, source_target_pairs={{2,0},{3,1},{0,2},{1,3},{6,4},{7,5},{4,6},{5,7},{10,8},{11,9},{8,1... | collective-permute-start | bytes 245768 | tf_op jit(solution)/shard_map/ppermute | solution.py:25
  47.4 1.5 %collective-permute-start.14 = (bf16[320,128]{1,0:T(8,128)(2,1)S(1)}, bf16[320,128]{1,0:T(8,128)(2,1)S(1)}, u32[]{:S(2)}, u32[]{:S(2)}) collective-permute-start(bf16[320,128]{1,0:T(8,128)(2,1)S(1)} %get-tuple-element.114), channel_id=1, source_target_pairs={{1,0},{0,1},{3,2},{2,3},{5,4},{4,5},{7,6},{6,7},{9,8},{8,9},{11,10... | collective-permute-start | bytes 245768 | tf_op jit(solution)/shard_map/ppermute | solution.py:25
  48.9 2.8 %hot_back.1.hot_ref = bf16[3072,2304]{1,0:T(8,128)(2,1)S(1)} custom-call(s32[1,3072]{1,0:T(1,128)S(1)} %get-tuple-element.83.ids_ref), custom_call_target="tpu_custom_call" | custom-call | flops 2000000000 | bytes 1000000 | tf_op jit(solution)/shard_map/hot_back/pallas_call | solution.py:47
  51.7 0.7 collective-permute-done.15.refs_3_
  52.5 1.5 %fold_far.1 = (bf16[4,80,256]{2,1,0:T(8,128)(2,1)S(1)}, f32[640,64]{1,0:T(8,128)S(1)}) custom-call(s32[2,8,128]{2,1,0:T(8,128)S(1)} %broadcast_in_dim.4.place_ref, f32[320,128]{1,0:T(8,128)S(1)} %green.1.refs_0_, f32[320,128]{1,0:T(8,128)S(1)} %get-tuple-element.128.refs_1_, bf16[320,128]{1,0:T(8,128)(2,1)S(1)} %collective-permute-done.14.refs_2_, ...), custom_call_target="tpu_custom_call" | custom-call | flops 10000000 | bytes 1000000 | tf_op jit(solution)/shard_map/fold_far/pallas_call | solution.py:47
  54.1 1.2 %fold_near.1.near_ref = f32[4,80,256]{2,1,0:T(8,128)S(1)} custom-call(s32[2,8,128]{2,1,0:T(8,128)S(1)} %broadcast_in_dim.4.place_ref, f32[640,64]{1,0:T(8,128)S(1)} %get-tuple-element.138.refs_0_, f32[32,1024]{1,0:T(8,128)S(1)} %get-tuple-element.139.refs_1_, f32[32,1024]{1,0:T(8,128)S(1)} %get-tuple-element.140.refs_2_, ...), custom_call_target="tpu_custom_call" | custom-call | flops 1000000000 | bytes 1000000 | tf_op jit(solution)/shard_map/fold_near/pallas_call | solution.py:47
  55.3 0.1 collective-permute-done.17.far_ref
  55.5 1.5 %collective-permute-start.18 = (bf16[80,256]{1,0:T(8,128)(2,1)S(1)}, bf16[80,256]{1,0:T(8,128)(2,1)S(1)}, u32[]{:S(2)}, u32[]{:S(2)}) collective-permute-start(bf16[80,256]{1,0:T(8,128)(2,1)S(1)} %get-tuple-element.147), channel_id=1, source_target_pairs={{8,0},{12,4},{0,8},{4,12},{24,16},{28,20},{16,24},{20,28},{9,1},{1... | collective-permute-start | bytes 122888 | tf_op jit(solution)/shard_map/ppermute | solution.py:25
  57.0 0.9 %collective-permute-start.19 = (bf16[80,256]{1,0:T(8,128)(2,1)S(1)}, bf16[80,256]{1,0:T(8,128)(2,1)S(1)}, u32[]{:S(2)}, u32[]{:S(2)}) collective-permute-start(bf16[80,256]{1,0:T(8,128)(2,1)S(1)} %get-tuple-element.148), channel_id=1, source_target_pairs={{16,0},{20,4},{24,8},{28,12},{0,16},{4,20},{8,24},{12,28},{17,1},{... | collective-permute-start | bytes 122888 | tf_op jit(solution)/shard_map/ppermute | solution.py:25
  58.0 2.0 %collective-permute-start.20 = (bf16[80,256]{1,0:T(8,128)(2,1)S(1)}, bf16[80,256]{1,0:T(8,128)(2,1)S(1)}, u32[]{:S(2)}, u32[]{:S(2)}) collective-permute-start(bf16[80,256]{1,0:T(8,128)(2,1)S(1)} %get-tuple-element.149), channel_id=1, source_target_pairs={{24,0},{28,4},{16,8},{20,12},{8,16},{12,20},{0,24},{4,28},{25,1},{... | collective-permute-start | bytes 122888 | tf_op jit(solution)/shard_map/ppermute | solution.py:25
  60.0 0.5 readout.1
  60.6 2.7 %collective-permute-done.19.refs_2_ = bf16[80,256]{1,0:T(8,128)(2,1)S(1)} collective-permute-done((bf16[80,256]{1,0:T(8,128)(2,1)S(1)}, bf16[80,256]{1,0:T(8,128)(2,1)S(1)}, u32[]{:S(2)}, u32[]{:S(2)}) %collective-permute-start.19) | collective-permute-done | bytes 40992 | tf_op jit(solution)/shard_map/ppermute | solution.py:25
  63.2 0.7 collective-permute-done.20.refs_3_
  63.9 3.1 %second_back.1 = (f32[1,1,256]{2,1,0:T(1,128)}, f32[8,256]{1,0:T(8,128)S(1)}, f32[128,256]{1,0:T(8,128)S(1)}, f32[4,128,256]{2,1,0:T(8,128)S(1)}, bf16[128,3072]...) custom-call(bf16[3072,2304]{1,0:T(8,128)(2,1)S(1)} %hot_back.1.hot_r, ...), custom_call_target="tpu_custom_call" | custom-call | flops 10000000 | bytes 1000000 | tf_op jit(solution)/shard_map/second_back/pallas_call | solution.py:47
  66.9 0.9 collective-permute-start.22
  67.8 1.5 %collective-permute-start.23 = (bf16[128,256]{1,0:T(8,128)(2,1)S(1)}, bf16[128,256]{1,0:T(8,128)(2,1)S(1)}, u32[]{:S(2)}, u32[]{:S(2)}) collective-permute-start(bf16[128,256]{1,0:T(8,128)(2,1)S(1)} %get-tuple-element.157), channel_id=1, source_target_pairs={{3,0},{2,1},{1,2},{0,3},{7,4},{6,5},{5,6},{4,7},{11,8},{10,9},{9,1... | collective-permute-start | bytes 196616 | tf_op jit(solution)/shard_map/ppermute | solution.py:31
  69.3 0.8 second_middle.1.middle_ref
  70.1 1.1 %collective-permute-done.22 = bf16[128,256]{1,0:T(8,128)(2,1)S(1)} collective-permute-done((bf16[128,256]{1,0:T(8,128)(2,1)S(1)}, bf16[128,256]{1,0:T(8,128)(2,1)S(1)}, u32[]{:S(2)}, u32[]{:S(2)}) %collective-permute-start.22) | collective-permute-done | bytes 65568 | tf_op jit(solution)/shard_map/ppermute | solution.py:25
  71.2 1.8 %collective-permute-done.23 = bf16[128,256]{1,0:T(8,128)(2,1)S(1)} collective-permute-done((bf16[128,256]{1,0:T(8,128)(2,1)S(1)}, bf16[128,256]{1,0:T(8,128)(2,1)S(1)}, u32[]{:S(2)}, u32[]{:S(2)}) %collective-permute-start.23) | collective-permute-done | bytes 65568 | tf_op jit(solution)/shard_map/ppermute | solution.py:31
  73.1 1.5 %collective-permute-start.26 = (bf16[128,256]{1,0:T(8,128)(2,1)S(1)}, bf16[128,256]{1,0:T(8,128)(2,1)S(1)}, u32[]{:S(2)}, u32[]{:S(2)}) collective-permute-start(bf16[128,256]{1,0:T(8,128)(2,1)S(1)} %get-tuple-element.164), channel_id=1, source_target_pairs={{3,0},{2,1},{1,2},{0,3},{7,4},{6,5},{5,6},{4,7},{11,8},{10,9},{9,1... | collective-permute-start | bytes 196616 | tf_op jit(solution)/shard_map/ppermute | solution.py:31
  74.7 0.9 collective-permute-start.25
  75.5 1.2 %second_edge.1.edge_ref = f32[32,3072]{1,0:T(8,128)S(1)} custom-call(bf16[2,16,256]{2,1,0:T(8,128)(2,1)S(1)} %get-tuple-element.99.back_ref, bf16[128,3072]{1,0:T(8,128)(2,1)S(1)} %get-tuple-element.109.feature_ref, f32[4,128,256]{2,1,0:T(8,128)S(1)} %get-tuple-element.150.grad_ref), custom_call_target="tpu_custom_call" | custom-call | flops 1000000000 | bytes 1000000 | tf_op jit(solution)/shard_map/second_edge/pallas_call | solution.py:47
  76.7 1.8 %collective-permute-done.24.refs_1_ = bf16[128,256]{1,0:T(8,128)(2,1)S(1)} collective-permute-done((bf16[128,256]{1,0:T(8,128)(2,1)S(1)}, bf16[128,256]{1,0:T(8,128)(2,1)S(1)}, u32[]{:S(2)}, u32[]{:S(2)}) %collective-permute-start.24) | collective-permute-done | bytes 65568 | tf_op jit(solution)/shard_map/ppermute | solution.py:31
  78.6 0.5 collective-permute-done.26.refs_3_
  79.1 0.7 collective-permute-done.25.refs_2_
  79.8 1.5 %first_back.1 = (f32[3,8,256]{2,1,0:T(8,128)S(1)}, f32[3,8,256]{2,1,0:T(8,128)S(1)}, f32[3,8,256]{2,1,0:T(8,128)S(1)}) custom-call(s32[1,3072]{1,0:T(1,128)S(1)} %get-tuple-element.83.ids_ref, f32[8,3072]{1,0:T(8,128)S(1)} %get-tuple-element.90.basis_ref, f32[8,3072]{1,0:T(8,128)S(1)} %get-tuple-element.91.slope_ref, ...), custom_call_target="tpu_custom_call" | custom-call | flops 10000000 | bytes 1000000 | tf_op jit(solution)/shard_map/first_back/pallas_call | solution.py:47
  81.3 0.1 collective-permute-start.27
  81.4 1.9 %collective-permute-start.28 = (f32[3,8,256]{2,1,0:T(8,128)S(1)}, f32[3,8,256]{2,1,0:T(8,128)S(1)}, u32[]{:S(2)}, u32[]{:S(2)}) collective-permute-start(f32[3,8,256]{2,1,0:T(8,128)S(1)} %get-tuple-element.160), channel_id=1, source_target_pairs={{28,0},{8,4},{4,8},{16,12},{12,16},{24,20},{20,24},{0,28},{29,1},{... | collective-permute-start | bytes 73736 | tf_op jit(solution)/shard_map/ppermute | solution.py:31
  83.3 3.2 %collective-permute-done.28 = f32[3,8,256]{2,1,0:T(8,128)S(1)} collective-permute-done((f32[3,8,256]{2,1,0:T(8,128)S(1)}, f32[3,8,256]{2,1,0:T(8,128)S(1)}, u32[]{:S(2)}, u32[]{:S(2)}) %collective-permute-start.28) | collective-permute-done | bytes 24608 | tf_op jit(solution)/shard_map/ppermute | solution.py:31
  86.5 1.8 %collective-permute-start.30 = (f32[8,256]{1,0:T(8,128)S(1)}, f32[8,256]{1,0:T(8,128)S(1)}, u32[]{:S(2)}, u32[]{:S(2)}) collective-permute-start(f32[8,256]{1,0:T(8,128)S(1)} %get-tuple-element.167), channel_id=1, source_target_pairs={{3,0},{2,1},{1,2},{0,3},{7,4},{6,5},{5,6},{4,7},{11,8},{10,9},{9,1... | collective-permute-start | bytes 24584 | tf_op jit(solution)/shard_map/ppermute | solution.py:31
  88.3 0.9 collective-permute-start.29
  89.2 2.0 %collective-permute-done.30 = f32[8,256]{1,0:T(8,128)S(1)} collective-permute-done((f32[8,256]{1,0:T(8,128)S(1)}, f32[8,256]{1,0:T(8,128)S(1)}, u32[]{:S(2)}, u32[]{:S(2)}) %collective-permute-start.30) | collective-permute-done | bytes 8224 | tf_op jit(solution)/shard_map/ppermute | solution.py:31
  91.1 0.8 collective-permute-done.29
  92.0 0.6 copy.13
  (51 shorter events, 0.7 us)
Async XLA Ops:
  0.8 0.7 copy-start.9
  1.5 0.7 copy-start.10
  2.1 4.5 %copy-start = (f32[2,2,128,128]{3,2,1,0:T(8,128)S(1)}, f32[2,2,128,128]{3,2,1,0:T(8,128)}, u32[]{:S(2)}) copy-start(f32[2,2,128,128]{3,2,1,0:T(8,128)} %mixing_in.1) | copy-start | bytes 786436
  2.2 4.5 %copy-start.4 = (f32[2,2,8,128]{3,2,1,0:T(8,128)S(1)}, f32[2,2,8,128]{3,2,1,0:T(8,128)}, u32[]{:S(2)}) copy-start(f32[2,2,8,128]{3,2,1,0:T(8,128)} %radial_in.1) | copy-start | bytes 49156
  2.2 4.5 %copy-start.5 = (s32[1,1,256,12]{2,1,3,0:T(1,128)S(1)}, s32[1,1,256,12]{2,1,3,0:T(1,128)}, u32[]{:S(2)}) copy-start(s32[1,1,256,12]{2,1,3,0:T(1,128)} %param.13) | copy-start | bytes 36868
  2.2 4.5 %copy-start.6 = (f32[6,128]{1,0:T(8,128)S(1)}, f32[6,128]{1,0:T(8,128)}, u32[]{:S(2)}) copy-start(f32[6,128]{1,0:T(8,128)} %embed_in.1) | copy-start | bytes 9220
  2.2 4.5 %copy-start.7 = (s32[1,1,256]{2,1,0:T(1,128)S(1)}, s32[1,1,256]{2,1,0:T(1,128)}, u32[]{:S(2)}) copy-start(s32[1,1,256]{2,1,0:T(1,128)} %count_in.1) | copy-start | bytes 3076
  2.2 5.5 %collective-permute-start.1 = (f32[8,128]{1,0:T(8,128)S(1)}, f32[8,128]{1,0:T(8,128)S(1)}, u32[]{:S(2)}, u32[]{:S(2)}) collective-permute-start(f32[8,128]{1,0:T(8,128)S(1)} %pack.1), channel_id=1, source_target_pairs={{3,0},{2,1},{1,2},{0,3},{7,4},{6,5},{5,6},{4,7},{11,8},{10,9},{9,1... | collective-permute-start | bytes 12296 | tf_op jit(solution)/shard_map/ppermute | solution.py:31
  6.1 3.6 %collective-permute-start = (f32[8,128]{1,0:T(8,128)S(1)}, f32[8,128]{1,0:T(8,128)S(1)}, u32[]{:S(2)}, u32[]{:S(2)}) collective-permute-start(f32[8,128]{1,0:T(8,128)S(1)} %pack.1), channel_id=1, source_target_pairs={{1,0},{0,1},{3,2},{2,3},{5,4},{4,5},{7,6},{6,7},{9,8},{8,9},{11,10... | collective-permute-start | bytes 12296 | tf_op jit(solution)/shard_map/ppermute | solution.py:25
  9.8 4.9 %collective-permute-start.3 = (f32[3,8,128]{2,1,0:T(8,128)S(1)}, f32[3,8,128]{2,1,0:T(8,128)S(1)}, u32[]{:S(2)}, u32[]{:S(2)}) collective-permute-start(f32[3,8,128]{2,1,0:T(8,128)S(1)} %pad_maximum_fusion.2.column_ref.cell_ref), channel_id=1, source_target_pairs={{28,0},{8,4},{4,8},{16,12},{12,16},{24,20},{20,24},{0,28},{29,1},{... | collective-permute-start | bytes 36872 | tf_op jit(solution)/shard_map/ppermute | solution.py:31
  11.5 3.1 %collective-permute-start.2 = (f32[3,8,128]{2,1,0:T(8,128)S(1)}, f32[3,8,128]{2,1,0:T(8,128)S(1)}, u32[]{:S(2)}, u32[]{:S(2)}) collective-permute-start(f32[3,8,128]{2,1,0:T(8,128)S(1)} %pad_maximum_fusion.2.column_ref.cell_ref), channel_id=1, source_target_pairs={{4,0},{0,4},{12,8},{8,12},{20,16},{16,20},{28,24},{24,28},{5,1},{1... | collective-permute-start | bytes 36872 | tf_op jit(solution)/shard_map/ppermute | solution.py:25
  16.0 9.7 %copy-start.1 = (f32[128,128]{1,0:T(8,128)S(1)}, f32[128,128]{1,0:T(8,128)}, u32[]{:S(2)}) copy-start(f32[128,128]{1,0:T(8,128)} %hidden_in.1) | copy-start | bytes 196612
  16.0 9.7 %copy-start.3 = (f32[128,64]{0,1:T(8,128)S(1)}, f32[128,64]{0,1:T(8,128)}, u32[]{:S(2)}) copy-start(f32[128,64]{0,1:T(8,128)} %param.20) | copy-start | bytes 98308
  16.0 9.7 %copy-start.8 = (f32[128]{0:T(128)S(1)}, f32[128]{0:T(128)}, u32[]{:S(2)}) copy-start(f32[128]{0:T(128)} %param.19) | copy-start | bytes 1540
  16.0 5.3 %collective-permute-start.5 = (bf16[128,256]{1,0:T(8,128)(2,1)S(1)}, bf16[128,256]{1,0:T(8,128)(2,1)S(1)}, u32[]{:S(2)}, u32[]{:S(2)}) collective-permute-start(bf16[128,256]{1,0:T(8,128)(2,1)S(1)} %get-tuple-element.101), channel_id=1, source_target_pairs={{3,0},{2,1},{1,2},{0,3},{7,4},{6,5},{5,6},{4,7},{11,8},{10,9},{9,1... | collective-permute-start | bytes 196616 | tf_op jit(solution)/shard_map/ppermute | solution.py:31
  17.0 4.3 %collective-permute-start.4 = (bf16[128,256]{1,0:T(8,128)(2,1)S(1)}, bf16[128,256]{1,0:T(8,128)(2,1)S(1)}, u32[]{:S(2)}, u32[]{:S(2)}) collective-permute-start(bf16[128,256]{1,0:T(8,128)(2,1)S(1)} %get-tuple-element.101), channel_id=1, source_target_pairs={{1,0},{0,1},{3,2},{2,3},{5,4},{4,5},{7,6},{6,7},{9,8},{8,9},{11,10... | collective-permute-start | bytes 196616 | tf_op jit(solution)/shard_map/ppermute | solution.py:25
  20.2 5.6 %collective-permute-start.6 = (bf16[128,256]{1,0:T(8,128)(2,1)S(1)}, bf16[128,256]{1,0:T(8,128)(2,1)S(1)}, u32[]{:S(2)}, u32[]{:S(2)}) collective-permute-start(bf16[128,256]{1,0:T(8,128)(2,1)S(1)} %get-tuple-element.101), channel_id=1, source_target_pairs={{28,0},{8,4},{4,8},{16,12},{12,16},{24,20},{20,24},{0,28},{29,1},{... | collective-permute-start | bytes 196616 | tf_op jit(solution)/shard_map/ppermute | solution.py:31
  25.7 7.1 %collective-permute-start.7 = (bf16[3,128,256]{2,1,0:T(8,128)(2,1)S(1)}, bf16[3,128,256]{2,1,0:T(8,128)(2,1)S(1)}, u32[]{:S(2)}, u32[]{:S(2)}) collective-permute-start(bf16[3,128,256]{2,1,0:T(8,128)(2,1)S(1)} %pad_maximum_fusion.column_ref), channel_id=1, source_target_pairs={{4,0},{0,4},{12,8},{8,12},{20,16},{16,20},{28,24},{24,28},{5,1},{1... | collective-permute-start | bytes 589832 | tf_op jit(solution)/shard_map/ppermute | solution.py:25
  26.2 7.4 %collective-permute-start.9 = (bf16[128,256]{1,0:T(8,128)(2,1)S(1)}, bf16[128,256]{1,0:T(8,128)(2,1)S(1)}, u32[]{:S(2)}, u32[]{:S(2)}) collective-permute-start(bf16[128,256]{1,0:T(8,128)(2,1)S(1)} %collective-permute-done.6.beyond_ref), channel_id=1, source_target_pairs={{3,0},{2,1},{1,2},{0,3},{7,4},{6,5},{5,6},{4,7},{11,8},{10,9},{9,1... | collective-permute-start | bytes 196616 | tf_op jit(solution)/shard_map/ppermute | solution.py:31
  27.8 5.8 %collective-permute-start.8 = (bf16[128,256]{1,0:T(8,128)(2,1)S(1)}, bf16[128,256]{1,0:T(8,128)(2,1)S(1)}, u32[]{:S(2)}, u32[]{:S(2)}) collective-permute-start(bf16[128,256]{1,0:T(8,128)(2,1)S(1)} %collective-permute-done.6.beyond_ref), channel_id=1, source_target_pairs={{1,0},{0,1},{3,2},{2,3},{5,4},{4,5},{7,6},{6,7},{9,8},{8,9},{11,10... | collective-permute-start | bytes 196616 | tf_op jit(solution)/shard_map/ppermute | solution.py:25
  33.6 6.4 %copy-start.2 = (s32[3,4096]{1,0:T(4,128)S(1)}, s32[3,4096]{1,0:T(4,128)}, u32[]{:S(2)}) copy-start(s32[3,4096]{1,0:T(4,128)} %vec_ref.1) | copy-start | bytes 147460
  35.5 6.2 %collective-permute-start.12 = (bf16[80,256]{1,0:T(8,128)(2,1)S(1)}, bf16[80,256]{1,0:T(8,128)(2,1)S(1)}, u32[]{:S(2)}, u32[]{:S(2)}) collective-permute-start(bf16[80,256]{1,0:T(8,128)(2,1)S(1)} %get-tuple-element.110), channel_id=1, source_target_pairs={{24,0},{28,4},{16,8},{20,12},{8,16},{12,20},{0,24},{4,28},{25,1},{... | collective-permute-start | bytes 122888 | tf_op jit(solution)/shard_map/ppermute | solution.py:25
  37.2 5.4 %collective-permute-start.11 = (bf16[80,256]{1,0:T(8,128)(2,1)S(1)}, bf16[80,256]{1,0:T(8,128)(2,1)S(1)}, u32[]{:S(2)}, u32[]{:S(2)}) collective-permute-start(bf16[80,256]{1,0:T(8,128)(2,1)S(1)} %get-tuple-element.110), channel_id=1, source_target_pairs={{16,0},{20,4},{24,8},{28,12},{0,16},{4,20},{8,24},{12,28},{17,1},{... | collective-permute-start | bytes 122888 | tf_op jit(solution)/shard_map/ppermute | solution.py:25
  37.2 5.4 %collective-permute-start.10 = (bf16[80,256]{1,0:T(8,128)(2,1)S(1)}, bf16[80,256]{1,0:T(8,128)(2,1)S(1)}, u32[]{:S(2)}, u32[]{:S(2)}) collective-permute-start(bf16[80,256]{1,0:T(8,128)(2,1)S(1)} %get-tuple-element.110), channel_id=1, source_target_pairs={{8,0},{12,4},{0,8},{4,12},{24,16},{28,20},{16,24},{20,28},{9,1},{1... | collective-permute-start | bytes 122888 | tf_op jit(solution)/shard_map/ppermute | solution.py:25
  42.6 1.5 %collective-permute-start.13 = (bf16[4,80,256]{2,1,0:T(8,128)(2,1)S(1)}, bf16[4,80,256]{2,1,0:T(8,128)(2,1)S(1)}, u32[]{:S(2)}, u32[]{:S(2)}) collective-permute-start(bf16[4,80,256]{2,1,0:T(8,128)(2,1)S(1)} %pad_maximum_fusion.1.blocks.refs_7_), channel_id=1, source_target_pairs={{4,0},{0,4},{12,8},{8,12},{20,16},{16,20},{28,24},{24,28},{5,1},{1... | collective-permute-start | bytes 491528 | tf_op jit(solution)/shard_map/ppermute | solution.py:25
  45.3 6.4 %collective-permute-start.16 = (bf16[320,128]{1,0:T(8,128)(2,1)S(1)}, bf16[320,128]{1,0:T(8,128)(2,1)S(1)}, u32[]{:S(2)}, u32[]{:S(2)}) collective-permute-start(bf16[320,128]{1,0:T(8,128)(2,1)S(1)} %get-tuple-element.114), channel_id=1, source_target_pairs={{3,0},{2,1},{1,2},{0,3},{7,4},{6,5},{5,6},{4,7},{11,8},{10,9},{9,1... | collective-permute-start | bytes 245768 | tf_op jit(solution)/shard_map/ppermute | solution.py:25
  46.3 6.2 %collective-permute-start.15 = (bf16[320,128]{1,0:T(8,128)(2,1)S(1)}, bf16[320,128]{1,0:T(8,128)(2,1)S(1)}, u32[]{:S(2)}, u32[]{:S(2)}) collective-permute-start(bf16[320,128]{1,0:T(8,128)(2,1)S(1)} %get-tuple-element.114), channel_id=1, source_target_pairs={{2,0},{3,1},{0,2},{1,3},{6,4},{7,5},{4,6},{5,7},{10,8},{11,9},{8,1... | collective-permute-start | bytes 245768 | tf_op jit(solution)/shard_map/ppermute | solution.py:25
  47.4 5.1 %collective-permute-start.14 = (bf16[320,128]{1,0:T(8,128)(2,1)S(1)}, bf16[320,128]{1,0:T(8,128)(2,1)S(1)}, u32[]{:S(2)}, u32[]{:S(2)}) collective-permute-start(bf16[320,128]{1,0:T(8,128)(2,1)S(1)} %get-tuple-element.114), channel_id=1, source_target_pairs={{1,0},{0,1},{3,2},{2,3},{5,4},{4,5},{7,6},{6,7},{9,8},{8,9},{11,10... | collective-permute-start | bytes 245768 | tf_op jit(solution)/shard_map/ppermute | solution.py:25
  54.0 1.5 %collective-permute-start.17 = (bf16[4,80,256]{2,1,0:T(8,128)(2,1)S(1)}, bf16[4,80,256]{2,1,0:T(8,128)(2,1)S(1)}, u32[]{:S(2)}, u32[]{:S(2)}) collective-permute-start(bf16[4,80,256]{2,1,0:T(8,128)(2,1)S(1)} %get-tuple-element.145), channel_id=1, source_target_pairs={{4,0},{0,4},{12,8},{8,12},{20,16},{16,20},{28,24},{24,28},{5,1},{1... | collective-permute-start | bytes 491528 | tf_op jit(solution)/shard_map/ppermute | solution.py:25
  55.5 5.0 %collective-permute-start.18 = (bf16[80,256]{1,0:T(8,128)(2,1)S(1)}, bf16[80,256]{1,0:T(8,128)(2,1)S(1)}, u32[]{:S(2)}, u32[]{:S(2)}) collective-permute-start(bf16[80,256]{1,0:T(8,128)(2,1)S(1)} %get-tuple-element.147), channel_id=1, source_target_pairs={{8,0},{12,4},{0,8},{4,12},{24,16},{28,20},{16,24},{20,28},{9,1},{1... | collective-permute-start | bytes 122888 | tf_op jit(solution)/shard_map/ppermute | solution.py:25
  57.0 6.2 %collective-permute-start.19 = (bf16[80,256]{1,0:T(8,128)(2,1)S(1)}, bf16[80,256]{1,0:T(8,128)(2,1)S(1)}, u32[]{:S(2)}, u32[]{:S(2)}) collective-permute-start(bf16[80,256]{1,0:T(8,128)(2,1)S(1)} %get-tuple-element.148), channel_id=1, source_target_pairs={{16,0},{20,4},{24,8},{28,12},{0,16},{4,20},{8,24},{12,28},{17,1},{... | collective-permute-start | bytes 122888 | tf_op jit(solution)/shard_map/ppermute | solution.py:25
  58.0 5.9 %collective-permute-start.20 = (bf16[80,256]{1,0:T(8,128)(2,1)S(1)}, bf16[80,256]{1,0:T(8,128)(2,1)S(1)}, u32[]{:S(2)}, u32[]{:S(2)}) collective-permute-start(bf16[80,256]{1,0:T(8,128)(2,1)S(1)} %get-tuple-element.149), channel_id=1, source_target_pairs={{24,0},{28,4},{16,8},{20,12},{8,16},{12,20},{0,24},{4,28},{25,1},{... | collective-permute-start | bytes 122888 | tf_op jit(solution)/shard_map/ppermute | solution.py:25
  66.9 4.3 %collective-permute-start.22 = (bf16[128,256]{1,0:T(8,128)(2,1)S(1)}, bf16[128,256]{1,0:T(8,128)(2,1)S(1)}, u32[]{:S(2)}, u32[]{:S(2)}) collective-permute-start(bf16[128,256]{1,0:T(8,128)(2,1)S(1)} %get-tuple-element.156), channel_id=1, source_target_pairs={{1,0},{0,1},{3,2},{2,3},{5,4},{4,5},{7,6},{6,7},{9,8},{8,9},{11,10... | collective-permute-start | bytes 196616 | tf_op jit(solution)/shard_map/ppermute | solution.py:25
  67.8 5.2 %collective-permute-start.23 = (bf16[128,256]{1,0:T(8,128)(2,1)S(1)}, bf16[128,256]{1,0:T(8,128)(2,1)S(1)}, u32[]{:S(2)}, u32[]{:S(2)}) collective-permute-start(bf16[128,256]{1,0:T(8,128)(2,1)S(1)} %get-tuple-element.157), channel_id=1, source_target_pairs={{3,0},{2,1},{1,2},{0,3},{7,4},{6,5},{5,6},{4,7},{11,8},{10,9},{9,1... | collective-permute-start | bytes 196616 | tf_op jit(solution)/shard_map/ppermute | solution.py:31
  69.3 3.8 %collective-permute-start.21 = (bf16[3,128,256]{2,1,0:T(8,128)(2,1)S(1)}, bf16[3,128,256]{2,1,0:T(8,128)(2,1)S(1)}, u32[]{:S(2)}, u32[]{:S(2)}) collective-permute-start(bf16[3,128,256]{2,1,0:T(8,128)(2,1)S(1)} %get-tuple-element.154), channel_id=1, source_target_pairs={{4,0},{0,4},{12,8},{8,12},{20,16},{16,20},{28,24},{24,28},{5,1},{1... | collective-permute-start | bytes 589832 | tf_op jit(solution)/shard_map/ppermute | solution.py:25
  73.0 5.6 %collective-permute-start.24 = (bf16[128,256]{1,0:T(8,128)(2,1)S(1)}, bf16[128,256]{1,0:T(8,128)(2,1)S(1)}, u32[]{:S(2)}, u32[]{:S(2)}) collective-permute-start(bf16[128,256]{1,0:T(8,128)(2,1)S(1)} %add_convert_fusion), channel_id=1, source_target_pairs={{28,0},{8,4},{4,8},{16,12},{12,16},{24,20},{20,24},{0,28},{29,1},{... | collective-permute-start | bytes 196616 | tf_op jit(solution)/shard_map/ppermute | solution.py:31
  73.1 5.9 %collective-permute-start.26 = (bf16[128,256]{1,0:T(8,128)(2,1)S(1)}, bf16[128,256]{1,0:T(8,128)(2,1)S(1)}, u32[]{:S(2)}, u32[]{:S(2)}) collective-permute-start(bf16[128,256]{1,0:T(8,128)(2,1)S(1)} %get-tuple-element.164), channel_id=1, source_target_pairs={{3,0},{2,1},{1,2},{0,3},{7,4},{6,5},{5,6},{4,7},{11,8},{10,9},{9,1... | collective-permute-start | bytes 196616 | tf_op jit(solution)/shard_map/ppermute | solution.py:31
  74.7 5.1 %collective-permute-start.25 = (bf16[128,256]{1,0:T(8,128)(2,1)S(1)}, bf16[128,256]{1,0:T(8,128)(2,1)S(1)}, u32[]{:S(2)}, u32[]{:S(2)}) collective-permute-start(bf16[128,256]{1,0:T(8,128)(2,1)S(1)} %get-tuple-element.165), channel_id=1, source_target_pairs={{1,0},{0,1},{3,2},{2,3},{5,4},{4,5},{7,6},{6,7},{9,8},{8,9},{11,10... | collective-permute-start | bytes 196616 | tf_op jit(solution)/shard_map/ppermute | solution.py:25
  81.3 2.0 %collective-permute-start.27 = (f32[3,8,256]{2,1,0:T(8,128)S(1)}, f32[3,8,256]{2,1,0:T(8,128)S(1)}, u32[]{:S(2)}, u32[]{:S(2)}) collective-permute-start(f32[3,8,256]{2,1,0:T(8,128)S(1)} %get-tuple-element.159), channel_id=1, source_target_pairs={{4,0},{0,4},{12,8},{8,12},{20,16},{16,20},{28,24},{24,28},{5,1},{1... | collective-permute-start | bytes 73736 | tf_op jit(solution)/shard_map/ppermute | solution.py:25
  81.4 5.1 %collective-permute-start.28 = (f32[3,8,256]{2,1,0:T(8,128)S(1)}, f32[3,8,256]{2,1,0:T(8,128)S(1)}, u32[]{:S(2)}, u32[]{:S(2)}) collective-permute-start(f32[3,8,256]{2,1,0:T(8,128)S(1)} %get-tuple-element.160), channel_id=1, source_target_pairs={{28,0},{8,4},{4,8},{16,12},{12,16},{24,20},{20,24},{0,28},{29,1},{... | collective-permute-start | bytes 73736 | tf_op jit(solution)/shard_map/ppermute | solution.py:31
  86.5 4.6 %collective-permute-start.30 = (f32[8,256]{1,0:T(8,128)S(1)}, f32[8,256]{1,0:T(8,128)S(1)}, u32[]{:S(2)}, u32[]{:S(2)}) collective-permute-start(f32[8,256]{1,0:T(8,128)S(1)} %get-tuple-element.167), channel_id=1, source_target_pairs={{3,0},{2,1},{1,2},{0,3},{7,4},{6,5},{5,6},{4,7},{11,8},{10,9},{9,1... | collective-permute-start | bytes 24584 | tf_op jit(solution)/shard_map/ppermute | solution.py:31
  88.3 3.7 %collective-permute-start.29 = (f32[8,256]{1,0:T(8,128)S(1)}, f32[8,256]{1,0:T(8,128)S(1)}, u32[]{:S(2)}, u32[]{:S(2)}) collective-permute-start(f32[8,256]{1,0:T(8,128)S(1)} %get-tuple-element.168), channel_id=1, source_target_pairs={{1,0},{0,1},{3,2},{2,3},{5,4},{4,5},{7,6},{6,7},{9,8},{8,9},{11,10... | collective-permute-start | bytes 24584 | tf_op jit(solution)/shard_map/ppermute | solution.py:25

commit v12 on v10

--- a/solution.py
+++ b/solution.py
@@ -408,9 +408,9 @@
     folds, refs = refs[:count], refs[count:]
     site_ref, long_ref, cotangent_ref, grad_ref, term_ref, sides_ref, beyond_ref, pair_ref = refs
     atoms = gate_ref.shape[1]
-    total = folds[0][...].astype(F32)
+    total = folds[0][0].astype(F32)
     for part in folds[1:]:
-        total = total + part[...].astype(F32)
+        total = total + part[0].astype(F32)
     wide = full_charge_ref.shape[0]
     potential = total[:wide] * (2.0 * scale)
     slopes = total[wide : wide + 3] + total[wide + 3 : wide + 6] + total[wide + 6 : wide + 9]
@@ -735,15 +735,15 @@
     return block[:wide], slopes
 
 
-def join_kernel(wide, near_ref, far_ref, own_ref, *outs):
-    for d in range(near_ref.shape[0]):
-        pot, slopes = unpieced(near_ref[d], wide)
-        pot_far, slopes_far = unpieced(far_ref[d].astype(F32), wide)
-        block = pieced(pot + pot_far, slopes + slopes_far, near_ref.shape[1])
-        if d:
-            outs[d - 1][...] = block.astype(BF16)
+def join_kernel(wide, kept_ref, come_ref, keep_ref, send_ref):
+    for d in range(kept_ref.shape[0]):
+        pot, slopes = unpieced(kept_ref[d], wide)
+        pot_come, slopes_come = unpieced(come_ref[d].astype(F32), wide)
+        block = pieced(pot + pot_come, slopes + slopes_come, kept_ref.shape[1])
+        if d % 2:
+            send_ref[d // 2] = block.astype(BF16)
         else:
-            own_ref[...] = block
+            keep_ref[d // 2] = block
 
 
 def per_device(
@@ -942,16 +942,24 @@
         flops=1_000_000_000,
         name="fold_near",
     )
-    folds = run(
-        functools.partial(join_kernel, lat_width),
-        [shape(block_rows, atoms)] + [shape(block_rows, atoms, dtype=BF16)] * (half - 1),
-        [near_folds, far_folds],
-        name="fold_join",
-    )
-    folds = [folds[0]] + [paired(folds[d], "gx", 2 * d) for d in range(1, half)]
+    kept, come, mask = near_folds, far_folds, 2
+    while mask < grid_x:
+        count = kept.shape[0] // 2
+        kept, sent = run(
+            functools.partial(join_kernel, lat_width),
+            [
+                shape(count, block_rows, atoms),
+                shape(count, block_rows, atoms, dtype=BF16),
+            ],
+            [kept, come],
+            name="fold_join",
+        )
+        come = paired(sent, "gx", mask)
+        mask *= 2
+    folds = [kept, come]
 
     site, long, cotangent, grads, term, to_sides, to_beyond, to_pair = run(
-        functools.partial(second_back_kernel, slots, scale, half),
+        functools.partial(second_back_kernel, slots, scale, len(folds)),
         [
             shape(1, 1, atoms),
             shape(8, atoms),

time: 90.9 us -> 93.1 us (1.024)
  waiting for transfers between devices: 28.1 us -> 30.9 us
    ppermute x19 -> x18, waiting for transfers between devices: 9.4 us -> 13.1 us  [paired(): lax.ppermute(block, axis, [(i ^ mask, i) for i in range(lax.axis_size(axi...]
    ppermute x19 -> x18, starting transfers between devices: 16.2 us -> 14.8 us  [paired(): lax.ppermute(block, axis, [(i ^ mask, i) for i in range(lax.axis_size(axi...]
    pallas_call x20 -> x21, Pallas kernels: 26.5 us -> 26.6 us  [run(): pl.pallas_call(kernel, out_shape=outs, in_specs=specs, out_specs=[whole()...]
  transfers between devices with their start and end apart: 28 -> 27, of which waited for: 19 -> 19; matrix products, arithmetic and copies ran while one was open for 0% -> 0% of each run, Pallas kernels for 17% -> 17%
where the time goes in v12:
time: 93.1 us; the launch traced here: 92.9 us
  starting transfers between devices  32.2 us (35%)
  waiting for transfers between devices  30.9 us (33%)
  Pallas kernels  26.6 us (29%)
  local copies, waits for them, and re-layouts  2.07 us (2%)
    pallas_call x21, Pallas kernels, run(): pl.pallas_call(kernel, out_shape=outs, in_specs=specs, out_specs=[whole()...  26.6 us
    ppermute x9, waiting for transfers between devices, beyond(): return lax.ppermute(block, axis, route)  17.9 us
    ppermute x9, starting transfers between devices, beyond(): return lax.ppermute(block, axis, route)  17.4 us
    ppermute x18, starting transfers between devices, paired(): lax.ppermute(block, axis, [(i ^ mask, i) for i in range(lax.axis_size(axi...  14.8 us
    ppermute x18, waiting for transfers between devices, paired(): lax.ppermute(block, axis, [(i ^ mask, i) for i in range(lax.axis_size(axi...  13.1 us
    unnamed x23, local copies, waits for them, and re-layouts  1.99 us
  transfers between devices with their start and end apart: 27, of which 19 were waited for; matrix products, arithmetic and copies ran while one was open for 0% of the time, Pallas kernels for 17%

profile of v12, /device:TPU:0, one launch (start us, length us, event | category | flops | bytes accessed | tf_op | source)
XLA Modules:
  0.0 92.9 jit_solution(84495896772063283)
XLA Ops:
  0.6 0.1 pad_add_fusion
  0.7 0.1 broadcast_in_dim.4.place_ref
  0.8 0.7 copy-done.9
  1.5 0.7 copy-done.10
  2.2 4.0 %collective-permute-start.1 = (f32[8,128]{1,0:T(8,128)S(1)}, f32[8,128]{1,0:T(8,128)S(1)}, u32[]{:S(2)}, u32[]{:S(2)}) collective-permute-start(f32[8,128]{1,0:T(8,128)S(1)} %pack.1), channel_id=1, source_target_pairs={{3,0},{2,1},{1,2},{0,3},{7,4},{6,5},{5,6},{4,7},{11,8},{10,9},{9,1... | collective-permute-start | bytes 12296 | tf_op jit(solution)/shard_map/ppermute | solution.py:31
  6.1 0.5 collective-permute-start
  6.7 0.4 prep_first.1
  7.1 0.7 collective-permute-done.1
  7.7 2.0 %collective-permute-done = f32[8,128]{1,0:T(8,128)S(1)} collective-permute-done((f32[8,128]{1,0:T(8,128)S(1)}, f32[8,128]{1,0:T(8,128)S(1)}, u32[]{:S(2)}, u32[]{:S(2)}) %collective-permute-start) | collective-permute-done | bytes 4128 | tf_op jit(solution)/shard_map/ppermute | solution.py:25
  9.8 1.8 %collective-permute-start.3 = (f32[3,8,128]{2,1,0:T(8,128)S(1)}, f32[3,8,128]{2,1,0:T(8,128)S(1)}, u32[]{:S(2)}, u32[]{:S(2)}) collective-permute-start(f32[3,8,128]{2,1,0:T(8,128)S(1)} %pad_maximum_fusion.2.column_ref.cell_ref), channel_id=1, source_target_pairs={{28,0},{8,4},{4,8},{16,12},{12,16},{24,20},{20,24},{0,28},{29,1},{... | collective-permute-start | bytes 36872 | tf_op jit(solution)/shard_map/ppermute | solution.py:31
  11.5 3.1 %collective-permute-done.3.beyond_ref = f32[3,8,128]{2,1,0:T(8,128)S(1)} collective-permute-done((f32[3,8,128]{2,1,0:T(8,128)S(1)}, f32[3,8,128]{2,1,0:T(8,128)S(1)}, u32[]{:S(2)}, u32[]{:S(2)}) %collective-permute-start.3) | collective-permute-done | bytes 12320 | tf_op jit(solution)/shard_map/ppermute | solution.py:31
  14.7 1.3 %first.1 = (bf16[128,256]{1,0:T(8,128)(2,1)S(1)}, f32[8,3072]{1,0:T(8,128)S(1)}, f32[8,3072]{1,0:T(8,128)S(1)}, f32[8,3072]{1,0:T(8,128)S(1)}, f32[3,128,256]{2,1,0:T(8,128)S(1)}, /*index=5*/f32[128,256]{1,0:T(8,128)S(1)}) custom-call(s32[2,8,128]{2,1,0:T(8,128)S(1)} %broadcast_in_dim.4.place_ref, s32[1,3072]{1,0:T(1,128)S(1)} %get-tuple-element.84.ids_ref, ...), custom_call_target="tpu_custom_call" | custom-call | flops 10000000 | bytes 1000000 | tf_op jit(solution)/shard_map/first/pallas_call | solution.py:47
  16.0 1.0 %collective-permute-start.5 = (bf16[128,256]{1,0:T(8,128)(2,1)S(1)}, bf16[128,256]{1,0:T(8,128)(2,1)S(1)}, u32[]{:S(2)}, u32[]{:S(2)}) collective-permute-start(bf16[128,256]{1,0:T(8,128)(2,1)S(1)} %get-tuple-element.102), channel_id=1, source_target_pairs={{3,0},{2,1},{1,2},{0,3},{7,4},{6,5},{5,6},{4,7},{11,8},{10,9},{9,1... | collective-permute-start | bytes 196616 | tf_op jit(solution)/shard_map/ppermute | solution.py:31
  17.0 1.1 %collective-permute-start.4 = (bf16[128,256]{1,0:T(8,128)(2,1)S(1)}, bf16[128,256]{1,0:T(8,128)(2,1)S(1)}, u32[]{:S(2)}, u32[]{:S(2)}) collective-permute-start(bf16[128,256]{1,0:T(8,128)(2,1)S(1)} %get-tuple-element.102), channel_id=1, source_target_pairs={{1,0},{0,1},{3,2},{2,3},{5,4},{4,5},{7,6},{6,7},{9,8},{8,9},{11,10... | collective-permute-start | bytes 196616 | tf_op jit(solution)/shard_map/ppermute | solution.py:25
  18.1 2.1 %hot.1.hot_ref = bf16[1536,3072]{1,0:T(8,128)(2,1)S(1)} custom-call(s32[1,3072]{1,0:T(1,128)S(1)} %get-tuple-element.84.ids_ref), custom_call_target="tpu_custom_call" | custom-call | flops 1000000 | bytes 1000000 | tf_op jit(solution)/shard_map/hot/pallas_call | solution.py:47
  20.2 1.1 %collective-permute-done.5 = bf16[128,256]{1,0:T(8,128)(2,1)S(1)} collective-permute-done((bf16[128,256]{1,0:T(8,128)(2,1)S(1)}, bf16[128,256]{1,0:T(8,128)(2,1)S(1)}, u32[]{:S(2)}, u32[]{:S(2)}) %collective-permute-start.5) | collective-permute-done | bytes 65568 | tf_op jit(solution)/shard_map/ppermute | solution.py:31
  21.3 0.1 collective-permute-start.6
  21.4 0.4 prep_second.1
  21.9 2.6 %collective-permute-start.7 = (bf16[3,128,256]{2,1,0:T(8,128)(2,1)S(1)}, bf16[3,128,256]{2,1,0:T(8,128)(2,1)S(1)}, u32[]{:S(2)}, u32[]{:S(2)}) collective-permute-start(bf16[3,128,256]{2,1,0:T(8,128)(2,1)S(1)} %pad_maximum_fusion.column_ref), channel_id=1, source_target_pairs={{28,0},{8,4},{4,8},{16,12},{12,16},{24,20},{20,24},{0,28},{29,1},{... | collective-permute-start | bytes 589832 | tf_op jit(solution)/shard_map/ppermute | solution.py:31
  24.5 3.5 %second_near.1 = (f32[4,128,3072]{2,1,0:T(8,128)S(1)}, f32[128,3072]{1,0:T(8,128)S(1)}, bf16[768,3072]{1,0:T(8,128)(2,1)S(1)}) custom-call(s32[1,3072]{1,0:T(1,128)S(1)} %get-tuple-element.84.ids_ref, f32[8,3072]{1,0:T(8,128)S(1)} %get-tuple-element.91.basis_ref, f32[8,3072]{1,0:T(8,128)S(1)} %get-tuple-element.93.unit_ref, ...), custom_call_target="tpu_custom_call" | custom-call | flops 2000000000 | bytes 1000000 | tf_op jit(solution)/shard_map/second_near/pallas_call | solution.py:47
  28.0 0.8 second_side.1.near_ref
  28.8 1.7 %collective-permute-done.7.beyond_ref = bf16[3,128,256]{2,1,0:T(8,128)(2,1)S(1)} collective-permute-done((bf16[3,128,256]{2,1,0:T(8,128)(2,1)S(1)}, bf16[3,128,256]{2,1,0:T(8,128)(2,1)S(1)}, u32[]{:S(2)}, u32[]{:S(2)}) %collective-permute-start.7) | collective-permute-done | bytes 196640 | tf_op jit(solution)/shard_map/ppermute | solution.py:31
  30.6 1.9 %second.1 = (bf16[128,3072]{1,0:T(8,128)(2,1)S(1)}, f32[3,128,256]{2,1,0:T(8,128)S(1)}, f32[128,256]{1,0:T(8,128)S(1)}, bf16[80,256]{1,0:T(8,128)(2,1)S(1)}, f32...) custom-call(bf16[768,3072]{1,0:T(8,128)(2,1)S(1)} %get-tuple-element.105.hot_ref, ...), custom_call_target="tpu_custom_call" | custom-call | flops 10000000 | bytes 1000000 | tf_op jit(solution)/shard_map/second/pallas_call | solution.py:47
  32.5 0.1 collective-permute-start.9
  32.6 4.3 %collective-permute-start.8 = (bf16[80,256]{1,0:T(8,128)(2,1)S(1)}, bf16[80,256]{1,0:T(8,128)(2,1)S(1)}, u32[]{:S(2)}, u32[]{:S(2)}) collective-permute-start(bf16[80,256]{1,0:T(8,128)(2,1)S(1)} %get-tuple-element.110), channel_id=1, source_target_pairs={{8,0},{12,4},{0,8},{4,12},{24,16},{28,20},{16,24},{20,28},{9,1},{1... | collective-permute-start | bytes 122888 | tf_op jit(solution)/shard_map/ppermute | solution.py:25
  36.9 0.8 green.1.refs_0_
  37.7 0.8 collective-permute-done.10
  38.6 0.4 collective-permute-done.8
  39.0 1.2 %structure_near.1 = (f32[32,1024]{1,0:T(8,128)S(1)}, f32[32,1024]{1,0:T(8,128)S(1)}, f32[8,1024]{1,0:T(8,128)S(1)}, f32[8,1024]{1,0:T(8,128)S(1)}, bf16[640,1024...) custom-call(s32[2,8,128]{2,1,0:T(8,128)S(1)} %broadcast_in_dim.4.place_ref, ...), custom_call_target="tpu_custom_call" | custom-call | flops 1000000000 | bytes 1000000 | tf_op jit(solution)/shard_map/structure_near/pallas_call | solution.py:47
  40.3 0.2 collective-permute-done.11.blocks.refs_11_
  40.4 1.3 %structure_far.1 = (f32[32,1024]{1,0:T(8,128)S(1)}, f32[32,1024]{1,0:T(8,128)S(1)}, f32[8,1024]{1,0:T(8,128)S(1)}, f32[8,1024]{1,0:T(8,128)S(1)}, bf16[640,1024]...) custom-call(s32[2,8,128]{2,1,0:T(8,128)S(1)} %broadcast_in_dim.4.place_r, ...), custom_call_target="tpu_custom_call" | custom-call | flops 10000000 | bytes 1000000 | tf_op jit(solution)/shard_map/structure_far/pallas_call | solution.py:47
  41.7 1.6 %collective-permute-start.14 = (bf16[320,128]{1,0:T(8,128)(2,1)S(1)}, bf16[320,128]{1,0:T(8,128)(2,1)S(1)}, u32[]{:S(2)}, u32[]{:S(2)}) collective-permute-start(bf16[320,128]{1,0:T(8,128)(2,1)S(1)} %get-tuple-element.114), channel_id=1, source_target_pairs={{3,0},{2,1},{1,2},{0,3},{7,4},{6,5},{5,6},{4,7},{11,8},{10,9},{9,1... | collective-permute-start | bytes 245768 | tf_op jit(solution)/shard_map/ppermute | solution.py:25
  43.3 0.7 collective-permute-start.13
  43.9 1.3 %collective-permute-start.12 = (bf16[320,128]{1,0:T(8,128)(2,1)S(1)}, bf16[320,128]{1,0:T(8,128)(2,1)S(1)}, u32[]{:S(2)}, u32[]{:S(2)}) collective-permute-start(bf16[320,128]{1,0:T(8,128)(2,1)S(1)} %get-tuple-element.114), channel_id=1, source_target_pairs={{1,0},{0,1},{3,2},{2,3},{5,4},{4,5},{7,6},{6,7},{9,8},{8,9},{11,10... | collective-permute-start | bytes 245768 | tf_op jit(solution)/shard_map/ppermute | solution.py:25
  45.2 2.8 %hot_back.1.hot_ref = bf16[3072,2304]{1,0:T(8,128)(2,1)S(1)} custom-call(s32[1,3072]{1,0:T(1,128)S(1)} %get-tuple-element.84.ids_ref), custom_call_target="tpu_custom_call" | custom-call | flops 2000000000 | bytes 1000000 | tf_op jit(solution)/shard_map/hot_back/pallas_call | solution.py:47
  48.1 1.0 %collective-permute-done.13.refs_3_ = bf16[320,128]{1,0:T(8,128)(2,1)S(1)} collective-permute-done((bf16[320,128]{1,0:T(8,128)(2,1)S(1)}, bf16[320,128]{1,0:T(8,128)(2,1)S(1)}, u32[]{:S(2)}, u32[]{:S(2)}) %collective-permute-start.13) | collective-permute-done | bytes 81952 | tf_op jit(solution)/shard_map/ppermute | solution.py:25
  49.1 1.5 %fold_far.1 = (bf16[4,80,256]{2,1,0:T(8,128)(2,1)S(1)}, f32[640,64]{1,0:T(8,128)S(1)}) custom-call(s32[2,8,128]{2,1,0:T(8,128)S(1)} %broadcast_in_dim.4.place_ref, f32[320,128]{1,0:T(8,128)S(1)} %green.1.refs_0_, f32[320,128]{1,0:T(8,128)S(1)} %get-tuple-element.128.refs_1_, bf16[320,128]{1,0:T(8,128)(2,1)S(1)} %collective-permute-done.12.refs_2_, ...), custom_call_target="tpu_custom_call" | custom-call | flops 10000000 | bytes 1000000 | tf_op jit(solution)/shard_map/fold_far/pallas_call | solution.py:47
  50.7 0.1 collective-permute-start.15
  50.8 1.2 %fold_near.1.kept_ref = f32[4,80,256]{2,1,0:T(8,128)S(1)} custom-call(s32[2,8,128]{2,1,0:T(8,128)S(1)} %broadcast_in_dim.4.place_ref, f32[640,64]{1,0:T(8,128)S(1)} %get-tuple-element.138.refs_0_, f32[32,1024]{1,0:T(8,128)S(1)} %get-tuple-element.139.refs_1_, f32[32,1024]{1,0:T(8,128)S(1)} %get-tuple-element.140.refs_2_, ...), custom_call_target="tpu_custom_call" | custom-call | flops 1000000000 | bytes 1000000 | tf_op jit(solution)/shard_map/fold_near/pallas_call | solution.py:47
  52.0 0.1 collective-permute-done.15.come_ref
  52.2 2.0 %collective-permute-start.16 = (bf16[2,80,256]{2,1,0:T(8,128)(2,1)S(1)}, bf16[2,80,256]{2,1,0:T(8,128)(2,1)S(1)}, u32[]{:S(2)}, u32[]{:S(2)}) collective-permute-start(bf16[2,80,256]{2,1,0:T(8,128)(2,1)S(1)} %get-tuple-element.147), channel_id=1, source_target_pairs={{8,0},{12,4},{0,8},{4,12},{24,16},{28,20},{16,24},{20,28},{9,1},{1... | collective-permute-start | bytes 245768 | tf_op jit(solution)/shard_map/ppermute | solution.py:25
  54.2 3.0 %collective-permute-done.16.come_ref = bf16[2,80,256]{2,1,0:T(8,128)(2,1)S(1)} collective-permute-done((bf16[2,80,256]{2,1,0:T(8,128)(2,1)S(1)}, bf16[2,80,256]{2,1,0:T(8,128)(2,1)S(1)}, u32[]{:S(2)}, u32[]{:S(2)}) %collective-permute-start.16) | collective-permute-done | bytes 81952 | tf_op jit(solution)/shard_map/ppermute | solution.py:25
  57.2 1.1 %collective-permute-start.17 = (bf16[1,80,256]{2,1,0:T(8,128)(2,1)S(1)}, bf16[1,80,256]{2,1,0:T(8,128)(2,1)S(1)}, u32[]{:S(2)}, u32[]{:S(2)}) collective-permute-start(bf16[1,80,256]{2,1,0:T(8,128)(2,1)S(1)} %get-tuple-element.149), channel_id=1, source_target_pairs={{16,0},{20,4},{24,8},{28,12},{0,16},{4,20},{8,24},{12,28},{17,1},{... | collective-permute-start | bytes 122888 | tf_op jit(solution)/shard_map/ppermute | solution.py:25
  58.3 0.5 readout.1
  58.9 3.5 %collective-permute-done.17.refs_1_ = bf16[1,80,256]{2,1,0:T(8,128)(2,1)S(1)} collective-permute-done((bf16[1,80,256]{2,1,0:T(8,128)(2,1)S(1)}, bf16[1,80,256]{2,1,0:T(8,128)(2,1)S(1)}, u32[]{:S(2)}, u32[]{:S(2)}) %collective-permute-start.17) | collective-permute-done | bytes 40992 | tf_op jit(solution)/shard_map/ppermute | solution.py:25
  62.4 3.1 %second_back.1 = (f32[1,1,256]{2,1,0:T(1,128)}, f32[8,256]{1,0:T(8,128)S(1)}, f32[128,256]{1,0:T(8,128)S(1)}, f32[4,128,256]{2,1,0:T(8,128)S(1)}, bf16[128,3072]...) custom-call(bf16[3072,2304]{1,0:T(8,128)(2,1)S(1)} %hot_back.1.hot_r, ...), custom_call_target="tpu_custom_call" | custom-call | flops 10000000 | bytes 1000000 | tf_op jit(solution)/shard_map/second_back/pallas_call | solution.py:47
  65.4 2.3 %collective-permute-start.19 = (bf16[2,128,256]{2,1,0:T(8,128)(2,1)S(1)}, bf16[2,128,256]{2,1,0:T(8,128)(2,1)S(1)}, u32[]{:S(2)}, u32[]{:S(2)}) collective-permute-start(bf16[2,128,256]{2,1,0:T(8,128)(2,1)S(1)} %get-tuple-element.155), channel_id=1, source_target_pairs={{28,0},{8,4},{4,8},{16,12},{12,16},{24,20},{20,24},{0,28},{29,1},{... | collective-permute-start | bytes 393224 | tf_op jit(solution)/shard_map/ppermute | solution.py:31
  67.7 0.8 second_middle.1.middle_ref
  68.6 3.7 %collective-permute-done.19 = bf16[2,128,256]{2,1,0:T(8,128)(2,1)S(1)} collective-permute-done((bf16[2,128,256]{2,1,0:T(8,128)(2,1)S(1)}, bf16[2,128,256]{2,1,0:T(8,128)(2,1)S(1)}, u32[]{:S(2)}, u32[]{:S(2)}) %collective-permute-start.19) | collective-permute-done | bytes 131104 | tf_op jit(solution)/shard_map/ppermute | solution.py:31
  72.3 1.8 %collective-permute-start.20 = (bf16[128,256]{1,0:T(8,128)(2,1)S(1)}, bf16[128,256]{1,0:T(8,128)(2,1)S(1)}, u32[]{:S(2)}, u32[]{:S(2)}) collective-permute-start(bf16[128,256]{1,0:T(8,128)(2,1)S(1)} %get-tuple-element.157), channel_id=1, source_target_pairs={{28,0},{8,4},{4,8},{16,12},{12,16},{24,20},{20,24},{0,28},{29,1},{... | collective-permute-start | bytes 196616 | tf_op jit(solution)/shard_map/ppermute | solution.py:31
  74.1 0.8 collective-permute-start.21
  74.9 1.8 %collective-permute-start.22 = (bf16[128,256]{1,0:T(8,128)(2,1)S(1)}, bf16[128,256]{1,0:T(8,128)(2,1)S(1)}, u32[]{:S(2)}, u32[]{:S(2)}) collective-permute-start(bf16[128,256]{1,0:T(8,128)(2,1)S(1)} %get-tuple-element.159), channel_id=1, source_target_pairs={{3,0},{2,1},{1,2},{0,3},{7,4},{6,5},{5,6},{4,7},{11,8},{10,9},{9,1... | collective-permute-start | bytes 196616 | tf_op jit(solution)/shard_map/ppermute | solution.py:31
  76.7 1.2 %second_edge.1.edge_ref = f32[32,3072]{1,0:T(8,128)S(1)} custom-call(bf16[2,16,256]{2,1,0:T(8,128)(2,1)S(1)} %get-tuple-element.100.back_ref, bf16[128,3072]{1,0:T(8,128)(2,1)S(1)} %get-tuple-element.109.feature_ref, f32[4,128,256]{2,1,0:T(8,128)S(1)} %get-tuple-element.150.grad_ref), custom_call_target="tpu_custom_call" | custom-call | flops 1000000000 | bytes 1000000 | tf_op jit(solution)/shard_map/second_edge/pallas_call | solution.py:47
  77.9 0.5 collective-permute-done.21.refs_2_
  78.4 1.7 %collective-permute-done.22.refs_3_ = bf16[128,256]{1,0:T(8,128)(2,1)S(1)} collective-permute-done((bf16[128,256]{1,0:T(8,128)(2,1)S(1)}, bf16[128,256]{1,0:T(8,128)(2,1)S(1)}, u32[]{:S(2)}, u32[]{:S(2)}) %collective-permute-start.22) | collective-permute-done | bytes 65568 | tf_op jit(solution)/shard_map/ppermute | solution.py:31
  80.1 1.5 %first_back.1 = (f32[3,8,256]{2,1,0:T(8,128)S(1)}, f32[3,8,256]{2,1,0:T(8,128)S(1)}, f32[3,8,256]{2,1,0:T(8,128)S(1)}) custom-call(s32[1,3072]{1,0:T(1,128)S(1)} %get-tuple-element.84.ids_ref, f32[8,3072]{1,0:T(8,128)S(1)} %get-tuple-element.91.basis_ref, f32[8,3072]{1,0:T(8,128)S(1)} %get-tuple-element.92.slope_ref, ...), custom_call_target="tpu_custom_call" | custom-call | flops 10000000 | bytes 1000000 | tf_op jit(solution)/shard_map/first_back/pallas_call | solution.py:47
  81.7 0.5 collective-permute-start.24
  82.1 0.7 collective-permute-done.23
  82.9 3.9 %collective-permute-done.24 = f32[3,8,256]{2,1,0:T(8,128)S(1)} collective-permute-done((f32[3,8,256]{2,1,0:T(8,128)S(1)}, f32[3,8,256]{2,1,0:T(8,128)S(1)}, u32[]{:S(2)}, u32[]{:S(2)}) %collective-permute-start.24) | collective-permute-done | bytes 24608 | tf_op jit(solution)/shard_map/ppermute | solution.py:31
  86.8 1.8 %collective-permute-start.26 = (f32[8,256]{1,0:T(8,128)S(1)}, f32[8,256]{1,0:T(8,128)S(1)}, u32[]{:S(2)}, u32[]{:S(2)}) collective-permute-start(f32[8,256]{1,0:T(8,128)S(1)} %get-tuple-element.169), channel_id=1, source_target_pairs={{3,0},{2,1},{1,2},{0,3},{7,4},{6,5},{5,6},{4,7},{11,8},{10,9},{9,1... | collective-permute-start | bytes 24584 | tf_op jit(solution)/shard_map/ppermute | solution.py:31
  88.6 1.0 %collective-permute-start.25 = (f32[8,256]{1,0:T(8,128)S(1)}, f32[8,256]{1,0:T(8,128)S(1)}, u32[]{:S(2)}, u32[]{:S(2)}) collective-permute-start(f32[8,256]{1,0:T(8,128)S(1)} %get-tuple-element.170), channel_id=1, source_target_pairs={{1,0},{0,1},{3,2},{2,3},{5,4},{4,5},{7,6},{6,7},{9,8},{8,9},{11,10... | collective-permute-start | bytes 24584 | tf_op jit(solution)/shard_map/ppermute | solution.py:25
  89.6 1.8 %collective-permute-done.26 = f32[8,256]{1,0:T(8,128)S(1)} collective-permute-done((f32[8,256]{1,0:T(8,128)S(1)}, f32[8,256]{1,0:T(8,128)S(1)}, u32[]{:S(2)}, u32[]{:S(2)}) %collective-permute-start.26) | collective-permute-done | bytes 8224 | tf_op jit(solution)/shard_map/ppermute | solution.py:31
  91.4 0.9 collective-permute-done.25
  92.3 0.6 copy.13
  (43 shorter events, 0.5 us)
Async XLA Ops:
  0.8 0.7 copy-start.9
  1.5 0.7 copy-start.10
  2.1 4.5 %copy-start = (f32[2,2,128,128]{3,2,1,0:T(8,128)S(1)}, f32[2,2,128,128]{3,2,1,0:T(8,128)}, u32[]{:S(2)}) copy-start(f32[2,2,128,128]{3,2,1,0:T(8,128)} %mixing_in.1) | copy-start | bytes 786436
  2.2 4.5 %copy-start.4 = (f32[2,2,8,128]{3,2,1,0:T(8,128)S(1)}, f32[2,2,8,128]{3,2,1,0:T(8,128)}, u32[]{:S(2)}) copy-start(f32[2,2,8,128]{3,2,1,0:T(8,128)} %radial_in.1) | copy-start | bytes 49156
  2.2 4.5 %copy-start.5 = (s32[1,1,256,12]{2,1,3,0:T(1,128)S(1)}, s32[1,1,256,12]{2,1,3,0:T(1,128)}, u32[]{:S(2)}) copy-start(s32[1,1,256,12]{2,1,3,0:T(1,128)} %param.13) | copy-start | bytes 36868
  2.2 4.5 %copy-start.6 = (f32[6,128]{1,0:T(8,128)S(1)}, f32[6,128]{1,0:T(8,128)}, u32[]{:S(2)}) copy-start(f32[6,128]{1,0:T(8,128)} %embed_in.1) | copy-start | bytes 9220
  2.2 4.5 %copy-start.7 = (s32[1,1,256]{2,1,0:T(1,128)S(1)}, s32[1,1,256]{2,1,0:T(1,128)}, u32[]{:S(2)}) copy-start(s32[1,1,256]{2,1,0:T(1,128)} %count_in.1) | copy-start | bytes 3076
  2.2 5.5 %collective-permute-start.1 = (f32[8,128]{1,0:T(8,128)S(1)}, f32[8,128]{1,0:T(8,128)S(1)}, u32[]{:S(2)}, u32[]{:S(2)}) collective-permute-start(f32[8,128]{1,0:T(8,128)S(1)} %pack.1), channel_id=1, source_target_pairs={{3,0},{2,1},{1,2},{0,3},{7,4},{6,5},{5,6},{4,7},{11,8},{10,9},{9,1... | collective-permute-start | bytes 12296 | tf_op jit(solution)/shard_map/ppermute | solution.py:31
  6.1 3.6 %collective-permute-start = (f32[8,128]{1,0:T(8,128)S(1)}, f32[8,128]{1,0:T(8,128)S(1)}, u32[]{:S(2)}, u32[]{:S(2)}) collective-permute-start(f32[8,128]{1,0:T(8,128)S(1)} %pack.1), channel_id=1, source_target_pairs={{1,0},{0,1},{3,2},{2,3},{5,4},{4,5},{7,6},{6,7},{9,8},{8,9},{11,10... | collective-permute-start | bytes 12296 | tf_op jit(solution)/shard_map/ppermute | solution.py:25
  9.8 4.9 %collective-permute-start.3 = (f32[3,8,128]{2,1,0:T(8,128)S(1)}, f32[3,8,128]{2,1,0:T(8,128)S(1)}, u32[]{:S(2)}, u32[]{:S(2)}) collective-permute-start(f32[3,8,128]{2,1,0:T(8,128)S(1)} %pad_maximum_fusion.2.column_ref.cell_ref), channel_id=1, source_target_pairs={{28,0},{8,4},{4,8},{16,12},{12,16},{24,20},{20,24},{0,28},{29,1},{... | collective-permute-start | bytes 36872 | tf_op jit(solution)/shard_map/ppermute | solution.py:31
  11.5 3.1 %collective-permute-start.2 = (f32[3,8,128]{2,1,0:T(8,128)S(1)}, f32[3,8,128]{2,1,0:T(8,128)S(1)}, u32[]{:S(2)}, u32[]{:S(2)}) collective-permute-start(f32[3,8,128]{2,1,0:T(8,128)S(1)} %pad_maximum_fusion.2.column_ref.cell_ref), channel_id=1, source_target_pairs={{4,0},{0,4},{12,8},{8,12},{20,16},{16,20},{28,24},{24,28},{5,1},{1... | collective-permute-start | bytes 36872 | tf_op jit(solution)/shard_map/ppermute | solution.py:25
  16.0 5.4 %copy-start.1 = (f32[128,128]{1,0:T(8,128)S(1)}, f32[128,128]{1,0:T(8,128)}, u32[]{:S(2)}) copy-start(f32[128,128]{1,0:T(8,128)} %hidden_in.1) | copy-start | bytes 196612
  16.0 5.4 %copy-start.3 = (f32[128,64]{0,1:T(8,128)S(1)}, f32[128,64]{0,1:T(8,128)}, u32[]{:S(2)}) copy-start(f32[128,64]{0,1:T(8,128)} %param.20) | copy-start | bytes 98308
  16.0 5.4 %copy-start.8 = (f32[128]{0:T(128)S(1)}, f32[128]{0:T(128)}, u32[]{:S(2)}) copy-start(f32[128]{0:T(128)} %param.19) | copy-start | bytes 1540
  16.0 5.2 %collective-permute-start.5 = (bf16[128,256]{1,0:T(8,128)(2,1)S(1)}, bf16[128,256]{1,0:T(8,128)(2,1)S(1)}, u32[]{:S(2)}, u32[]{:S(2)}) collective-permute-start(bf16[128,256]{1,0:T(8,128)(2,1)S(1)} %get-tuple-element.102), channel_id=1, source_target_pairs={{3,0},{2,1},{1,2},{0,3},{7,4},{6,5},{5,6},{4,7},{11,8},{10,9},{9,1... | collective-permute-start | bytes 196616 | tf_op jit(solution)/shard_map/ppermute | solution.py:31
  17.0 4.3 %collective-permute-start.4 = (bf16[128,256]{1,0:T(8,128)(2,1)S(1)}, bf16[128,256]{1,0:T(8,128)(2,1)S(1)}, u32[]{:S(2)}, u32[]{:S(2)}) collective-permute-start(bf16[128,256]{1,0:T(8,128)(2,1)S(1)} %get-tuple-element.102), channel_id=1, source_target_pairs={{1,0},{0,1},{3,2},{2,3},{5,4},{4,5},{7,6},{6,7},{9,8},{8,9},{11,10... | collective-permute-start | bytes 196616 | tf_op jit(solution)/shard_map/ppermute | solution.py:25
  21.3 6.7 %collective-permute-start.6 = (bf16[3,128,256]{2,1,0:T(8,128)(2,1)S(1)}, bf16[3,128,256]{2,1,0:T(8,128)(2,1)S(1)}, u32[]{:S(2)}, u32[]{:S(2)}) collective-permute-start(bf16[3,128,256]{2,1,0:T(8,128)(2,1)S(1)} %pad_maximum_fusion.column_ref), channel_id=1, source_target_pairs={{4,0},{0,4},{12,8},{8,12},{20,16},{16,20},{28,24},{24,28},{5,1},{1... | collective-permute-start | bytes 589832 | tf_op jit(solution)/shard_map/ppermute | solution.py:25
  21.9 8.7 %collective-permute-start.7 = (bf16[3,128,256]{2,1,0:T(8,128)(2,1)S(1)}, bf16[3,128,256]{2,1,0:T(8,128)(2,1)S(1)}, u32[]{:S(2)}, u32[]{:S(2)}) collective-permute-start(bf16[3,128,256]{2,1,0:T(8,128)(2,1)S(1)} %pad_maximum_fusion.column_ref), channel_id=1, source_target_pairs={{28,0},{8,4},{4,8},{16,12},{12,16},{24,20},{20,24},{0,28},{29,1},{... | collective-permute-start | bytes 589832 | tf_op jit(solution)/shard_map/ppermute | solution.py:31
  30.6 6.4 %copy-start.2 = (s32[3,4096]{1,0:T(4,128)S(1)}, s32[3,4096]{1,0:T(4,128)}, u32[]{:S(2)}) copy-start(s32[3,4096]{1,0:T(4,128)} %vec_ref.1) | copy-start | bytes 147460
  32.5 6.1 %collective-permute-start.10 = (bf16[80,256]{1,0:T(8,128)(2,1)S(1)}, bf16[80,256]{1,0:T(8,128)(2,1)S(1)}, u32[]{:S(2)}, u32[]{:S(2)}) collective-permute-start(bf16[80,256]{1,0:T(8,128)(2,1)S(1)} %get-tuple-element.110), channel_id=1, source_target_pairs={{24,0},{28,4},{16,8},{20,12},{8,16},{12,20},{0,24},{4,28},{25,1},{... | collective-permute-start | bytes 122888 | tf_op jit(solution)/shard_map/ppermute | solution.py:25
  32.5 6.0 %collective-permute-start.9 = (bf16[80,256]{1,0:T(8,128)(2,1)S(1)}, bf16[80,256]{1,0:T(8,128)(2,1)S(1)}, u32[]{:S(2)}, u32[]{:S(2)}) collective-permute-start(bf16[80,256]{1,0:T(8,128)(2,1)S(1)} %get-tuple-element.110), channel_id=1, source_target_pairs={{16,0},{20,4},{24,8},{28,12},{0,16},{4,20},{8,24},{12,28},{17,1},{... | collective-permute-start | bytes 122888 | tf_op jit(solution)/shard_map/ppermute | solution.py:25
  32.6 6.3 %collective-permute-start.8 = (bf16[80,256]{1,0:T(8,128)(2,1)S(1)}, bf16[80,256]{1,0:T(8,128)(2,1)S(1)}, u32[]{:S(2)}, u32[]{:S(2)}) collective-permute-start(bf16[80,256]{1,0:T(8,128)(2,1)S(1)} %get-tuple-element.110), channel_id=1, source_target_pairs={{8,0},{12,4},{0,8},{4,12},{24,16},{28,20},{16,24},{20,28},{9,1},{1... | collective-permute-start | bytes 122888 | tf_op jit(solution)/shard_map/ppermute | solution.py:25
  39.0 1.5 %collective-permute-start.11 = (bf16[4,80,256]{2,1,0:T(8,128)(2,1)S(1)}, bf16[4,80,256]{2,1,0:T(8,128)(2,1)S(1)}, u32[]{:S(2)}, u32[]{:S(2)}) collective-permute-start(bf16[4,80,256]{2,1,0:T(8,128)(2,1)S(1)} %pad_maximum_fusion.1.blocks.refs_7_), channel_id=1, source_target_pairs={{4,0},{0,4},{12,8},{8,12},{20,16},{16,20},{28,24},{24,28},{5,1},{1... | collective-permute-start | bytes 491528 | tf_op jit(solution)/shard_map/ppermute | solution.py:25
  41.7 6.4 %collective-permute-start.14 = (bf16[320,128]{1,0:T(8,128)(2,1)S(1)}, bf16[320,128]{1,0:T(8,128)(2,1)S(1)}, u32[]{:S(2)}, u32[]{:S(2)}) collective-permute-start(bf16[320,128]{1,0:T(8,128)(2,1)S(1)} %get-tuple-element.114), channel_id=1, source_target_pairs={{3,0},{2,1},{1,2},{0,3},{7,4},{6,5},{5,6},{4,7},{11,8},{10,9},{9,1... | collective-permute-start | bytes 245768 | tf_op jit(solution)/shard_map/ppermute | solution.py:25
  43.3 5.8 %collective-permute-start.13 = (bf16[320,128]{1,0:T(8,128)(2,1)S(1)}, bf16[320,128]{1,0:T(8,128)(2,1)S(1)}, u32[]{:S(2)}, u32[]{:S(2)}) collective-permute-start(bf16[320,128]{1,0:T(8,128)(2,1)S(1)} %get-tuple-element.114), channel_id=1, source_target_pairs={{2,0},{3,1},{0,2},{1,3},{6,4},{7,5},{4,6},{5,7},{10,8},{11,9},{8,1... | collective-permute-start | bytes 245768 | tf_op jit(solution)/shard_map/ppermute | solution.py:25
  43.9 5.2 %collective-permute-start.12 = (bf16[320,128]{1,0:T(8,128)(2,1)S(1)}, bf16[320,128]{1,0:T(8,128)(2,1)S(1)}, u32[]{:S(2)}, u32[]{:S(2)}) collective-permute-start(bf16[320,128]{1,0:T(8,128)(2,1)S(1)} %get-tuple-element.114), channel_id=1, source_target_pairs={{1,0},{0,1},{3,2},{2,3},{5,4},{4,5},{7,6},{6,7},{9,8},{8,9},{11,10... | collective-permute-start | bytes 245768 | tf_op jit(solution)/shard_map/ppermute | solution.py:25
  50.7 1.5 %collective-permute-start.15 = (bf16[4,80,256]{2,1,0:T(8,128)(2,1)S(1)}, bf16[4,80,256]{2,1,0:T(8,128)(2,1)S(1)}, u32[]{:S(2)}, u32[]{:S(2)}) collective-permute-start(bf16[4,80,256]{2,1,0:T(8,128)(2,1)S(1)} %get-tuple-element.145), channel_id=1, source_target_pairs={{4,0},{0,4},{12,8},{8,12},{20,16},{16,20},{28,24},{24,28},{5,1},{1... | collective-permute-start | bytes 491528 | tf_op jit(solution)/shard_map/ppermute | solution.py:25
  52.2 5.0 %collective-permute-start.16 = (bf16[2,80,256]{2,1,0:T(8,128)(2,1)S(1)}, bf16[2,80,256]{2,1,0:T(8,128)(2,1)S(1)}, u32[]{:S(2)}, u32[]{:S(2)}) collective-permute-start(bf16[2,80,256]{2,1,0:T(8,128)(2,1)S(1)} %get-tuple-element.147), channel_id=1, source_target_pairs={{8,0},{12,4},{0,8},{4,12},{24,16},{28,20},{16,24},{20,28},{9,1},{1... | collective-permute-start | bytes 245768 | tf_op jit(solution)/shard_map/ppermute | solution.py:25
  57.2 5.2 %collective-permute-start.17 = (bf16[1,80,256]{2,1,0:T(8,128)(2,1)S(1)}, bf16[1,80,256]{2,1,0:T(8,128)(2,1)S(1)}, u32[]{:S(2)}, u32[]{:S(2)}) collective-permute-start(bf16[1,80,256]{2,1,0:T(8,128)(2,1)S(1)} %get-tuple-element.149), channel_id=1, source_target_pairs={{16,0},{20,4},{24,8},{28,12},{0,16},{4,20},{8,24},{12,28},{17,1},{... | collective-permute-start | bytes 122888 | tf_op jit(solution)/shard_map/ppermute | solution.py:25
  65.4 6.9 %collective-permute-start.18 = (bf16[3,128,256]{2,1,0:T(8,128)(2,1)S(1)}, bf16[3,128,256]{2,1,0:T(8,128)(2,1)S(1)}, u32[]{:S(2)}, u32[]{:S(2)}) collective-permute-start(bf16[3,128,256]{2,1,0:T(8,128)(2,1)S(1)} %get-tuple-element.154), channel_id=1, source_target_pairs={{4,0},{0,4},{12,8},{8,12},{20,16},{16,20},{28,24},{24,28},{5,1},{1... | collective-permute-start | bytes 589832 | tf_op jit(solution)/shard_map/ppermute | solution.py:25
  65.4 6.9 %collective-permute-start.19 = (bf16[2,128,256]{2,1,0:T(8,128)(2,1)S(1)}, bf16[2,128,256]{2,1,0:T(8,128)(2,1)S(1)}, u32[]{:S(2)}, u32[]{:S(2)}) collective-permute-start(bf16[2,128,256]{2,1,0:T(8,128)(2,1)S(1)} %get-tuple-element.155), channel_id=1, source_target_pairs={{28,0},{8,4},{4,8},{16,12},{12,16},{24,20},{20,24},{0,28},{29,1},{... | collective-permute-start | bytes 393224 | tf_op jit(solution)/shard_map/ppermute | solution.py:31
  72.3 5.6 %collective-permute-start.20 = (bf16[128,256]{1,0:T(8,128)(2,1)S(1)}, bf16[128,256]{1,0:T(8,128)(2,1)S(1)}, u32[]{:S(2)}, u32[]{:S(2)}) collective-permute-start(bf16[128,256]{1,0:T(8,128)(2,1)S(1)} %get-tuple-element.157), channel_id=1, source_target_pairs={{28,0},{8,4},{4,8},{16,12},{12,16},{24,20},{20,24},{0,28},{29,1},{... | collective-permute-start | bytes 196616 | tf_op jit(solution)/shard_map/ppermute | solution.py:31
  74.1 4.3 %collective-permute-start.21 = (bf16[128,256]{1,0:T(8,128)(2,1)S(1)}, bf16[128,256]{1,0:T(8,128)(2,1)S(1)}, u32[]{:S(2)}, u32[]{:S(2)}) collective-permute-start(bf16[128,256]{1,0:T(8,128)(2,1)S(1)} %get-tuple-element.158), channel_id=1, source_target_pairs={{1,0},{0,1},{3,2},{2,3},{5,4},{4,5},{7,6},{6,7},{9,8},{8,9},{11,10... | collective-permute-start | bytes 196616 | tf_op jit(solution)/shard_map/ppermute | solution.py:25
  74.9 5.2 %collective-permute-start.22 = (bf16[128,256]{1,0:T(8,128)(2,1)S(1)}, bf16[128,256]{1,0:T(8,128)(2,1)S(1)}, u32[]{:S(2)}, u32[]{:S(2)}) collective-permute-start(bf16[128,256]{1,0:T(8,128)(2,1)S(1)} %get-tuple-element.159), channel_id=1, source_target_pairs={{3,0},{2,1},{1,2},{0,3},{7,4},{6,5},{5,6},{4,7},{11,8},{10,9},{9,1... | collective-permute-start | bytes 196616 | tf_op jit(solution)/shard_map/ppermute | solution.py:31
  81.6 1.3 %collective-permute-start.23 = (f32[3,8,256]{2,1,0:T(8,128)S(1)}, f32[3,8,256]{2,1,0:T(8,128)S(1)}, u32[]{:S(2)}, u32[]{:S(2)}) collective-permute-start(f32[3,8,256]{2,1,0:T(8,128)S(1)} %get-tuple-element.161), channel_id=1, source_target_pairs={{4,0},{0,4},{12,8},{8,12},{20,16},{16,20},{28,24},{24,28},{5,1},{1... | collective-permute-start | bytes 73736 | tf_op jit(solution)/shard_map/ppermute | solution.py:25
  81.7 5.1 %collective-permute-start.24 = (f32[3,8,256]{2,1,0:T(8,128)S(1)}, f32[3,8,256]{2,1,0:T(8,128)S(1)}, u32[]{:S(2)}, u32[]{:S(2)}) collective-permute-start(f32[3,8,256]{2,1,0:T(8,128)S(1)} %get-tuple-element.162), channel_id=1, source_target_pairs={{28,0},{8,4},{4,8},{16,12},{12,16},{24,20},{20,24},{0,28},{29,1},{... | collective-permute-start | bytes 73736 | tf_op jit(solution)/shard_map/ppermute | solution.py:31
  86.8 4.6 %collective-permute-start.26 = (f32[8,256]{1,0:T(8,128)S(1)}, f32[8,256]{1,0:T(8,128)S(1)}, u32[]{:S(2)}, u32[]{:S(2)}) collective-permute-start(f32[8,256]{1,0:T(8,128)S(1)} %get-tuple-element.169), channel_id=1, source_target_pairs={{3,0},{2,1},{1,2},{0,3},{7,4},{6,5},{5,6},{4,7},{11,8},{10,9},{9,1... | collective-permute-start | bytes 24584 | tf_op jit(solution)/shard_map/ppermute | solution.py:31
  88.6 3.7 %collective-permute-start.25 = (f32[8,256]{1,0:T(8,128)S(1)}, f32[8,256]{1,0:T(8,128)S(1)}, u32[]{:S(2)}, u32[]{:S(2)}) collective-permute-start(f32[8,256]{1,0:T(8,128)S(1)} %get-tuple-element.170), channel_id=1, source_target_pairs={{1,0},{0,1},{3,2},{2,3},{5,4},{4,5},{7,6},{6,7},{9,8},{8,9},{11,10... | collective-permute-start | bytes 24584 | tf_op jit(solution)/shard_map/ppermute | solution.py:25

commit v13 on v10

--- a/solution.py
+++ b/solution.py
@@ -18,23 +18,31 @@
 WAVE_REACH = 8
 F32 = jnp.float32
 BF16 = jnp.bfloat16
-CENTRE = 4
 
 
 def paired(block, axis, mask):
     return lax.ppermute(block, axis, [(i ^ mask, i) for i in range(lax.axis_size(axis))])
 
 
+def other_side(index, count):
+    return (index + (1 if index % 2 else -1)) % count
+
+
 def beyond(block, axis):
     count = lax.axis_size(axis)
-    route = [((i + (1 if i % 2 else -1)) % count, i) for i in range(count)]
+    return lax.ppermute(block, axis, [(other_side(i, count), i) for i in range(count)])
+
+
+def far(block, axis, over_pair):
+    count = lax.axis_size(axis)
+    if over_pair:
+        route = [(other_side(i ^ 1, count), i) for i in range(count)]
+    else:
+        route = [(other_side(i, count) ^ 1, i) for i in range(count)]
     return lax.ppermute(block, axis, route)
 
 
-def around(block, beside):
-    column = jnp.stack([paired(block, "gy", 1), block, beyond(block, "gy")])
-    column, beside = lax.optimization_barrier((column, beside))
-    return [paired(column, "gx", 1), column, beyond(column, "gx")], beside
+SLOT_CELLS = ((2, 1, 0), (1, 2, 3), (4, 3, 2))
 
 
 def whole(space=pltpu.VMEM):
@@ -148,12 +156,26 @@
     return [basis] + [basis * unit[i : i + 1] for i in range(3)]
 
 
-def pack_kernel(place_ref, position_ref, species_ref, out_ref):
-    rows = [position_ref[0, i] for i in range(3)] + [species_ref[0].astype(F32)]
+def pack_kernel(place_ref, position_in, species_in, ids_in, count_in, place_out, block_out, position,
+                species, ids, count, sems):
+    fetch([position_in, species_in, ids_in, count_in], [position, species, ids, count], sems)
+    rows = [position[0, i] for i in range(3)] + [species[0].astype(F32)]
     atoms = rows[0].shape[1]
-    out_ref[...] = jnp.concatenate(
-        [row[:, s : s + 128] for row in rows for s in range(0, atoms, 128)], axis=0
-    )
+    rows = [row[:, s : s + 128] for row in rows for s in range(0, atoms, 128)]
+    place_out[...] = jnp.concatenate(rows, axis=0)
+    order = slot_order(ids[...], place_ref, atoms).astype(F32)
+    rows += [order[:, s : s + 128] for s in range(0, order.shape[1], 128)]
+    rows += [count[0, :, s : s + 128].astype(F32) for s in range(0, atoms, 128)]
+    rows += [jnp.zeros((block_out.shape[0] - len(rows), 128), F32)]
+    block_out[...] = jnp.concatenate(rows, axis=0)
+
+
+def block_ids(block, atoms, edges):
+    start = 4 * atoms // 128
+    middle, end = start + edges // 128, start + edges // 128 + atoms // 128
+    rows = [block[r : r + 1] for r in range(start, end)]
+    ids = jnp.concatenate(rows[: middle - start], axis=1).astype(jnp.int32)
+    return ids, jnp.concatenate(rows[middle - start :], axis=1)
 
 
 def radial_left(radial):
@@ -190,15 +212,10 @@
         copy.wait()
 
 
-def prep_first_kernel(norm, place_ref, ids_in, count_in, embed_in, radial_in, mixing_in, id_ref, count_ref,
-                      embed_out, kind_left, left_out, back_out, kind_high, kind_low, mix_high,
-                      mix_low, turn_high, turn_low, embed_ref, radial_ref, mixing_ref, sems):
-    fetch(
-        [ids_in, count_in, embed_in, radial_in, mixing_in],
-        [id_ref, count_ref, embed_ref, radial_ref, mixing_ref],
-        sems,
-    )
-    id_ref[...] = slot_order(id_ref[...], place_ref, count_ref.shape[2])
+def prep_first_kernel(norm, embed_in, radial_in, mixing_in, embed_out, kind_left, left_out, back_out,
+                      kind_high, kind_low, mix_high, mix_low, turn_high, turn_low, embed_ref,
+                      radial_ref, mixing_ref, sems):
+    fetch([embed_in, radial_in, mixing_in], [embed_ref, radial_ref, mixing_ref], sems)
     embed = embed_ref[...]
     kinds = embed.shape[0]
     for path in range(2):
@@ -228,18 +245,25 @@
     charge_pair[1] = (charge - high).astype(BF16)
 
 
-def hot_kernel(ids_ref, hot_ref):
-    edges = ids_ref.shape[1]
-    for start in range(0, edges, 256):
+def hot_kernel(atoms, block_ref, hot_ref):
+    ids, _ = block_ids(block_ref[...], atoms, hot_ref.shape[1])
+    for start in range(0, hot_ref.shape[1], 256):
         lanes = slice(start, start + 256)
-        hot_ref[:, lanes] = hot_columns(ids_ref[:, lanes], hot_ref.shape[0])
+        hot_ref[:, lanes] = hot_columns(ids[:, lanes], hot_ref.shape[0])
+
+
+def hot_beyond_kernel(ids_ref, near_ref, hot_ref):
+    ids = ids_ref[1:2, :] - 2 * hot_ref.shape[0]
+    for start in range(0, hot_ref.shape[1], 256):
+        lanes = slice(start, start + 256)
+        hot_ref[:, lanes] = hot_columns(ids[:, lanes], hot_ref.shape[0])
 
 
 def hot_back_kernel(ids_ref, hot_ref):
     edges = ids_ref.shape[1]
     entry = lax.broadcasted_iota(jnp.int32, (128, hot_ref.shape[1]), 1).astype(F32)
     for start in range(0, edges, 128):
-        row = jnp.broadcast_to(ids_ref[:, start : start + 128].astype(F32), (8, 128))
+        row = jnp.broadcast_to(ids_ref[1:2, start : start + 128].astype(F32), (8, 128))
         column = row.T[:, 0:1]
         hot_ref[start : start + 128] = jnp.where(column == entry, 1.0, 0.0).astype(BF16)
 
@@ -250,25 +274,39 @@
     return [jnp.concatenate(rows[q * parts : (q + 1) * parts], axis=1) for q in range(4)]
 
 
-def first_kernel(slots, place_ref, ids_ref, count_ref, embed_ref, kind_left, mix_high, mix_low,
-                 pair_ref, column_ref, beyond_ref, low_ref, basis_ref, slope_ref, unit_ref, sums_ref,
-                 gate_ref):
-    atoms = low_ref.shape[1]
-    ids = ids_ref[...]
+def first_kernel(slots, place_ref, embed_ref, kind_left, mix_high, mix_low, y_pair_ref, own_ref,
+                 y_beyond_ref, pair_ref, column_ref, beyond_ref, low_ref, ids_ref, basis_ref, slope_ref,
+                 unit_ref, sums_ref, gate_ref):
+    atoms = low_ref.shape[2]
     frame = [pair_ref, column_ref, beyond_ref]
-    own = unfold_block(column_ref[1], atoms)
     per_cell = atoms // 128
     places = lax.broadcasted_iota(jnp.int32, (4 * per_cell, 128), 0)
     upper = places % per_cell
     kind_of_row = places // per_cell
-    rows = []
     to_x = jnp.where(kind_of_row == 0, cell_width, 0.0)
     to_x = jnp.where((place_ref[0] & 1) == 0, to_x, -to_x)
     to_y = jnp.where(kind_of_row == 1, cell_width, 0.0)
     to_y = jnp.where((place_ref[1] & 1) == 0, to_y, -to_y)
-    for a in range(3):
-        for b in range(3):
-            rows.append(frame[a][b] + ((1 - a) * to_x + (1 - b) * to_y))
+    for cell, block_ref in enumerate((y_pair_ref, own_ref, y_beyond_ref)):
+        ids, count = block_ids(block_ref[...], atoms, slots * atoms)
+        ids_ref[cell : cell + 1, :] = ids
+        own = unfold_block(column_ref[cell + 1], atoms)
+        step_y = to_y if cell == 1 else -to_y
+        rows = []
+        for a in range(3):
+            for b in range(3):
+                block = frame[a][SLOT_CELLS[cell][b]]
+                rows.append(block + ((1 - a) * to_x + (1 - b) * step_y))
+        first_cell(
+            slots, atoms, ids, count, rows, places, upper, own, embed_ref, kind_left, mix_high,
+            mix_low, low_ref.at[cell], basis_ref.at[cell], slope_ref.at[cell], unit_ref.at[cell],
+            sums_ref.at[cell], gate_ref.at[cell],
+        )
+
+
+def first_cell(slots, atoms, ids, count, rows, places, upper, own, embed_ref, kind_left, mix_high,
+               mix_low, low_ref, basis_ref, slope_ref, unit_ref, sums_ref, gate_ref):
+    per_cell = atoms // 128
     pieces = []
     for start in range(0, ids.shape[1], 128):
         part = jnp.broadcast_to(ids[:, start : start + 128], places.shape)
@@ -289,7 +327,6 @@
     order = (lax.broadcasted_iota(jnp.int32, (8, 1), 0) + 1).astype(F32)
     sine, cosine = sin_cos((order * (0.5 / cut_radius)) * distance)
     wave = sine / ((order * (math.pi / cut_radius)) * distance)
-    count = count_ref[0]
     live = jnp.concatenate([jnp.where(count > n, 1.0, 0.0) for n in range(slots)], axis=1)
     basis = wave * live
     basis_ref[...] = basis
@@ -328,17 +365,16 @@
     return jnp.where(ids == place, 1.0, 0.0).astype(BF16)
 
 
-def second_near_kernel(slots, ids_ref, basis_ref, unit_ref, left_ref, hot_ref, column_ref,
-                       weight_ref, near_ref, beyond_ref):
+def second_near_kernel(slots, basis_ref, unit_ref, left_ref, hot_ref, column_ref, weight_ref,
+                       near_ref):
     atoms = column_ref.shape[2]
-    parts = edge_parts(basis_ref[...], unit_ref[...])
+    parts = edge_parts(basis_ref[1], unit_ref[1])
     source = jnp.concatenate([column_ref[b] for b in range(3)], axis=1)
     for n in range(slots):
         lanes = slice(n * atoms, (n + 1) * atoms)
         for part in range(4):
             weight_ref[part, :, lanes] = weights_of(left_ref, part, parts[part][:, lanes])
         near_ref[:, lanes] = dot(source, hot_ref[3 * atoms : 6 * atoms, lanes])
-        beyond_ref[:, lanes] = hot_columns(ids_ref[:, lanes] - 6 * atoms, 3 * atoms)
 
 
 def second_side_kernel(slots, hot_ref, near_ref, pair_ref, out_ref):
@@ -370,7 +406,7 @@
     gate_ref[...] = gate
     charge = dot_split((charge_ref[0], charge_ref[1]), hidden)
     full_charge_ref[...] = charge
-    place = jnp.concatenate(unfold_block(cell_ref[1], atoms)[:3], axis=0)
+    place = jnp.concatenate(unfold_block(cell_ref[2], atoms)[:3], axis=0)
     high = place.astype(BF16).astype(F32)
     rest = place - high
     middle = rest.astype(BF16).astype(F32)
@@ -406,7 +442,7 @@
 def second_back_kernel(slots, scale, count, hot_ref, weight_ref, turn_high, turn_low, charge_ref,
                        sums_ref, gate_ref, full_charge_ref, energy_ref, slope_ref, *refs):
     folds, refs = refs[:count], refs[count:]
-    site_ref, long_ref, cotangent_ref, grad_ref, term_ref, sides_ref, beyond_ref, pair_ref = refs
+    site_ref, long_ref, cotangent_ref, grad_ref, term_ref, beyond_ref, pair_ref = refs
     atoms = gate_ref.shape[1]
     total = folds[0][...].astype(F32)
     for part in folds[1:]:
@@ -438,11 +474,7 @@
         term_ref[:, lanes] = term.astype(BF16)
     for b in range(3):
         start = (6 + b) * atoms
-        grad = dot(term_ref[...], hot_ref[:, start : start + atoms]).astype(BF16)
-        if b == 1:
-            beyond_ref[...] = grad
-        else:
-            sides_ref[b // 2] = grad
+        beyond_ref[b] = dot(term_ref[...], hot_ref[:, start : start + atoms]).astype(BF16)
     for b in range(3):
         pair_ref[b] = dot(term_ref[...], hot_ref[:, b * atoms : (b + 1) * atoms]).astype(BF16)
 
@@ -465,15 +497,34 @@
             )
 
 
-def first_back_kernel(slots, ids_ref, basis_ref, slope_ref, unit_ref, kind_high, kind_low,
-                      turn_high, turn_low, sums_ref, gate_ref, edge_ref, long_ref, middle_ref,
-                      *refs):
-    from_x, from_y, outs = refs[:2], refs[2:4], refs[4:]
+def first_back_kernel(slots, ids_ref, basis_ref, slope_ref, unit_ref, kind_high, kind_low, turn_high,
+                      turn_low, sums_ref, gate_ref, edge_ref, long_ref, middle_ref, from_pair,
+                      from_beyond, *outs):
+    sums = {(1, 2): long_ref[...]}
+    for cell in range(3):
+        cotangent = middle_ref[cell] + (
+            from_pair[cell].astype(F32) + from_beyond[cell].astype(F32)
+        )
+        own, found = first_back_cell(
+            slots, ids_ref[cell : cell + 1, :], basis_ref.at[cell], slope_ref.at[cell],
+            unit_ref.at[cell], kind_high, kind_low, turn_high, turn_low, sums_ref.at[cell],
+            gate_ref.at[cell], edge_ref if cell == 1 else None, cotangent,
+        )
+        terms = [((1, cell + 1), own)]
+        terms += [((n // 3, SLOT_CELLS[cell][n % 3]), found[n]) for n in range(9)]
+        for key, term in terms:
+            sums[key] = sums[key] + term if key in sums else term
+    for (x, y), total in sums.items():
+        outs[x][y] = total
+
+
+def first_back_cell(slots, ids, basis_ref, slope_ref, unit_ref, kind_high, kind_low, turn_high,
+                    turn_low, sums_ref, gate_ref, edge_ref, cotangent):
     atoms = gate_ref.shape[1]
-    cotangent = middle_ref[1]
-    for block in (from_x[0][1], from_x[1][...], from_y[0][...], from_y[1][...]):
-        cotangent = cotangent + block.astype(F32)
-    grads = message_grads(cotangent, gate_ref, sums_ref, turn_high, turn_low, 0)
+    pre = cotangent * gate_ref[...]
+    both = dot_split((turn_high[0], turn_low[0]), pre)
+    wide = both.shape[0] // 2
+    grads = [both[:wide]] + [both[wide:] * sums_ref[i] for i in range(3)]
     unit = unit_ref[...]
     kinds = unit[4:5]
     by_kind = [dot_split((kind_high[0], kind_low[0]), grads[0])]
@@ -489,9 +540,9 @@
             for k, match in enumerate(matches):
                 found = jnp.where(match, rows[8 * k + 8 : 8 * k + 16], found)
             edges[part].append(found)
-    edges = [
-        edge_ref[8 * part : 8 * part + 8] + jnp.concatenate(edges[part], axis=1) for part in range(4)
-    ]
+    edges = [jnp.concatenate(rows, axis=1) for rows in edges]
+    if edge_ref is not None:
+        edges = [edge_ref[8 * part : 8 * part + 8] + edges[part] for part in range(4)]
     basis = basis_ref[...]
     units = [unit[i : i + 1] for i in range(3)]
     inverse = unit[3:4]
@@ -505,10 +556,9 @@
     moves = [by_unit[i] + by_distance * units[i] for i in range(3)]
     zero = jnp.zeros_like(moves[0])
     move = jnp.concatenate(moves + [zero] * 5, axis=0)
-    own = long_ref[...]
-    for n in range(slots):
+    own = -move[:, :atoms]
+    for n in range(1, slots):
         own = own - move[:, n * atoms : (n + 1) * atoms]
-    ids = ids_ref[...]
     lane_hot = hot_columns(ids & 127, 128)
     half = ids >> 7
     high = move.astype(BF16).astype(F32)
@@ -518,14 +568,13 @@
         [jnp.where(half == h, both, 0.0).astype(BF16) for h in range(9 * per_cell)], axis=0
     )
     spread = dot(rows, lane_hot, ((1,), (1,)))
+    grads = []
     for cell in range(9):
         found = []
         for h in range(cell * per_cell, (cell + 1) * per_cell):
             found.append(spread[16 * h : 16 * h + 8] + spread[16 * h + 8 : 16 * h + 16])
-        grad = jnp.concatenate(found, axis=1)
-        if cell == CENTRE:
-            grad = own + grad
-        outs[cell // 3][cell % 3] = grad
+        grads.append(jnp.concatenate(found, axis=1))
+    return own, grads
 
 
 def pair_counts(parts):
@@ -771,23 +820,39 @@
     place = jnp.broadcast_to(place[:, None, None], (2, 8, 128))
     _, share, padded = pair_counts(grid_x)
     ids = neighbours.transpose(0, 3, 1, 2).reshape(1, edges)
+    cell_rows = 4 * atoms // 128
+    block_total = -(-(cell_rows + (edges + atoms) // 128) // 8) * 8
     dma = pltpu.SemaphoreType.DMA
-    (own,) = run(
+    shown = positions.transpose(0, 2, 1, 3)
+    own_place, own = run(
         pack_kernel,
-        [shape(4 * atoms // 128, 128)],
-        [place, positions.transpose(0, 2, 1, 3), species],
-        flops=10_000_000_000,
+        [shape(cell_rows, 128), shape(block_total, 128)],
+        [place, shown, species, ids, counts],
+        scratch=[
+            pltpu.VMEM(shown.shape, F32),
+            pltpu.VMEM(species.shape, jnp.int32),
+            pltpu.VMEM(ids.shape, jnp.int32),
+            pltpu.VMEM(counts.shape, jnp.int32),
+            dma((4,)),
+        ],
+        hbm=4,
+        grant=60,
         name="pack",
     )
+    y_pair, y_beyond = paired(own, "gy", 1), beyond(own, "gy")
+    over_pair = far(own_place, "gy", True)
+    over_beyond = over_pair if grid_y == 4 else far(own_place, "gy", False)
+    cells = jnp.stack(
+        [over_pair, y_pair[:cell_rows], own_place, y_beyond[:cell_rows], over_beyond]
+    )
+    cells = [paired(cells, "gx", 1), cells, beyond(cells, "gx")]
+
     norm = 1.0 / math.sqrt(slots)
     kind_rows = 8 * species_embed.shape[0]
     low_pair = lambda *dims: [shape(*dims, dtype=BF16)] * 2
-    (ids, counts, embed, kind_left, left, back, kind_high, kind_low, mix_high, mix_low, turn_high,
-     turn_low) = run(
+    embed, kind_left, left, back, kind_high, kind_low, mix_high, mix_low, turn_high, turn_low = run(
         functools.partial(prep_first_kernel, norm),
         [
-            shape(1, edges, dtype=jnp.int32),
-            shape(*counts.shape, dtype=jnp.int32),
             shape(features, 32, dtype=BF16),
             shape(2, features, 4 * kind_rows, dtype=BF16),
             shape(2, features, 32, dtype=BF16),
@@ -796,21 +861,20 @@
         + low_pair(2, kind_rows, features)
         + low_pair(2, features, 2 * features)
         + low_pair(2, 2 * features, features),
-        [place, ids, counts, species_embed, radial, mixing],
+        [species_embed, radial, mixing],
         scratch=[
             pltpu.VMEM(species_embed.shape, F32),
             pltpu.VMEM(radial.shape, F32),
             pltpu.VMEM(mixing.shape, F32),
-            dma((5,)),
+            dma((3,)),
         ],
-        hbm=5,
+        hbm=3,
         name="prep_first",
     )
-    cells, ids = around(own, ids)
     (hot,) = run(
-        hot_kernel,
+        functools.partial(hot_kernel, atoms),
         [shape(6 * atoms, edges, dtype=BF16)],
-        [ids],
+        [own],
         flops=1_000_000,
         name="hot",
     )
@@ -829,30 +893,34 @@
         hbm=3,
         name="prep_second",
     )
-    low, basis, slope, unit, sums_one, gate_one = run(
+    low, ids, basis, slope, unit, sums_one, gate_one = run(
         functools.partial(first_kernel, slots),
         [
-            shape(features, atoms, dtype=BF16),
-            shape(8, edges),
-            shape(8, edges),
-            shape(8, edges),
+            shape(3, features, atoms, dtype=BF16),
+            shape(3, edges, dtype=jnp.int32),
+            shape(3, 8, edges),
+            shape(3, 8, edges),
+            shape(3, 8, edges),
+            shape(3, 3, features, atoms),
             shape(3, features, atoms),
-            shape(features, atoms),
         ],
-        [place, ids, counts, embed, kind_left, mix_high, mix_low] + cells,
+        [place, embed, kind_left, mix_high, mix_low, y_pair, own, y_beyond] + cells,
         name="first",
     )
-    hidden, hot = around(low, hot)
-    edge_weights, near, hot_beyond = run(
+    hidden = [paired(low, "gx", 1), low, beyond(low, "gx")]
+    edge_weights, near = run(
         functools.partial(second_near_kernel, slots),
-        [
-            shape(4, features, edges),
-            shape(features, edges),
-            shape(3 * atoms, edges, dtype=BF16),
-        ],
-        [ids, basis, unit, left, hot, hidden[1]],
+        [shape(4, features, edges), shape(features, edges)],
+        [basis, unit, left, hot, low],
         flops=2_000_000_000,
         name="second_near",
+    )
+    (hot_beyond,) = run(
+        hot_beyond_kernel,
+        [shape(3 * atoms, edges, dtype=BF16)],
+        [ids, near],
+        flops=1_000_000,
+        name="hot_beyond",
     )
     (near,) = run(
         functools.partial(second_side_kernel, slots),
@@ -950,7 +1018,7 @@
     )
     folds = [folds[0]] + [paired(folds[d], "gx", 2 * d) for d in range(1, half)]
 
-    site, long, cotangent, grads, term, to_sides, to_beyond, to_pair = run(
+    site, long, cotangent, grads, term, to_beyond, to_pair = run(
         functools.partial(second_back_kernel, slots, scale, half),
         [
             shape(1, 1, atoms),
@@ -958,15 +1026,14 @@
             shape(features, atoms),
             shape(4, features, atoms),
             shape(features, edges, dtype=BF16),
-            shape(2, features, atoms, dtype=BF16),
-            shape(features, atoms, dtype=BF16),
+            shape(3, features, atoms, dtype=BF16),
             shape(3, features, atoms, dtype=BF16),
         ],
         [hot_back, edge_weights, turn_high, turn_low, charge_pair, sums_two, gate_two, charge,
          energy, energy_slope] + folds,
         name="second_back",
     )
-    from_pair, from_sides = paired(to_pair, "gx", 1), beyond(to_sides, "gx")
+    from_pair, from_beyond = paired(to_pair, "gx", 1), beyond(to_beyond, "gx")
     (middle,) = run(
         second_middle_kernel,
         [shape(3, features, atoms)],
@@ -974,13 +1041,6 @@
         flops=1_000_000_000,
         name="second_middle",
     )
-    sides = [
-        (middle[2 * b] + from_pair[2 * b].astype(F32) + from_sides[b].astype(F32)).astype(BF16)
-        for b in range(2)
-    ]
-    sides, to_beyond = lax.optimization_barrier((sides, to_beyond))
-    from_beyond = beyond(to_beyond, "gx")
-    from_y = [paired(sides[0], "gy", 1), beyond(sides[1], "gy")]
     (edge,) = run(
         functools.partial(second_edge_kernel, slots),
         [shape(32, edges)],
@@ -990,13 +1050,17 @@
     )
     to_pair, middle, to_beyond = run(
         functools.partial(first_back_kernel, slots),
-        [shape(3, 8, atoms)] * 3,
+        [shape(5, 8, atoms)] * 3,
         [ids, basis, slope, unit, kind_high, kind_low, turn_high, turn_low, sums_one, gate_one, edge,
-         long, middle, from_pair, from_beyond] + from_y,
+         long, middle, from_pair, from_beyond],
         name="first_back",
     )
     total = middle + paired(to_pair, "gx", 1) + beyond(to_beyond, "gx")
-    total = total[1] + paired(total[0], "gy", 1) + beyond(total[2], "gy")
+    if grid_y == 4:
+        distant = far(total[0] + total[4], "gy", True)
+    else:
+        distant = far(total[0], "gy", False) + far(total[4], "gy", True)
+    total = total[2] + paired(total[1], "gy", 1) + beyond(total[3], "gy") + distant
     forces = -total[None, :3, None, :]
     return (forces.transpose(0, 2, 1, 3), site)
 

time: 90.9 us -> 90.7 us (level)
  starting transfers between devices: 32.9 us -> 27.5 us
  Pallas kernels: 26.5 us -> 30.9 us
  local copies, waits for them, and re-layouts: 2.07 us -> 5.74 us
  waiting for transfers between devices: 28.1 us -> 25.1 us
    ppermute x9 -> x8, waiting for transfers between devices: 18.7 us -> 14.3 us  [the longest x6 13.9 us: beyond(): lax.ppermute(block, axis, [(other_side(i, count), i) for i in range(count)])]
    pallas_call x20 -> x21, Pallas kernels: 26.5 us -> 30.9 us  [run(): pl.pallas_call(kernel, out_shape=outs, in_specs=specs, out_specs=[whole()...]
    ppermute x9 -> x8, starting transfers between devices: 16.7 us -> 12.8 us  [the longest x6 9.05 us: beyond(): lax.ppermute(block, axis, [(other_side(i, count), i) for i in range(count)])]
    unnamed x23 -> x25, local copies, waits for them, and re-layouts: 1.99 us -> 5.07 us
    ppermute x19 -> x17, starting transfers between devices: 16.2 us -> 14.7 us  [paired(): lax.ppermute(block, axis, [(i ^ mask, i) for i in range(lax.axis_size(axi...]
    ppermute x19 -> x17, waiting for transfers between devices: 9.4 us -> 10.7 us  [paired(): lax.ppermute(block, axis, [(i ^ mask, i) for i in range(lax.axis_size(axi...]
  transfers between devices with their start and end apart: 28 -> 25, of which waited for: 19 -> 18; matrix products, arithmetic and copies ran while one was open for 0% -> 1% of each run, Pallas kernels for 17% -> 16%
where the time goes in v13:
time: 90.7 us; the launch traced here: 90.2 us
  Pallas kernels  30.9 us (34%)
  starting transfers between devices  27.5 us (30%)
  waiting for transfers between devices  25.1 us (28%)
  local copies, waits for them, and re-layouts  5.74 us (6%)
  between operations  0.92 us (1%)
    pallas_call x21, Pallas kernels, run(): pl.pallas_call(kernel, out_shape=outs, in_specs=specs, out_specs=[whole()...  30.9 us
    ppermute x17, starting transfers between devices, paired(): lax.ppermute(block, axis, [(i ^ mask, i) for i in range(lax.axis_size(axi...  14.7 us
    ppermute x6, waiting for transfers between devices, beyond(): lax.ppermute(block, axis, [(other_side(i, count), i) for i in range(count)])  13.9 us
    ppermute x17, waiting for transfers between devices, paired(): lax.ppermute(block, axis, [(i ^ mask, i) for i in range(lax.axis_size(axi...  10.7 us
    ppermute x6, starting transfers between devices, beyond(): lax.ppermute(block, axis, [(other_side(i, count), i) for i in range(count)])  9.05 us
    unnamed x25, local copies, waits for them, and re-layouts  5.07 us
    ppermute x2, starting transfers between devices, far(): return lax.ppermute(block, axis, route)  3.7 us
  transfers between devices with their start and end apart: 25, of which 18 were waited for; matrix products, arithmetic and copies ran while one was open for 1% of the time, Pallas kernels for 16%

profile of v13, /device:TPU:0, one launch (start us, length us, event | category | flops | bytes accessed | tf_op | source)
XLA Modules:
  0.0 90.2 jit_solution(10094049690638836429)
XLA Ops:
  0.7 0.7 broadcast_in_dim.4.place_ref
  1.4 2.2 %pack.1 = (f32[8,128]{1,0:T(8,128)}, f32[40,128]{1,0:T(8,128)}) custom-call(s32[2,8,128]{2,1,0:T(8,128)} %broadcast_in_dim.4.place_ref, f32[1,3,1,256]{3,2,1,0:T(1,128)} %bitcast.42, s32[1,1,256]{2,1,0:T(1,128)} %species_in.1, s32[1,3072]{1,0:T(1,128)} %bitcast.41, s32[1,1,256]{2,1,0:T(1,128)} %count_in.1), custom_call_target="tpu_custom_call" | custom-call | flops 10000000 | bytes 1000000 | tf_op jit(solution)/shard_map/pack/pallas_call | solution.py:55
  3.6 3.0 %collective-permute-start.2 = (f32[8,128]{1,0:T(8,128)}, f32[8,128]{1,0:T(8,128)S(1)}, u32[]{:S(2)}, u32[]{:S(2)}) collective-permute-start(f32[8,128]{1,0:T(8,128)} %get-tuple-element.80), channel_id=1, source_target_pairs={{2,0},{3,1},{0,2},{1,3},{6,4},{7,5},{4,6},{5,7},{10,8},{11,9},{8,1... | collective-permute-start | bytes 12296 | tf_op jit(solution)/shard_map/ppermute | solution.py:42
  6.6 1.4 %collective-permute-start.1 = (f32[40,128]{1,0:T(8,128)}, f32[40,128]{1,0:T(8,128)S(1)}, u32[]{:S(2)}, u32[]{:S(2)}) collective-permute-start(f32[40,128]{1,0:T(8,128)} %get-tuple-element.79.own_ref.block_ref), channel_id=1, source_target_pairs={{3,0},{2,1},{1,2},{0,3},{7,4},{6,5},{5,6},{4,7},{11,8},{10,9},{9,1... | collective-permute-start | bytes 61448 | tf_op jit(solution)/shard_map/ppermute | solution.py:33
  8.0 0.1 collective-permute-start
  8.1 0.3 collective-permute-done.2
  8.4 3.6 %collective-permute-done.y_pair_ref = f32[40,128]{1,0:T(8,128)S(1)} collective-permute-done((f32[40,128]{1,0:T(8,128)}, f32[40,128]{1,0:T(8,128)S(1)}, u32[]{:S(2)}, u32[]{:S(2)}) %collective-permute-start) | collective-permute-done | bytes 20512 | tf_op jit(solution)/shard_map/ppermute | solution.py:24
  12.0 0.7 constant_dynamic-update-slice_fusion.2
  12.7 1.4 %collective-permute-start.4 = (f32[5,8,128]{2,1,0:T(8,128)S(1)}, f32[5,8,128]{2,1,0:T(8,128)S(1)}, u32[]{:S(2)}, u32[]{:S(2)}) collective-permute-start(f32[5,8,128]{2,1,0:T(8,128)S(1)} %constant_dynamic-update-slice_fusion.column_ref.cell_ref), channel_id=1, source_target_pairs={{28,0},{8,4},{4,8},{16,12},{12,16},{24,20},{20,24},{0,28},{29,1},{... | collective-permute-start | bytes 61448 | tf_op jit(solution)/shard_map/ppermute | solution.py:33
  14.1 0.3 collective-permute-start.3
  14.5 0.9 %copy-done.2 = f32[2,2,128,128]{3,2,1,0:T(8,128)S(1)} copy-done((f32[2,2,128,128]{3,2,1,0:T(8,128)S(1)}, f32[2,2,128,128]{3,2,1,0:T(8,128)}, u32[]{:S(2)}) %copy-start.2) | copy-done | bytes 262168
  15.4 0.7 copy-done.7
  16.1 0.7 copy-done.8
  16.8 0.3 prep_first.1
  17.1 0.7 collective-permute-done.4.beyond_ref
  17.8 0.7 copy-done
  18.5 0.7 copy-done.3
  19.2 2.9 %first.1 = (bf16[3,128,256]{2,1,0:T(8,128)(2,1)S(1)}, s32[3,3072]{1,0:T(4,128)S(1)}, f32[3,8,3072]{2,1,0:T(8,128)S(1)}, f32[3,8,3072]{2,1,0:T(8,128)S(1)}, f32[3...) custom-call(s32[2,8,128]{2,1,0:T(8,128)S(1)} %copy-done, ...), custom_call_target="tpu_custom_call" | custom-call | flops 10000000 | bytes 1000000 | tf_op jit(solution)/shard_map/first/pallas_call | solution.py:55
  22.2 2.1 %hot.1.hot_ref = bf16[1536,3072]{1,0:T(8,128)(2,1)S(1)} custom-call(f32[40,128]{1,0:T(8,128)S(1)} %copy-done.3), custom_call_target="tpu_custom_call" | custom-call | flops 1000000 | bytes 1000000 | tf_op jit(solution)/shard_map/hot/pallas_call | solution.py:55
  24.4 0.4 prep_second.1
  24.9 2.2 %collective-permute-start.6 = (bf16[3,128,256]{2,1,0:T(8,128)(2,1)S(1)}, bf16[3,128,256]{2,1,0:T(8,128)(2,1)S(1)}, u32[]{:S(2)}, u32[]{:S(2)}) collective-permute-start(bf16[3,128,256]{2,1,0:T(8,128)(2,1)S(1)} %get-tuple-element.93.column_ref), channel_id=1, source_target_pairs={{28,0},{8,4},{4,8},{16,12},{12,16},{24,20},{20,24},{0,28},{29,1},{... | collective-permute-start | bytes 589832 | tf_op jit(solution)/shard_map/ppermute | solution.py:33
  27.0 1.6 %second_near.1 = (f32[4,128,3072]{2,1,0:T(8,128)S(1)}, f32[128,3072]{1,0:T(8,128)S(1)}) custom-call(f32[3,8,3072]{2,1,0:T(8,128)S(1)} %get-tuple-element.82.basis_ref, f32[3,8,3072]{2,1,0:T(8,128)S(1)} %get-tuple-element.84.unit_ref, bf16[2,128,32]{2,1,0:T(8,128)(2,1)S(1)} %get-tuple-element.92.left_ref, bf16[1536,3072]{1,0:T(8,128)(2,1)S(1)} %hot.1.hot_ref, ...), custom_call_target="tpu_custom_call" | custom-call | flops 2000000000 | bytes 1000000 | tf_op jit(solution)/shard_map/second_near/pallas_call | solution.py:55
  28.6 1.0 %hot_beyond.1.hot_ref = bf16[768,3072]{1,0:T(8,128)(2,1)S(1)} custom-call(s32[3,3072]{1,0:T(4,128)S(1)} %get-tuple-element.81.ids_ref, f32[128,3072]{1,0:T(8,128)S(1)} %get-tuple-element.94.near_ref), custom_call_target="tpu_custom_call" | custom-call | flops 1000000 | bytes 1000000 | tf_op jit(solution)/shard_map/hot_beyond/pallas_call | solution.py:55
  29.6 0.8 second_side.1.near_ref
  30.4 3.2 %collective-permute-done.6.beyond_ref = bf16[3,128,256]{2,1,0:T(8,128)(2,1)S(1)} collective-permute-done((bf16[3,128,256]{2,1,0:T(8,128)(2,1)S(1)}, bf16[3,128,256]{2,1,0:T(8,128)(2,1)S(1)}, u32[]{:S(2)}, u32[]{:S(2)}) %collective-permute-start.6) | collective-permute-done | bytes 196640 | tf_op jit(solution)/shard_map/ppermute | solution.py:33
  33.7 1.9 %second.1 = (bf16[128,3072]{1,0:T(8,128)(2,1)S(1)}, f32[3,128,256]{2,1,0:T(8,128)S(1)}, f32[128,256]{1,0:T(8,128)S(1)}, bf16[80,256]{1,0:T(8,128)(2,1)S(1)}, f32...) custom-call(bf16[768,3072]{1,0:T(8,128)(2,1)S(1)} %hot_beyond.1.hot_ref, f32[4,128,3072]{2,1,0:T(8,128)S(1)} %get-tuple-element.95.weight_ref, ...), custom_call_target="tpu_custom_call" | custom-call | flops 10000000 | bytes 1000000 | tf_op jit(solution)/shard_map/second/pallas_call | solution.py:55
  35.6 0.4 collective-permute-start.8
  36.1 3.9 %collective-permute-start.7 = (bf16[80,256]{1,0:T(8,128)(2,1)S(1)}, bf16[80,256]{1,0:T(8,128)(2,1)S(1)}, u32[]{:S(2)}, u32[]{:S(2)}) collective-permute-start(bf16[80,256]{1,0:T(8,128)(2,1)S(1)} %get-tuple-element.98), channel_id=1, source_target_pairs={{8,0},{12,4},{0,8},{4,12},{24,16},{28,20},{16,24},{20,28},{9,1},{1... | collective-permute-start | bytes 122888 | tf_op jit(solution)/shard_map/ppermute | solution.py:24
  40.0 0.8 green.1.refs_0_
  40.8 0.9 %collective-permute-done.9 = bf16[80,256]{1,0:T(8,128)(2,1)S(1)} collective-permute-done((bf16[80,256]{1,0:T(8,128)(2,1)S(1)}, bf16[80,256]{1,0:T(8,128)(2,1)S(1)}, u32[]{:S(2)}, u32[]{:S(2)}) %collective-permute-start.9) | collective-permute-done | bytes 40992 | tf_op jit(solution)/shard_map/ppermute | solution.py:24
  41.7 0.3 collective-permute-done.7
  42.2 1.2 %structure_near.1 = (f32[32,1024]{1,0:T(8,128)S(1)}, f32[32,1024]{1,0:T(8,128)S(1)}, f32[8,1024]{1,0:T(8,128)S(1)}, f32[8,1024]{1,0:T(8,128)S(1)}, bf16[640,1024...) custom-call(s32[2,8,128]{2,1,0:T(8,128)S(1)} %copy-done, ...), custom_call_target="tpu_custom_call" | custom-call | flops 1000000000 | bytes 1000000 | tf_op jit(solution)/shard_map/structure_near/pallas_call | solution.py:55
  43.4 0.2 collective-permute-done.10.blocks.refs_11_
  43.6 1.3 %structure_far.1 = (f32[32,1024]{1,0:T(8,128)S(1)}, f32[32,1024]{1,0:T(8,128)S(1)}, f32[8,1024]{1,0:T(8,128)S(1)}, f32[8,1024]{1,0:T(8,128)S(1)}, bf16[640,1024]...) custom-call(s32[2,8,128]{2,1,0:T(8,128)S(1)} %copy-done.1, ...), custom_call_target="tpu_custom_call" | custom-call | flops 10000000 | bytes 1000000 | tf_op jit(solution)/shard_map/structure_far/pallas_call | solution.py:55
  44.8 1.6 %collective-permute-start.13 = (bf16[320,128]{1,0:T(8,128)(2,1)S(1)}, bf16[320,128]{1,0:T(8,128)(2,1)S(1)}, u32[]{:S(2)}, u32[]{:S(2)}) collective-permute-start(bf16[320,128]{1,0:T(8,128)(2,1)S(1)} %get-tuple-element.102), channel_id=1, source_target_pairs={{3,0},{2,1},{1,2},{0,3},{7,4},{6,5},{5,6},{4,7},{11,8},{10,9},{9,1... | collective-permute-start | bytes 245768 | tf_op jit(solution)/shard_map/ppermute | solution.py:24
  46.4 0.1 collective-permute-start.12
  46.5 1.9 %collective-permute-start.11 = (bf16[320,128]{1,0:T(8,128)(2,1)S(1)}, bf16[320,128]{1,0:T(8,128)(2,1)S(1)}, u32[]{:S(2)}, u32[]{:S(2)}) collective-permute-start(bf16[320,128]{1,0:T(8,128)(2,1)S(1)} %get-tuple-element.102), channel_id=1, source_target_pairs={{1,0},{0,1},{3,2},{2,3},{5,4},{4,5},{7,6},{6,7},{9,8},{8,9},{11,10... | collective-permute-start | bytes 245768 | tf_op jit(solution)/shard_map/ppermute | solution.py:24
  48.4 2.8 %hot_back.1.hot_ref = bf16[3072,2304]{1,0:T(8,128)(2,1)S(1)} custom-call(s32[3,3072]{1,0:T(4,128)S(1)} %get-tuple-element.81.ids_ref), custom_call_target="tpu_custom_call" | custom-call | flops 2000000000 | bytes 1000000 | tf_op jit(solution)/shard_map/hot_back/pallas_call | solution.py:55
  51.3 1.0 %collective-permute-done.12.refs_3_ = bf16[320,128]{1,0:T(8,128)(2,1)S(1)} collective-permute-done((bf16[320,128]{1,0:T(8,128)(2,1)S(1)}, bf16[320,128]{1,0:T(8,128)(2,1)S(1)}, u32[]{:S(2)}, u32[]{:S(2)}) %collective-permute-start.12) | collective-permute-done | bytes 81952 | tf_op jit(solution)/shard_map/ppermute | solution.py:24
  52.4 1.5 %fold_far.1 = (bf16[4,80,256]{2,1,0:T(8,128)(2,1)S(1)}, f32[640,64]{1,0:T(8,128)S(1)}) custom-call(s32[2,8,128]{2,1,0:T(8,128)S(1)} %copy-done.1, f32[320,128]{1,0:T(8,128)S(1)} %green.1.refs_0_, f32[320,128]{1,0:T(8,128)S(1)} %get-tuple-element.116.refs_1_, bf16[320,128]{1,0:T(8,128)(2,1)S(1)} %collective-permute-done.11.refs_2_, ...), custom_call_target="tpu_custom_call" | custom-call | flops 10000000 | bytes 1000000 | tf_op jit(solution)/shard_map/fold_far/pallas_call | solution.py:55
  54.0 1.2 %fold_near.1.near_ref = f32[4,80,256]{2,1,0:T(8,128)S(1)} custom-call(s32[2,8,128]{2,1,0:T(8,128)S(1)} %copy-done.1, f32[640,64]{1,0:T(8,128)S(1)} %get-tuple-element.126.refs_0_, f32[32,1024]{1,0:T(8,128)S(1)} %get-tuple-element.127.refs_1_, f32[32,1024]{1,0:T(8,128)S(1)} %get-tuple-element.128.refs_2_, f32[8,1024]{1,0:T(8,128)S(1)} %get-tuple-element.129.refs_3_, ...), custom_call_target="tpu_custom_call" | custom-call | flops 1000000000 | bytes 1000000 | tf_op jit(solution)/shard_map/fold_near/pallas_call | solution.py:55
  55.2 0.2 collective-permute-done.14.far_ref
  55.4 2.0 %collective-permute-start.15 = (bf16[80,256]{1,0:T(8,128)(2,1)S(1)}, bf16[80,256]{1,0:T(8,128)(2,1)S(1)}, u32[]{:S(2)}, u32[]{:S(2)}) collective-permute-start(bf16[80,256]{1,0:T(8,128)(2,1)S(1)} %get-tuple-element.135), channel_id=1, source_target_pairs={{8,0},{12,4},{0,8},{4,12},{24,16},{28,20},{16,24},{20,28},{9,1},{1... | collective-permute-start | bytes 122888 | tf_op jit(solution)/shard_map/ppermute | solution.py:24
  57.4 0.9 %collective-permute-start.16 = (bf16[80,256]{1,0:T(8,128)(2,1)S(1)}, bf16[80,256]{1,0:T(8,128)(2,1)S(1)}, u32[]{:S(2)}, u32[]{:S(2)}) collective-permute-start(bf16[80,256]{1,0:T(8,128)(2,1)S(1)} %get-tuple-element.136), channel_id=1, source_target_pairs={{16,0},{20,4},{24,8},{28,12},{0,16},{4,20},{8,24},{12,28},{17,1},{... | collective-permute-start | bytes 122888 | tf_op jit(solution)/shard_map/ppermute | solution.py:24
  58.3 1.6 %collective-permute-start.17 = (bf16[80,256]{1,0:T(8,128)(2,1)S(1)}, bf16[80,256]{1,0:T(8,128)(2,1)S(1)}, u32[]{:S(2)}, u32[]{:S(2)}) collective-permute-start(bf16[80,256]{1,0:T(8,128)(2,1)S(1)} %get-tuple-element.137), channel_id=1, source_target_pairs={{24,0},{28,4},{16,8},{20,12},{8,16},{12,20},{0,24},{4,28},{25,1},{... | collective-permute-start | bytes 122888 | tf_op jit(solution)/shard_map/ppermute | solution.py:24
  59.9 0.5 readout.1
  60.4 2.8 %collective-permute-done.16.refs_2_ = bf16[80,256]{1,0:T(8,128)(2,1)S(1)} collective-permute-done((bf16[80,256]{1,0:T(8,128)(2,1)S(1)}, bf16[80,256]{1,0:T(8,128)(2,1)S(1)}, u32[]{:S(2)}, u32[]{:S(2)}) %collective-permute-start.16) | collective-permute-done | bytes 40992 | tf_op jit(solution)/shard_map/ppermute | solution.py:24
  63.2 1.0 %collective-permute-done.17.refs_3_ = bf16[80,256]{1,0:T(8,128)(2,1)S(1)} collective-permute-done((bf16[80,256]{1,0:T(8,128)(2,1)S(1)}, bf16[80,256]{1,0:T(8,128)(2,1)S(1)}, u32[]{:S(2)}, u32[]{:S(2)}) %collective-permute-start.17) | collective-permute-done | bytes 40992 | tf_op jit(solution)/shard_map/ppermute | solution.py:24
  64.3 2.7 %second_back.1 = (f32[1,1,256]{2,1,0:T(1,128)}, f32[8,256]{1,0:T(8,128)S(1)}, f32[128,256]{1,0:T(8,128)S(1)}, f32[4,128,256]{2,1,0:T(8,128)S(1)}, bf16[128,3072]...) custom-call(bf16[3072,2304]{1,0:T(8,128)(2,1)S(1)} %hot_back.1.hot_ref, ...), custom_call_target="tpu_custom_call" | custom-call | flops 10000000 | bytes 1000000 | tf_op jit(solution)/shard_map/second_back/pallas_call | solution.py:55
  66.9 1.6 %collective-permute-start.19 = (bf16[3,128,256]{2,1,0:T(8,128)(2,1)S(1)}, bf16[3,128,256]{2,1,0:T(8,128)(2,1)S(1)}, u32[]{:S(2)}, u32[]{:S(2)}) collective-permute-start(bf16[3,128,256]{2,1,0:T(8,128)(2,1)S(1)} %get-tuple-element.143), channel_id=1, source_target_pairs={{28,0},{8,4},{4,8},{16,12},{12,16},{24,20},{20,24},{0,28},{29,1},{... | collective-permute-start | bytes 589832 | tf_op jit(solution)/shard_map/ppermute | solution.py:33
  68.5 0.8 second_middle.1.middle_ref
  69.3 1.2 %second_edge.1.edge_ref = f32[32,3072]{1,0:T(8,128)S(1)} custom-call(bf16[2,16,256]{2,1,0:T(8,128)(2,1)S(1)} %get-tuple-element.91.back_ref, bf16[128,3072]{1,0:T(8,128)(2,1)S(1)} %get-tuple-element.97.feature_ref, f32[4,128,256]{2,1,0:T(8,128)S(1)} %get-tuple-element.138.grad_ref), custom_call_target="tpu_custom_call" | custom-call | flops 1000000000 | bytes 1000000 | tf_op jit(solution)/shard_map/second_edge/pallas_call | solution.py:55
  70.5 4.4 %collective-permute-done.19.from_beyond = bf16[3,128,256]{2,1,0:T(8,128)(2,1)S(1)} collective-permute-done((bf16[3,128,256]{2,1,0:T(8,128)(2,1)S(1)}, bf16[3,128,256]{2,1,0:T(8,128)(2,1)S(1)}, u32[]{:S(2)}, u32[]{:S(2)}) %collective-permute-start.19) | collective-permute-done | bytes 196640 | tf_op jit(solution)/shard_map/ppermute | solution.py:33
  74.9 3.6 %first_back.1 = (f32[5,8,256]{2,1,0:T(8,128)S(1)}, f32[5,8,256]{2,1,0:T(8,128)S(1)}, f32[5,8,256]{2,1,0:T(8,128)S(1)}) custom-call(s32[3,3072]{1,0:T(4,128)S(1)} %get-tuple-element.81.ids_ref, f32[3,8,3072]{2,1,0:T(8,128)S(1)} %get-tuple-element.82.basis_ref, f32[3,8,3072]{2,1,0:T(8,128)S(1)} %get-tuple-element.83.slope_ref, ...), custom_call_target="tpu_custom_call" | custom-call | flops 10000000 | bytes 1000000 | tf_op jit(solution)/shard_map/first_back/pallas_call | solution.py:55
  78.6 1.1 %collective-permute-start.21 = (f32[5,8,256]{2,1,0:T(8,128)S(1)}, f32[5,8,256]{2,1,0:T(8,128)S(1)}, u32[]{:S(2)}, u32[]{:S(2)}) collective-permute-start(f32[5,8,256]{2,1,0:T(8,128)S(1)} %get-tuple-element.146), channel_id=1, source_target_pairs={{28,0},{8,4},{4,8},{16,12},{12,16},{24,20},{20,24},{0,28},{29,1},{... | collective-permute-start | bytes 122888 | tf_op jit(solution)/shard_map/ppermute | solution.py:33
  79.7 0.1 collective-permute-done.20
  79.9 4.1 %collective-permute-done.21 = f32[5,8,256]{2,1,0:T(8,128)S(1)} collective-permute-done((f32[5,8,256]{2,1,0:T(8,128)S(1)}, f32[5,8,256]{2,1,0:T(8,128)S(1)}, u32[]{:S(2)}, u32[]{:S(2)}) %collective-permute-start.21) | collective-permute-done | bytes 40992 | tf_op jit(solution)/shard_map/ppermute | solution.py:33
  84.0 0.7 collective-permute-start.24
  84.6 1.3 %collective-permute-start.23 = (f32[8,256]{1,0:T(8,128)S(1)}, f32[8,256]{1,0:T(8,128)S(1)}, u32[]{:S(2)}, u32[]{:S(2)}) collective-permute-start(f32[8,256]{1,0:T(8,128)S(1)} %get-tuple-element.152), channel_id=1, source_target_pairs={{3,0},{2,1},{1,2},{0,3},{7,4},{6,5},{5,6},{4,7},{11,8},{10,9},{9,1... | collective-permute-start | bytes 24584 | tf_op jit(solution)/shard_map/ppermute | solution.py:33
  86.0 1.5 %collective-permute-start.22 = (f32[8,256]{1,0:T(8,128)S(1)}, f32[8,256]{1,0:T(8,128)S(1)}, u32[]{:S(2)}, u32[]{:S(2)}) collective-permute-start(f32[8,256]{1,0:T(8,128)S(1)} %get-tuple-element.153), channel_id=1, source_target_pairs={{1,0},{0,1},{3,2},{2,3},{5,4},{4,5},{7,6},{6,7},{9,8},{8,9},{11,10... | collective-permute-start | bytes 24584 | tf_op jit(solution)/shard_map/ppermute | solution.py:24
  87.5 0.2 collective-permute-done.24
  87.7 1.5 %collective-permute-done.23 = f32[8,256]{1,0:T(8,128)S(1)} collective-permute-done((f32[8,256]{1,0:T(8,128)S(1)}, f32[8,256]{1,0:T(8,128)S(1)}, u32[]{:S(2)}, u32[]{:S(2)}) %collective-permute-start.23) | collective-permute-done | bytes 8224 | tf_op jit(solution)/shard_map/ppermute | solution.py:33
  89.2 0.4 collective-permute-done.22
  89.6 0.6 copy.13
  (39 shorter events, 0.7 us)
Async XLA Ops:
  3.6 4.8 %collective-permute-start.2 = (f32[8,128]{1,0:T(8,128)}, f32[8,128]{1,0:T(8,128)S(1)}, u32[]{:S(2)}, u32[]{:S(2)}) collective-permute-start(f32[8,128]{1,0:T(8,128)} %get-tuple-element.80), channel_id=1, source_target_pairs={{2,0},{3,1},{0,2},{1,3},{6,4},{7,5},{4,6},{5,7},{10,8},{11,9},{8,1... | collective-permute-start | bytes 12296 | tf_op jit(solution)/shard_map/ppermute | solution.py:42
  6.6 6.1 %collective-permute-start.1 = (f32[40,128]{1,0:T(8,128)}, f32[40,128]{1,0:T(8,128)S(1)}, u32[]{:S(2)}, u32[]{:S(2)}) collective-permute-start(f32[40,128]{1,0:T(8,128)} %get-tuple-element.79.own_ref.block_ref), channel_id=1, source_target_pairs={{3,0},{2,1},{1,2},{0,3},{7,4},{6,5},{5,6},{4,7},{11,8},{10,9},{9,1... | collective-permute-start | bytes 61448 | tf_op jit(solution)/shard_map/ppermute | solution.py:33
  8.0 4.0 %collective-permute-start = (f32[40,128]{1,0:T(8,128)}, f32[40,128]{1,0:T(8,128)S(1)}, u32[]{:S(2)}, u32[]{:S(2)}) collective-permute-start(f32[40,128]{1,0:T(8,128)} %get-tuple-element.79.own_ref.block_ref), channel_id=1, source_target_pairs={{1,0},{0,1},{3,2},{2,3},{5,4},{4,5},{7,6},{6,7},{9,8},{8,9},{11,10... | collective-permute-start | bytes 61448 | tf_op jit(solution)/shard_map/ppermute | solution.py:24
  12.7 5.1 %collective-permute-start.4 = (f32[5,8,128]{2,1,0:T(8,128)S(1)}, f32[5,8,128]{2,1,0:T(8,128)S(1)}, u32[]{:S(2)}, u32[]{:S(2)}) collective-permute-start(f32[5,8,128]{2,1,0:T(8,128)S(1)} %constant_dynamic-update-slice_fusion.column_ref.cell_ref), channel_id=1, source_target_pairs={{28,0},{8,4},{4,8},{16,12},{12,16},{24,20},{20,24},{0,28},{29,1},{... | collective-permute-start | bytes 61448 | tf_op jit(solution)/shard_map/ppermute | solution.py:33
  14.1 3.7 %collective-permute-start.3 = (f32[5,8,128]{2,1,0:T(8,128)S(1)}, f32[5,8,128]{2,1,0:T(8,128)S(1)}, u32[]{:S(2)}, u32[]{:S(2)}) collective-permute-start(f32[5,8,128]{2,1,0:T(8,128)S(1)} %constant_dynamic-update-slice_fusion.column_ref.cell_ref), channel_id=1, source_target_pairs={{4,0},{0,4},{12,8},{8,12},{20,16},{16,20},{28,24},{24,28},{5,1},{1... | collective-permute-start | bytes 61448 | tf_op jit(solution)/shard_map/ppermute | solution.py:24
  14.5 0.9 %copy-start.2 = (f32[2,2,128,128]{3,2,1,0:T(8,128)S(1)}, f32[2,2,128,128]{3,2,1,0:T(8,128)}, u32[]{:S(2)}) copy-start(f32[2,2,128,128]{3,2,1,0:T(8,128)} %mixing_in.1) | copy-start | bytes 786436
  15.4 0.7 copy-start.7
  16.1 0.7 copy-start.8
  17.8 0.7 copy-start
  18.5 0.7 copy-start.3
  22.1 2.3 %copy-start.4 = (f32[128,128]{1,0:T(8,128)S(1)}, f32[128,128]{1,0:T(8,128)}, u32[]{:S(2)}) copy-start(f32[128,128]{1,0:T(8,128)} %hidden_in.1) | copy-start | bytes 196612
  22.1 2.3 %copy-start.6 = (f32[128,64]{0,1:T(8,128)S(1)}, f32[128,64]{0,1:T(8,128)}, u32[]{:S(2)}) copy-start(f32[128,64]{0,1:T(8,128)} %param.20) | copy-start | bytes 98308
  22.1 2.3 %copy-start.9 = (f32[128]{0:T(128)S(1)}, f32[128]{0:T(128)}, u32[]{:S(2)}) copy-start(f32[128]{0:T(128)} %param.19) | copy-start | bytes 1540
  22.2 7.4 %collective-permute-start.5 = (bf16[3,128,256]{2,1,0:T(8,128)(2,1)S(1)}, bf16[3,128,256]{2,1,0:T(8,128)(2,1)S(1)}, u32[]{:S(2)}, u32[]{:S(2)}) collective-permute-start(bf16[3,128,256]{2,1,0:T(8,128)(2,1)S(1)} %get-tuple-element.93.column_ref), channel_id=1, source_target_pairs={{4,0},{0,4},{12,8},{8,12},{20,16},{16,20},{28,24},{24,28},{5,1},{1... | collective-permute-start | bytes 589832 | tf_op jit(solution)/shard_map/ppermute | solution.py:24
  24.9 8.8 %collective-permute-start.6 = (bf16[3,128,256]{2,1,0:T(8,128)(2,1)S(1)}, bf16[3,128,256]{2,1,0:T(8,128)(2,1)S(1)}, u32[]{:S(2)}, u32[]{:S(2)}) collective-permute-start(bf16[3,128,256]{2,1,0:T(8,128)(2,1)S(1)} %get-tuple-element.93.column_ref), channel_id=1, source_target_pairs={{28,0},{8,4},{4,8},{16,12},{12,16},{24,20},{20,24},{0,28},{29,1},{... | collective-permute-start | bytes 589832 | tf_op jit(solution)/shard_map/ppermute | solution.py:33
  33.7 6.3 %copy-start.5 = (s32[3,4096]{1,0:T(4,128)S(1)}, s32[3,4096]{1,0:T(4,128)}, u32[]{:S(2)}) copy-start(s32[3,4096]{1,0:T(4,128)} %vec_ref.1) | copy-start | bytes 147460
  35.6 6.2 %collective-permute-start.9 = (bf16[80,256]{1,0:T(8,128)(2,1)S(1)}, bf16[80,256]{1,0:T(8,128)(2,1)S(1)}, u32[]{:S(2)}, u32[]{:S(2)}) collective-permute-start(bf16[80,256]{1,0:T(8,128)(2,1)S(1)} %get-tuple-element.98), channel_id=1, source_target_pairs={{24,0},{28,4},{16,8},{20,12},{8,16},{12,20},{0,24},{4,28},{25,1},{... | collective-permute-start | bytes 122888 | tf_op jit(solution)/shard_map/ppermute | solution.py:24
  35.6 6.1 %collective-permute-start.8 = (bf16[80,256]{1,0:T(8,128)(2,1)S(1)}, bf16[80,256]{1,0:T(8,128)(2,1)S(1)}, u32[]{:S(2)}, u32[]{:S(2)}) collective-permute-start(bf16[80,256]{1,0:T(8,128)(2,1)S(1)} %get-tuple-element.98), channel_id=1, source_target_pairs={{16,0},{20,4},{24,8},{28,12},{0,16},{4,20},{8,24},{12,28},{17,1},{... | collective-permute-start | bytes 122888 | tf_op jit(solution)/shard_map/ppermute | solution.py:24
  36.1 6.0 %collective-permute-start.7 = (bf16[80,256]{1,0:T(8,128)(2,1)S(1)}, bf16[80,256]{1,0:T(8,128)(2,1)S(1)}, u32[]{:S(2)}, u32[]{:S(2)}) collective-permute-start(bf16[80,256]{1,0:T(8,128)(2,1)S(1)} %get-tuple-element.98), channel_id=1, source_target_pairs={{8,0},{12,4},{0,8},{4,12},{24,16},{28,20},{16,24},{20,28},{9,1},{1... | collective-permute-start | bytes 122888 | tf_op jit(solution)/shard_map/ppermute | solution.py:24
  42.1 1.5 %copy-start.1 = (s32[2,8,128]{2,1,0:T(8,128)S(1)}, s32[2,8,128]{2,1,0:T(8,128)}, u32[]{:S(2)}) copy-start(s32[2,8,128]{2,1,0:T(8,128)} %broadcast_in_dim.4.place_ref) | copy-start | bytes 24580
  42.1 1.5 %collective-permute-start.10 = (bf16[4,80,256]{2,1,0:T(8,128)(2,1)S(1)}, bf16[4,80,256]{2,1,0:T(8,128)(2,1)S(1)}, u32[]{:S(2)}, u32[]{:S(2)}) collective-permute-start(bf16[4,80,256]{2,1,0:T(8,128)(2,1)S(1)} %pad_maximum_fusion.blocks.refs_7_), channel_id=1, source_target_pairs={{4,0},{0,4},{12,8},{8,12},{20,16},{16,20},{28,24},{24,28},{5,1},{1... | collective-permute-start | bytes 491528 | tf_op jit(solution)/shard_map/ppermute | solution.py:24
  44.8 6.4 %collective-permute-start.13 = (bf16[320,128]{1,0:T(8,128)(2,1)S(1)}, bf16[320,128]{1,0:T(8,128)(2,1)S(1)}, u32[]{:S(2)}, u32[]{:S(2)}) collective-permute-start(bf16[320,128]{1,0:T(8,128)(2,1)S(1)} %get-tuple-element.102), channel_id=1, source_target_pairs={{3,0},{2,1},{1,2},{0,3},{7,4},{6,5},{5,6},{4,7},{11,8},{10,9},{9,1... | collective-permute-start | bytes 245768 | tf_op jit(solution)/shard_map/ppermute | solution.py:24
  46.4 5.9 %collective-permute-start.12 = (bf16[320,128]{1,0:T(8,128)(2,1)S(1)}, bf16[320,128]{1,0:T(8,128)(2,1)S(1)}, u32[]{:S(2)}, u32[]{:S(2)}) collective-permute-start(bf16[320,128]{1,0:T(8,128)(2,1)S(1)} %get-tuple-element.102), channel_id=1, source_target_pairs={{2,0},{3,1},{0,2},{1,3},{6,4},{7,5},{4,6},{5,7},{10,8},{11,9},{8,1... | collective-permute-start | bytes 245768 | tf_op jit(solution)/shard_map/ppermute | solution.py:24
  46.5 5.9 %collective-permute-start.11 = (bf16[320,128]{1,0:T(8,128)(2,1)S(1)}, bf16[320,128]{1,0:T(8,128)(2,1)S(1)}, u32[]{:S(2)}, u32[]{:S(2)}) collective-permute-start(bf16[320,128]{1,0:T(8,128)(2,1)S(1)} %get-tuple-element.102), channel_id=1, source_target_pairs={{1,0},{0,1},{3,2},{2,3},{5,4},{4,5},{7,6},{6,7},{9,8},{8,9},{11,10... | collective-permute-start | bytes 245768 | tf_op jit(solution)/shard_map/ppermute | solution.py:24
  53.9 1.5 %collective-permute-start.14 = (bf16[4,80,256]{2,1,0:T(8,128)(2,1)S(1)}, bf16[4,80,256]{2,1,0:T(8,128)(2,1)S(1)}, u32[]{:S(2)}, u32[]{:S(2)}) collective-permute-start(bf16[4,80,256]{2,1,0:T(8,128)(2,1)S(1)} %get-tuple-element.133), channel_id=1, source_target_pairs={{4,0},{0,4},{12,8},{8,12},{20,16},{16,20},{28,24},{24,28},{5,1},{1... | collective-permute-start | bytes 491528 | tf_op jit(solution)/shard_map/ppermute | solution.py:24
  55.4 5.0 %collective-permute-start.15 = (bf16[80,256]{1,0:T(8,128)(2,1)S(1)}, bf16[80,256]{1,0:T(8,128)(2,1)S(1)}, u32[]{:S(2)}, u32[]{:S(2)}) collective-permute-start(bf16[80,256]{1,0:T(8,128)(2,1)S(1)} %get-tuple-element.135), channel_id=1, source_target_pairs={{8,0},{12,4},{0,8},{4,12},{24,16},{28,20},{16,24},{20,28},{9,1},{1... | collective-permute-start | bytes 122888 | tf_op jit(solution)/shard_map/ppermute | solution.py:24
  57.4 5.8 %collective-permute-start.16 = (bf16[80,256]{1,0:T(8,128)(2,1)S(1)}, bf16[80,256]{1,0:T(8,128)(2,1)S(1)}, u32[]{:S(2)}, u32[]{:S(2)}) collective-permute-start(bf16[80,256]{1,0:T(8,128)(2,1)S(1)} %get-tuple-element.136), channel_id=1, source_target_pairs={{16,0},{20,4},{24,8},{28,12},{0,16},{4,20},{8,24},{12,28},{17,1},{... | collective-permute-start | bytes 122888 | tf_op jit(solution)/shard_map/ppermute | solution.py:24
  58.3 5.9 %collective-permute-start.17 = (bf16[80,256]{1,0:T(8,128)(2,1)S(1)}, bf16[80,256]{1,0:T(8,128)(2,1)S(1)}, u32[]{:S(2)}, u32[]{:S(2)}) collective-permute-start(bf16[80,256]{1,0:T(8,128)(2,1)S(1)} %get-tuple-element.137), channel_id=1, source_target_pairs={{24,0},{28,4},{16,8},{20,12},{8,16},{12,20},{0,24},{4,28},{25,1},{... | collective-permute-start | bytes 122888 | tf_op jit(solution)/shard_map/ppermute | solution.py:24
  66.9 3.6 %collective-permute-start.18 = (bf16[3,128,256]{2,1,0:T(8,128)(2,1)S(1)}, bf16[3,128,256]{2,1,0:T(8,128)(2,1)S(1)}, u32[]{:S(2)}, u32[]{:S(2)}) collective-permute-start(bf16[3,128,256]{2,1,0:T(8,128)(2,1)S(1)} %get-tuple-element.142), channel_id=1, source_target_pairs={{4,0},{0,4},{12,8},{8,12},{20,16},{16,20},{28,24},{24,28},{5,1},{1... | collective-permute-start | bytes 589832 | tf_op jit(solution)/shard_map/ppermute | solution.py:24
  66.9 8.0 %collective-permute-start.19 = (bf16[3,128,256]{2,1,0:T(8,128)(2,1)S(1)}, bf16[3,128,256]{2,1,0:T(8,128)(2,1)S(1)}, u32[]{:S(2)}, u32[]{:S(2)}) collective-permute-start(bf16[3,128,256]{2,1,0:T(8,128)(2,1)S(1)} %get-tuple-element.143), channel_id=1, source_target_pairs={{28,0},{8,4},{4,8},{16,12},{12,16},{24,20},{20,24},{0,28},{29,1},{... | collective-permute-start | bytes 589832 | tf_op jit(solution)/shard_map/ppermute | solution.py:33
  78.6 1.3 %collective-permute-start.20 = (f32[5,8,256]{2,1,0:T(8,128)S(1)}, f32[5,8,256]{2,1,0:T(8,128)S(1)}, u32[]{:S(2)}, u32[]{:S(2)}) collective-permute-start(f32[5,8,256]{2,1,0:T(8,128)S(1)} %get-tuple-element.145), channel_id=1, source_target_pairs={{4,0},{0,4},{12,8},{8,12},{20,16},{16,20},{28,24},{24,28},{5,1},{1... | collective-permute-start | bytes 122888 | tf_op jit(solution)/shard_map/ppermute | solution.py:24
  78.6 5.3 %collective-permute-start.21 = (f32[5,8,256]{2,1,0:T(8,128)S(1)}, f32[5,8,256]{2,1,0:T(8,128)S(1)}, u32[]{:S(2)}, u32[]{:S(2)}) collective-permute-start(f32[5,8,256]{2,1,0:T(8,128)S(1)} %get-tuple-element.146), channel_id=1, source_target_pairs={{28,0},{8,4},{4,8},{16,12},{12,16},{24,20},{20,24},{0,28},{29,1},{... | collective-permute-start | bytes 122888 | tf_op jit(solution)/shard_map/ppermute | solution.py:33
  84.0 3.7 %collective-permute-start.24 = (f32[8,256]{1,0:T(8,128)S(1)}, f32[8,256]{1,0:T(8,128)S(1)}, u32[]{:S(2)}, u32[]{:S(2)}) collective-permute-start(f32[8,256]{1,0:T(8,128)S(1)} %get-tuple-element.151), channel_id=1, source_target_pairs={{2,0},{3,1},{0,2},{1,3},{6,4},{7,5},{4,6},{5,7},{10,8},{11,9},{8,1... | collective-permute-start | bytes 24584 | tf_op jit(solution)/shard_map/ppermute | solution.py:42
  84.6 4.5 %collective-permute-start.23 = (f32[8,256]{1,0:T(8,128)S(1)}, f32[8,256]{1,0:T(8,128)S(1)}, u32[]{:S(2)}, u32[]{:S(2)}) collective-permute-start(f32[8,256]{1,0:T(8,128)S(1)} %get-tuple-element.152), channel_id=1, source_target_pairs={{3,0},{2,1},{1,2},{0,3},{7,4},{6,5},{5,6},{4,7},{11,8},{10,9},{9,1... | collective-permute-start | bytes 24584 | tf_op jit(solution)/shard_map/ppermute | solution.py:33
  86.0 3.7 %collective-permute-start.22 = (f32[8,256]{1,0:T(8,128)S(1)}, f32[8,256]{1,0:T(8,128)S(1)}, u32[]{:S(2)}, u32[]{:S(2)}) collective-permute-start(f32[8,256]{1,0:T(8,128)S(1)} %get-tuple-element.153), channel_id=1, source_target_pairs={{1,0},{0,1},{3,2},{2,3},{5,4},{4,5},{7,6},{6,7},{9,8},{8,9},{11,10... | collective-permute-start | bytes 24584 | tf_op jit(solution)/shard_map/ppermute | solution.py:24

commit v14 on v13

--- a/solution.py
+++ b/solution.py
@@ -156,18 +156,22 @@
     return [basis] + [basis * unit[i : i + 1] for i in range(3)]
 
 
-def pack_kernel(place_ref, position_in, species_in, ids_in, count_in, place_out, block_out, position,
-                species, ids, count, sems):
-    fetch([position_in, species_in, ids_in, count_in], [position, species, ids, count], sems)
-    rows = [position[0, i] for i in range(3)] + [species[0].astype(F32)]
+def pack_kernel(place_ref, position_ref, species_ref, out_ref):
+    rows = [position_ref[0, i] for i in range(3)] + [species_ref[0].astype(F32)]
     atoms = rows[0].shape[1]
-    rows = [row[:, s : s + 128] for row in rows for s in range(0, atoms, 128)]
-    place_out[...] = jnp.concatenate(rows, axis=0)
-    order = slot_order(ids[...], place_ref, atoms).astype(F32)
+    out_ref[...] = jnp.concatenate(
+        [row[:, s : s + 128] for row in rows for s in range(0, atoms, 128)], axis=0
+    )
+
+
+def pack_more_kernel(place_ref, ids_ref, count_ref, first_ref, out_ref):
+    atoms = count_ref.shape[2]
+    order = slot_order(ids_ref[...], place_ref, atoms).astype(F32)
+    rows = [first_ref[...]]
     rows += [order[:, s : s + 128] for s in range(0, order.shape[1], 128)]
-    rows += [count[0, :, s : s + 128].astype(F32) for s in range(0, atoms, 128)]
-    rows += [jnp.zeros((block_out.shape[0] - len(rows), 128), F32)]
-    block_out[...] = jnp.concatenate(rows, axis=0)
+    rows += [count_ref[0, :, s : s + 128].astype(F32) for s in range(0, atoms, 128)]
+    missing = out_ref.shape[0] - sum(row.shape[0] for row in rows)
+    out_ref[...] = jnp.concatenate(rows + [jnp.zeros((missing, 128), F32)], axis=0)
 
 
 def block_ids(block, atoms, edges):
@@ -243,13 +247,6 @@
     high = charge.astype(BF16).astype(F32)
     charge_pair[0] = high.astype(BF16)
     charge_pair[1] = (charge - high).astype(BF16)
-
-
-def hot_kernel(atoms, block_ref, hot_ref):
-    ids, _ = block_ids(block_ref[...], atoms, hot_ref.shape[1])
-    for start in range(0, hot_ref.shape[1], 256):
-        lanes = slice(start, start + 256)
-        hot_ref[:, lanes] = hot_columns(ids[:, lanes], hot_ref.shape[0])
 
 
 def hot_beyond_kernel(ids_ref, near_ref, hot_ref):
@@ -365,7 +362,7 @@
     return jnp.where(ids == place, 1.0, 0.0).astype(BF16)
 
 
-def second_near_kernel(slots, basis_ref, unit_ref, left_ref, hot_ref, column_ref, weight_ref,
+def second_near_kernel(slots, ids_ref, basis_ref, unit_ref, left_ref, column_ref, weight_ref,
                        near_ref):
     atoms = column_ref.shape[2]
     parts = edge_parts(basis_ref[1], unit_ref[1])
@@ -374,15 +371,17 @@
         lanes = slice(n * atoms, (n + 1) * atoms)
         for part in range(4):
             weight_ref[part, :, lanes] = weights_of(left_ref, part, parts[part][:, lanes])
-        near_ref[:, lanes] = dot(source, hot_ref[3 * atoms : 6 * atoms, lanes])
-
-
-def second_side_kernel(slots, hot_ref, near_ref, pair_ref, out_ref):
+        ids = ids_ref[1:2, lanes] - 3 * atoms
+        near_ref[:, lanes] = dot(source, hot_columns(ids, 3 * atoms))
+
+
+def second_side_kernel(slots, ids_ref, near_ref, pair_ref, out_ref):
     atoms = pair_ref.shape[2]
     source = jnp.concatenate([pair_ref[b] for b in range(3)], axis=1)
     for n in range(slots):
         lanes = slice(n * atoms, (n + 1) * atoms)
-        out_ref[:, lanes] = near_ref[:, lanes] + dot(source, hot_ref[: 3 * atoms, lanes])
+        hot = hot_columns(ids_ref[1:2, lanes], 3 * atoms)
+        out_ref[:, lanes] = near_ref[:, lanes] + dot(source, hot)
 
 
 def second_kernel(slots, hot_ref, weight_ref, near_ref, mix_high, mix_low, charge_ref, cell_ref,
@@ -824,20 +823,18 @@
     block_total = -(-(cell_rows + (edges + atoms) // 128) // 8) * 8
     dma = pltpu.SemaphoreType.DMA
     shown = positions.transpose(0, 2, 1, 3)
-    own_place, own = run(
+    (own_place,) = run(
         pack_kernel,
-        [shape(cell_rows, 128), shape(block_total, 128)],
-        [place, shown, species, ids, counts],
-        scratch=[
-            pltpu.VMEM(shown.shape, F32),
-            pltpu.VMEM(species.shape, jnp.int32),
-            pltpu.VMEM(ids.shape, jnp.int32),
-            pltpu.VMEM(counts.shape, jnp.int32),
-            dma((4,)),
-        ],
-        hbm=4,
-        grant=60,
+        [shape(cell_rows, 128)],
+        [place, shown, species],
+        flops=10_000_000_000,
         name="pack",
+    )
+    (own,) = run(
+        pack_more_kernel,
+        [shape(block_total, 128)],
+        [place, ids, counts, own_place],
+        name="pack_more",
     )
     y_pair, y_beyond = paired(own, "gy", 1), beyond(own, "gy")
     over_pair = far(own_place, "gy", True)
@@ -871,13 +868,6 @@
         hbm=3,
         name="prep_first",
     )
-    (hot,) = run(
-        functools.partial(hot_kernel, atoms),
-        [shape(6 * atoms, edges, dtype=BF16)],
-        [own],
-        flops=1_000_000,
-        name="hot",
-    )
     read_out, hidden_high, hidden_low, hidden_turn_high, hidden_turn_low, charge_pair = run(
         prep_second_kernel,
         [shape(1, features)]
@@ -893,6 +883,7 @@
         hbm=3,
         name="prep_second",
     )
+    cells, hidden_high = lax.optimization_barrier((cells, hidden_high))
     low, ids, basis, slope, unit, sums_one, gate_one = run(
         functools.partial(first_kernel, slots),
         [
@@ -911,7 +902,7 @@
     edge_weights, near = run(
         functools.partial(second_near_kernel, slots),
         [shape(4, features, edges), shape(features, edges)],
-        [basis, unit, left, hot, low],
+        [ids, basis, unit, left, low],
         flops=2_000_000_000,
         name="second_near",
     )
@@ -925,7 +916,7 @@
     (near,) = run(
         functools.partial(second_side_kernel, slots),
         [shape(features, edges)],
-        [hot, near, hidden[0]],
+        [ids, near, hidden[0]],
         flops=1_000_000_000,
         name="second_side",
     )

time: 90.7 us -> 83.9 us (0.925)
  Pallas kernels: 30.9 us -> 26.9 us
  local copies, waits for them, and re-layouts: 5.74 us -> 2.08 us
    pallas_call x21, Pallas kernels: 30.9 us -> 26.9 us  [run(): pl.pallas_call(kernel, out_shape=outs, in_specs=specs, out_specs=[whole()...]
    unnamed x25 -> x27, local copies, waits for them, and re-layouts: 5.07 us -> 2 us
    ppermute x6, waiting for transfers between devices: 13.9 us -> 15.7 us  [beyond(): lax.ppermute(block, axis, [(other_side(i, count), i) for i in range(count)])]
  transfers between devices with their start and end apart: 25 -> 25, of which waited for: 18 -> 16; matrix products, arithmetic and copies ran while one was open for 1% -> 0% of each run, Pallas kernels for 16% -> 15%
where the time goes in v14:
time: 83.9 us; the launch traced here: 83.7 us
  starting transfers between devices  27.9 us (33%)
  Pallas kernels  26.9 us (32%)
  waiting for transfers between devices  25.8 us (31%)
  local copies, waits for them, and re-layouts  2.08 us (2%)
  between operations  0.95 us (1%)
    pallas_call x21, Pallas kernels, run(): pl.pallas_call(kernel, out_shape=outs, in_specs=specs, out_specs=[whole()...  26.9 us
    ppermute x6, waiting for transfers between devices, beyond(): lax.ppermute(block, axis, [(other_side(i, count), i) for i in range(count)])  15.7 us
    ppermute x17, starting transfers between devices, paired(): lax.ppermute(block, axis, [(i ^ mask, i) for i in range(lax.axis_size(axi...  14.5 us
    ppermute x17, waiting for transfers between devices, paired(): lax.ppermute(block, axis, [(i ^ mask, i) for i in range(lax.axis_size(axi...  9.93 us
    ppermute x6, starting transfers between devices, beyond(): lax.ppermute(block, axis, [(other_side(i, count), i) for i in range(count)])  9.19 us
    ppermute x2, starting transfers between devices, far(): return lax.ppermute(block, axis, route)  4.14 us
    unnamed x27, local copies, waits for them, and re-layouts  2 us
  transfers between devices with their start and end apart: 25, of which 16 were waited for; matrix products, arithmetic and copies ran while one was open for 0% of the time, Pallas kernels for 15%

profile of v14, /device:TPU:0, one launch (start us, length us, event | category | flops | bytes accessed | tf_op | source)
XLA Modules:
  0.0 83.7 jit_solution(16448220542885920771)
XLA Ops:
  0.6 0.1 pad_add_fusion
  0.7 0.1 broadcast_in_dim.4.place_ref
  0.8 0.7 copy-done.9
  1.5 0.7 copy-done.10
  2.2 3.0 %collective-permute-start.2 = (f32[8,128]{1,0:T(8,128)S(1)}, f32[8,128]{1,0:T(8,128)S(1)}, u32[]{:S(2)}, u32[]{:S(2)}) collective-permute-start(f32[8,128]{1,0:T(8,128)S(1)} %pack.1.first_ref), channel_id=1, source_target_pairs={{2,0},{3,1},{0,2},{1,3},{6,4},{7,5},{4,6},{5,7},{10,8},{11,9},{8,1... | collective-permute-start | bytes 12296 | tf_op jit(solution)/shard_map/ppermute | solution.py:42
  5.3 0.1 pack_more.1.own_ref
  5.4 1.6 %collective-permute-start.1 = (f32[40,128]{1,0:T(8,128)S(1)}, f32[40,128]{1,0:T(8,128)S(1)}, u32[]{:S(2)}, u32[]{:S(2)}) collective-permute-start(f32[40,128]{1,0:T(8,128)S(1)} %pack_more.1.own_ref), channel_id=1, source_target_pairs={{3,0},{2,1},{1,2},{0,3},{7,4},{6,5},{5,6},{4,7},{11,8},{10,9},{9,1... | collective-permute-start | bytes 61448 | tf_op jit(solution)/shard_map/ppermute | solution.py:33
  6.9 0.5 collective-permute-start
  7.5 3.2 %collective-permute-done.y_pair_ref = f32[40,128]{1,0:T(8,128)S(1)} collective-permute-done((f32[40,128]{1,0:T(8,128)S(1)}, f32[40,128]{1,0:T(8,128)S(1)}, u32[]{:S(2)}, u32[]{:S(2)}) %collective-permute-start) | collective-permute-done | bytes 20512 | tf_op jit(solution)/shard_map/ppermute | solution.py:24
  10.7 1.8 %collective-permute-start.4 = (f32[5,8,128]{2,1,0:T(8,128)S(1)}, f32[5,8,128]{2,1,0:T(8,128)S(1)}, u32[]{:S(2)}, u32[]{:S(2)}) collective-permute-start(f32[5,8,128]{2,1,0:T(8,128)S(1)} %constant_dynamic-update-slice_fusion.column_ref.cell_ref), channel_id=1, source_target_pairs={{28,0},{8,4},{4,8},{16,12},{12,16},{24,20},{20,24},{0,28},{29,1},{... | collective-permute-start | bytes 61448 | tf_op jit(solution)/shard_map/ppermute | solution.py:33
  12.6 0.3 prep_second.1
  12.9 0.3 prep_first.1
  13.2 2.6 %collective-permute-done.4.beyond_ref = f32[5,8,128]{2,1,0:T(8,128)S(1)} collective-permute-done((f32[5,8,128]{2,1,0:T(8,128)S(1)}, f32[5,8,128]{2,1,0:T(8,128)S(1)}, u32[]{:S(2)}, u32[]{:S(2)}) %collective-permute-start.4) | collective-permute-done | bytes 20512 | tf_op jit(solution)/shard_map/ppermute | solution.py:33
  15.8 2.9 %first.1 = (bf16[3,128,256]{2,1,0:T(8,128)(2,1)S(1)}, s32[3,3072]{1,0:T(4,128)S(1)}, f32[3,8,3072]{2,1,0:T(8,128)S(1)}, f32[3,8,3072]{2,1,0:T(8,128)S(1)}, f32[3...) custom-call(s32[2,8,128]{2,1,0:T(8,128)S(1)} %broadcast_in_dim.4.place_ref, ...), custom_call_target="tpu_custom_call" | custom-call | flops 10000000 | bytes 1000000 | tf_op jit(solution)/shard_map/first/pallas_call | solution.py:55
  18.7 0.1 collective-permute-start.5
  18.8 1.9 %collective-permute-start.6 = (bf16[3,128,256]{2,1,0:T(8,128)(2,1)S(1)}, bf16[3,128,256]{2,1,0:T(8,128)(2,1)S(1)}, u32[]{:S(2)}, u32[]{:S(2)}) collective-permute-start(bf16[3,128,256]{2,1,0:T(8,128)(2,1)S(1)} %get-tuple-element.97.column_ref), channel_id=1, source_target_pairs={{28,0},{8,4},{4,8},{16,12},{12,16},{24,20},{20,24},{0,28},{29,1},{... | collective-permute-start | bytes 589832 | tf_op jit(solution)/shard_map/ppermute | solution.py:33
  20.7 1.7 %second_near.1 = (f32[4,128,3072]{2,1,0:T(8,128)S(1)}, f32[128,3072]{1,0:T(8,128)S(1)}) custom-call(s32[3,3072]{1,0:T(4,128)S(1)} %get-tuple-element.85.ids_ref, f32[3,8,3072]{2,1,0:T(8,128)S(1)} %get-tuple-element.86.basis_ref, f32[3,8,3072]{2,1,0:T(8,128)S(1)} %get-tuple-element.88.unit_ref, bf16[2,128,32]{2,1,0:T(8,128)(2,1)S(1)} %get-tuple-element.96.left_ref, ...), custom_call_target="tpu_custom_call" | custom-call | flops 2000000000 | bytes 1000000 | tf_op jit(solution)/shard_map/second_near/pallas_call | solution.py:55
  22.4 1.0 %hot_beyond.1.hot_ref = bf16[768,3072]{1,0:T(8,128)(2,1)S(1)} custom-call(s32[3,3072]{1,0:T(4,128)S(1)} %get-tuple-element.85.ids_ref, f32[128,3072]{1,0:T(8,128)S(1)} %get-tuple-element.98.near_ref), custom_call_target="tpu_custom_call" | custom-call | flops 1000000 | bytes 1000000 | tf_op jit(solution)/shard_map/hot_beyond/pallas_call | solution.py:55
  23.4 0.8 second_side.1.near_ref
  24.2 2.7 %collective-permute-done.6.beyond_ref = bf16[3,128,256]{2,1,0:T(8,128)(2,1)S(1)} collective-permute-done((bf16[3,128,256]{2,1,0:T(8,128)(2,1)S(1)}, bf16[3,128,256]{2,1,0:T(8,128)(2,1)S(1)}, u32[]{:S(2)}, u32[]{:S(2)}) %collective-permute-start.6) | collective-permute-done | bytes 196640 | tf_op jit(solution)/shard_map/ppermute | solution.py:33
  26.9 1.8 %second.1 = (bf16[128,3072]{1,0:T(8,128)(2,1)S(1)}, f32[3,128,256]{2,1,0:T(8,128)S(1)}, f32[128,256]{1,0:T(8,128)S(1)}, bf16[80,256]{1,0:T(8,128)(2,1)S(1)}, f32...) custom-call(bf16[768,3072]{1,0:T(8,128)(2,1)S(1)} %hot_beyond.1.hot_ref, f32[4,128,3072]{2,1,0:T(8,128)S(1)} %get-tuple-element.99.weight_ref, ...), custom_call_target="tpu_custom_call" | custom-call | flops 10000000 | bytes 1000000 | tf_op jit(solution)/shard_map/second/pallas_call | solution.py:55
  28.7 0.1 collective-permute-start.9
  28.8 0.1 collective-permute-start.8
  28.9 4.3 %collective-permute-start.7 = (bf16[80,256]{1,0:T(8,128)(2,1)S(1)}, bf16[80,256]{1,0:T(8,128)(2,1)S(1)}, u32[]{:S(2)}, u32[]{:S(2)}) collective-permute-start(bf16[80,256]{1,0:T(8,128)(2,1)S(1)} %get-tuple-element.102), channel_id=1, source_target_pairs={{8,0},{12,4},{0,8},{4,12},{24,16},{28,20},{16,24},{20,28},{9,1},{1... | collective-permute-start | bytes 122888 | tf_op jit(solution)/shard_map/ppermute | solution.py:24
  33.2 0.8 green.1.refs_0_
  34.0 0.9 %collective-permute-done.9 = bf16[80,256]{1,0:T(8,128)(2,1)S(1)} collective-permute-done((bf16[80,256]{1,0:T(8,128)(2,1)S(1)}, bf16[80,256]{1,0:T(8,128)(2,1)S(1)}, u32[]{:S(2)}, u32[]{:S(2)}) %collective-permute-start.9) | collective-permute-done | bytes 40992 | tf_op jit(solution)/shard_map/ppermute | solution.py:24
  34.9 0.3 collective-permute-done.7
  35.3 0.1 collective-permute-start.10
  35.4 1.2 %structure_near.1 = (f32[32,1024]{1,0:T(8,128)S(1)}, f32[32,1024]{1,0:T(8,128)S(1)}, f32[8,1024]{1,0:T(8,128)S(1)}, f32[8,1024]{1,0:T(8,128)S(1)}, bf16[640,1024...) custom-call(s32[2,8,128]{2,1,0:T(8,128)S(1)} %broadcast_in_dim.4.place_ref, ...), custom_call_target="tpu_custom_call" | custom-call | flops 1000000000 | bytes 1000000 | tf_op jit(solution)/shard_map/structure_near/pallas_call | solution.py:55
  36.6 0.2 collective-permute-done.10.blocks.refs_11_
  36.8 1.3 %structure_far.1 = (f32[32,1024]{1,0:T(8,128)S(1)}, f32[32,1024]{1,0:T(8,128)S(1)}, f32[8,1024]{1,0:T(8,128)S(1)}, f32[8,1024]{1,0:T(8,128)S(1)}, bf16[640,1024]...) custom-call(s32[2,8,128]{2,1,0:T(8,128)S(1)} %broadcast_in_dim.4.place_r, ...), custom_call_target="tpu_custom_call" | custom-call | flops 10000000 | bytes 1000000 | tf_op jit(solution)/shard_map/structure_far/pallas_call | solution.py:55
  38.0 1.4 %collective-permute-start.13 = (bf16[320,128]{1,0:T(8,128)(2,1)S(1)}, bf16[320,128]{1,0:T(8,128)(2,1)S(1)}, u32[]{:S(2)}, u32[]{:S(2)}) collective-permute-start(bf16[320,128]{1,0:T(8,128)(2,1)S(1)} %get-tuple-element.106), channel_id=1, source_target_pairs={{3,0},{2,1},{1,2},{0,3},{7,4},{6,5},{5,6},{4,7},{11,8},{10,9},{9,1... | collective-permute-start | bytes 245768 | tf_op jit(solution)/shard_map/ppermute | solution.py:24
  39.4 0.9 %collective-permute-start.12 = (bf16[320,128]{1,0:T(8,128)(2,1)S(1)}, bf16[320,128]{1,0:T(8,128)(2,1)S(1)}, u32[]{:S(2)}, u32[]{:S(2)}) collective-permute-start(bf16[320,128]{1,0:T(8,128)(2,1)S(1)} %get-tuple-element.106), channel_id=1, source_target_pairs={{2,0},{3,1},{0,2},{1,3},{6,4},{7,5},{4,6},{5,7},{10,8},{11,9},{8,1... | collective-permute-start | bytes 245768 | tf_op jit(solution)/shard_map/ppermute | solution.py:24
  40.4 1.2 %collective-permute-start.11 = (bf16[320,128]{1,0:T(8,128)(2,1)S(1)}, bf16[320,128]{1,0:T(8,128)(2,1)S(1)}, u32[]{:S(2)}, u32[]{:S(2)}) collective-permute-start(bf16[320,128]{1,0:T(8,128)(2,1)S(1)} %get-tuple-element.106), channel_id=1, source_target_pairs={{1,0},{0,1},{3,2},{2,3},{5,4},{4,5},{7,6},{6,7},{9,8},{8,9},{11,10... | collective-permute-start | bytes 245768 | tf_op jit(solution)/shard_map/ppermute | solution.py:24
  41.6 3.0 %hot_back.1.hot_ref = bf16[3072,2304]{1,0:T(8,128)(2,1)S(1)} custom-call(s32[3,3072]{1,0:T(4,128)S(1)} %get-tuple-element.85.ids_ref), custom_call_target="tpu_custom_call" | custom-call | flops 2000000000 | bytes 1000000 | tf_op jit(solution)/shard_map/hot_back/pallas_call | solution.py:55
  44.6 0.8 collective-permute-done.12.refs_3_
  45.5 1.3 %fold_far.1 = (bf16[4,80,256]{2,1,0:T(8,128)(2,1)S(1)}, f32[640,64]{1,0:T(8,128)S(1)}) custom-call(s32[2,8,128]{2,1,0:T(8,128)S(1)} %broadcast_in_dim.4.place_ref, f32[320,128]{1,0:T(8,128)S(1)} %green.1.refs_0_, f32[320,128]{1,0:T(8,128)S(1)} %get-tuple-element.120.refs_1_, bf16[320,128]{1,0:T(8,128)(2,1)S(1)} %collective-permute-done.11.refs_2_, ...), custom_call_target="tpu_custom_call" | custom-call | flops 10000000 | bytes 1000000 | tf_op jit(solution)/shard_map/fold_far/pallas_call | solution.py:55
  46.8 0.1 collective-permute-start.14
  46.9 1.2 %fold_near.1.near_ref = f32[4,80,256]{2,1,0:T(8,128)S(1)} custom-call(s32[2,8,128]{2,1,0:T(8,128)S(1)} %broadcast_in_dim.4.place_ref, f32[640,64]{1,0:T(8,128)S(1)} %get-tuple-element.130.refs_0_, f32[32,1024]{1,0:T(8,128)S(1)} %get-tuple-element.131.refs_1_, f32[32,1024]{1,0:T(8,128)S(1)} %get-tuple-element.132.refs_2_, ...), custom_call_target="tpu_custom_call" | custom-call | flops 1000000000 | bytes 1000000 | tf_op jit(solution)/shard_map/fold_near/pallas_call | solution.py:55
  48.1 0.2 collective-permute-done.14.far_ref
  48.3 0.1 fold_join.1
  48.3 2.0 %collective-permute-start.15 = (bf16[80,256]{1,0:T(8,128)(2,1)S(1)}, bf16[80,256]{1,0:T(8,128)(2,1)S(1)}, u32[]{:S(2)}, u32[]{:S(2)}) collective-permute-start(bf16[80,256]{1,0:T(8,128)(2,1)S(1)} %get-tuple-element.139), channel_id=1, source_target_pairs={{8,0},{12,4},{0,8},{4,12},{24,16},{28,20},{16,24},{20,28},{9,1},{1... | collective-permute-start | bytes 122888 | tf_op jit(solution)/shard_map/ppermute | solution.py:24
  50.3 0.9 %collective-permute-start.16 = (bf16[80,256]{1,0:T(8,128)(2,1)S(1)}, bf16[80,256]{1,0:T(8,128)(2,1)S(1)}, u32[]{:S(2)}, u32[]{:S(2)}) collective-permute-start(bf16[80,256]{1,0:T(8,128)(2,1)S(1)} %get-tuple-element.140), channel_id=1, source_target_pairs={{16,0},{20,4},{24,8},{28,12},{0,16},{4,20},{8,24},{12,28},{17,1},{... | collective-permute-start | bytes 122888 | tf_op jit(solution)/shard_map/ppermute | solution.py:24
  51.2 1.5 %collective-permute-start.17 = (bf16[80,256]{1,0:T(8,128)(2,1)S(1)}, bf16[80,256]{1,0:T(8,128)(2,1)S(1)}, u32[]{:S(2)}, u32[]{:S(2)}) collective-permute-start(bf16[80,256]{1,0:T(8,128)(2,1)S(1)} %get-tuple-element.141), channel_id=1, source_target_pairs={{24,0},{28,4},{16,8},{20,12},{8,16},{12,20},{0,24},{4,28},{25,1},{... | collective-permute-start | bytes 122888 | tf_op jit(solution)/shard_map/ppermute | solution.py:24
  52.8 0.5 readout.1
  53.3 2.8 %collective-permute-done.16.refs_2_ = bf16[80,256]{1,0:T(8,128)(2,1)S(1)} collective-permute-done((bf16[80,256]{1,0:T(8,128)(2,1)S(1)}, bf16[80,256]{1,0:T(8,128)(2,1)S(1)}, u32[]{:S(2)}, u32[]{:S(2)}) %collective-permute-start.16) | collective-permute-done | bytes 40992 | tf_op jit(solution)/shard_map/ppermute | solution.py:24
  56.1 1.0 %collective-permute-done.17.refs_3_ = bf16[80,256]{1,0:T(8,128)(2,1)S(1)} collective-permute-done((bf16[80,256]{1,0:T(8,128)(2,1)S(1)}, bf16[80,256]{1,0:T(8,128)(2,1)S(1)}, u32[]{:S(2)}, u32[]{:S(2)}) %collective-permute-start.17) | collective-permute-done | bytes 40992 | tf_op jit(solution)/shard_map/ppermute | solution.py:24
  57.2 3.0 %second_back.1 = (f32[1,1,256]{2,1,0:T(1,128)}, f32[8,256]{1,0:T(8,128)S(1)}, f32[128,256]{1,0:T(8,128)S(1)}, f32[4,128,256]{2,1,0:T(8,128)S(1)}, bf16[128,3072]...) custom-call(bf16[3072,2304]{1,0:T(8,128)(2,1)S(1)} %hot_back.1.hot_ref, ...), custom_call_target="tpu_custom_call" | custom-call | flops 10000000 | bytes 1000000 | tf_op jit(solution)/shard_map/second_back/pallas_call | solution.py:55
  60.2 1.7 %collective-permute-start.19 = (bf16[3,128,256]{2,1,0:T(8,128)(2,1)S(1)}, bf16[3,128,256]{2,1,0:T(8,128)(2,1)S(1)}, u32[]{:S(2)}, u32[]{:S(2)}) collective-permute-start(bf16[3,128,256]{2,1,0:T(8,128)(2,1)S(1)} %get-tuple-element.147), channel_id=1, source_target_pairs={{28,0},{8,4},{4,8},{16,12},{12,16},{24,20},{20,24},{0,28},{29,1},{... | collective-permute-start | bytes 589832 | tf_op jit(solution)/shard_map/ppermute | solution.py:33
  61.9 0.8 second_middle.1.middle_ref
  62.7 1.2 %second_edge.1.edge_ref = f32[32,3072]{1,0:T(8,128)S(1)} custom-call(bf16[2,16,256]{2,1,0:T(8,128)(2,1)S(1)} %get-tuple-element.95.back_ref, bf16[128,3072]{1,0:T(8,128)(2,1)S(1)} %get-tuple-element.101.feature_ref, f32[4,128,256]{2,1,0:T(8,128)S(1)} %get-tuple-element.142.grad_ref), custom_call_target="tpu_custom_call" | custom-call | flops 1000000000 | bytes 1000000 | tf_op jit(solution)/shard_map/second_edge/pallas_call | solution.py:55
  63.9 4.4 %collective-permute-done.19.from_beyond = bf16[3,128,256]{2,1,0:T(8,128)(2,1)S(1)} collective-permute-done((bf16[3,128,256]{2,1,0:T(8,128)(2,1)S(1)}, bf16[3,128,256]{2,1,0:T(8,128)(2,1)S(1)}, u32[]{:S(2)}, u32[]{:S(2)}) %collective-permute-start.19) | collective-permute-done | bytes 196640 | tf_op jit(solution)/shard_map/ppermute | solution.py:33
  68.2 3.6 %first_back.1 = (f32[5,8,256]{2,1,0:T(8,128)S(1)}, f32[5,8,256]{2,1,0:T(8,128)S(1)}, f32[5,8,256]{2,1,0:T(8,128)S(1)}) custom-call(s32[3,3072]{1,0:T(4,128)S(1)} %get-tuple-element.85.ids_ref, f32[3,8,3072]{2,1,0:T(8,128)S(1)} %get-tuple-element.86.basis_ref, f32[3,8,3072]{2,1,0:T(8,128)S(1)} %get-tuple-element.87.slope_ref, ...), custom_call_target="tpu_custom_call" | custom-call | flops 10000000 | bytes 1000000 | tf_op jit(solution)/shard_map/first_back/pallas_call | solution.py:55
  71.8 0.1 collective-permute-start.20
  71.9 1.1 %collective-permute-start.21 = (f32[5,8,256]{2,1,0:T(8,128)S(1)}, f32[5,8,256]{2,1,0:T(8,128)S(1)}, u32[]{:S(2)}, u32[]{:S(2)}) collective-permute-start(f32[5,8,256]{2,1,0:T(8,128)S(1)} %get-tuple-element.150), channel_id=1, source_target_pairs={{28,0},{8,4},{4,8},{16,12},{12,16},{24,20},{20,24},{0,28},{29,1},{... | collective-permute-start | bytes 122888 | tf_op jit(solution)/shard_map/ppermute | solution.py:33
  72.9 0.1 collective-permute-done.20
  73.1 4.1 %collective-permute-done.21 = f32[5,8,256]{2,1,0:T(8,128)S(1)} collective-permute-done((f32[5,8,256]{2,1,0:T(8,128)S(1)}, f32[5,8,256]{2,1,0:T(8,128)S(1)}, u32[]{:S(2)}, u32[]{:S(2)}) %collective-permute-start.21) | collective-permute-done | bytes 40992 | tf_op jit(solution)/shard_map/ppermute | solution.py:33
  77.2 1.1 %collective-permute-start.24 = (f32[8,256]{1,0:T(8,128)S(1)}, f32[8,256]{1,0:T(8,128)S(1)}, u32[]{:S(2)}, u32[]{:S(2)}) collective-permute-start(f32[8,256]{1,0:T(8,128)S(1)} %get-tuple-element.155), channel_id=1, source_target_pairs={{2,0},{3,1},{0,2},{1,3},{6,4},{7,5},{4,6},{5,7},{10,8},{11,9},{8,1... | collective-permute-start | bytes 24584 | tf_op jit(solution)/shard_map/ppermute | solution.py:42
  78.3 1.2 %collective-permute-start.23 = (f32[8,256]{1,0:T(8,128)S(1)}, f32[8,256]{1,0:T(8,128)S(1)}, u32[]{:S(2)}, u32[]{:S(2)}) collective-permute-start(f32[8,256]{1,0:T(8,128)S(1)} %get-tuple-element.156), channel_id=1, source_target_pairs={{3,0},{2,1},{1,2},{0,3},{7,4},{6,5},{5,6},{4,7},{11,8},{10,9},{9,1... | collective-permute-start | bytes 24584 | tf_op jit(solution)/shard_map/ppermute | solution.py:33
  79.5 1.3 %collective-permute-start.22 = (f32[8,256]{1,0:T(8,128)S(1)}, f32[8,256]{1,0:T(8,128)S(1)}, u32[]{:S(2)}, u32[]{:S(2)}) collective-permute-start(f32[8,256]{1,0:T(8,128)S(1)} %get-tuple-element.157), channel_id=1, source_target_pairs={{1,0},{0,1},{3,2},{2,3},{5,4},{4,5},{7,6},{6,7},{9,8},{8,9},{11,10... | collective-permute-start | bytes 24584 | tf_op jit(solution)/shard_map/ppermute | solution.py:24
  80.8 0.2 collective-permute-done.24
  80.9 1.9 %collective-permute-done.23 = f32[8,256]{1,0:T(8,128)S(1)} collective-permute-done((f32[8,256]{1,0:T(8,128)S(1)}, f32[8,256]{1,0:T(8,128)S(1)}, u32[]{:S(2)}, u32[]{:S(2)}) %collective-permute-start.23) | collective-permute-done | bytes 8224 | tf_op jit(solution)/shard_map/ppermute | solution.py:33
  82.9 0.3 collective-permute-done.22
  83.1 0.6 copy.13
  (41 shorter events, 0.2 us)
Async XLA Ops:
  0.8 0.7 copy-start.9
  1.5 0.7 copy-start.10
  2.1 3.1 %copy-start.5 = (s32[1,1,256,12]{2,1,3,0:T(1,128)S(1)}, s32[1,1,256,12]{2,1,3,0:T(1,128)}, u32[]{:S(2)}) copy-start(s32[1,1,256,12]{2,1,3,0:T(1,128)} %param.13) | copy-start | bytes 36868
  2.2 3.1 %copy-start.7 = (s32[1,1,256]{2,1,0:T(1,128)S(1)}, s32[1,1,256]{2,1,0:T(1,128)}, u32[]{:S(2)}) copy-start(s32[1,1,256]{2,1,0:T(1,128)} %count_ref.1) | copy-start | bytes 3076
  2.2 10.4 %copy-start.1 = (f32[128,128]{1,0:T(8,128)S(1)}, f32[128,128]{1,0:T(8,128)}, u32[]{:S(2)}) copy-start(f32[128,128]{1,0:T(8,128)} %hidden_in.1) | copy-start | bytes 196612
  2.2 10.4 %copy-start.3 = (f32[128,64]{0,1:T(8,128)S(1)}, f32[128,64]{0,1:T(8,128)}, u32[]{:S(2)}) copy-start(f32[128,64]{0,1:T(8,128)} %param.20) | copy-start | bytes 98308
  2.2 10.4 %copy-start.8 = (f32[128]{0:T(128)S(1)}, f32[128]{0:T(128)}, u32[]{:S(2)}) copy-start(f32[128]{0:T(128)} %param.19) | copy-start | bytes 1540
  2.2 10.7 %copy-start = (f32[2,2,128,128]{3,2,1,0:T(8,128)S(1)}, f32[2,2,128,128]{3,2,1,0:T(8,128)}, u32[]{:S(2)}) copy-start(f32[2,2,128,128]{3,2,1,0:T(8,128)} %mixing_in.1) | copy-start | bytes 786436
  2.2 10.7 %copy-start.4 = (f32[2,2,8,128]{3,2,1,0:T(8,128)S(1)}, f32[2,2,8,128]{3,2,1,0:T(8,128)}, u32[]{:S(2)}) copy-start(f32[2,2,8,128]{3,2,1,0:T(8,128)} %radial_in.1) | copy-start | bytes 49156
  2.2 10.7 %copy-start.6 = (f32[6,128]{1,0:T(8,128)S(1)}, f32[6,128]{1,0:T(8,128)}, u32[]{:S(2)}) copy-start(f32[6,128]{1,0:T(8,128)} %embed_in.1) | copy-start | bytes 9220
  2.2 5.3 %collective-permute-start.2 = (f32[8,128]{1,0:T(8,128)S(1)}, f32[8,128]{1,0:T(8,128)S(1)}, u32[]{:S(2)}, u32[]{:S(2)}) collective-permute-start(f32[8,128]{1,0:T(8,128)S(1)} %pack.1.first_ref), channel_id=1, source_target_pairs={{2,0},{3,1},{0,2},{1,3},{6,4},{7,5},{4,6},{5,7},{10,8},{11,9},{8,1... | collective-permute-start | bytes 12296 | tf_op jit(solution)/shard_map/ppermute | solution.py:42
  5.4 5.3 %collective-permute-start.1 = (f32[40,128]{1,0:T(8,128)S(1)}, f32[40,128]{1,0:T(8,128)S(1)}, u32[]{:S(2)}, u32[]{:S(2)}) collective-permute-start(f32[40,128]{1,0:T(8,128)S(1)} %pack_more.1.own_ref), channel_id=1, source_target_pairs={{3,0},{2,1},{1,2},{0,3},{7,4},{6,5},{5,6},{4,7},{11,8},{10,9},{9,1... | collective-permute-start | bytes 61448 | tf_op jit(solution)/shard_map/ppermute | solution.py:33
  6.9 3.8 %collective-permute-start = (f32[40,128]{1,0:T(8,128)S(1)}, f32[40,128]{1,0:T(8,128)S(1)}, u32[]{:S(2)}, u32[]{:S(2)}) collective-permute-start(f32[40,128]{1,0:T(8,128)S(1)} %pack_more.1.own_ref), channel_id=1, source_target_pairs={{1,0},{0,1},{3,2},{2,3},{5,4},{4,5},{7,6},{6,7},{9,8},{8,9},{11,10... | collective-permute-start | bytes 61448 | tf_op jit(solution)/shard_map/ppermute | solution.py:24
  10.7 5.1 %collective-permute-start.4 = (f32[5,8,128]{2,1,0:T(8,128)S(1)}, f32[5,8,128]{2,1,0:T(8,128)S(1)}, u32[]{:S(2)}, u32[]{:S(2)}) collective-permute-start(f32[5,8,128]{2,1,0:T(8,128)S(1)} %constant_dynamic-update-slice_fusion.column_ref.cell_ref), channel_id=1, source_target_pairs={{28,0},{8,4},{4,8},{16,12},{12,16},{24,20},{20,24},{0,28},{29,1},{... | collective-permute-start | bytes 61448 | tf_op jit(solution)/shard_map/ppermute | solution.py:33
  12.6 3.3 %collective-permute-start.3 = (f32[5,8,128]{2,1,0:T(8,128)S(1)}, f32[5,8,128]{2,1,0:T(8,128)S(1)}, u32[]{:S(2)}, u32[]{:S(2)}) collective-permute-start(f32[5,8,128]{2,1,0:T(8,128)S(1)} %constant_dynamic-update-slice_fusion.column_ref.cell_ref), channel_id=1, source_target_pairs={{4,0},{0,4},{12,8},{8,12},{20,16},{16,20},{28,24},{24,28},{5,1},{1... | collective-permute-start | bytes 61448 | tf_op jit(solution)/shard_map/ppermute | solution.py:24
  18.7 4.7 %collective-permute-start.5 = (bf16[3,128,256]{2,1,0:T(8,128)(2,1)S(1)}, bf16[3,128,256]{2,1,0:T(8,128)(2,1)S(1)}, u32[]{:S(2)}, u32[]{:S(2)}) collective-permute-start(bf16[3,128,256]{2,1,0:T(8,128)(2,1)S(1)} %get-tuple-element.97.column_ref), channel_id=1, source_target_pairs={{4,0},{0,4},{12,8},{8,12},{20,16},{16,20},{28,24},{24,28},{5,1},{1... | collective-permute-start | bytes 589832 | tf_op jit(solution)/shard_map/ppermute | solution.py:24
  18.8 8.1 %collective-permute-start.6 = (bf16[3,128,256]{2,1,0:T(8,128)(2,1)S(1)}, bf16[3,128,256]{2,1,0:T(8,128)(2,1)S(1)}, u32[]{:S(2)}, u32[]{:S(2)}) collective-permute-start(bf16[3,128,256]{2,1,0:T(8,128)(2,1)S(1)} %get-tuple-element.97.column_ref), channel_id=1, source_target_pairs={{28,0},{8,4},{4,8},{16,12},{12,16},{24,20},{20,24},{0,28},{29,1},{... | collective-permute-start | bytes 589832 | tf_op jit(solution)/shard_map/ppermute | solution.py:33
  26.9 6.3 %copy-start.2 = (s32[3,4096]{1,0:T(4,128)S(1)}, s32[3,4096]{1,0:T(4,128)}, u32[]{:S(2)}) copy-start(s32[3,4096]{1,0:T(4,128)} %vec_ref.1) | copy-start | bytes 147460
  28.7 6.2 %collective-permute-start.9 = (bf16[80,256]{1,0:T(8,128)(2,1)S(1)}, bf16[80,256]{1,0:T(8,128)(2,1)S(1)}, u32[]{:S(2)}, u32[]{:S(2)}) collective-permute-start(bf16[80,256]{1,0:T(8,128)(2,1)S(1)} %get-tuple-element.102), channel_id=1, source_target_pairs={{24,0},{28,4},{16,8},{20,12},{8,16},{12,20},{0,24},{4,28},{25,1},{... | collective-permute-start | bytes 122888 | tf_op jit(solution)/shard_map/ppermute | solution.py:24
  28.8 6.1 %collective-permute-start.8 = (bf16[80,256]{1,0:T(8,128)(2,1)S(1)}, bf16[80,256]{1,0:T(8,128)(2,1)S(1)}, u32[]{:S(2)}, u32[]{:S(2)}) collective-permute-start(bf16[80,256]{1,0:T(8,128)(2,1)S(1)} %get-tuple-element.102), channel_id=1, source_target_pairs={{16,0},{20,4},{24,8},{28,12},{0,16},{4,20},{8,24},{12,28},{17,1},{... | collective-permute-start | bytes 122888 | tf_op jit(solution)/shard_map/ppermute | solution.py:24
  28.9 6.4 %collective-permute-start.7 = (bf16[80,256]{1,0:T(8,128)(2,1)S(1)}, bf16[80,256]{1,0:T(8,128)(2,1)S(1)}, u32[]{:S(2)}, u32[]{:S(2)}) collective-permute-start(bf16[80,256]{1,0:T(8,128)(2,1)S(1)} %get-tuple-element.102), channel_id=1, source_target_pairs={{8,0},{12,4},{0,8},{4,12},{24,16},{28,20},{16,24},{20,28},{9,1},{1... | collective-permute-start | bytes 122888 | tf_op jit(solution)/shard_map/ppermute | solution.py:24
  35.3 1.5 %collective-permute-start.10 = (bf16[4,80,256]{2,1,0:T(8,128)(2,1)S(1)}, bf16[4,80,256]{2,1,0:T(8,128)(2,1)S(1)}, u32[]{:S(2)}, u32[]{:S(2)}) collective-permute-start(bf16[4,80,256]{2,1,0:T(8,128)(2,1)S(1)} %pad_maximum_fusion.blocks.refs_7_), channel_id=1, source_target_pairs={{4,0},{0,4},{12,8},{8,12},{20,16},{16,20},{28,24},{24,28},{5,1},{1... | collective-permute-start | bytes 491528 | tf_op jit(solution)/shard_map/ppermute | solution.py:24
  38.0 6.6 %collective-permute-start.13 = (bf16[320,128]{1,0:T(8,128)(2,1)S(1)}, bf16[320,128]{1,0:T(8,128)(2,1)S(1)}, u32[]{:S(2)}, u32[]{:S(2)}) collective-permute-start(bf16[320,128]{1,0:T(8,128)(2,1)S(1)} %get-tuple-element.106), channel_id=1, source_target_pairs={{3,0},{2,1},{1,2},{0,3},{7,4},{6,5},{5,6},{4,7},{11,8},{10,9},{9,1... | collective-permute-start | bytes 245768 | tf_op jit(solution)/shard_map/ppermute | solution.py:24
  39.4 6.0 %collective-permute-start.12 = (bf16[320,128]{1,0:T(8,128)(2,1)S(1)}, bf16[320,128]{1,0:T(8,128)(2,1)S(1)}, u32[]{:S(2)}, u32[]{:S(2)}) collective-permute-start(bf16[320,128]{1,0:T(8,128)(2,1)S(1)} %get-tuple-element.106), channel_id=1, source_target_pairs={{2,0},{3,1},{0,2},{1,3},{6,4},{7,5},{4,6},{5,7},{10,8},{11,9},{8,1... | collective-permute-start | bytes 245768 | tf_op jit(solution)/shard_map/ppermute | solution.py:24
  40.4 5.1 %collective-permute-start.11 = (bf16[320,128]{1,0:T(8,128)(2,1)S(1)}, bf16[320,128]{1,0:T(8,128)(2,1)S(1)}, u32[]{:S(2)}, u32[]{:S(2)}) collective-permute-start(bf16[320,128]{1,0:T(8,128)(2,1)S(1)} %get-tuple-element.106), channel_id=1, source_target_pairs={{1,0},{0,1},{3,2},{2,3},{5,4},{4,5},{7,6},{6,7},{9,8},{8,9},{11,10... | collective-permute-start | bytes 245768 | tf_op jit(solution)/shard_map/ppermute | solution.py:24
  46.8 1.5 %collective-permute-start.14 = (bf16[4,80,256]{2,1,0:T(8,128)(2,1)S(1)}, bf16[4,80,256]{2,1,0:T(8,128)(2,1)S(1)}, u32[]{:S(2)}, u32[]{:S(2)}) collective-permute-start(bf16[4,80,256]{2,1,0:T(8,128)(2,1)S(1)} %get-tuple-element.137), channel_id=1, source_target_pairs={{4,0},{0,4},{12,8},{8,12},{20,16},{16,20},{28,24},{24,28},{5,1},{1... | collective-permute-start | bytes 491528 | tf_op jit(solution)/shard_map/ppermute | solution.py:24
  48.3 5.0 %collective-permute-start.15 = (bf16[80,256]{1,0:T(8,128)(2,1)S(1)}, bf16[80,256]{1,0:T(8,128)(2,1)S(1)}, u32[]{:S(2)}, u32[]{:S(2)}) collective-permute-start(bf16[80,256]{1,0:T(8,128)(2,1)S(1)} %get-tuple-element.139), channel_id=1, source_target_pairs={{8,0},{12,4},{0,8},{4,12},{24,16},{28,20},{16,24},{20,28},{9,1},{1... | collective-permute-start | bytes 122888 | tf_op jit(solution)/shard_map/ppermute | solution.py:24
  50.3 5.8 %collective-permute-start.16 = (bf16[80,256]{1,0:T(8,128)(2,1)S(1)}, bf16[80,256]{1,0:T(8,128)(2,1)S(1)}, u32[]{:S(2)}, u32[]{:S(2)}) collective-permute-start(bf16[80,256]{1,0:T(8,128)(2,1)S(1)} %get-tuple-element.140), channel_id=1, source_target_pairs={{16,0},{20,4},{24,8},{28,12},{0,16},{4,20},{8,24},{12,28},{17,1},{... | collective-permute-start | bytes 122888 | tf_op jit(solution)/shard_map/ppermute | solution.py:24
  51.2 5.9 %collective-permute-start.17 = (bf16[80,256]{1,0:T(8,128)(2,1)S(1)}, bf16[80,256]{1,0:T(8,128)(2,1)S(1)}, u32[]{:S(2)}, u32[]{:S(2)}) collective-permute-start(bf16[80,256]{1,0:T(8,128)(2,1)S(1)} %get-tuple-element.141), channel_id=1, source_target_pairs={{24,0},{28,4},{16,8},{20,12},{8,16},{12,20},{0,24},{4,28},{25,1},{... | collective-permute-start | bytes 122888 | tf_op jit(solution)/shard_map/ppermute | solution.py:24
  60.2 3.7 %collective-permute-start.18 = (bf16[3,128,256]{2,1,0:T(8,128)(2,1)S(1)}, bf16[3,128,256]{2,1,0:T(8,128)(2,1)S(1)}, u32[]{:S(2)}, u32[]{:S(2)}) collective-permute-start(bf16[3,128,256]{2,1,0:T(8,128)(2,1)S(1)} %get-tuple-element.146), channel_id=1, source_target_pairs={{4,0},{0,4},{12,8},{8,12},{20,16},{16,20},{28,24},{24,28},{5,1},{1... | collective-permute-start | bytes 589832 | tf_op jit(solution)/shard_map/ppermute | solution.py:24
  60.2 8.0 %collective-permute-start.19 = (bf16[3,128,256]{2,1,0:T(8,128)(2,1)S(1)}, bf16[3,128,256]{2,1,0:T(8,128)(2,1)S(1)}, u32[]{:S(2)}, u32[]{:S(2)}) collective-permute-start(bf16[3,128,256]{2,1,0:T(8,128)(2,1)S(1)} %get-tuple-element.147), channel_id=1, source_target_pairs={{28,0},{8,4},{4,8},{16,12},{12,16},{24,20},{20,24},{0,28},{29,1},{... | collective-permute-start | bytes 589832 | tf_op jit(solution)/shard_map/ppermute | solution.py:33
  71.8 1.3 %collective-permute-start.20 = (f32[5,8,256]{2,1,0:T(8,128)S(1)}, f32[5,8,256]{2,1,0:T(8,128)S(1)}, u32[]{:S(2)}, u32[]{:S(2)}) collective-permute-start(f32[5,8,256]{2,1,0:T(8,128)S(1)} %get-tuple-element.149), channel_id=1, source_target_pairs={{4,0},{0,4},{12,8},{8,12},{20,16},{16,20},{28,24},{24,28},{5,1},{1... | collective-permute-start | bytes 122888 | tf_op jit(solution)/shard_map/ppermute | solution.py:24
  71.9 5.3 %collective-permute-start.21 = (f32[5,8,256]{2,1,0:T(8,128)S(1)}, f32[5,8,256]{2,1,0:T(8,128)S(1)}, u32[]{:S(2)}, u32[]{:S(2)}) collective-permute-start(f32[5,8,256]{2,1,0:T(8,128)S(1)} %get-tuple-element.150), channel_id=1, source_target_pairs={{28,0},{8,4},{4,8},{16,12},{12,16},{24,20},{20,24},{0,28},{29,1},{... | collective-permute-start | bytes 122888 | tf_op jit(solution)/shard_map/ppermute | solution.py:33
  77.2 3.7 %collective-permute-start.24 = (f32[8,256]{1,0:T(8,128)S(1)}, f32[8,256]{1,0:T(8,128)S(1)}, u32[]{:S(2)}, u32[]{:S(2)}) collective-permute-start(f32[8,256]{1,0:T(8,128)S(1)} %get-tuple-element.155), channel_id=1, source_target_pairs={{2,0},{3,1},{0,2},{1,3},{6,4},{7,5},{4,6},{5,7},{10,8},{11,9},{8,1... | collective-permute-start | bytes 24584 | tf_op jit(solution)/shard_map/ppermute | solution.py:42
  78.3 4.5 %collective-permute-start.23 = (f32[8,256]{1,0:T(8,128)S(1)}, f32[8,256]{1,0:T(8,128)S(1)}, u32[]{:S(2)}, u32[]{:S(2)}) collective-permute-start(f32[8,256]{1,0:T(8,128)S(1)} %get-tuple-element.156), channel_id=1, source_target_pairs={{3,0},{2,1},{1,2},{0,3},{7,4},{6,5},{5,6},{4,7},{11,8},{10,9},{9,1... | collective-permute-start | bytes 24584 | tf_op jit(solution)/shard_map/ppermute | solution.py:33
  79.5 3.7 %collective-permute-start.22 = (f32[8,256]{1,0:T(8,128)S(1)}, f32[8,256]{1,0:T(8,128)S(1)}, u32[]{:S(2)}, u32[]{:S(2)}) collective-permute-start(f32[8,256]{1,0:T(8,128)S(1)} %get-tuple-element.157), channel_id=1, source_target_pairs={{1,0},{0,1},{3,2},{2,3},{5,4},{4,5},{7,6},{6,7},{9,8},{8,9},{11,10... | collective-permute-start | bytes 24584 | tf_op jit(solution)/shard_map/ppermute | solution.py:24

commit v15 on v14

--- a/solution.py
+++ b/solution.py
@@ -265,6 +265,16 @@
         hot_ref[start : start + 128] = jnp.where(column == entry, 1.0, 0.0).astype(BF16)
 
 
+def lane_hot_kernel(ids_ref, hot_ref):
+    edges = ids_ref.shape[1]
+    lane = lax.broadcasted_iota(jnp.int32, (128, 128), 1).astype(F32)
+    for cell in range(3):
+        for start in range(0, edges, 128):
+            row = (ids_ref[cell : cell + 1, start : start + 128] & 127).astype(F32)
+            column = jnp.broadcast_to(row, (8, 128)).T[:, 0:1]
+            hot_ref[cell, start : start + 128] = jnp.where(column == lane, 1.0, 0.0).astype(BF16)
+
+
 def unfold_block(block, atoms):
     parts = atoms // 128
     rows = [block[r : r + 1] for r in range(4 * parts)]
@@ -284,6 +294,7 @@
     to_x = jnp.where((place_ref[0] & 1) == 0, to_x, -to_x)
     to_y = jnp.where(kind_of_row == 1, cell_width, 0.0)
     to_y = jnp.where((place_ref[1] & 1) == 0, to_y, -to_y)
+    cells = []
     for cell, block_ref in enumerate((y_pair_ref, own_ref, y_beyond_ref)):
         ids, count = block_ids(block_ref[...], atoms, slots * atoms)
         ids_ref[cell : cell + 1, :] = ids
@@ -294,16 +305,26 @@
             for b in range(3):
                 block = frame[a][SLOT_CELLS[cell][b]]
                 rows.append(block + ((1 - a) * to_x + (1 - b) * step_y))
+        cells.append((count, own, gathered_rows(ids, rows, places, upper)))
+    rel = []
+    for q in range(3):
+        found = jnp.concatenate([found[q] for _, _, found in cells], axis=0)
+        own = jnp.concatenate([own[q] for _, own, _ in cells], axis=0)
+        rel.append(found - jnp.concatenate([own] * slots, axis=1))
+    distance = jnp.sqrt(rel[0] * rel[0] + rel[1] * rel[1] + rel[2] * rel[2] + soften)
+    inverse = 1.0 / distance
+    units = [r * inverse for r in rel]
+    for cell, (count, own, found) in enumerate(cells):
+        one = slice(cell, cell + 1)
         first_cell(
-            slots, atoms, ids, count, rows, places, upper, own, embed_ref, kind_left, mix_high,
-            mix_low, low_ref.at[cell], basis_ref.at[cell], slope_ref.at[cell], unit_ref.at[cell],
-            sums_ref.at[cell], gate_ref.at[cell],
+            slots, atoms, count, [u[one] for u in units], distance[one], inverse[one], found[3],
+            own[3], embed_ref, kind_left, mix_high, mix_low, low_ref.at[cell], basis_ref.at[cell],
+            slope_ref.at[cell], unit_ref.at[cell], sums_ref.at[cell], gate_ref.at[cell],
         )
 
 
-def first_cell(slots, atoms, ids, count, rows, places, upper, own, embed_ref, kind_left, mix_high,
-               mix_low, low_ref, basis_ref, slope_ref, unit_ref, sums_ref, gate_ref):
-    per_cell = atoms // 128
+def gathered_rows(ids, rows, places, upper):
+    per_cell = places.shape[0] // 4
     pieces = []
     for start in range(0, ids.shape[1], 128):
         part = jnp.broadcast_to(ids[:, start : start + 128], places.shape)
@@ -318,9 +339,11 @@
         pieces.append(total)
     found = jnp.concatenate(pieces, axis=1)
     found = [found[q * per_cell : q * per_cell + 1] for q in range(4)]
-    rel = [found[q] - jnp.concatenate([own[q]] * slots, axis=1) for q in range(3)]
-    distance = jnp.sqrt(rel[0] * rel[0] + rel[1] * rel[1] + rel[2] * rel[2] + soften)
-    inverse = 1.0 / distance
+    return found
+
+
+def first_cell(slots, atoms, count, units, distance, inverse, kinds, own_kinds, embed_ref, kind_left,
+               mix_high, mix_low, low_ref, basis_ref, slope_ref, unit_ref, sums_ref, gate_ref):
     order = (lax.broadcasted_iota(jnp.int32, (8, 1), 0) + 1).astype(F32)
     sine, cosine = sin_cos((order * (0.5 / cut_radius)) * distance)
     wave = sine / ((order * (math.pi / cut_radius)) * distance)
@@ -328,9 +351,8 @@
     basis = wave * live
     basis_ref[...] = basis
     slope_ref[...] = (cosine - wave) * (inverse * live)
-    kinds = found[3]
     unit = jnp.concatenate(
-        [r * inverse for r in rel] + [inverse, kinds] + [jnp.zeros_like(kinds)] * 3, axis=0
+        units + [inverse, kinds] + [jnp.zeros_like(kinds)] * 3, axis=0
     )
     unit_ref[...] = unit
     stack = embed_ref[...]
@@ -351,7 +373,7 @@
     sums = [dot(kind_left[0], stacks[0])]
     sums += [vectors[:, i * atoms : (i + 1) * atoms] for i in range(3)]
     step, gate = mixed(sums, mix_high, mix_low, 0)
-    low_ref[...] = (embedded(stack, own[3]) + step).astype(BF16)
+    low_ref[...] = (embedded(stack, own_kinds) + step).astype(BF16)
     for part in range(3):
         sums_ref[part] = sums[part + 1]
     gate_ref[...] = gate
@@ -496,7 +518,7 @@
             )
 
 
-def first_back_kernel(slots, ids_ref, basis_ref, slope_ref, unit_ref, kind_high, kind_low, turn_high,
+def first_back_kernel(slots, ids_ref, lane_ref, basis_ref, slope_ref, unit_ref, kind_high, kind_low, turn_high,
                       turn_low, sums_ref, gate_ref, edge_ref, long_ref, middle_ref, from_pair,
                       from_beyond, *outs):
     sums = {(1, 2): long_ref[...]}
@@ -505,7 +527,7 @@
             from_pair[cell].astype(F32) + from_beyond[cell].astype(F32)
         )
         own, found = first_back_cell(
-            slots, ids_ref[cell : cell + 1, :], basis_ref.at[cell], slope_ref.at[cell],
+            slots, ids_ref[cell : cell + 1, :], lane_ref.at[cell], basis_ref.at[cell], slope_ref.at[cell],
             unit_ref.at[cell], kind_high, kind_low, turn_high, turn_low, sums_ref.at[cell],
             gate_ref.at[cell], edge_ref if cell == 1 else None, cotangent,
         )
@@ -517,7 +539,7 @@
         outs[x][y] = total
 
 
-def first_back_cell(slots, ids, basis_ref, slope_ref, unit_ref, kind_high, kind_low, turn_high,
+def first_back_cell(slots, ids, lane_ref, basis_ref, slope_ref, unit_ref, kind_high, kind_low, turn_high,
                     turn_low, sums_ref, gate_ref, edge_ref, cotangent):
     atoms = gate_ref.shape[1]
     pre = cotangent * gate_ref[...]
@@ -558,7 +580,6 @@
     own = -move[:, :atoms]
     for n in range(1, slots):
         own = own - move[:, n * atoms : (n + 1) * atoms]
-    lane_hot = hot_columns(ids & 127, 128)
     half = ids >> 7
     high = move.astype(BF16).astype(F32)
     both = jnp.concatenate([high, move - high], axis=0)
@@ -566,7 +587,7 @@
     rows = jnp.concatenate(
         [jnp.where(half == h, both, 0.0).astype(BF16) for h in range(9 * per_cell)], axis=0
     )
-    spread = dot(rows, lane_hot, ((1,), (1,)))
+    spread = dot(rows, lane_ref[...])
     grads = []
     for cell in range(9):
         found = []
@@ -1007,7 +1028,7 @@
         [near_folds, far_folds],
         name="fold_join",
     )
-    folds = [folds[0]] + [paired(folds[d], "gx", 2 * d) for d in range(1, half)]
+    folds = [folds[0]] + [paired(folds[d], "gx", 2 * d) for d in reversed(range(1, half))]
 
     site, long, cotangent, grads, term, to_beyond, to_pair = run(
         functools.partial(second_back_kernel, slots, scale, half),
@@ -1039,11 +1060,18 @@
         flops=1_000_000_000,
         name="second_edge",
     )
+    (lane_hot,) = run(
+        lane_hot_kernel,
+        [shape(3, edges, 128, dtype=BF16)],
+        [ids],
+        flops=1_000_000_000,
+        name="lane_hot",
+    )
     to_pair, middle, to_beyond = run(
         functools.partial(first_back_kernel, slots),
         [shape(5, 8, atoms)] * 3,
-        [ids, basis, slope, unit, kind_high, kind_low, turn_high, turn_low, sums_one, gate_one, edge,
-         long, middle, from_pair, from_beyond],
+        [ids, lane_hot, basis, slope, unit, kind_high, kind_low, turn_high, turn_low, sums_one,
+         gate_one, edge, long, middle, from_pair, from_beyond],
         name="first_back",
     )
     total = middle + paired(to_pair, "gx", 1) + beyond(to_beyond, "gx")

time: 83.9 us -> 86 us (1.025)
  waiting for transfers between devices: 25.8 us -> 21.3 us
  starting transfers between devices: 27.9 us -> 31.6 us
  Pallas kernels: 26.9 us -> 29.8 us
    pallas_call x21 -> x22, Pallas kernels: 26.9 us -> 29.8 us  [run(): pl.pallas_call(kernel, out_shape=outs, in_specs=specs, out_specs=[whole()...]
    ppermute x6, waiting for transfers between devices: 15.7 us -> 13 us  [beyond(): lax.ppermute(block, axis, [(other_side(i, count), i) for i in range(count)])]
    ppermute x6, starting transfers between devices: 9.19 us -> 11.7 us  [beyond(): lax.ppermute(block, axis, [(other_side(i, count), i) for i in range(count)])]
    ppermute x17, waiting for transfers between devices: 9.93 us -> 8.06 us  [paired(): lax.ppermute(block, axis, [(i ^ mask, i) for i in range(lax.axis_size(axi...]
    ppermute x17, starting transfers between devices: 14.5 us -> 16 us  [paired(): lax.ppermute(block, axis, [(i ^ mask, i) for i in range(lax.axis_size(axi...]
  transfers between devices with their start and end apart: 25 -> 25, of which waited for: 16 -> 16; matrix products, arithmetic and copies ran while one was open for 0% -> 0% of each run, Pallas kernels for 15% -> 18%
where the time goes in v15:
time: 86 us; the launch traced here: 85.8 us
  starting transfers between devices  31.6 us (37%)
  Pallas kernels  29.8 us (35%)
  waiting for transfers between devices  21.3 us (25%)
  local copies, waits for them, and re-layouts  2.07 us (2%)
  between operations  0.92 us (1%)
    pallas_call x22, Pallas kernels, run(): pl.pallas_call(kernel, out_shape=outs, in_specs=specs, out_specs=[whole()...  29.8 us
    ppermute x17, starting transfers between devices, paired(): lax.ppermute(block, axis, [(i ^ mask, i) for i in range(lax.axis_size(axi...  16 us
    ppermute x6, waiting for transfers between devices, beyond(): lax.ppermute(block, axis, [(other_side(i, count), i) for i in range(count)])  13 us
    ppermute x6, starting transfers between devices, beyond(): lax.ppermute(block, axis, [(other_side(i, count), i) for i in range(count)])  11.7 us
    ppermute x17, waiting for transfers between devices, paired(): lax.ppermute(block, axis, [(i ^ mask, i) for i in range(lax.axis_size(axi...  8.06 us
    ppermute x2, starting transfers between devices, far(): return lax.ppermute(block, axis, route)  3.88 us
    unnamed x27, local copies, waits for them, and re-layouts  2 us
  transfers between devices with their start and end apart: 25, of which 16 were waited for; matrix products, arithmetic and copies ran while one was open for 0% of the time, Pallas kernels for 18%

profile of v15, /device:TPU:0, one launch (start us, length us, event | category | flops | bytes accessed | tf_op | source)
XLA Modules:
  0.0 85.8 jit_solution(11207709373385039990)
XLA Ops:
  0.6 0.1 pad_add_fusion
  0.7 0.1 broadcast_in_dim.4.place_ref
  0.8 0.7 copy-done.9
  1.5 0.7 copy-done.10
  2.2 3.0 %collective-permute-start.2 = (f32[8,128]{1,0:T(8,128)S(1)}, f32[8,128]{1,0:T(8,128)S(1)}, u32[]{:S(2)}, u32[]{:S(2)}) collective-permute-start(f32[8,128]{1,0:T(8,128)S(1)} %pack.1.first_ref), channel_id=1, source_target_pairs={{2,0},{3,1},{0,2},{1,3},{6,4},{7,5},{4,6},{5,7},{10,8},{11,9},{8,1... | collective-permute-start | bytes 12296 | tf_op jit(solution)/shard_map/ppermute | solution.py:42
  5.3 0.1 pack_more.1.own_ref
  5.4 1.6 %collective-permute-start = (f32[40,128]{1,0:T(8,128)S(1)}, f32[40,128]{1,0:T(8,128)S(1)}, u32[]{:S(2)}, u32[]{:S(2)}) collective-permute-start(f32[40,128]{1,0:T(8,128)S(1)} %pack_more.1.own_ref), channel_id=1, source_target_pairs={{1,0},{0,1},{3,2},{2,3},{5,4},{4,5},{7,6},{6,7},{9,8},{8,9},{11,10... | collective-permute-start | bytes 61448 | tf_op jit(solution)/shard_map/ppermute | solution.py:24
  6.9 0.5 collective-permute-start.1
  7.5 1.9 %collective-permute-done.y_pair_ref = f32[40,128]{1,0:T(8,128)S(1)} collective-permute-done((f32[40,128]{1,0:T(8,128)S(1)}, f32[40,128]{1,0:T(8,128)S(1)}, u32[]{:S(2)}, u32[]{:S(2)}) %collective-permute-start) | collective-permute-done | bytes 20512 | tf_op jit(solution)/shard_map/ppermute | solution.py:24
  9.4 2.2 %collective-permute-done.1.y_beyond_ref = f32[40,128]{1,0:T(8,128)S(1)} collective-permute-done((f32[40,128]{1,0:T(8,128)S(1)}, f32[40,128]{1,0:T(8,128)S(1)}, u32[]{:S(2)}, u32[]{:S(2)}) %collective-permute-start.1) | collective-permute-done | bytes 20512 | tf_op jit(solution)/shard_map/ppermute | solution.py:33
  11.6 3.7 %collective-permute-start.4 = (f32[5,8,128]{2,1,0:T(8,128)S(1)}, f32[5,8,128]{2,1,0:T(8,128)S(1)}, u32[]{:S(2)}, u32[]{:S(2)}) collective-permute-start(f32[5,8,128]{2,1,0:T(8,128)S(1)} %constant_dynamic-update-slice_fusion.column_ref.cell_ref), channel_id=1, source_target_pairs={{28,0},{8,4},{4,8},{16,12},{12,16},{24,20},{20,24},{0,28},{29,1},{... | collective-permute-start | bytes 61448 | tf_op jit(solution)/shard_map/ppermute | solution.py:33
  15.4 0.3 prep_second.1
  15.7 0.3 prep_first.1
  16.0 0.9 %collective-permute-done.4.beyond_ref = f32[5,8,128]{2,1,0:T(8,128)S(1)} collective-permute-done((f32[5,8,128]{2,1,0:T(8,128)S(1)}, f32[5,8,128]{2,1,0:T(8,128)S(1)}, u32[]{:S(2)}, u32[]{:S(2)}) %collective-permute-start.4) | collective-permute-done | bytes 20512 | tf_op jit(solution)/shard_map/ppermute | solution.py:33
  16.8 3.3 %first.1 = (bf16[3,128,256]{2,1,0:T(8,128)(2,1)S(1)}, s32[3,3072]{1,0:T(4,128)S(1)}, f32[3,8,3072]{2,1,0:T(8,128)S(1)}, f32[3,8,3072]{2,1,0:T(8,128)S(1)}, f32[3...) custom-call(s32[2,8,128]{2,1,0:T(8,128)S(1)} %broadcast_in_dim.4.place_ref, ...), custom_call_target="tpu_custom_call" | custom-call | flops 10000000 | bytes 1000000 | tf_op jit(solution)/shard_map/first/pallas_call | solution.py:55
  20.1 0.1 collective-permute-start.5
  20.2 3.6 %collective-permute-start.6 = (bf16[3,128,256]{2,1,0:T(8,128)(2,1)S(1)}, bf16[3,128,256]{2,1,0:T(8,128)(2,1)S(1)}, u32[]{:S(2)}, u32[]{:S(2)}) collective-permute-start(bf16[3,128,256]{2,1,0:T(8,128)(2,1)S(1)} %get-tuple-element.97.column_ref), channel_id=1, source_target_pairs={{28,0},{8,4},{4,8},{16,12},{12,16},{24,20},{20,24},{0,28},{29,1},{... | collective-permute-start | bytes 589832 | tf_op jit(solution)/shard_map/ppermute | solution.py:33
  23.8 1.7 %second_near.1 = (f32[4,128,3072]{2,1,0:T(8,128)S(1)}, f32[128,3072]{1,0:T(8,128)S(1)}) custom-call(s32[3,3072]{1,0:T(4,128)S(1)} %get-tuple-element.85.ids_ref, f32[3,8,3072]{2,1,0:T(8,128)S(1)} %get-tuple-element.86.basis_ref, f32[3,8,3072]{2,1,0:T(8,128)S(1)} %get-tuple-element.88.unit_ref, bf16[2,128,32]{2,1,0:T(8,128)(2,1)S(1)} %get-tuple-element.96.left_ref, ...), custom_call_target="tpu_custom_call" | custom-call | flops 2000000000 | bytes 1000000 | tf_op jit(solution)/shard_map/second_near/pallas_call | solution.py:55
  25.5 1.0 %hot_beyond.1.hot_ref = bf16[768,3072]{1,0:T(8,128)(2,1)S(1)} custom-call(s32[3,3072]{1,0:T(4,128)S(1)} %get-tuple-element.85.ids_ref, f32[128,3072]{1,0:T(8,128)S(1)} %get-tuple-element.98.near_ref), custom_call_target="tpu_custom_call" | custom-call | flops 1000000 | bytes 1000000 | tf_op jit(solution)/shard_map/hot_beyond/pallas_call | solution.py:55
  26.5 0.8 second_side.1.near_ref
  27.3 1.4 %collective-permute-done.6.beyond_ref = bf16[3,128,256]{2,1,0:T(8,128)(2,1)S(1)} collective-permute-done((bf16[3,128,256]{2,1,0:T(8,128)(2,1)S(1)}, bf16[3,128,256]{2,1,0:T(8,128)(2,1)S(1)}, u32[]{:S(2)}, u32[]{:S(2)}) %collective-permute-start.6) | collective-permute-done | bytes 196640 | tf_op jit(solution)/shard_map/ppermute | solution.py:33
  28.7 1.8 %second.1 = (bf16[128,3072]{1,0:T(8,128)(2,1)S(1)}, f32[3,128,256]{2,1,0:T(8,128)S(1)}, f32[128,256]{1,0:T(8,128)S(1)}, bf16[80,256]{1,0:T(8,128)(2,1)S(1)}, f32...) custom-call(bf16[768,3072]{1,0:T(8,128)(2,1)S(1)} %hot_beyond.1.hot_ref, f32[4,128,3072]{2,1,0:T(8,128)S(1)} %get-tuple-element.99.weight_ref, ...), custom_call_target="tpu_custom_call" | custom-call | flops 10000000 | bytes 1000000 | tf_op jit(solution)/shard_map/second/pallas_call | solution.py:55
  30.6 0.1 collective-permute-start.7
  30.7 1.0 %collective-permute-start.8 = (bf16[80,256]{1,0:T(8,128)(2,1)S(1)}, bf16[80,256]{1,0:T(8,128)(2,1)S(1)}, u32[]{:S(2)}, u32[]{:S(2)}) collective-permute-start(bf16[80,256]{1,0:T(8,128)(2,1)S(1)} %get-tuple-element.102), channel_id=1, source_target_pairs={{16,0},{20,4},{24,8},{28,12},{0,16},{4,20},{8,24},{12,28},{17,1},{... | collective-permute-start | bytes 122888 | tf_op jit(solution)/shard_map/ppermute | solution.py:24
  31.7 3.3 %collective-permute-start.9 = (bf16[80,256]{1,0:T(8,128)(2,1)S(1)}, bf16[80,256]{1,0:T(8,128)(2,1)S(1)}, u32[]{:S(2)}, u32[]{:S(2)}) collective-permute-start(bf16[80,256]{1,0:T(8,128)(2,1)S(1)} %get-tuple-element.102), channel_id=1, source_target_pairs={{24,0},{28,4},{16,8},{20,12},{8,16},{12,20},{0,24},{4,28},{25,1},{... | collective-permute-start | bytes 122888 | tf_op jit(solution)/shard_map/ppermute | solution.py:24
  35.0 0.8 green.1.refs_0_
  35.8 1.8 %collective-permute-done.9 = bf16[80,256]{1,0:T(8,128)(2,1)S(1)} collective-permute-done((bf16[80,256]{1,0:T(8,128)(2,1)S(1)}, bf16[80,256]{1,0:T(8,128)(2,1)S(1)}, u32[]{:S(2)}, u32[]{:S(2)}) %collective-permute-start.9) | collective-permute-done | bytes 40992 | tf_op jit(solution)/shard_map/ppermute | solution.py:24
  37.7 0.2 collective-permute-start.10
  37.8 1.2 %structure_near.1 = (f32[32,1024]{1,0:T(8,128)S(1)}, f32[32,1024]{1,0:T(8,128)S(1)}, f32[8,1024]{1,0:T(8,128)S(1)}, f32[8,1024]{1,0:T(8,128)S(1)}, bf16[640,1024...) custom-call(s32[2,8,128]{2,1,0:T(8,128)S(1)} %broadcast_in_dim.4.place_ref, ...), custom_call_target="tpu_custom_call" | custom-call | flops 1000000000 | bytes 1000000 | tf_op jit(solution)/shard_map/structure_near/pallas_call | solution.py:55
  39.1 0.1 collective-permute-done.10.blocks.refs_11_
  39.1 1.3 %structure_far.1 = (f32[32,1024]{1,0:T(8,128)S(1)}, f32[32,1024]{1,0:T(8,128)S(1)}, f32[8,1024]{1,0:T(8,128)S(1)}, f32[8,1024]{1,0:T(8,128)S(1)}, bf16[640,1024]...) custom-call(s32[2,8,128]{2,1,0:T(8,128)S(1)} %broadcast_in_dim.4.place_r, ...), custom_call_target="tpu_custom_call" | custom-call | flops 10000000 | bytes 1000000 | tf_op jit(solution)/shard_map/structure_far/pallas_call | solution.py:55
  40.4 0.6 collective-permute-start.11
  41.0 0.6 collective-permute-start.12
  41.5 2.4 %collective-permute-start.13 = (bf16[320,128]{1,0:T(8,128)(2,1)S(1)}, bf16[320,128]{1,0:T(8,128)(2,1)S(1)}, u32[]{:S(2)}, u32[]{:S(2)}) collective-permute-start(bf16[320,128]{1,0:T(8,128)(2,1)S(1)} %get-tuple-element.106), channel_id=1, source_target_pairs={{3,0},{2,1},{1,2},{0,3},{7,4},{6,5},{5,6},{4,7},{11,8},{10,9},{9,1... | collective-permute-start | bytes 245768 | tf_op jit(solution)/shard_map/ppermute | solution.py:24
  43.9 3.0 %hot_back.1.hot_ref = bf16[3072,2304]{1,0:T(8,128)(2,1)S(1)} custom-call(s32[3,3072]{1,0:T(4,128)S(1)} %get-tuple-element.85.ids_ref), custom_call_target="tpu_custom_call" | custom-call | flops 2000000000 | bytes 1000000 | tf_op jit(solution)/shard_map/hot_back/pallas_call | solution.py:55
  47.0 0.2 collective-permute-done.12.refs_3_
  47.2 1.3 %fold_far.1 = (bf16[4,80,256]{2,1,0:T(8,128)(2,1)S(1)}, f32[640,64]{1,0:T(8,128)S(1)}) custom-call(s32[2,8,128]{2,1,0:T(8,128)S(1)} %broadcast_in_dim.4.place_ref, f32[320,128]{1,0:T(8,128)S(1)} %green.1.refs_0_, f32[320,128]{1,0:T(8,128)S(1)} %get-tuple-element.120.refs_1_, bf16[320,128]{1,0:T(8,128)(2,1)S(1)} %collective-permute-done.11.refs_2_, ...), custom_call_target="tpu_custom_call" | custom-call | flops 10000000 | bytes 1000000 | tf_op jit(solution)/shard_map/fold_far/pallas_call | solution.py:55
  48.5 0.1 collective-permute-start.14
  48.6 1.2 %fold_near.1.near_ref = f32[4,80,256]{2,1,0:T(8,128)S(1)} custom-call(s32[2,8,128]{2,1,0:T(8,128)S(1)} %broadcast_in_dim.4.place_ref, f32[640,64]{1,0:T(8,128)S(1)} %get-tuple-element.130.refs_0_, f32[32,1024]{1,0:T(8,128)S(1)} %get-tuple-element.131.refs_1_, f32[32,1024]{1,0:T(8,128)S(1)} %get-tuple-element.132.refs_2_, ...), custom_call_target="tpu_custom_call" | custom-call | flops 1000000000 | bytes 1000000 | tf_op jit(solution)/shard_map/fold_near/pallas_call | solution.py:55
  49.8 0.2 collective-permute-done.14.far_ref
  50.0 0.1 fold_join.1
  50.0 3.3 %collective-permute-start.15 = (bf16[80,256]{1,0:T(8,128)(2,1)S(1)}, bf16[80,256]{1,0:T(8,128)(2,1)S(1)}, u32[]{:S(2)}, u32[]{:S(2)}) collective-permute-start(bf16[80,256]{1,0:T(8,128)(2,1)S(1)} %get-tuple-element.139), channel_id=1, source_target_pairs={{24,0},{28,4},{16,8},{20,12},{8,16},{12,20},{0,24},{4,28},{25,1},{... | collective-permute-start | bytes 122888 | tf_op jit(solution)/shard_map/ppermute | solution.py:24
  53.3 1.2 %collective-permute-start.17 = (bf16[80,256]{1,0:T(8,128)(2,1)S(1)}, bf16[80,256]{1,0:T(8,128)(2,1)S(1)}, u32[]{:S(2)}, u32[]{:S(2)}) collective-permute-start(bf16[80,256]{1,0:T(8,128)(2,1)S(1)} %get-tuple-element.141), channel_id=1, source_target_pairs={{8,0},{12,4},{0,8},{4,12},{24,16},{28,20},{16,24},{20,28},{9,1},{1... | collective-permute-start | bytes 122888 | tf_op jit(solution)/shard_map/ppermute | solution.py:24
  54.5 0.5 readout.1
  55.0 1.2 %collective-permute-done.15.refs_1_ = bf16[80,256]{1,0:T(8,128)(2,1)S(1)} collective-permute-done((bf16[80,256]{1,0:T(8,128)(2,1)S(1)}, bf16[80,256]{1,0:T(8,128)(2,1)S(1)}, u32[]{:S(2)}, u32[]{:S(2)}) %collective-permute-start.15) | collective-permute-done | bytes 40992 | tf_op jit(solution)/shard_map/ppermute | solution.py:24
  56.3 2.0 %collective-permute-done.16.refs_2_ = bf16[80,256]{1,0:T(8,128)(2,1)S(1)} collective-permute-done((bf16[80,256]{1,0:T(8,128)(2,1)S(1)}, bf16[80,256]{1,0:T(8,128)(2,1)S(1)}, u32[]{:S(2)}, u32[]{:S(2)}) %collective-permute-start.16) | collective-permute-done | bytes 40992 | tf_op jit(solution)/shard_map/ppermute | solution.py:24
  58.2 3.0 %second_back.1 = (f32[1,1,256]{2,1,0:T(1,128)}, f32[8,256]{1,0:T(8,128)S(1)}, f32[128,256]{1,0:T(8,128)S(1)}, f32[4,128,256]{2,1,0:T(8,128)S(1)}, bf16[128,3072]...) custom-call(bf16[3072,2304]{1,0:T(8,128)(2,1)S(1)} %hot_back.1.hot_ref, ...), custom_call_target="tpu_custom_call" | custom-call | flops 10000000 | bytes 1000000 | tf_op jit(solution)/shard_map/second_back/pallas_call | solution.py:55
  61.3 2.1 %collective-permute-start.19 = (bf16[3,128,256]{2,1,0:T(8,128)(2,1)S(1)}, bf16[3,128,256]{2,1,0:T(8,128)(2,1)S(1)}, u32[]{:S(2)}, u32[]{:S(2)}) collective-permute-start(bf16[3,128,256]{2,1,0:T(8,128)(2,1)S(1)} %get-tuple-element.147), channel_id=1, source_target_pairs={{28,0},{8,4},{4,8},{16,12},{12,16},{24,20},{20,24},{0,28},{29,1},{... | collective-permute-start | bytes 589832 | tf_op jit(solution)/shard_map/ppermute | solution.py:33
  63.4 2.5 %lane_hot.1.lane_ref = bf16[3,3072,128]{2,1,0:T(8,128)(2,1)S(1)} custom-call(s32[3,3072]{1,0:T(4,128)S(1)} %get-tuple-element.85.ids_ref), custom_call_target="tpu_custom_call" | custom-call | flops 1000000000 | bytes 1000000 | tf_op jit(solution)/shard_map/lane_hot/pallas_call | solution.py:55
  66.0 0.8 second_middle.1.middle_ref
  66.7 1.2 %second_edge.1.edge_ref = f32[32,3072]{1,0:T(8,128)S(1)} custom-call(bf16[2,16,256]{2,1,0:T(8,128)(2,1)S(1)} %get-tuple-element.95.back_ref, bf16[128,3072]{1,0:T(8,128)(2,1)S(1)} %get-tuple-element.101.feature_ref, f32[4,128,256]{2,1,0:T(8,128)S(1)} %get-tuple-element.142.grad_ref), custom_call_target="tpu_custom_call" | custom-call | flops 1000000000 | bytes 1000000 | tf_op jit(solution)/shard_map/second_edge/pallas_call | solution.py:55
  67.9 2.0 %collective-permute-done.19.from_beyond = bf16[3,128,256]{2,1,0:T(8,128)(2,1)S(1)} collective-permute-done((bf16[3,128,256]{2,1,0:T(8,128)(2,1)S(1)}, bf16[3,128,256]{2,1,0:T(8,128)(2,1)S(1)}, u32[]{:S(2)}, u32[]{:S(2)}) %collective-permute-start.19) | collective-permute-done | bytes 196640 | tf_op jit(solution)/shard_map/ppermute | solution.py:33
  69.9 3.5 %first_back.1 = (f32[5,8,256]{2,1,0:T(8,128)S(1)}, f32[5,8,256]{2,1,0:T(8,128)S(1)}, f32[5,8,256]{2,1,0:T(8,128)S(1)}) custom-call(s32[3,3072]{1,0:T(4,128)S(1)} %get-tuple-element.85.ids_ref, bf16[3,3072,128]{2,1,0:T(8,128)(2,1)S(1)} %lane_hot.1.lane_ref, f32[3,8,3072]{2,1,0:T(8,128)S(1)} %get-tuple-element.86.basis_ref, ...), custom_call_target="tpu_custom_call" | custom-call | flops 10000000 | bytes 1000000 | tf_op jit(solution)/shard_map/first_back/pallas_call | solution.py:55
  73.4 0.1 collective-permute-start.20
  73.5 0.6 collective-permute-start.21
  74.1 0.6 collective-permute-done.20
  74.7 4.1 %collective-permute-done.21 = f32[5,8,256]{2,1,0:T(8,128)S(1)} collective-permute-done((f32[5,8,256]{2,1,0:T(8,128)S(1)}, f32[5,8,256]{2,1,0:T(8,128)S(1)}, u32[]{:S(2)}, u32[]{:S(2)}) %collective-permute-start.21) | collective-permute-done | bytes 40992 | tf_op jit(solution)/shard_map/ppermute | solution.py:33
  78.8 1.6 %collective-permute-start.22 = (f32[8,256]{1,0:T(8,128)S(1)}, f32[8,256]{1,0:T(8,128)S(1)}, u32[]{:S(2)}, u32[]{:S(2)}) collective-permute-start(f32[8,256]{1,0:T(8,128)S(1)} %get-tuple-element.157), channel_id=1, source_target_pairs={{1,0},{0,1},{3,2},{2,3},{5,4},{4,5},{7,6},{6,7},{9,8},{8,9},{11,10... | collective-permute-start | bytes 24584 | tf_op jit(solution)/shard_map/ppermute | solution.py:24
  80.4 1.2 %collective-permute-start.23 = (f32[8,256]{1,0:T(8,128)S(1)}, f32[8,256]{1,0:T(8,128)S(1)}, u32[]{:S(2)}, u32[]{:S(2)}) collective-permute-start(f32[8,256]{1,0:T(8,128)S(1)} %get-tuple-element.156), channel_id=1, source_target_pairs={{3,0},{2,1},{1,2},{0,3},{7,4},{6,5},{5,6},{4,7},{11,8},{10,9},{9,1... | collective-permute-start | bytes 24584 | tf_op jit(solution)/shard_map/ppermute | solution.py:33
  81.5 0.8 collective-permute-start.24
  82.4 0.2 collective-permute-done.22
  82.5 2.4 %collective-permute-done.23 = f32[8,256]{1,0:T(8,128)S(1)} collective-permute-done((f32[8,256]{1,0:T(8,128)S(1)}, f32[8,256]{1,0:T(8,128)S(1)}, u32[]{:S(2)}, u32[]{:S(2)}) %collective-permute-start.23) | collective-permute-done | bytes 8224 | tf_op jit(solution)/shard_map/ppermute | solution.py:33
  84.9 0.3 collective-permute-done.24
  85.2 0.6 copy.13
  (42 shorter events, 0.1 us)
Async XLA Ops:
  0.8 0.7 copy-start.9
  1.5 0.7 copy-start.10
  2.1 3.1 %copy-start.5 = (s32[1,1,256,12]{2,1,3,0:T(1,128)S(1)}, s32[1,1,256,12]{2,1,3,0:T(1,128)}, u32[]{:S(2)}) copy-start(s32[1,1,256,12]{2,1,3,0:T(1,128)} %param.13) | copy-start | bytes 36868
  2.2 3.1 %copy-start.7 = (s32[1,1,256]{2,1,0:T(1,128)S(1)}, s32[1,1,256]{2,1,0:T(1,128)}, u32[]{:S(2)}) copy-start(s32[1,1,256]{2,1,0:T(1,128)} %count_ref.1) | copy-start | bytes 3076
  2.2 13.2 %copy-start.1 = (f32[128,128]{1,0:T(8,128)S(1)}, f32[128,128]{1,0:T(8,128)}, u32[]{:S(2)}) copy-start(f32[128,128]{1,0:T(8,128)} %hidden_in.1) | copy-start | bytes 196612
  2.2 13.2 %copy-start.3 = (f32[128,64]{0,1:T(8,128)S(1)}, f32[128,64]{0,1:T(8,128)}, u32[]{:S(2)}) copy-start(f32[128,64]{0,1:T(8,128)} %param.20) | copy-start | bytes 98308
  2.2 13.2 %copy-start.8 = (f32[128]{0:T(128)S(1)}, f32[128]{0:T(128)}, u32[]{:S(2)}) copy-start(f32[128]{0:T(128)} %param.19) | copy-start | bytes 1540
  2.2 13.5 %copy-start = (f32[2,2,128,128]{3,2,1,0:T(8,128)S(1)}, f32[2,2,128,128]{3,2,1,0:T(8,128)}, u32[]{:S(2)}) copy-start(f32[2,2,128,128]{3,2,1,0:T(8,128)} %mixing_in.1) | copy-start | bytes 786436
  2.2 13.4 %copy-start.4 = (f32[2,2,8,128]{3,2,1,0:T(8,128)S(1)}, f32[2,2,8,128]{3,2,1,0:T(8,128)}, u32[]{:S(2)}) copy-start(f32[2,2,8,128]{3,2,1,0:T(8,128)} %radial_in.1) | copy-start | bytes 49156
  2.2 13.4 %copy-start.6 = (f32[6,128]{1,0:T(8,128)S(1)}, f32[6,128]{1,0:T(8,128)}, u32[]{:S(2)}) copy-start(f32[6,128]{1,0:T(8,128)} %embed_in.1) | copy-start | bytes 9220
  2.2 5.3 %collective-permute-start.2 = (f32[8,128]{1,0:T(8,128)S(1)}, f32[8,128]{1,0:T(8,128)S(1)}, u32[]{:S(2)}, u32[]{:S(2)}) collective-permute-start(f32[8,128]{1,0:T(8,128)S(1)} %pack.1.first_ref), channel_id=1, source_target_pairs={{2,0},{3,1},{0,2},{1,3},{6,4},{7,5},{4,6},{5,7},{10,8},{11,9},{8,1... | collective-permute-start | bytes 12296 | tf_op jit(solution)/shard_map/ppermute | solution.py:42
  5.4 4.0 %collective-permute-start = (f32[40,128]{1,0:T(8,128)S(1)}, f32[40,128]{1,0:T(8,128)S(1)}, u32[]{:S(2)}, u32[]{:S(2)}) collective-permute-start(f32[40,128]{1,0:T(8,128)S(1)} %pack_more.1.own_ref), channel_id=1, source_target_pairs={{1,0},{0,1},{3,2},{2,3},{5,4},{4,5},{7,6},{6,7},{9,8},{8,9},{11,10... | collective-permute-start | bytes 61448 | tf_op jit(solution)/shard_map/ppermute | solution.py:24
  6.9 4.7 %collective-permute-start.1 = (f32[40,128]{1,0:T(8,128)S(1)}, f32[40,128]{1,0:T(8,128)S(1)}, u32[]{:S(2)}, u32[]{:S(2)}) collective-permute-start(f32[40,128]{1,0:T(8,128)S(1)} %pack_more.1.own_ref), channel_id=1, source_target_pairs={{3,0},{2,1},{1,2},{0,3},{7,4},{6,5},{5,6},{4,7},{11,8},{10,9},{9,1... | collective-permute-start | bytes 61448 | tf_op jit(solution)/shard_map/ppermute | solution.py:33
  11.6 4.3 %collective-permute-start.3 = (f32[5,8,128]{2,1,0:T(8,128)S(1)}, f32[5,8,128]{2,1,0:T(8,128)S(1)}, u32[]{:S(2)}, u32[]{:S(2)}) collective-permute-start(f32[5,8,128]{2,1,0:T(8,128)S(1)} %constant_dynamic-update-slice_fusion.column_ref.cell_ref), channel_id=1, source_target_pairs={{4,0},{0,4},{12,8},{8,12},{20,16},{16,20},{28,24},{24,28},{5,1},{1... | collective-permute-start | bytes 61448 | tf_op jit(solution)/shard_map/ppermute | solution.py:24
  11.6 5.2 %collective-permute-start.4 = (f32[5,8,128]{2,1,0:T(8,128)S(1)}, f32[5,8,128]{2,1,0:T(8,128)S(1)}, u32[]{:S(2)}, u32[]{:S(2)}) collective-permute-start(f32[5,8,128]{2,1,0:T(8,128)S(1)} %constant_dynamic-update-slice_fusion.column_ref.cell_ref), channel_id=1, source_target_pairs={{28,0},{8,4},{4,8},{16,12},{12,16},{24,20},{20,24},{0,28},{29,1},{... | collective-permute-start | bytes 61448 | tf_op jit(solution)/shard_map/ppermute | solution.py:33
  20.1 6.4 %collective-permute-start.5 = (bf16[3,128,256]{2,1,0:T(8,128)(2,1)S(1)}, bf16[3,128,256]{2,1,0:T(8,128)(2,1)S(1)}, u32[]{:S(2)}, u32[]{:S(2)}) collective-permute-start(bf16[3,128,256]{2,1,0:T(8,128)(2,1)S(1)} %get-tuple-element.97.column_ref), channel_id=1, source_target_pairs={{4,0},{0,4},{12,8},{8,12},{20,16},{16,20},{28,24},{24,28},{5,1},{1... | collective-permute-start | bytes 589832 | tf_op jit(solution)/shard_map/ppermute | solution.py:24
  20.2 8.5 %collective-permute-start.6 = (bf16[3,128,256]{2,1,0:T(8,128)(2,1)S(1)}, bf16[3,128,256]{2,1,0:T(8,128)(2,1)S(1)}, u32[]{:S(2)}, u32[]{:S(2)}) collective-permute-start(bf16[3,128,256]{2,1,0:T(8,128)(2,1)S(1)} %get-tuple-element.97.column_ref), channel_id=1, source_target_pairs={{28,0},{8,4},{4,8},{16,12},{12,16},{24,20},{20,24},{0,28},{29,1},{... | collective-permute-start | bytes 589832 | tf_op jit(solution)/shard_map/ppermute | solution.py:33
  28.7 6.3 %copy-start.2 = (s32[3,4096]{1,0:T(4,128)S(1)}, s32[3,4096]{1,0:T(4,128)}, u32[]{:S(2)}) copy-start(s32[3,4096]{1,0:T(4,128)} %vec_ref.1) | copy-start | bytes 147460
  30.6 5.3 %collective-permute-start.7 = (bf16[80,256]{1,0:T(8,128)(2,1)S(1)}, bf16[80,256]{1,0:T(8,128)(2,1)S(1)}, u32[]{:S(2)}, u32[]{:S(2)}) collective-permute-start(bf16[80,256]{1,0:T(8,128)(2,1)S(1)} %get-tuple-element.102), channel_id=1, source_target_pairs={{8,0},{12,4},{0,8},{4,12},{24,16},{28,20},{16,24},{20,28},{9,1},{1... | collective-permute-start | bytes 122888 | tf_op jit(solution)/shard_map/ppermute | solution.py:24
  30.7 5.2 %collective-permute-start.8 = (bf16[80,256]{1,0:T(8,128)(2,1)S(1)}, bf16[80,256]{1,0:T(8,128)(2,1)S(1)}, u32[]{:S(2)}, u32[]{:S(2)}) collective-permute-start(bf16[80,256]{1,0:T(8,128)(2,1)S(1)} %get-tuple-element.102), channel_id=1, source_target_pairs={{16,0},{20,4},{24,8},{28,12},{0,16},{4,20},{8,24},{12,28},{17,1},{... | collective-permute-start | bytes 122888 | tf_op jit(solution)/shard_map/ppermute | solution.py:24
  31.7 5.9 %collective-permute-start.9 = (bf16[80,256]{1,0:T(8,128)(2,1)S(1)}, bf16[80,256]{1,0:T(8,128)(2,1)S(1)}, u32[]{:S(2)}, u32[]{:S(2)}) collective-permute-start(bf16[80,256]{1,0:T(8,128)(2,1)S(1)} %get-tuple-element.102), channel_id=1, source_target_pairs={{24,0},{28,4},{16,8},{20,12},{8,16},{12,20},{0,24},{4,28},{25,1},{... | collective-permute-start | bytes 122888 | tf_op jit(solution)/shard_map/ppermute | solution.py:24
  37.7 1.5 %collective-permute-start.10 = (bf16[4,80,256]{2,1,0:T(8,128)(2,1)S(1)}, bf16[4,80,256]{2,1,0:T(8,128)(2,1)S(1)}, u32[]{:S(2)}, u32[]{:S(2)}) collective-permute-start(bf16[4,80,256]{2,1,0:T(8,128)(2,1)S(1)} %pad_maximum_fusion.blocks.refs_7_), channel_id=1, source_target_pairs={{4,0},{0,4},{12,8},{8,12},{20,16},{16,20},{28,24},{24,28},{5,1},{1... | collective-permute-start | bytes 491528 | tf_op jit(solution)/shard_map/ppermute | solution.py:24
  40.4 6.6 %collective-permute-start.11 = (bf16[320,128]{1,0:T(8,128)(2,1)S(1)}, bf16[320,128]{1,0:T(8,128)(2,1)S(1)}, u32[]{:S(2)}, u32[]{:S(2)}) collective-permute-start(bf16[320,128]{1,0:T(8,128)(2,1)S(1)} %get-tuple-element.106), channel_id=1, source_target_pairs={{1,0},{0,1},{3,2},{2,3},{5,4},{4,5},{7,6},{6,7},{9,8},{8,9},{11,10... | collective-permute-start | bytes 245768 | tf_op jit(solution)/shard_map/ppermute | solution.py:24
  41.0 6.2 %collective-permute-start.12 = (bf16[320,128]{1,0:T(8,128)(2,1)S(1)}, bf16[320,128]{1,0:T(8,128)(2,1)S(1)}, u32[]{:S(2)}, u32[]{:S(2)}) collective-permute-start(bf16[320,128]{1,0:T(8,128)(2,1)S(1)} %get-tuple-element.106), channel_id=1, source_target_pairs={{2,0},{3,1},{0,2},{1,3},{6,4},{7,5},{4,6},{5,7},{10,8},{11,9},{8,1... | collective-permute-start | bytes 245768 | tf_op jit(solution)/shard_map/ppermute | solution.py:24
  41.5 5.6 %collective-permute-start.13 = (bf16[320,128]{1,0:T(8,128)(2,1)S(1)}, bf16[320,128]{1,0:T(8,128)(2,1)S(1)}, u32[]{:S(2)}, u32[]{:S(2)}) collective-permute-start(bf16[320,128]{1,0:T(8,128)(2,1)S(1)} %get-tuple-element.106), channel_id=1, source_target_pairs={{3,0},{2,1},{1,2},{0,3},{7,4},{6,5},{5,6},{4,7},{11,8},{10,9},{9,1... | collective-permute-start | bytes 245768 | tf_op jit(solution)/shard_map/ppermute | solution.py:24
  48.5 1.5 %collective-permute-start.14 = (bf16[4,80,256]{2,1,0:T(8,128)(2,1)S(1)}, bf16[4,80,256]{2,1,0:T(8,128)(2,1)S(1)}, u32[]{:S(2)}, u32[]{:S(2)}) collective-permute-start(bf16[4,80,256]{2,1,0:T(8,128)(2,1)S(1)} %get-tuple-element.137), channel_id=1, source_target_pairs={{4,0},{0,4},{12,8},{8,12},{20,16},{16,20},{28,24},{24,28},{5,1},{1... | collective-permute-start | bytes 491528 | tf_op jit(solution)/shard_map/ppermute | solution.py:24
  50.0 6.2 %collective-permute-start.15 = (bf16[80,256]{1,0:T(8,128)(2,1)S(1)}, bf16[80,256]{1,0:T(8,128)(2,1)S(1)}, u32[]{:S(2)}, u32[]{:S(2)}) collective-permute-start(bf16[80,256]{1,0:T(8,128)(2,1)S(1)} %get-tuple-element.139), channel_id=1, source_target_pairs={{24,0},{28,4},{16,8},{20,12},{8,16},{12,20},{0,24},{4,28},{25,1},{... | collective-permute-start | bytes 122888 | tf_op jit(solution)/shard_map/ppermute | solution.py:24
  53.3 4.9 %collective-permute-start.16 = (bf16[80,256]{1,0:T(8,128)(2,1)S(1)}, bf16[80,256]{1,0:T(8,128)(2,1)S(1)}, u32[]{:S(2)}, u32[]{:S(2)}) collective-permute-start(bf16[80,256]{1,0:T(8,128)(2,1)S(1)} %get-tuple-element.140), channel_id=1, source_target_pairs={{16,0},{20,4},{24,8},{28,12},{0,16},{4,20},{8,24},{12,28},{17,1},{... | collective-permute-start | bytes 122888 | tf_op jit(solution)/shard_map/ppermute | solution.py:24
  53.3 4.9 %collective-permute-start.17 = (bf16[80,256]{1,0:T(8,128)(2,1)S(1)}, bf16[80,256]{1,0:T(8,128)(2,1)S(1)}, u32[]{:S(2)}, u32[]{:S(2)}) collective-permute-start(bf16[80,256]{1,0:T(8,128)(2,1)S(1)} %get-tuple-element.141), channel_id=1, source_target_pairs={{8,0},{12,4},{0,8},{4,12},{24,16},{28,20},{16,24},{20,28},{9,1},{1... | collective-permute-start | bytes 122888 | tf_op jit(solution)/shard_map/ppermute | solution.py:24
  61.3 6.7 %collective-permute-start.18 = (bf16[3,128,256]{2,1,0:T(8,128)(2,1)S(1)}, bf16[3,128,256]{2,1,0:T(8,128)(2,1)S(1)}, u32[]{:S(2)}, u32[]{:S(2)}) collective-permute-start(bf16[3,128,256]{2,1,0:T(8,128)(2,1)S(1)} %get-tuple-element.146), channel_id=1, source_target_pairs={{4,0},{0,4},{12,8},{8,12},{20,16},{16,20},{28,24},{24,28},{5,1},{1... | collective-permute-start | bytes 589832 | tf_op jit(solution)/shard_map/ppermute | solution.py:24
  61.3 8.7 %collective-permute-start.19 = (bf16[3,128,256]{2,1,0:T(8,128)(2,1)S(1)}, bf16[3,128,256]{2,1,0:T(8,128)(2,1)S(1)}, u32[]{:S(2)}, u32[]{:S(2)}) collective-permute-start(bf16[3,128,256]{2,1,0:T(8,128)(2,1)S(1)} %get-tuple-element.147), channel_id=1, source_target_pairs={{28,0},{8,4},{4,8},{16,12},{12,16},{24,20},{20,24},{0,28},{29,1},{... | collective-permute-start | bytes 589832 | tf_op jit(solution)/shard_map/ppermute | solution.py:33
  73.4 1.3 %collective-permute-start.20 = (f32[5,8,256]{2,1,0:T(8,128)S(1)}, f32[5,8,256]{2,1,0:T(8,128)S(1)}, u32[]{:S(2)}, u32[]{:S(2)}) collective-permute-start(f32[5,8,256]{2,1,0:T(8,128)S(1)} %get-tuple-element.149), channel_id=1, source_target_pairs={{4,0},{0,4},{12,8},{8,12},{20,16},{16,20},{28,24},{24,28},{5,1},{1... | collective-permute-start | bytes 122888 | tf_op jit(solution)/shard_map/ppermute | solution.py:24
  73.5 5.3 %collective-permute-start.21 = (f32[5,8,256]{2,1,0:T(8,128)S(1)}, f32[5,8,256]{2,1,0:T(8,128)S(1)}, u32[]{:S(2)}, u32[]{:S(2)}) collective-permute-start(f32[5,8,256]{2,1,0:T(8,128)S(1)} %get-tuple-element.150), channel_id=1, source_target_pairs={{28,0},{8,4},{4,8},{16,12},{12,16},{24,20},{20,24},{0,28},{29,1},{... | collective-permute-start | bytes 122888 | tf_op jit(solution)/shard_map/ppermute | solution.py:33
  78.8 3.7 %collective-permute-start.22 = (f32[8,256]{1,0:T(8,128)S(1)}, f32[8,256]{1,0:T(8,128)S(1)}, u32[]{:S(2)}, u32[]{:S(2)}) collective-permute-start(f32[8,256]{1,0:T(8,128)S(1)} %get-tuple-element.157), channel_id=1, source_target_pairs={{1,0},{0,1},{3,2},{2,3},{5,4},{4,5},{7,6},{6,7},{9,8},{8,9},{11,10... | collective-permute-start | bytes 24584 | tf_op jit(solution)/shard_map/ppermute | solution.py:24
  80.4 4.5 %collective-permute-start.23 = (f32[8,256]{1,0:T(8,128)S(1)}, f32[8,256]{1,0:T(8,128)S(1)}, u32[]{:S(2)}, u32[]{:S(2)}) collective-permute-start(f32[8,256]{1,0:T(8,128)S(1)} %get-tuple-element.156), channel_id=1, source_target_pairs={{3,0},{2,1},{1,2},{0,3},{7,4},{6,5},{5,6},{4,7},{11,8},{10,9},{9,1... | collective-permute-start | bytes 24584 | tf_op jit(solution)/shard_map/ppermute | solution.py:33
  81.5 3.7 %collective-permute-start.24 = (f32[8,256]{1,0:T(8,128)S(1)}, f32[8,256]{1,0:T(8,128)S(1)}, u32[]{:S(2)}, u32[]{:S(2)}) collective-permute-start(f32[8,256]{1,0:T(8,128)S(1)} %get-tuple-element.155), channel_id=1, source_target_pairs={{2,0},{3,1},{0,2},{1,3},{6,4},{7,5},{4,6},{5,7},{10,8},{11,9},{8,1... | collective-permute-start | bytes 24584 | tf_op jit(solution)/shard_map/ppermute | solution.py:42

commit v16 on v14

--- a/solution.py
+++ b/solution.py
@@ -256,13 +256,17 @@
         hot_ref[:, lanes] = hot_columns(ids[:, lanes], hot_ref.shape[0])
 
 
-def hot_back_kernel(ids_ref, hot_ref):
+def hot_back_kernel(slots_x, ids_ref, hot_ref):
     edges = ids_ref.shape[1]
-    entry = lax.broadcasted_iota(jnp.int32, (128, hot_ref.shape[1]), 1).astype(F32)
+    width = hot_ref.shape[1] // len(slots_x)
+    entry = lax.broadcasted_iota(jnp.int32, (128, width), 1).astype(F32)
     for start in range(0, edges, 128):
         row = jnp.broadcast_to(ids_ref[1:2, start : start + 128].astype(F32), (8, 128))
         column = row.T[:, 0:1]
-        hot_ref[start : start + 128] = jnp.where(column == entry, 1.0, 0.0).astype(BF16)
+        for n, slot in enumerate(slots_x):
+            hot_ref[start : start + 128, n * width : (n + 1) * width] = jnp.where(
+                column - float(slot * width) == entry, 1.0, 0.0
+            ).astype(BF16)
 
 
 def unfold_block(block, atoms):
@@ -271,8 +275,8 @@
     return [jnp.concatenate(rows[q * parts : (q + 1) * parts], axis=1) for q in range(4)]
 
 
-def first_kernel(slots, place_ref, embed_ref, kind_left, mix_high, mix_low, y_pair_ref, own_ref,
-                 y_beyond_ref, pair_ref, column_ref, beyond_ref, low_ref, ids_ref, basis_ref, slope_ref,
+def first_kernel(slots, place_ref, embed_ref, kind_left, mix_high, mix_low, y_beyond_ref, own_ref,
+                 y_pair_ref, beyond_ref, column_ref, pair_ref, low_ref, ids_ref, basis_ref, slope_ref,
                  unit_ref, sums_ref, gate_ref):
     atoms = low_ref.shape[2]
     frame = [pair_ref, column_ref, beyond_ref]
@@ -472,7 +476,7 @@
             term = term + weight_ref[part, :, lanes] * grads[part]
         term_ref[:, lanes] = term.astype(BF16)
     for b in range(3):
-        start = (6 + b) * atoms
+        start = (3 + b) * atoms
         beyond_ref[b] = dot(term_ref[...], hot_ref[:, start : start + atoms]).astype(BF16)
     for b in range(3):
         pair_ref[b] = dot(term_ref[...], hot_ref[:, b * atoms : (b + 1) * atoms]).astype(BF16)
@@ -481,7 +485,7 @@
 def second_middle_kernel(hot_ref, term_ref, cotangent_ref, middle_ref):
     atoms = cotangent_ref.shape[1]
     for b in range(3):
-        grad = dot(term_ref[...], hot_ref[:, (3 + b) * atoms : (4 + b) * atoms])
+        grad = dot(term_ref[...], hot_ref[:, b * atoms : (b + 1) * atoms])
         middle_ref[b] = grad + cotangent_ref[...] if b == 1 else grad
 
 
@@ -513,8 +517,9 @@
         terms += [((n // 3, SLOT_CELLS[cell][n % 3]), found[n]) for n in range(9)]
         for key, term in terms:
             sums[key] = sums[key] + term if key in sums else term
-    for (x, y), total in sums.items():
-        outs[x][y] = total
+    for x in range(3):
+        rows = [sums[(x, y)][:3] for y in range(5)]
+        outs[x][...] = jnp.concatenate(rows + [jnp.zeros((1, rows[0].shape[1]), F32)], axis=0)
 
 
 def first_back_cell(slots, ids, basis_ref, slope_ref, unit_ref, kind_high, kind_low, turn_high,
@@ -836,13 +841,14 @@
         [place, ids, counts, own_place],
         name="pack_more",
     )
-    y_pair, y_beyond = paired(own, "gy", 1), beyond(own, "gy")
+    y_beyond, y_pair = beyond(own, "gy"), paired(own, "gy", 1)
     over_pair = far(own_place, "gy", True)
     over_beyond = over_pair if grid_y == 4 else far(own_place, "gy", False)
     cells = jnp.stack(
         [over_pair, y_pair[:cell_rows], own_place, y_beyond[:cell_rows], over_beyond]
     )
-    cells = [paired(cells, "gx", 1), cells, beyond(cells, "gx")]
+    x_beyond, x_pair = beyond(cells, "gx"), paired(cells, "gx", 1)
+    cells = [x_pair, cells, x_beyond]
 
     norm = 1.0 / math.sqrt(slots)
     kind_rows = 8 * species_embed.shape[0]
@@ -895,7 +901,7 @@
             shape(3, 3, features, atoms),
             shape(3, features, atoms),
         ],
-        [place, embed, kind_left, mix_high, mix_low, y_pair, own, y_beyond] + cells,
+        [place, embed, kind_left, mix_high, mix_low, y_beyond, own, y_pair] + cells[::-1],
         name="first",
     )
     hidden = [paired(low, "gx", 1), low, beyond(low, "gx")]
@@ -980,8 +986,8 @@
     )
     parts = [own_part] + [paired(part, "gy", d) for d in range(1, grid_y)]
     (hot_back,) = run(
-        hot_back_kernel,
-        [shape(edges, 9 * atoms, dtype=BF16)],
+        functools.partial(hot_back_kernel, (0, 2)),
+        [shape(edges, 6 * atoms, dtype=BF16)],
         [ids],
         flops=2_000_000_000,
         name="hot_back",
@@ -1025,10 +1031,17 @@
         name="second_back",
     )
     from_pair, from_beyond = paired(to_pair, "gx", 1), beyond(to_beyond, "gx")
+    (hot_middle,) = run(
+        functools.partial(hot_back_kernel, (1,)),
+        [shape(edges, 3 * atoms, dtype=BF16)],
+        [ids],
+        flops=1_000_000_000,
+        name="hot_middle",
+    )
     (middle,) = run(
         second_middle_kernel,
         [shape(3, features, atoms)],
-        [hot_back, term, cotangent],
+        [hot_middle, term, cotangent],
         flops=1_000_000_000,
         name="second_middle",
     )
@@ -1041,18 +1054,19 @@
     )
     to_pair, middle, to_beyond = run(
         functools.partial(first_back_kernel, slots),
-        [shape(5, 8, atoms)] * 3,
+        [shape(16, atoms)] * 3,
         [ids, basis, slope, unit, kind_high, kind_low, turn_high, turn_low, sums_one, gate_one, edge,
          long, middle, from_pair, from_beyond],
         name="first_back",
     )
     total = middle + paired(to_pair, "gx", 1) + beyond(to_beyond, "gx")
+    total = [total[3 * y : 3 * y + 3] for y in range(5)]
     if grid_y == 4:
         distant = far(total[0] + total[4], "gy", True)
     else:
         distant = far(total[0], "gy", False) + far(total[4], "gy", True)
     total = total[2] + paired(total[1], "gy", 1) + beyond(total[3], "gy") + distant
-    forces = -total[None, :3, None, :]
+    forces = -total[None, :, None, :]
     return (forces.transpose(0, 2, 1, 3), site)
 
 

time: 83.9 us -> 84.5 us (level)
  starting transfers between devices: 27.9 us -> 32 us
  waiting for transfers between devices: 25.8 us -> 21.8 us
    ppermute x6, waiting for transfers between devices: 15.7 us -> 10 us  [beyond(): lax.ppermute(block, axis, [(other_side(i, count), i) for i in range(count)])]
    ppermute x6, starting transfers between devices: 9.19 us -> 14.2 us  [beyond(): lax.ppermute(block, axis, [(other_side(i, count), i) for i in range(count)])]
    ppermute x17, waiting for transfers between devices: 9.93 us -> 11.6 us  [paired(): lax.ppermute(block, axis, [(i ^ mask, i) for i in range(lax.axis_size(axi...]
    pallas_call x21 -> x22, Pallas kernels: 26.9 us -> 27.4 us  [run(): pl.pallas_call(kernel, out_shape=outs, in_specs=specs, out_specs=[whole()...]
  transfers between devices with their start and end apart: 25 -> 25, of which waited for: 16 -> 15; matrix products, arithmetic and copies ran while one was open for 0% -> 0% of each run, Pallas kernels for 15% -> 16%
where the time goes in v16:
time: 84.5 us; the launch traced here: 84.3 us
  starting transfers between devices  32 us (38%)
  Pallas kernels  27.4 us (32%)
  waiting for transfers between devices  21.8 us (26%)
  local copies, waits for them, and re-layouts  2.07 us (2%)
  between operations  0.96 us (1%)
    pallas_call x22, Pallas kernels, run(): pl.pallas_call(kernel, out_shape=outs, in_specs=specs, out_specs=[whole()...  27.4 us
    ppermute x6, starting transfers between devices, beyond(): lax.ppermute(block, axis, [(other_side(i, count), i) for i in range(count)])  14.2 us
    ppermute x17, starting transfers between devices, paired(): lax.ppermute(block, axis, [(i ^ mask, i) for i in range(lax.axis_size(axi...  13.8 us
    ppermute x17, waiting for transfers between devices, paired(): lax.ppermute(block, axis, [(i ^ mask, i) for i in range(lax.axis_size(axi...  11.6 us
    ppermute x6, waiting for transfers between devices, beyond(): lax.ppermute(block, axis, [(other_side(i, count), i) for i in range(count)])  10 us
    ppermute x2, starting transfers between devices, far(): return lax.ppermute(block, axis, route)  3.93 us
    unnamed x27, local copies, waits for them, and re-layouts  2 us
  transfers between devices with their start and end apart: 25, of which 15 were waited for; matrix products, arithmetic and copies ran while one was open for 0% of the time, Pallas kernels for 16%

profile of v16, /device:TPU:0, one launch (start us, length us, event | category | flops | bytes accessed | tf_op | source)
XLA Modules:
  0.0 84.3 jit_solution(4235691978580555469)
XLA Ops:
  0.6 0.1 pad_add_fusion
  0.7 0.1 broadcast_in_dim.4.place_ref
  0.8 0.7 copy-done.9
  1.5 0.7 copy-done.10
  2.2 0.0 copy-start.6
  2.2 3.0 %collective-permute-start.2 = (f32[8,128]{1,0:T(8,128)S(1)}, f32[8,128]{1,0:T(8,128)S(1)}, u32[]{:S(2)}, u32[]{:S(2)}) collective-permute-start(f32[8,128]{1,0:T(8,128)S(1)} %pack.1.first_ref), channel_id=1, source_target_pairs={{2,0},{3,1},{0,2},{1,3},{6,4},{7,5},{4,6},{5,7},{10,8},{11,9},{8,1... | collective-permute-start | bytes 12296 | tf_op jit(solution)/shard_map/ppermute | solution.py:42
  5.3 0.1 pack_more.1.own_ref
  5.4 1.6 %collective-permute-start = (f32[40,128]{1,0:T(8,128)S(1)}, f32[40,128]{1,0:T(8,128)S(1)}, u32[]{:S(2)}, u32[]{:S(2)}) collective-permute-start(f32[40,128]{1,0:T(8,128)S(1)} %pack_more.1.own_ref), channel_id=1, source_target_pairs={{3,0},{2,1},{1,2},{0,3},{7,4},{6,5},{5,6},{4,7},{11,8},{10,9},{9,1... | collective-permute-start | bytes 61448 | tf_op jit(solution)/shard_map/ppermute | solution.py:33
  6.9 0.5 collective-permute-start.1
  7.5 3.2 %collective-permute-done.1.y_pair_ref = f32[40,128]{1,0:T(8,128)S(1)} collective-permute-done((f32[40,128]{1,0:T(8,128)S(1)}, f32[40,128]{1,0:T(8,128)S(1)}, u32[]{:S(2)}, u32[]{:S(2)}) %collective-permute-start.1) | collective-permute-done | bytes 20512 | tf_op jit(solution)/shard_map/ppermute | solution.py:24
  10.7 0.1 collective-permute-start.3
  10.8 3.7 %collective-permute-start.4 = (f32[5,8,128]{2,1,0:T(8,128)S(1)}, f32[5,8,128]{2,1,0:T(8,128)S(1)}, u32[]{:S(2)}, u32[]{:S(2)}) collective-permute-start(f32[5,8,128]{2,1,0:T(8,128)S(1)} %constant_dynamic-update-slice_fusion.column_ref.cell_ref), channel_id=1, source_target_pairs={{28,0},{8,4},{4,8},{16,12},{12,16},{24,20},{20,24},{0,28},{29,1},{... | collective-permute-start | bytes 61448 | tf_op jit(solution)/shard_map/ppermute | solution.py:33
  14.5 0.3 prep_first.1
  14.9 0.3 prep_second.1
  15.1 0.9 %collective-permute-done.4.beyond_ref = f32[5,8,128]{2,1,0:T(8,128)S(1)} collective-permute-done((f32[5,8,128]{2,1,0:T(8,128)S(1)}, f32[5,8,128]{2,1,0:T(8,128)S(1)}, u32[]{:S(2)}, u32[]{:S(2)}) %collective-permute-start.4) | collective-permute-done | bytes 20512 | tf_op jit(solution)/shard_map/ppermute | solution.py:33
  16.0 2.9 %first.1 = (bf16[3,128,256]{2,1,0:T(8,128)(2,1)S(1)}, s32[3,3072]{1,0:T(4,128)S(1)}, f32[3,8,3072]{2,1,0:T(8,128)S(1)}, f32[3,8,3072]{2,1,0:T(8,128)S(1)}, f32[3...) custom-call(s32[2,8,128]{2,1,0:T(8,128)S(1)} %broadcast_in_dim.4.place_ref, ...), custom_call_target="tpu_custom_call" | custom-call | flops 10000000 | bytes 1000000 | tf_op jit(solution)/shard_map/first/pallas_call | solution.py:55
  18.9 0.1 collective-permute-start.5
  19.0 3.6 %collective-permute-start.6 = (bf16[3,128,256]{2,1,0:T(8,128)(2,1)S(1)}, bf16[3,128,256]{2,1,0:T(8,128)(2,1)S(1)}, u32[]{:S(2)}, u32[]{:S(2)}) collective-permute-start(bf16[3,128,256]{2,1,0:T(8,128)(2,1)S(1)} %get-tuple-element.97.column_ref), channel_id=1, source_target_pairs={{28,0},{8,4},{4,8},{16,12},{12,16},{24,20},{20,24},{0,28},{29,1},{... | collective-permute-start | bytes 589832 | tf_op jit(solution)/shard_map/ppermute | solution.py:33
  22.6 1.7 %second_near.1 = (f32[4,128,3072]{2,1,0:T(8,128)S(1)}, f32[128,3072]{1,0:T(8,128)S(1)}) custom-call(s32[3,3072]{1,0:T(4,128)S(1)} %get-tuple-element.85.ids_ref, f32[3,8,3072]{2,1,0:T(8,128)S(1)} %get-tuple-element.86.basis_ref, f32[3,8,3072]{2,1,0:T(8,128)S(1)} %get-tuple-element.88.unit_ref, bf16[2,128,32]{2,1,0:T(8,128)(2,1)S(1)} %get-tuple-element.96.left_ref, ...), custom_call_target="tpu_custom_call" | custom-call | flops 2000000000 | bytes 1000000 | tf_op jit(solution)/shard_map/second_near/pallas_call | solution.py:55
  24.3 1.0 %hot_beyond.1.hot_ref = bf16[768,3072]{1,0:T(8,128)(2,1)S(1)} custom-call(s32[3,3072]{1,0:T(4,128)S(1)} %get-tuple-element.85.ids_ref, f32[128,3072]{1,0:T(8,128)S(1)} %get-tuple-element.98.near_ref), custom_call_target="tpu_custom_call" | custom-call | flops 1000000 | bytes 1000000 | tf_op jit(solution)/shard_map/hot_beyond/pallas_call | solution.py:55
  25.3 0.8 second_side.1.near_ref
  26.1 1.4 %collective-permute-done.6.beyond_ref = bf16[3,128,256]{2,1,0:T(8,128)(2,1)S(1)} collective-permute-done((bf16[3,128,256]{2,1,0:T(8,128)(2,1)S(1)}, bf16[3,128,256]{2,1,0:T(8,128)(2,1)S(1)}, u32[]{:S(2)}, u32[]{:S(2)}) %collective-permute-start.6) | collective-permute-done | bytes 196640 | tf_op jit(solution)/shard_map/ppermute | solution.py:33
  27.5 1.9 %second.1 = (bf16[128,3072]{1,0:T(8,128)(2,1)S(1)}, f32[3,128,256]{2,1,0:T(8,128)S(1)}, f32[128,256]{1,0:T(8,128)S(1)}, bf16[80,256]{1,0:T(8,128)(2,1)S(1)}, f32...) custom-call(bf16[768,3072]{1,0:T(8,128)(2,1)S(1)} %hot_beyond.1.hot_ref, f32[4,128,3072]{2,1,0:T(8,128)S(1)} %get-tuple-element.99.weight_ref, ...), custom_call_target="tpu_custom_call" | custom-call | flops 10000000 | bytes 1000000 | tf_op jit(solution)/shard_map/second/pallas_call | solution.py:55
  29.4 0.5 collective-permute-start.9
  30.0 3.9 %collective-permute-start.7 = (bf16[80,256]{1,0:T(8,128)(2,1)S(1)}, bf16[80,256]{1,0:T(8,128)(2,1)S(1)}, u32[]{:S(2)}, u32[]{:S(2)}) collective-permute-start(bf16[80,256]{1,0:T(8,128)(2,1)S(1)} %get-tuple-element.102), channel_id=1, source_target_pairs={{8,0},{12,4},{0,8},{4,12},{24,16},{28,20},{16,24},{20,28},{9,1},{1... | collective-permute-start | bytes 122888 | tf_op jit(solution)/shard_map/ppermute | solution.py:24
  33.9 0.8 green.1.refs_0_
  34.7 0.7 collective-permute-done.9
  35.4 1.0 %collective-permute-done.7 = bf16[80,256]{1,0:T(8,128)(2,1)S(1)} collective-permute-done((bf16[80,256]{1,0:T(8,128)(2,1)S(1)}, bf16[80,256]{1,0:T(8,128)(2,1)S(1)}, u32[]{:S(2)}, u32[]{:S(2)}) %collective-permute-start.7) | collective-permute-done | bytes 40992 | tf_op jit(solution)/shard_map/ppermute | solution.py:24
  36.4 0.1 collective-permute-start.10
  36.5 1.2 %structure_near.1 = (f32[32,1024]{1,0:T(8,128)S(1)}, f32[32,1024]{1,0:T(8,128)S(1)}, f32[8,1024]{1,0:T(8,128)S(1)}, f32[8,1024]{1,0:T(8,128)S(1)}, bf16[640,1024...) custom-call(s32[2,8,128]{2,1,0:T(8,128)S(1)} %broadcast_in_dim.4.place_ref, ...), custom_call_target="tpu_custom_call" | custom-call | flops 1000000000 | bytes 1000000 | tf_op jit(solution)/shard_map/structure_near/pallas_call | solution.py:55
  37.7 0.2 collective-permute-done.10.blocks.refs_11_
  37.9 1.2 %structure_far.1 = (f32[32,1024]{1,0:T(8,128)S(1)}, f32[32,1024]{1,0:T(8,128)S(1)}, f32[8,1024]{1,0:T(8,128)S(1)}, f32[8,1024]{1,0:T(8,128)S(1)}, bf16[640,1024]...) custom-call(s32[2,8,128]{2,1,0:T(8,128)S(1)} %broadcast_in_dim.4.place_r, ...), custom_call_target="tpu_custom_call" | custom-call | flops 10000000 | bytes 1000000 | tf_op jit(solution)/shard_map/structure_far/pallas_call | solution.py:55
  39.1 0.9 %collective-permute-start.11 = (bf16[320,128]{1,0:T(8,128)(2,1)S(1)}, bf16[320,128]{1,0:T(8,128)(2,1)S(1)}, u32[]{:S(2)}, u32[]{:S(2)}) collective-permute-start(bf16[320,128]{1,0:T(8,128)(2,1)S(1)} %get-tuple-element.106), channel_id=1, source_target_pairs={{1,0},{0,1},{3,2},{2,3},{5,4},{4,5},{7,6},{6,7},{9,8},{8,9},{11,10... | collective-permute-start | bytes 245768 | tf_op jit(solution)/shard_map/ppermute | solution.py:24
  40.0 1.2 %collective-permute-start.12 = (bf16[320,128]{1,0:T(8,128)(2,1)S(1)}, bf16[320,128]{1,0:T(8,128)(2,1)S(1)}, u32[]{:S(2)}, u32[]{:S(2)}) collective-permute-start(bf16[320,128]{1,0:T(8,128)(2,1)S(1)} %get-tuple-element.106), channel_id=1, source_target_pairs={{2,0},{3,1},{0,2},{1,3},{6,4},{7,5},{4,6},{5,7},{10,8},{11,9},{8,1... | collective-permute-start | bytes 245768 | tf_op jit(solution)/shard_map/ppermute | solution.py:24
  41.2 1.5 %collective-permute-start.13 = (bf16[320,128]{1,0:T(8,128)(2,1)S(1)}, bf16[320,128]{1,0:T(8,128)(2,1)S(1)}, u32[]{:S(2)}, u32[]{:S(2)}) collective-permute-start(bf16[320,128]{1,0:T(8,128)(2,1)S(1)} %get-tuple-element.106), channel_id=1, source_target_pairs={{3,0},{2,1},{1,2},{0,3},{7,4},{6,5},{5,6},{4,7},{11,8},{10,9},{9,1... | collective-permute-start | bytes 245768 | tf_op jit(solution)/shard_map/ppermute | solution.py:24
  42.7 2.3 %hot_back.1.hot_ref = bf16[3072,1536]{1,0:T(8,128)(2,1)S(1)} custom-call(s32[3,3072]{1,0:T(4,128)S(1)} %get-tuple-element.85.ids_ref), custom_call_target="tpu_custom_call" | custom-call | flops 2000000000 | bytes 1000000 | tf_op jit(solution)/shard_map/hot_back/pallas_call | solution.py:55
  45.0 1.6 %collective-permute-done.13.refs_4_ = bf16[320,128]{1,0:T(8,128)(2,1)S(1)} collective-permute-done((bf16[320,128]{1,0:T(8,128)(2,1)S(1)}, bf16[320,128]{1,0:T(8,128)(2,1)S(1)}, u32[]{:S(2)}, u32[]{:S(2)}) %collective-permute-start.13) | collective-permute-done | bytes 81952 | tf_op jit(solution)/shard_map/ppermute | solution.py:24
  46.6 1.3 %fold_far.1 = (bf16[4,80,256]{2,1,0:T(8,128)(2,1)S(1)}, f32[640,64]{1,0:T(8,128)S(1)}) custom-call(s32[2,8,128]{2,1,0:T(8,128)S(1)} %broadcast_in_dim.4.place_ref, f32[320,128]{1,0:T(8,128)S(1)} %green.1.refs_0_, f32[320,128]{1,0:T(8,128)S(1)} %get-tuple-element.120.refs_1_, bf16[320,128]{1,0:T(8,128)(2,1)S(1)} %collective-permute-done.11.refs_2_, ...), custom_call_target="tpu_custom_call" | custom-call | flops 10000000 | bytes 1000000 | tf_op jit(solution)/shard_map/fold_far/pallas_call | solution.py:55
  47.9 0.1 collective-permute-start.14
  48.0 1.2 %fold_near.1.near_ref = f32[4,80,256]{2,1,0:T(8,128)S(1)} custom-call(s32[2,8,128]{2,1,0:T(8,128)S(1)} %broadcast_in_dim.4.place_ref, f32[640,64]{1,0:T(8,128)S(1)} %get-tuple-element.130.refs_0_, f32[32,1024]{1,0:T(8,128)S(1)} %get-tuple-element.131.refs_1_, f32[32,1024]{1,0:T(8,128)S(1)} %get-tuple-element.132.refs_2_, ...), custom_call_target="tpu_custom_call" | custom-call | flops 1000000000 | bytes 1000000 | tf_op jit(solution)/shard_map/fold_near/pallas_call | solution.py:55
  49.2 0.2 collective-permute-done.14.far_ref
  49.4 0.1 fold_join.1
  49.4 1.5 %collective-permute-start.15 = (bf16[80,256]{1,0:T(8,128)(2,1)S(1)}, bf16[80,256]{1,0:T(8,128)(2,1)S(1)}, u32[]{:S(2)}, u32[]{:S(2)}) collective-permute-start(bf16[80,256]{1,0:T(8,128)(2,1)S(1)} %get-tuple-element.139), channel_id=1, source_target_pairs={{8,0},{12,4},{0,8},{4,12},{24,16},{28,20},{16,24},{20,28},{9,1},{1... | collective-permute-start | bytes 122888 | tf_op jit(solution)/shard_map/ppermute | solution.py:24
  50.9 1.1 %collective-permute-start.16 = (bf16[80,256]{1,0:T(8,128)(2,1)S(1)}, bf16[80,256]{1,0:T(8,128)(2,1)S(1)}, u32[]{:S(2)}, u32[]{:S(2)}) collective-permute-start(bf16[80,256]{1,0:T(8,128)(2,1)S(1)} %get-tuple-element.140), channel_id=1, source_target_pairs={{16,0},{20,4},{24,8},{28,12},{0,16},{4,20},{8,24},{12,28},{17,1},{... | collective-permute-start | bytes 122888 | tf_op jit(solution)/shard_map/ppermute | solution.py:24
  52.1 1.8 %collective-permute-start.17 = (bf16[80,256]{1,0:T(8,128)(2,1)S(1)}, bf16[80,256]{1,0:T(8,128)(2,1)S(1)}, u32[]{:S(2)}, u32[]{:S(2)}) collective-permute-start(bf16[80,256]{1,0:T(8,128)(2,1)S(1)} %get-tuple-element.141), channel_id=1, source_target_pairs={{24,0},{28,4},{16,8},{20,12},{8,16},{12,20},{0,24},{4,28},{25,1},{... | collective-permute-start | bytes 122888 | tf_op jit(solution)/shard_map/ppermute | solution.py:24
  53.9 0.5 readout.1
  54.4 2.7 %collective-permute-done.16.refs_2_ = bf16[80,256]{1,0:T(8,128)(2,1)S(1)} collective-permute-done((bf16[80,256]{1,0:T(8,128)(2,1)S(1)}, bf16[80,256]{1,0:T(8,128)(2,1)S(1)}, u32[]{:S(2)}, u32[]{:S(2)}) %collective-permute-start.16) | collective-permute-done | bytes 40992 | tf_op jit(solution)/shard_map/ppermute | solution.py:24
  57.1 0.8 %collective-permute-done.17.refs_3_ = bf16[80,256]{1,0:T(8,128)(2,1)S(1)} collective-permute-done((bf16[80,256]{1,0:T(8,128)(2,1)S(1)}, bf16[80,256]{1,0:T(8,128)(2,1)S(1)}, u32[]{:S(2)}, u32[]{:S(2)}) %collective-permute-start.17) | collective-permute-done | bytes 40992 | tf_op jit(solution)/shard_map/ppermute | solution.py:24
  58.0 2.8 %second_back.1 = (f32[1,1,256]{2,1,0:T(1,128)}, f32[8,256]{1,0:T(8,128)S(1)}, f32[128,256]{1,0:T(8,128)S(1)}, f32[4,128,256]{2,1,0:T(8,128)S(1)}, bf16[128,3072]...) custom-call(bf16[3072,1536]{1,0:T(8,128)(2,1)S(1)} %hot_back.1.hot_ref, ...), custom_call_target="tpu_custom_call" | custom-call | flops 10000000 | bytes 1000000 | tf_op jit(solution)/shard_map/second_back/pallas_call | solution.py:55
  60.8 1.8 %collective-permute-start.19 = (bf16[3,128,256]{2,1,0:T(8,128)(2,1)S(1)}, bf16[3,128,256]{2,1,0:T(8,128)(2,1)S(1)}, u32[]{:S(2)}, u32[]{:S(2)}) collective-permute-start(bf16[3,128,256]{2,1,0:T(8,128)(2,1)S(1)} %get-tuple-element.147), channel_id=1, source_target_pairs={{28,0},{8,4},{4,8},{16,12},{12,16},{24,20},{20,24},{0,28},{29,1},{... | collective-permute-start | bytes 589832 | tf_op jit(solution)/shard_map/ppermute | solution.py:33
  62.6 1.3 %hot_middle.1.hot_ref = bf16[3072,768]{1,0:T(8,128)(2,1)S(1)} custom-call(s32[3,3072]{1,0:T(4,128)S(1)} %get-tuple-element.85.ids_ref), custom_call_target="tpu_custom_call" | custom-call | flops 1000000000 | bytes 1000000 | tf_op jit(solution)/shard_map/hot_middle/pallas_call | solution.py:55
  63.9 1.2 %second_edge.1.edge_ref = f32[32,3072]{1,0:T(8,128)S(1)} custom-call(bf16[2,16,256]{2,1,0:T(8,128)(2,1)S(1)} %get-tuple-element.95.back_ref, bf16[128,3072]{1,0:T(8,128)(2,1)S(1)} %get-tuple-element.101.feature_ref, f32[4,128,256]{2,1,0:T(8,128)S(1)} %get-tuple-element.142.grad_ref), custom_call_target="tpu_custom_call" | custom-call | flops 1000000000 | bytes 1000000 | tf_op jit(solution)/shard_map/second_edge/pallas_call | solution.py:55
  65.1 0.8 second_middle.1.middle_ref
  66.0 2.4 %collective-permute-done.19.from_beyond = bf16[3,128,256]{2,1,0:T(8,128)(2,1)S(1)} collective-permute-done((bf16[3,128,256]{2,1,0:T(8,128)(2,1)S(1)}, bf16[3,128,256]{2,1,0:T(8,128)(2,1)S(1)}, u32[]{:S(2)}, u32[]{:S(2)}) %collective-permute-start.19) | collective-permute-done | bytes 196640 | tf_op jit(solution)/shard_map/ppermute | solution.py:33
  68.4 3.6 %first_back.1 = (f32[16,256]{1,0:T(8,128)S(1)}, f32[16,256]{1,0:T(8,128)S(1)}, f32[16,256]{1,0:T(8,128)S(1)}) custom-call(s32[3,3072]{1,0:T(4,128)S(1)} %get-tuple-element.85.ids_ref, f32[3,8,3072]{2,1,0:T(8,128)S(1)} %get-tuple-element.86.basis_ref, f32[3,8,3072]{2,1,0:T(8,128)S(1)} %get-tuple-element.87.slope_ref, ...), custom_call_target="tpu_custom_call" | custom-call | flops 10000000 | bytes 1000000 | tf_op jit(solution)/shard_map/first_back/pallas_call | solution.py:55
  72.0 1.5 %collective-permute-start.21 = (f32[16,256]{1,0:T(8,128)S(1)}, f32[16,256]{1,0:T(8,128)S(1)}, u32[]{:S(2)}, u32[]{:S(2)}) collective-permute-start(f32[16,256]{1,0:T(8,128)S(1)} %get-tuple-element.150), channel_id=1, source_target_pairs={{28,0},{8,4},{4,8},{16,12},{12,16},{24,20},{20,24},{0,28},{29,1},{... | collective-permute-start | bytes 49160 | tf_op jit(solution)/shard_map/ppermute | solution.py:33
  73.5 3.6 %collective-permute-done.21 = f32[16,256]{1,0:T(8,128)S(1)} collective-permute-done((f32[16,256]{1,0:T(8,128)S(1)}, f32[16,256]{1,0:T(8,128)S(1)}, u32[]{:S(2)}, u32[]{:S(2)}) %collective-permute-start.21) | collective-permute-done | bytes 16416 | tf_op jit(solution)/shard_map/ppermute | solution.py:33
  77.1 0.9 %collective-permute-start.24 = (f32[3,256]{1,0:T(4,128)S(1)}, f32[3,256]{1,0:T(4,128)S(1)}, u32[]{:S(2)}, u32[]{:S(2)}) collective-permute-start(f32[3,256]{1,0:T(4,128)S(1)} %get-tuple-element.155), channel_id=1, source_target_pairs={{2,0},{3,1},{0,2},{1,3},{6,4},{7,5},{4,6},{5,7},{10,8},{11,9},{8,1... | collective-permute-start | bytes 9224 | tf_op jit(solution)/shard_map/ppermute | solution.py:42
  78.0 2.1 %collective-permute-start.23 = (f32[3,256]{1,0:T(4,128)S(1)}, f32[3,256]{1,0:T(4,128)S(1)}, u32[]{:S(2)}, u32[]{:S(2)}) collective-permute-start(f32[3,256]{1,0:T(4,128)S(1)} %get-tuple-element.156), channel_id=1, source_target_pairs={{3,0},{2,1},{1,2},{0,3},{7,4},{6,5},{5,6},{4,7},{11,8},{10,9},{9,1... | collective-permute-start | bytes 9224 | tf_op jit(solution)/shard_map/ppermute | solution.py:33
  80.1 0.5 collective-permute-start.22
  80.7 0.1 collective-permute-done.24
  80.8 1.7 %collective-permute-done.23 = f32[3,256]{1,0:T(4,128)S(1)} collective-permute-done((f32[3,256]{1,0:T(4,128)S(1)}, f32[3,256]{1,0:T(4,128)S(1)}, u32[]{:S(2)}, u32[]{:S(2)}) %collective-permute-start.23) | collective-permute-done | bytes 3104 | tf_op jit(solution)/shard_map/ppermute | solution.py:33
  82.5 1.2 %collective-permute-done.22 = f32[3,256]{1,0:T(4,128)S(1)} collective-permute-done((f32[3,256]{1,0:T(4,128)S(1)}, f32[3,256]{1,0:T(4,128)S(1)}, u32[]{:S(2)}, u32[]{:S(2)}) %collective-permute-start.22) | collective-permute-done | bytes 3104 | tf_op jit(solution)/shard_map/ppermute | solution.py:24
  83.7 0.6 copy.13
  (42 shorter events, 0.1 us)
Async XLA Ops:
  0.8 0.7 copy-start.9
  1.5 0.7 copy-start.10
  2.1 3.1 %copy-start.5 = (s32[1,1,256,12]{2,1,3,0:T(1,128)S(1)}, s32[1,1,256,12]{2,1,3,0:T(1,128)}, u32[]{:S(2)}) copy-start(s32[1,1,256,12]{2,1,3,0:T(1,128)} %param.13) | copy-start | bytes 36868
  2.2 3.1 %copy-start.7 = (s32[1,1,256]{2,1,0:T(1,128)S(1)}, s32[1,1,256]{2,1,0:T(1,128)}, u32[]{:S(2)}) copy-start(s32[1,1,256]{2,1,0:T(1,128)} %count_ref.1) | copy-start | bytes 3076
  2.2 12.4 %copy-start = (f32[2,2,128,128]{3,2,1,0:T(8,128)S(1)}, f32[2,2,128,128]{3,2,1,0:T(8,128)}, u32[]{:S(2)}) copy-start(f32[2,2,128,128]{3,2,1,0:T(8,128)} %mixing_in.1) | copy-start | bytes 786436
  2.2 12.4 %copy-start.4 = (f32[2,2,8,128]{3,2,1,0:T(8,128)S(1)}, f32[2,2,8,128]{3,2,1,0:T(8,128)}, u32[]{:S(2)}) copy-start(f32[2,2,8,128]{3,2,1,0:T(8,128)} %radial_in.1) | copy-start | bytes 49156
  2.2 12.4 %copy-start.6 = (f32[6,128]{1,0:T(8,128)S(1)}, f32[6,128]{1,0:T(8,128)}, u32[]{:S(2)}) copy-start(f32[6,128]{1,0:T(8,128)} %embed_in.1) | copy-start | bytes 9220
  2.2 12.7 %copy-start.1 = (f32[128,128]{1,0:T(8,128)S(1)}, f32[128,128]{1,0:T(8,128)}, u32[]{:S(2)}) copy-start(f32[128,128]{1,0:T(8,128)} %hidden_in.1) | copy-start | bytes 196612
  2.2 12.7 %copy-start.3 = (f32[128,64]{0,1:T(8,128)S(1)}, f32[128,64]{0,1:T(8,128)}, u32[]{:S(2)}) copy-start(f32[128,64]{0,1:T(8,128)} %param.20) | copy-start | bytes 98308
  2.2 12.7 %copy-start.8 = (f32[128]{0:T(128)S(1)}, f32[128]{0:T(128)}, u32[]{:S(2)}) copy-start(f32[128]{0:T(128)} %param.19) | copy-start | bytes 1540
  2.2 5.3 %collective-permute-start.2 = (f32[8,128]{1,0:T(8,128)S(1)}, f32[8,128]{1,0:T(8,128)S(1)}, u32[]{:S(2)}, u32[]{:S(2)}) collective-permute-start(f32[8,128]{1,0:T(8,128)S(1)} %pack.1.first_ref), channel_id=1, source_target_pairs={{2,0},{3,1},{0,2},{1,3},{6,4},{7,5},{4,6},{5,7},{10,8},{11,9},{8,1... | collective-permute-start | bytes 12296 | tf_op jit(solution)/shard_map/ppermute | solution.py:42
  5.4 5.3 %collective-permute-start = (f32[40,128]{1,0:T(8,128)S(1)}, f32[40,128]{1,0:T(8,128)S(1)}, u32[]{:S(2)}, u32[]{:S(2)}) collective-permute-start(f32[40,128]{1,0:T(8,128)S(1)} %pack_more.1.own_ref), channel_id=1, source_target_pairs={{3,0},{2,1},{1,2},{0,3},{7,4},{6,5},{5,6},{4,7},{11,8},{10,9},{9,1... | collective-permute-start | bytes 61448 | tf_op jit(solution)/shard_map/ppermute | solution.py:33
  6.9 3.8 %collective-permute-start.1 = (f32[40,128]{1,0:T(8,128)S(1)}, f32[40,128]{1,0:T(8,128)S(1)}, u32[]{:S(2)}, u32[]{:S(2)}) collective-permute-start(f32[40,128]{1,0:T(8,128)S(1)} %pack_more.1.own_ref), channel_id=1, source_target_pairs={{1,0},{0,1},{3,2},{2,3},{5,4},{4,5},{7,6},{6,7},{9,8},{8,9},{11,10... | collective-permute-start | bytes 61448 | tf_op jit(solution)/shard_map/ppermute | solution.py:24
  10.7 4.4 %collective-permute-start.3 = (f32[5,8,128]{2,1,0:T(8,128)S(1)}, f32[5,8,128]{2,1,0:T(8,128)S(1)}, u32[]{:S(2)}, u32[]{:S(2)}) collective-permute-start(f32[5,8,128]{2,1,0:T(8,128)S(1)} %constant_dynamic-update-slice_fusion.column_ref.cell_ref), channel_id=1, source_target_pairs={{4,0},{0,4},{12,8},{8,12},{20,16},{16,20},{28,24},{24,28},{5,1},{1... | collective-permute-start | bytes 61448 | tf_op jit(solution)/shard_map/ppermute | solution.py:24
  10.8 5.2 %collective-permute-start.4 = (f32[5,8,128]{2,1,0:T(8,128)S(1)}, f32[5,8,128]{2,1,0:T(8,128)S(1)}, u32[]{:S(2)}, u32[]{:S(2)}) collective-permute-start(f32[5,8,128]{2,1,0:T(8,128)S(1)} %constant_dynamic-update-slice_fusion.column_ref.cell_ref), channel_id=1, source_target_pairs={{28,0},{8,4},{4,8},{16,12},{12,16},{24,20},{20,24},{0,28},{29,1},{... | collective-permute-start | bytes 61448 | tf_op jit(solution)/shard_map/ppermute | solution.py:33
  18.9 6.4 %collective-permute-start.5 = (bf16[3,128,256]{2,1,0:T(8,128)(2,1)S(1)}, bf16[3,128,256]{2,1,0:T(8,128)(2,1)S(1)}, u32[]{:S(2)}, u32[]{:S(2)}) collective-permute-start(bf16[3,128,256]{2,1,0:T(8,128)(2,1)S(1)} %get-tuple-element.97.column_ref), channel_id=1, source_target_pairs={{4,0},{0,4},{12,8},{8,12},{20,16},{16,20},{28,24},{24,28},{5,1},{1... | collective-permute-start | bytes 589832 | tf_op jit(solution)/shard_map/ppermute | solution.py:24
  19.0 8.5 %collective-permute-start.6 = (bf16[3,128,256]{2,1,0:T(8,128)(2,1)S(1)}, bf16[3,128,256]{2,1,0:T(8,128)(2,1)S(1)}, u32[]{:S(2)}, u32[]{:S(2)}) collective-permute-start(bf16[3,128,256]{2,1,0:T(8,128)(2,1)S(1)} %get-tuple-element.97.column_ref), channel_id=1, source_target_pairs={{28,0},{8,4},{4,8},{16,12},{12,16},{24,20},{20,24},{0,28},{29,1},{... | collective-permute-start | bytes 589832 | tf_op jit(solution)/shard_map/ppermute | solution.py:33
  27.5 6.3 %copy-start.2 = (s32[3,4096]{1,0:T(4,128)S(1)}, s32[3,4096]{1,0:T(4,128)}, u32[]{:S(2)}) copy-start(s32[3,4096]{1,0:T(4,128)} %vec_ref.1) | copy-start | bytes 147460
  29.4 6.0 %collective-permute-start.9 = (bf16[80,256]{1,0:T(8,128)(2,1)S(1)}, bf16[80,256]{1,0:T(8,128)(2,1)S(1)}, u32[]{:S(2)}, u32[]{:S(2)}) collective-permute-start(bf16[80,256]{1,0:T(8,128)(2,1)S(1)} %get-tuple-element.102), channel_id=1, source_target_pairs={{24,0},{28,4},{16,8},{20,12},{8,16},{12,20},{0,24},{4,28},{25,1},{... | collective-permute-start | bytes 122888 | tf_op jit(solution)/shard_map/ppermute | solution.py:24
  30.0 5.5 %collective-permute-start.8 = (bf16[80,256]{1,0:T(8,128)(2,1)S(1)}, bf16[80,256]{1,0:T(8,128)(2,1)S(1)}, u32[]{:S(2)}, u32[]{:S(2)}) collective-permute-start(bf16[80,256]{1,0:T(8,128)(2,1)S(1)} %get-tuple-element.102), channel_id=1, source_target_pairs={{16,0},{20,4},{24,8},{28,12},{0,16},{4,20},{8,24},{12,28},{17,1},{... | collective-permute-start | bytes 122888 | tf_op jit(solution)/shard_map/ppermute | solution.py:24
  30.0 6.4 %collective-permute-start.7 = (bf16[80,256]{1,0:T(8,128)(2,1)S(1)}, bf16[80,256]{1,0:T(8,128)(2,1)S(1)}, u32[]{:S(2)}, u32[]{:S(2)}) collective-permute-start(bf16[80,256]{1,0:T(8,128)(2,1)S(1)} %get-tuple-element.102), channel_id=1, source_target_pairs={{8,0},{12,4},{0,8},{4,12},{24,16},{28,20},{16,24},{20,28},{9,1},{1... | collective-permute-start | bytes 122888 | tf_op jit(solution)/shard_map/ppermute | solution.py:24
  36.4 1.5 %collective-permute-start.10 = (bf16[4,80,256]{2,1,0:T(8,128)(2,1)S(1)}, bf16[4,80,256]{2,1,0:T(8,128)(2,1)S(1)}, u32[]{:S(2)}, u32[]{:S(2)}) collective-permute-start(bf16[4,80,256]{2,1,0:T(8,128)(2,1)S(1)} %pad_maximum_fusion.blocks.refs_7_), channel_id=1, source_target_pairs={{4,0},{0,4},{12,8},{8,12},{20,16},{16,20},{28,24},{24,28},{5,1},{1... | collective-permute-start | bytes 491528 | tf_op jit(solution)/shard_map/ppermute | solution.py:24
  39.1 5.8 %collective-permute-start.11 = (bf16[320,128]{1,0:T(8,128)(2,1)S(1)}, bf16[320,128]{1,0:T(8,128)(2,1)S(1)}, u32[]{:S(2)}, u32[]{:S(2)}) collective-permute-start(bf16[320,128]{1,0:T(8,128)(2,1)S(1)} %get-tuple-element.106), channel_id=1, source_target_pairs={{1,0},{0,1},{3,2},{2,3},{5,4},{4,5},{7,6},{6,7},{9,8},{8,9},{11,10... | collective-permute-start | bytes 245768 | tf_op jit(solution)/shard_map/ppermute | solution.py:24
  40.0 5.0 %collective-permute-start.12 = (bf16[320,128]{1,0:T(8,128)(2,1)S(1)}, bf16[320,128]{1,0:T(8,128)(2,1)S(1)}, u32[]{:S(2)}, u32[]{:S(2)}) collective-permute-start(bf16[320,128]{1,0:T(8,128)(2,1)S(1)} %get-tuple-element.106), channel_id=1, source_target_pairs={{2,0},{3,1},{0,2},{1,3},{6,4},{7,5},{4,6},{5,7},{10,8},{11,9},{8,1... | collective-permute-start | bytes 245768 | tf_op jit(solution)/shard_map/ppermute | solution.py:24
  41.2 5.4 %collective-permute-start.13 = (bf16[320,128]{1,0:T(8,128)(2,1)S(1)}, bf16[320,128]{1,0:T(8,128)(2,1)S(1)}, u32[]{:S(2)}, u32[]{:S(2)}) collective-permute-start(bf16[320,128]{1,0:T(8,128)(2,1)S(1)} %get-tuple-element.106), channel_id=1, source_target_pairs={{3,0},{2,1},{1,2},{0,3},{7,4},{6,5},{5,6},{4,7},{11,8},{10,9},{9,1... | collective-permute-start | bytes 245768 | tf_op jit(solution)/shard_map/ppermute | solution.py:24
  47.9 1.5 %collective-permute-start.14 = (bf16[4,80,256]{2,1,0:T(8,128)(2,1)S(1)}, bf16[4,80,256]{2,1,0:T(8,128)(2,1)S(1)}, u32[]{:S(2)}, u32[]{:S(2)}) collective-permute-start(bf16[4,80,256]{2,1,0:T(8,128)(2,1)S(1)} %get-tuple-element.137), channel_id=1, source_target_pairs={{4,0},{0,4},{12,8},{8,12},{20,16},{16,20},{28,24},{24,28},{5,1},{1... | collective-permute-start | bytes 491528 | tf_op jit(solution)/shard_map/ppermute | solution.py:24
  49.4 5.0 %collective-permute-start.15 = (bf16[80,256]{1,0:T(8,128)(2,1)S(1)}, bf16[80,256]{1,0:T(8,128)(2,1)S(1)}, u32[]{:S(2)}, u32[]{:S(2)}) collective-permute-start(bf16[80,256]{1,0:T(8,128)(2,1)S(1)} %get-tuple-element.139), channel_id=1, source_target_pairs={{8,0},{12,4},{0,8},{4,12},{24,16},{28,20},{16,24},{20,28},{9,1},{1... | collective-permute-start | bytes 122888 | tf_op jit(solution)/shard_map/ppermute | solution.py:24
  50.9 6.2 %collective-permute-start.16 = (bf16[80,256]{1,0:T(8,128)(2,1)S(1)}, bf16[80,256]{1,0:T(8,128)(2,1)S(1)}, u32[]{:S(2)}, u32[]{:S(2)}) collective-permute-start(bf16[80,256]{1,0:T(8,128)(2,1)S(1)} %get-tuple-element.140), channel_id=1, source_target_pairs={{16,0},{20,4},{24,8},{28,12},{0,16},{4,20},{8,24},{12,28},{17,1},{... | collective-permute-start | bytes 122888 | tf_op jit(solution)/shard_map/ppermute | solution.py:24
  52.1 5.9 %collective-permute-start.17 = (bf16[80,256]{1,0:T(8,128)(2,1)S(1)}, bf16[80,256]{1,0:T(8,128)(2,1)S(1)}, u32[]{:S(2)}, u32[]{:S(2)}) collective-permute-start(bf16[80,256]{1,0:T(8,128)(2,1)S(1)} %get-tuple-element.141), channel_id=1, source_target_pairs={{24,0},{28,4},{16,8},{20,12},{8,16},{12,20},{0,24},{4,28},{25,1},{... | collective-permute-start | bytes 122888 | tf_op jit(solution)/shard_map/ppermute | solution.py:24
  60.8 5.2 %collective-permute-start.18 = (bf16[3,128,256]{2,1,0:T(8,128)(2,1)S(1)}, bf16[3,128,256]{2,1,0:T(8,128)(2,1)S(1)}, u32[]{:S(2)}, u32[]{:S(2)}) collective-permute-start(bf16[3,128,256]{2,1,0:T(8,128)(2,1)S(1)} %get-tuple-element.146), channel_id=1, source_target_pairs={{4,0},{0,4},{12,8},{8,12},{20,16},{16,20},{28,24},{24,28},{5,1},{1... | collective-permute-start | bytes 589832 | tf_op jit(solution)/shard_map/ppermute | solution.py:24
  60.8 7.6 %collective-permute-start.19 = (bf16[3,128,256]{2,1,0:T(8,128)(2,1)S(1)}, bf16[3,128,256]{2,1,0:T(8,128)(2,1)S(1)}, u32[]{:S(2)}, u32[]{:S(2)}) collective-permute-start(bf16[3,128,256]{2,1,0:T(8,128)(2,1)S(1)} %get-tuple-element.147), channel_id=1, source_target_pairs={{28,0},{8,4},{4,8},{16,12},{12,16},{24,20},{20,24},{0,28},{29,1},{... | collective-permute-start | bytes 589832 | tf_op jit(solution)/shard_map/ppermute | solution.py:33
  72.0 5.0 %collective-permute-start.21 = (f32[16,256]{1,0:T(8,128)S(1)}, f32[16,256]{1,0:T(8,128)S(1)}, u32[]{:S(2)}, u32[]{:S(2)}) collective-permute-start(f32[16,256]{1,0:T(8,128)S(1)} %get-tuple-element.150), channel_id=1, source_target_pairs={{28,0},{8,4},{4,8},{16,12},{12,16},{24,20},{20,24},{0,28},{29,1},{... | collective-permute-start | bytes 49160 | tf_op jit(solution)/shard_map/ppermute | solution.py:33
  73.5 3.6 %collective-permute-start.20 = (f32[16,256]{1,0:T(8,128)S(1)}, f32[16,256]{1,0:T(8,128)S(1)}, u32[]{:S(2)}, u32[]{:S(2)}) collective-permute-start(f32[16,256]{1,0:T(8,128)S(1)} %get-tuple-element.149), channel_id=1, source_target_pairs={{4,0},{0,4},{12,8},{8,12},{20,16},{16,20},{28,24},{24,28},{5,1},{1... | collective-permute-start | bytes 49160 | tf_op jit(solution)/shard_map/ppermute | solution.py:24
  77.1 3.7 %collective-permute-start.24 = (f32[3,256]{1,0:T(4,128)S(1)}, f32[3,256]{1,0:T(4,128)S(1)}, u32[]{:S(2)}, u32[]{:S(2)}) collective-permute-start(f32[3,256]{1,0:T(4,128)S(1)} %get-tuple-element.155), channel_id=1, source_target_pairs={{2,0},{3,1},{0,2},{1,3},{6,4},{7,5},{4,6},{5,7},{10,8},{11,9},{8,1... | collective-permute-start | bytes 9224 | tf_op jit(solution)/shard_map/ppermute | solution.py:42
  78.0 4.5 %collective-permute-start.23 = (f32[3,256]{1,0:T(4,128)S(1)}, f32[3,256]{1,0:T(4,128)S(1)}, u32[]{:S(2)}, u32[]{:S(2)}) collective-permute-start(f32[3,256]{1,0:T(4,128)S(1)} %get-tuple-element.156), channel_id=1, source_target_pairs={{3,0},{2,1},{1,2},{0,3},{7,4},{6,5},{5,6},{4,7},{11,8},{10,9},{9,1... | collective-permute-start | bytes 9224 | tf_op jit(solution)/shard_map/ppermute | solution.py:33
  80.1 3.6 %collective-permute-start.22 = (f32[3,256]{1,0:T(4,128)S(1)}, f32[3,256]{1,0:T(4,128)S(1)}, u32[]{:S(2)}, u32[]{:S(2)}) collective-permute-start(f32[3,256]{1,0:T(4,128)S(1)} %get-tuple-element.154), channel_id=1, source_target_pairs={{1,0},{0,1},{3,2},{2,3},{5,4},{4,5},{7,6},{6,7},{9,8},{8,9},{11,10... | collective-permute-start | bytes 9224 | tf_op jit(solution)/shard_map/ppermute | solution.py:24

commit v17 on v16

--- a/solution.py
+++ b/solution.py
@@ -889,7 +889,7 @@
         hbm=3,
         name="prep_second",
     )
-    cells, hidden_high = lax.optimization_barrier((cells, hidden_high))
+    cells[2], hidden_high = lax.optimization_barrier((cells[2], hidden_high))
     low, ids, basis, slope, unit, sums_one, gate_one = run(
         functools.partial(first_kernel, slots),
         [

time: 84.5 us -> 84.1 us (level)
  starting transfers between devices: 32 us -> 27.8 us
  waiting for transfers between devices: 21.8 us -> 25.5 us
    ppermute x6, starting transfers between devices: 14.2 us -> 10.1 us  [beyond(): lax.ppermute(block, axis, [(other_side(i, count), i) for i in range(count)])]
    ppermute x6, waiting for transfers between devices: 10 us -> 13.9 us  [beyond(): lax.ppermute(block, axis, [(other_side(i, count), i) for i in range(count)])]
where the time goes in v17:
time: 84.1 us; the launch traced here: 83.9 us
  starting transfers between devices  27.8 us (33%)
  Pallas kernels  27.4 us (33%)
  waiting for transfers between devices  25.5 us (30%)
  local copies, waits for them, and re-layouts  2.07 us (2%)
  between operations  0.97 us (1%)
    pallas_call x22, Pallas kernels, run(): pl.pallas_call(kernel, out_shape=outs, in_specs=specs, out_specs=[whole()...  27.4 us
    ppermute x6, waiting for transfers between devices, beyond(): lax.ppermute(block, axis, [(other_side(i, count), i) for i in range(count)])  13.9 us
    ppermute x17, starting transfers between devices, paired(): lax.ppermute(block, axis, [(i ^ mask, i) for i in range(lax.axis_size(axi...  13.7 us
    ppermute x17, waiting for transfers between devices, paired(): lax.ppermute(block, axis, [(i ^ mask, i) for i in range(lax.axis_size(axi...  11.5 us
    ppermute x6, starting transfers between devices, beyond(): lax.ppermute(block, axis, [(other_side(i, count), i) for i in range(count)])  10.1 us
    ppermute x2, starting transfers between devices, far(): return lax.ppermute(block, axis, route)  3.93 us
    unnamed x27, local copies, waits for them, and re-layouts  2 us
  transfers between devices with their start and end apart: 25, of which 15 were waited for; matrix products, arithmetic and copies ran while one was open for 0% of the time, Pallas kernels for 16%

profile of v17, /device:TPU:0, one launch (start us, length us, event | category | flops | bytes accessed | tf_op | source)
XLA Modules:
  0.0 83.9 jit_solution(3247206389551860958)
XLA Ops:
  0.6 0.1 pad_add_fusion
  0.7 0.1 broadcast_in_dim.4.place_ref
  0.8 0.7 copy-done.9
  1.5 0.7 copy-done.10
  2.2 0.0 copy-start.6
  2.2 3.0 %collective-permute-start.2 = (f32[8,128]{1,0:T(8,128)S(1)}, f32[8,128]{1,0:T(8,128)S(1)}, u32[]{:S(2)}, u32[]{:S(2)}) collective-permute-start(f32[8,128]{1,0:T(8,128)S(1)} %pack.1.first_ref), channel_id=1, source_target_pairs={{2,0},{3,1},{0,2},{1,3},{6,4},{7,5},{4,6},{5,7},{10,8},{11,9},{8,1... | collective-permute-start | bytes 12296 | tf_op jit(solution)/shard_map/ppermute | solution.py:42
  5.3 0.1 pack_more.1.own_ref
  5.4 1.6 %collective-permute-start = (f32[40,128]{1,0:T(8,128)S(1)}, f32[40,128]{1,0:T(8,128)S(1)}, u32[]{:S(2)}, u32[]{:S(2)}) collective-permute-start(f32[40,128]{1,0:T(8,128)S(1)} %pack_more.1.own_ref), channel_id=1, source_target_pairs={{3,0},{2,1},{1,2},{0,3},{7,4},{6,5},{5,6},{4,7},{11,8},{10,9},{9,1... | collective-permute-start | bytes 61448 | tf_op jit(solution)/shard_map/ppermute | solution.py:33
  6.9 0.5 collective-permute-start.1
  7.5 3.2 %collective-permute-done.1.y_pair_ref = f32[40,128]{1,0:T(8,128)S(1)} collective-permute-done((f32[40,128]{1,0:T(8,128)S(1)}, f32[40,128]{1,0:T(8,128)S(1)}, u32[]{:S(2)}, u32[]{:S(2)}) %collective-permute-start.1) | collective-permute-done | bytes 20512 | tf_op jit(solution)/shard_map/ppermute | solution.py:24
  10.7 1.8 %collective-permute-start.3 = (f32[5,8,128]{2,1,0:T(8,128)S(1)}, f32[5,8,128]{2,1,0:T(8,128)S(1)}, u32[]{:S(2)}, u32[]{:S(2)}) collective-permute-start(f32[5,8,128]{2,1,0:T(8,128)S(1)} %constant_dynamic-update-slice_fusion.column_ref.cell_ref), channel_id=1, source_target_pairs={{28,0},{8,4},{4,8},{16,12},{12,16},{24,20},{20,24},{0,28},{29,1},{... | collective-permute-start | bytes 61448 | tf_op jit(solution)/shard_map/ppermute | solution.py:33
  12.6 0.3 prep_first.1
  12.9 0.3 prep_second.1
  13.2 2.6 %collective-permute-done.3.beyond_ref = f32[5,8,128]{2,1,0:T(8,128)S(1)} collective-permute-done((f32[5,8,128]{2,1,0:T(8,128)S(1)}, f32[5,8,128]{2,1,0:T(8,128)S(1)}, u32[]{:S(2)}, u32[]{:S(2)}) %collective-permute-start.3) | collective-permute-done | bytes 20512 | tf_op jit(solution)/shard_map/ppermute | solution.py:33
  15.8 2.9 %first.1 = (bf16[3,128,256]{2,1,0:T(8,128)(2,1)S(1)}, s32[3,3072]{1,0:T(4,128)S(1)}, f32[3,8,3072]{2,1,0:T(8,128)S(1)}, f32[3,8,3072]{2,1,0:T(8,128)S(1)}, f32[3...) custom-call(s32[2,8,128]{2,1,0:T(8,128)S(1)} %broadcast_in_dim.4.place_ref, ...), custom_call_target="tpu_custom_call" | custom-call | flops 10000000 | bytes 1000000 | tf_op jit(solution)/shard_map/first/pallas_call | solution.py:55
  18.7 0.1 collective-permute-start.5
  18.8 1.9 %collective-permute-start.6 = (bf16[3,128,256]{2,1,0:T(8,128)(2,1)S(1)}, bf16[3,128,256]{2,1,0:T(8,128)(2,1)S(1)}, u32[]{:S(2)}, u32[]{:S(2)}) collective-permute-start(bf16[3,128,256]{2,1,0:T(8,128)(2,1)S(1)} %get-tuple-element.93.column_ref), channel_id=1, source_target_pairs={{28,0},{8,4},{4,8},{16,12},{12,16},{24,20},{20,24},{0,28},{29,1},{... | collective-permute-start | bytes 589832 | tf_op jit(solution)/shard_map/ppermute | solution.py:33
  20.7 1.7 %second_near.1 = (f32[4,128,3072]{2,1,0:T(8,128)S(1)}, f32[128,3072]{1,0:T(8,128)S(1)}) custom-call(s32[3,3072]{1,0:T(4,128)S(1)} %get-tuple-element.81.ids_ref, f32[3,8,3072]{2,1,0:T(8,128)S(1)} %get-tuple-element.82.basis_ref, f32[3,8,3072]{2,1,0:T(8,128)S(1)} %get-tuple-element.84.unit_ref, bf16[2,128,32]{2,1,0:T(8,128)(2,1)S(1)} %get-tuple-element.92.left_ref, ...), custom_call_target="tpu_custom_call" | custom-call | flops 2000000000 | bytes 1000000 | tf_op jit(solution)/shard_map/second_near/pallas_call | solution.py:55
  22.5 1.0 %hot_beyond.1.hot_ref = bf16[768,3072]{1,0:T(8,128)(2,1)S(1)} custom-call(s32[3,3072]{1,0:T(4,128)S(1)} %get-tuple-element.81.ids_ref, f32[128,3072]{1,0:T(8,128)S(1)} %get-tuple-element.94.near_ref), custom_call_target="tpu_custom_call" | custom-call | flops 1000000 | bytes 1000000 | tf_op jit(solution)/shard_map/hot_beyond/pallas_call | solution.py:55
  23.4 0.8 second_side.1.near_ref
  24.3 2.7 %collective-permute-done.6.beyond_ref = bf16[3,128,256]{2,1,0:T(8,128)(2,1)S(1)} collective-permute-done((bf16[3,128,256]{2,1,0:T(8,128)(2,1)S(1)}, bf16[3,128,256]{2,1,0:T(8,128)(2,1)S(1)}, u32[]{:S(2)}, u32[]{:S(2)}) %collective-permute-start.6) | collective-permute-done | bytes 196640 | tf_op jit(solution)/shard_map/ppermute | solution.py:33
  26.9 1.9 %second.1 = (bf16[128,3072]{1,0:T(8,128)(2,1)S(1)}, f32[3,128,256]{2,1,0:T(8,128)S(1)}, f32[128,256]{1,0:T(8,128)S(1)}, bf16[80,256]{1,0:T(8,128)(2,1)S(1)}, f32...) custom-call(bf16[768,3072]{1,0:T(8,128)(2,1)S(1)} %hot_beyond.1.hot_ref, f32[4,128,3072]{2,1,0:T(8,128)S(1)} %get-tuple-element.95.weight_ref, ...), custom_call_target="tpu_custom_call" | custom-call | flops 10000000 | bytes 1000000 | tf_op jit(solution)/shard_map/second/pallas_call | solution.py:55
  28.8 0.1 collective-permute-start.9
  28.9 0.1 collective-permute-start.8
  28.9 4.3 %collective-permute-start.7 = (bf16[80,256]{1,0:T(8,128)(2,1)S(1)}, bf16[80,256]{1,0:T(8,128)(2,1)S(1)}, u32[]{:S(2)}, u32[]{:S(2)}) collective-permute-start(bf16[80,256]{1,0:T(8,128)(2,1)S(1)} %get-tuple-element.98), channel_id=1, source_target_pairs={{8,0},{12,4},{0,8},{4,12},{24,16},{28,20},{16,24},{20,28},{9,1},{1... | collective-permute-start | bytes 122888 | tf_op jit(solution)/shard_map/ppermute | solution.py:24
  33.2 0.8 green.1.refs_0_
  34.1 0.9 %collective-permute-done.9 = bf16[80,256]{1,0:T(8,128)(2,1)S(1)} collective-permute-done((bf16[80,256]{1,0:T(8,128)(2,1)S(1)}, bf16[80,256]{1,0:T(8,128)(2,1)S(1)}, u32[]{:S(2)}, u32[]{:S(2)}) %collective-permute-start.9) | collective-permute-done | bytes 40992 | tf_op jit(solution)/shard_map/ppermute | solution.py:24
  35.0 0.3 collective-permute-done.7
  35.3 0.1 collective-permute-start.10
  35.4 1.2 %structure_near.1 = (f32[32,1024]{1,0:T(8,128)S(1)}, f32[32,1024]{1,0:T(8,128)S(1)}, f32[8,1024]{1,0:T(8,128)S(1)}, f32[8,1024]{1,0:T(8,128)S(1)}, bf16[640,1024...) custom-call(s32[2,8,128]{2,1,0:T(8,128)S(1)} %broadcast_in_dim.4.place_ref, ...), custom_call_target="tpu_custom_call" | custom-call | flops 1000000000 | bytes 1000000 | tf_op jit(solution)/shard_map/structure_near/pallas_call | solution.py:55
  36.6 0.2 collective-permute-done.10.blocks.refs_11_
  36.8 1.3 %structure_far.1 = (f32[32,1024]{1,0:T(8,128)S(1)}, f32[32,1024]{1,0:T(8,128)S(1)}, f32[8,1024]{1,0:T(8,128)S(1)}, f32[8,1024]{1,0:T(8,128)S(1)}, bf16[640,1024]...) custom-call(s32[2,8,128]{2,1,0:T(8,128)S(1)} %broadcast_in_dim.4.place_r, ...), custom_call_target="tpu_custom_call" | custom-call | flops 10000000 | bytes 1000000 | tf_op jit(solution)/shard_map/structure_far/pallas_call | solution.py:55
  38.1 0.9 %collective-permute-start.11 = (bf16[320,128]{1,0:T(8,128)(2,1)S(1)}, bf16[320,128]{1,0:T(8,128)(2,1)S(1)}, u32[]{:S(2)}, u32[]{:S(2)}) collective-permute-start(bf16[320,128]{1,0:T(8,128)(2,1)S(1)} %get-tuple-element.102), channel_id=1, source_target_pairs={{1,0},{0,1},{3,2},{2,3},{5,4},{4,5},{7,6},{6,7},{9,8},{8,9},{11,10... | collective-permute-start | bytes 245768 | tf_op jit(solution)/shard_map/ppermute | solution.py:24
  38.9 1.1 %collective-permute-start.12 = (bf16[320,128]{1,0:T(8,128)(2,1)S(1)}, bf16[320,128]{1,0:T(8,128)(2,1)S(1)}, u32[]{:S(2)}, u32[]{:S(2)}) collective-permute-start(bf16[320,128]{1,0:T(8,128)(2,1)S(1)} %get-tuple-element.102), channel_id=1, source_target_pairs={{2,0},{3,1},{0,2},{1,3},{6,4},{7,5},{4,6},{5,7},{10,8},{11,9},{8,1... | collective-permute-start | bytes 245768 | tf_op jit(solution)/shard_map/ppermute | solution.py:24
  40.0 1.6 %collective-permute-start.13 = (bf16[320,128]{1,0:T(8,128)(2,1)S(1)}, bf16[320,128]{1,0:T(8,128)(2,1)S(1)}, u32[]{:S(2)}, u32[]{:S(2)}) collective-permute-start(bf16[320,128]{1,0:T(8,128)(2,1)S(1)} %get-tuple-element.102), channel_id=1, source_target_pairs={{3,0},{2,1},{1,2},{0,3},{7,4},{6,5},{5,6},{4,7},{11,8},{10,9},{9,1... | collective-permute-start | bytes 245768 | tf_op jit(solution)/shard_map/ppermute | solution.py:24
  41.6 2.3 %hot_back.1.hot_ref = bf16[3072,1536]{1,0:T(8,128)(2,1)S(1)} custom-call(s32[3,3072]{1,0:T(4,128)S(1)} %get-tuple-element.81.ids_ref), custom_call_target="tpu_custom_call" | custom-call | flops 2000000000 | bytes 1000000 | tf_op jit(solution)/shard_map/hot_back/pallas_call | solution.py:55
  43.9 1.6 %collective-permute-done.13.refs_4_ = bf16[320,128]{1,0:T(8,128)(2,1)S(1)} collective-permute-done((bf16[320,128]{1,0:T(8,128)(2,1)S(1)}, bf16[320,128]{1,0:T(8,128)(2,1)S(1)}, u32[]{:S(2)}, u32[]{:S(2)}) %collective-permute-start.13) | collective-permute-done | bytes 81952 | tf_op jit(solution)/shard_map/ppermute | solution.py:24
  45.5 1.3 %fold_far.1 = (bf16[4,80,256]{2,1,0:T(8,128)(2,1)S(1)}, f32[640,64]{1,0:T(8,128)S(1)}) custom-call(s32[2,8,128]{2,1,0:T(8,128)S(1)} %broadcast_in_dim.4.place_ref, f32[320,128]{1,0:T(8,128)S(1)} %green.1.refs_0_, f32[320,128]{1,0:T(8,128)S(1)} %get-tuple-element.116.refs_1_, bf16[320,128]{1,0:T(8,128)(2,1)S(1)} %collective-permute-done.11.refs_2_, ...), custom_call_target="tpu_custom_call" | custom-call | flops 10000000 | bytes 1000000 | tf_op jit(solution)/shard_map/fold_far/pallas_call | solution.py:55
  46.8 0.1 collective-permute-start.14
  46.9 1.2 %fold_near.1.near_ref = f32[4,80,256]{2,1,0:T(8,128)S(1)} custom-call(s32[2,8,128]{2,1,0:T(8,128)S(1)} %broadcast_in_dim.4.place_ref, f32[640,64]{1,0:T(8,128)S(1)} %get-tuple-element.126.refs_0_, f32[32,1024]{1,0:T(8,128)S(1)} %get-tuple-element.127.refs_1_, f32[32,1024]{1,0:T(8,128)S(1)} %get-tuple-element.128.refs_2_, ...), custom_call_target="tpu_custom_call" | custom-call | flops 1000000000 | bytes 1000000 | tf_op jit(solution)/shard_map/fold_near/pallas_call | solution.py:55
  48.1 0.2 collective-permute-done.14.far_ref
  48.3 0.1 fold_join.1
  48.3 2.0 %collective-permute-start.15 = (bf16[80,256]{1,0:T(8,128)(2,1)S(1)}, bf16[80,256]{1,0:T(8,128)(2,1)S(1)}, u32[]{:S(2)}, u32[]{:S(2)}) collective-permute-start(bf16[80,256]{1,0:T(8,128)(2,1)S(1)} %get-tuple-element.135), channel_id=1, source_target_pairs={{8,0},{12,4},{0,8},{4,12},{24,16},{28,20},{16,24},{20,28},{9,1},{1... | collective-permute-start | bytes 122888 | tf_op jit(solution)/shard_map/ppermute | solution.py:24
  50.3 0.9 %collective-permute-start.16 = (bf16[80,256]{1,0:T(8,128)(2,1)S(1)}, bf16[80,256]{1,0:T(8,128)(2,1)S(1)}, u32[]{:S(2)}, u32[]{:S(2)}) collective-permute-start(bf16[80,256]{1,0:T(8,128)(2,1)S(1)} %get-tuple-element.136), channel_id=1, source_target_pairs={{16,0},{20,4},{24,8},{28,12},{0,16},{4,20},{8,24},{12,28},{17,1},{... | collective-permute-start | bytes 122888 | tf_op jit(solution)/shard_map/ppermute | solution.py:24
  51.2 1.5 %collective-permute-start.17 = (bf16[80,256]{1,0:T(8,128)(2,1)S(1)}, bf16[80,256]{1,0:T(8,128)(2,1)S(1)}, u32[]{:S(2)}, u32[]{:S(2)}) collective-permute-start(bf16[80,256]{1,0:T(8,128)(2,1)S(1)} %get-tuple-element.137), channel_id=1, source_target_pairs={{24,0},{28,4},{16,8},{20,12},{8,16},{12,20},{0,24},{4,28},{25,1},{... | collective-permute-start | bytes 122888 | tf_op jit(solution)/shard_map/ppermute | solution.py:24
  52.8 0.5 readout.1
  53.3 2.8 %collective-permute-done.16.refs_2_ = bf16[80,256]{1,0:T(8,128)(2,1)S(1)} collective-permute-done((bf16[80,256]{1,0:T(8,128)(2,1)S(1)}, bf16[80,256]{1,0:T(8,128)(2,1)S(1)}, u32[]{:S(2)}, u32[]{:S(2)}) %collective-permute-start.16) | collective-permute-done | bytes 40992 | tf_op jit(solution)/shard_map/ppermute | solution.py:24
  56.1 1.0 %collective-permute-done.17.refs_3_ = bf16[80,256]{1,0:T(8,128)(2,1)S(1)} collective-permute-done((bf16[80,256]{1,0:T(8,128)(2,1)S(1)}, bf16[80,256]{1,0:T(8,128)(2,1)S(1)}, u32[]{:S(2)}, u32[]{:S(2)}) %collective-permute-start.17) | collective-permute-done | bytes 40992 | tf_op jit(solution)/shard_map/ppermute | solution.py:24
  57.2 2.8 %second_back.1 = (f32[1,1,256]{2,1,0:T(1,128)}, f32[8,256]{1,0:T(8,128)S(1)}, f32[128,256]{1,0:T(8,128)S(1)}, f32[4,128,256]{2,1,0:T(8,128)S(1)}, bf16[128,3072]...) custom-call(bf16[3072,1536]{1,0:T(8,128)(2,1)S(1)} %hot_back.1.hot_ref, ...), custom_call_target="tpu_custom_call" | custom-call | flops 10000000 | bytes 1000000 | tf_op jit(solution)/shard_map/second_back/pallas_call | solution.py:55
  60.0 1.7 %collective-permute-start.19 = (bf16[3,128,256]{2,1,0:T(8,128)(2,1)S(1)}, bf16[3,128,256]{2,1,0:T(8,128)(2,1)S(1)}, u32[]{:S(2)}, u32[]{:S(2)}) collective-permute-start(bf16[3,128,256]{2,1,0:T(8,128)(2,1)S(1)} %get-tuple-element.143), channel_id=1, source_target_pairs={{28,0},{8,4},{4,8},{16,12},{12,16},{24,20},{20,24},{0,28},{29,1},{... | collective-permute-start | bytes 589832 | tf_op jit(solution)/shard_map/ppermute | solution.py:33
  61.6 1.3 %hot_middle.1.hot_ref = bf16[3072,768]{1,0:T(8,128)(2,1)S(1)} custom-call(s32[3,3072]{1,0:T(4,128)S(1)} %get-tuple-element.81.ids_ref), custom_call_target="tpu_custom_call" | custom-call | flops 1000000000 | bytes 1000000 | tf_op jit(solution)/shard_map/hot_middle/pallas_call | solution.py:55
  63.0 1.2 %second_edge.1.edge_ref = f32[32,3072]{1,0:T(8,128)S(1)} custom-call(bf16[2,16,256]{2,1,0:T(8,128)(2,1)S(1)} %get-tuple-element.91.back_ref, bf16[128,3072]{1,0:T(8,128)(2,1)S(1)} %get-tuple-element.97.feature_ref, f32[4,128,256]{2,1,0:T(8,128)S(1)} %get-tuple-element.138.grad_ref), custom_call_target="tpu_custom_call" | custom-call | flops 1000000000 | bytes 1000000 | tf_op jit(solution)/shard_map/second_edge/pallas_call | solution.py:55
  64.2 0.8 second_middle.1.middle_ref
  65.0 3.0 %collective-permute-done.19.from_beyond = bf16[3,128,256]{2,1,0:T(8,128)(2,1)S(1)} collective-permute-done((bf16[3,128,256]{2,1,0:T(8,128)(2,1)S(1)}, bf16[3,128,256]{2,1,0:T(8,128)(2,1)S(1)}, u32[]{:S(2)}, u32[]{:S(2)}) %collective-permute-start.19) | collective-permute-done | bytes 196640 | tf_op jit(solution)/shard_map/ppermute | solution.py:33
  68.0 3.6 %first_back.1 = (f32[16,256]{1,0:T(8,128)S(1)}, f32[16,256]{1,0:T(8,128)S(1)}, f32[16,256]{1,0:T(8,128)S(1)}) custom-call(s32[3,3072]{1,0:T(4,128)S(1)} %get-tuple-element.81.ids_ref, f32[3,8,3072]{2,1,0:T(8,128)S(1)} %get-tuple-element.82.basis_ref, f32[3,8,3072]{2,1,0:T(8,128)S(1)} %get-tuple-element.83.slope_ref, ...), custom_call_target="tpu_custom_call" | custom-call | flops 10000000 | bytes 1000000 | tf_op jit(solution)/shard_map/first_back/pallas_call | solution.py:55
  71.6 1.1 %collective-permute-start.21 = (f32[16,256]{1,0:T(8,128)S(1)}, f32[16,256]{1,0:T(8,128)S(1)}, u32[]{:S(2)}, u32[]{:S(2)}) collective-permute-start(f32[16,256]{1,0:T(8,128)S(1)} %get-tuple-element.146), channel_id=1, source_target_pairs={{28,0},{8,4},{4,8},{16,12},{12,16},{24,20},{20,24},{0,28},{29,1},{... | collective-permute-start | bytes 49160 | tf_op jit(solution)/shard_map/ppermute | solution.py:33
  72.7 3.9 %collective-permute-done.21 = f32[16,256]{1,0:T(8,128)S(1)} collective-permute-done((f32[16,256]{1,0:T(8,128)S(1)}, f32[16,256]{1,0:T(8,128)S(1)}, u32[]{:S(2)}, u32[]{:S(2)}) %collective-permute-start.21) | collective-permute-done | bytes 16416 | tf_op jit(solution)/shard_map/ppermute | solution.py:33
  76.7 0.9 %collective-permute-start.24 = (f32[3,256]{1,0:T(4,128)S(1)}, f32[3,256]{1,0:T(4,128)S(1)}, u32[]{:S(2)}, u32[]{:S(2)}) collective-permute-start(f32[3,256]{1,0:T(4,128)S(1)} %get-tuple-element.151), channel_id=1, source_target_pairs={{2,0},{3,1},{0,2},{1,3},{6,4},{7,5},{4,6},{5,7},{10,8},{11,9},{8,1... | collective-permute-start | bytes 9224 | tf_op jit(solution)/shard_map/ppermute | solution.py:42
  77.6 2.1 %collective-permute-start.23 = (f32[3,256]{1,0:T(4,128)S(1)}, f32[3,256]{1,0:T(4,128)S(1)}, u32[]{:S(2)}, u32[]{:S(2)}) collective-permute-start(f32[3,256]{1,0:T(4,128)S(1)} %get-tuple-element.152), channel_id=1, source_target_pairs={{3,0},{2,1},{1,2},{0,3},{7,4},{6,5},{5,6},{4,7},{11,8},{10,9},{9,1... | collective-permute-start | bytes 9224 | tf_op jit(solution)/shard_map/ppermute | solution.py:33
  79.7 0.5 collective-permute-start.22
  80.2 0.1 collective-permute-done.24
  80.3 1.7 %collective-permute-done.23 = f32[3,256]{1,0:T(4,128)S(1)} collective-permute-done((f32[3,256]{1,0:T(4,128)S(1)}, f32[3,256]{1,0:T(4,128)S(1)}, u32[]{:S(2)}, u32[]{:S(2)}) %collective-permute-start.23) | collective-permute-done | bytes 3104 | tf_op jit(solution)/shard_map/ppermute | solution.py:33
  82.1 1.2 %collective-permute-done.22 = f32[3,256]{1,0:T(4,128)S(1)} collective-permute-done((f32[3,256]{1,0:T(4,128)S(1)}, f32[3,256]{1,0:T(4,128)S(1)}, u32[]{:S(2)}, u32[]{:S(2)}) %collective-permute-start.22) | collective-permute-done | bytes 3104 | tf_op jit(solution)/shard_map/ppermute | solution.py:24
  83.3 0.6 copy.13
  (42 shorter events, 0.1 us)
Async XLA Ops:
  0.8 0.7 copy-start.9
  1.5 0.7 copy-start.10
  2.1 3.1 %copy-start.5 = (s32[1,1,256,12]{2,1,3,0:T(1,128)S(1)}, s32[1,1,256,12]{2,1,3,0:T(1,128)}, u32[]{:S(2)}) copy-start(s32[1,1,256,12]{2,1,3,0:T(1,128)} %param.13) | copy-start | bytes 36868
  2.2 3.1 %copy-start.7 = (s32[1,1,256]{2,1,0:T(1,128)S(1)}, s32[1,1,256]{2,1,0:T(1,128)}, u32[]{:S(2)}) copy-start(s32[1,1,256]{2,1,0:T(1,128)} %count_ref.1) | copy-start | bytes 3076
  2.2 10.4 %copy-start = (f32[2,2,128,128]{3,2,1,0:T(8,128)S(1)}, f32[2,2,128,128]{3,2,1,0:T(8,128)}, u32[]{:S(2)}) copy-start(f32[2,2,128,128]{3,2,1,0:T(8,128)} %mixing_in.1) | copy-start | bytes 786436
  2.2 10.4 %copy-start.4 = (f32[2,2,8,128]{3,2,1,0:T(8,128)S(1)}, f32[2,2,8,128]{3,2,1,0:T(8,128)}, u32[]{:S(2)}) copy-start(f32[2,2,8,128]{3,2,1,0:T(8,128)} %radial_in.1) | copy-start | bytes 49156
  2.2 10.4 %copy-start.6 = (f32[6,128]{1,0:T(8,128)S(1)}, f32[6,128]{1,0:T(8,128)}, u32[]{:S(2)}) copy-start(f32[6,128]{1,0:T(8,128)} %embed_in.1) | copy-start | bytes 9220
  2.2 10.7 %copy-start.1 = (f32[128,128]{1,0:T(8,128)S(1)}, f32[128,128]{1,0:T(8,128)}, u32[]{:S(2)}) copy-start(f32[128,128]{1,0:T(8,128)} %hidden_in.1) | copy-start | bytes 196612
  2.2 10.7 %copy-start.3 = (f32[128,64]{0,1:T(8,128)S(1)}, f32[128,64]{0,1:T(8,128)}, u32[]{:S(2)}) copy-start(f32[128,64]{0,1:T(8,128)} %param.20) | copy-start | bytes 98308
  2.2 10.7 %copy-start.8 = (f32[128]{0:T(128)S(1)}, f32[128]{0:T(128)}, u32[]{:S(2)}) copy-start(f32[128]{0:T(128)} %param.19) | copy-start | bytes 1540
  2.2 5.3 %collective-permute-start.2 = (f32[8,128]{1,0:T(8,128)S(1)}, f32[8,128]{1,0:T(8,128)S(1)}, u32[]{:S(2)}, u32[]{:S(2)}) collective-permute-start(f32[8,128]{1,0:T(8,128)S(1)} %pack.1.first_ref), channel_id=1, source_target_pairs={{2,0},{3,1},{0,2},{1,3},{6,4},{7,5},{4,6},{5,7},{10,8},{11,9},{8,1... | collective-permute-start | bytes 12296 | tf_op jit(solution)/shard_map/ppermute | solution.py:42
  5.4 5.3 %collective-permute-start = (f32[40,128]{1,0:T(8,128)S(1)}, f32[40,128]{1,0:T(8,128)S(1)}, u32[]{:S(2)}, u32[]{:S(2)}) collective-permute-start(f32[40,128]{1,0:T(8,128)S(1)} %pack_more.1.own_ref), channel_id=1, source_target_pairs={{3,0},{2,1},{1,2},{0,3},{7,4},{6,5},{5,6},{4,7},{11,8},{10,9},{9,1... | collective-permute-start | bytes 61448 | tf_op jit(solution)/shard_map/ppermute | solution.py:33
  6.9 3.8 %collective-permute-start.1 = (f32[40,128]{1,0:T(8,128)S(1)}, f32[40,128]{1,0:T(8,128)S(1)}, u32[]{:S(2)}, u32[]{:S(2)}) collective-permute-start(f32[40,128]{1,0:T(8,128)S(1)} %pack_more.1.own_ref), channel_id=1, source_target_pairs={{1,0},{0,1},{3,2},{2,3},{5,4},{4,5},{7,6},{6,7},{9,8},{8,9},{11,10... | collective-permute-start | bytes 61448 | tf_op jit(solution)/shard_map/ppermute | solution.py:24
  10.7 5.1 %collective-permute-start.3 = (f32[5,8,128]{2,1,0:T(8,128)S(1)}, f32[5,8,128]{2,1,0:T(8,128)S(1)}, u32[]{:S(2)}, u32[]{:S(2)}) collective-permute-start(f32[5,8,128]{2,1,0:T(8,128)S(1)} %constant_dynamic-update-slice_fusion.column_ref.cell_ref), channel_id=1, source_target_pairs={{28,0},{8,4},{4,8},{16,12},{12,16},{24,20},{20,24},{0,28},{29,1},{... | collective-permute-start | bytes 61448 | tf_op jit(solution)/shard_map/ppermute | solution.py:33
  12.6 3.3 %collective-permute-start.4 = (f32[5,8,128]{2,1,0:T(8,128)S(1)}, f32[5,8,128]{2,1,0:T(8,128)S(1)}, u32[]{:S(2)}, u32[]{:S(2)}) collective-permute-start(f32[5,8,128]{2,1,0:T(8,128)S(1)} %constant_dynamic-update-slice_fusion.column_ref.cell_ref), channel_id=1, source_target_pairs={{4,0},{0,4},{12,8},{8,12},{20,16},{16,20},{28,24},{24,28},{5,1},{1... | collective-permute-start | bytes 61448 | tf_op jit(solution)/shard_map/ppermute | solution.py:24
  18.7 4.7 %collective-permute-start.5 = (bf16[3,128,256]{2,1,0:T(8,128)(2,1)S(1)}, bf16[3,128,256]{2,1,0:T(8,128)(2,1)S(1)}, u32[]{:S(2)}, u32[]{:S(2)}) collective-permute-start(bf16[3,128,256]{2,1,0:T(8,128)(2,1)S(1)} %get-tuple-element.93.column_ref), channel_id=1, source_target_pairs={{4,0},{0,4},{12,8},{8,12},{20,16},{16,20},{28,24},{24,28},{5,1},{1... | collective-permute-start | bytes 589832 | tf_op jit(solution)/shard_map/ppermute | solution.py:24
  18.8 8.1 %collective-permute-start.6 = (bf16[3,128,256]{2,1,0:T(8,128)(2,1)S(1)}, bf16[3,128,256]{2,1,0:T(8,128)(2,1)S(1)}, u32[]{:S(2)}, u32[]{:S(2)}) collective-permute-start(bf16[3,128,256]{2,1,0:T(8,128)(2,1)S(1)} %get-tuple-element.93.column_ref), channel_id=1, source_target_pairs={{28,0},{8,4},{4,8},{16,12},{12,16},{24,20},{20,24},{0,28},{29,1},{... | collective-permute-start | bytes 589832 | tf_op jit(solution)/shard_map/ppermute | solution.py:33
  26.9 6.3 %copy-start.2 = (s32[3,4096]{1,0:T(4,128)S(1)}, s32[3,4096]{1,0:T(4,128)}, u32[]{:S(2)}) copy-start(s32[3,4096]{1,0:T(4,128)} %vec_ref.1) | copy-start | bytes 147460
  28.8 6.2 %collective-permute-start.9 = (bf16[80,256]{1,0:T(8,128)(2,1)S(1)}, bf16[80,256]{1,0:T(8,128)(2,1)S(1)}, u32[]{:S(2)}, u32[]{:S(2)}) collective-permute-start(bf16[80,256]{1,0:T(8,128)(2,1)S(1)} %get-tuple-element.98), channel_id=1, source_target_pairs={{24,0},{28,4},{16,8},{20,12},{8,16},{12,20},{0,24},{4,28},{25,1},{... | collective-permute-start | bytes 122888 | tf_op jit(solution)/shard_map/ppermute | solution.py:24
  28.9 6.1 %collective-permute-start.8 = (bf16[80,256]{1,0:T(8,128)(2,1)S(1)}, bf16[80,256]{1,0:T(8,128)(2,1)S(1)}, u32[]{:S(2)}, u32[]{:S(2)}) collective-permute-start(bf16[80,256]{1,0:T(8,128)(2,1)S(1)} %get-tuple-element.98), channel_id=1, source_target_pairs={{16,0},{20,4},{24,8},{28,12},{0,16},{4,20},{8,24},{12,28},{17,1},{... | collective-permute-start | bytes 122888 | tf_op jit(solution)/shard_map/ppermute | solution.py:24
  28.9 6.4 %collective-permute-start.7 = (bf16[80,256]{1,0:T(8,128)(2,1)S(1)}, bf16[80,256]{1,0:T(8,128)(2,1)S(1)}, u32[]{:S(2)}, u32[]{:S(2)}) collective-permute-start(bf16[80,256]{1,0:T(8,128)(2,1)S(1)} %get-tuple-element.98), channel_id=1, source_target_pairs={{8,0},{12,4},{0,8},{4,12},{24,16},{28,20},{16,24},{20,28},{9,1},{1... | collective-permute-start | bytes 122888 | tf_op jit(solution)/shard_map/ppermute | solution.py:24
  35.3 1.5 %collective-permute-start.10 = (bf16[4,80,256]{2,1,0:T(8,128)(2,1)S(1)}, bf16[4,80,256]{2,1,0:T(8,128)(2,1)S(1)}, u32[]{:S(2)}, u32[]{:S(2)}) collective-permute-start(bf16[4,80,256]{2,1,0:T(8,128)(2,1)S(1)} %pad_maximum_fusion.blocks.refs_7_), channel_id=1, source_target_pairs={{4,0},{0,4},{12,8},{8,12},{20,16},{16,20},{28,24},{24,28},{5,1},{1... | collective-permute-start | bytes 491528 | tf_op jit(solution)/shard_map/ppermute | solution.py:24
  38.1 5.8 %collective-permute-start.11 = (bf16[320,128]{1,0:T(8,128)(2,1)S(1)}, bf16[320,128]{1,0:T(8,128)(2,1)S(1)}, u32[]{:S(2)}, u32[]{:S(2)}) collective-permute-start(bf16[320,128]{1,0:T(8,128)(2,1)S(1)} %get-tuple-element.102), channel_id=1, source_target_pairs={{1,0},{0,1},{3,2},{2,3},{5,4},{4,5},{7,6},{6,7},{9,8},{8,9},{11,10... | collective-permute-start | bytes 245768 | tf_op jit(solution)/shard_map/ppermute | solution.py:24
  38.9 5.0 %collective-permute-start.12 = (bf16[320,128]{1,0:T(8,128)(2,1)S(1)}, bf16[320,128]{1,0:T(8,128)(2,1)S(1)}, u32[]{:S(2)}, u32[]{:S(2)}) collective-permute-start(bf16[320,128]{1,0:T(8,128)(2,1)S(1)} %get-tuple-element.102), channel_id=1, source_target_pairs={{2,0},{3,1},{0,2},{1,3},{6,4},{7,5},{4,6},{5,7},{10,8},{11,9},{8,1... | collective-permute-start | bytes 245768 | tf_op jit(solution)/shard_map/ppermute | solution.py:24
  40.0 5.4 %collective-permute-start.13 = (bf16[320,128]{1,0:T(8,128)(2,1)S(1)}, bf16[320,128]{1,0:T(8,128)(2,1)S(1)}, u32[]{:S(2)}, u32[]{:S(2)}) collective-permute-start(bf16[320,128]{1,0:T(8,128)(2,1)S(1)} %get-tuple-element.102), channel_id=1, source_target_pairs={{3,0},{2,1},{1,2},{0,3},{7,4},{6,5},{5,6},{4,7},{11,8},{10,9},{9,1... | collective-permute-start | bytes 245768 | tf_op jit(solution)/shard_map/ppermute | solution.py:24
  46.8 1.5 %collective-permute-start.14 = (bf16[4,80,256]{2,1,0:T(8,128)(2,1)S(1)}, bf16[4,80,256]{2,1,0:T(8,128)(2,1)S(1)}, u32[]{:S(2)}, u32[]{:S(2)}) collective-permute-start(bf16[4,80,256]{2,1,0:T(8,128)(2,1)S(1)} %get-tuple-element.133), channel_id=1, source_target_pairs={{4,0},{0,4},{12,8},{8,12},{20,16},{16,20},{28,24},{24,28},{5,1},{1... | collective-permute-start | bytes 491528 | tf_op jit(solution)/shard_map/ppermute | solution.py:24
  48.3 5.0 %collective-permute-start.15 = (bf16[80,256]{1,0:T(8,128)(2,1)S(1)}, bf16[80,256]{1,0:T(8,128)(2,1)S(1)}, u32[]{:S(2)}, u32[]{:S(2)}) collective-permute-start(bf16[80,256]{1,0:T(8,128)(2,1)S(1)} %get-tuple-element.135), channel_id=1, source_target_pairs={{8,0},{12,4},{0,8},{4,12},{24,16},{28,20},{16,24},{20,28},{9,1},{1... | collective-permute-start | bytes 122888 | tf_op jit(solution)/shard_map/ppermute | solution.py:24
  50.3 5.8 %collective-permute-start.16 = (bf16[80,256]{1,0:T(8,128)(2,1)S(1)}, bf16[80,256]{1,0:T(8,128)(2,1)S(1)}, u32[]{:S(2)}, u32[]{:S(2)}) collective-permute-start(bf16[80,256]{1,0:T(8,128)(2,1)S(1)} %get-tuple-element.136), channel_id=1, source_target_pairs={{16,0},{20,4},{24,8},{28,12},{0,16},{4,20},{8,24},{12,28},{17,1},{... | collective-permute-start | bytes 122888 | tf_op jit(solution)/shard_map/ppermute | solution.py:24
  51.2 5.9 %collective-permute-start.17 = (bf16[80,256]{1,0:T(8,128)(2,1)S(1)}, bf16[80,256]{1,0:T(8,128)(2,1)S(1)}, u32[]{:S(2)}, u32[]{:S(2)}) collective-permute-start(bf16[80,256]{1,0:T(8,128)(2,1)S(1)} %get-tuple-element.137), channel_id=1, source_target_pairs={{24,0},{28,4},{16,8},{20,12},{8,16},{12,20},{0,24},{4,28},{25,1},{... | collective-permute-start | bytes 122888 | tf_op jit(solution)/shard_map/ppermute | solution.py:24
  60.0 5.0 %collective-permute-start.18 = (bf16[3,128,256]{2,1,0:T(8,128)(2,1)S(1)}, bf16[3,128,256]{2,1,0:T(8,128)(2,1)S(1)}, u32[]{:S(2)}, u32[]{:S(2)}) collective-permute-start(bf16[3,128,256]{2,1,0:T(8,128)(2,1)S(1)} %get-tuple-element.142), channel_id=1, source_target_pairs={{4,0},{0,4},{12,8},{8,12},{20,16},{16,20},{28,24},{24,28},{5,1},{1... | collective-permute-start | bytes 589832 | tf_op jit(solution)/shard_map/ppermute | solution.py:24
  60.0 8.0 %collective-permute-start.19 = (bf16[3,128,256]{2,1,0:T(8,128)(2,1)S(1)}, bf16[3,128,256]{2,1,0:T(8,128)(2,1)S(1)}, u32[]{:S(2)}, u32[]{:S(2)}) collective-permute-start(bf16[3,128,256]{2,1,0:T(8,128)(2,1)S(1)} %get-tuple-element.143), channel_id=1, source_target_pairs={{28,0},{8,4},{4,8},{16,12},{12,16},{24,20},{20,24},{0,28},{29,1},{... | collective-permute-start | bytes 589832 | tf_op jit(solution)/shard_map/ppermute | solution.py:33
  71.6 5.0 %collective-permute-start.21 = (f32[16,256]{1,0:T(8,128)S(1)}, f32[16,256]{1,0:T(8,128)S(1)}, u32[]{:S(2)}, u32[]{:S(2)}) collective-permute-start(f32[16,256]{1,0:T(8,128)S(1)} %get-tuple-element.146), channel_id=1, source_target_pairs={{28,0},{8,4},{4,8},{16,12},{12,16},{24,20},{20,24},{0,28},{29,1},{... | collective-permute-start | bytes 49160 | tf_op jit(solution)/shard_map/ppermute | solution.py:33
  72.7 3.9 %collective-permute-start.20 = (f32[16,256]{1,0:T(8,128)S(1)}, f32[16,256]{1,0:T(8,128)S(1)}, u32[]{:S(2)}, u32[]{:S(2)}) collective-permute-start(f32[16,256]{1,0:T(8,128)S(1)} %get-tuple-element.145), channel_id=1, source_target_pairs={{4,0},{0,4},{12,8},{8,12},{20,16},{16,20},{28,24},{24,28},{5,1},{1... | collective-permute-start | bytes 49160 | tf_op jit(solution)/shard_map/ppermute | solution.py:24
  76.7 3.7 %collective-permute-start.24 = (f32[3,256]{1,0:T(4,128)S(1)}, f32[3,256]{1,0:T(4,128)S(1)}, u32[]{:S(2)}, u32[]{:S(2)}) collective-permute-start(f32[3,256]{1,0:T(4,128)S(1)} %get-tuple-element.151), channel_id=1, source_target_pairs={{2,0},{3,1},{0,2},{1,3},{6,4},{7,5},{4,6},{5,7},{10,8},{11,9},{8,1... | collective-permute-start | bytes 9224 | tf_op jit(solution)/shard_map/ppermute | solution.py:42
  77.6 4.5 %collective-permute-start.23 = (f32[3,256]{1,0:T(4,128)S(1)}, f32[3,256]{1,0:T(4,128)S(1)}, u32[]{:S(2)}, u32[]{:S(2)}) collective-permute-start(f32[3,256]{1,0:T(4,128)S(1)} %get-tuple-element.152), channel_id=1, source_target_pairs={{3,0},{2,1},{1,2},{0,3},{7,4},{6,5},{5,6},{4,7},{11,8},{10,9},{9,1... | collective-permute-start | bytes 9224 | tf_op jit(solution)/shard_map/ppermute | solution.py:33
  79.7 3.6 %collective-permute-start.22 = (f32[3,256]{1,0:T(4,128)S(1)}, f32[3,256]{1,0:T(4,128)S(1)}, u32[]{:S(2)}, u32[]{:S(2)}) collective-permute-start(f32[3,256]{1,0:T(4,128)S(1)} %get-tuple-element.150), channel_id=1, source_target_pairs={{1,0},{0,1},{3,2},{2,3},{5,4},{4,5},{7,6},{6,7},{9,8},{8,9},{11,10... | collective-permute-start | bytes 9224 | tf_op jit(solution)/shard_map/ppermute | solution.py:24

commit v18 on v17

--- a/solution.py
+++ b/solution.py
@@ -501,8 +501,8 @@
 
 
 def first_back_kernel(slots, ids_ref, basis_ref, slope_ref, unit_ref, kind_high, kind_low, turn_high,
-                      turn_low, sums_ref, gate_ref, edge_ref, long_ref, middle_ref, from_pair,
-                      from_beyond, *outs):
+                      turn_low, sums_ref, gate_ref, edge_ref, from_beyond, long_ref, middle_ref,
+                      from_pair, *outs):
     sums = {(1, 2): long_ref[...]}
     for cell in range(3):
         cotangent = middle_ref[cell] + (
@@ -1056,7 +1056,7 @@
         functools.partial(first_back_kernel, slots),
         [shape(16, atoms)] * 3,
         [ids, basis, slope, unit, kind_high, kind_low, turn_high, turn_low, sums_one, gate_one, edge,
-         long, middle, from_pair, from_beyond],
+         from_beyond, long, middle, from_pair],
         name="first_back",
     )
     total = middle + paired(to_pair, "gx", 1) + beyond(to_beyond, "gx")

time: 84.1 us -> 83.4 us (level)
    ppermute x6, starting transfers between devices: 10.1 us -> 9.21 us  [beyond(): lax.ppermute(block, axis, [(other_side(i, count), i) for i in range(count)])]
where the time goes in v18:
time: 83.4 us; the launch traced here: 83.2 us
  starting transfers between devices  27.5 us (33%)
  Pallas kernels  27.4 us (33%)
  waiting for transfers between devices  25.1 us (30%)
  local copies, waits for them, and re-layouts  2.07 us (2%)
  between operations  0.96 us (1%)
    pallas_call x22, Pallas kernels, run(): pl.pallas_call(kernel, out_shape=outs, in_specs=specs, out_specs=[whole()...  27.4 us
    ppermute x17, starting transfers between devices, paired(): lax.ppermute(block, axis, [(i ^ mask, i) for i in range(lax.axis_size(axi...  14.4 us
    ppermute x6, waiting for transfers between devices, beyond(): lax.ppermute(block, axis, [(other_side(i, count), i) for i in range(count)])  13.5 us
    ppermute x17, waiting for transfers between devices, paired(): lax.ppermute(block, axis, [(i ^ mask, i) for i in range(lax.axis_size(axi...  11.5 us
    ppermute x6, starting transfers between devices, beyond(): lax.ppermute(block, axis, [(other_side(i, count), i) for i in range(count)])  9.21 us
    ppermute x2, starting transfers between devices, far(): return lax.ppermute(block, axis, route)  3.87 us
    unnamed x27, local copies, waits for them, and re-layouts  2 us
  transfers between devices with their start and end apart: 25, of which 15 were waited for; matrix products, arithmetic and copies ran while one was open for 0% of the time, Pallas kernels for 16%

profile of v18, /device:TPU:0, one launch (start us, length us, event | category | flops | bytes accessed | tf_op | source)
XLA Modules:
  0.0 83.2 jit_solution(14136785231178558253)
XLA Ops:
  0.6 0.1 pad_add_fusion
  0.7 0.1 broadcast_in_dim.4.place_ref
  0.8 0.7 copy-done.9
  1.5 0.7 copy-done.10
  2.2 0.0 copy-start.6
  2.2 3.0 %collective-permute-start.2 = (f32[8,128]{1,0:T(8,128)S(1)}, f32[8,128]{1,0:T(8,128)S(1)}, u32[]{:S(2)}, u32[]{:S(2)}) collective-permute-start(f32[8,128]{1,0:T(8,128)S(1)} %pack.1.first_ref), channel_id=1, source_target_pairs={{2,0},{3,1},{0,2},{1,3},{6,4},{7,5},{4,6},{5,7},{10,8},{11,9},{8,1... | collective-permute-start | bytes 12296 | tf_op jit(solution)/shard_map/ppermute | solution.py:42
  5.3 0.1 pack_more.1.own_ref
  5.4 1.6 %collective-permute-start = (f32[40,128]{1,0:T(8,128)S(1)}, f32[40,128]{1,0:T(8,128)S(1)}, u32[]{:S(2)}, u32[]{:S(2)}) collective-permute-start(f32[40,128]{1,0:T(8,128)S(1)} %pack_more.1.own_ref), channel_id=1, source_target_pairs={{3,0},{2,1},{1,2},{0,3},{7,4},{6,5},{5,6},{4,7},{11,8},{10,9},{9,1... | collective-permute-start | bytes 61448 | tf_op jit(solution)/shard_map/ppermute | solution.py:33
  6.9 0.5 collective-permute-start.1
  7.5 3.2 %collective-permute-done.1.y_pair_ref = f32[40,128]{1,0:T(8,128)S(1)} collective-permute-done((f32[40,128]{1,0:T(8,128)S(1)}, f32[40,128]{1,0:T(8,128)S(1)}, u32[]{:S(2)}, u32[]{:S(2)}) %collective-permute-start.1) | collective-permute-done | bytes 20512 | tf_op jit(solution)/shard_map/ppermute | solution.py:24
  10.7 1.8 %collective-permute-start.3 = (f32[5,8,128]{2,1,0:T(8,128)S(1)}, f32[5,8,128]{2,1,0:T(8,128)S(1)}, u32[]{:S(2)}, u32[]{:S(2)}) collective-permute-start(f32[5,8,128]{2,1,0:T(8,128)S(1)} %constant_dynamic-update-slice_fusion.column_ref.cell_ref), channel_id=1, source_target_pairs={{28,0},{8,4},{4,8},{16,12},{12,16},{24,20},{20,24},{0,28},{29,1},{... | collective-permute-start | bytes 61448 | tf_op jit(solution)/shard_map/ppermute | solution.py:33
  12.6 0.3 prep_first.1
  12.9 0.3 prep_second.1
  13.2 2.6 %collective-permute-done.3.beyond_ref = f32[5,8,128]{2,1,0:T(8,128)S(1)} collective-permute-done((f32[5,8,128]{2,1,0:T(8,128)S(1)}, f32[5,8,128]{2,1,0:T(8,128)S(1)}, u32[]{:S(2)}, u32[]{:S(2)}) %collective-permute-start.3) | collective-permute-done | bytes 20512 | tf_op jit(solution)/shard_map/ppermute | solution.py:33
  15.8 2.9 %first.1 = (bf16[3,128,256]{2,1,0:T(8,128)(2,1)S(1)}, s32[3,3072]{1,0:T(4,128)S(1)}, f32[3,8,3072]{2,1,0:T(8,128)S(1)}, f32[3,8,3072]{2,1,0:T(8,128)S(1)}, f32[3...) custom-call(s32[2,8,128]{2,1,0:T(8,128)S(1)} %broadcast_in_dim.4.place_ref, ...), custom_call_target="tpu_custom_call" | custom-call | flops 10000000 | bytes 1000000 | tf_op jit(solution)/shard_map/first/pallas_call | solution.py:55
  18.7 0.1 collective-permute-start.5
  18.8 1.9 %collective-permute-start.6 = (bf16[3,128,256]{2,1,0:T(8,128)(2,1)S(1)}, bf16[3,128,256]{2,1,0:T(8,128)(2,1)S(1)}, u32[]{:S(2)}, u32[]{:S(2)}) collective-permute-start(bf16[3,128,256]{2,1,0:T(8,128)(2,1)S(1)} %get-tuple-element.93.column_ref), channel_id=1, source_target_pairs={{28,0},{8,4},{4,8},{16,12},{12,16},{24,20},{20,24},{0,28},{29,1},{... | collective-permute-start | bytes 589832 | tf_op jit(solution)/shard_map/ppermute | solution.py:33
  20.7 1.7 %second_near.1 = (f32[4,128,3072]{2,1,0:T(8,128)S(1)}, f32[128,3072]{1,0:T(8,128)S(1)}) custom-call(s32[3,3072]{1,0:T(4,128)S(1)} %get-tuple-element.81.ids_ref, f32[3,8,3072]{2,1,0:T(8,128)S(1)} %get-tuple-element.82.basis_ref, f32[3,8,3072]{2,1,0:T(8,128)S(1)} %get-tuple-element.84.unit_ref, bf16[2,128,32]{2,1,0:T(8,128)(2,1)S(1)} %get-tuple-element.92.left_ref, ...), custom_call_target="tpu_custom_call" | custom-call | flops 2000000000 | bytes 1000000 | tf_op jit(solution)/shard_map/second_near/pallas_call | solution.py:55
  22.5 1.0 %hot_beyond.1.hot_ref = bf16[768,3072]{1,0:T(8,128)(2,1)S(1)} custom-call(s32[3,3072]{1,0:T(4,128)S(1)} %get-tuple-element.81.ids_ref, f32[128,3072]{1,0:T(8,128)S(1)} %get-tuple-element.94.near_ref), custom_call_target="tpu_custom_call" | custom-call | flops 1000000 | bytes 1000000 | tf_op jit(solution)/shard_map/hot_beyond/pallas_call | solution.py:55
  23.4 0.8 second_side.1.near_ref
  24.3 2.7 %collective-permute-done.6.beyond_ref = bf16[3,128,256]{2,1,0:T(8,128)(2,1)S(1)} collective-permute-done((bf16[3,128,256]{2,1,0:T(8,128)(2,1)S(1)}, bf16[3,128,256]{2,1,0:T(8,128)(2,1)S(1)}, u32[]{:S(2)}, u32[]{:S(2)}) %collective-permute-start.6) | collective-permute-done | bytes 196640 | tf_op jit(solution)/shard_map/ppermute | solution.py:33
  26.9 1.9 %second.1 = (bf16[128,3072]{1,0:T(8,128)(2,1)S(1)}, f32[3,128,256]{2,1,0:T(8,128)S(1)}, f32[128,256]{1,0:T(8,128)S(1)}, bf16[80,256]{1,0:T(8,128)(2,1)S(1)}, f32...) custom-call(bf16[768,3072]{1,0:T(8,128)(2,1)S(1)} %hot_beyond.1.hot_ref, f32[4,128,3072]{2,1,0:T(8,128)S(1)} %get-tuple-element.95.weight_ref, ...), custom_call_target="tpu_custom_call" | custom-call | flops 10000000 | bytes 1000000 | tf_op jit(solution)/shard_map/second/pallas_call | solution.py:55
  28.8 0.1 collective-permute-start.9
  28.9 0.1 collective-permute-start.8
  28.9 4.3 %collective-permute-start.7 = (bf16[80,256]{1,0:T(8,128)(2,1)S(1)}, bf16[80,256]{1,0:T(8,128)(2,1)S(1)}, u32[]{:S(2)}, u32[]{:S(2)}) collective-permute-start(bf16[80,256]{1,0:T(8,128)(2,1)S(1)} %get-tuple-element.98), channel_id=1, source_target_pairs={{8,0},{12,4},{0,8},{4,12},{24,16},{28,20},{16,24},{20,28},{9,1},{1... | collective-permute-start | bytes 122888 | tf_op jit(solution)/shard_map/ppermute | solution.py:24
  33.2 0.8 green.1.refs_0_
  34.1 0.9 %collective-permute-done.9 = bf16[80,256]{1,0:T(8,128)(2,1)S(1)} collective-permute-done((bf16[80,256]{1,0:T(8,128)(2,1)S(1)}, bf16[80,256]{1,0:T(8,128)(2,1)S(1)}, u32[]{:S(2)}, u32[]{:S(2)}) %collective-permute-start.9) | collective-permute-done | bytes 40992 | tf_op jit(solution)/shard_map/ppermute | solution.py:24
  35.0 0.3 collective-permute-done.7
  35.3 0.1 collective-permute-start.10
  35.4 1.2 %structure_near.1 = (f32[32,1024]{1,0:T(8,128)S(1)}, f32[32,1024]{1,0:T(8,128)S(1)}, f32[8,1024]{1,0:T(8,128)S(1)}, f32[8,1024]{1,0:T(8,128)S(1)}, bf16[640,1024...) custom-call(s32[2,8,128]{2,1,0:T(8,128)S(1)} %broadcast_in_dim.4.place_ref, ...), custom_call_target="tpu_custom_call" | custom-call | flops 1000000000 | bytes 1000000 | tf_op jit(solution)/shard_map/structure_near/pallas_call | solution.py:55
  36.6 0.2 collective-permute-done.10.blocks.refs_11_
  36.8 1.3 %structure_far.1 = (f32[32,1024]{1,0:T(8,128)S(1)}, f32[32,1024]{1,0:T(8,128)S(1)}, f32[8,1024]{1,0:T(8,128)S(1)}, f32[8,1024]{1,0:T(8,128)S(1)}, bf16[640,1024]...) custom-call(s32[2,8,128]{2,1,0:T(8,128)S(1)} %broadcast_in_dim.4.place_r, ...), custom_call_target="tpu_custom_call" | custom-call | flops 10000000 | bytes 1000000 | tf_op jit(solution)/shard_map/structure_far/pallas_call | solution.py:55
  38.1 0.9 %collective-permute-start.11 = (bf16[320,128]{1,0:T(8,128)(2,1)S(1)}, bf16[320,128]{1,0:T(8,128)(2,1)S(1)}, u32[]{:S(2)}, u32[]{:S(2)}) collective-permute-start(bf16[320,128]{1,0:T(8,128)(2,1)S(1)} %get-tuple-element.102), channel_id=1, source_target_pairs={{1,0},{0,1},{3,2},{2,3},{5,4},{4,5},{7,6},{6,7},{9,8},{8,9},{11,10... | collective-permute-start | bytes 245768 | tf_op jit(solution)/shard_map/ppermute | solution.py:24
  38.9 1.1 %collective-permute-start.12 = (bf16[320,128]{1,0:T(8,128)(2,1)S(1)}, bf16[320,128]{1,0:T(8,128)(2,1)S(1)}, u32[]{:S(2)}, u32[]{:S(2)}) collective-permute-start(bf16[320,128]{1,0:T(8,128)(2,1)S(1)} %get-tuple-element.102), channel_id=1, source_target_pairs={{2,0},{3,1},{0,2},{1,3},{6,4},{7,5},{4,6},{5,7},{10,8},{11,9},{8,1... | collective-permute-start | bytes 245768 | tf_op jit(solution)/shard_map/ppermute | solution.py:24
  40.0 1.6 %collective-permute-start.13 = (bf16[320,128]{1,0:T(8,128)(2,1)S(1)}, bf16[320,128]{1,0:T(8,128)(2,1)S(1)}, u32[]{:S(2)}, u32[]{:S(2)}) collective-permute-start(bf16[320,128]{1,0:T(8,128)(2,1)S(1)} %get-tuple-element.102), channel_id=1, source_target_pairs={{3,0},{2,1},{1,2},{0,3},{7,4},{6,5},{5,6},{4,7},{11,8},{10,9},{9,1... | collective-permute-start | bytes 245768 | tf_op jit(solution)/shard_map/ppermute | solution.py:24
  41.6 2.3 %hot_back.1.hot_ref = bf16[3072,1536]{1,0:T(8,128)(2,1)S(1)} custom-call(s32[3,3072]{1,0:T(4,128)S(1)} %get-tuple-element.81.ids_ref), custom_call_target="tpu_custom_call" | custom-call | flops 2000000000 | bytes 1000000 | tf_op jit(solution)/shard_map/hot_back/pallas_call | solution.py:55
  43.9 1.6 %collective-permute-done.13.refs_4_ = bf16[320,128]{1,0:T(8,128)(2,1)S(1)} collective-permute-done((bf16[320,128]{1,0:T(8,128)(2,1)S(1)}, bf16[320,128]{1,0:T(8,128)(2,1)S(1)}, u32[]{:S(2)}, u32[]{:S(2)}) %collective-permute-start.13) | collective-permute-done | bytes 81952 | tf_op jit(solution)/shard_map/ppermute | solution.py:24
  45.5 1.3 %fold_far.1 = (bf16[4,80,256]{2,1,0:T(8,128)(2,1)S(1)}, f32[640,64]{1,0:T(8,128)S(1)}) custom-call(s32[2,8,128]{2,1,0:T(8,128)S(1)} %broadcast_in_dim.4.place_ref, f32[320,128]{1,0:T(8,128)S(1)} %green.1.refs_0_, f32[320,128]{1,0:T(8,128)S(1)} %get-tuple-element.116.refs_1_, bf16[320,128]{1,0:T(8,128)(2,1)S(1)} %collective-permute-done.11.refs_2_, ...), custom_call_target="tpu_custom_call" | custom-call | flops 10000000 | bytes 1000000 | tf_op jit(solution)/shard_map/fold_far/pallas_call | solution.py:55
  46.8 0.1 collective-permute-start.14
  46.9 1.2 %fold_near.1.near_ref = f32[4,80,256]{2,1,0:T(8,128)S(1)} custom-call(s32[2,8,128]{2,1,0:T(8,128)S(1)} %broadcast_in_dim.4.place_ref, f32[640,64]{1,0:T(8,128)S(1)} %get-tuple-element.126.refs_0_, f32[32,1024]{1,0:T(8,128)S(1)} %get-tuple-element.127.refs_1_, f32[32,1024]{1,0:T(8,128)S(1)} %get-tuple-element.128.refs_2_, ...), custom_call_target="tpu_custom_call" | custom-call | flops 1000000000 | bytes 1000000 | tf_op jit(solution)/shard_map/fold_near/pallas_call | solution.py:55
  48.1 0.2 collective-permute-done.14.far_ref
  48.3 0.1 fold_join.1
  48.3 2.0 %collective-permute-start.15 = (bf16[80,256]{1,0:T(8,128)(2,1)S(1)}, bf16[80,256]{1,0:T(8,128)(2,1)S(1)}, u32[]{:S(2)}, u32[]{:S(2)}) collective-permute-start(bf16[80,256]{1,0:T(8,128)(2,1)S(1)} %get-tuple-element.135), channel_id=1, source_target_pairs={{8,0},{12,4},{0,8},{4,12},{24,16},{28,20},{16,24},{20,28},{9,1},{1... | collective-permute-start | bytes 122888 | tf_op jit(solution)/shard_map/ppermute | solution.py:24
  50.3 0.9 %collective-permute-start.16 = (bf16[80,256]{1,0:T(8,128)(2,1)S(1)}, bf16[80,256]{1,0:T(8,128)(2,1)S(1)}, u32[]{:S(2)}, u32[]{:S(2)}) collective-permute-start(bf16[80,256]{1,0:T(8,128)(2,1)S(1)} %get-tuple-element.136), channel_id=1, source_target_pairs={{16,0},{20,4},{24,8},{28,12},{0,16},{4,20},{8,24},{12,28},{17,1},{... | collective-permute-start | bytes 122888 | tf_op jit(solution)/shard_map/ppermute | solution.py:24
  51.2 1.5 %collective-permute-start.17 = (bf16[80,256]{1,0:T(8,128)(2,1)S(1)}, bf16[80,256]{1,0:T(8,128)(2,1)S(1)}, u32[]{:S(2)}, u32[]{:S(2)}) collective-permute-start(bf16[80,256]{1,0:T(8,128)(2,1)S(1)} %get-tuple-element.137), channel_id=1, source_target_pairs={{24,0},{28,4},{16,8},{20,12},{8,16},{12,20},{0,24},{4,28},{25,1},{... | collective-permute-start | bytes 122888 | tf_op jit(solution)/shard_map/ppermute | solution.py:24
  52.8 0.5 readout.1
  53.3 2.8 %collective-permute-done.16.refs_2_ = bf16[80,256]{1,0:T(8,128)(2,1)S(1)} collective-permute-done((bf16[80,256]{1,0:T(8,128)(2,1)S(1)}, bf16[80,256]{1,0:T(8,128)(2,1)S(1)}, u32[]{:S(2)}, u32[]{:S(2)}) %collective-permute-start.16) | collective-permute-done | bytes 40992 | tf_op jit(solution)/shard_map/ppermute | solution.py:24
  56.1 1.0 %collective-permute-done.17.refs_3_ = bf16[80,256]{1,0:T(8,128)(2,1)S(1)} collective-permute-done((bf16[80,256]{1,0:T(8,128)(2,1)S(1)}, bf16[80,256]{1,0:T(8,128)(2,1)S(1)}, u32[]{:S(2)}, u32[]{:S(2)}) %collective-permute-start.17) | collective-permute-done | bytes 40992 | tf_op jit(solution)/shard_map/ppermute | solution.py:24
  57.2 2.8 %second_back.1 = (f32[1,1,256]{2,1,0:T(1,128)}, f32[8,256]{1,0:T(8,128)S(1)}, f32[128,256]{1,0:T(8,128)S(1)}, f32[4,128,256]{2,1,0:T(8,128)S(1)}, bf16[128,3072]...) custom-call(bf16[3072,1536]{1,0:T(8,128)(2,1)S(1)} %hot_back.1.hot_ref, ...), custom_call_target="tpu_custom_call" | custom-call | flops 10000000 | bytes 1000000 | tf_op jit(solution)/shard_map/second_back/pallas_call | solution.py:55
  60.0 0.7 collective-permute-start.19
  60.7 1.3 %hot_middle.1.hot_ref = bf16[3072,768]{1,0:T(8,128)(2,1)S(1)} custom-call(s32[3,3072]{1,0:T(4,128)S(1)} %get-tuple-element.81.ids_ref), custom_call_target="tpu_custom_call" | custom-call | flops 1000000000 | bytes 1000000 | tf_op jit(solution)/shard_map/hot_middle/pallas_call | solution.py:55
  62.0 1.2 %second_edge.1.edge_ref = f32[32,3072]{1,0:T(8,128)S(1)} custom-call(bf16[2,16,256]{2,1,0:T(8,128)(2,1)S(1)} %get-tuple-element.91.back_ref, bf16[128,3072]{1,0:T(8,128)(2,1)S(1)} %get-tuple-element.97.feature_ref, f32[4,128,256]{2,1,0:T(8,128)S(1)} %get-tuple-element.138.grad_ref), custom_call_target="tpu_custom_call" | custom-call | flops 1000000000 | bytes 1000000 | tf_op jit(solution)/shard_map/second_edge/pallas_call | solution.py:55
  63.2 0.8 second_middle.1.middle_ref
  64.0 3.2 %collective-permute-done.18.from_beyond = bf16[3,128,256]{2,1,0:T(8,128)(2,1)S(1)} collective-permute-done((bf16[3,128,256]{2,1,0:T(8,128)(2,1)S(1)}, bf16[3,128,256]{2,1,0:T(8,128)(2,1)S(1)}, u32[]{:S(2)}, u32[]{:S(2)}) %collective-permute-start.18) | collective-permute-done | bytes 196640 | tf_op jit(solution)/shard_map/ppermute | solution.py:33
  67.3 3.6 %first_back.1 = (f32[16,256]{1,0:T(8,128)S(1)}, f32[16,256]{1,0:T(8,128)S(1)}, f32[16,256]{1,0:T(8,128)S(1)}) custom-call(s32[3,3072]{1,0:T(4,128)S(1)} %get-tuple-element.81.ids_ref, f32[3,8,3072]{2,1,0:T(8,128)S(1)} %get-tuple-element.82.basis_ref, f32[3,8,3072]{2,1,0:T(8,128)S(1)} %get-tuple-element.83.slope_ref, ...), custom_call_target="tpu_custom_call" | custom-call | flops 10000000 | bytes 1000000 | tf_op jit(solution)/shard_map/first_back/pallas_call | solution.py:55
  70.9 1.7 %collective-permute-start.21 = (f32[16,256]{1,0:T(8,128)S(1)}, f32[16,256]{1,0:T(8,128)S(1)}, u32[]{:S(2)}, u32[]{:S(2)}) collective-permute-start(f32[16,256]{1,0:T(8,128)S(1)} %get-tuple-element.146), channel_id=1, source_target_pairs={{28,0},{8,4},{4,8},{16,12},{12,16},{24,20},{20,24},{0,28},{29,1},{... | collective-permute-start | bytes 49160 | tf_op jit(solution)/shard_map/ppermute | solution.py:33
  72.7 3.3 %collective-permute-done.21 = f32[16,256]{1,0:T(8,128)S(1)} collective-permute-done((f32[16,256]{1,0:T(8,128)S(1)}, f32[16,256]{1,0:T(8,128)S(1)}, u32[]{:S(2)}, u32[]{:S(2)}) %collective-permute-start.21) | collective-permute-done | bytes 16416 | tf_op jit(solution)/shard_map/ppermute | solution.py:33
  76.0 0.8 %collective-permute-start.24 = (f32[3,256]{1,0:T(4,128)S(1)}, f32[3,256]{1,0:T(4,128)S(1)}, u32[]{:S(2)}, u32[]{:S(2)}) collective-permute-start(f32[3,256]{1,0:T(4,128)S(1)} %get-tuple-element.151), channel_id=1, source_target_pairs={{2,0},{3,1},{0,2},{1,3},{6,4},{7,5},{4,6},{5,7},{10,8},{11,9},{8,1... | collective-permute-start | bytes 9224 | tf_op jit(solution)/shard_map/ppermute | solution.py:42
  76.8 2.2 %collective-permute-start.23 = (f32[3,256]{1,0:T(4,128)S(1)}, f32[3,256]{1,0:T(4,128)S(1)}, u32[]{:S(2)}, u32[]{:S(2)}) collective-permute-start(f32[3,256]{1,0:T(4,128)S(1)} %get-tuple-element.152), channel_id=1, source_target_pairs={{3,0},{2,1},{1,2},{0,3},{7,4},{6,5},{5,6},{4,7},{11,8},{10,9},{9,1... | collective-permute-start | bytes 9224 | tf_op jit(solution)/shard_map/ppermute | solution.py:33
  79.0 0.5 collective-permute-start.22
  79.5 0.1 collective-permute-done.24
  79.6 1.7 %collective-permute-done.23 = f32[3,256]{1,0:T(4,128)S(1)} collective-permute-done((f32[3,256]{1,0:T(4,128)S(1)}, f32[3,256]{1,0:T(4,128)S(1)}, u32[]{:S(2)}, u32[]{:S(2)}) %collective-permute-start.23) | collective-permute-done | bytes 3104 | tf_op jit(solution)/shard_map/ppermute | solution.py:33
  81.3 1.3 %collective-permute-done.22 = f32[3,256]{1,0:T(4,128)S(1)} collective-permute-done((f32[3,256]{1,0:T(4,128)S(1)}, f32[3,256]{1,0:T(4,128)S(1)}, u32[]{:S(2)}, u32[]{:S(2)}) %collective-permute-start.22) | collective-permute-done | bytes 3104 | tf_op jit(solution)/shard_map/ppermute | solution.py:24
  82.6 0.6 copy.13
  (42 shorter events, 0.1 us)
Async XLA Ops:
  0.8 0.7 copy-start.9
  1.5 0.7 copy-start.10
  2.1 3.1 %copy-start.5 = (s32[1,1,256,12]{2,1,3,0:T(1,128)S(1)}, s32[1,1,256,12]{2,1,3,0:T(1,128)}, u32[]{:S(2)}) copy-start(s32[1,1,256,12]{2,1,3,0:T(1,128)} %param.13) | copy-start | bytes 36868
  2.2 3.1 %copy-start.7 = (s32[1,1,256]{2,1,0:T(1,128)S(1)}, s32[1,1,256]{2,1,0:T(1,128)}, u32[]{:S(2)}) copy-start(s32[1,1,256]{2,1,0:T(1,128)} %count_ref.1) | copy-start | bytes 3076
  2.2 10.4 %copy-start = (f32[2,2,128,128]{3,2,1,0:T(8,128)S(1)}, f32[2,2,128,128]{3,2,1,0:T(8,128)}, u32[]{:S(2)}) copy-start(f32[2,2,128,128]{3,2,1,0:T(8,128)} %mixing_in.1) | copy-start | bytes 786436
  2.2 10.4 %copy-start.4 = (f32[2,2,8,128]{3,2,1,0:T(8,128)S(1)}, f32[2,2,8,128]{3,2,1,0:T(8,128)}, u32[]{:S(2)}) copy-start(f32[2,2,8,128]{3,2,1,0:T(8,128)} %radial_in.1) | copy-start | bytes 49156
  2.2 10.4 %copy-start.6 = (f32[6,128]{1,0:T(8,128)S(1)}, f32[6,128]{1,0:T(8,128)}, u32[]{:S(2)}) copy-start(f32[6,128]{1,0:T(8,128)} %embed_in.1) | copy-start | bytes 9220
  2.2 10.7 %copy-start.1 = (f32[128,128]{1,0:T(8,128)S(1)}, f32[128,128]{1,0:T(8,128)}, u32[]{:S(2)}) copy-start(f32[128,128]{1,0:T(8,128)} %hidden_in.1) | copy-start | bytes 196612
  2.2 10.7 %copy-start.3 = (f32[128,64]{0,1:T(8,128)S(1)}, f32[128,64]{0,1:T(8,128)}, u32[]{:S(2)}) copy-start(f32[128,64]{0,1:T(8,128)} %param.20) | copy-start | bytes 98308
  2.2 10.7 %copy-start.8 = (f32[128]{0:T(128)S(1)}, f32[128]{0:T(128)}, u32[]{:S(2)}) copy-start(f32[128]{0:T(128)} %param.19) | copy-start | bytes 1540
  2.2 5.3 %collective-permute-start.2 = (f32[8,128]{1,0:T(8,128)S(1)}, f32[8,128]{1,0:T(8,128)S(1)}, u32[]{:S(2)}, u32[]{:S(2)}) collective-permute-start(f32[8,128]{1,0:T(8,128)S(1)} %pack.1.first_ref), channel_id=1, source_target_pairs={{2,0},{3,1},{0,2},{1,3},{6,4},{7,5},{4,6},{5,7},{10,8},{11,9},{8,1... | collective-permute-start | bytes 12296 | tf_op jit(solution)/shard_map/ppermute | solution.py:42
  5.4 5.3 %collective-permute-start = (f32[40,128]{1,0:T(8,128)S(1)}, f32[40,128]{1,0:T(8,128)S(1)}, u32[]{:S(2)}, u32[]{:S(2)}) collective-permute-start(f32[40,128]{1,0:T(8,128)S(1)} %pack_more.1.own_ref), channel_id=1, source_target_pairs={{3,0},{2,1},{1,2},{0,3},{7,4},{6,5},{5,6},{4,7},{11,8},{10,9},{9,1... | collective-permute-start | bytes 61448 | tf_op jit(solution)/shard_map/ppermute | solution.py:33
  6.9 3.8 %collective-permute-start.1 = (f32[40,128]{1,0:T(8,128)S(1)}, f32[40,128]{1,0:T(8,128)S(1)}, u32[]{:S(2)}, u32[]{:S(2)}) collective-permute-start(f32[40,128]{1,0:T(8,128)S(1)} %pack_more.1.own_ref), channel_id=1, source_target_pairs={{1,0},{0,1},{3,2},{2,3},{5,4},{4,5},{7,6},{6,7},{9,8},{8,9},{11,10... | collective-permute-start | bytes 61448 | tf_op jit(solution)/shard_map/ppermute | solution.py:24
  10.7 5.1 %collective-permute-start.3 = (f32[5,8,128]{2,1,0:T(8,128)S(1)}, f32[5,8,128]{2,1,0:T(8,128)S(1)}, u32[]{:S(2)}, u32[]{:S(2)}) collective-permute-start(f32[5,8,128]{2,1,0:T(8,128)S(1)} %constant_dynamic-update-slice_fusion.column_ref.cell_ref), channel_id=1, source_target_pairs={{28,0},{8,4},{4,8},{16,12},{12,16},{24,20},{20,24},{0,28},{29,1},{... | collective-permute-start | bytes 61448 | tf_op jit(solution)/shard_map/ppermute | solution.py:33
  12.6 3.3 %collective-permute-start.4 = (f32[5,8,128]{2,1,0:T(8,128)S(1)}, f32[5,8,128]{2,1,0:T(8,128)S(1)}, u32[]{:S(2)}, u32[]{:S(2)}) collective-permute-start(f32[5,8,128]{2,1,0:T(8,128)S(1)} %constant_dynamic-update-slice_fusion.column_ref.cell_ref), channel_id=1, source_target_pairs={{4,0},{0,4},{12,8},{8,12},{20,16},{16,20},{28,24},{24,28},{5,1},{1... | collective-permute-start | bytes 61448 | tf_op jit(solution)/shard_map/ppermute | solution.py:24
  18.7 4.7 %collective-permute-start.5 = (bf16[3,128,256]{2,1,0:T(8,128)(2,1)S(1)}, bf16[3,128,256]{2,1,0:T(8,128)(2,1)S(1)}, u32[]{:S(2)}, u32[]{:S(2)}) collective-permute-start(bf16[3,128,256]{2,1,0:T(8,128)(2,1)S(1)} %get-tuple-element.93.column_ref), channel_id=1, source_target_pairs={{4,0},{0,4},{12,8},{8,12},{20,16},{16,20},{28,24},{24,28},{5,1},{1... | collective-permute-start | bytes 589832 | tf_op jit(solution)/shard_map/ppermute | solution.py:24
  18.8 8.1 %collective-permute-start.6 = (bf16[3,128,256]{2,1,0:T(8,128)(2,1)S(1)}, bf16[3,128,256]{2,1,0:T(8,128)(2,1)S(1)}, u32[]{:S(2)}, u32[]{:S(2)}) collective-permute-start(bf16[3,128,256]{2,1,0:T(8,128)(2,1)S(1)} %get-tuple-element.93.column_ref), channel_id=1, source_target_pairs={{28,0},{8,4},{4,8},{16,12},{12,16},{24,20},{20,24},{0,28},{29,1},{... | collective-permute-start | bytes 589832 | tf_op jit(solution)/shard_map/ppermute | solution.py:33
  26.9 6.3 %copy-start.2 = (s32[3,4096]{1,0:T(4,128)S(1)}, s32[3,4096]{1,0:T(4,128)}, u32[]{:S(2)}) copy-start(s32[3,4096]{1,0:T(4,128)} %vec_ref.1) | copy-start | bytes 147460
  28.8 6.2 %collective-permute-start.9 = (bf16[80,256]{1,0:T(8,128)(2,1)S(1)}, bf16[80,256]{1,0:T(8,128)(2,1)S(1)}, u32[]{:S(2)}, u32[]{:S(2)}) collective-permute-start(bf16[80,256]{1,0:T(8,128)(2,1)S(1)} %get-tuple-element.98), channel_id=1, source_target_pairs={{24,0},{28,4},{16,8},{20,12},{8,16},{12,20},{0,24},{4,28},{25,1},{... | collective-permute-start | bytes 122888 | tf_op jit(solution)/shard_map/ppermute | solution.py:24
  28.9 6.1 %collective-permute-start.8 = (bf16[80,256]{1,0:T(8,128)(2,1)S(1)}, bf16[80,256]{1,0:T(8,128)(2,1)S(1)}, u32[]{:S(2)}, u32[]{:S(2)}) collective-permute-start(bf16[80,256]{1,0:T(8,128)(2,1)S(1)} %get-tuple-element.98), channel_id=1, source_target_pairs={{16,0},{20,4},{24,8},{28,12},{0,16},{4,20},{8,24},{12,28},{17,1},{... | collective-permute-start | bytes 122888 | tf_op jit(solution)/shard_map/ppermute | solution.py:24
  28.9 6.4 %collective-permute-start.7 = (bf16[80,256]{1,0:T(8,128)(2,1)S(1)}, bf16[80,256]{1,0:T(8,128)(2,1)S(1)}, u32[]{:S(2)}, u32[]{:S(2)}) collective-permute-start(bf16[80,256]{1,0:T(8,128)(2,1)S(1)} %get-tuple-element.98), channel_id=1, source_target_pairs={{8,0},{12,4},{0,8},{4,12},{24,16},{28,20},{16,24},{20,28},{9,1},{1... | collective-permute-start | bytes 122888 | tf_op jit(solution)/shard_map/ppermute | solution.py:24
  35.3 1.5 %collective-permute-start.10 = (bf16[4,80,256]{2,1,0:T(8,128)(2,1)S(1)}, bf16[4,80,256]{2,1,0:T(8,128)(2,1)S(1)}, u32[]{:S(2)}, u32[]{:S(2)}) collective-permute-start(bf16[4,80,256]{2,1,0:T(8,128)(2,1)S(1)} %pad_maximum_fusion.blocks.refs_7_), channel_id=1, source_target_pairs={{4,0},{0,4},{12,8},{8,12},{20,16},{16,20},{28,24},{24,28},{5,1},{1... | collective-permute-start | bytes 491528 | tf_op jit(solution)/shard_map/ppermute | solution.py:24
  38.1 5.8 %collective-permute-start.11 = (bf16[320,128]{1,0:T(8,128)(2,1)S(1)}, bf16[320,128]{1,0:T(8,128)(2,1)S(1)}, u32[]{:S(2)}, u32[]{:S(2)}) collective-permute-start(bf16[320,128]{1,0:T(8,128)(2,1)S(1)} %get-tuple-element.102), channel_id=1, source_target_pairs={{1,0},{0,1},{3,2},{2,3},{5,4},{4,5},{7,6},{6,7},{9,8},{8,9},{11,10... | collective-permute-start | bytes 245768 | tf_op jit(solution)/shard_map/ppermute | solution.py:24
  38.9 5.0 %collective-permute-start.12 = (bf16[320,128]{1,0:T(8,128)(2,1)S(1)}, bf16[320,128]{1,0:T(8,128)(2,1)S(1)}, u32[]{:S(2)}, u32[]{:S(2)}) collective-permute-start(bf16[320,128]{1,0:T(8,128)(2,1)S(1)} %get-tuple-element.102), channel_id=1, source_target_pairs={{2,0},{3,1},{0,2},{1,3},{6,4},{7,5},{4,6},{5,7},{10,8},{11,9},{8,1... | collective-permute-start | bytes 245768 | tf_op jit(solution)/shard_map/ppermute | solution.py:24
  40.0 5.4 %collective-permute-start.13 = (bf16[320,128]{1,0:T(8,128)(2,1)S(1)}, bf16[320,128]{1,0:T(8,128)(2,1)S(1)}, u32[]{:S(2)}, u32[]{:S(2)}) collective-permute-start(bf16[320,128]{1,0:T(8,128)(2,1)S(1)} %get-tuple-element.102), channel_id=1, source_target_pairs={{3,0},{2,1},{1,2},{0,3},{7,4},{6,5},{5,6},{4,7},{11,8},{10,9},{9,1... | collective-permute-start | bytes 245768 | tf_op jit(solution)/shard_map/ppermute | solution.py:24
  46.8 1.5 %collective-permute-start.14 = (bf16[4,80,256]{2,1,0:T(8,128)(2,1)S(1)}, bf16[4,80,256]{2,1,0:T(8,128)(2,1)S(1)}, u32[]{:S(2)}, u32[]{:S(2)}) collective-permute-start(bf16[4,80,256]{2,1,0:T(8,128)(2,1)S(1)} %get-tuple-element.133), channel_id=1, source_target_pairs={{4,0},{0,4},{12,8},{8,12},{20,16},{16,20},{28,24},{24,28},{5,1},{1... | collective-permute-start | bytes 491528 | tf_op jit(solution)/shard_map/ppermute | solution.py:24
  48.3 5.0 %collective-permute-start.15 = (bf16[80,256]{1,0:T(8,128)(2,1)S(1)}, bf16[80,256]{1,0:T(8,128)(2,1)S(1)}, u32[]{:S(2)}, u32[]{:S(2)}) collective-permute-start(bf16[80,256]{1,0:T(8,128)(2,1)S(1)} %get-tuple-element.135), channel_id=1, source_target_pairs={{8,0},{12,4},{0,8},{4,12},{24,16},{28,20},{16,24},{20,28},{9,1},{1... | collective-permute-start | bytes 122888 | tf_op jit(solution)/shard_map/ppermute | solution.py:24
  50.3 5.8 %collective-permute-start.16 = (bf16[80,256]{1,0:T(8,128)(2,1)S(1)}, bf16[80,256]{1,0:T(8,128)(2,1)S(1)}, u32[]{:S(2)}, u32[]{:S(2)}) collective-permute-start(bf16[80,256]{1,0:T(8,128)(2,1)S(1)} %get-tuple-element.136), channel_id=1, source_target_pairs={{16,0},{20,4},{24,8},{28,12},{0,16},{4,20},{8,24},{12,28},{17,1},{... | collective-permute-start | bytes 122888 | tf_op jit(solution)/shard_map/ppermute | solution.py:24
  51.2 5.9 %collective-permute-start.17 = (bf16[80,256]{1,0:T(8,128)(2,1)S(1)}, bf16[80,256]{1,0:T(8,128)(2,1)S(1)}, u32[]{:S(2)}, u32[]{:S(2)}) collective-permute-start(bf16[80,256]{1,0:T(8,128)(2,1)S(1)} %get-tuple-element.137), channel_id=1, source_target_pairs={{24,0},{28,4},{16,8},{20,12},{8,16},{12,20},{0,24},{4,28},{25,1},{... | collective-permute-start | bytes 122888 | tf_op jit(solution)/shard_map/ppermute | solution.py:24
  60.0 7.3 %collective-permute-start.18 = (bf16[3,128,256]{2,1,0:T(8,128)(2,1)S(1)}, bf16[3,128,256]{2,1,0:T(8,128)(2,1)S(1)}, u32[]{:S(2)}, u32[]{:S(2)}) collective-permute-start(bf16[3,128,256]{2,1,0:T(8,128)(2,1)S(1)} %get-tuple-element.139), channel_id=1, source_target_pairs={{28,0},{8,4},{4,8},{16,12},{12,16},{24,20},{20,24},{0,28},{29,1},{... | collective-permute-start | bytes 589832 | tf_op jit(solution)/shard_map/ppermute | solution.py:33
  60.0 7.3 %collective-permute-start.19 = (bf16[3,128,256]{2,1,0:T(8,128)(2,1)S(1)}, bf16[3,128,256]{2,1,0:T(8,128)(2,1)S(1)}, u32[]{:S(2)}, u32[]{:S(2)}) collective-permute-start(bf16[3,128,256]{2,1,0:T(8,128)(2,1)S(1)} %get-tuple-element.143), channel_id=1, source_target_pairs={{4,0},{0,4},{12,8},{8,12},{20,16},{16,20},{28,24},{24,28},{5,1},{1... | collective-permute-start | bytes 589832 | tf_op jit(solution)/shard_map/ppermute | solution.py:24
  70.9 5.0 %collective-permute-start.21 = (f32[16,256]{1,0:T(8,128)S(1)}, f32[16,256]{1,0:T(8,128)S(1)}, u32[]{:S(2)}, u32[]{:S(2)}) collective-permute-start(f32[16,256]{1,0:T(8,128)S(1)} %get-tuple-element.146), channel_id=1, source_target_pairs={{28,0},{8,4},{4,8},{16,12},{12,16},{24,20},{20,24},{0,28},{29,1},{... | collective-permute-start | bytes 49160 | tf_op jit(solution)/shard_map/ppermute | solution.py:33
  72.7 3.3 %collective-permute-start.20 = (f32[16,256]{1,0:T(8,128)S(1)}, f32[16,256]{1,0:T(8,128)S(1)}, u32[]{:S(2)}, u32[]{:S(2)}) collective-permute-start(f32[16,256]{1,0:T(8,128)S(1)} %get-tuple-element.145), channel_id=1, source_target_pairs={{4,0},{0,4},{12,8},{8,12},{20,16},{16,20},{28,24},{24,28},{5,1},{1... | collective-permute-start | bytes 49160 | tf_op jit(solution)/shard_map/ppermute | solution.py:24
  76.0 3.7 %collective-permute-start.24 = (f32[3,256]{1,0:T(4,128)S(1)}, f32[3,256]{1,0:T(4,128)S(1)}, u32[]{:S(2)}, u32[]{:S(2)}) collective-permute-start(f32[3,256]{1,0:T(4,128)S(1)} %get-tuple-element.151), channel_id=1, source_target_pairs={{2,0},{3,1},{0,2},{1,3},{6,4},{7,5},{4,6},{5,7},{10,8},{11,9},{8,1... | collective-permute-start | bytes 9224 | tf_op jit(solution)/shard_map/ppermute | solution.py:42
  76.8 4.5 %collective-permute-start.23 = (f32[3,256]{1,0:T(4,128)S(1)}, f32[3,256]{1,0:T(4,128)S(1)}, u32[]{:S(2)}, u32[]{:S(2)}) collective-permute-start(f32[3,256]{1,0:T(4,128)S(1)} %get-tuple-element.152), channel_id=1, source_target_pairs={{3,0},{2,1},{1,2},{0,3},{7,4},{6,5},{5,6},{4,7},{11,8},{10,9},{9,1... | collective-permute-start | bytes 9224 | tf_op jit(solution)/shard_map/ppermute | solution.py:33
  79.0 3.6 %collective-permute-start.22 = (f32[3,256]{1,0:T(4,128)S(1)}, f32[3,256]{1,0:T(4,128)S(1)}, u32[]{:S(2)}, u32[]{:S(2)}) collective-permute-start(f32[3,256]{1,0:T(4,128)S(1)} %get-tuple-element.150), channel_id=1, source_target_pairs={{1,0},{0,1},{3,2},{2,3},{5,4},{4,5},{7,6},{6,7},{9,8},{8,9},{11,10... | collective-permute-start | bytes 9224 | tf_op jit(solution)/shard_map/ppermute | solution.py:24

commit v19 on v18

--- a/solution.py
+++ b/solution.py
@@ -445,7 +445,7 @@
 def second_back_kernel(slots, scale, count, hot_ref, weight_ref, turn_high, turn_low, charge_ref,
                        sums_ref, gate_ref, full_charge_ref, energy_ref, slope_ref, *refs):
     folds, refs = refs[:count], refs[count:]
-    site_ref, long_ref, cotangent_ref, grad_ref, term_ref, beyond_ref, pair_ref = refs
+    site_ref, long_ref, cotangent_ref, grad_ref, term_ref, beyond_ref = refs
     atoms = gate_ref.shape[1]
     total = folds[0][...].astype(F32)
     for part in folds[1:]:
@@ -478,6 +478,10 @@
     for b in range(3):
         start = (3 + b) * atoms
         beyond_ref[b] = dot(term_ref[...], hot_ref[:, start : start + atoms]).astype(BF16)
+
+
+def second_pair_kernel(hot_ref, term_ref, pair_ref):
+    atoms = pair_ref.shape[2]
     for b in range(3):
         pair_ref[b] = dot(term_ref[...], hot_ref[:, b * atoms : (b + 1) * atoms]).astype(BF16)
 
@@ -1015,7 +1019,7 @@
     )
     folds = [folds[0]] + [paired(folds[d], "gx", 2 * d) for d in range(1, half)]
 
-    site, long, cotangent, grads, term, to_beyond, to_pair = run(
+    site, long, cotangent, grads, term, to_beyond = run(
         functools.partial(second_back_kernel, slots, scale, half),
         [
             shape(1, 1, atoms),
@@ -1024,11 +1028,17 @@
             shape(4, features, atoms),
             shape(features, edges, dtype=BF16),
             shape(3, features, atoms, dtype=BF16),
-            shape(3, features, atoms, dtype=BF16),
         ],
         [hot_back, edge_weights, turn_high, turn_low, charge_pair, sums_two, gate_two, charge,
          energy, energy_slope] + folds,
         name="second_back",
+    )
+    (to_pair,) = run(
+        second_pair_kernel,
+        [shape(3, features, atoms, dtype=BF16)],
+        [hot_back, term],
+        flops=1_000_000,
+        name="second_pair",
     )
     from_pair, from_beyond = paired(to_pair, "gx", 1), beyond(to_beyond, "gx")
     (hot_middle,) = run(

time: 83.4 us -> 82.7 us (level)
  waiting for transfers between devices: 25.1 us -> 24.2 us
    ppermute x6, waiting for transfers between devices: 13.5 us -> 12.6 us  [beyond(): lax.ppermute(block, axis, [(other_side(i, count), i) for i in range(count)])]
    pallas_call x22 -> x23, Pallas kernels: 27.4 us -> 27.5 us  [run(): pl.pallas_call(kernel, out_shape=outs, in_specs=specs, out_specs=[whole()...]
  transfers between devices with their start and end apart: 25 -> 25, of which waited for: 15 -> 15; matrix products, arithmetic and copies ran while one was open for 0% -> 0% of each run, Pallas kernels for 16% -> 17%
where the time goes in v19:
time: 82.7 us; the launch traced here: 82.5 us
  starting transfers between devices  27.6 us (33%)
  Pallas kernels  27.5 us (33%)
  waiting for transfers between devices  24.2 us (29%)
  local copies, waits for them, and re-layouts  2.07 us (3%)
  between operations  0.97 us (1%)
    pallas_call x23, Pallas kernels, run(): pl.pallas_call(kernel, out_shape=outs, in_specs=specs, out_specs=[whole()...  27.5 us
    ppermute x17, starting transfers between devices, paired(): lax.ppermute(block, axis, [(i ^ mask, i) for i in range(lax.axis_size(axi...  14.5 us
    ppermute x6, waiting for transfers between devices, beyond(): lax.ppermute(block, axis, [(other_side(i, count), i) for i in range(count)])  12.6 us
    ppermute x17, waiting for transfers between devices, paired(): lax.ppermute(block, axis, [(i ^ mask, i) for i in range(lax.axis_size(axi...  11.5 us
    ppermute x6, starting transfers between devices, beyond(): lax.ppermute(block, axis, [(other_side(i, count), i) for i in range(count)])  9.25 us
    ppermute x2, starting transfers between devices, far(): return lax.ppermute(block, axis, route)  3.94 us
    unnamed x27, local copies, waits for them, and re-layouts  2 us
  transfers between devices with their start and end apart: 25, of which 15 were waited for; matrix products, arithmetic and copies ran while one was open for 0% of the time, Pallas kernels for 17%

profile of v19, /device:TPU:0, one launch (start us, length us, event | category | flops | bytes accessed | tf_op | source)
XLA Modules:
  0.0 82.5 jit_solution(8810838229026235829)
XLA Ops:
  0.6 0.1 pad_add_fusion
  0.7 0.1 broadcast_in_dim.4.place_ref
  0.8 0.7 copy-done.9
  1.5 0.7 copy-done.10
  2.2 3.0 %collective-permute-start.2 = (f32[8,128]{1,0:T(8,128)S(1)}, f32[8,128]{1,0:T(8,128)S(1)}, u32[]{:S(2)}, u32[]{:S(2)}) collective-permute-start(f32[8,128]{1,0:T(8,128)S(1)} %pack.1.first_ref), channel_id=1, source_target_pairs={{2,0},{3,1},{0,2},{1,3},{6,4},{7,5},{4,6},{5,7},{10,8},{11,9},{8,1... | collective-permute-start | bytes 12296 | tf_op jit(solution)/shard_map/ppermute | solution.py:42
  5.3 0.1 pack_more.1.own_ref
  5.4 1.6 %collective-permute-start = (f32[40,128]{1,0:T(8,128)S(1)}, f32[40,128]{1,0:T(8,128)S(1)}, u32[]{:S(2)}, u32[]{:S(2)}) collective-permute-start(f32[40,128]{1,0:T(8,128)S(1)} %pack_more.1.own_ref), channel_id=1, source_target_pairs={{3,0},{2,1},{1,2},{0,3},{7,4},{6,5},{5,6},{4,7},{11,8},{10,9},{9,1... | collective-permute-start | bytes 61448 | tf_op jit(solution)/shard_map/ppermute | solution.py:33
  6.9 0.5 collective-permute-start.1
  7.5 3.2 %collective-permute-done.1.y_pair_ref = f32[40,128]{1,0:T(8,128)S(1)} collective-permute-done((f32[40,128]{1,0:T(8,128)S(1)}, f32[40,128]{1,0:T(8,128)S(1)}, u32[]{:S(2)}, u32[]{:S(2)}) %collective-permute-start.1) | collective-permute-done | bytes 20512 | tf_op jit(solution)/shard_map/ppermute | solution.py:24
  10.7 1.8 %collective-permute-start.3 = (f32[5,8,128]{2,1,0:T(8,128)S(1)}, f32[5,8,128]{2,1,0:T(8,128)S(1)}, u32[]{:S(2)}, u32[]{:S(2)}) collective-permute-start(f32[5,8,128]{2,1,0:T(8,128)S(1)} %constant_dynamic-update-slice_fusion.column_ref.cell_ref), channel_id=1, source_target_pairs={{28,0},{8,4},{4,8},{16,12},{12,16},{24,20},{20,24},{0,28},{29,1},{... | collective-permute-start | bytes 61448 | tf_op jit(solution)/shard_map/ppermute | solution.py:33
  12.6 0.3 prep_first.1
  12.9 0.3 prep_second.1
  13.2 2.6 %collective-permute-done.3.beyond_ref = f32[5,8,128]{2,1,0:T(8,128)S(1)} collective-permute-done((f32[5,8,128]{2,1,0:T(8,128)S(1)}, f32[5,8,128]{2,1,0:T(8,128)S(1)}, u32[]{:S(2)}, u32[]{:S(2)}) %collective-permute-start.3) | collective-permute-done | bytes 20512 | tf_op jit(solution)/shard_map/ppermute | solution.py:33
  15.8 2.9 %first.1 = (bf16[3,128,256]{2,1,0:T(8,128)(2,1)S(1)}, s32[3,3072]{1,0:T(4,128)S(1)}, f32[3,8,3072]{2,1,0:T(8,128)S(1)}, f32[3,8,3072]{2,1,0:T(8,128)S(1)}, f32[3...) custom-call(s32[2,8,128]{2,1,0:T(8,128)S(1)} %broadcast_in_dim.4.place_ref, ...), custom_call_target="tpu_custom_call" | custom-call | flops 10000000 | bytes 1000000 | tf_op jit(solution)/shard_map/first/pallas_call | solution.py:55
  18.7 0.1 collective-permute-start.5
  18.8 1.9 %collective-permute-start.6 = (bf16[3,128,256]{2,1,0:T(8,128)(2,1)S(1)}, bf16[3,128,256]{2,1,0:T(8,128)(2,1)S(1)}, u32[]{:S(2)}, u32[]{:S(2)}) collective-permute-start(bf16[3,128,256]{2,1,0:T(8,128)(2,1)S(1)} %get-tuple-element.92.column_ref), channel_id=1, source_target_pairs={{28,0},{8,4},{4,8},{16,12},{12,16},{24,20},{20,24},{0,28},{29,1},{... | collective-permute-start | bytes 589832 | tf_op jit(solution)/shard_map/ppermute | solution.py:33
  20.7 1.7 %second_near.1 = (f32[4,128,3072]{2,1,0:T(8,128)S(1)}, f32[128,3072]{1,0:T(8,128)S(1)}) custom-call(s32[3,3072]{1,0:T(4,128)S(1)} %get-tuple-element.80.ids_ref, f32[3,8,3072]{2,1,0:T(8,128)S(1)} %get-tuple-element.81.basis_ref, f32[3,8,3072]{2,1,0:T(8,128)S(1)} %get-tuple-element.83.unit_ref, bf16[2,128,32]{2,1,0:T(8,128)(2,1)S(1)} %get-tuple-element.91.left_ref, ...), custom_call_target="tpu_custom_call" | custom-call | flops 2000000000 | bytes 1000000 | tf_op jit(solution)/shard_map/second_near/pallas_call | solution.py:55
  22.4 1.0 %hot_beyond.1.hot_ref = bf16[768,3072]{1,0:T(8,128)(2,1)S(1)} custom-call(s32[3,3072]{1,0:T(4,128)S(1)} %get-tuple-element.80.ids_ref, f32[128,3072]{1,0:T(8,128)S(1)} %get-tuple-element.93.near_ref), custom_call_target="tpu_custom_call" | custom-call | flops 1000000 | bytes 1000000 | tf_op jit(solution)/shard_map/hot_beyond/pallas_call | solution.py:55
  23.4 0.8 second_side.1.near_ref
  24.2 2.7 %collective-permute-done.6.beyond_ref = bf16[3,128,256]{2,1,0:T(8,128)(2,1)S(1)} collective-permute-done((bf16[3,128,256]{2,1,0:T(8,128)(2,1)S(1)}, bf16[3,128,256]{2,1,0:T(8,128)(2,1)S(1)}, u32[]{:S(2)}, u32[]{:S(2)}) %collective-permute-start.6) | collective-permute-done | bytes 196640 | tf_op jit(solution)/shard_map/ppermute | solution.py:33
  26.9 1.9 %second.1 = (bf16[128,3072]{1,0:T(8,128)(2,1)S(1)}, f32[3,128,256]{2,1,0:T(8,128)S(1)}, f32[128,256]{1,0:T(8,128)S(1)}, bf16[80,256]{1,0:T(8,128)(2,1)S(1)}, f32...) custom-call(bf16[768,3072]{1,0:T(8,128)(2,1)S(1)} %hot_beyond.1.hot_ref, f32[4,128,3072]{2,1,0:T(8,128)S(1)} %get-tuple-element.94.weight_ref, ...), custom_call_target="tpu_custom_call" | custom-call | flops 10000000 | bytes 1000000 | tf_op jit(solution)/shard_map/second/pallas_call | solution.py:55
  28.8 0.1 collective-permute-start.9
  28.9 0.1 collective-permute-start.8
  28.9 4.3 %collective-permute-start.7 = (bf16[80,256]{1,0:T(8,128)(2,1)S(1)}, bf16[80,256]{1,0:T(8,128)(2,1)S(1)}, u32[]{:S(2)}, u32[]{:S(2)}) collective-permute-start(bf16[80,256]{1,0:T(8,128)(2,1)S(1)} %get-tuple-element.97), channel_id=1, source_target_pairs={{8,0},{12,4},{0,8},{4,12},{24,16},{28,20},{16,24},{20,28},{9,1},{1... | collective-permute-start | bytes 122888 | tf_op jit(solution)/shard_map/ppermute | solution.py:24
  33.2 0.8 green.1.refs_0_
  34.0 0.9 %collective-permute-done.9 = bf16[80,256]{1,0:T(8,128)(2,1)S(1)} collective-permute-done((bf16[80,256]{1,0:T(8,128)(2,1)S(1)}, bf16[80,256]{1,0:T(8,128)(2,1)S(1)}, u32[]{:S(2)}, u32[]{:S(2)}) %collective-permute-start.9) | collective-permute-done | bytes 40992 | tf_op jit(solution)/shard_map/ppermute | solution.py:24
  35.0 0.3 collective-permute-done.7
  35.3 0.1 collective-permute-start.10
  35.4 1.2 %structure_near.1 = (f32[32,1024]{1,0:T(8,128)S(1)}, f32[32,1024]{1,0:T(8,128)S(1)}, f32[8,1024]{1,0:T(8,128)S(1)}, f32[8,1024]{1,0:T(8,128)S(1)}, bf16[640,1024...) custom-call(s32[2,8,128]{2,1,0:T(8,128)S(1)} %broadcast_in_dim.4.place_ref, ...), custom_call_target="tpu_custom_call" | custom-call | flops 1000000000 | bytes 1000000 | tf_op jit(solution)/shard_map/structure_near/pallas_call | solution.py:55
  36.6 0.2 collective-permute-done.10.blocks.refs_11_
  36.8 1.3 %structure_far.1 = (f32[32,1024]{1,0:T(8,128)S(1)}, f32[32,1024]{1,0:T(8,128)S(1)}, f32[8,1024]{1,0:T(8,128)S(1)}, f32[8,1024]{1,0:T(8,128)S(1)}, bf16[640,1024]...) custom-call(s32[2,8,128]{2,1,0:T(8,128)S(1)} %broadcast_in_dim.4.place_r, ...), custom_call_target="tpu_custom_call" | custom-call | flops 10000000 | bytes 1000000 | tf_op jit(solution)/shard_map/structure_far/pallas_call | solution.py:55
  38.1 0.9 %collective-permute-start.11 = (bf16[320,128]{1,0:T(8,128)(2,1)S(1)}, bf16[320,128]{1,0:T(8,128)(2,1)S(1)}, u32[]{:S(2)}, u32[]{:S(2)}) collective-permute-start(bf16[320,128]{1,0:T(8,128)(2,1)S(1)} %get-tuple-element.101), channel_id=1, source_target_pairs={{1,0},{0,1},{3,2},{2,3},{5,4},{4,5},{7,6},{6,7},{9,8},{8,9},{11,10... | collective-permute-start | bytes 245768 | tf_op jit(solution)/shard_map/ppermute | solution.py:24
  38.9 1.1 %collective-permute-start.12 = (bf16[320,128]{1,0:T(8,128)(2,1)S(1)}, bf16[320,128]{1,0:T(8,128)(2,1)S(1)}, u32[]{:S(2)}, u32[]{:S(2)}) collective-permute-start(bf16[320,128]{1,0:T(8,128)(2,1)S(1)} %get-tuple-element.101), channel_id=1, source_target_pairs={{2,0},{3,1},{0,2},{1,3},{6,4},{7,5},{4,6},{5,7},{10,8},{11,9},{8,1... | collective-permute-start | bytes 245768 | tf_op jit(solution)/shard_map/ppermute | solution.py:24
  40.0 1.6 %collective-permute-start.13 = (bf16[320,128]{1,0:T(8,128)(2,1)S(1)}, bf16[320,128]{1,0:T(8,128)(2,1)S(1)}, u32[]{:S(2)}, u32[]{:S(2)}) collective-permute-start(bf16[320,128]{1,0:T(8,128)(2,1)S(1)} %get-tuple-element.101), channel_id=1, source_target_pairs={{3,0},{2,1},{1,2},{0,3},{7,4},{6,5},{5,6},{4,7},{11,8},{10,9},{9,1... | collective-permute-start | bytes 245768 | tf_op jit(solution)/shard_map/ppermute | solution.py:24
  41.6 2.3 %hot_back.1.hot_ref = bf16[3072,1536]{1,0:T(8,128)(2,1)S(1)} custom-call(s32[3,3072]{1,0:T(4,128)S(1)} %get-tuple-element.80.ids_ref), custom_call_target="tpu_custom_call" | custom-call | flops 2000000000 | bytes 1000000 | tf_op jit(solution)/shard_map/hot_back/pallas_call | solution.py:55
  43.9 1.6 %collective-permute-done.13.refs_4_ = bf16[320,128]{1,0:T(8,128)(2,1)S(1)} collective-permute-done((bf16[320,128]{1,0:T(8,128)(2,1)S(1)}, bf16[320,128]{1,0:T(8,128)(2,1)S(1)}, u32[]{:S(2)}, u32[]{:S(2)}) %collective-permute-start.13) | collective-permute-done | bytes 81952 | tf_op jit(solution)/shard_map/ppermute | solution.py:24
  45.5 1.3 %fold_far.1 = (bf16[4,80,256]{2,1,0:T(8,128)(2,1)S(1)}, f32[640,64]{1,0:T(8,128)S(1)}) custom-call(s32[2,8,128]{2,1,0:T(8,128)S(1)} %broadcast_in_dim.4.place_ref, f32[320,128]{1,0:T(8,128)S(1)} %green.1.refs_0_, f32[320,128]{1,0:T(8,128)S(1)} %get-tuple-element.115.refs_1_, bf16[320,128]{1,0:T(8,128)(2,1)S(1)} %collective-permute-done.11.refs_2_, ...), custom_call_target="tpu_custom_call" | custom-call | flops 10000000 | bytes 1000000 | tf_op jit(solution)/shard_map/fold_far/pallas_call | solution.py:55
  46.8 0.1 collective-permute-start.14
  46.9 1.2 %fold_near.1.near_ref = f32[4,80,256]{2,1,0:T(8,128)S(1)} custom-call(s32[2,8,128]{2,1,0:T(8,128)S(1)} %broadcast_in_dim.4.place_ref, f32[640,64]{1,0:T(8,128)S(1)} %get-tuple-element.125.refs_0_, f32[32,1024]{1,0:T(8,128)S(1)} %get-tuple-element.126.refs_1_, f32[32,1024]{1,0:T(8,128)S(1)} %get-tuple-element.127.refs_2_, ...), custom_call_target="tpu_custom_call" | custom-call | flops 1000000000 | bytes 1000000 | tf_op jit(solution)/shard_map/fold_near/pallas_call | solution.py:55
  48.1 0.2 collective-permute-done.14.far_ref
  48.3 0.1 fold_join.1
  48.3 2.0 %collective-permute-start.15 = (bf16[80,256]{1,0:T(8,128)(2,1)S(1)}, bf16[80,256]{1,0:T(8,128)(2,1)S(1)}, u32[]{:S(2)}, u32[]{:S(2)}) collective-permute-start(bf16[80,256]{1,0:T(8,128)(2,1)S(1)} %get-tuple-element.134), channel_id=1, source_target_pairs={{8,0},{12,4},{0,8},{4,12},{24,16},{28,20},{16,24},{20,28},{9,1},{1... | collective-permute-start | bytes 122888 | tf_op jit(solution)/shard_map/ppermute | solution.py:24
  50.3 0.9 %collective-permute-start.16 = (bf16[80,256]{1,0:T(8,128)(2,1)S(1)}, bf16[80,256]{1,0:T(8,128)(2,1)S(1)}, u32[]{:S(2)}, u32[]{:S(2)}) collective-permute-start(bf16[80,256]{1,0:T(8,128)(2,1)S(1)} %get-tuple-element.135), channel_id=1, source_target_pairs={{16,0},{20,4},{24,8},{28,12},{0,16},{4,20},{8,24},{12,28},{17,1},{... | collective-permute-start | bytes 122888 | tf_op jit(solution)/shard_map/ppermute | solution.py:24
  51.2 1.5 %collective-permute-start.17 = (bf16[80,256]{1,0:T(8,128)(2,1)S(1)}, bf16[80,256]{1,0:T(8,128)(2,1)S(1)}, u32[]{:S(2)}, u32[]{:S(2)}) collective-permute-start(bf16[80,256]{1,0:T(8,128)(2,1)S(1)} %get-tuple-element.136), channel_id=1, source_target_pairs={{24,0},{28,4},{16,8},{20,12},{8,16},{12,20},{0,24},{4,28},{25,1},{... | collective-permute-start | bytes 122888 | tf_op jit(solution)/shard_map/ppermute | solution.py:24
  52.8 0.5 readout.1
  53.3 2.8 %collective-permute-done.16.refs_2_ = bf16[80,256]{1,0:T(8,128)(2,1)S(1)} collective-permute-done((bf16[80,256]{1,0:T(8,128)(2,1)S(1)}, bf16[80,256]{1,0:T(8,128)(2,1)S(1)}, u32[]{:S(2)}, u32[]{:S(2)}) %collective-permute-start.16) | collective-permute-done | bytes 40992 | tf_op jit(solution)/shard_map/ppermute | solution.py:24
  56.1 1.0 %collective-permute-done.17.refs_3_ = bf16[80,256]{1,0:T(8,128)(2,1)S(1)} collective-permute-done((bf16[80,256]{1,0:T(8,128)(2,1)S(1)}, bf16[80,256]{1,0:T(8,128)(2,1)S(1)}, u32[]{:S(2)}, u32[]{:S(2)}) %collective-permute-start.17) | collective-permute-done | bytes 40992 | tf_op jit(solution)/shard_map/ppermute | solution.py:24
  57.1 2.2 %second_back.1 = (f32[1,1,256]{2,1,0:T(1,128)}, f32[8,256]{1,0:T(8,128)S(1)}, f32[128,256]{1,0:T(8,128)S(1)}, f32[4,128,256]{2,1,0:T(8,128)S(1)}, bf16[128,3072]...) custom-call(bf16[3072,1536]{1,0:T(8,128)(2,1)S(1)} %hot_back.1.hot_ref, ...), custom_call_target="tpu_custom_call" | custom-call | flops 10000000 | bytes 1000000 | tf_op jit(solution)/shard_map/second_back/pallas_call | solution.py:55
  59.3 0.8 second_pair.1
  60.1 0.8 collective-permute-start.19
  60.9 1.3 %hot_middle.1.hot_ref = bf16[3072,768]{1,0:T(8,128)(2,1)S(1)} custom-call(s32[3,3072]{1,0:T(4,128)S(1)} %get-tuple-element.80.ids_ref), custom_call_target="tpu_custom_call" | custom-call | flops 1000000000 | bytes 1000000 | tf_op jit(solution)/shard_map/hot_middle/pallas_call | solution.py:55
  62.2 0.8 second_middle.1.middle_ref
  63.1 1.2 %second_edge.1.edge_ref = f32[32,3072]{1,0:T(8,128)S(1)} custom-call(bf16[2,16,256]{2,1,0:T(8,128)(2,1)S(1)} %get-tuple-element.90.back_ref, bf16[128,3072]{1,0:T(8,128)(2,1)S(1)} %get-tuple-element.96.feature_ref, f32[4,128,256]{2,1,0:T(8,128)S(1)} %get-tuple-element.137.grad_ref), custom_call_target="tpu_custom_call" | custom-call | flops 1000000000 | bytes 1000000 | tf_op jit(solution)/shard_map/second_edge/pallas_call | solution.py:55
  64.3 2.3 %collective-permute-done.18.from_beyond = bf16[3,128,256]{2,1,0:T(8,128)(2,1)S(1)} collective-permute-done((bf16[3,128,256]{2,1,0:T(8,128)(2,1)S(1)}, bf16[3,128,256]{2,1,0:T(8,128)(2,1)S(1)}, u32[]{:S(2)}, u32[]{:S(2)}) %collective-permute-start.18) | collective-permute-done | bytes 196640 | tf_op jit(solution)/shard_map/ppermute | solution.py:33
  66.6 3.6 %first_back.1 = (f32[16,256]{1,0:T(8,128)S(1)}, f32[16,256]{1,0:T(8,128)S(1)}, f32[16,256]{1,0:T(8,128)S(1)}) custom-call(s32[3,3072]{1,0:T(4,128)S(1)} %get-tuple-element.80.ids_ref, f32[3,8,3072]{2,1,0:T(8,128)S(1)} %get-tuple-element.81.basis_ref, f32[3,8,3072]{2,1,0:T(8,128)S(1)} %get-tuple-element.82.slope_ref, ...), custom_call_target="tpu_custom_call" | custom-call | flops 10000000 | bytes 1000000 | tf_op jit(solution)/shard_map/first_back/pallas_call | solution.py:55
  70.2 1.8 %collective-permute-start.21 = (f32[16,256]{1,0:T(8,128)S(1)}, f32[16,256]{1,0:T(8,128)S(1)}, u32[]{:S(2)}, u32[]{:S(2)}) collective-permute-start(f32[16,256]{1,0:T(8,128)S(1)} %get-tuple-element.144), channel_id=1, source_target_pairs={{28,0},{8,4},{4,8},{16,12},{12,16},{24,20},{20,24},{0,28},{29,1},{... | collective-permute-start | bytes 49160 | tf_op jit(solution)/shard_map/ppermute | solution.py:33
  72.0 3.2 %collective-permute-done.21 = f32[16,256]{1,0:T(8,128)S(1)} collective-permute-done((f32[16,256]{1,0:T(8,128)S(1)}, f32[16,256]{1,0:T(8,128)S(1)}, u32[]{:S(2)}, u32[]{:S(2)}) %collective-permute-start.21) | collective-permute-done | bytes 16416 | tf_op jit(solution)/shard_map/ppermute | solution.py:33
  75.2 0.9 %collective-permute-start.24 = (f32[3,256]{1,0:T(4,128)S(1)}, f32[3,256]{1,0:T(4,128)S(1)}, u32[]{:S(2)}, u32[]{:S(2)}) collective-permute-start(f32[3,256]{1,0:T(4,128)S(1)} %get-tuple-element.149), channel_id=1, source_target_pairs={{2,0},{3,1},{0,2},{1,3},{6,4},{7,5},{4,6},{5,7},{10,8},{11,9},{8,1... | collective-permute-start | bytes 9224 | tf_op jit(solution)/shard_map/ppermute | solution.py:42
  76.1 2.2 %collective-permute-start.23 = (f32[3,256]{1,0:T(4,128)S(1)}, f32[3,256]{1,0:T(4,128)S(1)}, u32[]{:S(2)}, u32[]{:S(2)}) collective-permute-start(f32[3,256]{1,0:T(4,128)S(1)} %get-tuple-element.150), channel_id=1, source_target_pairs={{3,0},{2,1},{1,2},{0,3},{7,4},{6,5},{5,6},{4,7},{11,8},{10,9},{9,1... | collective-permute-start | bytes 9224 | tf_op jit(solution)/shard_map/ppermute | solution.py:33
  78.3 0.5 collective-permute-start.22
  78.8 0.1 collective-permute-done.24
  78.9 1.7 %collective-permute-done.23 = f32[3,256]{1,0:T(4,128)S(1)} collective-permute-done((f32[3,256]{1,0:T(4,128)S(1)}, f32[3,256]{1,0:T(4,128)S(1)}, u32[]{:S(2)}, u32[]{:S(2)}) %collective-permute-start.23) | collective-permute-done | bytes 3104 | tf_op jit(solution)/shard_map/ppermute | solution.py:33
  80.6 1.3 %collective-permute-done.22 = f32[3,256]{1,0:T(4,128)S(1)} collective-permute-done((f32[3,256]{1,0:T(4,128)S(1)}, f32[3,256]{1,0:T(4,128)S(1)}, u32[]{:S(2)}, u32[]{:S(2)}) %collective-permute-start.22) | collective-permute-done | bytes 3104 | tf_op jit(solution)/shard_map/ppermute | solution.py:24
  81.9 0.6 copy.13
  (43 shorter events, 0.1 us)
Async XLA Ops:
  0.8 0.7 copy-start.9
  1.5 0.7 copy-start.10
  2.1 3.1 %copy-start.5 = (s32[1,1,256,12]{2,1,3,0:T(1,128)S(1)}, s32[1,1,256,12]{2,1,3,0:T(1,128)}, u32[]{:S(2)}) copy-start(s32[1,1,256,12]{2,1,3,0:T(1,128)} %param.13) | copy-start | bytes 36868
  2.2 3.1 %copy-start.7 = (s32[1,1,256]{2,1,0:T(1,128)S(1)}, s32[1,1,256]{2,1,0:T(1,128)}, u32[]{:S(2)}) copy-start(s32[1,1,256]{2,1,0:T(1,128)} %count_ref.1) | copy-start | bytes 3076
  2.2 10.4 %copy-start = (f32[2,2,128,128]{3,2,1,0:T(8,128)S(1)}, f32[2,2,128,128]{3,2,1,0:T(8,128)}, u32[]{:S(2)}) copy-start(f32[2,2,128,128]{3,2,1,0:T(8,128)} %mixing_in.1) | copy-start | bytes 786436
  2.2 10.4 %copy-start.4 = (f32[2,2,8,128]{3,2,1,0:T(8,128)S(1)}, f32[2,2,8,128]{3,2,1,0:T(8,128)}, u32[]{:S(2)}) copy-start(f32[2,2,8,128]{3,2,1,0:T(8,128)} %radial_in.1) | copy-start | bytes 49156
  2.2 10.4 %copy-start.6 = (f32[6,128]{1,0:T(8,128)S(1)}, f32[6,128]{1,0:T(8,128)}, u32[]{:S(2)}) copy-start(f32[6,128]{1,0:T(8,128)} %embed_in.1) | copy-start | bytes 9220
  2.2 10.7 %copy-start.1 = (f32[128,128]{1,0:T(8,128)S(1)}, f32[128,128]{1,0:T(8,128)}, u32[]{:S(2)}) copy-start(f32[128,128]{1,0:T(8,128)} %hidden_in.1) | copy-start | bytes 196612
  2.2 10.7 %copy-start.3 = (f32[128,64]{0,1:T(8,128)S(1)}, f32[128,64]{0,1:T(8,128)}, u32[]{:S(2)}) copy-start(f32[128,64]{0,1:T(8,128)} %param.20) | copy-start | bytes 98308
  2.2 10.7 %copy-start.8 = (f32[128]{0:T(128)S(1)}, f32[128]{0:T(128)}, u32[]{:S(2)}) copy-start(f32[128]{0:T(128)} %param.19) | copy-start | bytes 1540
  2.2 5.3 %collective-permute-start.2 = (f32[8,128]{1,0:T(8,128)S(1)}, f32[8,128]{1,0:T(8,128)S(1)}, u32[]{:S(2)}, u32[]{:S(2)}) collective-permute-start(f32[8,128]{1,0:T(8,128)S(1)} %pack.1.first_ref), channel_id=1, source_target_pairs={{2,0},{3,1},{0,2},{1,3},{6,4},{7,5},{4,6},{5,7},{10,8},{11,9},{8,1... | collective-permute-start | bytes 12296 | tf_op jit(solution)/shard_map/ppermute | solution.py:42
  5.4 5.3 %collective-permute-start = (f32[40,128]{1,0:T(8,128)S(1)}, f32[40,128]{1,0:T(8,128)S(1)}, u32[]{:S(2)}, u32[]{:S(2)}) collective-permute-start(f32[40,128]{1,0:T(8,128)S(1)} %pack_more.1.own_ref), channel_id=1, source_target_pairs={{3,0},{2,1},{1,2},{0,3},{7,4},{6,5},{5,6},{4,7},{11,8},{10,9},{9,1... | collective-permute-start | bytes 61448 | tf_op jit(solution)/shard_map/ppermute | solution.py:33
  6.9 3.8 %collective-permute-start.1 = (f32[40,128]{1,0:T(8,128)S(1)}, f32[40,128]{1,0:T(8,128)S(1)}, u32[]{:S(2)}, u32[]{:S(2)}) collective-permute-start(f32[40,128]{1,0:T(8,128)S(1)} %pack_more.1.own_ref), channel_id=1, source_target_pairs={{1,0},{0,1},{3,2},{2,3},{5,4},{4,5},{7,6},{6,7},{9,8},{8,9},{11,10... | collective-permute-start | bytes 61448 | tf_op jit(solution)/shard_map/ppermute | solution.py:24
  10.7 5.1 %collective-permute-start.3 = (f32[5,8,128]{2,1,0:T(8,128)S(1)}, f32[5,8,128]{2,1,0:T(8,128)S(1)}, u32[]{:S(2)}, u32[]{:S(2)}) collective-permute-start(f32[5,8,128]{2,1,0:T(8,128)S(1)} %constant_dynamic-update-slice_fusion.column_ref.cell_ref), channel_id=1, source_target_pairs={{28,0},{8,4},{4,8},{16,12},{12,16},{24,20},{20,24},{0,28},{29,1},{... | collective-permute-start | bytes 61448 | tf_op jit(solution)/shard_map/ppermute | solution.py:33
  12.6 3.3 %collective-permute-start.4 = (f32[5,8,128]{2,1,0:T(8,128)S(1)}, f32[5,8,128]{2,1,0:T(8,128)S(1)}, u32[]{:S(2)}, u32[]{:S(2)}) collective-permute-start(f32[5,8,128]{2,1,0:T(8,128)S(1)} %constant_dynamic-update-slice_fusion.column_ref.cell_ref), channel_id=1, source_target_pairs={{4,0},{0,4},{12,8},{8,12},{20,16},{16,20},{28,24},{24,28},{5,1},{1... | collective-permute-start | bytes 61448 | tf_op jit(solution)/shard_map/ppermute | solution.py:24
  18.7 4.7 %collective-permute-start.5 = (bf16[3,128,256]{2,1,0:T(8,128)(2,1)S(1)}, bf16[3,128,256]{2,1,0:T(8,128)(2,1)S(1)}, u32[]{:S(2)}, u32[]{:S(2)}) collective-permute-start(bf16[3,128,256]{2,1,0:T(8,128)(2,1)S(1)} %get-tuple-element.92.column_ref), channel_id=1, source_target_pairs={{4,0},{0,4},{12,8},{8,12},{20,16},{16,20},{28,24},{24,28},{5,1},{1... | collective-permute-start | bytes 589832 | tf_op jit(solution)/shard_map/ppermute | solution.py:24
  18.8 8.1 %collective-permute-start.6 = (bf16[3,128,256]{2,1,0:T(8,128)(2,1)S(1)}, bf16[3,128,256]{2,1,0:T(8,128)(2,1)S(1)}, u32[]{:S(2)}, u32[]{:S(2)}) collective-permute-start(bf16[3,128,256]{2,1,0:T(8,128)(2,1)S(1)} %get-tuple-element.92.column_ref), channel_id=1, source_target_pairs={{28,0},{8,4},{4,8},{16,12},{12,16},{24,20},{20,24},{0,28},{29,1},{... | collective-permute-start | bytes 589832 | tf_op jit(solution)/shard_map/ppermute | solution.py:33
  26.9 6.3 %copy-start.2 = (s32[3,4096]{1,0:T(4,128)S(1)}, s32[3,4096]{1,0:T(4,128)}, u32[]{:S(2)}) copy-start(s32[3,4096]{1,0:T(4,128)} %vec_ref.1) | copy-start | bytes 147460
  28.8 6.2 %collective-permute-start.9 = (bf16[80,256]{1,0:T(8,128)(2,1)S(1)}, bf16[80,256]{1,0:T(8,128)(2,1)S(1)}, u32[]{:S(2)}, u32[]{:S(2)}) collective-permute-start(bf16[80,256]{1,0:T(8,128)(2,1)S(1)} %get-tuple-element.97), channel_id=1, source_target_pairs={{24,0},{28,4},{16,8},{20,12},{8,16},{12,20},{0,24},{4,28},{25,1},{... | collective-permute-start | bytes 122888 | tf_op jit(solution)/shard_map/ppermute | solution.py:24
  28.9 6.1 %collective-permute-start.8 = (bf16[80,256]{1,0:T(8,128)(2,1)S(1)}, bf16[80,256]{1,0:T(8,128)(2,1)S(1)}, u32[]{:S(2)}, u32[]{:S(2)}) collective-permute-start(bf16[80,256]{1,0:T(8,128)(2,1)S(1)} %get-tuple-element.97), channel_id=1, source_target_pairs={{16,0},{20,4},{24,8},{28,12},{0,16},{4,20},{8,24},{12,28},{17,1},{... | collective-permute-start | bytes 122888 | tf_op jit(solution)/shard_map/ppermute | solution.py:24
  28.9 6.4 %collective-permute-start.7 = (bf16[80,256]{1,0:T(8,128)(2,1)S(1)}, bf16[80,256]{1,0:T(8,128)(2,1)S(1)}, u32[]{:S(2)}, u32[]{:S(2)}) collective-permute-start(bf16[80,256]{1,0:T(8,128)(2,1)S(1)} %get-tuple-element.97), channel_id=1, source_target_pairs={{8,0},{12,4},{0,8},{4,12},{24,16},{28,20},{16,24},{20,28},{9,1},{1... | collective-permute-start | bytes 122888 | tf_op jit(solution)/shard_map/ppermute | solution.py:24
  35.3 1.5 %collective-permute-start.10 = (bf16[4,80,256]{2,1,0:T(8,128)(2,1)S(1)}, bf16[4,80,256]{2,1,0:T(8,128)(2,1)S(1)}, u32[]{:S(2)}, u32[]{:S(2)}) collective-permute-start(bf16[4,80,256]{2,1,0:T(8,128)(2,1)S(1)} %pad_maximum_fusion.blocks.refs_7_), channel_id=1, source_target_pairs={{4,0},{0,4},{12,8},{8,12},{20,16},{16,20},{28,24},{24,28},{5,1},{1... | collective-permute-start | bytes 491528 | tf_op jit(solution)/shard_map/ppermute | solution.py:24
  38.1 5.8 %collective-permute-start.11 = (bf16[320,128]{1,0:T(8,128)(2,1)S(1)}, bf16[320,128]{1,0:T(8,128)(2,1)S(1)}, u32[]{:S(2)}, u32[]{:S(2)}) collective-permute-start(bf16[320,128]{1,0:T(8,128)(2,1)S(1)} %get-tuple-element.101), channel_id=1, source_target_pairs={{1,0},{0,1},{3,2},{2,3},{5,4},{4,5},{7,6},{6,7},{9,8},{8,9},{11,10... | collective-permute-start | bytes 245768 | tf_op jit(solution)/shard_map/ppermute | solution.py:24
  38.9 5.0 %collective-permute-start.12 = (bf16[320,128]{1,0:T(8,128)(2,1)S(1)}, bf16[320,128]{1,0:T(8,128)(2,1)S(1)}, u32[]{:S(2)}, u32[]{:S(2)}) collective-permute-start(bf16[320,128]{1,0:T(8,128)(2,1)S(1)} %get-tuple-element.101), channel_id=1, source_target_pairs={{2,0},{3,1},{0,2},{1,3},{6,4},{7,5},{4,6},{5,7},{10,8},{11,9},{8,1... | collective-permute-start | bytes 245768 | tf_op jit(solution)/shard_map/ppermute | solution.py:24
  40.0 5.4 %collective-permute-start.13 = (bf16[320,128]{1,0:T(8,128)(2,1)S(1)}, bf16[320,128]{1,0:T(8,128)(2,1)S(1)}, u32[]{:S(2)}, u32[]{:S(2)}) collective-permute-start(bf16[320,128]{1,0:T(8,128)(2,1)S(1)} %get-tuple-element.101), channel_id=1, source_target_pairs={{3,0},{2,1},{1,2},{0,3},{7,4},{6,5},{5,6},{4,7},{11,8},{10,9},{9,1... | collective-permute-start | bytes 245768 | tf_op jit(solution)/shard_map/ppermute | solution.py:24
  46.8 1.5 %collective-permute-start.14 = (bf16[4,80,256]{2,1,0:T(8,128)(2,1)S(1)}, bf16[4,80,256]{2,1,0:T(8,128)(2,1)S(1)}, u32[]{:S(2)}, u32[]{:S(2)}) collective-permute-start(bf16[4,80,256]{2,1,0:T(8,128)(2,1)S(1)} %get-tuple-element.132), channel_id=1, source_target_pairs={{4,0},{0,4},{12,8},{8,12},{20,16},{16,20},{28,24},{24,28},{5,1},{1... | collective-permute-start | bytes 491528 | tf_op jit(solution)/shard_map/ppermute | solution.py:24
  48.3 5.0 %collective-permute-start.15 = (bf16[80,256]{1,0:T(8,128)(2,1)S(1)}, bf16[80,256]{1,0:T(8,128)(2,1)S(1)}, u32[]{:S(2)}, u32[]{:S(2)}) collective-permute-start(bf16[80,256]{1,0:T(8,128)(2,1)S(1)} %get-tuple-element.134), channel_id=1, source_target_pairs={{8,0},{12,4},{0,8},{4,12},{24,16},{28,20},{16,24},{20,28},{9,1},{1... | collective-permute-start | bytes 122888 | tf_op jit(solution)/shard_map/ppermute | solution.py:24
  50.3 5.8 %collective-permute-start.16 = (bf16[80,256]{1,0:T(8,128)(2,1)S(1)}, bf16[80,256]{1,0:T(8,128)(2,1)S(1)}, u32[]{:S(2)}, u32[]{:S(2)}) collective-permute-start(bf16[80,256]{1,0:T(8,128)(2,1)S(1)} %get-tuple-element.135), channel_id=1, source_target_pairs={{16,0},{20,4},{24,8},{28,12},{0,16},{4,20},{8,24},{12,28},{17,1},{... | collective-permute-start | bytes 122888 | tf_op jit(solution)/shard_map/ppermute | solution.py:24
  51.2 5.9 %collective-permute-start.17 = (bf16[80,256]{1,0:T(8,128)(2,1)S(1)}, bf16[80,256]{1,0:T(8,128)(2,1)S(1)}, u32[]{:S(2)}, u32[]{:S(2)}) collective-permute-start(bf16[80,256]{1,0:T(8,128)(2,1)S(1)} %get-tuple-element.136), channel_id=1, source_target_pairs={{24,0},{28,4},{16,8},{20,12},{8,16},{12,20},{0,24},{4,28},{25,1},{... | collective-permute-start | bytes 122888 | tf_op jit(solution)/shard_map/ppermute | solution.py:24
  59.3 7.2 %collective-permute-start.18 = (bf16[3,128,256]{2,1,0:T(8,128)(2,1)S(1)}, bf16[3,128,256]{2,1,0:T(8,128)(2,1)S(1)}, u32[]{:S(2)}, u32[]{:S(2)}) collective-permute-start(bf16[3,128,256]{2,1,0:T(8,128)(2,1)S(1)} %get-tuple-element.138), channel_id=1, source_target_pairs={{28,0},{8,4},{4,8},{16,12},{12,16},{24,20},{20,24},{0,28},{29,1},{... | collective-permute-start | bytes 589832 | tf_op jit(solution)/shard_map/ppermute | solution.py:33
  60.1 6.5 %collective-permute-start.19 = (bf16[3,128,256]{2,1,0:T(8,128)(2,1)S(1)}, bf16[3,128,256]{2,1,0:T(8,128)(2,1)S(1)}, u32[]{:S(2)}, u32[]{:S(2)}) collective-permute-start(bf16[3,128,256]{2,1,0:T(8,128)(2,1)S(1)} %second_pair.1), channel_id=1, source_target_pairs={{4,0},{0,4},{12,8},{8,12},{20,16},{16,20},{28,24},{24,28},{5,1},{1... | collective-permute-start | bytes 589832 | tf_op jit(solution)/shard_map/ppermute | solution.py:24
  70.2 5.0 %collective-permute-start.21 = (f32[16,256]{1,0:T(8,128)S(1)}, f32[16,256]{1,0:T(8,128)S(1)}, u32[]{:S(2)}, u32[]{:S(2)}) collective-permute-start(f32[16,256]{1,0:T(8,128)S(1)} %get-tuple-element.144), channel_id=1, source_target_pairs={{28,0},{8,4},{4,8},{16,12},{12,16},{24,20},{20,24},{0,28},{29,1},{... | collective-permute-start | bytes 49160 | tf_op jit(solution)/shard_map/ppermute | solution.py:33
  72.0 3.2 %collective-permute-start.20 = (f32[16,256]{1,0:T(8,128)S(1)}, f32[16,256]{1,0:T(8,128)S(1)}, u32[]{:S(2)}, u32[]{:S(2)}) collective-permute-start(f32[16,256]{1,0:T(8,128)S(1)} %get-tuple-element.143), channel_id=1, source_target_pairs={{4,0},{0,4},{12,8},{8,12},{20,16},{16,20},{28,24},{24,28},{5,1},{1... | collective-permute-start | bytes 49160 | tf_op jit(solution)/shard_map/ppermute | solution.py:24
  75.2 3.7 %collective-permute-start.24 = (f32[3,256]{1,0:T(4,128)S(1)}, f32[3,256]{1,0:T(4,128)S(1)}, u32[]{:S(2)}, u32[]{:S(2)}) collective-permute-start(f32[3,256]{1,0:T(4,128)S(1)} %get-tuple-element.149), channel_id=1, source_target_pairs={{2,0},{3,1},{0,2},{1,3},{6,4},{7,5},{4,6},{5,7},{10,8},{11,9},{8,1... | collective-permute-start | bytes 9224 | tf_op jit(solution)/shard_map/ppermute | solution.py:42
  76.1 4.5 %collective-permute-start.23 = (f32[3,256]{1,0:T(4,128)S(1)}, f32[3,256]{1,0:T(4,128)S(1)}, u32[]{:S(2)}, u32[]{:S(2)}) collective-permute-start(f32[3,256]{1,0:T(4,128)S(1)} %get-tuple-element.150), channel_id=1, source_target_pairs={{3,0},{2,1},{1,2},{0,3},{7,4},{6,5},{5,6},{4,7},{11,8},{10,9},{9,1... | collective-permute-start | bytes 9224 | tf_op jit(solution)/shard_map/ppermute | solution.py:33
  78.3 3.6 %collective-permute-start.22 = (f32[3,256]{1,0:T(4,128)S(1)}, f32[3,256]{1,0:T(4,128)S(1)}, u32[]{:S(2)}, u32[]{:S(2)}) collective-permute-start(f32[3,256]{1,0:T(4,128)S(1)} %get-tuple-element.148), channel_id=1, source_target_pairs={{1,0},{0,1},{3,2},{2,3},{5,4},{4,5},{7,6},{6,7},{9,8},{8,9},{11,10... | collective-permute-start | bytes 9224 | tf_op jit(solution)/shard_map/ppermute | solution.py:24

commit v20 on v19

--- a/solution.py
+++ b/solution.py
@@ -196,8 +196,12 @@
     low_ref[at] = low
 
 
+def cell_of(ids, atoms):
+    return ids >> (atoms.bit_length() - 1) if atoms & (atoms - 1) == 0 else ids // atoms
+
+
 def slot_order(ids, place_ref, atoms):
-    cell = ids >> (atoms.bit_length() - 1) if atoms & (atoms - 1) == 0 else ids // atoms
+    cell = cell_of(ids, atoms)
     a = (cell * 11) >> 5
     b = cell - 3 * a
     a = jnp.where((place_ref[0, 0:1, 0:1] & 1) == 0, 2 - a, a)
@@ -567,21 +571,18 @@
     own = -move[:, :atoms]
     for n in range(1, slots):
         own = own - move[:, n * atoms : (n + 1) * atoms]
-    lane_hot = hot_columns(ids & 127, 128)
-    half = ids >> 7
+    source = cell_of(ids, atoms)
+    atom_hot = hot_columns(ids - source * atoms, atoms)
     high = move.astype(BF16).astype(F32)
     both = jnp.concatenate([high, move - high], axis=0)
-    per_cell = atoms // 128
     rows = jnp.concatenate(
-        [jnp.where(half == h, both, 0.0).astype(BF16) for h in range(9 * per_cell)], axis=0
-    )
-    spread = dot(rows, lane_hot, ((1,), (1,)))
-    grads = []
-    for cell in range(9):
-        found = []
-        for h in range(cell * per_cell, (cell + 1) * per_cell):
-            found.append(spread[16 * h : 16 * h + 8] + spread[16 * h + 8 : 16 * h + 16])
-        grads.append(jnp.concatenate(found, axis=1))
+        [jnp.where(source == cell, both, 0.0).astype(BF16) for cell in range(9)], axis=0
+    )
+    spread = dot(rows, atom_hot, ((1,), (1,)))
+    grads = [
+        spread[16 * cell : 16 * cell + 8] + spread[16 * cell + 8 : 16 * cell + 16]
+        for cell in range(9)
+    ]
     return own, grads
 
 

time: 82.7 us -> 83.4 us (level)
  no operation moved by 1% of the time
where the time goes in v20:
time: 83.4 us; the launch traced here: 83.2 us
  Pallas kernels  28.3 us (34%)
  starting transfers between devices  27.6 us (33%)
  waiting for transfers between devices  24.2 us (29%)
  local copies, waits for them, and re-layouts  2.07 us (2%)
  between operations  0.97 us (1%)
    pallas_call x23, Pallas kernels, run(): pl.pallas_call(kernel, out_shape=outs, in_specs=specs, out_specs=[whole()...  28.3 us
    ppermute x17, starting transfers between devices, paired(): lax.ppermute(block, axis, [(i ^ mask, i) for i in range(lax.axis_size(axi...  14.5 us
    ppermute x6, waiting for transfers between devices, beyond(): lax.ppermute(block, axis, [(other_side(i, count), i) for i in range(count)])  12.6 us
    ppermute x17, waiting for transfers between devices, paired(): lax.ppermute(block, axis, [(i ^ mask, i) for i in range(lax.axis_size(axi...  11.5 us
    ppermute x6, starting transfers between devices, beyond(): lax.ppermute(block, axis, [(other_side(i, count), i) for i in range(count)])  9.25 us
    ppermute x2, starting transfers between devices, far(): return lax.ppermute(block, axis, route)  3.94 us
    unnamed x27, local copies, waits for them, and re-layouts  2 us
  transfers between devices with their start and end apart: 25, of which 15 were waited for; matrix products, arithmetic and copies ran while one was open for 0% of the time, Pallas kernels for 17%

profile of v20, /device:TPU:0, one launch (start us, length us, event | category | flops | bytes accessed | tf_op | source)
XLA Modules:
  0.0 83.2 jit_solution(7679664619808637433)
XLA Ops:
  0.6 0.1 pad_add_fusion
  0.7 0.1 broadcast_in_dim.4.place_ref
  0.8 0.7 copy-done.9
  1.5 0.7 copy-done.10
  2.2 3.0 %collective-permute-start.2 = (f32[8,128]{1,0:T(8,128)S(1)}, f32[8,128]{1,0:T(8,128)S(1)}, u32[]{:S(2)}, u32[]{:S(2)}) collective-permute-start(f32[8,128]{1,0:T(8,128)S(1)} %pack.1.first_ref), channel_id=1, source_target_pairs={{2,0},{3,1},{0,2},{1,3},{6,4},{7,5},{4,6},{5,7},{10,8},{11,9},{8,1... | collective-permute-start | bytes 12296 | tf_op jit(solution)/shard_map/ppermute | solution.py:42
  5.3 0.1 pack_more.1.own_ref
  5.4 1.6 %collective-permute-start = (f32[40,128]{1,0:T(8,128)S(1)}, f32[40,128]{1,0:T(8,128)S(1)}, u32[]{:S(2)}, u32[]{:S(2)}) collective-permute-start(f32[40,128]{1,0:T(8,128)S(1)} %pack_more.1.own_ref), channel_id=1, source_target_pairs={{3,0},{2,1},{1,2},{0,3},{7,4},{6,5},{5,6},{4,7},{11,8},{10,9},{9,1... | collective-permute-start | bytes 61448 | tf_op jit(solution)/shard_map/ppermute | solution.py:33
  6.9 0.5 collective-permute-start.1
  7.5 3.2 %collective-permute-done.1.y_pair_ref = f32[40,128]{1,0:T(8,128)S(1)} collective-permute-done((f32[40,128]{1,0:T(8,128)S(1)}, f32[40,128]{1,0:T(8,128)S(1)}, u32[]{:S(2)}, u32[]{:S(2)}) %collective-permute-start.1) | collective-permute-done | bytes 20512 | tf_op jit(solution)/shard_map/ppermute | solution.py:24
  10.7 1.8 %collective-permute-start.3 = (f32[5,8,128]{2,1,0:T(8,128)S(1)}, f32[5,8,128]{2,1,0:T(8,128)S(1)}, u32[]{:S(2)}, u32[]{:S(2)}) collective-permute-start(f32[5,8,128]{2,1,0:T(8,128)S(1)} %constant_dynamic-update-slice_fusion.column_ref.cell_ref), channel_id=1, source_target_pairs={{28,0},{8,4},{4,8},{16,12},{12,16},{24,20},{20,24},{0,28},{29,1},{... | collective-permute-start | bytes 61448 | tf_op jit(solution)/shard_map/ppermute | solution.py:33
  12.6 0.3 prep_first.1
  12.9 0.3 prep_second.1
  13.2 2.6 %collective-permute-done.3.beyond_ref = f32[5,8,128]{2,1,0:T(8,128)S(1)} collective-permute-done((f32[5,8,128]{2,1,0:T(8,128)S(1)}, f32[5,8,128]{2,1,0:T(8,128)S(1)}, u32[]{:S(2)}, u32[]{:S(2)}) %collective-permute-start.3) | collective-permute-done | bytes 20512 | tf_op jit(solution)/shard_map/ppermute | solution.py:33
  15.8 2.9 %first.1 = (bf16[3,128,256]{2,1,0:T(8,128)(2,1)S(1)}, s32[3,3072]{1,0:T(4,128)S(1)}, f32[3,8,3072]{2,1,0:T(8,128)S(1)}, f32[3,8,3072]{2,1,0:T(8,128)S(1)}, f32[3...) custom-call(s32[2,8,128]{2,1,0:T(8,128)S(1)} %broadcast_in_dim.4.place_ref, ...), custom_call_target="tpu_custom_call" | custom-call | flops 10000000 | bytes 1000000 | tf_op jit(solution)/shard_map/first/pallas_call | solution.py:55
  18.7 0.1 collective-permute-start.5
  18.8 1.9 %collective-permute-start.6 = (bf16[3,128,256]{2,1,0:T(8,128)(2,1)S(1)}, bf16[3,128,256]{2,1,0:T(8,128)(2,1)S(1)}, u32[]{:S(2)}, u32[]{:S(2)}) collective-permute-start(bf16[3,128,256]{2,1,0:T(8,128)(2,1)S(1)} %get-tuple-element.92.column_ref), channel_id=1, source_target_pairs={{28,0},{8,4},{4,8},{16,12},{12,16},{24,20},{20,24},{0,28},{29,1},{... | collective-permute-start | bytes 589832 | tf_op jit(solution)/shard_map/ppermute | solution.py:33
  20.7 1.7 %second_near.1 = (f32[4,128,3072]{2,1,0:T(8,128)S(1)}, f32[128,3072]{1,0:T(8,128)S(1)}) custom-call(s32[3,3072]{1,0:T(4,128)S(1)} %get-tuple-element.80.ids_ref, f32[3,8,3072]{2,1,0:T(8,128)S(1)} %get-tuple-element.81.basis_ref, f32[3,8,3072]{2,1,0:T(8,128)S(1)} %get-tuple-element.83.unit_ref, bf16[2,128,32]{2,1,0:T(8,128)(2,1)S(1)} %get-tuple-element.91.left_ref, ...), custom_call_target="tpu_custom_call" | custom-call | flops 2000000000 | bytes 1000000 | tf_op jit(solution)/shard_map/second_near/pallas_call | solution.py:55
  22.4 1.0 %hot_beyond.1.hot_ref = bf16[768,3072]{1,0:T(8,128)(2,1)S(1)} custom-call(s32[3,3072]{1,0:T(4,128)S(1)} %get-tuple-element.80.ids_ref, f32[128,3072]{1,0:T(8,128)S(1)} %get-tuple-element.93.near_ref), custom_call_target="tpu_custom_call" | custom-call | flops 1000000 | bytes 1000000 | tf_op jit(solution)/shard_map/hot_beyond/pallas_call | solution.py:55
  23.4 0.8 second_side.1.near_ref
  24.2 2.7 %collective-permute-done.6.beyond_ref = bf16[3,128,256]{2,1,0:T(8,128)(2,1)S(1)} collective-permute-done((bf16[3,128,256]{2,1,0:T(8,128)(2,1)S(1)}, bf16[3,128,256]{2,1,0:T(8,128)(2,1)S(1)}, u32[]{:S(2)}, u32[]{:S(2)}) %collective-permute-start.6) | collective-permute-done | bytes 196640 | tf_op jit(solution)/shard_map/ppermute | solution.py:33
  26.9 1.9 %second.1 = (bf16[128,3072]{1,0:T(8,128)(2,1)S(1)}, f32[3,128,256]{2,1,0:T(8,128)S(1)}, f32[128,256]{1,0:T(8,128)S(1)}, bf16[80,256]{1,0:T(8,128)(2,1)S(1)}, f32...) custom-call(bf16[768,3072]{1,0:T(8,128)(2,1)S(1)} %hot_beyond.1.hot_ref, f32[4,128,3072]{2,1,0:T(8,128)S(1)} %get-tuple-element.94.weight_ref, ...), custom_call_target="tpu_custom_call" | custom-call | flops 10000000 | bytes 1000000 | tf_op jit(solution)/shard_map/second/pallas_call | solution.py:55
  28.8 0.1 collective-permute-start.9
  28.9 0.1 collective-permute-start.8
  28.9 4.3 %collective-permute-start.7 = (bf16[80,256]{1,0:T(8,128)(2,1)S(1)}, bf16[80,256]{1,0:T(8,128)(2,1)S(1)}, u32[]{:S(2)}, u32[]{:S(2)}) collective-permute-start(bf16[80,256]{1,0:T(8,128)(2,1)S(1)} %get-tuple-element.97), channel_id=1, source_target_pairs={{8,0},{12,4},{0,8},{4,12},{24,16},{28,20},{16,24},{20,28},{9,1},{1... | collective-permute-start | bytes 122888 | tf_op jit(solution)/shard_map/ppermute | solution.py:24
  33.2 0.8 green.1.refs_0_
  34.0 0.9 %collective-permute-done.9 = bf16[80,256]{1,0:T(8,128)(2,1)S(1)} collective-permute-done((bf16[80,256]{1,0:T(8,128)(2,1)S(1)}, bf16[80,256]{1,0:T(8,128)(2,1)S(1)}, u32[]{:S(2)}, u32[]{:S(2)}) %collective-permute-start.9) | collective-permute-done | bytes 40992 | tf_op jit(solution)/shard_map/ppermute | solution.py:24
  35.0 0.3 collective-permute-done.7
  35.3 0.1 collective-permute-start.10
  35.4 1.2 %structure_near.1 = (f32[32,1024]{1,0:T(8,128)S(1)}, f32[32,1024]{1,0:T(8,128)S(1)}, f32[8,1024]{1,0:T(8,128)S(1)}, f32[8,1024]{1,0:T(8,128)S(1)}, bf16[640,1024...) custom-call(s32[2,8,128]{2,1,0:T(8,128)S(1)} %broadcast_in_dim.4.place_ref, ...), custom_call_target="tpu_custom_call" | custom-call | flops 1000000000 | bytes 1000000 | tf_op jit(solution)/shard_map/structure_near/pallas_call | solution.py:55
  36.6 0.2 collective-permute-done.10.blocks.refs_11_
  36.8 1.3 %structure_far.1 = (f32[32,1024]{1,0:T(8,128)S(1)}, f32[32,1024]{1,0:T(8,128)S(1)}, f32[8,1024]{1,0:T(8,128)S(1)}, f32[8,1024]{1,0:T(8,128)S(1)}, bf16[640,1024]...) custom-call(s32[2,8,128]{2,1,0:T(8,128)S(1)} %broadcast_in_dim.4.place_r, ...), custom_call_target="tpu_custom_call" | custom-call | flops 10000000 | bytes 1000000 | tf_op jit(solution)/shard_map/structure_far/pallas_call | solution.py:55
  38.1 0.9 %collective-permute-start.11 = (bf16[320,128]{1,0:T(8,128)(2,1)S(1)}, bf16[320,128]{1,0:T(8,128)(2,1)S(1)}, u32[]{:S(2)}, u32[]{:S(2)}) collective-permute-start(bf16[320,128]{1,0:T(8,128)(2,1)S(1)} %get-tuple-element.101), channel_id=1, source_target_pairs={{1,0},{0,1},{3,2},{2,3},{5,4},{4,5},{7,6},{6,7},{9,8},{8,9},{11,10... | collective-permute-start | bytes 245768 | tf_op jit(solution)/shard_map/ppermute | solution.py:24
  38.9 1.1 %collective-permute-start.12 = (bf16[320,128]{1,0:T(8,128)(2,1)S(1)}, bf16[320,128]{1,0:T(8,128)(2,1)S(1)}, u32[]{:S(2)}, u32[]{:S(2)}) collective-permute-start(bf16[320,128]{1,0:T(8,128)(2,1)S(1)} %get-tuple-element.101), channel_id=1, source_target_pairs={{2,0},{3,1},{0,2},{1,3},{6,4},{7,5},{4,6},{5,7},{10,8},{11,9},{8,1... | collective-permute-start | bytes 245768 | tf_op jit(solution)/shard_map/ppermute | solution.py:24
  40.0 1.6 %collective-permute-start.13 = (bf16[320,128]{1,0:T(8,128)(2,1)S(1)}, bf16[320,128]{1,0:T(8,128)(2,1)S(1)}, u32[]{:S(2)}, u32[]{:S(2)}) collective-permute-start(bf16[320,128]{1,0:T(8,128)(2,1)S(1)} %get-tuple-element.101), channel_id=1, source_target_pairs={{3,0},{2,1},{1,2},{0,3},{7,4},{6,5},{5,6},{4,7},{11,8},{10,9},{9,1... | collective-permute-start | bytes 245768 | tf_op jit(solution)/shard_map/ppermute | solution.py:24
  41.6 2.3 %hot_back.1.hot_ref = bf16[3072,1536]{1,0:T(8,128)(2,1)S(1)} custom-call(s32[3,3072]{1,0:T(4,128)S(1)} %get-tuple-element.80.ids_ref), custom_call_target="tpu_custom_call" | custom-call | flops 2000000000 | bytes 1000000 | tf_op jit(solution)/shard_map/hot_back/pallas_call | solution.py:55
  43.9 1.6 %collective-permute-done.13.refs_4_ = bf16[320,128]{1,0:T(8,128)(2,1)S(1)} collective-permute-done((bf16[320,128]{1,0:T(8,128)(2,1)S(1)}, bf16[320,128]{1,0:T(8,128)(2,1)S(1)}, u32[]{:S(2)}, u32[]{:S(2)}) %collective-permute-start.13) | collective-permute-done | bytes 81952 | tf_op jit(solution)/shard_map/ppermute | solution.py:24
  45.5 1.3 %fold_far.1 = (bf16[4,80,256]{2,1,0:T(8,128)(2,1)S(1)}, f32[640,64]{1,0:T(8,128)S(1)}) custom-call(s32[2,8,128]{2,1,0:T(8,128)S(1)} %broadcast_in_dim.4.place_ref, f32[320,128]{1,0:T(8,128)S(1)} %green.1.refs_0_, f32[320,128]{1,0:T(8,128)S(1)} %get-tuple-element.115.refs_1_, bf16[320,128]{1,0:T(8,128)(2,1)S(1)} %collective-permute-done.11.refs_2_, ...), custom_call_target="tpu_custom_call" | custom-call | flops 10000000 | bytes 1000000 | tf_op jit(solution)/shard_map/fold_far/pallas_call | solution.py:55
  46.8 0.1 collective-permute-start.14
  46.9 1.2 %fold_near.1.near_ref = f32[4,80,256]{2,1,0:T(8,128)S(1)} custom-call(s32[2,8,128]{2,1,0:T(8,128)S(1)} %broadcast_in_dim.4.place_ref, f32[640,64]{1,0:T(8,128)S(1)} %get-tuple-element.125.refs_0_, f32[32,1024]{1,0:T(8,128)S(1)} %get-tuple-element.126.refs_1_, f32[32,1024]{1,0:T(8,128)S(1)} %get-tuple-element.127.refs_2_, ...), custom_call_target="tpu_custom_call" | custom-call | flops 1000000000 | bytes 1000000 | tf_op jit(solution)/shard_map/fold_near/pallas_call | solution.py:55
  48.1 0.2 collective-permute-done.14.far_ref
  48.3 0.1 fold_join.1
  48.3 2.0 %collective-permute-start.15 = (bf16[80,256]{1,0:T(8,128)(2,1)S(1)}, bf16[80,256]{1,0:T(8,128)(2,1)S(1)}, u32[]{:S(2)}, u32[]{:S(2)}) collective-permute-start(bf16[80,256]{1,0:T(8,128)(2,1)S(1)} %get-tuple-element.134), channel_id=1, source_target_pairs={{8,0},{12,4},{0,8},{4,12},{24,16},{28,20},{16,24},{20,28},{9,1},{1... | collective-permute-start | bytes 122888 | tf_op jit(solution)/shard_map/ppermute | solution.py:24
  50.3 0.9 %collective-permute-start.16 = (bf16[80,256]{1,0:T(8,128)(2,1)S(1)}, bf16[80,256]{1,0:T(8,128)(2,1)S(1)}, u32[]{:S(2)}, u32[]{:S(2)}) collective-permute-start(bf16[80,256]{1,0:T(8,128)(2,1)S(1)} %get-tuple-element.135), channel_id=1, source_target_pairs={{16,0},{20,4},{24,8},{28,12},{0,16},{4,20},{8,24},{12,28},{17,1},{... | collective-permute-start | bytes 122888 | tf_op jit(solution)/shard_map/ppermute | solution.py:24
  51.2 1.5 %collective-permute-start.17 = (bf16[80,256]{1,0:T(8,128)(2,1)S(1)}, bf16[80,256]{1,0:T(8,128)(2,1)S(1)}, u32[]{:S(2)}, u32[]{:S(2)}) collective-permute-start(bf16[80,256]{1,0:T(8,128)(2,1)S(1)} %get-tuple-element.136), channel_id=1, source_target_pairs={{24,0},{28,4},{16,8},{20,12},{8,16},{12,20},{0,24},{4,28},{25,1},{... | collective-permute-start | bytes 122888 | tf_op jit(solution)/shard_map/ppermute | solution.py:24
  52.8 0.5 readout.1
  53.3 2.8 %collective-permute-done.16.refs_2_ = bf16[80,256]{1,0:T(8,128)(2,1)S(1)} collective-permute-done((bf16[80,256]{1,0:T(8,128)(2,1)S(1)}, bf16[80,256]{1,0:T(8,128)(2,1)S(1)}, u32[]{:S(2)}, u32[]{:S(2)}) %collective-permute-start.16) | collective-permute-done | bytes 40992 | tf_op jit(solution)/shard_map/ppermute | solution.py:24
  56.1 1.0 %collective-permute-done.17.refs_3_ = bf16[80,256]{1,0:T(8,128)(2,1)S(1)} collective-permute-done((bf16[80,256]{1,0:T(8,128)(2,1)S(1)}, bf16[80,256]{1,0:T(8,128)(2,1)S(1)}, u32[]{:S(2)}, u32[]{:S(2)}) %collective-permute-start.17) | collective-permute-done | bytes 40992 | tf_op jit(solution)/shard_map/ppermute | solution.py:24
  57.1 2.2 %second_back.1 = (f32[1,1,256]{2,1,0:T(1,128)}, f32[8,256]{1,0:T(8,128)S(1)}, f32[128,256]{1,0:T(8,128)S(1)}, f32[4,128,256]{2,1,0:T(8,128)S(1)}, bf16[128,3072]...) custom-call(bf16[3072,1536]{1,0:T(8,128)(2,1)S(1)} %hot_back.1.hot_ref, ...), custom_call_target="tpu_custom_call" | custom-call | flops 10000000 | bytes 1000000 | tf_op jit(solution)/shard_map/second_back/pallas_call | solution.py:55
  59.3 0.8 second_pair.1
  60.1 0.8 collective-permute-start.19
  60.9 1.3 %hot_middle.1.hot_ref = bf16[3072,768]{1,0:T(8,128)(2,1)S(1)} custom-call(s32[3,3072]{1,0:T(4,128)S(1)} %get-tuple-element.80.ids_ref), custom_call_target="tpu_custom_call" | custom-call | flops 1000000000 | bytes 1000000 | tf_op jit(solution)/shard_map/hot_middle/pallas_call | solution.py:55
  62.2 0.8 second_middle.1.middle_ref
  63.1 1.2 %second_edge.1.edge_ref = f32[32,3072]{1,0:T(8,128)S(1)} custom-call(bf16[2,16,256]{2,1,0:T(8,128)(2,1)S(1)} %get-tuple-element.90.back_ref, bf16[128,3072]{1,0:T(8,128)(2,1)S(1)} %get-tuple-element.96.feature_ref, f32[4,128,256]{2,1,0:T(8,128)S(1)} %get-tuple-element.137.grad_ref), custom_call_target="tpu_custom_call" | custom-call | flops 1000000000 | bytes 1000000 | tf_op jit(solution)/shard_map/second_edge/pallas_call | solution.py:55
  64.3 2.3 %collective-permute-done.18.from_beyond = bf16[3,128,256]{2,1,0:T(8,128)(2,1)S(1)} collective-permute-done((bf16[3,128,256]{2,1,0:T(8,128)(2,1)S(1)}, bf16[3,128,256]{2,1,0:T(8,128)(2,1)S(1)}, u32[]{:S(2)}, u32[]{:S(2)}) %collective-permute-start.18) | collective-permute-done | bytes 196640 | tf_op jit(solution)/shard_map/ppermute | solution.py:33
  66.6 4.3 %first_back.1 = (f32[16,256]{1,0:T(8,128)S(1)}, f32[16,256]{1,0:T(8,128)S(1)}, f32[16,256]{1,0:T(8,128)S(1)}) custom-call(s32[3,3072]{1,0:T(4,128)S(1)} %get-tuple-element.80.ids_ref, f32[3,8,3072]{2,1,0:T(8,128)S(1)} %get-tuple-element.81.basis_ref, f32[3,8,3072]{2,1,0:T(8,128)S(1)} %get-tuple-element.82.slope_ref, ...), custom_call_target="tpu_custom_call" | custom-call | flops 10000000 | bytes 1000000 | tf_op jit(solution)/shard_map/first_back/pallas_call | solution.py:55
  70.9 1.8 %collective-permute-start.21 = (f32[16,256]{1,0:T(8,128)S(1)}, f32[16,256]{1,0:T(8,128)S(1)}, u32[]{:S(2)}, u32[]{:S(2)}) collective-permute-start(f32[16,256]{1,0:T(8,128)S(1)} %get-tuple-element.144), channel_id=1, source_target_pairs={{28,0},{8,4},{4,8},{16,12},{12,16},{24,20},{20,24},{0,28},{29,1},{... | collective-permute-start | bytes 49160 | tf_op jit(solution)/shard_map/ppermute | solution.py:33
  72.7 3.2 %collective-permute-done.21 = f32[16,256]{1,0:T(8,128)S(1)} collective-permute-done((f32[16,256]{1,0:T(8,128)S(1)}, f32[16,256]{1,0:T(8,128)S(1)}, u32[]{:S(2)}, u32[]{:S(2)}) %collective-permute-start.21) | collective-permute-done | bytes 16416 | tf_op jit(solution)/shard_map/ppermute | solution.py:33
  76.0 0.9 %collective-permute-start.24 = (f32[3,256]{1,0:T(4,128)S(1)}, f32[3,256]{1,0:T(4,128)S(1)}, u32[]{:S(2)}, u32[]{:S(2)}) collective-permute-start(f32[3,256]{1,0:T(4,128)S(1)} %get-tuple-element.149), channel_id=1, source_target_pairs={{2,0},{3,1},{0,2},{1,3},{6,4},{7,5},{4,6},{5,7},{10,8},{11,9},{8,1... | collective-permute-start | bytes 9224 | tf_op jit(solution)/shard_map/ppermute | solution.py:42
  76.9 2.2 %collective-permute-start.23 = (f32[3,256]{1,0:T(4,128)S(1)}, f32[3,256]{1,0:T(4,128)S(1)}, u32[]{:S(2)}, u32[]{:S(2)}) collective-permute-start(f32[3,256]{1,0:T(4,128)S(1)} %get-tuple-element.150), channel_id=1, source_target_pairs={{3,0},{2,1},{1,2},{0,3},{7,4},{6,5},{5,6},{4,7},{11,8},{10,9},{9,1... | collective-permute-start | bytes 9224 | tf_op jit(solution)/shard_map/ppermute | solution.py:33
  79.0 0.5 collective-permute-start.22
  79.5 0.1 collective-permute-done.24
  79.6 1.7 %collective-permute-done.23 = f32[3,256]{1,0:T(4,128)S(1)} collective-permute-done((f32[3,256]{1,0:T(4,128)S(1)}, f32[3,256]{1,0:T(4,128)S(1)}, u32[]{:S(2)}, u32[]{:S(2)}) %collective-permute-start.23) | collective-permute-done | bytes 3104 | tf_op jit(solution)/shard_map/ppermute | solution.py:33
  81.4 1.3 %collective-permute-done.22 = f32[3,256]{1,0:T(4,128)S(1)} collective-permute-done((f32[3,256]{1,0:T(4,128)S(1)}, f32[3,256]{1,0:T(4,128)S(1)}, u32[]{:S(2)}, u32[]{:S(2)}) %collective-permute-start.22) | collective-permute-done | bytes 3104 | tf_op jit(solution)/shard_map/ppermute | solution.py:24
  82.7 0.6 copy.13
  (43 shorter events, 0.1 us)
Async XLA Ops:
  0.8 0.7 copy-start.9
  1.5 0.7 copy-start.10
  2.1 3.1 %copy-start.5 = (s32[1,1,256,12]{2,1,3,0:T(1,128)S(1)}, s32[1,1,256,12]{2,1,3,0:T(1,128)}, u32[]{:S(2)}) copy-start(s32[1,1,256,12]{2,1,3,0:T(1,128)} %param.13) | copy-start | bytes 36868
  2.2 3.1 %copy-start.7 = (s32[1,1,256]{2,1,0:T(1,128)S(1)}, s32[1,1,256]{2,1,0:T(1,128)}, u32[]{:S(2)}) copy-start(s32[1,1,256]{2,1,0:T(1,128)} %count_ref.1) | copy-start | bytes 3076
  2.2 10.4 %copy-start = (f32[2,2,128,128]{3,2,1,0:T(8,128)S(1)}, f32[2,2,128,128]{3,2,1,0:T(8,128)}, u32[]{:S(2)}) copy-start(f32[2,2,128,128]{3,2,1,0:T(8,128)} %mixing_in.1) | copy-start | bytes 786436
  2.2 10.4 %copy-start.4 = (f32[2,2,8,128]{3,2,1,0:T(8,128)S(1)}, f32[2,2,8,128]{3,2,1,0:T(8,128)}, u32[]{:S(2)}) copy-start(f32[2,2,8,128]{3,2,1,0:T(8,128)} %radial_in.1) | copy-start | bytes 49156
  2.2 10.4 %copy-start.6 = (f32[6,128]{1,0:T(8,128)S(1)}, f32[6,128]{1,0:T(8,128)}, u32[]{:S(2)}) copy-start(f32[6,128]{1,0:T(8,128)} %embed_in.1) | copy-start | bytes 9220
  2.2 10.7 %copy-start.1 = (f32[128,128]{1,0:T(8,128)S(1)}, f32[128,128]{1,0:T(8,128)}, u32[]{:S(2)}) copy-start(f32[128,128]{1,0:T(8,128)} %hidden_in.1) | copy-start | bytes 196612
  2.2 10.7 %copy-start.3 = (f32[128,64]{0,1:T(8,128)S(1)}, f32[128,64]{0,1:T(8,128)}, u32[]{:S(2)}) copy-start(f32[128,64]{0,1:T(8,128)} %param.20) | copy-start | bytes 98308
  2.2 10.7 %copy-start.8 = (f32[128]{0:T(128)S(1)}, f32[128]{0:T(128)}, u32[]{:S(2)}) copy-start(f32[128]{0:T(128)} %param.19) | copy-start | bytes 1540
  2.2 5.3 %collective-permute-start.2 = (f32[8,128]{1,0:T(8,128)S(1)}, f32[8,128]{1,0:T(8,128)S(1)}, u32[]{:S(2)}, u32[]{:S(2)}) collective-permute-start(f32[8,128]{1,0:T(8,128)S(1)} %pack.1.first_ref), channel_id=1, source_target_pairs={{2,0},{3,1},{0,2},{1,3},{6,4},{7,5},{4,6},{5,7},{10,8},{11,9},{8,1... | collective-permute-start | bytes 12296 | tf_op jit(solution)/shard_map/ppermute | solution.py:42
  5.4 5.3 %collective-permute-start = (f32[40,128]{1,0:T(8,128)S(1)}, f32[40,128]{1,0:T(8,128)S(1)}, u32[]{:S(2)}, u32[]{:S(2)}) collective-permute-start(f32[40,128]{1,0:T(8,128)S(1)} %pack_more.1.own_ref), channel_id=1, source_target_pairs={{3,0},{2,1},{1,2},{0,3},{7,4},{6,5},{5,6},{4,7},{11,8},{10,9},{9,1... | collective-permute-start | bytes 61448 | tf_op jit(solution)/shard_map/ppermute | solution.py:33
  6.9 3.8 %collective-permute-start.1 = (f32[40,128]{1,0:T(8,128)S(1)}, f32[40,128]{1,0:T(8,128)S(1)}, u32[]{:S(2)}, u32[]{:S(2)}) collective-permute-start(f32[40,128]{1,0:T(8,128)S(1)} %pack_more.1.own_ref), channel_id=1, source_target_pairs={{1,0},{0,1},{3,2},{2,3},{5,4},{4,5},{7,6},{6,7},{9,8},{8,9},{11,10... | collective-permute-start | bytes 61448 | tf_op jit(solution)/shard_map/ppermute | solution.py:24
  10.7 5.1 %collective-permute-start.3 = (f32[5,8,128]{2,1,0:T(8,128)S(1)}, f32[5,8,128]{2,1,0:T(8,128)S(1)}, u32[]{:S(2)}, u32[]{:S(2)}) collective-permute-start(f32[5,8,128]{2,1,0:T(8,128)S(1)} %constant_dynamic-update-slice_fusion.column_ref.cell_ref), channel_id=1, source_target_pairs={{28,0},{8,4},{4,8},{16,12},{12,16},{24,20},{20,24},{0,28},{29,1},{... | collective-permute-start | bytes 61448 | tf_op jit(solution)/shard_map/ppermute | solution.py:33
  12.6 3.3 %collective-permute-start.4 = (f32[5,8,128]{2,1,0:T(8,128)S(1)}, f32[5,8,128]{2,1,0:T(8,128)S(1)}, u32[]{:S(2)}, u32[]{:S(2)}) collective-permute-start(f32[5,8,128]{2,1,0:T(8,128)S(1)} %constant_dynamic-update-slice_fusion.column_ref.cell_ref), channel_id=1, source_target_pairs={{4,0},{0,4},{12,8},{8,12},{20,16},{16,20},{28,24},{24,28},{5,1},{1... | collective-permute-start | bytes 61448 | tf_op jit(solution)/shard_map/ppermute | solution.py:24
  18.7 4.7 %collective-permute-start.5 = (bf16[3,128,256]{2,1,0:T(8,128)(2,1)S(1)}, bf16[3,128,256]{2,1,0:T(8,128)(2,1)S(1)}, u32[]{:S(2)}, u32[]{:S(2)}) collective-permute-start(bf16[3,128,256]{2,1,0:T(8,128)(2,1)S(1)} %get-tuple-element.92.column_ref), channel_id=1, source_target_pairs={{4,0},{0,4},{12,8},{8,12},{20,16},{16,20},{28,24},{24,28},{5,1},{1... | collective-permute-start | bytes 589832 | tf_op jit(solution)/shard_map/ppermute | solution.py:24
  18.8 8.1 %collective-permute-start.6 = (bf16[3,128,256]{2,1,0:T(8,128)(2,1)S(1)}, bf16[3,128,256]{2,1,0:T(8,128)(2,1)S(1)}, u32[]{:S(2)}, u32[]{:S(2)}) collective-permute-start(bf16[3,128,256]{2,1,0:T(8,128)(2,1)S(1)} %get-tuple-element.92.column_ref), channel_id=1, source_target_pairs={{28,0},{8,4},{4,8},{16,12},{12,16},{24,20},{20,24},{0,28},{29,1},{... | collective-permute-start | bytes 589832 | tf_op jit(solution)/shard_map/ppermute | solution.py:33
  26.9 6.3 %copy-start.2 = (s32[3,4096]{1,0:T(4,128)S(1)}, s32[3,4096]{1,0:T(4,128)}, u32[]{:S(2)}) copy-start(s32[3,4096]{1,0:T(4,128)} %vec_ref.1) | copy-start | bytes 147460
  28.8 6.2 %collective-permute-start.9 = (bf16[80,256]{1,0:T(8,128)(2,1)S(1)}, bf16[80,256]{1,0:T(8,128)(2,1)S(1)}, u32[]{:S(2)}, u32[]{:S(2)}) collective-permute-start(bf16[80,256]{1,0:T(8,128)(2,1)S(1)} %get-tuple-element.97), channel_id=1, source_target_pairs={{24,0},{28,4},{16,8},{20,12},{8,16},{12,20},{0,24},{4,28},{25,1},{... | collective-permute-start | bytes 122888 | tf_op jit(solution)/shard_map/ppermute | solution.py:24
  28.9 6.1 %collective-permute-start.8 = (bf16[80,256]{1,0:T(8,128)(2,1)S(1)}, bf16[80,256]{1,0:T(8,128)(2,1)S(1)}, u32[]{:S(2)}, u32[]{:S(2)}) collective-permute-start(bf16[80,256]{1,0:T(8,128)(2,1)S(1)} %get-tuple-element.97), channel_id=1, source_target_pairs={{16,0},{20,4},{24,8},{28,12},{0,16},{4,20},{8,24},{12,28},{17,1},{... | collective-permute-start | bytes 122888 | tf_op jit(solution)/shard_map/ppermute | solution.py:24
  28.9 6.4 %collective-permute-start.7 = (bf16[80,256]{1,0:T(8,128)(2,1)S(1)}, bf16[80,256]{1,0:T(8,128)(2,1)S(1)}, u32[]{:S(2)}, u32[]{:S(2)}) collective-permute-start(bf16[80,256]{1,0:T(8,128)(2,1)S(1)} %get-tuple-element.97), channel_id=1, source_target_pairs={{8,0},{12,4},{0,8},{4,12},{24,16},{28,20},{16,24},{20,28},{9,1},{1... | collective-permute-start | bytes 122888 | tf_op jit(solution)/shard_map/ppermute | solution.py:24
  35.3 1.5 %collective-permute-start.10 = (bf16[4,80,256]{2,1,0:T(8,128)(2,1)S(1)}, bf16[4,80,256]{2,1,0:T(8,128)(2,1)S(1)}, u32[]{:S(2)}, u32[]{:S(2)}) collective-permute-start(bf16[4,80,256]{2,1,0:T(8,128)(2,1)S(1)} %pad_maximum_fusion.blocks.refs_7_), channel_id=1, source_target_pairs={{4,0},{0,4},{12,8},{8,12},{20,16},{16,20},{28,24},{24,28},{5,1},{1... | collective-permute-start | bytes 491528 | tf_op jit(solution)/shard_map/ppermute | solution.py:24
  38.1 5.8 %collective-permute-start.11 = (bf16[320,128]{1,0:T(8,128)(2,1)S(1)}, bf16[320,128]{1,0:T(8,128)(2,1)S(1)}, u32[]{:S(2)}, u32[]{:S(2)}) collective-permute-start(bf16[320,128]{1,0:T(8,128)(2,1)S(1)} %get-tuple-element.101), channel_id=1, source_target_pairs={{1,0},{0,1},{3,2},{2,3},{5,4},{4,5},{7,6},{6,7},{9,8},{8,9},{11,10... | collective-permute-start | bytes 245768 | tf_op jit(solution)/shard_map/ppermute | solution.py:24
  38.9 5.0 %collective-permute-start.12 = (bf16[320,128]{1,0:T(8,128)(2,1)S(1)}, bf16[320,128]{1,0:T(8,128)(2,1)S(1)}, u32[]{:S(2)}, u32[]{:S(2)}) collective-permute-start(bf16[320,128]{1,0:T(8,128)(2,1)S(1)} %get-tuple-element.101), channel_id=1, source_target_pairs={{2,0},{3,1},{0,2},{1,3},{6,4},{7,5},{4,6},{5,7},{10,8},{11,9},{8,1... | collective-permute-start | bytes 245768 | tf_op jit(solution)/shard_map/ppermute | solution.py:24
  40.0 5.4 %collective-permute-start.13 = (bf16[320,128]{1,0:T(8,128)(2,1)S(1)}, bf16[320,128]{1,0:T(8,128)(2,1)S(1)}, u32[]{:S(2)}, u32[]{:S(2)}) collective-permute-start(bf16[320,128]{1,0:T(8,128)(2,1)S(1)} %get-tuple-element.101), channel_id=1, source_target_pairs={{3,0},{2,1},{1,2},{0,3},{7,4},{6,5},{5,6},{4,7},{11,8},{10,9},{9,1... | collective-permute-start | bytes 245768 | tf_op jit(solution)/shard_map/ppermute | solution.py:24
  46.8 1.5 %collective-permute-start.14 = (bf16[4,80,256]{2,1,0:T(8,128)(2,1)S(1)}, bf16[4,80,256]{2,1,0:T(8,128)(2,1)S(1)}, u32[]{:S(2)}, u32[]{:S(2)}) collective-permute-start(bf16[4,80,256]{2,1,0:T(8,128)(2,1)S(1)} %get-tuple-element.132), channel_id=1, source_target_pairs={{4,0},{0,4},{12,8},{8,12},{20,16},{16,20},{28,24},{24,28},{5,1},{1... | collective-permute-start | bytes 491528 | tf_op jit(solution)/shard_map/ppermute | solution.py:24
  48.3 5.0 %collective-permute-start.15 = (bf16[80,256]{1,0:T(8,128)(2,1)S(1)}, bf16[80,256]{1,0:T(8,128)(2,1)S(1)}, u32[]{:S(2)}, u32[]{:S(2)}) collective-permute-start(bf16[80,256]{1,0:T(8,128)(2,1)S(1)} %get-tuple-element.134), channel_id=1, source_target_pairs={{8,0},{12,4},{0,8},{4,12},{24,16},{28,20},{16,24},{20,28},{9,1},{1... | collective-permute-start | bytes 122888 | tf_op jit(solution)/shard_map/ppermute | solution.py:24
  50.3 5.8 %collective-permute-start.16 = (bf16[80,256]{1,0:T(8,128)(2,1)S(1)}, bf16[80,256]{1,0:T(8,128)(2,1)S(1)}, u32[]{:S(2)}, u32[]{:S(2)}) collective-permute-start(bf16[80,256]{1,0:T(8,128)(2,1)S(1)} %get-tuple-element.135), channel_id=1, source_target_pairs={{16,0},{20,4},{24,8},{28,12},{0,16},{4,20},{8,24},{12,28},{17,1},{... | collective-permute-start | bytes 122888 | tf_op jit(solution)/shard_map/ppermute | solution.py:24
  51.2 5.9 %collective-permute-start.17 = (bf16[80,256]{1,0:T(8,128)(2,1)S(1)}, bf16[80,256]{1,0:T(8,128)(2,1)S(1)}, u32[]{:S(2)}, u32[]{:S(2)}) collective-permute-start(bf16[80,256]{1,0:T(8,128)(2,1)S(1)} %get-tuple-element.136), channel_id=1, source_target_pairs={{24,0},{28,4},{16,8},{20,12},{8,16},{12,20},{0,24},{4,28},{25,1},{... | collective-permute-start | bytes 122888 | tf_op jit(solution)/shard_map/ppermute | solution.py:24
  59.3 7.2 %collective-permute-start.18 = (bf16[3,128,256]{2,1,0:T(8,128)(2,1)S(1)}, bf16[3,128,256]{2,1,0:T(8,128)(2,1)S(1)}, u32[]{:S(2)}, u32[]{:S(2)}) collective-permute-start(bf16[3,128,256]{2,1,0:T(8,128)(2,1)S(1)} %get-tuple-element.138), channel_id=1, source_target_pairs={{28,0},{8,4},{4,8},{16,12},{12,16},{24,20},{20,24},{0,28},{29,1},{... | collective-permute-start | bytes 589832 | tf_op jit(solution)/shard_map/ppermute | solution.py:33
  60.1 6.5 %collective-permute-start.19 = (bf16[3,128,256]{2,1,0:T(8,128)(2,1)S(1)}, bf16[3,128,256]{2,1,0:T(8,128)(2,1)S(1)}, u32[]{:S(2)}, u32[]{:S(2)}) collective-permute-start(bf16[3,128,256]{2,1,0:T(8,128)(2,1)S(1)} %second_pair.1), channel_id=1, source_target_pairs={{4,0},{0,4},{12,8},{8,12},{20,16},{16,20},{28,24},{24,28},{5,1},{1... | collective-permute-start | bytes 589832 | tf_op jit(solution)/shard_map/ppermute | solution.py:24
  70.9 5.0 %collective-permute-start.21 = (f32[16,256]{1,0:T(8,128)S(1)}, f32[16,256]{1,0:T(8,128)S(1)}, u32[]{:S(2)}, u32[]{:S(2)}) collective-permute-start(f32[16,256]{1,0:T(8,128)S(1)} %get-tuple-element.144), channel_id=1, source_target_pairs={{28,0},{8,4},{4,8},{16,12},{12,16},{24,20},{20,24},{0,28},{29,1},{... | collective-permute-start | bytes 49160 | tf_op jit(solution)/shard_map/ppermute | solution.py:33
  72.7 3.2 %collective-permute-start.20 = (f32[16,256]{1,0:T(8,128)S(1)}, f32[16,256]{1,0:T(8,128)S(1)}, u32[]{:S(2)}, u32[]{:S(2)}) collective-permute-start(f32[16,256]{1,0:T(8,128)S(1)} %get-tuple-element.143), channel_id=1, source_target_pairs={{4,0},{0,4},{12,8},{8,12},{20,16},{16,20},{28,24},{24,28},{5,1},{1... | collective-permute-start | bytes 49160 | tf_op jit(solution)/shard_map/ppermute | solution.py:24
  76.0 3.7 %collective-permute-start.24 = (f32[3,256]{1,0:T(4,128)S(1)}, f32[3,256]{1,0:T(4,128)S(1)}, u32[]{:S(2)}, u32[]{:S(2)}) collective-permute-start(f32[3,256]{1,0:T(4,128)S(1)} %get-tuple-element.149), channel_id=1, source_target_pairs={{2,0},{3,1},{0,2},{1,3},{6,4},{7,5},{4,6},{5,7},{10,8},{11,9},{8,1... | collective-permute-start | bytes 9224 | tf_op jit(solution)/shard_map/ppermute | solution.py:42
  76.9 4.5 %collective-permute-start.23 = (f32[3,256]{1,0:T(4,128)S(1)}, f32[3,256]{1,0:T(4,128)S(1)}, u32[]{:S(2)}, u32[]{:S(2)}) collective-permute-start(f32[3,256]{1,0:T(4,128)S(1)} %get-tuple-element.150), channel_id=1, source_target_pairs={{3,0},{2,1},{1,2},{0,3},{7,4},{6,5},{5,6},{4,7},{11,8},{10,9},{9,1... | collective-permute-start | bytes 9224 | tf_op jit(solution)/shard_map/ppermute | solution.py:33
  79.0 3.6 %collective-permute-start.22 = (f32[3,256]{1,0:T(4,128)S(1)}, f32[3,256]{1,0:T(4,128)S(1)}, u32[]{:S(2)}, u32[]{:S(2)}) collective-permute-start(f32[3,256]{1,0:T(4,128)S(1)} %get-tuple-element.148), channel_id=1, source_target_pairs={{1,0},{0,1},{3,2},{2,3},{5,4},{4,5},{7,6},{6,7},{9,8},{8,9},{11,10... | collective-permute-start | bytes 9224 | tf_op jit(solution)/shard_map/ppermute | solution.py:24

commit v21 on v20

--- a/solution.py
+++ b/solution.py
@@ -271,6 +271,13 @@
             hot_ref[start : start + 128, n * width : (n + 1) * width] = jnp.where(
                 column - float(slot * width) == entry, 1.0, 0.0
             ).astype(BF16)
+
+
+def atom_hot_kernel(ids_ref, hot_ref):
+    atoms = hot_ref.shape[1]
+    for cell in range(3):
+        ids = ids_ref[cell : cell + 1, :]
+        hot_ref[cell] = hot_columns(ids - cell_of(ids, atoms) * atoms, atoms)
 
 
 def unfold_block(block, atoms):
@@ -508,7 +515,7 @@
             )
 
 
-def first_back_kernel(slots, ids_ref, basis_ref, slope_ref, unit_ref, kind_high, kind_low, turn_high,
+def first_back_kernel(slots, ids_ref, hot_ref, basis_ref, slope_ref, unit_ref, kind_high, kind_low, turn_high,
                       turn_low, sums_ref, gate_ref, edge_ref, from_beyond, long_ref, middle_ref,
                       from_pair, *outs):
     sums = {(1, 2): long_ref[...]}
@@ -517,7 +524,7 @@
             from_pair[cell].astype(F32) + from_beyond[cell].astype(F32)
         )
         own, found = first_back_cell(
-            slots, ids_ref[cell : cell + 1, :], basis_ref.at[cell], slope_ref.at[cell],
+            slots, ids_ref[cell : cell + 1, :], hot_ref.at[cell], basis_ref.at[cell], slope_ref.at[cell],
             unit_ref.at[cell], kind_high, kind_low, turn_high, turn_low, sums_ref.at[cell],
             gate_ref.at[cell], edge_ref if cell == 1 else None, cotangent,
         )
@@ -530,7 +537,7 @@
         outs[x][...] = jnp.concatenate(rows + [jnp.zeros((1, rows[0].shape[1]), F32)], axis=0)
 
 
-def first_back_cell(slots, ids, basis_ref, slope_ref, unit_ref, kind_high, kind_low, turn_high,
+def first_back_cell(slots, ids, hot_ref, basis_ref, slope_ref, unit_ref, kind_high, kind_low, turn_high,
                     turn_low, sums_ref, gate_ref, edge_ref, cotangent):
     atoms = gate_ref.shape[1]
     pre = cotangent * gate_ref[...]
@@ -572,13 +579,12 @@
     for n in range(1, slots):
         own = own - move[:, n * atoms : (n + 1) * atoms]
     source = cell_of(ids, atoms)
-    atom_hot = hot_columns(ids - source * atoms, atoms)
     high = move.astype(BF16).astype(F32)
     both = jnp.concatenate([high, move - high], axis=0)
     rows = jnp.concatenate(
         [jnp.where(source == cell, both, 0.0).astype(BF16) for cell in range(9)], axis=0
     )
-    spread = dot(rows, atom_hot, ((1,), (1,)))
+    spread = dot(rows, hot_ref[...], ((1,), (1,)))
     grads = [
         spread[16 * cell : 16 * cell + 8] + spread[16 * cell + 8 : 16 * cell + 16]
         for cell in range(9)
@@ -1020,6 +1026,14 @@
     )
     folds = [folds[0]] + [paired(folds[d], "gx", 2 * d) for d in range(1, half)]
 
+    (atom_hot,) = run(
+        atom_hot_kernel,
+        [shape(3, atoms, edges, dtype=BF16)],
+        [ids],
+        flops=1_000_000_000,
+        name="atom_hot",
+    )
+    folds[1], atom_hot = lax.optimization_barrier((folds[1], atom_hot))
     site, long, cotangent, grads, term, to_beyond = run(
         functools.partial(second_back_kernel, slots, scale, half),
         [
@@ -1066,7 +1080,7 @@
     to_pair, middle, to_beyond = run(
         functools.partial(first_back_kernel, slots),
         [shape(16, atoms)] * 3,
-        [ids, basis, slope, unit, kind_high, kind_low, turn_high, turn_low, sums_one, gate_one, edge,
+        [ids, atom_hot, basis, slope, unit, kind_high, kind_low, turn_high, turn_low, sums_one, gate_one, edge,
          from_beyond, long, middle, from_pair],
         name="first_back",
     )

time: 83.4 us -> 85.9 us (1.030)
  waiting for transfers between devices: 24.2 us -> 26.1 us
    ppermute x6, waiting for transfers between devices: 12.6 us -> 17 us  [beyond(): lax.ppermute(block, axis, [(other_side(i, count), i) for i in range(count)])]
    ppermute x17, waiting for transfers between devices: 11.5 us -> 8.93 us  [paired(): lax.ppermute(block, axis, [(i ^ mask, i) for i in range(lax.axis_size(axi...]
    ppermute x6, starting transfers between devices: 9.25 us -> 7.13 us  [beyond(): lax.ppermute(block, axis, [(other_side(i, count), i) for i in range(count)])]
    ppermute x17, starting transfers between devices: 14.5 us -> 16.4 us  [paired(): lax.ppermute(block, axis, [(i ^ mask, i) for i in range(lax.axis_size(axi...]
    pallas_call x23 -> x24, Pallas kernels: 28.3 us -> 29 us  [run(): pl.pallas_call(kernel, out_shape=outs, in_specs=specs, out_specs=[whole()...]
where the time goes in v21:
time: 85.9 us; the launch traced here: 85.7 us
  Pallas kernels  29 us (34%)
  starting transfers between devices  27.4 us (32%)
  waiting for transfers between devices  26.1 us (30%)
  local copies, waits for them, and re-layouts  2.07 us (2%)
  between operations  0.94 us (1%)
    pallas_call x24, Pallas kernels, run(): pl.pallas_call(kernel, out_shape=outs, in_specs=specs, out_specs=[whole()...  29 us
    ppermute x6, waiting for transfers between devices, beyond(): lax.ppermute(block, axis, [(other_side(i, count), i) for i in range(count)])  17 us
    ppermute x17, starting transfers between devices, paired(): lax.ppermute(block, axis, [(i ^ mask, i) for i in range(lax.axis_size(axi...  16.4 us
    ppermute x17, waiting for transfers between devices, paired(): lax.ppermute(block, axis, [(i ^ mask, i) for i in range(lax.axis_size(axi...  8.93 us
    ppermute x6, starting transfers between devices, beyond(): lax.ppermute(block, axis, [(other_side(i, count), i) for i in range(count)])  7.13 us
    ppermute x2, starting transfers between devices, far(): return lax.ppermute(block, axis, route)  3.89 us
    unnamed x27, local copies, waits for them, and re-layouts  2 us
  transfers between devices with their start and end apart: 25, of which 15 were waited for; matrix products, arithmetic and copies ran while one was open for 0% of the time, Pallas kernels for 17%

profile of v21, /device:TPU:0, one launch (start us, length us, event | category | flops | bytes accessed | tf_op | source)
XLA Modules:
  0.0 85.7 jit_solution(14688916211644509411)
XLA Ops:
  0.6 0.1 pad_add_fusion
  0.7 0.1 broadcast_in_dim.4.place_ref
  0.8 0.7 copy-done.9
  1.5 0.7 copy-done.10
  2.2 3.0 %collective-permute-start.2 = (f32[8,128]{1,0:T(8,128)S(1)}, f32[8,128]{1,0:T(8,128)S(1)}, u32[]{:S(2)}, u32[]{:S(2)}) collective-permute-start(f32[8,128]{1,0:T(8,128)S(1)} %pack.1.first_ref), channel_id=1, source_target_pairs={{2,0},{3,1},{0,2},{1,3},{6,4},{7,5},{4,6},{5,7},{10,8},{11,9},{8,1... | collective-permute-start | bytes 12296 | tf_op jit(solution)/shard_map/ppermute | solution.py:42
  5.3 0.1 pack_more.1.own_ref
  5.4 1.6 %collective-permute-start.1 = (f32[40,128]{1,0:T(8,128)S(1)}, f32[40,128]{1,0:T(8,128)S(1)}, u32[]{:S(2)}, u32[]{:S(2)}) collective-permute-start(f32[40,128]{1,0:T(8,128)S(1)} %pack_more.1.own_ref), channel_id=1, source_target_pairs={{1,0},{0,1},{3,2},{2,3},{5,4},{4,5},{7,6},{6,7},{9,8},{8,9},{11,10... | collective-permute-start | bytes 61448 | tf_op jit(solution)/shard_map/ppermute | solution.py:24
  6.9 0.5 collective-permute-start
  7.5 1.9 %collective-permute-done.1.y_pair_ref = f32[40,128]{1,0:T(8,128)S(1)} collective-permute-done((f32[40,128]{1,0:T(8,128)S(1)}, f32[40,128]{1,0:T(8,128)S(1)}, u32[]{:S(2)}, u32[]{:S(2)}) %collective-permute-start.1) | collective-permute-done | bytes 20512 | tf_op jit(solution)/shard_map/ppermute | solution.py:24
  9.4 2.2 %collective-permute-done.y_beyond_ref = f32[40,128]{1,0:T(8,128)S(1)} collective-permute-done((f32[40,128]{1,0:T(8,128)S(1)}, f32[40,128]{1,0:T(8,128)S(1)}, u32[]{:S(2)}, u32[]{:S(2)}) %collective-permute-start) | collective-permute-done | bytes 20512 | tf_op jit(solution)/shard_map/ppermute | solution.py:33
  11.6 1.3 %collective-permute-start.3 = (f32[5,8,128]{2,1,0:T(8,128)S(1)}, f32[5,8,128]{2,1,0:T(8,128)S(1)}, u32[]{:S(2)}, u32[]{:S(2)}) collective-permute-start(f32[5,8,128]{2,1,0:T(8,128)S(1)} %constant_dynamic-update-slice_fusion.column_ref.cell_ref), channel_id=1, source_target_pairs={{28,0},{8,4},{4,8},{16,12},{12,16},{24,20},{20,24},{0,28},{29,1},{... | collective-permute-start | bytes 61448 | tf_op jit(solution)/shard_map/ppermute | solution.py:33
  13.0 0.4 collective-permute-start.4
  13.3 0.3 prep_second.1
  13.6 0.3 prep_first.1
  13.9 2.7 %collective-permute-done.3.beyond_ref = f32[5,8,128]{2,1,0:T(8,128)S(1)} collective-permute-done((f32[5,8,128]{2,1,0:T(8,128)S(1)}, f32[5,8,128]{2,1,0:T(8,128)S(1)}, u32[]{:S(2)}, u32[]{:S(2)}) %collective-permute-start.3) | collective-permute-done | bytes 20512 | tf_op jit(solution)/shard_map/ppermute | solution.py:33
  16.6 2.9 %first.1 = (bf16[3,128,256]{2,1,0:T(8,128)(2,1)S(1)}, s32[3,3072]{1,0:T(4,128)S(1)}, f32[3,8,3072]{2,1,0:T(8,128)S(1)}, f32[3,8,3072]{2,1,0:T(8,128)S(1)}, f32[3...) custom-call(s32[2,8,128]{2,1,0:T(8,128)S(1)} %broadcast_in_dim.4.place_ref, ...), custom_call_target="tpu_custom_call" | custom-call | flops 10000000 | bytes 1000000 | tf_op jit(solution)/shard_map/first/pallas_call | solution.py:55
  19.6 2.1 %collective-permute-start.6 = (bf16[3,128,256]{2,1,0:T(8,128)(2,1)S(1)}, bf16[3,128,256]{2,1,0:T(8,128)(2,1)S(1)}, u32[]{:S(2)}, u32[]{:S(2)}) collective-permute-start(bf16[3,128,256]{2,1,0:T(8,128)(2,1)S(1)} %get-tuple-element.86.column_ref), channel_id=1, source_target_pairs={{28,0},{8,4},{4,8},{16,12},{12,16},{24,20},{20,24},{0,28},{29,1},{... | collective-permute-start | bytes 589832 | tf_op jit(solution)/shard_map/ppermute | solution.py:33
  21.8 1.7 %second_near.1 = (f32[4,128,3072]{2,1,0:T(8,128)S(1)}, f32[128,3072]{1,0:T(8,128)S(1)}) custom-call(s32[3,3072]{1,0:T(4,128)S(1)} %get-tuple-element.82.ids_ref, f32[3,8,3072]{2,1,0:T(8,128)S(1)} %get-tuple-element.83.basis_ref, f32[3,8,3072]{2,1,0:T(8,128)S(1)} %get-tuple-element.84.unit_ref, bf16[2,128,32]{2,1,0:T(8,128)(2,1)S(1)} %get-tuple-element.85.left_ref, ...), custom_call_target="tpu_custom_call" | custom-call | flops 2000000000 | bytes 1000000 | tf_op jit(solution)/shard_map/second_near/pallas_call | solution.py:55
  23.5 1.0 %hot_beyond.1.hot_ref = bf16[768,3072]{1,0:T(8,128)(2,1)S(1)} custom-call(s32[3,3072]{1,0:T(4,128)S(1)} %get-tuple-element.82.ids_ref, f32[128,3072]{1,0:T(8,128)S(1)} %get-tuple-element.87.near_ref), custom_call_target="tpu_custom_call" | custom-call | flops 1000000 | bytes 1000000 | tf_op jit(solution)/shard_map/hot_beyond/pallas_call | solution.py:55
  24.5 0.8 second_side.1.near_ref
  25.3 2.5 %collective-permute-done.6.beyond_ref = bf16[3,128,256]{2,1,0:T(8,128)(2,1)S(1)} collective-permute-done((bf16[3,128,256]{2,1,0:T(8,128)(2,1)S(1)}, bf16[3,128,256]{2,1,0:T(8,128)(2,1)S(1)}, u32[]{:S(2)}, u32[]{:S(2)}) %collective-permute-start.6) | collective-permute-done | bytes 196640 | tf_op jit(solution)/shard_map/ppermute | solution.py:33
  27.7 1.9 %second.1 = (bf16[128,3072]{1,0:T(8,128)(2,1)S(1)}, f32[3,128,256]{2,1,0:T(8,128)S(1)}, f32[128,256]{1,0:T(8,128)S(1)}, bf16[80,256]{1,0:T(8,128)(2,1)S(1)}, f32...) custom-call(bf16[768,3072]{1,0:T(8,128)(2,1)S(1)} %hot_beyond.1.hot_ref, f32[4,128,3072]{2,1,0:T(8,128)S(1)} %get-tuple-element.88.weight_ref, ...), custom_call_target="tpu_custom_call" | custom-call | flops 10000000 | bytes 1000000 | tf_op jit(solution)/shard_map/second/pallas_call | solution.py:55
  29.7 0.1 collective-permute-start.8
  29.8 4.3 %collective-permute-start.9 = (bf16[80,256]{1,0:T(8,128)(2,1)S(1)}, bf16[80,256]{1,0:T(8,128)(2,1)S(1)}, u32[]{:S(2)}, u32[]{:S(2)}) collective-permute-start(bf16[80,256]{1,0:T(8,128)(2,1)S(1)} %get-tuple-element.90), channel_id=1, source_target_pairs={{24,0},{28,4},{16,8},{20,12},{8,16},{12,20},{0,24},{4,28},{25,1},{... | collective-permute-start | bytes 122888 | tf_op jit(solution)/shard_map/ppermute | solution.py:24
  34.1 0.8 green.1.refs_0_
  34.9 1.8 %collective-permute-done.9 = bf16[80,256]{1,0:T(8,128)(2,1)S(1)} collective-permute-done((bf16[80,256]{1,0:T(8,128)(2,1)S(1)}, bf16[80,256]{1,0:T(8,128)(2,1)S(1)}, u32[]{:S(2)}, u32[]{:S(2)}) %collective-permute-start.9) | collective-permute-done | bytes 40992 | tf_op jit(solution)/shard_map/ppermute | solution.py:24
  36.7 0.1 collective-permute-start.10
  36.8 1.2 %structure_near.1 = (f32[32,1024]{1,0:T(8,128)S(1)}, f32[32,1024]{1,0:T(8,128)S(1)}, f32[8,1024]{1,0:T(8,128)S(1)}, f32[8,1024]{1,0:T(8,128)S(1)}, bf16[640,1024...) custom-call(s32[2,8,128]{2,1,0:T(8,128)S(1)} %broadcast_in_dim.4.place_ref, ...), custom_call_target="tpu_custom_call" | custom-call | flops 1000000000 | bytes 1000000 | tf_op jit(solution)/shard_map/structure_near/pallas_call | solution.py:55
  38.0 0.2 collective-permute-done.10.blocks.refs_11_
  38.2 1.2 %structure_far.1 = (f32[32,1024]{1,0:T(8,128)S(1)}, f32[32,1024]{1,0:T(8,128)S(1)}, f32[8,1024]{1,0:T(8,128)S(1)}, f32[8,1024]{1,0:T(8,128)S(1)}, bf16[640,1024]...) custom-call(s32[2,8,128]{2,1,0:T(8,128)S(1)} %broadcast_in_dim.4.place_r, ...), custom_call_target="tpu_custom_call" | custom-call | flops 10000000 | bytes 1000000 | tf_op jit(solution)/shard_map/structure_far/pallas_call | solution.py:55
  39.4 0.6 collective-permute-start.11
  40.0 0.3 collective-permute-start.12
  40.4 2.6 %collective-permute-start.13 = (bf16[320,128]{1,0:T(8,128)(2,1)S(1)}, bf16[320,128]{1,0:T(8,128)(2,1)S(1)}, u32[]{:S(2)}, u32[]{:S(2)}) collective-permute-start(bf16[320,128]{1,0:T(8,128)(2,1)S(1)} %get-tuple-element.95), channel_id=1, source_target_pairs={{3,0},{2,1},{1,2},{0,3},{7,4},{6,5},{5,6},{4,7},{11,8},{10,9},{9,1... | collective-permute-start | bytes 245768 | tf_op jit(solution)/shard_map/ppermute | solution.py:24
  43.0 2.3 %hot_back.1.hot_ref = bf16[3072,1536]{1,0:T(8,128)(2,1)S(1)} custom-call(s32[3,3072]{1,0:T(4,128)S(1)} %get-tuple-element.82.ids_ref), custom_call_target="tpu_custom_call" | custom-call | flops 2000000000 | bytes 1000000 | tf_op jit(solution)/shard_map/hot_back/pallas_call | solution.py:55
  45.3 1.0 %collective-permute-done.12.refs_3_ = bf16[320,128]{1,0:T(8,128)(2,1)S(1)} collective-permute-done((bf16[320,128]{1,0:T(8,128)(2,1)S(1)}, bf16[320,128]{1,0:T(8,128)(2,1)S(1)}, u32[]{:S(2)}, u32[]{:S(2)}) %collective-permute-start.12) | collective-permute-done | bytes 81952 | tf_op jit(solution)/shard_map/ppermute | solution.py:24
  46.2 1.3 %fold_far.1 = (bf16[4,80,256]{2,1,0:T(8,128)(2,1)S(1)}, f32[640,64]{1,0:T(8,128)S(1)}) custom-call(s32[2,8,128]{2,1,0:T(8,128)S(1)} %broadcast_in_dim.4.place_ref, f32[320,128]{1,0:T(8,128)S(1)} %green.1.refs_0_, f32[320,128]{1,0:T(8,128)S(1)} %get-tuple-element.96.refs_1_, bf16[320,128]{1,0:T(8,128)(2,1)S(1)} %collective-permute-done.11.refs_2_, ...), custom_call_target="tpu_custom_call" | custom-call | flops 10000000 | bytes 1000000 | tf_op jit(solution)/shard_map/fold_far/pallas_call | solution.py:55
  47.6 0.1 collective-permute-start.14
  47.7 1.2 %fold_near.1.near_ref = f32[4,80,256]{2,1,0:T(8,128)S(1)} custom-call(s32[2,8,128]{2,1,0:T(8,128)S(1)} %broadcast_in_dim.4.place_ref, f32[640,64]{1,0:T(8,128)S(1)} %get-tuple-element.106.refs_0_, f32[32,1024]{1,0:T(8,128)S(1)} %get-tuple-element.107.refs_1_, f32[32,1024]{1,0:T(8,128)S(1)} %get-tuple-element.108.refs_2_, ...), custom_call_target="tpu_custom_call" | custom-call | flops 1000000000 | bytes 1000000 | tf_op jit(solution)/shard_map/fold_near/pallas_call | solution.py:55
  48.9 0.2 collective-permute-done.14.far_ref
  49.1 0.2 collective-permute-start.15
  49.3 3.6 %collective-permute-start.16 = (bf16[80,256]{1,0:T(8,128)(2,1)S(1)}, bf16[80,256]{1,0:T(8,128)(2,1)S(1)}, u32[]{:S(2)}, u32[]{:S(2)}) collective-permute-start(bf16[80,256]{1,0:T(8,128)(2,1)S(1)} %get-tuple-element.139), channel_id=1, source_target_pairs={{16,0},{20,4},{24,8},{28,12},{0,16},{4,20},{8,24},{12,28},{17,1},{... | collective-permute-start | bytes 122888 | tf_op jit(solution)/shard_map/ppermute | solution.py:24
  52.9 0.7 collective-permute-start.17
  53.6 0.8 atom_hot.1.hot_ref
  54.4 0.5 readout.1
  54.9 0.8 collective-permute-done.16.refs_2_
  55.8 2.9 %collective-permute-done.17.refs_3_ = bf16[80,256]{1,0:T(8,128)(2,1)S(1)} collective-permute-done((bf16[80,256]{1,0:T(8,128)(2,1)S(1)}, bf16[80,256]{1,0:T(8,128)(2,1)S(1)}, u32[]{:S(2)}, u32[]{:S(2)}) %collective-permute-start.17) | collective-permute-done | bytes 40992 | tf_op jit(solution)/shard_map/ppermute | solution.py:24
  58.7 2.2 %second_back.1 = (f32[1,1,256]{2,1,0:T(1,128)}, f32[8,256]{1,0:T(8,128)S(1)}, f32[128,256]{1,0:T(8,128)S(1)}, f32[4,128,256]{2,1,0:T(8,128)S(1)}, bf16[128,3072]...) custom-call(bf16[3072,1536]{1,0:T(8,128)(2,1)S(1)} %hot_back.1.hot_ref, ...), custom_call_target="tpu_custom_call" | custom-call | flops 10000000 | bytes 1000000 | tf_op jit(solution)/shard_map/second_back/pallas_call | solution.py:55
  60.9 0.8 second_pair.1
  61.8 0.8 collective-permute-start.18
  62.6 1.3 %hot_middle.1.hot_ref = bf16[3072,768]{1,0:T(8,128)(2,1)S(1)} custom-call(s32[3,3072]{1,0:T(4,128)S(1)} %get-tuple-element.82.ids_ref), custom_call_target="tpu_custom_call" | custom-call | flops 1000000000 | bytes 1000000 | tf_op jit(solution)/shard_map/hot_middle/pallas_call | solution.py:55
  63.9 0.8 second_middle.1.middle_ref
  64.7 1.2 %second_edge.1.edge_ref = f32[32,3072]{1,0:T(8,128)S(1)} custom-call(bf16[2,16,256]{2,1,0:T(8,128)(2,1)S(1)} %get-tuple-element.123.back_ref, bf16[128,3072]{1,0:T(8,128)(2,1)S(1)} %get-tuple-element.124.feature_ref, f32[4,128,256]{2,1,0:T(8,128)S(1)} %get-tuple-element.141.grad_ref), custom_call_target="tpu_custom_call" | custom-call | flops 1000000000 | bytes 1000000 | tf_op jit(solution)/shard_map/second_edge/pallas_call | solution.py:55
  66.0 3.4 %collective-permute-done.18.from_beyond = bf16[3,128,256]{2,1,0:T(8,128)(2,1)S(1)} collective-permute-done((bf16[3,128,256]{2,1,0:T(8,128)(2,1)S(1)}, bf16[3,128,256]{2,1,0:T(8,128)(2,1)S(1)}, u32[]{:S(2)}, u32[]{:S(2)}) %collective-permute-start.18) | collective-permute-done | bytes 196640 | tf_op jit(solution)/shard_map/ppermute | solution.py:33
  69.4 4.3 %first_back.1 = (f32[16,256]{1,0:T(8,128)S(1)}, f32[16,256]{1,0:T(8,128)S(1)}, f32[16,256]{1,0:T(8,128)S(1)}) custom-call(s32[3,3072]{1,0:T(4,128)S(1)} %get-tuple-element.82.ids_ref, bf16[3,256,3072]{2,1,0:T(8,128)(2,1)S(1)} %atom_hot.1.hot_ref, f32[3,8,3072]{2,1,0:T(8,128)S(1)} %get-tuple-element.83.basis_ref, ...), custom_call_target="tpu_custom_call" | custom-call | flops 10000000 | bytes 1000000 | tf_op jit(solution)/shard_map/first_back/pallas_call | solution.py:55
  73.6 0.2 collective-permute-start.20
  73.8 1.2 %collective-permute-start.21 = (f32[16,256]{1,0:T(8,128)S(1)}, f32[16,256]{1,0:T(8,128)S(1)}, u32[]{:S(2)}, u32[]{:S(2)}) collective-permute-start(f32[16,256]{1,0:T(8,128)S(1)} %get-tuple-element.148), channel_id=1, source_target_pairs={{28,0},{8,4},{4,8},{16,12},{12,16},{24,20},{20,24},{0,28},{29,1},{... | collective-permute-start | bytes 49160 | tf_op jit(solution)/shard_map/ppermute | solution.py:33
  75.0 3.8 %collective-permute-done.21 = f32[16,256]{1,0:T(8,128)S(1)} collective-permute-done((f32[16,256]{1,0:T(8,128)S(1)}, f32[16,256]{1,0:T(8,128)S(1)}, u32[]{:S(2)}, u32[]{:S(2)}) %collective-permute-start.21) | collective-permute-done | bytes 16416 | tf_op jit(solution)/shard_map/ppermute | solution.py:33
  78.8 1.6 %collective-permute-start.22 = (f32[3,256]{1,0:T(4,128)S(1)}, f32[3,256]{1,0:T(4,128)S(1)}, u32[]{:S(2)}, u32[]{:S(2)}) collective-permute-start(f32[3,256]{1,0:T(4,128)S(1)} %get-tuple-element.152), channel_id=1, source_target_pairs={{1,0},{0,1},{3,2},{2,3},{5,4},{4,5},{7,6},{6,7},{9,8},{8,9},{11,10... | collective-permute-start | bytes 9224 | tf_op jit(solution)/shard_map/ppermute | solution.py:24
  80.3 1.1 %collective-permute-start.23 = (f32[3,256]{1,0:T(4,128)S(1)}, f32[3,256]{1,0:T(4,128)S(1)}, u32[]{:S(2)}, u32[]{:S(2)}) collective-permute-start(f32[3,256]{1,0:T(4,128)S(1)} %get-tuple-element.154), channel_id=1, source_target_pairs={{3,0},{2,1},{1,2},{0,3},{7,4},{6,5},{5,6},{4,7},{11,8},{10,9},{9,1... | collective-permute-start | bytes 9224 | tf_op jit(solution)/shard_map/ppermute | solution.py:33
  81.5 0.9 %collective-permute-start.24 = (f32[3,256]{1,0:T(4,128)S(1)}, f32[3,256]{1,0:T(4,128)S(1)}, u32[]{:S(2)}, u32[]{:S(2)}) collective-permute-start(f32[3,256]{1,0:T(4,128)S(1)} %get-tuple-element.153), channel_id=1, source_target_pairs={{2,0},{3,1},{0,2},{1,3},{6,4},{7,5},{4,6},{5,7},{10,8},{11,9},{8,1... | collective-permute-start | bytes 9224 | tf_op jit(solution)/shard_map/ppermute | solution.py:42
  82.3 0.1 collective-permute-done.22
  82.5 2.4 %collective-permute-done.23 = f32[3,256]{1,0:T(4,128)S(1)} collective-permute-done((f32[3,256]{1,0:T(4,128)S(1)}, f32[3,256]{1,0:T(4,128)S(1)}, u32[]{:S(2)}, u32[]{:S(2)}) %collective-permute-start.23) | collective-permute-done | bytes 3104 | tf_op jit(solution)/shard_map/ppermute | solution.py:33
  84.8 0.2 collective-permute-done.24
  85.1 0.6 copy.13
  (44 shorter events, 0.4 us)
Async XLA Ops:
  0.8 0.7 copy-start.9
  1.5 0.7 copy-start.10
  2.1 3.1 %copy-start.5 = (s32[1,1,256,12]{2,1,3,0:T(1,128)S(1)}, s32[1,1,256,12]{2,1,3,0:T(1,128)}, u32[]{:S(2)}) copy-start(s32[1,1,256,12]{2,1,3,0:T(1,128)} %param.13) | copy-start | bytes 36868
  2.2 3.1 %copy-start.7 = (s32[1,1,256]{2,1,0:T(1,128)S(1)}, s32[1,1,256]{2,1,0:T(1,128)}, u32[]{:S(2)}) copy-start(s32[1,1,256]{2,1,0:T(1,128)} %count_ref.1) | copy-start | bytes 3076
  2.2 11.2 %copy-start.1 = (f32[128,128]{1,0:T(8,128)S(1)}, f32[128,128]{1,0:T(8,128)}, u32[]{:S(2)}) copy-start(f32[128,128]{1,0:T(8,128)} %hidden_in.1) | copy-start | bytes 196612
  2.2 11.2 %copy-start.3 = (f32[128,64]{0,1:T(8,128)S(1)}, f32[128,64]{0,1:T(8,128)}, u32[]{:S(2)}) copy-start(f32[128,64]{0,1:T(8,128)} %param.20) | copy-start | bytes 98308
  2.2 11.2 %copy-start.8 = (f32[128]{0:T(128)S(1)}, f32[128]{0:T(128)}, u32[]{:S(2)}) copy-start(f32[128]{0:T(128)} %param.19) | copy-start | bytes 1540
  2.2 11.4 %copy-start = (f32[2,2,128,128]{3,2,1,0:T(8,128)S(1)}, f32[2,2,128,128]{3,2,1,0:T(8,128)}, u32[]{:S(2)}) copy-start(f32[2,2,128,128]{3,2,1,0:T(8,128)} %mixing_in.1) | copy-start | bytes 786436
  2.2 11.4 %copy-start.4 = (f32[2,2,8,128]{3,2,1,0:T(8,128)S(1)}, f32[2,2,8,128]{3,2,1,0:T(8,128)}, u32[]{:S(2)}) copy-start(f32[2,2,8,128]{3,2,1,0:T(8,128)} %radial_in.1) | copy-start | bytes 49156
  2.2 11.4 %copy-start.6 = (f32[6,128]{1,0:T(8,128)S(1)}, f32[6,128]{1,0:T(8,128)}, u32[]{:S(2)}) copy-start(f32[6,128]{1,0:T(8,128)} %embed_in.1) | copy-start | bytes 9220
  2.2 5.3 %collective-permute-start.2 = (f32[8,128]{1,0:T(8,128)S(1)}, f32[8,128]{1,0:T(8,128)S(1)}, u32[]{:S(2)}, u32[]{:S(2)}) collective-permute-start(f32[8,128]{1,0:T(8,128)S(1)} %pack.1.first_ref), channel_id=1, source_target_pairs={{2,0},{3,1},{0,2},{1,3},{6,4},{7,5},{4,6},{5,7},{10,8},{11,9},{8,1... | collective-permute-start | bytes 12296 | tf_op jit(solution)/shard_map/ppermute | solution.py:42
  5.4 4.0 %collective-permute-start.1 = (f32[40,128]{1,0:T(8,128)S(1)}, f32[40,128]{1,0:T(8,128)S(1)}, u32[]{:S(2)}, u32[]{:S(2)}) collective-permute-start(f32[40,128]{1,0:T(8,128)S(1)} %pack_more.1.own_ref), channel_id=1, source_target_pairs={{1,0},{0,1},{3,2},{2,3},{5,4},{4,5},{7,6},{6,7},{9,8},{8,9},{11,10... | collective-permute-start | bytes 61448 | tf_op jit(solution)/shard_map/ppermute | solution.py:24
  6.9 4.7 %collective-permute-start = (f32[40,128]{1,0:T(8,128)S(1)}, f32[40,128]{1,0:T(8,128)S(1)}, u32[]{:S(2)}, u32[]{:S(2)}) collective-permute-start(f32[40,128]{1,0:T(8,128)S(1)} %pack_more.1.own_ref), channel_id=1, source_target_pairs={{3,0},{2,1},{1,2},{0,3},{7,4},{6,5},{5,6},{4,7},{11,8},{10,9},{9,1... | collective-permute-start | bytes 61448 | tf_op jit(solution)/shard_map/ppermute | solution.py:33
  11.6 5.0 %collective-permute-start.3 = (f32[5,8,128]{2,1,0:T(8,128)S(1)}, f32[5,8,128]{2,1,0:T(8,128)S(1)}, u32[]{:S(2)}, u32[]{:S(2)}) collective-permute-start(f32[5,8,128]{2,1,0:T(8,128)S(1)} %constant_dynamic-update-slice_fusion.column_ref.cell_ref), channel_id=1, source_target_pairs={{28,0},{8,4},{4,8},{16,12},{12,16},{24,20},{20,24},{0,28},{29,1},{... | collective-permute-start | bytes 61448 | tf_op jit(solution)/shard_map/ppermute | solution.py:33
  13.0 3.7 %collective-permute-start.4 = (f32[5,8,128]{2,1,0:T(8,128)S(1)}, f32[5,8,128]{2,1,0:T(8,128)S(1)}, u32[]{:S(2)}, u32[]{:S(2)}) collective-permute-start(f32[5,8,128]{2,1,0:T(8,128)S(1)} %constant_dynamic-update-slice_fusion.column_ref.cell_ref), channel_id=1, source_target_pairs={{4,0},{0,4},{12,8},{8,12},{20,16},{16,20},{28,24},{24,28},{5,1},{1... | collective-permute-start | bytes 61448 | tf_op jit(solution)/shard_map/ppermute | solution.py:24
  19.5 4.9 %collective-permute-start.5 = (bf16[3,128,256]{2,1,0:T(8,128)(2,1)S(1)}, bf16[3,128,256]{2,1,0:T(8,128)(2,1)S(1)}, u32[]{:S(2)}, u32[]{:S(2)}) collective-permute-start(bf16[3,128,256]{2,1,0:T(8,128)(2,1)S(1)} %get-tuple-element.86.column_ref), channel_id=1, source_target_pairs={{4,0},{0,4},{12,8},{8,12},{20,16},{16,20},{28,24},{24,28},{5,1},{1... | collective-permute-start | bytes 589832 | tf_op jit(solution)/shard_map/ppermute | solution.py:24
  19.6 8.1 %collective-permute-start.6 = (bf16[3,128,256]{2,1,0:T(8,128)(2,1)S(1)}, bf16[3,128,256]{2,1,0:T(8,128)(2,1)S(1)}, u32[]{:S(2)}, u32[]{:S(2)}) collective-permute-start(bf16[3,128,256]{2,1,0:T(8,128)(2,1)S(1)} %get-tuple-element.86.column_ref), channel_id=1, source_target_pairs={{28,0},{8,4},{4,8},{16,12},{12,16},{24,20},{20,24},{0,28},{29,1},{... | collective-permute-start | bytes 589832 | tf_op jit(solution)/shard_map/ppermute | solution.py:33
  27.7 6.3 %copy-start.2 = (s32[3,4096]{1,0:T(4,128)S(1)}, s32[3,4096]{1,0:T(4,128)}, u32[]{:S(2)}) copy-start(s32[3,4096]{1,0:T(4,128)} %vec_ref.1) | copy-start | bytes 147460
  29.6 5.3 %collective-permute-start.7 = (bf16[80,256]{1,0:T(8,128)(2,1)S(1)}, bf16[80,256]{1,0:T(8,128)(2,1)S(1)}, u32[]{:S(2)}, u32[]{:S(2)}) collective-permute-start(bf16[80,256]{1,0:T(8,128)(2,1)S(1)} %get-tuple-element.90), channel_id=1, source_target_pairs={{8,0},{12,4},{0,8},{4,12},{24,16},{28,20},{16,24},{20,28},{9,1},{1... | collective-permute-start | bytes 122888 | tf_op jit(solution)/shard_map/ppermute | solution.py:24
  29.7 5.2 %collective-permute-start.8 = (bf16[80,256]{1,0:T(8,128)(2,1)S(1)}, bf16[80,256]{1,0:T(8,128)(2,1)S(1)}, u32[]{:S(2)}, u32[]{:S(2)}) collective-permute-start(bf16[80,256]{1,0:T(8,128)(2,1)S(1)} %get-tuple-element.90), channel_id=1, source_target_pairs={{16,0},{20,4},{24,8},{28,12},{0,16},{4,20},{8,24},{12,28},{17,1},{... | collective-permute-start | bytes 122888 | tf_op jit(solution)/shard_map/ppermute | solution.py:24
  29.8 6.9 %collective-permute-start.9 = (bf16[80,256]{1,0:T(8,128)(2,1)S(1)}, bf16[80,256]{1,0:T(8,128)(2,1)S(1)}, u32[]{:S(2)}, u32[]{:S(2)}) collective-permute-start(bf16[80,256]{1,0:T(8,128)(2,1)S(1)} %get-tuple-element.90), channel_id=1, source_target_pairs={{24,0},{28,4},{16,8},{20,12},{8,16},{12,20},{0,24},{4,28},{25,1},{... | collective-permute-start | bytes 122888 | tf_op jit(solution)/shard_map/ppermute | solution.py:24
  36.7 1.5 %collective-permute-start.10 = (bf16[4,80,256]{2,1,0:T(8,128)(2,1)S(1)}, bf16[4,80,256]{2,1,0:T(8,128)(2,1)S(1)}, u32[]{:S(2)}, u32[]{:S(2)}) collective-permute-start(bf16[4,80,256]{2,1,0:T(8,128)(2,1)S(1)} %pad_maximum_fusion.blocks.refs_7_), channel_id=1, source_target_pairs={{4,0},{0,4},{12,8},{8,12},{20,16},{16,20},{28,24},{24,28},{5,1},{1... | collective-permute-start | bytes 491528 | tf_op jit(solution)/shard_map/ppermute | solution.py:24
  39.4 5.8 %collective-permute-start.11 = (bf16[320,128]{1,0:T(8,128)(2,1)S(1)}, bf16[320,128]{1,0:T(8,128)(2,1)S(1)}, u32[]{:S(2)}, u32[]{:S(2)}) collective-permute-start(bf16[320,128]{1,0:T(8,128)(2,1)S(1)} %get-tuple-element.95), channel_id=1, source_target_pairs={{1,0},{0,1},{3,2},{2,3},{5,4},{4,5},{7,6},{6,7},{9,8},{8,9},{11,10... | collective-permute-start | bytes 245768 | tf_op jit(solution)/shard_map/ppermute | solution.py:24
  40.0 6.2 %collective-permute-start.12 = (bf16[320,128]{1,0:T(8,128)(2,1)S(1)}, bf16[320,128]{1,0:T(8,128)(2,1)S(1)}, u32[]{:S(2)}, u32[]{:S(2)}) collective-permute-start(bf16[320,128]{1,0:T(8,128)(2,1)S(1)} %get-tuple-element.95), channel_id=1, source_target_pairs={{2,0},{3,1},{0,2},{1,3},{6,4},{7,5},{4,6},{5,7},{10,8},{11,9},{8,1... | collective-permute-start | bytes 245768 | tf_op jit(solution)/shard_map/ppermute | solution.py:24
  40.4 5.9 %collective-permute-start.13 = (bf16[320,128]{1,0:T(8,128)(2,1)S(1)}, bf16[320,128]{1,0:T(8,128)(2,1)S(1)}, u32[]{:S(2)}, u32[]{:S(2)}) collective-permute-start(bf16[320,128]{1,0:T(8,128)(2,1)S(1)} %get-tuple-element.95), channel_id=1, source_target_pairs={{3,0},{2,1},{1,2},{0,3},{7,4},{6,5},{5,6},{4,7},{11,8},{10,9},{9,1... | collective-permute-start | bytes 245768 | tf_op jit(solution)/shard_map/ppermute | solution.py:24
  47.6 1.5 %collective-permute-start.14 = (bf16[4,80,256]{2,1,0:T(8,128)(2,1)S(1)}, bf16[4,80,256]{2,1,0:T(8,128)(2,1)S(1)}, u32[]{:S(2)}, u32[]{:S(2)}) collective-permute-start(bf16[4,80,256]{2,1,0:T(8,128)(2,1)S(1)} %get-tuple-element.113), channel_id=1, source_target_pairs={{4,0},{0,4},{12,8},{8,12},{20,16},{16,20},{28,24},{24,28},{5,1},{1... | collective-permute-start | bytes 491528 | tf_op jit(solution)/shard_map/ppermute | solution.py:24
  49.1 5.8 %collective-permute-start.15 = (bf16[80,256]{1,0:T(8,128)(2,1)S(1)}, bf16[80,256]{1,0:T(8,128)(2,1)S(1)}, u32[]{:S(2)}, u32[]{:S(2)}) collective-permute-start(bf16[80,256]{1,0:T(8,128)(2,1)S(1)} %get-tuple-element.114), channel_id=1, source_target_pairs={{8,0},{12,4},{0,8},{4,12},{24,16},{28,20},{16,24},{20,28},{9,1},{1... | collective-permute-start | bytes 122888 | tf_op jit(solution)/shard_map/ppermute | solution.py:24
  49.3 6.5 %collective-permute-start.16 = (bf16[80,256]{1,0:T(8,128)(2,1)S(1)}, bf16[80,256]{1,0:T(8,128)(2,1)S(1)}, u32[]{:S(2)}, u32[]{:S(2)}) collective-permute-start(bf16[80,256]{1,0:T(8,128)(2,1)S(1)} %get-tuple-element.139), channel_id=1, source_target_pairs={{16,0},{20,4},{24,8},{28,12},{0,16},{4,20},{8,24},{12,28},{17,1},{... | collective-permute-start | bytes 122888 | tf_op jit(solution)/shard_map/ppermute | solution.py:24
  52.9 5.8 %collective-permute-start.17 = (bf16[80,256]{1,0:T(8,128)(2,1)S(1)}, bf16[80,256]{1,0:T(8,128)(2,1)S(1)}, u32[]{:S(2)}, u32[]{:S(2)}) collective-permute-start(bf16[80,256]{1,0:T(8,128)(2,1)S(1)} %get-tuple-element.140), channel_id=1, source_target_pairs={{24,0},{28,4},{16,8},{20,12},{8,16},{12,20},{0,24},{4,28},{25,1},{... | collective-permute-start | bytes 122888 | tf_op jit(solution)/shard_map/ppermute | solution.py:24
  61.7 4.3 %collective-permute-start.19 = (bf16[3,128,256]{2,1,0:T(8,128)(2,1)S(1)}, bf16[3,128,256]{2,1,0:T(8,128)(2,1)S(1)}, u32[]{:S(2)}, u32[]{:S(2)}) collective-permute-start(bf16[3,128,256]{2,1,0:T(8,128)(2,1)S(1)} %second_pair.1), channel_id=1, source_target_pairs={{4,0},{0,4},{12,8},{8,12},{20,16},{16,20},{28,24},{24,28},{5,1},{1... | collective-permute-start | bytes 589832 | tf_op jit(solution)/shard_map/ppermute | solution.py:24
  61.8 7.6 %collective-permute-start.18 = (bf16[3,128,256]{2,1,0:T(8,128)(2,1)S(1)}, bf16[3,128,256]{2,1,0:T(8,128)(2,1)S(1)}, u32[]{:S(2)}, u32[]{:S(2)}) collective-permute-start(bf16[3,128,256]{2,1,0:T(8,128)(2,1)S(1)} %get-tuple-element.142), channel_id=1, source_target_pairs={{28,0},{8,4},{4,8},{16,12},{12,16},{24,20},{20,24},{0,28},{29,1},{... | collective-permute-start | bytes 589832 | tf_op jit(solution)/shard_map/ppermute | solution.py:33
  73.6 1.4 %collective-permute-start.20 = (f32[16,256]{1,0:T(8,128)S(1)}, f32[16,256]{1,0:T(8,128)S(1)}, u32[]{:S(2)}, u32[]{:S(2)}) collective-permute-start(f32[16,256]{1,0:T(8,128)S(1)} %get-tuple-element.147), channel_id=1, source_target_pairs={{4,0},{0,4},{12,8},{8,12},{20,16},{16,20},{28,24},{24,28},{5,1},{1... | collective-permute-start | bytes 49160 | tf_op jit(solution)/shard_map/ppermute | solution.py:24
  73.8 5.0 %collective-permute-start.21 = (f32[16,256]{1,0:T(8,128)S(1)}, f32[16,256]{1,0:T(8,128)S(1)}, u32[]{:S(2)}, u32[]{:S(2)}) collective-permute-start(f32[16,256]{1,0:T(8,128)S(1)} %get-tuple-element.148), channel_id=1, source_target_pairs={{28,0},{8,4},{4,8},{16,12},{12,16},{24,20},{20,24},{0,28},{29,1},{... | collective-permute-start | bytes 49160 | tf_op jit(solution)/shard_map/ppermute | solution.py:33
  78.8 3.7 %collective-permute-start.22 = (f32[3,256]{1,0:T(4,128)S(1)}, f32[3,256]{1,0:T(4,128)S(1)}, u32[]{:S(2)}, u32[]{:S(2)}) collective-permute-start(f32[3,256]{1,0:T(4,128)S(1)} %get-tuple-element.152), channel_id=1, source_target_pairs={{1,0},{0,1},{3,2},{2,3},{5,4},{4,5},{7,6},{6,7},{9,8},{8,9},{11,10... | collective-permute-start | bytes 9224 | tf_op jit(solution)/shard_map/ppermute | solution.py:24
  80.3 4.5 %collective-permute-start.23 = (f32[3,256]{1,0:T(4,128)S(1)}, f32[3,256]{1,0:T(4,128)S(1)}, u32[]{:S(2)}, u32[]{:S(2)}) collective-permute-start(f32[3,256]{1,0:T(4,128)S(1)} %get-tuple-element.154), channel_id=1, source_target_pairs={{3,0},{2,1},{1,2},{0,3},{7,4},{6,5},{5,6},{4,7},{11,8},{10,9},{9,1... | collective-permute-start | bytes 9224 | tf_op jit(solution)/shard_map/ppermute | solution.py:33
  81.5 3.6 %collective-permute-start.24 = (f32[3,256]{1,0:T(4,128)S(1)}, f32[3,256]{1,0:T(4,128)S(1)}, u32[]{:S(2)}, u32[]{:S(2)}) collective-permute-start(f32[3,256]{1,0:T(4,128)S(1)} %get-tuple-element.153), channel_id=1, source_target_pairs={{2,0},{3,1},{0,2},{1,3},{6,4},{7,5},{4,6},{5,7},{10,8},{11,9},{8,1... | collective-permute-start | bytes 9224 | tf_op jit(solution)/shard_map/ppermute | solution.py:42
